TPU v7x, 128 devices: a whole 4x4x4 slice. The times are simulated.
128 devices in a mesh: ctx: 8 (over z, y_lo), fsdp: 16 (over y_hi, x, core).
Axes of the slice: x: 4, y: 4 (y_hi: 2, y_lo: 2; y = y_hi * 2 + y_lo), z: 4, core: 2. Of those that a mesh axis runs over, the one named last changes fastest.
Arguments:
- tokens: bfloat16 [2, 16, 1024, 1024], P(None, 'fsdp', 'ctx'), may hold values from -6 to 6
- segments: int32 [2, 16, 1024], P(None, 'fsdp'), may hold values from 0 to 1, as said below
- routes: int32 [2, 16, 1024, 8], P(None, 'fsdp', 'ctx'), may hold values from 0 to 31, all different within a row; in each aligned block of 128 rows (0 to 127, 128 to 255, ..., all dimensions but the last counted through in order) at most 48 rows name the same one
- w_query: bfloat16 [1024, 1024], P(('ctx', 'fsdp')), may hold values from -0.1875 to 0.1875
- w_key: bfloat16 [1024, 512], P(('ctx', 'fsdp')), may hold values from -0.1875 to 0.1875
- w_value: bfloat16 [1024, 512], P(('ctx', 'fsdp')), may hold values from -0.1875 to 0.1875
- w_out: bfloat16 [1024, 1024], P(('ctx', 'fsdp')), may hold values from -3 to 3
- w_router: bfloat16 [1024, 32], P(('ctx', 'fsdp')), may hold values from -0.09375 to 0.09375
- attn_gain: bfloat16 [1024], P(('ctx', 'fsdp')), may hold values from 0.5 to 1.5
- mlp_gain: bfloat16 [1024], P(('ctx', 'fsdp')), may hold values from 0.5 to 1.5
- qk_gain: bfloat16 [128], P(('ctx', 'fsdp')), may hold values from 0.5 to 1.5
- w_gate: bfloat16 [32, 1024, 512], P('fsdp', 'ctx'), may hold values from -0.1875 to 0.1875
- w_up: bfloat16 [32, 1024, 512], P('fsdp', 'ctx'), may hold values from -0.1875 to 0.1875
- w_down: bfloat16 [32, 1024, 512], P('fsdp', 'ctx'), may hold values from -1 to 1
- cotangent: bfloat16 [2, 16, 1024, 1024], P(None, 'fsdp', 'ctx'), may hold values from -6 to 6
Outputs:
- out: bfloat16 [2, 16, 1024, 1024], P(None, 'fsdp', 'ctx')
- d_tokens: float32 [2, 16, 1024, 1024], P(None, 'fsdp', 'ctx')
- grad_query: float32 [1024, 1024], P(('ctx', 'fsdp'))
- grad_key: float32 [1024, 512], P(('ctx', 'fsdp'))
- grad_value: float32 [1024, 512], P(('ctx', 'fsdp'))
- grad_out: float32 [1024, 1024], P(('ctx', 'fsdp'))
- grad_router: float32 [1024, 32], P(('ctx', 'fsdp'))
- grad_attn_gain: float32 [1024], P(('ctx', 'fsdp'))
- grad_mlp_gain: float32 [1024], P(('ctx', 'fsdp'))
- grad_qk_gain: float32 [128], P(('ctx', 'fsdp'))
- grad_gate: float32 [32, 1024, 512], P('fsdp', 'ctx')
- grad_up: float32 [32, 1024, 512], P('fsdp', 'ctx')
- grad_down: float32 [32, 1024, 512], P('fsdp', 'ctx')
Inputs may be any that keep to these rules, and one draw needn't show every extreme that they name: `segments`: segment ids never fall along a sequence; a sequence holds one or two documents; for each of the 16 sequence slots, one of the 2 micro-batches, drawn from the seed, holds a single document of all 1024 tokens. `routes`: A token's 8 experts differ; among the 128 tokens of one device in one micro-batch no expert is named more than 48 times.
All inputs are finite; a program needn't handle non-finite values.
Results may differ from a plain program's by a relative error of at most 0.03.
Values may be sent and summed in bfloat16 or wider, within the bound.
No kernel may reach another device: no remote copies, remote signals or barrier semaphores. Data moves between devices by JAX's collectives and lax.ppermute only.
A program may use at most 192 MiB of HBM per device.

v0:
```python
import jax
import jax.numpy as jnp
from jax import lax
from jax.sharding import PartitionSpec as P

H = 16
KV = 8
DH = 64
TOPK = 8
WINDOW = 1024


EPS = 1e-06
THETA = 10000.0


def for_sending(x):

    def short(part):
        return part.astype(jnp.bfloat16) if part.dtype == jnp.float32 else part

    return jax.tree.map(short, x)


def rms_scale(values, gain):
    return values * lax.rsqrt(jnp.mean(values * values, axis=-1, keepdims=True) + EPS) * gain


def rope_tables(positions):
    half = DH // 2
    inverse = THETA ** (-(jnp.arange(half, dtype=jnp.float32) * 2.0) / DH)
    angles = positions.astype(jnp.float32)[:, None] * inverse[None, :]
    return (jnp.cos(angles), jnp.sin(angles))


def head_post(raw, gain, cosine, sine, heads):
    shaped = raw.reshape(raw.shape[:-1] + (heads, DH))
    normed = rms_scale(shaped, gain)
    half = DH // 2
    first_half = normed[..., :half]
    second_half = normed[..., half:]
    cos_grid = cosine[:, None, :]
    sin_grid = sine[:, None, :]
    return jnp.concatenate(
        [
            first_half * cos_grid - second_half * sin_grid,
            second_half * cos_grid + first_half * sin_grid,
        ],
        axis=-1,
    )


def body(
    tokens,
    segments,
    routes,
    w_query,
    w_key,
    w_value,
    w_out,
    w_router,
    attn_gain,
    mlp_gain,
    qk_gain,
    w_gate,
    w_up,
    w_down,
    cotangent,
):
    micro_count = tokens.shape[0]
    tok_rows = tokens.shape[2]
    width = tokens.shape[3]
    seq_length = segments.shape[2]
    cycle_place = lax.axis_index("ctx")
    shard_count = lax.axis_size("fsdp")
    local_experts = w_gate.shape[0]
    expert_count = local_experts * shard_count
    capacity = (3 * tok_rows * TOPK + 2 * expert_count - 1) // (2 * expert_count)
    positions = cycle_place * tok_rows + jnp.arange(tok_rows, dtype=jnp.int32)
    cosine, sine = rope_tables(positions)
    key_places = jnp.arange(seq_length, dtype=jnp.int32)
    window_mask = jnp.abs(positions[:, None] - key_places[None, :]) < WINDOW // 2
    scale = DH ** (-0.5)
    expert_ids = jnp.arange(expert_count, dtype=jnp.int32)
    head_ratio = H // KV

    def micro_step(weights, input_rows, seg_row, route_rows, grad_rows):
        layer_full, expert_full = weights
        (
            weight_query,
            weight_key,
            weight_value,
            weight_out,
            weight_router,
            gain_attn,
            gain_mlp,
            gain_heads,
        ) = layer_full
        weight_gate, weight_up, weight_down = expert_full
        gain_heads = gain_heads.astype(jnp.float32)
        start = input_rows.astype(jnp.float32)
        normed_one, norm_one_back = jax.vjp(rms_scale, start, gain_attn.astype(jnp.float32))
        hidden = normed_one.astype(jnp.bfloat16)
        query_raw = jnp.dot(hidden, weight_query, preferred_element_type=jnp.float32)
        key_raw = jnp.dot(hidden, weight_key, preferred_element_type=jnp.float32)
        value_raw = jnp.dot(hidden, weight_value, preferred_element_type=jnp.float32)

        def query_post(raw, gain):
            return head_post(raw, gain, cosine, sine, H)

        def key_post(raw, gain):
            return head_post(raw, gain, cosine, sine, KV)

        query_rot, query_back = jax.vjp(query_post, query_raw, gain_heads[:DH])
        key_rot, key_back = jax.vjp(key_post, key_raw, gain_heads[DH:])
        query_grouped = query_rot.astype(jnp.bfloat16).reshape(tok_rows, KV, head_ratio, DH)
        key_use = key_rot.astype(jnp.bfloat16)
        value_use = value_raw.astype(jnp.bfloat16).reshape(tok_rows, KV, DH)
        key_all, value_all = (
            lax.all_gather(key_use, "ctx", axis=0, tiled=True),
            lax.all_gather(value_use, "ctx", axis=0, tiled=True),
        )
        query_seg = lax.dynamic_slice_in_dim(seg_row, cycle_place * tok_rows, tok_rows)
        allowed = (query_seg[:, None] == seg_row[None, :]) & window_mask

        def scores_of():
            raw_scores = (
                jnp.einsum(
                    "qgrd,kgd->grqk", query_grouped, key_all, preferred_element_type=jnp.float32
                )
                * scale
            )
            return jnp.where(allowed[None, None], raw_scores, -1e30)

        scores = scores_of()
        highest = jnp.max(scores, axis=-1, keepdims=True)
        shifted = jnp.exp(scores - highest)
        total = jnp.sum(shifted, axis=-1, keepdims=True)
        log_total = highest + jnp.log(total)
        probs_low = (shifted / total).astype(jnp.bfloat16)
        mixed = jnp.einsum(
            "grqk,kgd->qgrd", probs_low, value_all, preferred_element_type=jnp.float32
        )
        mixed_low = mixed.reshape(tok_rows, H * DH).astype(jnp.bfloat16)
        middle = start + jnp.dot(mixed_low, weight_out, preferred_element_type=jnp.float32)
        normed_two, norm_two_back = jax.vjp(rms_scale, middle, gain_mlp.astype(jnp.float32))
        hidden_two = normed_two.astype(jnp.bfloat16)
        logits = jnp.dot(hidden_two, weight_router, preferred_element_type=jnp.float32)
        gates = jax.nn.softmax(jnp.take_along_axis(logits, route_rows, axis=1), axis=-1)
        flat_routes = route_rows.reshape(-1)
        one_hot = (flat_routes[:, None] == expert_ids[None, :]).astype(jnp.int32)
        slots = jnp.sum(jnp.cumsum(one_hot, axis=0) * one_hot, axis=1) - 1
        slot_pos = flat_routes * capacity + slots
        sentinel = tok_rows * TOPK
        table = (
            jnp.full((expert_count * capacity,), sentinel, jnp.int32)
            .at[slot_pos]
            .set(jnp.arange(sentinel, dtype=jnp.int32))
        )
        token_index = jnp.where(table == sentinel, tok_rows, table // TOPK)
        padded = jnp.concatenate([hidden_two, jnp.zeros((1, width), jnp.bfloat16)], axis=0)
        received = lax.all_to_all(
            padded[token_index], "fsdp", split_axis=0, concat_axis=0, tiled=True
        )
        expert_rows = received.reshape(shard_count, local_experts, capacity, width)
        gate_proj = jnp.einsum(
            "secd,edf->secf", expert_rows, weight_gate, preferred_element_type=jnp.float32
        )
        up_proj = jnp.einsum(
            "secd,edf->secf", expert_rows, weight_up, preferred_element_type=jnp.float32
        )
        sigmoid_gate = jax.nn.sigmoid(gate_proj)
        silu_gate = gate_proj * sigmoid_gate
        active = (silu_gate * up_proj).astype(jnp.bfloat16)
        expert_out = jnp.einsum(
            "secf,edf->secd", active, weight_down, preferred_element_type=jnp.float32
        ).astype(jnp.bfloat16)
        returned = lax.all_to_all(
            expert_out.reshape(expert_count * capacity, width),
            "fsdp",
            split_axis=0,
            concat_axis=0,
            tiled=True,
        )
        picked = returned[slot_pos].reshape(tok_rows, TOPK, width)
        output_rows = (
            middle + jnp.einsum("tk,tkd->td", gates, picked, preferred_element_type=jnp.float32)
        ).astype(jnp.bfloat16)
        grad_top = grad_rows.astype(jnp.float32)
        grad_gates = jnp.einsum("td,tkd->tk", grad_top, picked, preferred_element_type=jnp.float32)
        grad_expert = (
            (gates[:, :, None] * grad_top[:, None, :])
            .astype(jnp.bfloat16)
            .reshape(tok_rows * TOPK, width)
        )
        grad_send = (
            jnp.zeros((expert_count * capacity, width), jnp.bfloat16).at[slot_pos].set(grad_expert)
        )
        grad_arrived = lax.all_to_all(
            grad_send, "fsdp", split_axis=0, concat_axis=0, tiled=True
        ).reshape(shard_count, local_experts, capacity, width)
        grad_active = jnp.einsum(
            "secd,edf->secf", grad_arrived, weight_down, preferred_element_type=jnp.float32
        )
        silu_slope = sigmoid_gate * (1.0 + gate_proj * (1.0 - sigmoid_gate))
        grad_gate_proj = (grad_active * up_proj * silu_slope).astype(jnp.bfloat16)
        grad_up_proj = (grad_active * silu_gate).astype(jnp.bfloat16)
        grad_down_w = jnp.einsum(
            "secd,secf->edf", grad_arrived, active, preferred_element_type=jnp.float32
        )
        grad_gate_w = jnp.einsum(
            "secd,secf->edf", expert_rows, grad_gate_proj, preferred_element_type=jnp.float32
        )
        grad_up_w = jnp.einsum(
            "secd,secf->edf", expert_rows, grad_up_proj, preferred_element_type=jnp.float32
        )
        grad_rows_out = jnp.einsum(
            "secf,edf->secd", grad_gate_proj, weight_gate, preferred_element_type=jnp.float32
        )
        grad_rows_out = grad_rows_out + jnp.einsum(
            "secf,edf->secd", grad_up_proj, weight_up, preferred_element_type=jnp.float32
        )
        grad_back = lax.all_to_all(
            grad_rows_out.reshape(expert_count * capacity, width).astype(jnp.bfloat16),
            "fsdp",
            split_axis=0,
            concat_axis=0,
            tiled=True,
        ).astype(jnp.float32)
        grad_hidden_two = jnp.sum(grad_back[slot_pos].reshape(tok_rows, TOPK, width), axis=1)
        grad_select = gates * (grad_gates - jnp.sum(gates * grad_gates, axis=-1, keepdims=True))
        route_table = (route_rows[:, :, None] == expert_ids[None, None, :]).astype(jnp.float32)
        grad_logits = jnp.einsum("tk,tke->te", grad_select, route_table).astype(jnp.bfloat16)
        grad_router_w = jnp.einsum(
            "td,te->de", hidden_two, grad_logits, preferred_element_type=jnp.float32
        )
        grad_hidden_two = grad_hidden_two + jnp.einsum(
            "te,de->td", grad_logits, weight_router, preferred_element_type=jnp.float32
        )
        grad_middle_norm, grad_mlp_w = norm_two_back(grad_hidden_two)
        grad_middle = grad_top + grad_middle_norm
        grad_branch = grad_middle.astype(jnp.bfloat16)
        grad_out_w = jnp.einsum(
            "te,td->ed", mixed_low, grad_branch, preferred_element_type=jnp.float32
        )
        grad_mixed = jnp.einsum(
            "td,ed->te", grad_branch, weight_out, preferred_element_type=jnp.float32
        )
        grad_mixed = grad_mixed.astype(jnp.bfloat16).reshape(tok_rows, KV, head_ratio, DH)
        probs = jnp.exp(scores_of() - log_total)
        probs_again = probs.astype(jnp.bfloat16)
        grad_probs = jnp.einsum(
            "qgrd,kgd->grqk", grad_mixed, value_all, preferred_element_type=jnp.float32
        )
        grad_scores = (
            probs * (grad_probs - jnp.sum(probs * grad_probs, axis=-1, keepdims=True))
        ).astype(jnp.bfloat16)
        grad_query_rot = (
            jnp.einsum("grqk,kgd->qgrd", grad_scores, key_all, preferred_element_type=jnp.float32)
            * scale
        )
        grad_key_all = (
            jnp.einsum(
                "grqk,qgrd->kgd", grad_scores, query_grouped, preferred_element_type=jnp.float32
            )
            * scale
        )
        grad_value_all = jnp.einsum(
            "grqk,qgrd->kgd", probs_again, grad_mixed, preferred_element_type=jnp.float32
        )
        grad_key_rot, grad_value_use = (
            lax.psum_scatter(
                grad_key_all.astype(jnp.bfloat16), "ctx", scatter_dimension=0, tiled=True
            ).astype(jnp.float32),
            lax.psum_scatter(
                grad_value_all.astype(jnp.bfloat16), "ctx", scatter_dimension=0, tiled=True
            ).astype(jnp.float32),
        )
        grad_query_raw, grad_query_gain = query_back(grad_query_rot.reshape(tok_rows, H, DH))
        grad_key_raw, grad_key_gain = key_back(grad_key_rot)
        grad_query_low = grad_query_raw.astype(jnp.bfloat16)
        grad_key_low = grad_key_raw.astype(jnp.bfloat16)
        grad_value_low = grad_value_use.reshape(tok_rows, KV * DH).astype(jnp.bfloat16)
        grad_query_w = jnp.einsum(
            "td,te->de", hidden, grad_query_low, preferred_element_type=jnp.float32
        )
        grad_key_w = jnp.einsum(
            "td,te->de", hidden, grad_key_low, preferred_element_type=jnp.float32
        )
        grad_value_w = jnp.einsum(
            "td,te->de", hidden, grad_value_low, preferred_element_type=jnp.float32
        )
        grad_hidden = jnp.einsum(
            "te,de->td", grad_query_low, weight_query, preferred_element_type=jnp.float32
        )
        grad_hidden = grad_hidden + jnp.einsum(
            "te,de->td", grad_key_low, weight_key, preferred_element_type=jnp.float32
        )
        grad_hidden = grad_hidden + jnp.einsum(
            "te,de->td", grad_value_low, weight_value, preferred_element_type=jnp.float32
        )
        grad_start_norm, grad_attn_w = norm_one_back(grad_hidden)
        grad_input = grad_middle + grad_start_norm
        layer_grads = (
            grad_query_w,
            grad_key_w,
            grad_value_w,
            grad_out_w,
            grad_router_w,
            grad_attn_w,
            grad_mlp_w,
            jnp.concatenate([grad_query_gain, grad_key_gain]),
        )
        expert_grads = (grad_gate_w, grad_up_w, grad_down_w)
        return (output_rows, grad_input, layer_grads, expert_grads)

    outputs = []
    input_grads = []
    totals = None
    for micro_index in range(micro_count):
        fetch_layer_full = (
            lax.all_gather(w_query, ("ctx", "fsdp"), axis=0, tiled=True),
            lax.all_gather(w_key, ("ctx", "fsdp"), axis=0, tiled=True),
            lax.all_gather(w_value, ("ctx", "fsdp"), axis=0, tiled=True),
            lax.all_gather(w_out, ("ctx", "fsdp"), axis=0, tiled=True),
            lax.all_gather(w_router, ("ctx", "fsdp"), axis=0, tiled=True),
            lax.all_gather(attn_gain, ("ctx", "fsdp"), axis=0, tiled=True),
            lax.all_gather(mlp_gain, ("ctx", "fsdp"), axis=0, tiled=True),
            lax.all_gather(qk_gain, ("ctx", "fsdp"), axis=0, tiled=True),
        )
        fetch_expert_full = (
            lax.all_gather(w_gate, "ctx", axis=1, tiled=True),
            lax.all_gather(w_up, "ctx", axis=1, tiled=True),
            lax.all_gather(w_down, "ctx", axis=1, tiled=True),
        )
        current = (fetch_layer_full, fetch_expert_full)
        output_rows, grad_input, layer_grads, expert_grads = micro_step(
            current,
            tokens[micro_index, 0],
            segments[micro_index, 0],
            routes[micro_index, 0],
            cotangent[micro_index, 0],
        )
        outputs.append(output_rows)
        input_grads.append(grad_input)
        partial_sums = tuple(layer_grads) + tuple(expert_grads)
        totals = partial_sums if totals is None else jax.tree.map(jnp.add, totals, partial_sums)
    layer_part = lax.psum_scatter(totals[:8], ("ctx", "fsdp"), scatter_dimension=0, tiled=True)
    expert_part = jax.tree.map(
        lambda part: part.astype(jnp.float32),
        lax.psum_scatter(for_sending(totals[8:]), "ctx", scatter_dimension=1, tiled=True),
    )
    totals = tuple(layer_part) + tuple(expert_part)
    stacked_out = jnp.stack(outputs)[:, None]
    stacked_grad = jnp.stack(input_grads)[:, None]
    return (stacked_out, stacked_grad) + tuple(totals)


def solution(mesh):
    placed = (
        P(None, "fsdp", "ctx", None),
        P(None, "fsdp", None),
        P(None, "fsdp", "ctx", None),
        P(("ctx", "fsdp"), None),
        P(("ctx", "fsdp"), None),
        P(("ctx", "fsdp"), None),
        P(("ctx", "fsdp"), None),
        P(("ctx", "fsdp"), None),
        P(("ctx", "fsdp")),
        P(("ctx", "fsdp")),
        P(("ctx", "fsdp")),
        P("fsdp", "ctx", None),
        P("fsdp", "ctx", None),
        P("fsdp", "ctx", None),
        P(None, "fsdp", "ctx", None),
    )
    return jax.shard_map(
        body,
        mesh=mesh,
        in_specs=placed,
        out_specs=(
            P(None, "fsdp", "ctx", None),
            P(None, "fsdp", "ctx", None),
            P(("ctx", "fsdp"), None),
            P(("ctx", "fsdp"), None),
            P(("ctx", "fsdp"), None),
            P(("ctx", "fsdp"), None),
            P(("ctx", "fsdp"), None),
            P(("ctx", "fsdp")),
            P(("ctx", "fsdp")),
            P(("ctx", "fsdp")),
            P("fsdp", "ctx", None),
            P("fsdp", "ctx", None),
            P("fsdp", "ctx", None),
        ),
        check_vma=False,
    )
```

profile of v0, /device:TPU:0, one launch (start us, length us, event | category | flops | bytes accessed | tf_op | source)
XLA Modules:
  0.0 4795.7 jit_solution(12581808967325675178)
XLA Ops:
  11.9 68.4 %all-reduce.18 = (bf16[128]{0:T(256)(128)(2,1)S(1)}, bf16[1024]{0:T(1024)(128)(2,1)S(1)}, bf16[1024]{0:T(1024)(128)(2,1)S(1)}) all-reduce(bf16[128]{0:T(256)(128)(2,1)S(1)} %dynamic-update-slice.1, bf16[1024]{0:T(1024)(128)(2,1)S(1)} %dynamic-update-slice, ...), channel_id=1, replica_groups=mesh['ctx'=8,'fsdp'=16] {'ctx','fsdp'}, use_global_device_ids=true, to_apply=%add.11 | all-reduce | flops 2176 | bytes 8704
  82.3 120.8 %all-gather.16.cloned.1.call-done = bf16[1024,512]{1,0:T(8,128)(2,1)} async-done(((bf16[8,512]{1,0:T(8,128)(2,1)}), bf16[1024,512]{1,0:T(8,128)(2,1)}) %all-gather.16.cloned.1.call-update) | async-done | bytes 1048592 | tf_op jit(solution)/shard_map/all_gather | solution.py:323
  208.9 185.0 %all-gather.12.cloned.1.call-done = bf16[1024,512]{1,0:T(8,128)(2,1)} async-done(((bf16[8,512]{1,0:T(8,128)(2,1)}), bf16[1024,512]{1,0:T(8,128)(2,1)}) %all-gather.12.cloned.1.call-update) | async-done | bytes 1048592 | tf_op jit(solution)/shard_map/all_gather | solution.py:324
  414.1 174.5 %all-gather.20.cloned.1.call-done = bf16[1024,1024]{1,0:T(8,128)(2,1)} async-done(((bf16[8,1024]{1,0:T(8,128)(2,1)}), bf16[1024,1024]{1,0:T(8,128)(2,1)}) %all-gather.20.cloned.1.call-update) | async-done | bytes 2097168 | tf_op jit(solution)/shard_map/all_gather | solution.py:322
  594.7 34.6 all-gather.18.cloned.1.call-done
  636.5 35.8 all-gather.14.cloned.1.call-done
  677.5 191.3 %all-gather.22.cloned.1.call-done = bf16[1024,1024]{1,0:T(8,128)(2,1)} async-done(((bf16[8,1024]{1,0:T(8,128)(2,1)}), bf16[1024,1024]{1,0:T(8,128)(2,1)}) %all-gather.22.cloned.1.call-update) | async-done | bytes 2097168 | tf_op jit(solution)/shard_map/all_gather | solution.py:325
  884.2 70.7 %all-gather.24.cloned.1.call-done = bf16[2,1024,512]{2,1,0:T(8,128)(2,1)} async-done(((bf16[2,128,512]{2,1,0:T(8,128)(2,1)}), bf16[2,1024,512]{2,1,0:T(8,128)(2,1)}) %all-gather.24.cloned.1.call-update) | async-done | bytes 2097168 | tf_op jit(solution)/shard_map/all_gather | solution.py:332
  961.0 47.0 all-gather.26.cloned.1.call-done
  1014.6 46.5 all-gather.28.cloned.1.call-done
  1073.9 205.8 %all_gather.65 = bf16[1024,32]{1,0:T(8,128)(2,1)S(1)} all-gather(bf16[8,32]{1,0:T(8,128)(2,1)S(1)} %copy-done.139), channel_id=1, replica_groups=mesh['ctx'=8,'fsdp'=16] {'ctx','fsdp'}, dimensions={0}, use_global_device_ids=true | all-gather | bytes 66048 | tf_op jit(solution)/shard_map/all_gather | solution.py:326
  1330.8 26.7 all-to-all-done.4
  1377.4 39.0 all-gather.32.cloned.1.call-done
  1423.6 39.1 all-gather.30.cloned.1.call-done
  1474.5 9.2 gather_fusion.4
  1494.5 47.1 all_to_all.72
  1568.3 29.7 all-to-all-done.3
  1614.1 46.9 all_to_all.73
  1683.9 35.4 all-to-all-done.7
  1722.9 9.2 gather_fusion.5
  1817.8 14.4 reduce-scatter.40.cloned.1.call-done
  1835.1 39.3 reduce-scatter.38.cloned.1.call-done
  1875.5 41.7 reduce-scatter.34.cloned.1.call-done
  1936.8 128.7 %all-reduce.21.cloned.1.call-done = f32[1024,32]{1,0:T(8,128)} async-done(((f32[1024,32]{1,0:T(8,128)}), f32[1024,32]{1,0:T(8,128)}) %all-reduce.21.cloned.1.call-update) | async-done | bytes 131088
  2074.1 45.7 reduce-scatter.32.cloned.1.call-done
  2121.6 52.4 %reduce-scatter.28.cloned.1.call-done = bf16[2,128,512]{2,1,0:T(8,128)(2,1)} async-done(((bf16[2,1024,512]{2,1,0:T(8,128)(2,1)}), bf16[2,128,512]{2,1,0:T(8,128)(2,1)}) %reduce-scatter.28.cloned.1.call-update) | async-done | bytes 262160 | tf_op jit(solution)/shard_map/reduce_scatter | solution.py:351
  2175.8 52.6 %reduce-scatter.30.cloned.1.call-done = bf16[2,128,512]{2,1,0:T(8,128)(2,1)} async-done(((bf16[2,1024,512]{2,1,0:T(8,128)(2,1)}), bf16[2,128,512]{2,1,0:T(8,128)(2,1)}) %reduce-scatter.30.cloned.1.call-update) | async-done | bytes 262160 | tf_op jit(solution)/shard_map/reduce_scatter | solution.py:351
  2234.8 65.3 %all-reduce.17 = (f32[1024]{0:T(1024)S(1)}, f32[1024]{0:T(1024)S(1)}, f32[128]{0:T(128)S(1)}) all-reduce(f32[1024]{0:T(1024)S(1)} %add.396, f32[1024]{0:T(1024)S(1)} %copy-done.132, f32[128]{0:T(128)S(1)} %maximum_add_fusion), channel_id=11, replica_groups=mesh['ctx'=8,'fsdp'=16] {'ctx','fsdp'}, use_global_device_ids=true, to_apply=%region_51.53.clone | all-reduce | flops 2176 | bytes 17408
  2304.3 566.1 %reduce-scatter.24.cloned.1.call-done = f32[8,512]{1,0:T(8,128)} async-done(((f32[1024,512]{1,0:T(8,128)}), f32[8,512]{1,0:T(8,128)}) %reduce-scatter.24.cloned.1.call-update) | async-done | bytes 16400 | tf_op jit(solution)/shard_map/reduce_scatter | solution.py:348
  2870.4 636.3 %reduce-scatter.22.cloned.1.call-done = f32[8,512]{1,0:T(8,128)} async-done(((f32[1024,512]{1,0:T(8,128)}), f32[8,512]{1,0:T(8,128)}) %reduce-scatter.22.cloned.1.call-update) | async-done | bytes 16400 | tf_op jit(solution)/shard_map/reduce_scatter | solution.py:348
  3506.7 641.0 %reduce-scatter.26.cloned.1.call-done = f32[8,1024]{1,0:T(8,128)} async-done(((f32[1024,1024]{1,0:T(8,128)}), f32[8,1024]{1,0:T(8,128)}) %reduce-scatter.26.cloned.1.call-update) | async-done | bytes 32784 | tf_op jit(solution)/shard_map/reduce_scatter | solution.py:348
  4147.8 640.9 %reduce-scatter.20.cloned.1.call-done = f32[8,1024]{1,0:T(8,128)} async-done(((f32[1024,1024]{1,0:T(8,128)}), f32[8,1024]{1,0:T(8,128)}) %reduce-scatter.20.cloned.1.call-update) | async-done | bytes 32784 | tf_op jit(solution)/shard_map/reduce_scatter | solution.py:348
  (590 shorter events, 390.9 us)
Async XLA Ops:
  7.2 195.9 %all-gather.16.cloned.1.call-start = ((), (), s32[]{:S(2)}) async-start(), calls=%async_computation.21 | async-start | bytes 1056768 | tf_op jit(solution)/shard_map/all_gather | solution.py:323
  7.9 386.1 %all-gather.12.cloned.1.call-start = ((), (), s32[]{:S(2)}) async-start(), calls=%async_computation.19 | async-start | bytes 1056768 | tf_op jit(solution)/shard_map/all_gather | solution.py:324
  8.7 579.9 %all-gather.20.cloned.1.call-start = ((), (), s32[]{:S(2)}) async-start(), calls=%async_computation.23 | async-start | bytes 2113536 | tf_op jit(solution)/shard_map/all_gather | solution.py:322
  9.4 620.0 %all-gather.18.cloned.1.call-start = ((), (), s32[]{:S(2)}) async-start(), calls=%async_computation.22 | async-start | bytes 1179648 | tf_op jit(solution)/shard_map/all_gather | solution.py:120
  80.3 1249.3 %copy-start.91 = (f32[1024]{0:T(1024)}, f32[1024]{0:T(1024)S(1)}, u32[]{:S(2)}) copy-start(f32[1024]{0:T(1024)S(1)} %convert_element_type.333) | copy-start | bytes 12292
  82.1 1247.5 %copy-start.123 = (f32[128]{0:T(128)}, f32[128]{0:T(128)S(1)}, u32[]{:S(2)}) copy-start(f32[128]{0:T(128)S(1)} %fusion.219) | copy-start | bytes 1540
  82.3 511.6 %copy-start.93 = (f32[128,32]{0,1:T(8,128)}, f32[128,32]{0,1:T(8,128)S(1)}, u32[]{:S(2)}) copy-start(f32[128,32]{0,1:T(8,128)S(1)} %get-tuple-element.126) | copy-start | bytes 49156
  208.9 463.4 %all-gather.14.cloned.1.call-start = ((), (), s32[]{:S(2)}) async-start(), calls=%async_computation.20 | async-start | bytes 1179648 | tf_op jit(solution)/shard_map/all_gather | solution.py:121
  396.3 472.5 %all-gather.22.cloned.1.call-start = ((), (), s32[]{:S(2)}) async-start(), calls=%async_computation.24 | async-start | bytes 2113536 | tf_op jit(solution)/shard_map/all_gather | solution.py:325
  396.9 557.9 %all-gather.24.cloned.1.call-start = ((), (), s32[]{:S(2)}) async-start(), calls=%async_computation.25 | async-start | bytes 2359296 | tf_op jit(solution)/shard_map/all_gather | solution.py:332
  397.7 610.3 %all-gather.26.cloned.1.call-start = ((), (), s32[]{:S(2)}) async-start(), calls=%async_computation.26 | async-start | bytes 2359296 | tf_op jit(solution)/shard_map/all_gather | solution.py:333
  878.5 76.4 %all-to-all-start = ((bf16[16,96,1024]{2,1,0:T(8,128)(2,1)}), bf16[16,96,1024]{2,1,0:T(8,128)(2,1)S(1)}, u32[]{:S(2)}, u32[]{:S(2)}) async-start(bf16[16,96,1024]{2,1,0:T(8,128)(2,1)} %bitcast.28), calls=%async_computation | async-start | bytes 6291456 | tf_op jit(solution)/shard_map/all_to_all | solution.py:162
  883.5 177.7 %all-gather.28.cloned.1.call-start = ((), (), s32[]{:S(2)}) async-start(), calls=%async_computation.27 | async-start | bytes 2359296 | tf_op jit(solution)/shard_map/all_gather | solution.py:334
  1067.1 225.8 %all-to-all-start.1 = ((bf16[16,96,1024]{2,1,0:T(8,128)(2,1)}), bf16[16,96,1024]{2,1,0:T(8,128)(2,1)S(1)}, u32[]{:S(2)}, u32[]{:S(2)}) async-start(bf16[16,96,1024]{2,1,0:T(8,128)(2,1)} %bitcast.630), calls=%async_computation.1 | async-start | bytes 6291456 | tf_op jit(solution)/shard_map/all_to_all | solution.py:178
  1309.8 47.7 all-to-all-start.4
  1314.5 102.0 %all-gather.32.cloned.1.call-start = ((), (), s32[]{:S(2)}) async-start(), calls=%async_computation.29 | async-start | bytes 1179648 | tf_op jit(solution)/shard_map/all_gather | solution.py:120
  1315.5 147.1 %all-gather.30.cloned.1.call-start = ((), (), s32[]{:S(2)}) async-start(), calls=%async_computation.28 | async-start | bytes 1179648 | tf_op jit(solution)/shard_map/all_gather | solution.py:121
  1371.6 97.7 %all-to-all-start.5 = ((bf16[16,96,1024]{2,1,0:T(8,128)(2,1)}), bf16[16,96,1024]{2,1,0:T(8,128)(2,1)}, u32[]{:S(2)}, u32[]{:S(2)}) async-start(bf16[16,96,1024]{2,1,0:T(8,128)(2,1)} %bitcast.629), calls=%async_computation.5 | async-start | bytes 6291456 | tf_op jit(solution)/shard_map/all_to_all | solution.py:223
  1551.9 46.1 all-to-all-start.3
  1673.2 46.1 all-to-all-start.7
  1677.1 139.2 %reduce-scatter.36.cloned.1.call-start = ((), (), s32[]{:S(2)}) async-start(), calls=%async_computation.38 | async-start | bytes 1179648 | tf_op jit(solution)/shard_map/convert_element_type | solution.py:283
  1748.4 83.8 %reduce-scatter.40.cloned.1.call-start = ((), (), s32[]{:S(2)}) async-start(), calls=%async_computation.40 | async-start | bytes 1179648 | tf_op jit(solution)/shard_map/convert_element_type | solution.py:283
  1757.5 117.0 %reduce-scatter.38.cloned.1.call-start = ((), (), s32[]{:S(2)}) async-start(), calls=%async_computation.39 | async-start | bytes 1179648
  1772.2 145.0 %reduce-scatter.34.cloned.1.call-start = ((), (), s32[]{:S(2)}) async-start(), calls=%async_computation.37 | async-start | bytes 1179648
  1786.8 278.7 %all-reduce.21.cloned.1.call-start = ((), (), s32[]{:S(2)}) async-start(), calls=%async_computation.41 | async-start | bytes 1048576
  1794.5 325.3 %reduce-scatter.32.cloned.1.call-start = ((), (), s32[]{:S(2)}) async-start(), calls=%async_computation.36 | async-start | bytes 2359296 | tf_op jit(solution)/shard_map/reduce_scatter | solution.py:351
  1801.8 372.3 %reduce-scatter.28.cloned.1.call-start = ((), (), s32[]{:S(2)}) async-start(), calls=%async_computation.34 | async-start | bytes 2359296 | tf_op jit(solution)/shard_map/reduce_scatter | solution.py:351
  1809.0 419.4 %reduce-scatter.30.cloned.1.call-start = ((), (), s32[]{:S(2)}) async-start(), calls=%async_computation.35 | async-start | bytes 2359296 | tf_op jit(solution)/shard_map/reduce_scatter | solution.py:351
  1816.2 1054.2 %reduce-scatter.24.cloned.1.call-start = ((), (), s32[]{:S(2)}) async-start(), calls=%async_computation.32 | async-start | bytes 2113536 | tf_op jit(solution)/shard_map/reduce_scatter | solution.py:348
  1835.0 1671.7 %reduce-scatter.22.cloned.1.call-start = ((), (), s32[]{:S(2)}) async-start(), calls=%async_computation.31 | async-start | bytes 2113536 | tf_op jit(solution)/shard_map/reduce_scatter | solution.py:348
  1921.9 2225.8 %reduce-scatter.26.cloned.1.call-start = ((), (), s32[]{:S(2)}) async-start(), calls=%async_computation.33 | async-start | bytes 4227072 | tf_op jit(solution)/shard_map/reduce_scatter | solution.py:348
  1925.8 2862.9 %reduce-scatter.20.cloned.1.call-start = ((), (), s32[]{:S(2)}) async-start(), calls=%async_computation.30 | async-start | bytes 4227072 | tf_op jit(solution)/shard_map/reduce_scatter | solution.py:348
  (152 other events, 5907.2 us)
Sparse Core Ops, SparseCore 0:
  9.7 193.3 all-gather.15
  204.8 189.1 all-gather.11
  395.7 192.7 all-gather.19
  590.6 38.7 all-gather.17
  631.4 40.8 all-gather.13
  673.9 194.8 all-gather.21
  870.5 84.3 all-gather.23
  956.5 51.4 all-gather.25
  1009.6 51.4 all-gather.27
  1317.1 99.2 all-gather.31
  1418.6 44.0 all-gather.29
  1748.6 41.2 reduce-scatter.35
  1792.3 39.9 reduce-scatter.39
  1834.5 39.9 reduce-scatter.37
  1877.2 39.9 reduce-scatter.33
  1922.4 143.0 all-reduce.20
  2067.9 51.8 reduce-scatter.31
  2122.2 51.7 reduce-scatter.27
  2176.6 51.7 reduce-scatter.29
  2231.3 639.0 reduce-scatter.23
  2873.4 633.3 reduce-scatter.21
  3509.8 637.9 reduce-scatter.25
  4150.7 637.9 reduce-scatter.19
where the time goes:
time: 4800 us
  waiting for transfers between devices  3940 us (82%)
  blocking collectives  434 us (9%)
  matrix products  167 us (3%)
  local copies, waits for them, and re-layouts  117 us (2%)
  other arithmetic  89.3 us (2%)
    reduce_scatter x4, waiting for transfers between devices, body(): lax.psum_scatter(totals[:8], ('ctx', 'fsdp'), scatter_dimension=0, tiled=...  2480 us
    unnamed x26, waiting for transfers between devices  214 us
    all_gather x1, blocking collectives, body(): lax.all_gather(w_router, ('ctx', 'fsdp'), axis=0, tiled=True)  206 us
    all_gather x1, waiting for transfers between devices, body(): lax.all_gather(w_out, ('ctx', 'fsdp'), axis=0, tiled=True)  191 us
    all_gather x1, waiting for transfers between devices, body(): lax.all_gather(w_value, ('ctx', 'fsdp'), axis=0, tiled=True)  185 us
    all_gather x1, waiting for transfers between devices, body(): lax.all_gather(w_query, ('ctx', 'fsdp'), axis=0, tiled=True)  174 us
    reduce_scatter x3, waiting for transfers between devices, body(): lax.psum_scatter(for_sending(totals[8:]), 'ctx', scatter_dimension=1, til...  151 us
    unnamed x2, blocking collectives  134 us
  transfers between devices with their start and end apart: 29, of which 25 were waited for; matrix products, arithmetic and copies ran while one was open for 5% of the time, Pallas kernels for 0%

commit v1 on v0

v1 whole, which is shorter than its diff:
```python
import jax
import jax.numpy as jnp
from jax import lax
from jax.sharding import PartitionSpec as P

H = 16
KV = 8
DH = 64
TOPK = 8
WINDOW = 1024
EPS = 1e-06
THETA = 10000.0

BF = jnp.bfloat16
F32 = jnp.float32


def ctx_perm(dz, dyl):
    return [(z * 2 + y, ((z + dz) % 4) * 2 + (y + dyl) % 2) for z in range(4) for y in range(2)]


def fsdp_perm(dyh, dx, dcore):
    return [
        ((y * 4 + x) * 2 + c, (((y + dyh) % 2) * 4 + (x + dx) % 4) * 2 + (c + dcore) % 2)
        for y in range(2)
        for x in range(4)
        for c in range(2)
    ]


RING = {
    "z": ("ctx", ctx_perm(1, 0), ctx_perm(-1, 0)),
    "x": ("fsdp", fsdp_perm(0, 1, 0), fsdp_perm(0, -1, 0)),
}
PAIR = {
    "yl": ("ctx", ctx_perm(0, 1)),
    "yh": ("fsdp", fsdp_perm(1, 0, 0)),
    "core": ("fsdp", fsdp_perm(0, 0, 1)),
}


def gather_stage(block, name):
    if name in PAIR:
        axis, swap = PAIR[name]
        return jnp.concatenate([block, lax.ppermute(block, axis, swap)], axis=0)
    axis, up, down = RING[name]
    half = block.shape[0] // 2
    before = lax.ppermute(block, axis, up)
    after = lax.ppermute(block, axis, down)
    far_low = lax.ppermute(before[:half], axis, up)
    far_high = lax.ppermute(after[half:], axis, down)
    return jnp.concatenate([block, after, far_low, far_high, before], axis=0)


def gather_all(block, names):
    for name in names:
        block = gather_stage(block, name)
    return block


def add(a, b):
    return (a.astype(F32) + b.astype(F32)).astype(BF)


def scatter_stage(parts, name):
    if name in PAIR:
        axis, swap = PAIR[name]
        half = parts.shape[0] // 2
        return add(parts[:half], lax.ppermute(parts[half:], axis, swap))
    axis, up, down = RING[name]
    size = parts.shape[0] // 4
    half = size // 2
    own, after, far, before = (parts[k * size : (k + 1) * size] for k in range(4))
    low = lax.ppermute(far[:half], axis, up)
    high = lax.ppermute(far[half:], axis, down)
    after = jnp.concatenate([add(after[:half], low), after[half:]], axis=0)
    before = jnp.concatenate([before[:half], add(before[half:], high)], axis=0)
    from_before = lax.ppermute(after, axis, up)
    from_after = lax.ppermute(before, axis, down)
    return (own.astype(F32) + from_before.astype(F32) + from_after.astype(F32)).astype(BF)


def scatter_all(parts, names):
    for name in reversed(names):
        parts = scatter_stage(parts, name)
    return parts


SIZES = {"z": 4, "x": 4, "yl": 2, "yh": 2, "core": 2}


def coordinates():
    c = lax.axis_index("ctx")
    f = lax.axis_index("fsdp")
    return {"z": c // 2, "yl": c % 2, "yh": f // 8, "x": (f // 2) % 4, "core": f % 2}


def owner_order(names, rows):
    place = jnp.arange(128 * rows, dtype=jnp.int32)
    inner = place % rows
    rest = place // rows
    here = coordinates()
    digit = {}
    for name in names:
        digit[name] = (rest % SIZES[name] + here[name]) % SIZES[name]
        rest = rest // SIZES[name]
    block = (((digit["z"] * 2 + digit["yl"]) * 2 + digit["yh"]) * 4 + digit["x"]) * 2 + digit["core"]
    return block * rows + inner


def order_matrix(order):
    return (jnp.arange(order.shape[0], dtype=jnp.int32)[:, None] == order[None, :]).astype(BF)


PATH_A = ("yl", "z", "yh", "x", "core")
PATH_B = ("x", "yh", "yl", "z", "core")
PATH_E = ("yh", "x", "core")


def rms_scale(values, gain):
    return values * lax.rsqrt(jnp.mean(values * values, axis=-1, keepdims=True) + EPS) * gain


def rope_tables(positions):
    half = DH // 2
    inverse = THETA ** (-(jnp.arange(half, dtype=F32) * 2.0) / DH)
    angles = positions.astype(F32)[:, None] * inverse[None, :]
    return (jnp.cos(angles), jnp.sin(angles))


def head_post(raw, gain, cosine, sine, heads):
    shaped = raw.reshape(raw.shape[:-1] + (heads, DH))
    normed = rms_scale(shaped, gain)
    half = DH // 2
    first_half = normed[..., :half]
    second_half = normed[..., half:]
    cos_grid = cosine[:, None, :]
    sin_grid = sine[:, None, :]
    return jnp.concatenate(
        [
            first_half * cos_grid - second_half * sin_grid,
            second_half * cos_grid + first_half * sin_grid,
        ],
        axis=-1,
    )


def mm(a, b):
    return jnp.dot(a, b, preferred_element_type=F32)


def mm_t(a, b):
    return lax.dot_general(a, b, (((1,), (1,)), ((), ())), preferred_element_type=F32)


def t_mm(a, b):
    return lax.dot_general(a, b, (((0,), (0,)), ((), ())), preferred_element_type=F32)


def ein(spec, a, b):
    return jnp.einsum(spec, a, b, preferred_element_type=F32)


def split(v):
    high = v.astype(BF)
    return high, (v - high.astype(F32)).astype(BF)


def body(
    tokens,
    segments,
    routes,
    w_query,
    w_key,
    w_value,
    w_out,
    w_router,
    attn_gain,
    mlp_gain,
    qk_gain,
    w_gate,
    w_up,
    w_down,
    cotangent,
):
    micro = tokens.shape[0]
    tok = tokens.shape[2]
    width = tokens.shape[3]
    length = segments.shape[2]
    rows = w_query.shape[0]
    n_ctx = lax.axis_size("ctx")
    n_fsdp = lax.axis_size("fsdp")
    place = lax.axis_index("ctx")
    shard = lax.axis_index("fsdp")
    local = w_gate.shape[0]
    experts = local * n_fsdp
    cap = (3 * tok * TOPK + 2 * experts - 1) // (2 * experts)
    all_tok = micro * tok
    scale = DH ** (-0.5)

    small = jnp.concatenate(
        [
            w_router,
            attn_gain[:, None],
            mlp_gain[:, None],
            jnp.pad(qk_gain[:, None], ((0, rows - 1), (0, 0))),
        ],
        axis=1,
    )
    small = jnp.pad(small, ((0, 0), (0, 128 - small.shape[1])))
    rel_a = gather_all(jnp.concatenate([small, w_query], axis=1), PATH_A)
    rel_b = gather_all(jnp.concatenate([w_key, w_value], axis=1), PATH_B)
    out_rel = gather_all(w_out, PATH_A)
    order_a = order_matrix(owner_order(PATH_A, rows))
    order_b = order_matrix(owner_order(PATH_B, rows))
    query_rel = rel_a[:, 128:]
    small_all = mm(order_a, rel_a[:, :128])
    router = small_all[:, :experts].astype(BF)
    gain_attn = small_all[:, experts]
    gain_mlp = small_all[:, experts + 1]
    gain_heads = small_all[:, experts + 2].reshape(-1, rows)[:, 0]

    weight_gate = lax.all_gather(w_gate, "ctx", axis=1, tiled=True)
    weight_up = lax.all_gather(w_up, "ctx", axis=1, tiled=True)
    weight_down = lax.all_gather(w_down, "ctx", axis=1, tiled=True)

    cot = cotangent.reshape(all_tok, width)
    route_rows = routes.reshape(all_tok, TOPK)
    routes_low = route_rows.astype(BF).reshape(-1, width)
    pack = jnp.concatenate([cot, routes_low], axis=0)
    pack_all = gather_all(pack[None], PATH_E)
    cot_all = pack_all[:, :all_tok].reshape(n_fsdp, micro, tok, width)
    routes_all = (
        pack_all[:, all_tok:].reshape(n_fsdp, micro, tok, TOPK).astype(jnp.int32)
    )

    start = tokens.reshape(all_tok, width).astype(F32)
    normed_one, norm_one_back = jax.vjp(rms_scale, start, gain_attn)
    hidden = normed_one.astype(BF)
    hidden_a = mm(hidden, order_a).astype(BF)
    hidden_b = mm(hidden, order_b).astype(BF)
    query_raw = mm(hidden_a, query_rel)
    kv_raw = mm(hidden_b, rel_b)
    positions = place * tok + jnp.arange(tok, dtype=jnp.int32)
    cosine, sine = rope_tables(positions)
    cosine = jnp.tile(cosine, (micro, 1))
    sine = jnp.tile(sine, (micro, 1))

    def query_post(raw, gain):
        return head_post(raw, gain, cosine, sine, H)

    def key_post(raw, gain):
        return head_post(raw, gain, cosine, sine, KV)

    query_rot, query_back = jax.vjp(query_post, query_raw, gain_heads[:DH])
    key_rot, key_back = jax.vjp(key_post, kv_raw[:, : KV * DH], gain_heads[DH:])
    ratio = H // KV
    query_low = query_rot.astype(BF).reshape(all_tok, KV, ratio * DH)
    key_low = key_rot.astype(BF)
    value_low = kv_raw[:, KV * DH :].astype(BF).reshape(all_tok, KV, DH)
    qkv = jnp.concatenate([query_low, key_low, value_low], axis=2)
    qkv = qkv.transpose(1, 0, 2)
    qkv_heads = lax.all_to_all(qkv, "ctx", split_axis=0, concat_axis=0, tiled=True)
    qkv_heads = (
        qkv_heads.reshape(n_ctx, micro, tok, -1).transpose(1, 0, 2, 3).reshape(micro, length, -1)
    )
    q_h = qkv_heads[:, :, : ratio * DH].reshape(micro, length, ratio, DH)
    k_h = qkv_heads[:, :, ratio * DH : (ratio + 1) * DH]
    v_h = qkv_heads[:, :, (ratio + 1) * DH :]
    spots = jnp.arange(length, dtype=jnp.int32)
    near = jnp.abs(spots[:, None] - spots[None, :]) < WINDOW // 2
    seg = segments[:, 0]
    allowed = (seg[:, :, None] == seg[:, None, :]) & near[None]

    def scores_of():
        return jnp.where(allowed[:, None], ein("mqrd,mkd->mrqk", q_h, k_h) * scale, -1e30)

    scores = scores_of()
    highest = jnp.max(scores, axis=-1, keepdims=True)
    shifted = jnp.exp(scores - highest)
    total = jnp.sum(shifted, axis=-1, keepdims=True)
    log_total = highest + jnp.log(total)
    probs_low = (shifted / total).astype(BF)
    mixed_h = ein("mrqk,mkd->mqrd", probs_low, v_h).astype(BF).reshape(micro, length, ratio * DH)

    def to_tokens(v):
        v = v.reshape(micro, n_ctx, tok, -1).transpose(1, 0, 2, 3).reshape(n_ctx, all_tok, -1)
        v = lax.all_to_all(v, "ctx", split_axis=0, concat_axis=0, tiled=True)
        return v.transpose(1, 0, 2)

    mixed = to_tokens(mixed_h).reshape(all_tok, width)
    mixed_a = mm(mixed, order_a).astype(BF)
    middle = start + mm(mixed_a, out_rel)
    normed_two, norm_two_back = jax.vjp(rms_scale, middle, gain_mlp)
    hidden_two = normed_two.astype(BF)

    expert_ids = jnp.arange(experts, dtype=jnp.int32)

    def gates_of(rows_low, row_routes):
        logits = mm(rows_low, router)
        chosen = jnp.any(row_routes[:, :, None] == expert_ids, axis=1)
        logits = jnp.where(chosen, logits, -1e30)
        return jnp.where(chosen, jax.nn.softmax(logits, axis=-1), 0.0)

    gates_own = gates_of(hidden_two, route_rows)
    own_ids = shard * local + jnp.arange(local, dtype=jnp.int32)
    own_column = (expert_ids[:, None] == own_ids[None, :]).astype(F32)
    before = jnp.arange(tok, dtype=jnp.int32)
    lower = (before[:, None] >= before[None, :]).astype(BF)
    slot_ids = jnp.arange(cap, dtype=jnp.int32)

    moe_rows = []
    grad_two_rows = []
    grad_gate_rows = []
    expert_grads = None
    for m in range(micro):
        x_all = gather_all(hidden_two[m * tok : (m + 1) * tok][None], PATH_E)
        g_all = cot_all[:, m]
        r_all = routes_all[:, m]
        gates = gates_of(x_all.reshape(-1, width), r_all.reshape(-1, TOPK))
        gates = jnp.sum(gates[:, :, None] * own_column[None], axis=1).reshape(n_fsdp, tok, local)
        mask = jnp.any(r_all[..., None] == own_ids, axis=2)
        count = ein("ut,ste->sue", lower, mask.astype(BF)).astype(jnp.int32)
        slot = jnp.where(mask, count - 1, -1)
        pick = slot[..., None] == slot_ids
        pick_low = pick.astype(BF)
        gate_slots = jnp.sum(jnp.where(pick, gates[..., None], 0.0), axis=1)
        x_e = ein("stej,std->sejd", pick_low, x_all).astype(BF)
        g_e = ein("stej,std->sejd", pick_low, g_all).astype(BF)
        a = ein("sejd,edf->sejf", x_e, weight_gate)
        b = ein("sejd,edf->sejf", x_e, weight_up)
        sig = jax.nn.sigmoid(a)
        silu = a * sig
        active = (silu * b).astype(BF)
        expert_out = ein("sejf,edf->sejd", active, weight_down).astype(BF).astype(F32)
        g_wide = g_e.astype(F32)
        d_gate_slots = jnp.sum(expert_out * g_wide, axis=-1)
        d_gates = jnp.sum(jnp.where(pick, d_gate_slots[:, None], 0.0), axis=-1)
        d_expert = (gate_slots[..., None] * g_wide).astype(BF)
        moe_part = ein(
            "stej,sejd->std", pick_low, (gate_slots[..., None] * expert_out).astype(BF)
        ).astype(BF)
        d_active = ein("sejd,edf->sejf", d_expert, weight_down)
        da = (d_active * b * (sig * (1.0 + a * (1.0 - sig)))).astype(BF)
        db = (d_active * silu).astype(BF)
        grads = (
            ein("sejd,sejf->edf", x_e, da),
            ein("sejd,sejf->edf", x_e, db),
            ein("sejd,sejf->edf", d_expert, active),
        )
        expert_grads = (
            grads if expert_grads is None else jax.tree.map(jnp.add, expert_grads, grads)
        )
        d_route = ein("sejf,edf->sejd", da, weight_gate) + ein("sejf,edf->sejd", db, weight_up)
        d_two_part = ein("stej,sejd->std", pick_low, d_route.astype(BF)).astype(BF)
        d_gates_wide = jnp.sum(d_gates[:, :, None, :] * own_column, axis=-1)
        gate_pack = jnp.stack(split(d_gates_wide), axis=1).reshape(n_fsdp, -1, width)
        back = scatter_all(jnp.concatenate([d_two_part, gate_pack], axis=1), PATH_E)[0]
        grad_two_rows.append(back[:tok].astype(F32))
        gate_back = back[tok:].astype(F32).reshape(2, tok, experts)
        grad_gate_rows.append(gate_back[0] + gate_back[1])
        moe_rows.append(scatter_all(moe_part, PATH_E)[0])

    out = (middle + jnp.concatenate(moe_rows, axis=0).astype(F32)).astype(BF)
    grad_top = cot.astype(F32)
    d_gates = jnp.concatenate(grad_gate_rows, axis=0)
    d_select = gates_own * (d_gates - jnp.sum(gates_own * d_gates, axis=-1, keepdims=True))
    d_logits = d_select.astype(BF)
    grad_router = t_mm(hidden_two, d_logits)
    d_hidden_two = jnp.concatenate(grad_two_rows, axis=0) + mm_t(d_logits, router)
    d_middle, grad_mlp = norm_two_back(d_hidden_two)
    d_middle = d_middle + grad_top
    d_branch = d_middle.astype(BF)
    grad_out_rel = t_mm(mixed_a, d_branch)
    d_mixed = mm_t(mm_t(d_branch, out_rel).astype(BF), order_a).astype(BF)

    d_mixed = d_mixed.reshape(all_tok, KV, ratio * DH).transpose(1, 0, 2)
    d_mixed_h = lax.all_to_all(d_mixed, "ctx", split_axis=0, concat_axis=0, tiled=True)
    d_mixed_h = (
        d_mixed_h.reshape(n_ctx, micro, tok, -1)
        .transpose(1, 0, 2, 3)
        .reshape(micro, length, ratio, DH)
    )
    probs = jnp.exp(scores_of() - log_total)
    probs_again = probs.astype(BF)
    d_probs = ein("mqrd,mkd->mrqk", d_mixed_h, v_h)
    d_scores = (probs * (d_probs - jnp.sum(probs * d_probs, axis=-1, keepdims=True))).astype(BF)
    d_q = ein("mrqk,mkd->mqrd", d_scores, k_h) * scale
    d_k = ein("mrqk,mqrd->mkd", d_scores, q_h) * scale
    d_v = ein("mrqk,mqrd->mkd", probs_again, d_mixed_h)
    d_qkv = jnp.concatenate(
        [
            d_q.astype(BF).reshape(micro, length, ratio * DH),
            d_k.astype(BF),
            d_v.astype(BF),
        ],
        axis=2,
    )
    d_qkv = to_tokens(d_qkv)
    d_query_rot = d_qkv[:, :, : ratio * DH].reshape(all_tok, H, DH).astype(F32)
    d_key_rot = d_qkv[:, :, ratio * DH : (ratio + 1) * DH].astype(F32)
    d_value = d_qkv[:, :, (ratio + 1) * DH :].reshape(all_tok, KV * DH)
    d_query_raw, d_query_gain = query_back(d_query_rot)
    d_key_raw, d_key_gain = key_back(d_key_rot)
    dq = d_query_raw.reshape(all_tok, H * DH).astype(BF)
    dkv = jnp.concatenate([d_key_raw.reshape(all_tok, KV * DH).astype(BF), d_value], axis=1)
    grad_query_rel = t_mm(hidden_a, dq)
    grad_kv_rel = t_mm(hidden_b, dkv)
    d_hidden = 0.0
    for part, order in ((mm_t(dq, query_rel), order_a), (mm_t(dkv, rel_b), order_b)):
        for piece in split(part):
            d_hidden = d_hidden + mm_t(piece, order)
    d_start, grad_attn = norm_one_back(d_hidden)
    d_tokens = d_middle + d_start

    grad_heads = jnp.pad(
        jnp.concatenate([d_query_gain, d_key_gain])[:, None], ((0, 0), (0, rows - 1))
    ).reshape(-1)
    grad_small = jnp.concatenate(
        [grad_router, grad_attn[:, None], grad_mlp[:, None], grad_heads[:, None]], axis=1
    )
    grad_small = jnp.pad(grad_small, ((0, 0), (0, 128 - grad_small.shape[1]))).astype(BF)
    grad_small_rel = t_mm(order_a, grad_small)
    own_a = scatter_all(
        jnp.concatenate([grad_small_rel, grad_query_rel], axis=1).astype(BF), PATH_A
    ).astype(F32)
    own_b = scatter_all(grad_kv_rel.astype(BF), PATH_B).astype(F32)
    own_out = scatter_all(grad_out_rel.astype(BF), PATH_A).astype(F32)
    expert_own = tuple(
        lax.psum_scatter(g.astype(BF), "ctx", scatter_dimension=1, tiled=True).astype(F32)
        for g in expert_grads
    )
    return (
        out.reshape(micro, 1, tok, width),
        d_tokens.reshape(micro, 1, tok, width),
        own_a[:, 128:],
        own_b[:, : KV * DH],
        own_b[:, KV * DH :],
        own_out,
        own_a[:, :experts],
        own_a[:, experts],
        own_a[:, experts + 1],
        own_a[:1, experts + 2],
    ) + expert_own


def solution(mesh):
    weight = P(("ctx", "fsdp"), None)
    gain = P(("ctx", "fsdp"))
    rows = P(None, "fsdp", "ctx", None)
    expert = P("fsdp", "ctx", None)
    return jax.shard_map(
        body,
        mesh=mesh,
        in_specs=(rows, P(None, "fsdp", None), rows)
        + (weight,) * 5
        + (gain,) * 3
        + (expert,) * 3
        + (rows,),
        out_specs=(rows, rows) + (weight,) * 5 + (gain,) * 3 + (expert,) * 3,
        check_vma=False,
    )
```

time: 4800 us -> 822 us (0.17)
  waiting for transfers between devices: 3940 us -> 144 us
  blocking collectives: 434 us -> 0 us
  starting transfers between devices: 31.6 us -> 175 us
  local copies, waits for them, and re-layouts: 117 us -> 204 us
    reduce_scatter x7 -> x3, waiting for transfers between devices: 2640 us -> 0.03 us  [body(): lax.psum_scatter(g.astype(BF), 'ctx', scatter_dimension=1, tiled=True)]
    all_gather x11 -> x3, waiting for transfers between devices: 984 us -> 0.02 us  [the longest x1 0.02 us: body(): weight_gate = lax.all_gather(w_gate, 'ctx', axis=1, tiled=True)]
    unnamed x26 -> x6, waiting for transfers between devices: 214 us -> 1.44 us
    all_gather x1 -> x0, blocking collectives: 206 us -> none  [body(): lax.all_gather(w_router, ('ctx', 'fsdp'), axis=0, tiled=True)]
    ppermute x0 -> x108, starting transfers between devices: none -> 156 us  [the longest x10 34.2 us: scatter_stage(): high = lax.ppermute(far[half:], axis, down)]
    unnamed x2 -> x0, blocking collectives: 134 us -> none
    ppermute x0 -> x108, waiting for transfers between devices: none -> 132 us  [the longest x10 37 us: scatter_stage(): from_after = lax.ppermute(before, axis, down)]
    concatenate x2 -> x17, local copies, waits for them, and re-layouts: 0.04 us -> 95.5 us  [the longest x9 62.9 us: gather_stage(): return jnp.concatenate([block, lax.ppermute(block, axis, swap)], axis=0)]
  transfers between devices with their start and end apart: 29 -> 118, of which waited for: 25 -> 35; matrix products, arithmetic and copies ran while one was open for 5% -> 55% of each run, Pallas kernels for 0% -> 0%
where the time goes in v1:
time: 822 us; the launch traced here: 806 us
  local copies, waits for them, and re-layouts  204 us (25%)
  matrix products  187 us (23%)
  starting transfers between devices  175 us (21%)
  waiting for transfers between devices  144 us (18%)
  other arithmetic  78.5 us (10%)
  between operations  18.2 us (2%)
    dot_general x32, matrix products, ein(): return jnp.einsum(spec, a, b, preferred_element_type=F32)  149 us
    concatenate x9, local copies, waits for them, and re-layouts, gather_stage(): return jnp.concatenate([block, lax.ppermute(block, axis, swap)], axis=0)  62.9 us
    ppermute x10, waiting for transfers between devices, scatter_stage(): from_after = lax.ppermute(before, axis, down)  37 us
    ppermute x10, starting transfers between devices, scatter_stage(): high = lax.ppermute(far[half:], axis, down)  34.2 us
    unnamed x277, local copies, waits for them, and re-layouts  34 us
    concatenate x7, local copies, waits for them, and re-layouts, gather_stage(): return jnp.concatenate([block, after, far_low, far_high, before], axis=0)  31.9 us
    ppermute x10, starting transfers between devices, scatter_stage(): from_after = lax.ppermute(before, axis, down)  30 us
    ppermute x9, starting transfers between devices, gather_stage(): far_high = lax.ppermute(after[half:], axis, down)  24.4 us
  transfers between devices with their start and end apart: 118, of which 35 were waited for; matrix products, arithmetic and copies ran while one was open for 55% of the time, Pallas kernels for 0%

profile of v1, /device:TPU:0, one launch (start us, length us, event | category | flops | bytes accessed | tf_op | source)
XLA Modules:
  0.0 806.0 jit_solution(18173636907641615507)
XLA Ops:
  43.0 11.3 %collective-permute-done.16 = bf16[64,1024]{1,0:T(8,128)(2,1)S(1)} collective-permute-done((bf16[64,1024]{1,0:T(8,128)(2,1)S(1)}, bf16[64,1024]{1,0:T(8,128)(2,1)S(1)}, u32[]{:S(2)}, u32[]{:S(2)}) %collective-permute-start.16) | collective-permute-done | bytes 131104 | tf_op jit(solution)/shard_map/ppermute | solution.py:45
  71.8 5.4 collective-permute-done.8
  87.9 6.6 concatenate.227
  105.3 7.1 collective-permute-done.27
  121.8 10.4 %concatenate.228 = bf16[1024,1024]{1,0:T(8,128)(2,1)S(1)} concatenate(bf16[8,1024]{1,0:T(8,128)(2,1)} %copy-done.71, bf16[8,1024]{1,0:T(8,128)(2,1)} %copy-done.70, bf16[4,1024]{1,0:T(4,128)(2,1)S(1)} %collective-permute-done.13, bf16[4,1024]{1,0:T(4,128)(2,1)} %copy-done.75, bf16[8,1024]{1,0:T(8,128)(2,1)} %copy-done.69, bf16[32,1024]{1,0:T(8,128)(2,1)} %copy-done.54, ...), dimensions={0} | concatenate | bytes 4194304 | tf_op jit(solution)/shard_map/concatenate | solution.py:45
  184.9 20.3 %concatenate.237 = bf16[8,258,1024]{2,0,1:T(8,128)(2,1)} concatenate(bf16[1,258,1024]{2,0,1:T(2,128)(2,1)S(1)} %copy.622, bf16[1,258,1024]{2,0,1:T(2,128)(2,1)} %copy.623, bf16[2,258,1024]{2,0,1:T(2,128)(2,1)} %collective-permute-done.34, bf16[1,258,1024]{2,0,1:T(2,128)(2,1)} %copy.624, bf16[1,258,1024]{2,0,1:T(2,128)(2,1)} %copy.625, ...), dimensions={0} | concatenate | bytes 8454144 | tf_op jit(solution)/shard_map/concatenate | solution.py:52
  213.9 9.1 %fusion.311 = (f32[2,2,1024]{2,1,0:T(2,128)S(1)}, f32[2,2,1024,1024]{2,3,1,0:T(8,128)}) fusion(bf16[2,1024,2,64]{1,3,2,0:T(8,128)(2,1)S(1)} %bitcast.490, bf16[2,1024,256]{1,2,0:T(8,128)(2,1)} %reshape.849, pred[2,1024,1024]{1,2,0:T(8,128)(4,1)} %compare_and_fusion), kind=kOutput, calls=%fused_computation.715 | convolution fusion | flops 549449728 | bytes 19677184 | tf_op jit(solution)/shard_map/mqrd,mkd->mrqk/dot_general | solution.py:161
  223.1 8.0 fusion.3
  231.1 8.8 %fusion.144 = bf16[2,64,2,1024]{3,1,2,0:T(8,128)(2,1)S(1)} fusion(f32[2,2,1024,1024]{2,3,1,0:T(8,128)} %get-tuple-element.360, f32[2,2,1024]{2,1,0:T(2,128)S(1)} %fusion.3, f32[2,2,1024]{2,1,0:T(2,128)S(1)} %get-tuple-element.359, bf16[2,1024,256]{1,2,0:T(8,128)(2,1)} %reshape.849), kind=kOutput, calls=%fused_computation.194 | convolution fusion | flops 549715968 | bytes 17596416 | tf_op jit(solution)/shard_map/mrqk,mkd->mqrd/dot_general | solution.py:161
  248.9 7.9 all-to-all-done.1
  283.8 5.7 collective-permute-done.53
  292.9 7.8 collective-permute-done.41
  314.8 38.7 %concatenate.238 = bf16[16,258,1024]{2,0,1:T(8,128)(2,1)} concatenate(bf16[1,258,1024]{2,0,1:T(2,128)(2,1)S(1)} %copy.622, bf16[1,258,1024]{2,0,1:T(2,128)(2,1)} %copy.623, bf16[2,258,1024]{2,0,1:T(2,128)(2,1)} %collective-permute-done.34, bf16[1,258,1024]{2,0,1:T(2,128)(2,1)} %copy.624, bf16[1,258,1024]{2,0,1:T(2,128)(2,1)} %copy.625, ...), dimensions={0} | concatenate | bytes 16908288 | tf_op jit(solution)/shard_map/concatenate | solution.py:45
  353.5 8.6 %slice.831 = bf16[16,256,1024]{2,0,1:T(8,128)(2,1)} slice(bf16[16,258,1024]{2,0,1:T(8,128)(2,1)} %concatenate.238), slice={[0:16], [0:256], [0:1024]} | slice | bytes 16777216 | tf_op jit(solution)/shard_map/slice | solution.py:232
  365.4 6.9 fusion.297
  378.5 6.1 fusion.64
  384.7 6.7 fusion.50
  458.6 6.1 fusion.43
  469.2 8.3 %bitcast_convert_fusion.1 = bf16[16,128,1024]{2,1,0:T(8,128)(2,1)} fusion(f32[2,16,48,1024]{3,2,0,1:T(8,128)} %fusion.102, bf16[2,1024,512]{2,1,0:T(8,128)(2,1)S(1)} %copy-done.28, bf16[16,2,48,512]{3,2,0,1:T(8,128)(2,1)} %get-tuple-element.171, s32[16,128,2]{1,2,0:T(2,128)S(1)} %copy.630), kind=kOutput, calls=%fused_computation.13 | convolution fusion | flops 2018705408 | bytes 14172160 | tf_op jit(solution)/shard_map/stej,sejd->std/dot_general | solution.py:161
  481.2 6.1 fusion.40
  492.9 5.9 fusion.104
  498.9 8.8 %bitcast_convert_fusion = bf16[16,128,1024]{2,1,0:T(8,128)(2,1)} fusion(f32[2,16,48,1024]{3,2,0,1:T(8,128)} %fusion.104, bf16[2,1024,512]{2,1,0:T(8,128)(2,1)} %all-gather.6.cloned.1.call-done, bf16[16,2,48,512]{3,2,0,1:T(8,128)(2,1)} %get-tuple-element.173, s32[16,128,2]{1,2,0:T(2,128)S(1)} %copy.640), kind=kOutput, calls=%fused_computation.12 | convolution fusion | flops 2018705408 | bytes 14172160 | tf_op jit(solution)/shard_map/stej,sejd->std/dot_general | solution.py:161
  555.0 6.9 collective-permute-done.49
  566.0 7.1 collective-permute-done.61
  574.5 10.6 %collective-permute-done.67 = bf16[2,136,1024]{2,1,0:T(8,128)(2,1)S(1)} collective-permute-done((bf16[2,136,1024]{2,1,0:T(8,128)(2,1)S(1)}, bf16[2,136,1024]{2,1,0:T(8,128)(2,1)S(1)}, u32[]{:S(2)}, u32[]{:S(2)}) %collective-permute-start.67) | collective-permute-done | bytes 557088 | tf_op jit(solution)/shard_map/ppermute | solution.py:79
  589.0 5.7 collective-permute-done.73
  596.8 6.5 collective-permute-done.74
  615.0 6.8 fusion.22
  628.5 10.9 %fusion = (f32[2,2,1024]{2,1,0:T(2,128)S(1)}, f32[2,1024,1024,2]{2,1,3,0:T(8,128)}) fusion(f32[2,2,1024,1024]{2,3,1,0:T(8,128)} %get-tuple-element.360, f32[2,2,1024]{2,1,0:T(2,128)S(1)} %copy-done.72, bf16[2,1024,2,64]{1,3,2,0:T(8,128)(2,1)S(1)} %reshape.862, bf16[2,1024,256]{1,2,0:T(8,128)(2,1)S(1)} %copy-done.31), kind=kOutput, calls=%fused_computation.2 | convolution fusion | flops 549449728 | bytes 34373632 | tf_op jit(solution)/shard_map/mqrd,mkd->mrqk/dot_general | solution.py:161
  639.4 8.5 %fusion.150 = bf16[2,1024,64]{1,2,0:T(8,128)(2,1)S(1)} fusion(bf16[2,1024,2,64]{1,3,2,0:T(8,128)(2,1)S(1)} %reshape.862, f32[2,2,1024,1024]{2,3,1,0:T(8,128)} %get-tuple-element.360, f32[2,2,1024]{2,1,0:T(2,128)S(1)} %copy-done.72), kind=kOutput, calls=%fused_computation.199 | convolution fusion | flops 545390592 | bytes 17580032 | tf_op jit(solution)/shard_map/mrqk,mqrd->mkd/dot_general | solution.py:161
  647.9 12.3 %fusion.2 = bf16[2,2,1024,1024]{2,3,1,0:T(8,128)(2,1)S(1)} fusion(f32[2,1024,1024,2]{2,1,3,0:T(8,128)} %get-tuple-element.379, f32[2,2,1024,1024]{2,3,1,0:T(8,128)} %get-tuple-element.360, f32[2,2,1024]{2,1,0:T(2,128)S(1)} %get-tuple-element.378, f32[2,2,1024]{2,1,0:T(2,128)S(1)} %copy-done.72), kind=kLoop, calls=%fused_computation.4 | loop fusion | flops 16777216 | bytes 41975808 | tf_op jit(solution)/shard_map/convert_element_type | solution.py:387
  667.4 5.6 all-to-all-start.3
  (804 shorter events, 496.2 us)
Async XLA Ops:
  7.2 371.3 %all-gather.4.cloned.1.call-start = ((), (), s32[]{:S(2)}) async-start(), calls=%async_computation.7 | async-start | bytes 2359296 | tf_op jit(solution)/shard_map/all_gather | solution.py:223
  7.9 376.7 %all-gather.6.cloned.1.call-start = ((), (), s32[]{:S(2)}) async-start(), calls=%async_computation.8 | async-start | bytes 2359296 | tf_op jit(solution)/shard_map/all_gather | solution.py:224
  8.7 382.7 %all-gather.8.cloned.1.call-start = ((), (), s32[]{:S(2)}) async-start(), calls=%async_computation.9 | async-start | bytes 2359296 | tf_op jit(solution)/shard_map/all_gather | solution.py:225
  13.4 70.6 %collective-permute-start.22 = (bf16[8,1024]{1,0:T(8,128)(2,1)}, bf16[8,1024]{1,0:T(8,128)(2,1)S(1)}, u32[]{:S(2)}, u32[]{:S(2)}) collective-permute-start(bf16[8,1024]{1,0:T(8,128)(2,1)} %param.21), channel_id=1, source_target_pairs={{0,16},{16,0},{32,48},{48,32},{64,80},{80,64},{96,112},{112,96},{1... | collective-permute-start | bytes 49160 | tf_op jit(solution)/shard_map/ppermute | solution.py:45
  64.1 52.3 %collective-permute-start.33 = (bf16[1,258,1024]{2,1,0:T(8,128)(2,1)S(1)}, bf16[1,258,1024]{2,1,0:T(8,128)(2,1)S(1)}, u32[]{:S(2)}, u32[]{:S(2)}) collective-permute-start(bf16[1,258,1024]{2,1,0:T(8,128)(2,1)S(1)} %maximum_bitcast_fusion.2), channel_id=1, source_target_pairs={{0,8},{1,9},{2,10},{3,11},{4,12},{5,13},{6,14},{7,15},{8,0},{9,1},... | collective-permute-start | bytes 1585160 | tf_op jit(solution)/shard_map/ppermute | solution.py:45
  84.0 48.3 %collective-permute-start.10 = (bf16[512,1152]{1,0:T(8,128)(2,1)}, bf16[512,1152]{1,0:T(8,128)(2,1)}, u32[]{:S(2)}, u32[]{:S(2)}) collective-permute-start(bf16[512,1152]{1,0:T(8,128)(2,1)} %get-tuple-element.250), channel_id=1, source_target_pairs={{0,1},{1,0},{2,3},{3,2},{4,5},{5,4},{6,7},{7,6},{8,9},{9,8},{10,11... | collective-permute-start | bytes 3538952 | tf_op jit(solution)/shard_map/ppermute | solution.py:45
  94.5 24.1 %collective-permute-start.21 = (bf16[512,1024]{1,0:T(8,128)(2,1)}, bf16[512,1024]{1,0:T(8,128)(2,1)}, u32[]{:S(2)}, u32[]{:S(2)}) collective-permute-start(bf16[512,1024]{1,0:T(8,128)(2,1)} %concatenate.227), channel_id=1, source_target_pairs={{0,1},{1,0},{2,3},{3,2},{4,5},{5,4},{6,7},{7,6},{8,9},{9,8},{10,11... | collective-permute-start | bytes 3145736 | tf_op jit(solution)/shard_map/ppermute | solution.py:45
  113.1 41.8 %collective-permute-start.29 = (bf16[128,1024]{1,0:T(8,128)(2,1)}, bf16[128,1024]{1,0:T(8,128)(2,1)}, u32[]{:S(2)}, u32[]{:S(2)}) collective-permute-start(bf16[128,1024]{1,0:T(8,128)(2,1)} %get-tuple-element.295), channel_id=1, source_target_pairs={{0,2},{1,3},{2,4},{3,5},{4,6},{5,7},{6,0},{7,1},{8,10},{9,11},{10,... | collective-permute-start | bytes 786440 | tf_op jit(solution)/shard_map/ppermute | solution.py:48
  113.1 51.7 %collective-permute-start.28 = (bf16[128,1024]{1,0:T(8,128)(2,1)}, bf16[128,1024]{1,0:T(8,128)(2,1)}, u32[]{:S(2)}, u32[]{:S(2)}) collective-permute-start(bf16[128,1024]{1,0:T(8,128)(2,1)} %get-tuple-element.295), channel_id=1, source_target_pairs={{0,6},{1,7},{2,0},{3,1},{4,2},{5,3},{6,4},{7,5},{8,14},{9,15},{10,... | collective-permute-start | bytes 786440 | tf_op jit(solution)/shard_map/ppermute | solution.py:49
  118.6 37.4 %collective-permute-start.35 = (bf16[2,258,1024]{2,0,1:T(2,128)(2,1)}, bf16[2,258,1024]{2,0,1:T(2,128)(2,1)S(1)}, u32[]{:S(2)}, u32[]{:S(2)}) collective-permute-start(bf16[2,258,1024]{2,0,1:T(2,128)(2,1)} %copy.614), channel_id=1, source_target_pairs={{0,2},{1,3},{2,4},{3,5},{4,6},{5,7},{6,0},{7,1},{8,10},{9,11},{10,... | collective-permute-start | bytes 3170312 | tf_op jit(solution)/shard_map/ppermute | solution.py:48
  118.6 38.8 %collective-permute-start.34 = (bf16[2,258,1024]{2,0,1:T(2,128)(2,1)}, bf16[2,258,1024]{2,0,1:T(2,128)(2,1)}, u32[]{:S(2)}, u32[]{:S(2)}) collective-permute-start(bf16[2,258,1024]{2,0,1:T(2,128)(2,1)} %copy.614), channel_id=1, source_target_pairs={{0,6},{1,7},{2,0},{3,1},{4,2},{5,3},{6,4},{7,5},{8,14},{9,15},{10,... | collective-permute-start | bytes 3170312 | tf_op jit(solution)/shard_map/ppermute | solution.py:49
  148.0 57.8 %all-to-all-start = ((bf16[8,256,256]{1,2,0:T(8,128)(2,1)}), bf16[8,256,256]{1,2,0:T(8,128)(2,1)}, u32[]{:S(2)}, u32[]{:S(2)}) async-start(bf16[8,256,256]{1,2,0:T(8,128)(2,1)} %maximum_bitcast_fusion), calls=%async_computation | async-start | bytes 2097152 | tf_op jit(solution)/shard_map/all_to_all | solution.py:263
  179.2 67.4 %collective-permute-start.32 = (bf16[512,1024]{1,0:T(8,128)(2,1)}, bf16[512,1024]{1,0:T(8,128)(2,1)}, u32[]{:S(2)}, u32[]{:S(2)}) collective-permute-start(bf16[512,1024]{1,0:T(8,128)(2,1)} %get-tuple-element.266), channel_id=1, source_target_pairs={{0,1},{1,0},{2,3},{3,2},{4,5},{5,4},{6,7},{7,6},{8,9},{9,8},{10,11... | collective-permute-start | bytes 3145736 | tf_op jit(solution)/shard_map/ppermute | solution.py:45
  205.2 109.6 %collective-permute-start.38 = (bf16[8,258,1024]{2,0,1:T(8,128)(2,1)}, bf16[8,258,1024]{2,0,1:T(8,128)(2,1)}, u32[]{:S(2)}, u32[]{:S(2)}) collective-permute-start(bf16[8,258,1024]{2,0,1:T(8,128)(2,1)} %concatenate.237), channel_id=1, source_target_pairs={{0,1},{1,0},{2,3},{3,2},{4,5},{5,4},{6,7},{7,6},{8,9},{9,8},{10,11... | collective-permute-start | bytes 12681224 | tf_op jit(solution)/shard_map/ppermute | solution.py:45
  246.4 432.9 %reduce-scatter.8.cloned.1.call-start = ((), (), s32[]{:S(2)}) async-start(), calls=%async_computation.12 | async-start | bytes 2359296 | tf_op jit(solution)/shard_map/reduce_scatter | solution.py:430
  276.8 23.9 %collective-permute-start.41 = (bf16[2,128,1024]{2,1,0:T(8,128)(2,1)S(1)}, bf16[2,128,1024]{2,1,0:T(8,128)(2,1)S(1)}, u32[]{:S(2)}, u32[]{:S(2)}) collective-permute-start(bf16[2,128,1024]{2,1,0:T(8,128)(2,1)S(1)} %pad_maximum_fusion.9), channel_id=1, source_target_pairs={{0,2},{1,3},{2,4},{3,5},{4,6},{5,7},{6,0},{7,1},{8,10},{9,11},{10,... | collective-permute-start | bytes 1572872 | tf_op jit(solution)/shard_map/ppermute | solution.py:48
  311.3 61.0 %collective-permute-start.44 = (bf16[8,128,1024]{2,1,0:T(8,128)(2,1)}, bf16[8,128,1024]{2,1,0:T(8,128)(2,1)}, u32[]{:S(2)}, u32[]{:S(2)}) collective-permute-start(bf16[8,128,1024]{2,1,0:T(8,128)(2,1)} %get-tuple-element.233), channel_id=1, source_target_pairs={{0,1},{1,0},{2,3},{3,2},{4,5},{5,4},{6,7},{7,6},{8,9},{9,8},{10,11... | collective-permute-start | bytes 6291464 | tf_op jit(solution)/shard_map/ppermute | solution.py:45
  314.2 90.9 %collective-permute-start.56 = (bf16[8,128,1024]{2,1,0:T(8,128)(2,1)}, bf16[8,128,1024]{2,1,0:T(8,128)(2,1)}, u32[]{:S(2)}, u32[]{:S(2)}) collective-permute-start(bf16[8,128,1024]{2,1,0:T(8,128)(2,1)} %get-tuple-element.243), channel_id=1, source_target_pairs={{0,1},{1,0},{2,3},{3,2},{4,5},{5,4},{6,7},{7,6},{8,9},{9,8},{10,11... | collective-permute-start | bytes 6291464 | tf_op jit(solution)/shard_map/ppermute | solution.py:45
  416.0 99.5 %collective-permute-start.45 = (bf16[8,128,1024]{2,1,0:T(8,128)(2,1)}, bf16[8,128,1024]{2,1,0:T(8,128)(2,1)}, u32[]{:S(2)}, u32[]{:S(2)}) collective-permute-start(bf16[8,128,1024]{2,1,0:T(8,128)(2,1)} %slice.806), channel_id=1, source_target_pairs={{0,1},{1,0},{2,3},{3,2},{4,5},{5,4},{6,7},{7,6},{8,9},{9,8},{10,11... | collective-permute-start | bytes 6291464 | tf_op jit(solution)/shard_map/ppermute | solution.py:69
  443.1 238.0 %reduce-scatter.4.cloned.1.call-start = ((), (), s32[]{:S(2)}) async-start(), calls=%async_computation.10 | async-start | bytes 2359296 | tf_op jit(solution)/shard_map/reduce_scatter | solution.py:430
  458.0 64.3 %collective-permute-start.57 = (bf16[8,128,1024]{2,1,0:T(8,128)(2,1)}, bf16[8,128,1024]{2,1,0:T(8,128)(2,1)}, u32[]{:S(2)}, u32[]{:S(2)}) collective-permute-start(bf16[8,128,1024]{2,1,0:T(8,128)(2,1)} %slice.821), channel_id=1, source_target_pairs={{0,1},{1,0},{2,3},{3,2},{4,5},{5,4},{6,7},{7,6},{8,9},{9,8},{10,11... | collective-permute-start | bytes 6291464 | tf_op jit(solution)/shard_map/ppermute | solution.py:69
  480.9 44.4 %collective-permute-start.63 = (bf16[8,136,1024]{2,1,0:T(8,128)(2,1)}, bf16[8,136,1024]{2,1,0:T(8,128)(2,1)}, u32[]{:S(2)}, u32[]{:S(2)}) collective-permute-start(bf16[8,136,1024]{2,1,0:T(8,128)(2,1)} %pad_maximum_fusion.1), channel_id=1, source_target_pairs={{0,1},{1,0},{2,3},{3,2},{4,5},{5,4},{6,7},{7,6},{8,9},{9,8},{10,11... | collective-permute-start | bytes 6684680 | tf_op jit(solution)/shard_map/ppermute | solution.py:69
  544.7 28.4 %collective-permute-start.61 = (bf16[2,128,1024]{2,1,0:T(8,128)(2,1)S(1)}, bf16[2,128,1024]{2,1,0:T(8,128)(2,1)S(1)}, u32[]{:S(2)}, u32[]{:S(2)}) collective-permute-start(bf16[2,128,1024]{2,1,0:T(8,128)(2,1)S(1)} %pad_maximum_fusion.14), channel_id=1, source_target_pairs={{0,6},{1,7},{2,0},{3,1},{4,2},{5,3},{6,4},{7,5},{8,14},{9,15},{10,... | collective-permute-start | bytes 1572872 | tf_op jit(solution)/shard_map/ppermute | solution.py:79
  548.7 24.4 %collective-permute-start.59 = (bf16[2,128,1024]{2,1,0:T(8,128)(2,1)S(1)}, bf16[2,128,1024]{2,1,0:T(8,128)(2,1)S(1)}, u32[]{:S(2)}, u32[]{:S(2)}) collective-permute-start(bf16[2,128,1024]{2,1,0:T(8,128)(2,1)S(1)} %pad_maximum_fusion.13), channel_id=1, source_target_pairs={{0,2},{1,3},{2,4},{3,5},{4,6},{5,7},{6,0},{7,1},{8,10},{9,11},{10,... | collective-permute-start | bytes 1572872 | tf_op jit(solution)/shard_map/ppermute | solution.py:78
  550.7 34.4 %collective-permute-start.67 = (bf16[2,136,1024]{2,1,0:T(8,128)(2,1)S(1)}, bf16[2,136,1024]{2,1,0:T(8,128)(2,1)S(1)}, u32[]{:S(2)}, u32[]{:S(2)}) collective-permute-start(bf16[2,136,1024]{2,1,0:T(8,128)(2,1)S(1)} %pad_maximum_fusion.5), channel_id=1, source_target_pairs={{0,6},{1,7},{2,0},{3,1},{4,2},{5,3},{6,4},{7,5},{8,14},{9,15},{10,... | collective-permute-start | bytes 1671176 | tf_op jit(solution)/shard_map/ppermute | solution.py:79
  561.9 24.2 %collective-permute-start.65 = (bf16[2,136,1024]{2,1,0:T(8,128)(2,1)S(1)}, bf16[2,136,1024]{2,1,0:T(8,128)(2,1)S(1)}, u32[]{:S(2)}, u32[]{:S(2)}) collective-permute-start(bf16[2,136,1024]{2,1,0:T(8,128)(2,1)S(1)} %pad_maximum_fusion.4), channel_id=1, source_target_pairs={{0,2},{1,3},{2,4},{3,5},{4,6},{5,7},{6,0},{7,1},{8,10},{9,11},{10,... | collective-permute-start | bytes 1671176 | tf_op jit(solution)/shard_map/ppermute | solution.py:78
  562.0 32.7 %collective-permute-start.73 = (bf16[2,136,1024]{2,1,0:T(8,128)(2,1)S(1)}, bf16[2,136,1024]{2,1,0:T(8,128)(2,1)S(1)}, u32[]{:S(2)}, u32[]{:S(2)}) collective-permute-start(bf16[2,136,1024]{2,1,0:T(8,128)(2,1)S(1)} %pad_maximum_fusion.7), channel_id=1, source_target_pairs={{0,6},{1,7},{2,0},{3,1},{4,2},{5,3},{6,4},{7,5},{8,14},{9,15},{10,... | collective-permute-start | bytes 1671176 | tf_op jit(solution)/shard_map/ppermute | solution.py:79
  573.1 23.2 %collective-permute-start.50 = (bf16[1,128,1024]{2,1,0:T(8,128)(2,1)S(1)}, bf16[1,128,1024]{2,1,0:T(8,128)(2,1)S(1)}, u32[]{:S(2)}, u32[]{:S(2)}) collective-permute-start(bf16[1,128,1024]{2,1,0:T(8,128)(2,1)S(1)} %slice.815), channel_id=1, source_target_pairs={{0,8},{1,9},{2,10},{3,11},{4,12},{5,13},{6,14},{7,15},{8,0},{9,1},... | collective-permute-start | bytes 786440 | tf_op jit(solution)/shard_map/ppermute | solution.py:69
  614.9 68.0 %reduce-scatter.6.cloned.1.call-start = ((), (), s32[]{:S(2)}) async-start(), calls=%async_computation.11 | async-start | bytes 2359296 | tf_op jit(solution)/shard_map/reduce_scatter | solution.py:430
  625.9 47.0 %collective-permute-start.97 = (bf16[512,1024]{1,0:T(8,128)(2,1)}, bf16[512,1024]{1,0:T(8,128)(2,1)}, u32[]{:S(2)}, u32[]{:S(2)}) collective-permute-start(bf16[512,1024]{1,0:T(8,128)(2,1)} %slice.911), channel_id=1, source_target_pairs={{0,1},{1,0},{2,3},{3,2},{4,5},{5,4},{6,7},{7,6},{8,9},{9,8},{10,11... | collective-permute-start | bytes 3145736 | tf_op jit(solution)/shard_map/ppermute | solution.py:69
  684.9 25.8 %collective-permute-start.101 = (bf16[128,1024]{1,0:T(8,128)(2,1)S(1)}, bf16[128,1024]{1,0:T(8,128)(2,1)}, u32[]{:S(2)}, u32[]{:S(2)}) collective-permute-start(bf16[128,1024]{1,0:T(8,128)(2,1)S(1)} %pad_maximum_fusion.25), channel_id=1, source_target_pairs={{0,6},{1,7},{2,0},{3,1},{4,2},{5,3},{6,4},{7,5},{8,14},{9,15},{10,... | collective-permute-start | bytes 786440 | tf_op jit(solution)/shard_map/ppermute | solution.py:79
  709.8 27.8 %collective-permute-start.86 = (bf16[512,1024]{1,0:T(8,128)(2,1)S(1)}, bf16[512,1024]{1,0:T(8,128)(2,1)S(1)}, u32[]{:S(2)}, u32[]{:S(2)}) collective-permute-start(bf16[512,1024]{1,0:T(8,128)(2,1)S(1)} %slice.889), channel_id=1, source_target_pairs={{0,1},{1,0},{2,3},{3,2},{4,5},{5,4},{6,7},{7,6},{8,9},{9,8},{10,11... | collective-permute-start | bytes 3145736 | tf_op jit(solution)/shard_map/ppermute | solution.py:69
  (207 other events, 2448.4 us)
Sparse Core Ops, SparseCore 0:
  9.7 69.7 all-gather.3
  81.1 57.4 all-gather.5
  140.2 62.6 all-gather.7
  443.2 49.5 reduce-scatter.7
  515.5 49.2 reduce-scatter.3
  621.9 53.3 reduce-scatter.5

commit v2 on v1

v2 whole, which is shorter than its diff:
```python
import jax
import jax.numpy as jnp
from jax import lax
from jax.experimental import pallas as pl
from jax.experimental.pallas import tpu as pltpu
from jax.sharding import PartitionSpec as P

BF = jnp.bfloat16
F32 = jnp.float32


H = 16
KV = 8
DH = 64
TOPK = 8
WINDOW = 1024
EPS = 1e-06
THETA = 10000.0
PATH_E = ("yh", "x", "core")
ALL = ("ctx", "fsdp")


def ctx_perm(dz, dyl):
    return [(z * 2 + y, ((z + dz) % 4) * 2 + (y + dyl) % 2) for z in range(4) for y in range(2)]


def fsdp_perm(dyh, dx, dcore):
    return [
        ((y * 4 + x) * 2 + c, (((y + dyh) % 2) * 4 + (x + dx) % 4) * 2 + (c + dcore) % 2)
        for y in range(2)
        for x in range(4)
        for c in range(2)
    ]


RING = {
    "z": ("ctx", ctx_perm(1, 0), ctx_perm(-1, 0)),
    "x": ("fsdp", fsdp_perm(0, 1, 0), fsdp_perm(0, -1, 0)),
}
PAIR = {
    "yl": ("ctx", ctx_perm(0, 1)),
    "yh": ("fsdp", fsdp_perm(1, 0, 0)),
    "core": ("fsdp", fsdp_perm(0, 0, 1)),
}


def gather_stage(block, name):
    if name in PAIR:
        axis, swap = PAIR[name]
        return jnp.concatenate([block, lax.ppermute(block, axis, swap)], axis=0)
    axis, up, down = RING[name]
    half = block.shape[0] // 2
    before = lax.ppermute(block, axis, up)
    after = lax.ppermute(block, axis, down)
    far_low = lax.ppermute(before[:half], axis, up)
    far_high = lax.ppermute(after[half:], axis, down)
    return jnp.concatenate([block, after, far_low, far_high, before], axis=0)


def gather_all(block, names):
    for name in names:
        block = gather_stage(block, name)
    return block


def add(a, b):
    return (a.astype(F32) + b.astype(F32)).astype(BF)


def scatter_stage(parts, name):
    if name in PAIR:
        axis, swap = PAIR[name]
        half = parts.shape[0] // 2
        return add(parts[:half], lax.ppermute(parts[half:], axis, swap))
    axis, up, down = RING[name]
    size = parts.shape[0] // 4
    half = size // 2
    own, after, far, before = (parts[k * size : (k + 1) * size] for k in range(4))
    low = lax.ppermute(far[:half], axis, up)
    high = lax.ppermute(far[half:], axis, down)
    after = jnp.concatenate([add(after[:half], low), after[half:]], axis=0)
    before = jnp.concatenate([before[:half], add(before[half:], high)], axis=0)
    from_before = lax.ppermute(after, axis, up)
    from_after = lax.ppermute(before, axis, down)
    return (own.astype(F32) + from_before.astype(F32) + from_after.astype(F32)).astype(BF)


def scatter_all(parts, names):
    for name in reversed(names):
        parts = scatter_stage(parts, name)
    return parts


SIZES = {"z": 4, "x": 4, "yl": 2, "yh": 2, "core": 2}


def coordinates():
    c = lax.axis_index("ctx")
    f = lax.axis_index("fsdp")
    return {"z": c // 2, "yl": c % 2, "yh": f // 8, "x": (f // 2) % 4, "core": f % 2}


def rms_scale(values, gain):
    return values * lax.rsqrt(jnp.mean(values * values, axis=-1, keepdims=True) + EPS) * gain


def rope_tables(positions):
    half = DH // 2
    inverse = THETA ** (-(jnp.arange(half, dtype=F32) * 2.0) / DH)
    angles = positions.astype(F32)[:, None] * inverse[None, :]
    return (jnp.cos(angles), jnp.sin(angles))


def head_post(raw, gain, cosine, sine, heads):
    shaped = raw.reshape(raw.shape[:-1] + (heads, DH))
    normed = rms_scale(shaped, gain)
    half = DH // 2
    first_half = normed[..., :half]
    second_half = normed[..., half:]
    cos_grid = cosine[:, None, :]
    sin_grid = sine[:, None, :]
    return jnp.concatenate(
        [
            first_half * cos_grid - second_half * sin_grid,
            second_half * cos_grid + first_half * sin_grid,
        ],
        axis=-1,
    )


def dot(a, b, ca, cb):
    return lax.dot_general(a, b, (((ca,), (cb,)), ((), ())), preferred_element_type=F32)


def halves(v):
    high = v.astype(BF)
    return high, (v - high.astype(F32)).astype(BF)


def expert_kernel(
    scalar_ref,
    x_ref,
    g_ref,
    router_ref,
    gate_ref,
    up_ref,
    down_ref,
    out_ref,
    back_ref,
    xe_ref,
    de_ref,
    act_ref,
    da_ref,
    db_ref,
    pick_ref,
    weight_ref,
    dgate_ref,
    eo_ref,
    dr_ref,
):
    sources, tok, width = x_ref.shape
    local, slots, hidden = act_ref.shape
    cap = slots // sources
    first = scalar_ref[0]
    lane = lax.broadcasted_iota(jnp.int32, (tok, 128), 1)
    place = lax.broadcasted_iota(jnp.int32, (tok, local * cap), 1)
    row_expert = lax.broadcasted_iota(jnp.int32, (local * cap, 128), 0) // cap
    slot_lane = lax.broadcasted_iota(jnp.int32, (local * cap, 128), 1)
    own_lane = slot_lane == first + row_expert

    def fetch(s, carry):
        x = x_ref[s]
        held = g_ref[s, :, width:].astype(F32)
        chosen = held >= 0.0
        logits = jnp.where(chosen, dot(x, router_ref[...], 1, 0), -1e30)
        top = jnp.max(logits, axis=1, keepdims=True)
        raised = jnp.where(chosen, jnp.exp(logits - top), 0.0)
        gates = raised / jnp.sum(raised, axis=1, keepdims=True)
        pick = jnp.zeros((tok, local * cap), F32)
        for e in range(local):
            mine = jnp.max(jnp.where(lane == first + e, held, -1.0), axis=1, keepdims=True)
            goal = jnp.where(mine >= 0.0, mine + e * cap, -1.0).astype(jnp.int32)
            pick = jnp.where(place == goal, 1.0, pick)
        pick = pick.astype(BF)
        pick_ref[s] = pick
        rows = pl.ds(pl.multiple_of(s * cap, 16), cap)
        x_slots = dot(pick, x, 0, 0).astype(BF)
        g_slots = dot(pick, g_ref[s, :, :width], 0, 0).astype(BF)
        high, low = halves(gates)
        weight = dot(pick, high, 0, 0) + dot(pick, low, 0, 0)
        weight = jnp.sum(jnp.where(own_lane, weight, 0.0), axis=1, keepdims=True)
        for e in range(local):
            part = slice(e * cap, (e + 1) * cap)
            xe_ref[e, rows] = x_slots[part]
            de_ref[e, rows] = g_slots[part]
            weight_ref[e, rows] = weight[part]
        return carry

    lax.fori_loop(0, sources, fetch, 0)
    chunk = 256

    def work(i, carry):
        e = i // (slots // chunk)
        rows = pl.ds(pl.multiple_of((i % (slots // chunk)) * chunk, chunk), chunk)
        w_gate = gate_ref[:, e].reshape(width, hidden)
        w_up = up_ref[:, e].reshape(width, hidden)
        w_down = down_ref[:, e].reshape(width, hidden)
        x = xe_ref[e, rows]
        a = dot(x, w_gate, 1, 0)
        b = dot(x, w_up, 1, 0)
        sig = 1.0 / (1.0 + jnp.exp(-a))
        silu = a * sig
        active = (silu * b).astype(BF)
        act_ref[e, rows] = active
        slope = b * (sig * (1.0 + a * (1.0 - sig)))
        weight = weight_ref[e, rows]
        g = de_ref[e, rows].astype(F32)
        result = dot(active, w_down, 1, 1).astype(BF).astype(F32)
        dgate_ref[e, rows] = jnp.sum(result * g, axis=1, keepdims=True)
        eo_ref[e, rows] = (weight * result).astype(BF)
        d_expert = (weight * g).astype(BF)
        de_ref[e, rows] = d_expert
        d_active = dot(d_expert, w_down, 1, 0)
        da = (d_active * slope).astype(BF)
        db = (d_active * silu).astype(BF)
        da_ref[e, rows] = da
        db_ref[e, rows] = db
        dr_ref[e, rows] = (dot(da, w_gate, 1, 1) + dot(db, w_up, 1, 1)).astype(BF)
        return carry

    lax.fori_loop(0, local * (slots // chunk), work, 0)

    def give(s, carry):
        rows = pl.ds(pl.multiple_of(s * cap, 16), cap)
        pick = pick_ref[s]
        eo = jnp.concatenate([eo_ref[e, rows] for e in range(local)], axis=0)
        dr = jnp.concatenate([dr_ref[e, rows] for e in range(local)], axis=0)
        dgate = jnp.concatenate([dgate_ref[e, rows] for e in range(local)], axis=0)
        high, low = halves(dgate)
        spread = jnp.where(own_lane, high.astype(F32), 0.0) + jnp.where(
            slot_lane == first + row_expert + 64, low.astype(F32), 0.0
        )
        out_ref[scalar_ref[s + 1]] = dot(pick, eo, 1, 0).astype(BF)
        back_ref[s, :, :width] = dot(pick, dr, 1, 0).astype(BF)
        back_ref[s, :, width:] = dot(pick, spread.astype(BF), 1, 0).astype(BF)
        return carry

    lax.fori_loop(0, sources, give, 0)


def run_experts(scalars, x_all, g_all, micro, router, w_gate, w_up, w_down, cap):
    sources, tok, width = x_all.shape
    local, hidden = w_gate.shape[1], w_gate.shape[3]
    slots = sources * cap
    wide = g_all.shape[2]
    shape = jax.ShapeDtypeStruct
    outs = [
        shape((sources, tok, width), BF),
        shape((sources, tok, wide), BF),
        shape((local, slots, width), BF),
        shape((local, slots, width), BF),
        shape((local, slots, hidden), BF),
        shape((local, slots, hidden), BF),
        shape((local, slots, hidden), BF),
    ]
    one = lambda s: pl.BlockSpec(s.shape, lambda i: (0,) * len(s.shape), pipeline_mode=pl.Buffered(1))
    flops = 2 * local * slots * width * hidden * 6
    return pl.pallas_call(
        expert_kernel,
        out_shape=outs,
        grid=(1,),
        in_specs=[
            pl.BlockSpec(memory_space=pltpu.SMEM),
            one(x_all),
            pl.BlockSpec((sources, tok, wide), lambda i: (0, micro, 0), pipeline_mode=pl.Buffered(1)),
            one(router),
            one(w_gate),
            one(w_up),
            one(w_down),
        ],
        out_specs=[one(o) for o in outs],
        scratch_shapes=[
            pltpu.VMEM((sources, tok, local * cap), BF),
            pltpu.VMEM((local, slots, 1), F32),
            pltpu.VMEM((local, slots, 1), F32),
            pltpu.VMEM((local, slots, width), BF),
            pltpu.VMEM((local, slots, width), BF),
        ],
        compiler_params=pltpu.CompilerParams(vmem_limit_bytes=56 * 1024 * 1024),
        cost_estimate=pl.CostEstimate(flops=flops, bytes_accessed=40 << 20, transcendentals=0),
    )(scalars, x_all, g_all, router, w_gate, w_up, w_down)


def mm(a, b):
    return jnp.dot(a, b, preferred_element_type=F32)


def mm_t(a, b):
    return lax.dot_general(a, b, (((1,), (1,)), ((), ())), preferred_element_type=F32)


def t_mm(a, b):
    return lax.dot_general(a, b, (((0,), (0,)), ((), ())), preferred_element_type=F32)


def ein(spec, a, b):
    return jnp.einsum(spec, a, b, preferred_element_type=F32)


def spread(block, axis, copies):
    wide = jnp.broadcast_to(block[None], (copies,) + block.shape)
    return lax.all_to_all(wide, axis, split_axis=0, concat_axis=0, tiled=True)


def swap(parts, axis):
    return lax.all_to_all(parts, axis, split_axis=0, concat_axis=0, tiled=True)


def body(
    tokens,
    segments,
    routes,
    w_query,
    w_key,
    w_value,
    w_out,
    w_router,
    attn_gain,
    mlp_gain,
    qk_gain,
    w_gate,
    w_up,
    w_down,
    cotangent,
):
    micro = tokens.shape[0]
    tok = tokens.shape[2]
    width = tokens.shape[3]
    length = segments.shape[2]
    rows = w_query.shape[0]
    n_ctx = lax.axis_size("ctx")
    n_fsdp = lax.axis_size("fsdp")
    n_all = n_ctx * n_fsdp
    shard = lax.axis_index("fsdp")
    local = w_gate.shape[0]
    experts = local * n_fsdp
    cap = (3 * tok * TOPK + 2 * experts - 1) // (2 * experts)
    all_tok = micro * tok
    scale = DH ** (-0.5)
    ratio = H // KV
    heads = ratio * DH

    small = jnp.concatenate(
        [
            w_router,
            attn_gain[:, None],
            mlp_gain[:, None],
            jnp.pad(qk_gain[:, None], ((0, rows - 1), (0, 0))),
        ],
        axis=1,
    )
    small = jnp.pad(small, ((0, 0), (0, 128 - small.shape[1])))
    pieces = jnp.concatenate(
        [
            w_query.reshape(rows, n_ctx, heads),
            w_key.reshape(rows, n_ctx, DH),
            w_value.reshape(rows, n_ctx, DH),
            jnp.broadcast_to(small[:, None], (rows, n_ctx, 128)),
        ],
        axis=2,
    ).transpose(1, 0, 2)
    pieces = jnp.broadcast_to(pieces[:, None], (n_ctx, n_fsdp) + pieces.shape[1:])
    head_all = swap(pieces.reshape((n_all,) + pieces.shape[2:]), ALL).reshape(width, -1)
    w_heads = head_all[:, : heads + 2 * DH]
    small_all = head_all[:, heads + 2 * DH :]
    router = small_all[:, :experts]
    small_wide = small_all.astype(F32)
    gain_attn = small_wide[:, experts]
    gain_mlp = small_wide[:, experts + 1]
    gain_heads = small_wide[:, experts + 2].reshape(-1, rows)[:, 0]

    seq_rows = [
        spread(tokens[m, 0], "ctx", n_ctx).reshape(length, width) for m in range(micro)
    ]
    out_full = spread(w_out, ALL, n_all).reshape(width, width)

    weight_gate = lax.all_gather(w_gate, "ctx", axis=0)
    weight_up = lax.all_gather(w_up, "ctx", axis=0)
    weight_down = lax.all_gather(w_down, "ctx", axis=0)

    expert_ids = jnp.arange(experts, dtype=jnp.int32)
    cot = cotangent.reshape(all_tok, width)
    chosen = jnp.any(routes.reshape(all_tok, TOPK)[:, :, None] == expert_ids, axis=1)
    before = jnp.arange(tok, dtype=jnp.int32)
    lower = (before[:, None] >= before[None, :]).astype(BF)
    counts = ein("ut,mte->mue", lower, chosen.reshape(micro, tok, experts).astype(BF))
    held = jnp.where(chosen, counts.reshape(all_tok, experts) - 1.0, -1.0)
    held = jnp.pad(held, ((0, 0), (0, 128 - experts)), constant_values=-1.0).astype(BF)
    pack_all = gather_all(jnp.concatenate([cot, held], axis=1)[None], PATH_E)

    positions = jnp.arange(length, dtype=jnp.int32)
    cosine, sine = rope_tables(positions)
    near = jnp.abs(positions[:, None] - positions[None, :]) < WINDOW // 2

    def attend(m):
        normed, back = jax.vjp(rms_scale, seq_rows[m].astype(F32), gain_attn)
        hidden = normed.astype(BF)
        raw = mm(hidden, w_heads)
        query_rot, query_back = jax.vjp(
            lambda r, g: head_post(r, g, cosine, sine, ratio), raw[:, :heads], gain_heads[:DH]
        )
        key_rot, key_back = jax.vjp(
            lambda r, g: head_post(r, g, cosine, sine, 1),
            raw[:, heads : heads + DH],
            gain_heads[DH:],
        )
        q = query_rot.astype(BF)
        k = key_rot.astype(BF)[:, 0]
        v = raw[:, heads + DH :].astype(BF)
        seg = segments[m, 0]
        allowed = (seg[:, None] == seg[None, :]) & near

        def scores_of():
            return jnp.where(allowed[None], ein("qrd,kd->rqk", q, k) * scale, -1e30)

        scores = scores_of()
        highest = jnp.max(scores, axis=-1, keepdims=True)
        shifted = jnp.exp(scores - highest)
        total = jnp.sum(shifted, axis=-1, keepdims=True)
        log_total = highest + jnp.log(total)
        probs_low = (shifted / total).astype(BF)
        mixed = ein("rqk,kd->qrd", probs_low, v).astype(BF).reshape(length, heads)

        def backward(d_mixed):
            d_mixed = d_mixed.reshape(length, ratio, DH)
            probs = jnp.exp(scores_of() - log_total)
            d_probs = ein("qrd,kd->rqk", d_mixed, v)
            d_scores = (
                probs * (d_probs - jnp.sum(probs * d_probs, axis=-1, keepdims=True))
            ).astype(BF)
            d_q = ein("rqk,kd->qrd", d_scores, k) * scale
            d_k = ein("rqk,qrd->kd", d_scores, q) * scale
            d_v = ein("rqk,qrd->kd", probs.astype(BF), d_mixed)
            d_q_raw, d_q_gain = query_back(d_q)
            d_k_raw, d_k_gain = key_back(d_k[:, None])
            d_raw = jnp.concatenate([d_q_raw, d_k_raw, d_v], axis=1).astype(BF)
            grad_heads = t_mm(hidden, d_raw)
            d_hidden = mm_t(d_raw, w_heads)
            wide = seq_rows[m].astype(F32)
            inverse = lax.rsqrt(jnp.mean(wide * wide, axis=-1, keepdims=True) + EPS)
            grad_gain = jnp.sum(d_hidden * wide * inverse, axis=0)
            return (
                d_hidden.astype(BF),
                grad_heads,
                grad_gain,
                jnp.concatenate([d_q_gain, d_k_gain]),
            )

        return mixed, backward

    def to_owner(v):
        return swap(v.reshape(n_ctx, tok, -1), "ctx")

    router_pad = jnp.pad(router, ((0, 0), (0, 128 - experts)))
    first = jnp.full((1,), shard * local, jnp.int32)
    here = coordinates()
    rel = jnp.arange(n_fsdp, dtype=jnp.int32)
    digits = {}
    rest = rel
    for name in PATH_E:
        digits[name] = (rest % SIZES[name] + here[name]) % SIZES[name]
        rest = rest // SIZES[name]
    whole = (digits["yh"] * 4 + digits["x"]) * 2 + digits["core"]
    scalars = jnp.concatenate([first, whole])

    outs, d_inputs = [], []
    backs, kept, grads = [], [], []
    forward = []
    for m in range(micro):
        mixed_h, backward = attend(m)
        backs.append(backward)
        mixed = to_owner(mixed_h).transpose(1, 0, 2).reshape(tok, width)
        start = tokens[m, 0].astype(F32)
        middle = start + mm(mixed, out_full)
        normed, norm_back = jax.vjp(rms_scale, middle, gain_mlp)
        hidden_two = normed.astype(BF)
        chosen_m = chosen[m * tok : (m + 1) * tok]
        logits = jnp.where(chosen_m, mm(hidden_two, router), -1e30)
        gates = jnp.where(chosen_m, jax.nn.softmax(logits, axis=-1), 0.0)
        x_all = gather_all(hidden_two[None], PATH_E)
        forward.append((mixed, middle, norm_back, hidden_two, gates, x_all))
    expert_parts = []
    for m in range(micro):
        mixed, middle, norm_back, hidden_two, gates, x_all = forward[m]
        moe_part, back_part, *saved = run_experts(
            scalars, x_all, pack_all, m, router_pad, weight_gate, weight_up, weight_down, cap
        )
        kept.append(saved)
        back = scatter_all(back_part, PATH_E)[0]
        moe = lax.psum_scatter(moe_part, "fsdp", scatter_dimension=0, tiled=True)[0]
        outs.append((middle + moe.astype(F32)).astype(BF))
        grad_top = cot[m * tok : (m + 1) * tok].astype(F32)
        tail = back[:, width:].astype(F32)
        d_gates = tail[:, :experts] + tail[:, 64 : 64 + experts]
        d_select = gates * (d_gates - jnp.sum(gates * d_gates, axis=-1, keepdims=True))
        d_logits = d_select.astype(BF)
        grad_router = t_mm(hidden_two, d_logits)
        d_two = back[:, :width].astype(F32) + mm_t(d_logits, router)
        d_middle, grad_mlp = norm_back(d_two)
        d_middle = d_middle + grad_top
        d_branch = d_middle.astype(BF)
        grad_out = t_mm(mixed, d_branch)
        d_mixed = mm_t(d_branch, out_full).astype(BF)
        d_mixed = d_mixed.reshape(tok, n_ctx, heads).transpose(1, 0, 2)
        d_mixed = swap(d_mixed, "ctx").reshape(length, heads)
        d_hidden, grad_heads, grad_attn, grad_qk = backs[m](d_mixed)
        d_hidden = jnp.sum(to_owner(d_hidden).astype(F32), axis=0)
        start = tokens[m, 0].astype(F32)
        inverse = lax.rsqrt(jnp.mean(start * start, axis=-1, keepdims=True) + EPS)
        u = d_hidden * gain_attn
        d_inputs.append(
            d_middle
            + inverse * u
            - start * (inverse**3 * jnp.mean(u * start, axis=-1, keepdims=True))
        )
        grads.append((grad_out, grad_heads, grad_router, grad_attn, grad_mlp, grad_qk))
    grad_out, grad_heads, grad_router, grad_attn, grad_mlp, grad_qk = jax.tree.map(
        jnp.add, grads[0], grads[1]
    )

    grad_out = swap(grad_out.astype(BF).reshape(n_all, rows, width), ALL)
    own_out = jnp.sum(grad_out.astype(F32), axis=0)
    grad_qk = jnp.pad(grad_qk[:, None], ((0, 0), (0, rows - 1))).reshape(-1)
    grad_small = jnp.concatenate(
        [grad_router, grad_attn[:, None], grad_mlp[:, None], grad_qk[:, None]], axis=1
    )
    grad_small = jnp.pad(grad_small, ((0, 0), (0, 128 - grad_small.shape[1])))
    grad_pack = jnp.concatenate([grad_heads, grad_small], axis=1).astype(BF)
    grad_pack = swap(grad_pack.reshape(n_all, rows, -1), ALL).astype(F32)
    own_heads = jnp.sum(grad_pack[:, :, : heads + 2 * DH].reshape(n_ctx, n_fsdp, rows, -1), axis=1)
    own_heads = own_heads.transpose(1, 0, 2)
    own_small = jnp.sum(grad_pack[:, :, heads + 2 * DH :], axis=0)

    def expert_grad(left, right):
        total = None
        for m in range(micro):
            part = ein("ejd,ejf->edf", kept[m][left], kept[m][right])
            total = part if total is None else total + part
        parts = total.astype(BF).reshape(local, n_ctx, -1, total.shape[2]).transpose(1, 0, 2, 3)
        return jnp.sum(swap(parts, "ctx").astype(F32), axis=0)

    return (
        jnp.stack(outs)[:, None],
        jnp.stack(d_inputs)[:, None],
        own_heads[:, :, :heads].reshape(rows, -1),
        own_heads[:, :, heads : heads + DH].reshape(rows, -1),
        own_heads[:, :, heads + DH :].reshape(rows, -1),
        own_out,
        own_small[:, :experts],
        own_small[:, experts],
        own_small[:, experts + 1],
        own_small[:1, experts + 2],
        expert_grad(0, 3),
        expert_grad(0, 4),
        expert_grad(1, 2),
    )


def solution(mesh):
    weight = P(("ctx", "fsdp"), None)
    gain = P(("ctx", "fsdp"))
    rows = P(None, "fsdp", "ctx", None)
    expert = P("fsdp", "ctx", None)
    return jax.shard_map(
        body,
        mesh=mesh,
        in_specs=(rows, P(None, "fsdp", None), rows)
        + (weight,) * 5
        + (gain,) * 3
        + (expert,) * 3
        + (rows,),
        out_specs=(rows, rows) + (weight,) * 5 + (gain,) * 3 + (expert,) * 3,
        check_vma=False,
    )
```

time: 822 us -> 793 us (0.965)
  waiting for transfers between devices: 144 us -> 274 us
  matrix products: 187 us -> 74.2 us
  local copies, waits for them, and re-layouts: 204 us -> 92.7 us
  Pallas kernels: 0 us -> 79.8 us
  starting transfers between devices: 175 us -> 116 us
  blocking collectives: 0 us -> 54.6 us
    all_to_all x4 -> x13, waiting for transfers between devices: 9.7 us -> 117 us  [the longest x10 75.2 us: swap(): return lax.all_to_all(parts, axis, split_axis=0, concat_axis=0, tiled=True)]
    dot_general x32 -> x19, matrix products: 149 us -> 49.1 us  [ein(): return jnp.einsum(spec, a, b, preferred_element_type=F32)]
    pallas_call x0 -> x2, Pallas kernels: none -> 79.8 us  [run_experts(): pl.pallas_call(expert_kernel, out_shape=outs, grid=(1,), in_specs=[pl.Blo...]
    all_to_all x0 -> x2, blocking collectives: none -> 54.6 us  [swap(): return lax.all_to_all(parts, axis, split_axis=0, concat_axis=0, tiled=True)]
    concatenate x9 -> x3, local copies, waits for them, and re-layouts: 62.9 us -> 9.5 us  [gather_stage(): return jnp.concatenate([block, lax.ppermute(block, axis, swap)], axis=0)]
    ppermute x15 -> x6, waiting for transfers between devices: 23.8 us -> 74.7 us  [gather_stage(): return jnp.concatenate([block, lax.ppermute(block, axis, swap)], axis=0)]
    all_to_all x4 -> x13, starting transfers between devices: 18.6 us -> 68.4 us  [the longest x10 53 us: swap(): return lax.all_to_all(parts, axis, split_axis=0, concat_axis=0, tiled=True)]
    ppermute x10 -> x2, starting transfers between devices: 34.2 us -> 6.08 us  [scatter_stage(): high = lax.ppermute(far[half:], axis, down)]
  transfers between devices with their start and end apart: 118 -> 48, of which waited for: 35 -> 28; matrix products, arithmetic and copies ran while one was open for 55% -> 28% of each run, Pallas kernels for 0% -> 5%
where the time goes in v2:
time: 793 us; the launch traced here: 784 us
  waiting for transfers between devices  274 us (35%)
  starting transfers between devices  116 us (15%)
  local copies, waits for them, and re-layouts  92.7 us (12%)
  Pallas kernels  79.8 us (10%)
  other arithmetic  75.9 us (10%)
  matrix products  74.2 us (9%)
  blocking collectives  54.6 us (7%)
  between operations  17.5 us (2%)
    pallas_call x2, Pallas kernels, run_experts(): pl.pallas_call(expert_kernel, out_shape=outs, grid=(1,), in_specs=[pl.Blo...  79.8 us
    all_to_all x10, waiting for transfers between devices, swap(): return lax.all_to_all(parts, axis, split_axis=0, concat_axis=0, tiled=True)  75.2 us
    ppermute x6, waiting for transfers between devices, gather_stage(): return jnp.concatenate([block, lax.ppermute(block, axis, swap)], axis=0)  74.7 us
    all_to_all x2, blocking collectives, swap(): return lax.all_to_all(parts, axis, split_axis=0, concat_axis=0, tiled=True)  54.6 us
    all_to_all x10, starting transfers between devices, swap(): return lax.all_to_all(parts, axis, split_axis=0, concat_axis=0, tiled=True)  53 us
    dot_general x19, matrix products, ein(): return jnp.einsum(spec, a, b, preferred_element_type=F32)  49.1 us
    all_to_all x3, waiting for transfers between devices, spread(): return lax.all_to_all(wide, axis, split_axis=0, concat_axis=0, tiled=True)  41.8 us
    ppermute x3, waiting for transfers between devices, gather_stage(): before = lax.ppermute(block, axis, up)  36.2 us
  transfers between devices with their start and end apart: 48, of which 28 were waited for; matrix products, arithmetic and copies ran while one was open for 28% of the time, Pallas kernels for 5%

profile of v2, /device:TPU:0, one launch (start us, length us, event | category | flops | bytes accessed | tf_op | source)
XLA Modules:
  0.0 784.5 jit_solution(5950763530393905427)
XLA Ops:
  14.2 11.1 %all-to-all-start.1 = ((bf16[128,8,384]{2,1,0:T(8,128)(2,1)}), bf16[128,8,384]{2,1,0:T(8,128)(2,1)S(1)}, u32[]{:S(2)}, u32[]{:S(2)}) async-start(bf16[128,8,384]{2,1,0:T(8,128)(2,1)} %bitcast.8), calls=%async_computation.1 | async-start | bytes 1572864 | tf_op jit(solution)/shard_map/all_to_all | solution.py:316
  28.9 12.7 %all-to-all-done.1 = bf16[128,8,384]{2,1,0:T(8,128)(2,1)S(1)} async-done(((bf16[128,8,384]{2,1,0:T(8,128)(2,1)}), bf16[128,8,384]{2,1,0:T(8,128)(2,1)S(1)}, u32[]{:S(2)}, u32[]{:S(2)}) %all-to-all-start.1) | async-done | bytes 786464 | tf_op jit(solution)/shard_map/all_to_all | solution.py:316
  53.1 54.0 %collective-permute-done.6 = bf16[1,256,1152]{2,1,0:T(8,128)(2,1)} collective-permute-done((bf16[1,256,1152]{2,1,0:T(8,128)(2,1)}, bf16[1,256,1152]{2,1,0:T(8,128)(2,1)}, u32[]{:S(2)}, u32[]{:S(2)}) %collective-permute-start.6) | collective-permute-done | bytes 589856 | tf_op jit(solution)/shard_map/ppermute | solution.py:50
  125.0 16.3 %collective-permute-done.8 = bf16[2,256,1152]{2,1,0:T(8,128)(2,1)} collective-permute-done((bf16[2,256,1152]{2,1,0:T(8,128)(2,1)}, bf16[2,256,1152]{2,1,0:T(8,128)(2,1)}, u32[]{:S(2)}, u32[]{:S(2)}) %collective-permute-start.8) | collective-permute-done | bytes 1179680 | tf_op jit(solution)/shard_map/ppermute | solution.py:53
  149.4 20.4 %all-to-all-done.4 = bf16[8,128,1024]{2,1,0:T(8,128)(2,1)} async-done(((bf16[8,128,1024]{2,1,0:T(8,128)(2,1)}), bf16[8,128,1024]{2,1,0:T(8,128)(2,1)}, u32[]{:S(2)}, u32[]{:S(2)}) %all-to-all-start.4) | async-done | bytes 2097184 | tf_op jit(solution)/shard_map/all_to_all | solution.py:312
  199.0 7.2 all-to-all-start.3
  215.2 21.4 %all-to-all-done.3 = bf16[128,8,1024]{2,1,0:T(8,128)(2,1)S(1)} async-done(((bf16[128,8,1024]{2,1,0:T(8,128)(2,1)}), bf16[128,8,1024]{2,1,0:T(8,128)(2,1)S(1)}, u32[]{:S(2)}, u32[]{:S(2)}) %all-to-all-start.3) | async-done | bytes 2097184 | tf_op jit(solution)/shard_map/all_to_all | solution.py:312
  254.8 9.5 %collective-permute-done.12 = bf16[1,128,1024]{2,1,0:T(8,128)(2,1)S(1)} collective-permute-done((bf16[1,128,1024]{2,1,0:T(8,128)(2,1)S(1)}, bf16[1,128,1024]{2,1,0:T(8,128)(2,1)S(1)}, u32[]{:S(2)}, u32[]{:S(2)}) %collective-permute-start.12) | collective-permute-done | bytes 262176 | tf_op jit(solution)/shard_map/ppermute | solution.py:50
  269.9 11.0 %collective-permute-done.14 = bf16[2,128,1024]{2,1,0:T(8,128)(2,1)} collective-permute-done((bf16[2,128,1024]{2,1,0:T(8,128)(2,1)}, bf16[2,128,1024]{2,1,0:T(8,128)(2,1)}, u32[]{:S(2)}, u32[]{:S(2)}) %collective-permute-start.14) | collective-permute-done | bytes 524320 | tf_op jit(solution)/shard_map/ppermute | solution.py:53
  303.2 5.0 constant_dynamic-update-slice_fusion.19.g_ref
  308.2 11.1 %all-gather.11.cloned.1.call-done = bf16[16,128,512]{2,1,0:T(8,128)(2,1)} async-done(((bf16[2,128,512]{2,1,0:T(8,128)(2,1)}), bf16[16,128,512]{2,1,0:T(8,128)(2,1)}) %all-gather.11.cloned.1.call-update) | async-done | bytes 2097168 | tf_op jit(solution)/shard_map/all_gather | solution.py:389
  319.2 39.6 %shard_map.247 = (bf16[16,128,1024]{2,1,0:T(8,128)(2,1)}, bf16[16,128,1152]{2,1,0:T(8,128)(2,1)}, bf16[2,768,1024]{2,1,0:T(8,128)(2,1)}, bf16[2,768,1024]{2,1,0:...) custom-call(s32[17]{0:T(128)} %pad_add_fusion.4.scalar_ref, ...), custom_call_target="tpu_custom_call" | custom-call | flops 9663676416 | bytes 41943040 | tf_op jit(solution)/shard_map/pallas_call | solution.py:268
  361.7 6.8 collective-permute-done
  374.5 8.8 %collective-permute-done.2 = bf16[2,128,1024]{2,1,0:T(8,128)(2,1)S(1)} collective-permute-done((bf16[2,128,1024]{2,1,0:T(8,128)(2,1)S(1)}, bf16[2,128,1024]{2,1,0:T(8,128)(2,1)S(1)}, u32[]{:S(2)}, u32[]{:S(2)}) %collective-permute-start.2) | collective-permute-done | bytes 524320 | tf_op jit(solution)/shard_map/ppermute | solution.py:53
  399.8 40.2 %shard_map.246 = (bf16[16,128,1024]{2,1,0:T(8,128)(2,1)}, bf16[16,128,1152]{2,1,0:T(8,128)(2,1)}, bf16[2,768,1024]{2,1,0:T(8,128)(2,1)}, bf16[2,768,1024]{2,1,0:...) custom-call(s32[17]{0:T(128)} %pad_add_fusion.4.scalar_ref, ...), custom_call_target="tpu_custom_call" | custom-call | flops 9663676416 | bytes 41943040 | tf_op jit(solution)/shard_map/pallas_call | solution.py:268
  491.0 8.4 %collective-permute-done.22 = bf16[2,128,1152]{2,1,0:T(8,128)(2,1)S(1)} collective-permute-done((bf16[2,128,1152]{2,1,0:T(8,128)(2,1)S(1)}, bf16[2,128,1152]{2,1,0:T(8,128)(2,1)S(1)}, u32[]{:S(2)}, u32[]{:S(2)}) %collective-permute-start.22) | collective-permute-done | bytes 589856 | tf_op jit(solution)/shard_map/ppermute | solution.py:84
  502.1 4.9 collective-permute-start.23
  507.0 6.1 collective-permute-done.28
  517.0 9.1 %collective-permute-done.29 = bf16[1,128,1152]{2,1,0:T(8,128)(2,1)S(1)} collective-permute-done((bf16[1,128,1152]{2,1,0:T(8,128)(2,1)S(1)}, bf16[1,128,1152]{2,1,0:T(8,128)(2,1)S(1)}, u32[]{:S(2)}, u32[]{:S(2)}) %collective-permute-start.29) | collective-permute-done | bytes 294944 | tf_op jit(solution)/shard_map/ppermute | solution.py:74
  552.4 5.1 fusion.3
  565.6 5.7 all-to-all-start.12
  571.6 5.2 fusion
  596.3 6.0 all-to-all-start.13
  607.5 5.5 fusion.75
  613.0 4.9 fusion.72
  617.9 8.0 %all-to-all-done.13 = bf16[8,2,128,512]{3,2,1,0:T(8,128)(2,1)} async-done(((bf16[8,2,128,512]{3,2,1,0:T(8,128)(2,1)}), bf16[8,2,128,512]{3,2,1,0:T(8,128)(2,1)}, u32[]{:S(2)}, u32[]{:S(2)}) %all-to-all-start.13) | async-done | bytes 2097184 | tf_op jit(solution)/shard_map/all_to_all | solution.py:316
  642.1 11.8 %all-to-all-done.14 = bf16[8,2,128,512]{3,2,1,0:T(8,128)(2,1)} async-done(((bf16[8,2,128,512]{3,2,1,0:T(8,128)(2,1)}), bf16[8,2,128,512]{3,2,1,0:T(8,128)(2,1)}, u32[]{:S(2)}, u32[]{:S(2)}) %all-to-all-start.14) | async-done | bytes 2097184 | tf_op jit(solution)/shard_map/all_to_all | solution.py:316
  653.9 24.3 %all_to_all.75 = bf16[128,8,384]{2,1,0:T(8,128)(2,1)} all-to-all(bf16[128,8,384]{2,1,0:T(8,128)(2,1)S(1)} %pad_maximum_fusion.1), channel_id=1, replica_groups=mesh['ctx'=8,'fsdp'=16] {'ctx','fsdp'}, dimensions={0} | all-to-all | bytes 1572864 | tf_op jit(solution)/shard_map/all_to_all | solution.py:316
  678.2 30.3 %all_to_all.76 = bf16[8,128,1024]{2,1,0:T(8,128)(2,1)S(1)} all-to-all(bf16[8,128,1024]{2,1,0:T(8,128)(2,1)} %bitcast.413), channel_id=1, replica_groups=mesh['ctx'=8,'fsdp'=16] {'ctx'}, dimensions={0} | all-to-all | bytes 4194304 | tf_op jit(solution)/shard_map/all_to_all | solution.py:316
  726.2 12.5 %all-to-all-done.9 = bf16[8,128,1024]{2,1,0:T(8,128)(2,1)} async-done(((bf16[8,128,1024]{2,1,0:T(8,128)(2,1)}), bf16[8,128,1024]{2,1,0:T(8,128)(2,1)}, u32[]{:S(2)}, u32[]{:S(2)}) %all-to-all-start.9) | async-done | bytes 2097184 | tf_op jit(solution)/shard_map/all_to_all | solution.py:316
  738.7 6.3 all-to-all-start.11
  753.8 21.2 %all-to-all-done.11 = bf16[128,8,1024]{2,1,0:T(8,128)(2,1)} async-done(((bf16[128,8,1024]{2,1,0:T(8,128)(2,1)}), bf16[128,8,1024]{2,1,0:T(8,128)(2,1)}, u32[]{:S(2)}, u32[]{:S(2)}) %all-to-all-start.11) | async-done | bytes 2097184 | tf_op jit(solution)/shard_map/all_to_all | solution.py:316
  (596 shorter events, 316.4 us)
Async XLA Ops:
  7.2 301.0 %all-gather.7.cloned.1.call-start = ((), (), s32[]{:S(2)}) async-start(), calls=%async_computation.19 | async-start | bytes 2359296 | tf_op jit(solution)/shard_map/all_gather | solution.py:387
  14.2 27.5 %all-to-all-start.1 = ((bf16[128,8,384]{2,1,0:T(8,128)(2,1)}), bf16[128,8,384]{2,1,0:T(8,128)(2,1)S(1)}, u32[]{:S(2)}, u32[]{:S(2)}) async-start(bf16[128,8,384]{2,1,0:T(8,128)(2,1)} %bitcast.8), calls=%async_computation.1 | async-start | bytes 1572864 | tf_op jit(solution)/shard_map/all_to_all | solution.py:316
  43.4 68.9 %all-to-all-start = ((bf16[8,128,1024]{2,1,0:T(8,128)(2,1)}), bf16[8,128,1024]{2,1,0:T(8,128)(2,1)S(1)}, u32[]{:S(2)}, u32[]{:S(2)}) async-start(bf16[8,128,1024]{2,1,0:T(8,128)(2,1)} %broadcast_in_dim.81), calls=%async_computation | async-start | bytes 4194304 | tf_op jit(solution)/shard_map/all_to_all | solution.py:312
  47.1 261.0 %all-gather.9.cloned.1.call-start = ((), (), s32[]{:S(2)}) async-start(), calls=%async_computation.20 | async-start | bytes 2359296 | tf_op jit(solution)/shard_map/all_gather | solution.py:388
  48.9 58.3 %collective-permute-start.6 = (bf16[1,256,1152]{2,1,0:T(8,128)(2,1)}, bf16[1,256,1152]{2,1,0:T(8,128)(2,1)}, u32[]{:S(2)}, u32[]{:S(2)}) collective-permute-start(bf16[1,256,1152]{2,1,0:T(8,128)(2,1)} %fusion.81), channel_id=1, source_target_pairs={{0,8},{1,9},{2,10},{3,11},{4,12},{5,13},{6,14},{7,15},{8,0},{9,1},... | collective-permute-start | bytes 1769480 | tf_op jit(solution)/shard_map/ppermute | solution.py:50
  109.6 33.7 %collective-permute-start.7 = (bf16[2,256,1152]{2,1,0:T(8,128)(2,1)}, bf16[2,256,1152]{2,1,0:T(8,128)(2,1)}, u32[]{:S(2)}, u32[]{:S(2)}) collective-permute-start(bf16[2,256,1152]{2,1,0:T(8,128)(2,1)} %pad_maximum_fusion), channel_id=1, source_target_pairs={{0,6},{1,7},{2,0},{3,1},{4,2},{5,3},{6,4},{7,5},{8,14},{9,15},{10,... | collective-permute-start | bytes 3538952 | tf_op jit(solution)/shard_map/ppermute | solution.py:54
  112.3 29.1 %collective-permute-start.8 = (bf16[2,256,1152]{2,1,0:T(8,128)(2,1)}, bf16[2,256,1152]{2,1,0:T(8,128)(2,1)}, u32[]{:S(2)}, u32[]{:S(2)}) collective-permute-start(bf16[2,256,1152]{2,1,0:T(8,128)(2,1)} %pad_maximum_fusion), channel_id=1, source_target_pairs={{0,2},{1,3},{2,4},{3,5},{4,6},{5,7},{6,0},{7,1},{8,10},{9,11},{10,... | collective-permute-start | bytes 3538952 | tf_op jit(solution)/shard_map/ppermute | solution.py:53
  115.0 54.8 %all-to-all-start.4 = ((bf16[8,128,1024]{2,1,0:T(8,128)(2,1)}), bf16[8,128,1024]{2,1,0:T(8,128)(2,1)}, u32[]{:S(2)}, u32[]{:S(2)}) async-start(bf16[8,128,1024]{2,1,0:T(8,128)(2,1)} %broadcast_in_dim.93), calls=%async_computation.5 | async-start | bytes 4194304 | tf_op jit(solution)/shard_map/all_to_all | solution.py:312
  143.2 99.2 %collective-permute-start.9 = (bf16[1,256,1152]{2,1,0:T(8,128)(2,1)}, bf16[1,256,1152]{2,1,0:T(8,128)(2,1)}, u32[]{:S(2)}, u32[]{:S(2)}) collective-permute-start(bf16[1,256,1152]{2,1,0:T(8,128)(2,1)} %slice.350), channel_id=1, source_target_pairs={{0,2},{1,3},{2,4},{3,5},{4,6},{5,7},{6,0},{7,1},{8,10},{9,11},{10,... | collective-permute-start | bytes 1769480 | tf_op jit(solution)/shard_map/ppermute | solution.py:55
  145.2 99.4 %collective-permute-start.10 = (bf16[1,256,1152]{2,1,0:T(8,128)(2,1)}, bf16[1,256,1152]{2,1,0:T(8,128)(2,1)}, u32[]{:S(2)}, u32[]{:S(2)}) collective-permute-start(bf16[1,256,1152]{2,1,0:T(8,128)(2,1)} %slice.351), channel_id=1, source_target_pairs={{0,6},{1,7},{2,0},{3,1},{4,2},{5,3},{6,4},{7,5},{8,14},{9,15},{10,... | collective-permute-start | bytes 1769480 | tf_op jit(solution)/shard_map/ppermute | solution.py:56
  199.0 37.6 %all-to-all-start.3 = ((bf16[128,8,1024]{2,1,0:T(8,128)(2,1)}), bf16[128,8,1024]{2,1,0:T(8,128)(2,1)S(1)}, u32[]{:S(2)}, u32[]{:S(2)}) async-start(bf16[128,8,1024]{2,1,0:T(8,128)(2,1)} %broadcast_in_dim.89), calls=%async_computation.3 | async-start | bytes 4194304 | tf_op jit(solution)/shard_map/all_to_all | solution.py:312
  240.1 79.1 %all-gather.11.cloned.1.call-start = ((), (), s32[]{:S(2)}) async-start(), calls=%async_computation.21 | async-start | bytes 2359296 | tf_op jit(solution)/shard_map/all_gather | solution.py:389
  249.7 53.5 %collective-permute-start.11 = (bf16[8,256,1152]{2,1,0:T(8,128)(2,1)}, bf16[8,256,1152]{2,1,0:T(8,128)(2,1)}, u32[]{:S(2)}, u32[]{:S(2)}) collective-permute-start(bf16[8,256,1152]{2,1,0:T(8,128)(2,1)} %get-tuple-element.179), channel_id=1, source_target_pairs={{0,1},{1,0},{2,3},{3,2},{4,5},{5,4},{6,7},{7,6},{8,9},{9,8},{10,11... | collective-permute-start | bytes 14155784 | tf_op jit(solution)/shard_map/ppermute | solution.py:50
  265.9 15.1 %collective-permute-start.14 = (bf16[2,128,1024]{2,1,0:T(8,128)(2,1)}, bf16[2,128,1024]{2,1,0:T(8,128)(2,1)}, u32[]{:S(2)}, u32[]{:S(2)}) collective-permute-start(bf16[2,128,1024]{2,1,0:T(8,128)(2,1)} %pad_maximum_fusion.7), channel_id=1, source_target_pairs={{0,2},{1,3},{2,4},{3,5},{4,6},{5,7},{6,0},{7,1},{8,10},{9,11},{10,... | collective-permute-start | bytes 1572872 | tf_op jit(solution)/shard_map/ppermute | solution.py:53
  266.5 17.4 %collective-permute-start.13 = (bf16[2,128,1024]{2,1,0:T(8,128)(2,1)}, bf16[2,128,1024]{2,1,0:T(8,128)(2,1)}, u32[]{:S(2)}, u32[]{:S(2)}) collective-permute-start(bf16[2,128,1024]{2,1,0:T(8,128)(2,1)} %pad_maximum_fusion.7), channel_id=1, source_target_pairs={{0,6},{1,7},{2,0},{3,1},{4,2},{5,3},{6,4},{7,5},{8,14},{9,15},{10,... | collective-permute-start | bytes 1572872 | tf_op jit(solution)/shard_map/ppermute | solution.py:54
  269.2 261.7 %reduce-scatter.5.cloned.1.call-start = ((), (), s32[]{:S(2)}) async-start(), calls=%async_computation.18 | async-start | bytes 4456448 | tf_op jit(solution)/shard_map/reduce_scatter | solution.py:500
  358.8 172.1 %reduce-scatter.3.cloned.1.call-start = ((), (), s32[]{:S(2)}) async-start(), calls=%async_computation.17 | async-start | bytes 4456448 | tf_op jit(solution)/shard_map/reduce_scatter | solution.py:500
  369.5 13.8 %collective-permute-start.2 = (bf16[2,128,1024]{2,1,0:T(8,128)(2,1)S(1)}, bf16[2,128,1024]{2,1,0:T(8,128)(2,1)S(1)}, u32[]{:S(2)}, u32[]{:S(2)}) collective-permute-start(bf16[2,128,1024]{2,1,0:T(8,128)(2,1)S(1)} %pad_maximum_fusion.6), channel_id=1, source_target_pairs={{0,2},{1,3},{2,4},{3,5},{4,6},{5,7},{6,0},{7,1},{8,10},{9,11},{10,... | collective-permute-start | bytes 1572872 | tf_op jit(solution)/shard_map/ppermute | solution.py:53
  371.0 13.6 %collective-permute-start.1 = (bf16[2,128,1024]{2,1,0:T(8,128)(2,1)S(1)}, bf16[2,128,1024]{2,1,0:T(8,128)(2,1)S(1)}, u32[]{:S(2)}, u32[]{:S(2)}) collective-permute-start(bf16[2,128,1024]{2,1,0:T(8,128)(2,1)S(1)} %pad_maximum_fusion.6), channel_id=1, source_target_pairs={{0,6},{1,7},{2,0},{3,1},{4,2},{5,3},{6,4},{7,5},{8,14},{9,15},{10,... | collective-permute-start | bytes 1572872 | tf_op jit(solution)/shard_map/ppermute | solution.py:54
  443.4 17.2 %collective-permute-start.18 = (bf16[8,128,1152]{2,1,0:T(8,128)(2,1)}, bf16[8,128,1152]{2,1,0:T(8,128)(2,1)}, u32[]{:S(2)}, u32[]{:S(2)}) collective-permute-start(bf16[8,128,1152]{2,1,0:T(8,128)(2,1)} %slice.292), channel_id=1, source_target_pairs={{0,1},{1,0},{2,3},{3,2},{4,5},{5,4},{6,7},{7,6},{8,9},{9,8},{10,11... | collective-permute-start | bytes 7077896 | tf_op jit(solution)/shard_map/ppermute | solution.py:74
  445.2 21.4 %collective-permute-start.24 = (bf16[8,128,1152]{2,1,0:T(8,128)(2,1)}, bf16[8,128,1152]{2,1,0:T(8,128)(2,1)}, u32[]{:S(2)}, u32[]{:S(2)}) collective-permute-start(bf16[8,128,1152]{2,1,0:T(8,128)(2,1)} %slice.309), channel_id=1, source_target_pairs={{0,1},{1,0},{2,3},{3,2},{4,5},{5,4},{6,7},{7,6},{8,9},{9,8},{10,11... | collective-permute-start | bytes 7077896 | tf_op jit(solution)/shard_map/ppermute | solution.py:74
  474.5 24.9 %collective-permute-start.22 = (bf16[2,128,1152]{2,1,0:T(8,128)(2,1)S(1)}, bf16[2,128,1152]{2,1,0:T(8,128)(2,1)S(1)}, u32[]{:S(2)}, u32[]{:S(2)}) collective-permute-start(bf16[2,128,1152]{2,1,0:T(8,128)(2,1)S(1)} %pad_maximum_fusion.3), channel_id=1, source_target_pairs={{0,6},{1,7},{2,0},{3,1},{4,2},{5,3},{6,4},{7,5},{8,14},{9,15},{10,... | collective-permute-start | bytes 1769480 | tf_op jit(solution)/shard_map/ppermute | solution.py:84
  478.1 23.7 %collective-permute-start.20 = (bf16[2,128,1152]{2,1,0:T(8,128)(2,1)S(1)}, bf16[2,128,1152]{2,1,0:T(8,128)(2,1)S(1)}, u32[]{:S(2)}, u32[]{:S(2)}) collective-permute-start(bf16[2,128,1152]{2,1,0:T(8,128)(2,1)S(1)} %pad_maximum_fusion.2), channel_id=1, source_target_pairs={{0,2},{1,3},{2,4},{3,5},{4,6},{5,7},{6,0},{7,1},{8,10},{9,11},{10,... | collective-permute-start | bytes 1769480 | tf_op jit(solution)/shard_map/ppermute | solution.py:83
  480.4 32.7 %collective-permute-start.28 = (bf16[2,128,1152]{2,1,0:T(8,128)(2,1)S(1)}, bf16[2,128,1152]{2,1,0:T(8,128)(2,1)S(1)}, u32[]{:S(2)}, u32[]{:S(2)}) collective-permute-start(bf16[2,128,1152]{2,1,0:T(8,128)(2,1)S(1)} %pad_maximum_fusion.5), channel_id=1, source_target_pairs={{0,6},{1,7},{2,0},{3,1},{4,2},{5,3},{6,4},{7,5},{8,14},{9,15},{10,... | collective-permute-start | bytes 1769480 | tf_op jit(solution)/shard_map/ppermute | solution.py:84
  484.3 29.7 %collective-permute-start.26 = (bf16[2,128,1152]{2,1,0:T(8,128)(2,1)S(1)}, bf16[2,128,1152]{2,1,0:T(8,128)(2,1)S(1)}, u32[]{:S(2)}, u32[]{:S(2)}) collective-permute-start(bf16[2,128,1152]{2,1,0:T(8,128)(2,1)S(1)} %pad_maximum_fusion.4), channel_id=1, source_target_pairs={{0,2},{1,3},{2,4},{3,5},{4,6},{5,7},{6,0},{7,1},{8,10},{9,11},{10,... | collective-permute-start | bytes 1769480 | tf_op jit(solution)/shard_map/ppermute | solution.py:83
  502.1 14.8 %collective-permute-start.23 = (bf16[1,128,1152]{2,1,0:T(8,128)(2,1)S(1)}, bf16[1,128,1152]{2,1,0:T(8,128)(2,1)S(1)}, u32[]{:S(2)}, u32[]{:S(2)}) collective-permute-start(bf16[1,128,1152]{2,1,0:T(8,128)(2,1)S(1)} %slice.370), channel_id=1, source_target_pairs={{0,8},{1,9},{2,10},{3,11},{4,12},{5,13},{6,14},{7,15},{8,0},{9,1},... | collective-permute-start | bytes 884744 | tf_op jit(solution)/shard_map/ppermute | solution.py:74
  548.4 17.2 %all-to-all-start.8 = ((bf16[8,128,128]{2,1,0:T(8,128)(2,1)}), bf16[8,128,128]{2,1,0:T(8,128)(2,1)S(1)}, u32[]{:S(2)}, u32[]{:S(2)}) async-start(bf16[8,128,128]{2,1,0:T(8,128)(2,1)} %bitcast.374), calls=%async_computation.10 | async-start | bytes 524288 | tf_op jit(solution)/shard_map/all_to_all | solution.py:316
  565.6 30.6 %all-to-all-start.12 = ((bf16[8,2,128,512]{3,2,1,0:T(8,128)(2,1)}), bf16[8,2,128,512]{3,2,1,0:T(8,128)(2,1)}, u32[]{:S(2)}, u32[]{:S(2)}) async-start(bf16[8,2,128,512]{3,2,1,0:T(8,128)(2,1)} %bitcast.393), calls=%async_computation.14 | async-start | bytes 4194304 | tf_op jit(solution)/shard_map/all_to_all | solution.py:316
  596.3 29.7 %all-to-all-start.13 = ((bf16[8,2,128,512]{3,2,1,0:T(8,128)(2,1)}), bf16[8,2,128,512]{3,2,1,0:T(8,128)(2,1)}, u32[]{:S(2)}, u32[]{:S(2)}) async-start(bf16[8,2,128,512]{3,2,1,0:T(8,128)(2,1)} %bitcast.392), calls=%async_computation.15 | async-start | bytes 4194304 | tf_op jit(solution)/shard_map/all_to_all | solution.py:316
  625.9 28.0 %all-to-all-start.14 = ((bf16[8,2,128,512]{3,2,1,0:T(8,128)(2,1)}), bf16[8,2,128,512]{3,2,1,0:T(8,128)(2,1)}, u32[]{:S(2)}, u32[]{:S(2)}) async-start(bf16[8,2,128,512]{3,2,1,0:T(8,128)(2,1)} %bitcast.391), calls=%async_computation.16 | async-start | bytes 4194304 | tf_op jit(solution)/shard_map/all_to_all | solution.py:316
  708.5 30.2 %all-to-all-start.9 = ((bf16[8,128,1024]{2,1,0:T(8,128)(2,1)}), bf16[8,128,1024]{2,1,0:T(8,128)(2,1)}, u32[]{:S(2)}, u32[]{:S(2)}) async-start(bf16[8,128,1024]{2,1,0:T(8,128)(2,1)} %bitcast.412), calls=%async_computation.11 | async-start | bytes 4194304 | tf_op jit(solution)/shard_map/all_to_all | solution.py:316
  738.7 36.2 %all-to-all-start.11 = ((bf16[128,8,1024]{2,1,0:T(8,128)(2,1)}), bf16[128,8,1024]{2,1,0:T(8,128)(2,1)}, u32[]{:S(2)}, u32[]{:S(2)}) async-start(bf16[128,8,1024]{2,1,0:T(8,128)(2,1)} %fusion.36), calls=%async_computation.13 | async-start | bytes 4194304 | tf_op jit(solution)/shard_map/all_to_all | solution.py:316
  (171 other events, 2598.7 us)
Sparse Core Ops, SparseCore 0:
  9.7 83.5 all-gather.6
  94.9 76.2 all-gather.8
  269.3 49.8 all-gather.10
  359.0 79.5 reduce-scatter.4
  446.1 84.3 reduce-scatter.2

commit v3 on v2

v3 whole, which is shorter than its diff:
```python
import functools

import jax
import jax.numpy as jnp
from jax import lax
from jax.experimental import pallas as pl
from jax.experimental.pallas import tpu as pltpu
from jax.sharding import Mesh
from jax.sharding import PartitionSpec as P

BF = jnp.bfloat16
F32 = jnp.float32
H = 16
KV = 8
DH = 64
TOPK = 8
WINDOW = 1024
EPS = 1e-06
THETA = 10000.0


def dot(a, b, ca, cb):
    return lax.dot_general(a, b, (((ca,), (cb,)), ((), ())), preferred_element_type=F32)


def lanes_of(v):
    return lax.broadcasted_iota(jnp.int32, v.shape, v.ndim - 1)


def head_sums(v):
    low = lanes_of(v) < DH
    first = jnp.sum(jnp.where(low, v, 0.0), axis=1, keepdims=True)
    second = jnp.sum(jnp.where(low, 0.0, v), axis=1, keepdims=True)
    return jnp.where(low, first, second)


def trade(v):
    return jnp.where(
        lanes_of(v) % DH < DH // 2, pltpu.roll(v, 128 - DH // 2, 1), pltpu.roll(v, DH // 2, 1)
    )


def both_halves(v, second):
    low = lanes_of(v) < DH
    other = pltpu.roll(v, DH, 1)
    return jnp.where(low, other, v) if second else jnp.where(low, v, other)


def stack_heads(v):
    low = lanes_of(v) < DH
    zero = jnp.zeros_like(v)
    return jnp.concatenate([jnp.where(low, v, zero), jnp.where(low, zero, v)], axis=0)


def key_span(start, block, length):
    reach = WINDOW // 2 - 1
    low = max(0, start - reach) // 128 * 128
    high = min(length, -(-(start + block + reach) // 128) * 128)
    return low, high


def masked_probs(q_two, keys, seg_col, seg_row, start, low):
    block = q_two.shape[0] // 2
    scores = dot(q_two, keys, 1, 1)
    shape = (block, keys.shape[0])
    gap = (
        lax.broadcasted_iota(jnp.int32, shape, 0)
        - lax.broadcasted_iota(jnp.int32, shape, 1)
        + (start - low)
    )
    allowed = (seg_col == seg_row) & (jnp.abs(gap) < WINDOW // 2)
    bias = jnp.where(allowed, 0.0, -1e30)
    scores = scores + jnp.concatenate([bias, bias], axis=0)
    raised = jnp.exp(scores - jnp.max(scores, axis=1, keepdims=True))
    return raised * (1.0 / jnp.sum(raised, axis=1, keepdims=True))


def attend_kernel(
    order_ref,
    own_ref,
    after_ref,
    far_low_ref,
    far_high_ref,
    before_ref,
    gain_ref,
    w_ref,
    head_gain_ref,
    cos_ref,
    sin_ref,
    seg_col_ref,
    seg_row_ref,
    mixed_ref,
    hidden_ref,
    q_ref,
    kv_ref,
    keys_ref,
    values_ref,
):
    tok, width = own_ref.shape[1:]
    length = hidden_ref.shape[0]
    pieces = [
        (own_ref, 0),
        (own_ref, 1),
        (after_ref, 0),
        (after_ref, 1),
        (far_low_ref, 0),
        (far_high_ref, 0),
        (before_ref, 0),
        (before_ref, 1),
    ]
    for r, (ref, i) in enumerate(pieces):
        x = ref[i].astype(F32)
        x = x * lax.rsqrt(jnp.mean(x * x, axis=1, keepdims=True) + EPS) * gain_ref[...]
        rows = pl.ds(pl.multiple_of(order_ref[r] * tok, tok), tok)
        hidden_ref[rows] = x.astype(BF)
    raw = dot(hidden_ref[...], w_ref[...], 1, 0)
    for half in range(2):
        u = raw[:, half * 128 : half * 128 + 128]
        gain = head_gain_ref[:, half * 128 : half * 128 + 128]
        n = u * lax.rsqrt(head_sums(u * u) * (1.0 / DH) + EPS) * gain
        turned = n * cos_ref[...] + trade(n) * sin_ref[...]
        if half == 0:
            q_ref[...] = turned.astype(BF)
        else:
            kv = jnp.where(lanes_of(u) < DH, turned, u)
            kv_ref[...] = kv.astype(BF)
            keys_ref[...] = both_halves(kv, False).astype(BF)
            values_ref[...] = both_halves(kv, True).astype(BF)
    block = 256
    for start in range(0, length, block):
        low, high = key_span(start, block, length)
        q_two = stack_heads(q_ref[start : start + block].astype(F32) * DH**-0.5).astype(BF)
        probs = masked_probs(
            q_two,
            keys_ref[low:high],
            seg_col_ref[start : start + block],
            seg_row_ref[:, low:high],
            start,
            low,
        )
        result = dot(probs.astype(BF), values_ref[low:high], 1, 0)
        first = lanes_of(result[:block]) < DH
        mixed_ref[start : start + block] = jnp.where(first, result[:block], result[block:]).astype(
            BF
        )


def attend_back_kernel(
    hidden_ref,
    q_ref,
    kv_ref,
    d_mixed_ref,
    gain_ref,
    w_ref,
    head_gain_ref,
    cos_ref,
    sin_ref,
    seg_col_ref,
    seg_row_ref,
    d_hidden_ref,
    grad_w_ref,
    grad_gain_ref,
    grad_heads_ref,
    keys_ref,
    values_ref,
    d_q_ref,
    d_k_ref,
    d_v_ref,
    d_raw_ref,
):
    length = hidden_ref.shape[0]
    kv = kv_ref[...].astype(F32)
    keys_ref[...] = both_halves(kv, False).astype(BF)
    values_ref[...] = both_halves(kv, True).astype(BF)
    d_k_ref[...] = jnp.zeros_like(d_k_ref)
    d_v_ref[...] = jnp.zeros_like(d_v_ref)
    block = 256
    for start in range(0, length, block):
        low, high = key_span(start, block, length)
        q_two = stack_heads(q_ref[start : start + block].astype(F32) * DH**-0.5).astype(BF)
        m_two = stack_heads(d_mixed_ref[start : start + block].astype(F32)).astype(BF)
        probs = masked_probs(
            q_two,
            keys_ref[low:high],
            seg_col_ref[start : start + block],
            seg_row_ref[:, low:high],
            start,
            low,
        )
        d_probs = dot(m_two, values_ref[low:high], 1, 1)
        inner = jnp.sum(probs * d_probs, axis=1, keepdims=True)
        d_scores = (probs * (d_probs - inner)).astype(BF)
        result = dot(d_scores, keys_ref[low:high], 1, 0)
        first = lanes_of(result[:block]) < DH
        d_q_ref[start : start + block] = jnp.where(first, result[:block], result[block:]) * (
            DH**-0.5
        )
        d_k_ref[low:high] += dot(d_scores, q_two, 0, 0)
        d_v_ref[low:high] += dot(probs.astype(BF), m_two, 0, 0)
    raw = dot(hidden_ref[...], w_ref[...], 1, 0)
    d_k = d_k_ref[...]
    d_k = d_k + pltpu.roll(d_k, DH, 1)
    d_v = d_v_ref[...]
    d_v = d_v + pltpu.roll(d_v, DH, 1)
    for half in range(2):
        lanes = slice(half * 128, half * 128 + 128)
        u = raw[:, lanes]
        gain = head_gain_ref[:, lanes]
        d = d_q_ref[...] if half == 0 else d_k
        d = d * cos_ref[...] + trade(d * sin_ref[...])
        r = lax.rsqrt(head_sums(u * u) * (1.0 / DH) + EPS)
        grad_heads_ref[:, lanes] = jnp.sum(d * u * r, axis=0, keepdims=True)
        d = d * gain
        d = d * r - u * (r * r * r * (head_sums(d * u) * (1.0 / DH)))
        if half == 1:
            d = jnp.where(lanes_of(d) < DH, d, d_v)
        d_raw_ref[:, lanes] = d.astype(BF)
    grad_w_ref[...] = dot(hidden_ref[...], d_raw_ref[...], 0, 0)
    total = jnp.zeros(grad_gain_ref.shape, F32)
    for start in range(0, length, block):
        rows = slice(start, start + block)
        d_hidden = dot(d_raw_ref[rows], w_ref[...], 1, 1)
        d_hidden_ref[rows] = d_hidden.astype(BF)
        total = total + jnp.sum(d_hidden * hidden_ref[rows].astype(F32), axis=0, keepdims=True)
    grad_gain_ref[...] = total / gain_ref[...]


def whole(a):
    return pl.BlockSpec(a.shape, lambda i: (0,) * len(a.shape), pipeline_mode=pl.Buffered(1))


def attend_forward(order, pieces, gain, w_heads, head_gain, cosine, sine, seg_col, seg_row):
    length = cosine.shape[0]
    width = w_heads.shape[0]
    shape = jax.ShapeDtypeStruct
    outs = [
        shape((length, 128), BF),
        shape((length, width), BF),
        shape((length, 128), BF),
        shape((length, 128), BF),
    ]
    args = list(pieces) + [gain, w_heads, head_gain, cosine, sine, seg_col, seg_row]
    return pl.pallas_call(
        attend_kernel,
        out_shape=outs,
        grid=(1,),
        in_specs=[pl.BlockSpec(memory_space=pltpu.SMEM)] + [whole(a) for a in args],
        out_specs=[whole(o) for o in outs],
        scratch_shapes=[pltpu.VMEM((length, 128), BF), pltpu.VMEM((length, 128), BF)],
        compiler_params=pltpu.CompilerParams(vmem_limit_bytes=40 * 1024 * 1024),
        cost_estimate=pl.CostEstimate(flops=12 * 10**9, bytes_accessed=8 << 20, transcendentals=0),
    )(order, *args)


def attend_backward(
    hidden, q, kv, d_mixed, gain, w_heads, head_gain, cosine, sine, seg_col, seg_row
):
    length, width = hidden.shape
    shape = jax.ShapeDtypeStruct
    outs = [
        shape((length, width), BF),
        shape((width, 256), F32),
        shape((1, width), F32),
        shape((1, 256), F32),
    ]
    args = [hidden, q, kv, d_mixed, gain, w_heads, head_gain, cosine, sine, seg_col, seg_row]
    return pl.pallas_call(
        attend_back_kernel,
        out_shape=outs,
        grid=(1,),
        in_specs=[whole(a) for a in args],
        out_specs=[whole(o) for o in outs],
        scratch_shapes=[pltpu.VMEM((length, 128), BF)] * 2
        + [pltpu.VMEM((length, 128), F32)] * 3
        + [pltpu.VMEM((length, 256), BF)],
        compiler_params=pltpu.CompilerParams(vmem_limit_bytes=40 * 1024 * 1024),
        cost_estimate=pl.CostEstimate(flops=25 * 10**9, bytes_accessed=8 << 20, transcendentals=0),
    )(*args)


def halves(v):
    high = v.astype(BF)
    return high, (v - high.astype(F32)).astype(BF)


def expert_kernel(
    scalar_ref,
    x_own_ref,
    x_other_ref,
    g_own_ref,
    g_other_ref,
    router_ref,
    w_ref,
    out_ref,
    back_own_ref,
    back_other_ref,
    xe_ref,
    de_ref,
    act_ref,
    da_ref,
    db_ref,
    pick_ref,
    weight_ref,
    dgate_ref,
    eo_ref,
    dr_ref,
):
    half, tok, width = x_own_ref.shape
    sources = 2 * half
    core = scalar_ref[1]
    local, slots, hidden = act_ref.shape
    cap = slots // sources
    first = scalar_ref[0]
    lane = lax.broadcasted_iota(jnp.int32, (tok, 128), 1)
    place = lax.broadcasted_iota(jnp.int32, (tok, local * cap), 1)
    row_expert = lax.broadcasted_iota(jnp.int32, (local * cap, 128), 0) // cap
    slot_lane = lax.broadcasted_iota(jnp.int32, (local * cap, 128), 1)
    own_lane = slot_lane == first + row_expert

    def fetch(i, carry, x_ref, g_ref, offset):
        s = i + offset
        x = x_ref[i]
        from_g = scalar_ref[i + 2]
        held = g_ref[from_g, :, width:].astype(F32)
        chosen = held >= 0.0
        logits = jnp.where(chosen, dot(x, router_ref[...], 1, 0), -1e30)
        top = jnp.max(logits, axis=1, keepdims=True)
        raised = jnp.where(chosen, jnp.exp(logits - top), 0.0)
        gates = raised / jnp.sum(raised, axis=1, keepdims=True)
        pick = jnp.zeros((tok, local * cap), F32)
        for e in range(local):
            mine = jnp.max(jnp.where(lane == first + e, held, -1.0), axis=1, keepdims=True)
            goal = jnp.where(mine >= 0.0, mine + e * cap, -1.0).astype(jnp.int32)
            pick = jnp.where(place == goal, 1.0, pick)
        pick = pick.astype(BF)
        pick_ref[s] = pick
        rows = pl.ds(pl.multiple_of(s * cap, 16), cap)
        x_slots = dot(pick, x, 0, 0).astype(BF)
        g_slots = dot(pick, g_ref[from_g, :, :width], 0, 0).astype(BF)
        high, low = halves(gates)
        weight = dot(pick, high, 0, 0) + dot(pick, low, 0, 0)
        weight = jnp.sum(jnp.where(own_lane, weight, 0.0), axis=1, keepdims=True)
        for e in range(local):
            part = slice(e * cap, (e + 1) * cap)
            xe_ref[e, rows] = x_slots[part]
            de_ref[e, rows] = g_slots[part]
            weight_ref[e, rows] = weight[part]
        return carry

    for x_ref, g_ref, offset in ((x_own_ref, g_own_ref, 0), (x_other_ref, g_other_ref, half)):
        lax.fori_loop(
            0, half, functools.partial(fetch, x_ref=x_ref, g_ref=g_ref, offset=offset), 0
        )
    chunk = 256

    def work(i, carry):
        e = i // (slots // chunk)
        rows = pl.ds(pl.multiple_of((i % (slots // chunk)) * chunk, chunk), chunk)
        w_gate = w_ref[:, 0, e].reshape(width, hidden)
        w_up = w_ref[:, 1, e].reshape(width, hidden)
        w_down = w_ref[:, 2, e].reshape(width, hidden)
        x = xe_ref[e, rows]
        a = dot(x, w_gate, 1, 0)
        b = dot(x, w_up, 1, 0)
        sig = 1.0 / (1.0 + jnp.exp(-a))
        silu = a * sig
        active = (silu * b).astype(BF)
        act_ref[e, rows] = active
        slope = b * (sig * (1.0 + a * (1.0 - sig)))
        weight = weight_ref[e, rows]
        g = de_ref[e, rows].astype(F32)
        result = dot(active, w_down, 1, 1).astype(BF).astype(F32)
        dgate_ref[e, rows] = jnp.sum(result * g, axis=1, keepdims=True)
        eo_ref[e, rows] = (weight * result).astype(BF)
        d_expert = (weight * g).astype(BF)
        de_ref[e, rows] = d_expert
        d_active = dot(d_expert, w_down, 1, 0)
        da = (d_active * slope).astype(BF)
        db = (d_active * silu).astype(BF)
        da_ref[e, rows] = da
        db_ref[e, rows] = db
        dr_ref[e, rows] = (dot(da, w_gate, 1, 1) + dot(db, w_up, 1, 1)).astype(BF)
        return carry

    lax.fori_loop(0, local * (slots // chunk), work, 0)

    def give(i, carry, back_ref, offset, column):
        s = i + offset
        rows = pl.ds(pl.multiple_of(s * cap, 16), cap)
        pick = pick_ref[s]
        eo = jnp.concatenate([eo_ref[e, rows] for e in range(local)], axis=0)
        dr = jnp.concatenate([dr_ref[e, rows] for e in range(local)], axis=0)
        dgate = jnp.concatenate([dgate_ref[e, rows] for e in range(local)], axis=0)
        high, low = halves(dgate)
        spread = jnp.where(own_lane, high.astype(F32), 0.0) + jnp.where(
            slot_lane == first + row_expert + 64, low.astype(F32), 0.0
        )
        out_ref[2 * i + column] = dot(pick, eo, 1, 0).astype(BF)
        back_ref[i, :, :width] = dot(pick, dr, 1, 0).astype(BF)
        back_ref[i, :, width:] = dot(pick, spread.astype(BF), 1, 0).astype(BF)
        return carry

    for back_ref, offset, column in ((back_own_ref, 0, core), (back_other_ref, half, 1 - core)):
        lax.fori_loop(
            0, half, functools.partial(give, back_ref=back_ref, offset=offset, column=column), 0
        )


def run_experts(scalars, x_own, x_other, g_own, g_other, micro, router, weights, cap):
    half, tok, width = x_own.shape
    sources = 2 * half
    local, hidden = weights.shape[2], weights.shape[4]
    slots = sources * cap
    wide = g_own.shape[2]
    shape = jax.ShapeDtypeStruct
    outs = [
        shape((sources, tok, width), BF),
        shape((half, tok, wide), BF),
        shape((half, tok, wide), BF),
        shape((local, slots, width), BF),
        shape((local, slots, width), BF),
        shape((local, slots, hidden), BF),
        shape((local, slots, hidden), BF),
        shape((local, slots, hidden), BF),
    ]
    g_spec = pl.BlockSpec(
        (half, tok, wide), lambda i: (0, micro, 0), pipeline_mode=pl.Buffered(1)
    )
    args = [router, weights]
    return pl.pallas_call(
        expert_kernel,
        out_shape=outs,
        grid=(1,),
        in_specs=[pl.BlockSpec(memory_space=pltpu.SMEM), whole(x_own), whole(x_other)]
        + [g_spec, g_spec]
        + [whole(a) for a in args],
        out_specs=[whole(o) for o in outs],
        scratch_shapes=[
            pltpu.VMEM((sources, tok, local * cap), BF),
            pltpu.VMEM((local, slots, 1), F32),
            pltpu.VMEM((local, slots, 1), F32),
            pltpu.VMEM((local, slots, width), BF),
            pltpu.VMEM((local, slots, width), BF),
        ],
        compiler_params=pltpu.CompilerParams(vmem_limit_bytes=56 * 1024 * 1024),
        cost_estimate=pl.CostEstimate(flops=40 * 10**9, bytes_accessed=40 << 20, transcendentals=0),
    )(scalars, x_own, x_other, g_own, g_other, *args)


def expert_grad_kernel(xe0, xe1, de0, de1, act0, act1, da0, da1, db0, db1, out_ref):
    left = {0: (xe0, xe1), 1: (xe0, xe1), 2: (de0, de1)}
    right = {0: (da0, da1), 1: (db0, db1), 2: (act0, act1)}
    step = pl.program_id(0)
    pieces, depth = out_ref.shape[0], out_ref.shape[2]
    for kind in range(3):

        @pl.when(step % 3 == kind)
        def _(kind=kind):
            total = dot(left[kind][0][0], right[kind][0][0], 0, 0)
            total = total + dot(left[kind][1][0], right[kind][1][0], 0, 0)
            out_ref[:, 0] = total.reshape(pieces, depth, -1).astype(BF)


def expert_grads(kept, pieces):
    local, slots, width = kept[0][0].shape
    hidden = kept[0][2].shape[2]
    args = [kept[m][i] for i in range(5) for m in range(2)]
    spec = lambda a: pl.BlockSpec((1,) + a.shape[1:], lambda i: (i // 3, 0, 0))
    depth = width // pieces
    return pl.pallas_call(
        expert_grad_kernel,
        out_shape=jax.ShapeDtypeStruct((pieces, 3 * local, depth, hidden), BF),
        grid=(3 * local,),
        in_specs=[spec(a) for a in args],
        out_specs=pl.BlockSpec((pieces, 1, depth, hidden), lambda i: (0, i, 0, 0)),
        compiler_params=pltpu.CompilerParams(vmem_limit_bytes=48 * 1024 * 1024),
        cost_estimate=pl.CostEstimate(flops=14 * 10**9, bytes_accessed=28 << 20, transcendentals=0),
    )(*args)


CTX = ("z", "yl")
GROUP = ("yh", "x")
FSDP = ("yh", "x", "core")
ALL = CTX + FSDP
UP = [(i, (i + 1) % 4) for i in range(4)]
DOWN = [(i, (i - 1) % 4) for i in range(4)]
FLIP = [(0, 1), (1, 0)]


def mm(a, b):
    return jnp.dot(a, b, preferred_element_type=F32)


def mm_t(a, b):
    return lax.dot_general(a, b, (((1,), (1,)), ((), ())), preferred_element_type=F32)


def t_mm(a, b):
    return lax.dot_general(a, b, (((0,), (0,)), ((), ())), preferred_element_type=F32)


def ein(spec, a, b):
    return jnp.einsum(spec, a, b, preferred_element_type=F32)


def swap(parts, axis):
    return lax.all_to_all(parts, axis, split_axis=0, concat_axis=0, tiled=True)


def spread(block, axis, copies):
    return swap(jnp.broadcast_to(block[None], (copies,) + block.shape), axis)


def flip(block, axis):
    return lax.ppermute(block, axis, FLIP)


def pair_and_ring(block, pair, ring):
    both = jnp.concatenate([block, flip(block, pair)], axis=0)
    before = lax.ppermute(both, ring, UP)
    after = lax.ppermute(both, ring, DOWN)
    far_low = lax.ppermute(before[:1], ring, UP)
    far_high = lax.ppermute(after[1:], ring, DOWN)
    return [both, after, far_low, far_high, before]


def after_all(value, *others):
    return lax.optimization_barrier((value,) + others)[0]


def rope_tables(positions):
    half = DH // 2
    inverse = THETA ** (-(jnp.arange(half, dtype=F32) * 2.0) / DH)
    angles = positions.astype(F32)[:, None] * inverse[None, :]
    return (jnp.cos(angles), jnp.sin(angles))


def rms_scale(values, gain):
    return values * lax.rsqrt(jnp.mean(values * values, axis=-1, keepdims=True) + EPS) * gain


def body(
    tokens,
    segments,
    routes,
    w_query,
    w_key,
    w_value,
    w_out,
    w_router,
    attn_gain,
    mlp_gain,
    qk_gain,
    w_gate,
    w_up,
    w_down,
    cotangent,
):
    micro = tokens.shape[0]
    tok = tokens.shape[2]
    width = tokens.shape[3]
    length = segments.shape[2]
    rows = w_query.shape[0]
    n_ctx, n_fsdp = 8, 16
    n_all = n_ctx * n_fsdp
    z, yl, yh, x, core = (lax.axis_index(name) for name in ALL)
    shard = (yh * 4 + x) * 2 + core
    local = w_gate.shape[0]
    experts = local * n_fsdp
    cap = (3 * tok * TOPK + 2 * experts - 1) // (2 * experts)
    all_tok = micro * tok
    ratio = H // KV
    heads = ratio * DH
    span = heads + 2 * DH

    small = jnp.concatenate(
        [
            w_router,
            attn_gain[:, None],
            mlp_gain[:, None],
            jnp.pad(qk_gain[:, None], ((0, rows - 1), (0, 0))),
        ],
        axis=1,
    )
    small = jnp.pad(small, ((0, 0), (0, 128 - small.shape[1])))
    pieces = jnp.concatenate(
        [
            w_query.reshape(rows, n_ctx, heads),
            w_key.reshape(rows, n_ctx, DH),
            w_value.reshape(rows, n_ctx, DH),
            jnp.broadcast_to(small[:, None], (rows, n_ctx, 128)),
        ],
        axis=2,
    ).transpose(1, 0, 2)
    pieces = jnp.broadcast_to(pieces[:, None], (n_ctx, n_fsdp) + pieces.shape[1:])
    head_all = swap(pieces.reshape((n_all,) + pieces.shape[2:]), ALL).reshape(width, -1)
    w_heads = head_all[:, :span]
    small_all = head_all[:, span:]
    router = small_all[:, :experts]
    small_wide = small_all.astype(F32)
    gain_attn = small_wide[:, experts]
    gain_mlp = small_wide[:, experts + 1]
    gain_heads = small_wide[:, experts + 2].reshape(-1, rows)[:, 0]
    gain_row = gain_attn[None]
    head_row = jnp.concatenate(
        [gain_heads[:DH]] * ratio + [gain_heads[DH:], jnp.ones((DH,), F32)]
    )[None]
    router_pad = jnp.pad(router, ((0, 0), (0, 128 - experts)))

    seq_rows = [pair_and_ring(tokens[m], "yl", "z") for m in range(micro)]
    w_out = after_all(w_out, head_all)
    out_full = spread(w_out, ALL, n_all).reshape(width, width)

    expert_all = lax.all_gather(jnp.stack([w_gate, w_up, w_down]), CTX, axis=0)

    expert_ids = jnp.arange(experts, dtype=jnp.int32)
    cot = cotangent.reshape(all_tok, width)
    chosen = jnp.any(routes.reshape(all_tok, TOPK)[:, :, None] == expert_ids, axis=1)
    before = jnp.arange(tok, dtype=jnp.int32)
    lower = (before[:, None] >= before[None, :]).astype(BF)
    counts = ein("ut,mte->mue", lower, chosen.reshape(micro, tok, experts).astype(BF))
    held = jnp.where(chosen, counts.reshape(all_tok, experts) - 1.0, -1.0)
    held = jnp.pad(held, ((0, 0), (0, 128 - experts)), constant_values=-1.0).astype(BF)
    g_own = jnp.concatenate(
        pair_and_ring(jnp.concatenate([cot, held], axis=1)[None], "yh", "x"), axis=0
    )
    g_other = flip(g_own, "core")

    cosine, sine = rope_tables(jnp.arange(length, dtype=jnp.int32))
    cosine = jnp.tile(cosine, (1, 4))
    sine = jnp.tile(jnp.concatenate([-sine, sine], axis=1), (1, 2))
    rel = jnp.arange(n_ctx, dtype=jnp.int32)
    order = ((z + rel // 2) % 4) * 2 + (yl + rel % 2) % 2
    g_place = ((rel % 4 - x) % 4) * 2 + (rel // 4 - yh) % 2
    scalars = jnp.concatenate([jnp.stack([shard * local, core]), g_place]).astype(jnp.int32)

    def to_owner(v):
        return swap(v.reshape(n_ctx, tok, -1), CTX)

    def attention_args(m):
        seg = segments[m, 0]
        return gain_row, w_heads, head_row, cosine, sine, seg[:, None], seg[None, :]

    forward, saved = [], []
    for m in range(micro):
        mixed_h, *keep = attend_forward(order, seq_rows[m], *attention_args(m))
        saved.append(keep)
        mixed = to_owner(mixed_h).transpose(1, 0, 2).reshape(tok, width)
        start = tokens[m, 0].astype(F32)
        middle = start + mm(mixed, out_full)
        normed, norm_back = jax.vjp(rms_scale, middle, gain_mlp)
        hidden_two = normed.astype(BF)
        chosen_m = chosen[m * tok : (m + 1) * tok]
        logits = jnp.where(chosen_m, mm(hidden_two, router), -1e30)
        gates = jnp.where(chosen_m, jax.nn.softmax(logits, axis=-1), 0.0)
        x_own = spread(hidden_two, GROUP, n_ctx).reshape(n_ctx, tok, width)
        x_other = flip(x_own, "core")
        forward.append((mixed, middle, norm_back, hidden_two, gates, x_own, x_other))

    outs, d_inputs, kept, grads = [], [], [], []
    backs = []
    for m in range(micro):
        x_own, x_other = forward[m][5:]
        if m:
            x_other = after_all(x_other, *backs[-1][:1])
        moe_part, back_own, back_other, *keep = run_experts(
            scalars,
            x_own,
            x_other,
            g_own,
            g_other,
            m,
            router_pad,
            expert_all,
            cap,
        )
        kept.append(keep)
        back = (back_own.astype(F32) + flip(back_other, "core").astype(F32)).astype(BF)
        backs.append((back, moe_part))
    for m in range(micro):
        mixed, middle, norm_back, hidden_two, gates = forward[m][:5]
        back, moe_part = backs[m]
        back = jnp.sum(swap(back, GROUP).astype(F32), axis=0)
        moe = lax.psum_scatter(moe_part, FSDP, scatter_dimension=0, tiled=True)[0]
        outs.append((middle + moe.astype(F32)).astype(BF))
        grad_top = cot[m * tok : (m + 1) * tok].astype(F32)
        tail = back[:, width:]
        d_gates = tail[:, :experts] + tail[:, 64 : 64 + experts]
        d_select = gates * (d_gates - jnp.sum(gates * d_gates, axis=-1, keepdims=True))
        d_logits = d_select.astype(BF)
        grad_router = t_mm(hidden_two, d_logits)
        d_two = back[:, :width] + mm_t(d_logits, router)
        d_middle, grad_mlp = norm_back(d_two)
        d_middle = d_middle + grad_top
        d_branch = d_middle.astype(BF)
        grad_out = t_mm(mixed, d_branch)
        d_mixed = mm_t(d_branch, out_full).astype(BF)
        d_mixed = swap(d_mixed.reshape(tok, n_ctx, heads).transpose(1, 0, 2), CTX)
        d_hidden, grad_heads, grad_attn, grad_qk = attend_backward(
            *saved[m], d_mixed.reshape(length, heads), *attention_args(m)
        )
        d_hidden = jnp.sum(to_owner(d_hidden).astype(F32), axis=0)
        start = tokens[m, 0].astype(F32)
        inverse = lax.rsqrt(jnp.mean(start * start, axis=-1, keepdims=True) + EPS)
        u = d_hidden * gain_attn
        d_inputs.append(
            d_middle
            + inverse * u
            - start * (inverse**3 * jnp.mean(u * start, axis=-1, keepdims=True))
        )
        grad_qk = jnp.concatenate(
            [grad_qk[0, :DH] + grad_qk[0, DH : 2 * DH], grad_qk[0, 2 * DH : 3 * DH]]
        )
        grads.append((grad_out, grad_heads, grad_router, grad_attn[0], grad_mlp, grad_qk))
    grad_out, grad_heads, grad_router, grad_attn, grad_mlp, grad_qk = jax.tree.map(
        jnp.add, grads[0], grads[1]
    )

    grad_out = swap(grad_out.astype(BF).reshape(n_all, rows, width), ALL)
    own_out = jnp.sum(grad_out.astype(F32), axis=0)
    grad_qk = jnp.pad(grad_qk[:, None], ((0, 0), (0, rows - 1))).reshape(-1)
    grad_small = jnp.concatenate(
        [grad_router, grad_attn[:, None], grad_mlp[:, None], grad_qk[:, None]], axis=1
    )
    grad_small = jnp.pad(grad_small, ((0, 0), (0, 128 - grad_small.shape[1])))
    grad_pack = jnp.concatenate([grad_heads, grad_small], axis=1).astype(BF)
    grad_pack = swap(grad_pack.reshape(n_all, rows, -1), ALL).astype(F32)
    own_heads = jnp.sum(grad_pack[:, :, :span].reshape(n_ctx, n_fsdp, rows, -1), axis=1)
    own_heads = own_heads.transpose(1, 0, 2)
    own_small = jnp.sum(grad_pack[:, :, span:], axis=0)
    kept[1][0] = after_all(kept[1][0], backs[1][0])
    expert_own = lax.psum_scatter(
        expert_grads(kept, n_ctx), CTX, scatter_dimension=0, tiled=True
    )[0].astype(F32)
    expert_own = expert_own.reshape((local, 3) + expert_own.shape[1:])

    return (
        jnp.stack(outs)[:, None],
        jnp.stack(d_inputs)[:, None],
        own_heads[:, :, :heads].reshape(rows, -1),
        own_heads[:, :, heads : heads + DH].reshape(rows, -1),
        own_heads[:, :, heads + DH :].reshape(rows, -1),
        own_out,
        own_small[:, :experts],
        own_small[:, experts],
        own_small[:, experts + 1],
        own_small[:1, experts + 2],
        expert_own[:, 0],
        expert_own[:, 1],
        expert_own[:, 2],
    )


def solution(mesh):
    mesh = Mesh(mesh.devices.reshape(4, 2, 2, 4, 2), ALL)
    weight = P(ALL, None)
    gain = P(ALL)
    rows = P(None, FSDP, CTX, None)
    expert = P(FSDP, CTX, None)
    return jax.shard_map(
        body,
        mesh=mesh,
        in_specs=(rows, P(None, FSDP, None), rows)
        + (weight,) * 5
        + (gain,) * 3
        + (expert,) * 3
        + (rows,),
        out_specs=(rows, rows) + (weight,) * 5 + (gain,) * 3 + (expert,) * 3,
        check_vma=False,
    )
```

time: 793 us -> 698 us (0.88)
  waiting for transfers between devices: 274 us -> 196 us
  Pallas kernels: 79.8 us -> 140 us
  blocking collectives: 54.6 us -> 112 us
  matrix products: 74.2 us -> 19.2 us
  other arithmetic: 75.9 us -> 41.8 us
  starting transfers between devices: 116 us -> 86.5 us
  local copies, waits for them, and re-layouts: 92.7 us -> 76.6 us
    ppermute x30 -> x20, waiting for transfers between devices: 145 us -> 33.8 us  [the longest x8 16.1 us: flip(): return lax.ppermute(block, axis, FLIP)]
    pallas_call x0 -> x5, Pallas kernels: none -> 58.4 us  [the longest x2 21.9 us: attend_backward(): pl.pallas_call(attend_back_kernel, out_shape=outs, grid=(1,), in_specs=[w...]
    all_to_all x2 -> x3, blocking collectives: 54.6 us -> 112 us  [swap(): return lax.all_to_all(parts, axis, split_axis=0, concat_axis=0, tiled=True)]
    dot_general x19 -> x1, matrix products: 49.1 us -> 0.14 us  [ein(): return jnp.einsum(spec, a, b, preferred_element_type=F32)]
    all_to_all x10 -> x11, waiting for transfers between devices: 75.2 us -> 120 us  [swap(): return lax.all_to_all(parts, axis, split_axis=0, concat_axis=0, tiled=True)]
    reduce_scatter x2 -> x3, waiting for transfers between devices: 0.01 us -> 42.5 us  [the longest x2 42.5 us: body(): moe = lax.psum_scatter(moe_part, FSDP, scatter_dimension=0, tiled=True)[0]]
    all_to_all x3 -> x0, waiting for transfers between devices: 41.8 us -> none  [spread(): return lax.all_to_all(wide, axis, split_axis=0, concat_axis=0, tiled=True)]
    ppermute x30 -> x20, starting transfers between devices: 47.3 us -> 22.9 us  [the longest x3 6.33 us: pair_and_ring(): far_high = lax.ppermute(after[1:], ring, DOWN)]
  transfers between devices with their start and end apart: 48 -> 35, of which waited for: 28 -> 14; matrix products, arithmetic and copies ran while one was open for 28% -> 15% of each run, Pallas kernels for 5% -> 20%
where the time goes in v3:
time: 698 us; the launch traced here: 688 us
  waiting for transfers between devices  196 us (28%)
  Pallas kernels  140 us (20%)
  blocking collectives  112 us (16%)
  starting transfers between devices  86.5 us (12%)
  local copies, waits for them, and re-layouts  76.6 us (11%)
  other arithmetic  41.8 us (6%)
  matrix products  19.2 us (3%)
  between operations  15.9 us (2%)
    all_to_all x11, waiting for transfers between devices, swap(): return lax.all_to_all(parts, axis, split_axis=0, concat_axis=0, tiled=True)  120 us
    all_to_all x3, blocking collectives, swap(): return lax.all_to_all(parts, axis, split_axis=0, concat_axis=0, tiled=True)  112 us
    pallas_call x2, Pallas kernels, run_experts(): pl.pallas_call(expert_kernel, out_shape=outs, grid=(1,), in_specs=[pl.Blo...  81.2 us
    all_to_all x11, starting transfers between devices, swap(): return lax.all_to_all(parts, axis, split_axis=0, concat_axis=0, tiled=True)  62.8 us
    unnamed x208, local copies, waits for them, and re-layouts  42.6 us
    reduce_scatter x2, waiting for transfers between devices, body(): moe = lax.psum_scatter(moe_part, FSDP, scatter_dimension=0, tiled=True)[0]  42.5 us
    pallas_call x2, Pallas kernels, attend_backward(): pl.pallas_call(attend_back_kernel, out_shape=outs, grid=(1,), in_specs=[w...  21.9 us
    pallas_call x1, Pallas kernels, expert_grads(): pl.pallas_call(expert_grad_kernel, out_shape=jax.ShapeDtypeStruct((pieces...  18.9 us
  transfers between devices with their start and end apart: 35, of which 14 were waited for; matrix products, arithmetic and copies ran while one was open for 15% of the time, Pallas kernels for 20%

profile of v3, /device:TPU:0, one launch (start us, length us, event | category | flops | bytes accessed | tf_op | source)
XLA Modules:
  0.0 688.2 jit_solution(2030222917297228743)
XLA Ops:
  20.2 9.4 %all-to-all-start = ((bf16[128,8,384]{2,1,0:T(8,128)(2,1)}), bf16[128,8,384]{2,1,0:T(8,128)(2,1)}, u32[]{:S(2)}, u32[]{:S(2)}) async-start(bf16[128,8,384]{2,1,0:T(8,128)(2,1)} %bitcast.7), calls=%async_computation | async-start | bytes 1572864 | tf_op jit(solution)/shard_map/all_to_all | solution.py:507
  41.1 11.9 %collective-permute-done.6 = bf16[1,256,1152]{2,1,0:T(8,128)(2,1)} collective-permute-done((bf16[1,256,1152]{2,1,0:T(8,128)(2,1)}, bf16[1,256,1152]{2,1,0:T(8,128)(2,1)}, u32[]{:S(2)}, u32[]{:S(2)}) %collective-permute-start.6) | collective-permute-done | bytes 589856 | tf_op jit(solution)/shard_map/ppermute | solution.py:515
  70.8 12.3 %collective-permute-done.2.before_ref = bf16[2,128,1024]{2,1,0:T(8,128)(2,1)} collective-permute-done((bf16[2,128,1024]{2,1,0:T(8,128)(2,1)S(1)}, bf16[2,128,1024]{2,1,0:T(8,128)(2,1)}, u32[]{:S(2)}, u32[]{:S(2)}) %collective-permute-start.2) | collective-permute-done | bytes 524320 | tf_op jit(solution)/shard_map/ppermute | solution.py:520
  87.5 5.3 collective-permute-done.15.far_low_ref
  96.5 8.8 %shard_map.248 = (bf16[1024,128]{1,0:T(8,128)(2,1)S(1)}, bf16[1024,1024]{1,0:T(8,128)(2,1)S(1)}, bf16[1024,128]{1,0:T(8,128)(2,1)S(1)}, bf16[1024,128]{1,0:T(8,128)(2,1)S(1)}) custom-call(s32[8]{0:T(128)S(1)} %fusion.64.order_ref, bf16[2,128,1024]{2,1,0:T(8,128)(2,1)S(1)} %copy-done.16, bf16[2,128,1024]{2,1,0:T(8,128)(2,1)} %collective-permute-done.13.after_ref, ...), custom_call_target="tpu_custom_call" | custom-call | flops 12000000000 | bytes 8388608 | tf_op jit(solution)/shard_map/pallas_call | solution.py:243
  125.2 6.6 all-to-all-start.2
  131.9 8.8 %shard_map.246 = (bf16[1024,128]{1,0:T(8,128)(2,1)S(1)}, bf16[1024,1024]{1,0:T(8,128)(2,1)S(1)}, bf16[1024,128]{1,0:T(8,128)(2,1)S(1)}, bf16[1024,128]{1,0:T(8,128)(2,1)S(1)}) custom-call(s32[8]{0:T(128)S(1)} %fusion.64.order_ref, bf16[2,128,1024]{2,1,0:T(8,128)(2,1)S(1)} %pad_maximum_fusion.3.own_ref, ...), custom_call_target="tpu_custom_call" | custom-call | flops 12000000000 | bytes 8388608 | tf_op jit(solution)/shard_map/pallas_call | solution.py:243
  151.7 11.1 %all-to-all-done.2 = bf16[128,8,1024]{2,1,0:T(8,128)(2,1)} async-done(((bf16[128,8,1024]{2,1,0:T(8,128)(2,1)}), bf16[128,8,1024]{2,1,0:T(8,128)(2,1)}, u32[]{:S(2)}, u32[]{:S(2)}) %all-to-all-start.2) | async-done | bytes 2097184 | tf_op jit(solution)/shard_map/all_to_all | solution.py:507
  162.8 4.0 all-to-all-start.1
  169.0 8.9 %all-to-all-done.1 = bf16[8,128,128]{1,2,0:T(8,128)(2,1)S(1)} async-done(((bf16[8,128,128]{1,2,0:T(8,128)(2,1)}), bf16[8,128,128]{1,2,0:T(8,128)(2,1)S(1)}, u32[]{:S(2)}, u32[]{:S(2)}) %all-to-all-start.1) | async-done | bytes 262176 | tf_op jit(solution)/shard_map/all_to_all | solution.py:507
  181.2 33.8 %all_to_all.70.x_own_ref = bf16[8,128,1024]{2,1,0:T(8,128)(2,1)S(1)} all-to-all(bf16[8,128,1024]{2,1,0:T(8,128)(2,1)S(1)} %broadcast_in_dim.49), channel_id=1, replica_groups=mesh['z'=4,'yl'=2,'yh'=2,'x'=4,'core'=2] {'yh','x'}, dimensions={0} | all-to-all | bytes 4194304 | tf_op jit(solution)/shard_map/all_to_all | solution.py:507
  219.4 4.5 all-to-all-start.5
  224.5 40.2 %shard_map.247 = (bf16[16,128,1024]{2,1,0:T(8,128)(2,1)}, bf16[8,128,1152]{2,1,0:T(8,128)(2,1)}, bf16[8,128,1152]{2,1,0:T(8,128)(2,1)}, bf16[2,768,1024]{2,1,0:T...) custom-call(s32[10]{0:T(128)} %pad_add_fusion.scalar_ref, ...), custom_call_target="tpu_custom_call" | custom-call | flops 40000000000 | bytes 41943040 | tf_op jit(solution)/shard_map/pallas_call | solution.py:430
  265.4 4.2 collective-permute-done.18
  269.6 3.8 add_convert_fusion.1
  274.8 41.0 %shard_map.249 = (bf16[16,128,1024]{2,1,0:T(8,128)(2,1)}, bf16[8,128,1152]{2,1,0:T(8,128)(2,1)}, bf16[8,128,1152]{2,1,0:T(8,128)(2,1)}, bf16[2,768,1024]{2,1,0:T...) custom-call(s32[10]{0:T(128)} %pad_add_fusion.scalar_ref, ...), custom_call_target="tpu_custom_call" | custom-call | flops 40000000000 | bytes 41943040 | tf_op jit(solution)/shard_map/pallas_call | solution.py:430
  316.0 9.0 %all-to-all-start.6 = ((bf16[8,128,1152]{2,1,0:T(8,128)(2,1)}), bf16[8,128,1152]{2,1,0:T(8,128)(2,1)S(1)}, u32[]{:S(2)}, u32[]{:S(2)}) async-start(bf16[8,128,1152]{2,1,0:T(8,128)(2,1)} %add_convert_fusion.1), calls=%async_computation.8 | async-start | bytes 4718592 | tf_op jit(solution)/shard_map/all_to_all | solution.py:507
  325.0 4.5 add_convert_fusion
  329.5 31.2 %all-to-all-done.6 = bf16[8,128,1152]{2,1,0:T(8,128)(2,1)S(1)} async-done(((bf16[8,128,1152]{2,1,0:T(8,128)(2,1)}), bf16[8,128,1152]{2,1,0:T(8,128)(2,1)S(1)}, u32[]{:S(2)}, u32[]{:S(2)}) %all-to-all-start.6) | async-done | bytes 2359328 | tf_op jit(solution)/shard_map/all_to_all | solution.py:507
  362.1 6.1 all-to-all-start.9
  377.5 18.9 %shard_map.252 = bf16[8,6,128,512]{3,2,1,0:T(8,128)(2,1)} custom-call(bf16[2,768,1024]{2,1,0:T(8,128)(2,1)} %get-tuple-element.72.xe0, bf16[2,768,1024]{2,1,0:T(8,128)(2,1)} %get-tuple-element.74.xe1, bf16[2,768,1024]{2,1,0:T(8,128)(2,1)} %get-tuple-element.75.de0, bf16[2,768,1024]{2,1,0:T(8,128)(2,1)} %get-tuple-element.76.de1, ...), custom_call_target="tpu_custom_call" | custom-call | flops 14000000000 | bytes 29360128 | tf_op jit(solution)/shard_map/pallas_call | solution.py:470
  406.3 42.5 %reduce-scatter.6.cloned.1.call-done = bf16[1,128,1024]{2,1,0:T(8,128)(2,1)} async-done(((bf16[16,128,1024]{2,1,0:T(8,128)(2,1)}), bf16[1,128,1024]{2,1,0:T(8,128)(2,1)}) %reduce-scatter.6.cloned.1.call-update) | async-done | bytes 262160 | tf_op jit(solution)/shard_map/reduce_scatter | solution.py:684
  455.4 4.5 all-to-all-start.7
  463.1 7.3 %all-to-all-done.7 = bf16[8,128,128]{2,1,0:T(8,128)(2,1)S(1)} async-done(((bf16[8,128,128]{2,1,0:T(8,128)(2,1)}), bf16[8,128,128]{2,1,0:T(8,128)(2,1)S(1)}, u32[]{:S(2)}, u32[]{:S(2)}) %all-to-all-start.7) | async-done | bytes 262176 | tf_op jit(solution)/shard_map/all_to_all | solution.py:507
  482.6 10.8 %shard_map.250 = (bf16[1024,1024]{1,0:T(8,128)(2,1)S(1)}, f32[1024,256]{1,0:T(8,128)S(1)}, f32[1,1024]{1,0:T(1,128)S(1)}, f32[1,256]{1,0:T(1,128)S(1)}) custom-call(bf16[1024,1024]{1,0:T(8,128)(2,1)S(1)} %copy-done.29, bf16[1024,128]{1,0:T(8,128)(2,1)S(1)} %copy-done.35, bf16[1024,128]{1,0:T(8,128)(2,1)S(1)} %copy-done.37, bf16[1024,128]{1,0:T(8,128)(2,1)S(1)} %bitcast.198, ...), custom_call_target="tpu_custom_call" | custom-call | flops 24999999488 | bytes 8388608 | tf_op jit(solution)/shard_map/pallas_call | solution.py:267
  501.3 11.1 %shard_map.251 = (bf16[1024,1024]{1,0:T(8,128)(2,1)S(1)}, f32[1024,256]{1,0:T(8,128)S(1)}, f32[1,1024]{1,0:T(1,128)S(1)}, f32[1,256]{1,0:T(1,128)S(1)}) custom-call(bf16[1024,1024]{1,0:T(8,128)(2,1)S(1)} %copy-done.27, bf16[1024,128]{1,0:T(8,128)(2,1)S(1)} %copy-done.31, bf16[1024,128]{1,0:T(8,128)(2,1)S(1)} %copy-done.33, bf16[1024,128]{1,0:T(8,128)(2,1)S(1)} %bitcast.197, ...), custom_call_target="tpu_custom_call" | custom-call | flops 24999999488 | bytes 8388608 | tf_op jit(solution)/shard_map/pallas_call | solution.py:267
  517.8 24.8 %all_to_all.71 = bf16[128,8,384]{2,1,0:T(8,128)(2,1)} all-to-all(bf16[128,8,384]{2,1,0:T(8,128)(2,1)S(1)} %pad_maximum_fusion.2), channel_id=1, replica_groups=mesh['z'=4,'yl'=2,'yh'=2,'x'=4,'core'=2] {'z','yl','yh','x','core'}, dimensions={0} | all-to-all | bytes 1572864 | tf_op jit(solution)/shard_map/all_to_all | solution.py:507
  542.7 53.7 %all_to_all.72 = bf16[8,128,1024]{2,1,0:T(8,128)(2,1)} all-to-all(bf16[8,128,1024]{2,1,0:T(8,128)(2,1)S(1)} %bitcast.195), channel_id=1, replica_groups=mesh['z'=4,'yl'=2,'yh'=2,'x'=4,'core'=2] {'z','yl'}, dimensions={0} | all-to-all | bytes 4194304 | tf_op jit(solution)/shard_map/all_to_all | solution.py:507
  596.3 5.0 all-to-all-start.11
  606.6 33.5 %all-to-all-done.11 = bf16[8,128,1024]{2,1,0:T(8,128)(2,1)} async-done(((bf16[8,128,1024]{2,1,0:T(8,128)(2,1)}), bf16[8,128,1024]{2,1,0:T(8,128)(2,1)}, u32[]{:S(2)}, u32[]{:S(2)}) %all-to-all-start.11) | async-done | bytes 2097184 | tf_op jit(solution)/shard_map/all_to_all | solution.py:507
  640.0 6.4 all-to-all-start.13
  655.1 21.3 %all-to-all-done.13 = bf16[128,8,1024]{2,1,0:T(8,128)(2,1)} async-done(((bf16[128,8,1024]{2,1,0:T(8,128)(2,1)}), bf16[128,8,1024]{2,1,0:T(8,128)(2,1)}, u32[]{:S(2)}, u32[]{:S(2)}) %all-to-all-start.13) | async-done | bytes 2097184 | tf_op jit(solution)/shard_map/all_to_all | solution.py:507
  (379 shorter events, 167.0 us)
Async XLA Ops:
  7.2 217.3 %all-gather.3.cloned.1.call-start = ((), (), s32[]{:S(2)}) async-start(), calls=%async_computation.20 | async-start | bytes 7077888 | tf_op jit(solution)/shard_map/all_gather | solution.py:614
  8.5 28.3 %collective-permute-start = (bf16[1,128,1024]{2,1,0:T(8,128)(2,1)S(1)}, bf16[1,128,1024]{2,1,0:T(8,128)(2,1)}, u32[]{:S(2)}, u32[]{:S(2)}) collective-permute-start(bf16[1,128,1024]{2,1,0:T(8,128)(2,1)S(1)} %get-tuple-element.200), channel_id=1, source_target_pairs={{0,16},{16,0},{1,17},{17,1},{2,18},{18,2},{3,19},{19,3},{4,20},{20... | collective-permute-start | bytes 786440 | tf_op jit(solution)/shard_map/ppermute | solution.py:515
  10.2 22.0 %collective-permute-start.12 = (bf16[1,128,1024]{2,1,0:T(8,128)(2,1)S(1)}, bf16[1,128,1024]{2,1,0:T(8,128)(2,1)}, u32[]{:S(2)}, u32[]{:S(2)}) collective-permute-start(bf16[1,128,1024]{2,1,0:T(8,128)(2,1)S(1)} %get-tuple-element.201), channel_id=1, source_target_pairs={{0,16},{16,0},{1,17},{17,1},{2,18},{18,2},{3,19},{19,3},{4,20},{20... | collective-permute-start | bytes 786440 | tf_op jit(solution)/shard_map/ppermute | solution.py:515
  13.7 39.3 %collective-permute-start.6 = (bf16[1,256,1152]{2,1,0:T(8,128)(2,1)}, bf16[1,256,1152]{2,1,0:T(8,128)(2,1)}, u32[]{:S(2)}, u32[]{:S(2)}) collective-permute-start(bf16[1,256,1152]{2,1,0:T(8,128)(2,1)} %fusion.31), channel_id=1, source_target_pairs={{0,8},{8,0},{1,9},{9,1},{2,10},{10,2},{3,11},{11,3},{4,12},{12,4},... | collective-permute-start | bytes 1769480 | tf_op jit(solution)/shard_map/ppermute | solution.py:515
  20.2 39.2 %all-to-all-start = ((bf16[128,8,384]{2,1,0:T(8,128)(2,1)}), bf16[128,8,384]{2,1,0:T(8,128)(2,1)}, u32[]{:S(2)}, u32[]{:S(2)}) async-start(bf16[128,8,384]{2,1,0:T(8,128)(2,1)} %bitcast.7), calls=%async_computation | async-start | bytes 1572864 | tf_op jit(solution)/shard_map/all_to_all | solution.py:507
  33.5 27.0 %collective-permute-start.14 = (bf16[2,128,1024]{2,1,0:T(8,128)(2,1)S(1)}, bf16[2,128,1024]{2,1,0:T(8,128)(2,1)}, u32[]{:S(2)}, u32[]{:S(2)}) collective-permute-start(bf16[2,128,1024]{2,1,0:T(8,128)(2,1)S(1)} %pad_maximum_fusion.4.own_ref), channel_id=1, source_target_pairs={{0,32},{32,64},{64,96},{96,0},{1,33},{33,65},{65,97},{97,1},{2,34}... | collective-permute-start | bytes 1572872 | tf_op jit(solution)/shard_map/ppermute | solution.py:520
  34.5 27.6 %collective-permute-start.13 = (bf16[2,128,1024]{2,1,0:T(8,128)(2,1)S(1)}, bf16[2,128,1024]{2,1,0:T(8,128)(2,1)}, u32[]{:S(2)}, u32[]{:S(2)}) collective-permute-start(bf16[2,128,1024]{2,1,0:T(8,128)(2,1)S(1)} %pad_maximum_fusion.4.own_ref), channel_id=1, source_target_pairs={{0,96},{32,0},{64,32},{96,64},{1,97},{33,1},{65,33},{97,65},{2,98}... | collective-permute-start | bytes 1572872 | tf_op jit(solution)/shard_map/ppermute | solution.py:521
  37.8 45.4 %collective-permute-start.2 = (bf16[2,128,1024]{2,1,0:T(8,128)(2,1)S(1)}, bf16[2,128,1024]{2,1,0:T(8,128)(2,1)}, u32[]{:S(2)}, u32[]{:S(2)}) collective-permute-start(bf16[2,128,1024]{2,1,0:T(8,128)(2,1)S(1)} %pad_maximum_fusion.3.own_ref), channel_id=1, source_target_pairs={{0,32},{32,64},{64,96},{96,0},{1,33},{33,65},{65,97},{97,1},{2,34}... | collective-permute-start | bytes 1572872 | tf_op jit(solution)/shard_map/ppermute | solution.py:520
  37.8 47.0 %collective-permute-start.1 = (bf16[2,128,1024]{2,1,0:T(8,128)(2,1)S(1)}, bf16[2,128,1024]{2,1,0:T(8,128)(2,1)}, u32[]{:S(2)}, u32[]{:S(2)}) collective-permute-start(bf16[2,128,1024]{2,1,0:T(8,128)(2,1)S(1)} %pad_maximum_fusion.3.own_ref), channel_id=1, source_target_pairs={{0,96},{32,0},{64,32},{96,64},{1,97},{33,1},{65,33},{97,65},{2,98}... | collective-permute-start | bytes 1572872 | tf_op jit(solution)/shard_map/ppermute | solution.py:521
  55.3 59.3 %collective-permute-start.8 = (bf16[2,256,1152]{2,1,0:T(8,128)(2,1)}, bf16[2,256,1152]{2,1,0:T(8,128)(2,1)}, u32[]{:S(2)}, u32[]{:S(2)}) collective-permute-start(bf16[2,256,1152]{2,1,0:T(8,128)(2,1)} %pad_maximum_fusion), channel_id=1, source_target_pairs={{0,2},{2,4},{4,6},{6,0},{1,3},{3,5},{5,7},{7,1},{8,10},{10,12},{12... | collective-permute-start | bytes 3538952 | tf_op jit(solution)/shard_map/ppermute | solution.py:520
  62.1 30.7 %collective-permute-start.15 = (bf16[1,128,1024]{2,1,0:T(8,128)(2,1)}, bf16[1,128,1024]{2,1,0:T(8,128)(2,1)S(1)}, u32[]{:S(2)}, u32[]{:S(2)}) collective-permute-start(bf16[1,128,1024]{2,1,0:T(8,128)(2,1)} %slice.222), channel_id=1, source_target_pairs={{0,32},{32,64},{64,96},{96,0},{1,33},{33,65},{65,97},{97,1},{2,34}... | collective-permute-start | bytes 786440 | tf_op jit(solution)/shard_map/ppermute | solution.py:522
  63.8 30.7 %collective-permute-start.16 = (bf16[1,128,1024]{2,1,0:T(8,128)(2,1)}, bf16[1,128,1024]{2,1,0:T(8,128)(2,1)}, u32[]{:S(2)}, u32[]{:S(2)}) collective-permute-start(bf16[1,128,1024]{2,1,0:T(8,128)(2,1)} %slice.223), channel_id=1, source_target_pairs={{0,96},{32,0},{64,32},{96,64},{1,97},{33,1},{65,33},{97,65},{2,98}... | collective-permute-start | bytes 786440 | tf_op jit(solution)/shard_map/ppermute | solution.py:523
  83.1 34.4 %collective-permute-start.7 = (bf16[2,256,1152]{2,1,0:T(8,128)(2,1)}, bf16[2,256,1152]{2,1,0:T(8,128)(2,1)}, u32[]{:S(2)}, u32[]{:S(2)}) collective-permute-start(bf16[2,256,1152]{2,1,0:T(8,128)(2,1)} %pad_maximum_fusion), channel_id=1, source_target_pairs={{0,6},{2,0},{4,2},{6,4},{1,7},{3,1},{5,3},{7,5},{8,14},{10,8},{12,... | collective-permute-start | bytes 3538952 | tf_op jit(solution)/shard_map/ppermute | solution.py:521
  84.8 47.0 %collective-permute-start.3 = (bf16[1,128,1024]{2,1,0:T(8,128)(2,1)}, bf16[1,128,1024]{2,1,0:T(8,128)(2,1)}, u32[]{:S(2)}, u32[]{:S(2)}) collective-permute-start(bf16[1,128,1024]{2,1,0:T(8,128)(2,1)} %slice.210), channel_id=1, source_target_pairs={{0,32},{32,64},{64,96},{96,0},{1,33},{33,65},{65,97},{97,1},{2,34}... | collective-permute-start | bytes 786440 | tf_op jit(solution)/shard_map/ppermute | solution.py:522
  93.6 38.3 %collective-permute-start.4 = (bf16[1,128,1024]{2,1,0:T(8,128)(2,1)}, bf16[1,128,1024]{2,1,0:T(8,128)(2,1)}, u32[]{:S(2)}, u32[]{:S(2)}) collective-permute-start(bf16[1,128,1024]{2,1,0:T(8,128)(2,1)} %slice.211), channel_id=1, source_target_pairs={{0,96},{32,0},{64,32},{96,64},{1,97},{33,1},{65,33},{97,65},{2,98}... | collective-permute-start | bytes 786440 | tf_op jit(solution)/shard_map/ppermute | solution.py:523
  108.9 14.7 %all-to-all-start.4 = ((bf16[8,128,128]{1,2,0:T(8,128)(2,1)}), bf16[8,128,128]{1,2,0:T(8,128)(2,1)S(1)}, u32[]{:S(2)}, u32[]{:S(2)}) async-start(bf16[8,128,128]{1,2,0:T(8,128)(2,1)} %copy.227), calls=%async_computation.5 | async-start | bytes 524288 | tf_op jit(solution)/shard_map/all_to_all | solution.py:507
  116.5 28.8 %collective-permute-start.9 = (bf16[1,256,1152]{2,1,0:T(8,128)(2,1)}, bf16[1,256,1152]{2,1,0:T(8,128)(2,1)}, u32[]{:S(2)}, u32[]{:S(2)}) collective-permute-start(bf16[1,256,1152]{2,1,0:T(8,128)(2,1)} %slice.219), channel_id=1, source_target_pairs={{0,2},{2,4},{4,6},{6,0},{1,3},{3,5},{5,7},{7,1},{8,10},{10,12},{12... | collective-permute-start | bytes 1769480 | tf_op jit(solution)/shard_map/ppermute | solution.py:522
  119.5 27.7 %collective-permute-start.10 = (bf16[1,256,1152]{2,1,0:T(8,128)(2,1)}, bf16[1,256,1152]{2,1,0:T(8,128)(2,1)}, u32[]{:S(2)}, u32[]{:S(2)}) collective-permute-start(bf16[1,256,1152]{2,1,0:T(8,128)(2,1)} %slice.220), channel_id=1, source_target_pairs={{0,6},{2,0},{4,2},{6,4},{1,7},{3,1},{5,3},{7,5},{8,14},{10,8},{12,... | collective-permute-start | bytes 1769480 | tf_op jit(solution)/shard_map/ppermute | solution.py:523
  125.2 37.6 %all-to-all-start.2 = ((bf16[128,8,1024]{2,1,0:T(8,128)(2,1)}), bf16[128,8,1024]{2,1,0:T(8,128)(2,1)}, u32[]{:S(2)}, u32[]{:S(2)}) async-start(bf16[128,8,1024]{2,1,0:T(8,128)(2,1)} %broadcast_in_dim.48), calls=%async_computation.2 | async-start | bytes 4194304 | tf_op jit(solution)/shard_map/all_to_all | solution.py:507
  151.7 72.8 %collective-permute-start.11 = (bf16[8,256,1152]{2,1,0:T(8,128)(2,1)}, bf16[8,256,1152]{2,1,0:T(8,128)(2,1)}, u32[]{:S(2)}, u32[]{:S(2)}) collective-permute-start(bf16[8,256,1152]{2,1,0:T(8,128)(2,1)} %constant_dynamic-update-slice_fusion.g_own_ref), channel_id=1, source_target_pairs={{0,1},{1,0},{2,3},{3,2},{4,5},{5,4},{6,7},{7,6},{8,9},{9,8},{10,11... | collective-permute-start | bytes 14155784 | tf_op jit(solution)/shard_map/ppermute | solution.py:515
  162.8 15.2 %all-to-all-start.1 = ((bf16[8,128,128]{1,2,0:T(8,128)(2,1)}), bf16[8,128,128]{1,2,0:T(8,128)(2,1)S(1)}, u32[]{:S(2)}, u32[]{:S(2)}) async-start(bf16[8,128,128]{1,2,0:T(8,128)(2,1)} %copy.220), calls=%async_computation.1 | async-start | bytes 524288 | tf_op jit(solution)/shard_map/all_to_all | solution.py:507
  215.1 9.3 %collective-permute-start.5 = (bf16[8,128,1024]{2,1,0:T(8,128)(2,1)S(1)}, bf16[8,128,1024]{2,1,0:T(8,128)(2,1)}, u32[]{:S(2)}, u32[]{:S(2)}) collective-permute-start(bf16[8,128,1024]{2,1,0:T(8,128)(2,1)S(1)} %all_to_all.70.x_own_ref), channel_id=1, source_target_pairs={{0,1},{1,0},{2,3},{3,2},{4,5},{5,4},{6,7},{7,6},{8,9},{9,8},{10,11... | collective-permute-start | bytes 6291464 | tf_op jit(solution)/shard_map/ppermute | solution.py:515
  219.4 45.6 %all-to-all-start.5 = ((bf16[8,128,1024]{2,1,0:T(8,128)(2,1)}), bf16[8,128,1024]{2,1,0:T(8,128)(2,1)}, u32[]{:S(2)}, u32[]{:S(2)}) async-start(bf16[8,128,1024]{2,1,0:T(8,128)(2,1)} %broadcast_in_dim.51), calls=%async_computation.6 | async-start | bytes 4194304 | tf_op jit(solution)/shard_map/all_to_all | solution.py:507
  223.9 182.5 %reduce-scatter.4.cloned.1.call-start = ((), (), s32[]{:S(2)}) async-start(), calls=%async_computation.17 | async-start | bytes 4456448 | tf_op jit(solution)/shard_map/reduce_scatter | solution.py:684
  264.9 183.9 %reduce-scatter.6.cloned.1.call-start = ((), (), s32[]{:S(2)}) async-start(), calls=%async_computation.18 | async-start | bytes 4456448 | tf_op jit(solution)/shard_map/reduce_scatter | solution.py:684
  316.0 44.6 %all-to-all-start.6 = ((bf16[8,128,1152]{2,1,0:T(8,128)(2,1)}), bf16[8,128,1152]{2,1,0:T(8,128)(2,1)S(1)}, u32[]{:S(2)}, u32[]{:S(2)}) async-start(bf16[8,128,1152]{2,1,0:T(8,128)(2,1)} %add_convert_fusion.1), calls=%async_computation.8 | async-start | bytes 4718592 | tf_op jit(solution)/shard_map/all_to_all | solution.py:507
  362.1 36.4 %all-to-all-start.9 = ((bf16[8,128,1152]{2,1,0:T(8,128)(2,1)}), bf16[8,128,1152]{2,1,0:T(8,128)(2,1)}, u32[]{:S(2)}, u32[]{:S(2)}) async-start(bf16[8,128,1152]{2,1,0:T(8,128)(2,1)} %add_convert_fusion), calls=%async_computation.11 | async-start | bytes 4718592 | tf_op jit(solution)/shard_map/all_to_all | solution.py:507
  368.3 310.7 %reduce-scatter.8.cloned.1.call-start = ((), (), s32[]{:S(2)}) async-start(), calls=%async_computation.19 | async-start | bytes 7077888 | tf_op jit(solution)/shard_map/reduce_scatter | solution.py:732
  455.4 15.0 %all-to-all-start.7 = ((bf16[8,128,128]{2,1,0:T(8,128)(2,1)}), bf16[8,128,128]{2,1,0:T(8,128)(2,1)S(1)}, u32[]{:S(2)}, u32[]{:S(2)}) async-start(bf16[8,128,128]{2,1,0:T(8,128)(2,1)} %bitcast.192), calls=%async_computation.9 | async-start | bytes 524288 | tf_op jit(solution)/shard_map/all_to_all | solution.py:507
  470.4 23.2 %all-to-all-start.10 = ((bf16[8,128,128]{2,1,0:T(8,128)(2,1)}), bf16[8,128,128]{2,1,0:T(8,128)(2,1)S(1)}, u32[]{:S(2)}, u32[]{:S(2)}) async-start(bf16[8,128,128]{2,1,0:T(8,128)(2,1)} %bitcast.190), calls=%async_computation.12 | async-start | bytes 524288 | tf_op jit(solution)/shard_map/all_to_all | solution.py:507
  596.3 43.7 %all-to-all-start.11 = ((bf16[8,128,1024]{2,1,0:T(8,128)(2,1)}), bf16[8,128,1024]{2,1,0:T(8,128)(2,1)}, u32[]{:S(2)}, u32[]{:S(2)}) async-start(bf16[8,128,1024]{2,1,0:T(8,128)(2,1)} %bitcast.196), calls=%async_computation.13 | async-start | bytes 4194304 | tf_op jit(solution)/shard_map/all_to_all | solution.py:507
  640.0 36.4 %all-to-all-start.13 = ((bf16[128,8,1024]{2,1,0:T(8,128)(2,1)}), bf16[128,8,1024]{2,1,0:T(8,128)(2,1)}, u32[]{:S(2)}, u32[]{:S(2)}) async-start(bf16[128,8,1024]{2,1,0:T(8,128)(2,1)} %fusion.8), calls=%async_computation.15 | async-start | bytes 4194304 | tf_op jit(solution)/shard_map/all_to_all | solution.py:507
  (104 other events, 1827.5 us)
Sparse Core Ops, SparseCore 0:
  18.1 194.5 all-gather.2
  265.0 100.9 reduce-scatter.3
  370.6 78.1 reduce-scatter.5
  451.1 177.2 reduce-scatter.7

commit v4 on v3

--- a/solution.py
+++ b/solution.py
@@ -283,44 +283,54 @@
     return high, (v - high.astype(F32)).astype(BF)
 
 
-def expert_kernel(
-    scalar_ref,
-    x_own_ref,
-    x_other_ref,
-    g_own_ref,
-    g_other_ref,
-    router_ref,
-    w_ref,
-    out_ref,
-    back_own_ref,
-    back_other_ref,
-    xe_ref,
-    de_ref,
-    act_ref,
-    da_ref,
-    db_ref,
-    pick_ref,
-    weight_ref,
-    dgate_ref,
-    eo_ref,
-    dr_ref,
-):
+def expert_kernel(scalar_ref, *refs, joined):
+    x_own_ref, x_other_ref, g_ref, router_ref = refs[:4]
+    first_pieces, second_pieces = refs[4:9], refs[9:11]
+    refs = refs[11:]
+    if joined:
+        out_ref, refs = refs[0], refs[1:]
+    else:
+        (out_own_ref, out_other_ref), refs = refs[:2], refs[2:]
+    back_own_ref, back_other_ref, xe_ref, de_ref, act_ref, da_ref, db_ref = refs[:7]
+    pick_ref, weight_ref, dgate_ref, eo_ref, dr_ref, w_ref = refs[7:]
     half, tok, width = x_own_ref.shape
     sources = 2 * half
     core = scalar_ref[1]
+    depth = w_ref.shape[2] // 8
+
+    def place(expert, r, ref, i):
+        rows = pl.ds(pl.multiple_of(scalar_ref[2 + r] * depth, depth), depth)
+        w_ref[expert, :, rows] = ref[i]
+
+    both_ref, after_ref, far_low_ref, far_high_ref, before_ref = first_pieces
+    for r, (ref, i) in enumerate(
+        [
+            (both_ref, 0),
+            (both_ref, 1),
+            (after_ref, 0),
+            (after_ref, 1),
+            (far_low_ref, 0),
+            (far_high_ref, 0),
+            (before_ref, 0),
+            (before_ref, 1),
+        ]
+    ):
+        place(0, r, ref, i)
+    for r in range(8):
+        place(1, r, second_pieces[r % 2], r // 2)
     local, slots, hidden = act_ref.shape
     cap = slots // sources
     first = scalar_ref[0]
     lane = lax.broadcasted_iota(jnp.int32, (tok, 128), 1)
-    place = lax.broadcasted_iota(jnp.int32, (tok, local * cap), 1)
+    spot = lax.broadcasted_iota(jnp.int32, (tok, local * cap), 1)
     row_expert = lax.broadcasted_iota(jnp.int32, (local * cap, 128), 0) // cap
     slot_lane = lax.broadcasted_iota(jnp.int32, (local * cap, 128), 1)
     own_lane = slot_lane == first + row_expert
 
-    def fetch(i, carry, x_ref, g_ref, offset):
+    def fetch(i, carry, x_ref, offset, column):
         s = i + offset
         x = x_ref[i]
-        from_g = scalar_ref[i + 2]
+        from_g = 2 * i + column
         held = g_ref[from_g, :, width:].astype(F32)
         chosen = held >= 0.0
         logits = jnp.where(chosen, dot(x, router_ref[...], 1, 0), -1e30)
@@ -331,7 +341,7 @@
         for e in range(local):
             mine = jnp.max(jnp.where(lane == first + e, held, -1.0), axis=1, keepdims=True)
             goal = jnp.where(mine >= 0.0, mine + e * cap, -1.0).astype(jnp.int32)
-            pick = jnp.where(place == goal, 1.0, pick)
+            pick = jnp.where(spot == goal, 1.0, pick)
         pick = pick.astype(BF)
         pick_ref[s] = pick
         rows = pl.ds(pl.multiple_of(s * cap, 16), cap)
@@ -347,18 +357,18 @@
             weight_ref[e, rows] = weight[part]
         return carry
 
-    for x_ref, g_ref, offset in ((x_own_ref, g_own_ref, 0), (x_other_ref, g_other_ref, half)):
+    for x_ref, offset, column in ((x_own_ref, 0, core), (x_other_ref, half, 1 - core)):
         lax.fori_loop(
-            0, half, functools.partial(fetch, x_ref=x_ref, g_ref=g_ref, offset=offset), 0
+            0, half, functools.partial(fetch, x_ref=x_ref, offset=offset, column=column), 0
         )
     chunk = 256
 
     def work(i, carry):
         e = i // (slots // chunk)
         rows = pl.ds(pl.multiple_of((i % (slots // chunk)) * chunk, chunk), chunk)
-        w_gate = w_ref[:, 0, e].reshape(width, hidden)
-        w_up = w_ref[:, 1, e].reshape(width, hidden)
-        w_down = w_ref[:, 2, e].reshape(width, hidden)
+        w_gate = w_ref[e, 0]
+        w_up = w_ref[e, 1]
+        w_down = w_ref[e, 2]
         x = xe_ref[e, rows]
         a = dot(x, w_gate, 1, 0)
         b = dot(x, w_up, 1, 0)
@@ -384,7 +394,7 @@
 
     lax.fori_loop(0, local * (slots // chunk), work, 0)
 
-    def give(i, carry, back_ref, offset, column):
+    def give(i, carry, back_ref, part_ref, offset, column):
         s = i + offset
         rows = pl.ds(pl.multiple_of(s * cap, 16), cap)
         pick = pick_ref[s]
@@ -395,26 +405,32 @@
         spread = jnp.where(own_lane, high.astype(F32), 0.0) + jnp.where(
             slot_lane == first + row_expert + 64, low.astype(F32), 0.0
         )
-        out_ref[2 * i + column] = dot(pick, eo, 1, 0).astype(BF)
+        part_ref[2 * i + column if joined else i] = dot(pick, eo, 1, 0).astype(BF)
         back_ref[i, :, :width] = dot(pick, dr, 1, 0).astype(BF)
         back_ref[i, :, width:] = dot(pick, spread.astype(BF), 1, 0).astype(BF)
         return carry
 
-    for back_ref, offset, column in ((back_own_ref, 0, core), (back_other_ref, half, 1 - core)):
-        lax.fori_loop(
-            0, half, functools.partial(give, back_ref=back_ref, offset=offset, column=column), 0
-        )
-
-
-def run_experts(scalars, x_own, x_other, g_own, g_other, micro, router, weights, cap):
+    parts = (out_ref, out_ref) if joined else (out_own_ref, out_other_ref)
+    for back_ref, part_ref, offset, column in (
+        (back_own_ref, parts[0], 0, core),
+        (back_other_ref, parts[1], half, 1 - core),
+    ):
+        step = functools.partial(
+            give, back_ref=back_ref, part_ref=part_ref, offset=offset, column=column
+        )
+        lax.fori_loop(0, half, step, 0)
+
+
+def run_experts(scalars, x_own, x_other, g_all, micro, router, first, second, cap, joined):
     half, tok, width = x_own.shape
     sources = 2 * half
-    local, hidden = weights.shape[2], weights.shape[4]
+    local = 2
+    hidden = second[0].shape[3]
     slots = sources * cap
-    wide = g_own.shape[2]
+    wide = g_all.shape[2]
     shape = jax.ShapeDtypeStruct
-    outs = [
-        shape((sources, tok, width), BF),
+    outs = [shape((sources, tok, width), BF)] if joined else [shape((half, tok, width), BF)] * 2
+    outs = outs + [
         shape((half, tok, wide), BF),
         shape((half, tok, wide), BF),
         shape((local, slots, width), BF),
@@ -424,15 +440,14 @@
         shape((local, slots, hidden), BF),
     ]
     g_spec = pl.BlockSpec(
-        (half, tok, wide), lambda i: (0, micro, 0), pipeline_mode=pl.Buffered(1)
-    )
-    args = [router, weights]
+        (sources, tok, wide), lambda i: (0, micro, 0), pipeline_mode=pl.Buffered(1)
+    )
+    args = [router, *first, *second]
     return pl.pallas_call(
-        expert_kernel,
+        functools.partial(expert_kernel, joined=joined),
         out_shape=outs,
         grid=(1,),
-        in_specs=[pl.BlockSpec(memory_space=pltpu.SMEM), whole(x_own), whole(x_other)]
-        + [g_spec, g_spec]
+        in_specs=[pl.BlockSpec(memory_space=pltpu.SMEM), whole(x_own), whole(x_other), g_spec]
         + [whole(a) for a in args],
         out_specs=[whole(o) for o in outs],
         scratch_shapes=[
@@ -441,10 +456,11 @@
             pltpu.VMEM((local, slots, 1), F32),
             pltpu.VMEM((local, slots, width), BF),
             pltpu.VMEM((local, slots, width), BF),
+            pltpu.VMEM((local, 3, width, hidden), BF),
         ],
-        compiler_params=pltpu.CompilerParams(vmem_limit_bytes=56 * 1024 * 1024),
+        compiler_params=pltpu.CompilerParams(vmem_limit_bytes=60 * 1024 * 1024),
         cost_estimate=pl.CostEstimate(flops=40 * 10**9, bytes_accessed=40 << 20, transcendentals=0),
-    )(scalars, x_own, x_other, g_own, g_other, *args)
+    )(scalars, x_own, x_other, g_all, *args)
 
 
 def expert_grad_kernel(xe0, xe1, de0, de1, act0, act1, da0, da1, db0, db1, out_ref):
@@ -507,21 +523,34 @@
     return lax.all_to_all(parts, axis, split_axis=0, concat_axis=0, tiled=True)
 
 
-def spread(block, axis, copies):
-    return swap(jnp.broadcast_to(block[None], (copies,) + block.shape), axis)
-
-
 def flip(block, axis):
     return lax.ppermute(block, axis, FLIP)
 
 
-def pair_and_ring(block, pair, ring):
-    both = jnp.concatenate([block, flip(block, pair)], axis=0)
-    before = lax.ppermute(both, ring, UP)
-    after = lax.ppermute(both, ring, DOWN)
-    far_low = lax.ppermute(before[:1], ring, UP)
-    far_high = lax.ppermute(after[1:], ring, DOWN)
+def ring_of(both):
+    before = lax.ppermute(both, "z", UP)
+    after = lax.ppermute(both, "z", DOWN)
+    far_low = lax.ppermute(before[:1], "z", UP)
+    far_high = lax.ppermute(after[1:], "z", DOWN)
     return [both, after, far_low, far_high, before]
+
+
+class Exchange:
+    def __init__(self):
+        self.last = None
+
+    def __call__(self, parts, axis):
+        if self.last is not None:
+            parts = after_all(parts, self.last)
+        self.last = swap(parts, axis)
+        return self.last
+
+    def copies(self, block, axis, count):
+        return self(jnp.broadcast_to(block[None], (count,) + block.shape), axis)
+
+
+def sum_parts(parts):
+    return jnp.sum(parts.astype(F32), axis=0)
 
 
 def after_all(value, *others):
@@ -573,6 +602,7 @@
     heads = ratio * DH
     span = heads + 2 * DH
 
+    exchange = Exchange()
     small = jnp.concatenate(
         [
             w_router,
@@ -593,7 +623,7 @@
         axis=2,
     ).transpose(1, 0, 2)
     pieces = jnp.broadcast_to(pieces[:, None], (n_ctx, n_fsdp) + pieces.shape[1:])
-    head_all = swap(pieces.reshape((n_all,) + pieces.shape[2:]), ALL).reshape(width, -1)
+    head_all = exchange(pieces.reshape((n_all,) + pieces.shape[2:]), ALL).reshape(width, -1)
     w_heads = head_all[:, :span]
     small_all = head_all[:, span:]
     router = small_all[:, :experts]
@@ -607,11 +637,32 @@
     )[None]
     router_pad = jnp.pad(router, ((0, 0), (0, 128 - experts)))
 
-    seq_rows = [pair_and_ring(tokens[m], "yl", "z") for m in range(micro)]
-    w_out = after_all(w_out, head_all)
-    out_full = spread(w_out, ALL, n_all).reshape(width, width)
-
-    expert_all = lax.all_gather(jnp.stack([w_gate, w_up, w_down]), CTX, axis=0)
+    own = exchange.copies(w_out, CTX + GROUP, n_all // 2)
+    other = flip(own, "core")
+    out_full = jnp.where(
+        core == 0, jnp.stack([own, other], axis=1), jnp.stack([other, own], axis=1)
+    ).reshape(width, width)
+
+    both = [jnp.concatenate([tokens[m], flip(tokens[m], "yl")], axis=0) for m in range(micro)]
+    seq_rows = [ring_of(both[0])]
+    seq_rows.append(ring_of(after_all(both[1], seq_rows[0][1], seq_rows[0][4])))
+
+    stack = jnp.stack([w_gate, w_up, w_down], axis=1)
+    second_own = after_all(stack[1:], seq_rows[1][1], seq_rows[1][4])
+    second_before = lax.ppermute(second_own, "z", UP)
+    second_after = lax.ppermute(second_own, "z", DOWN)
+    half = stack.shape[2] // 2
+    second_far = jnp.concatenate(
+        [
+            lax.ppermute(second_before[:, :, :half], "z", UP),
+            lax.ppermute(second_after[:, :, half:], "z", DOWN),
+        ],
+        axis=2,
+    )
+    second_near = jnp.concatenate([second_own, second_after, second_far, second_before], axis=0)
+    second = [second_near, flip(second_near, "yl")]
+    first_own = jnp.concatenate([stack[:1], flip(stack[:1], "yl")], axis=0)
+    first = ring_of(after_all(first_own, second_before, second_after))
 
     expert_ids = jnp.arange(experts, dtype=jnp.int32)
     cot = cotangent.reshape(all_tok, width)
@@ -621,21 +672,17 @@
     counts = ein("ut,mte->mue", lower, chosen.reshape(micro, tok, experts).astype(BF))
     held = jnp.where(chosen, counts.reshape(all_tok, experts) - 1.0, -1.0)
     held = jnp.pad(held, ((0, 0), (0, 128 - experts)), constant_values=-1.0).astype(BF)
-    g_own = jnp.concatenate(
-        pair_and_ring(jnp.concatenate([cot, held], axis=1)[None], "yh", "x"), axis=0
-    )
-    g_other = flip(g_own, "core")
+    g_all = lax.all_gather(jnp.concatenate([cot, held], axis=1), FSDP, axis=0)
 
     cosine, sine = rope_tables(jnp.arange(length, dtype=jnp.int32))
     cosine = jnp.tile(cosine, (1, 4))
     sine = jnp.tile(jnp.concatenate([-sine, sine], axis=1), (1, 2))
     rel = jnp.arange(n_ctx, dtype=jnp.int32)
     order = ((z + rel // 2) % 4) * 2 + (yl + rel % 2) % 2
-    g_place = ((rel % 4 - x) % 4) * 2 + (rel // 4 - yh) % 2
-    scalars = jnp.concatenate([jnp.stack([shard * local, core]), g_place]).astype(jnp.int32)
+    scalars = jnp.concatenate([jnp.stack([shard * local, core]), order]).astype(jnp.int32)
 
     def to_owner(v):
-        return swap(v.reshape(n_ctx, tok, -1), CTX)
+        return exchange(v.reshape(n_ctx, tok, -1), CTX)
 
     def attention_args(m):
         seg = segments[m, 0]
@@ -645,6 +692,8 @@
     for m in range(micro):
         mixed_h, *keep = attend_forward(order, seq_rows[m], *attention_args(m))
         saved.append(keep)
+        if m == 0:
+            mixed_h = after_all(mixed_h, seq_rows[1][1], seq_rows[1][4])
         mixed = to_owner(mixed_h).transpose(1, 0, 2).reshape(tok, width)
         start = tokens[m, 0].astype(F32)
         middle = start + mm(mixed, out_full)
@@ -653,36 +702,28 @@
         chosen_m = chosen[m * tok : (m + 1) * tok]
         logits = jnp.where(chosen_m, mm(hidden_two, router), -1e30)
         gates = jnp.where(chosen_m, jax.nn.softmax(logits, axis=-1), 0.0)
-        x_own = spread(hidden_two, GROUP, n_ctx).reshape(n_ctx, tok, width)
-        x_other = flip(x_own, "core")
-        forward.append((mixed, middle, norm_back, hidden_two, gates, x_own, x_other))
-
-    outs, d_inputs, kept, grads = [], [], [], []
-    backs = []
-    for m in range(micro):
-        x_own, x_other = forward[m][5:]
-        if m:
-            x_other = after_all(x_other, *backs[-1][:1])
-        moe_part, back_own, back_other, *keep = run_experts(
+        x_own = exchange.copies(hidden_two, GROUP, n_ctx)
+        forward.append((mixed, middle, norm_back, hidden_two, gates, x_own))
+
+    def experts_of(m, x_own):
+        return run_experts(
             scalars,
             x_own,
-            x_other,
-            g_own,
-            g_other,
+            flip(x_own, "core"),
+            g_all,
             m,
             router_pad,
-            expert_all,
+            first,
+            second,
             cap,
-        )
-        kept.append(keep)
-        back = (back_own.astype(F32) + flip(back_other, "core").astype(F32)).astype(BF)
-        backs.append((back, moe_part))
-    for m in range(micro):
+            m == 0,
+        )
+
+    def back_sum(own, other):
+        return (own.astype(F32) + flip(other, "core").astype(F32)).astype(BF)
+
+    def middle_back(m, back):
         mixed, middle, norm_back, hidden_two, gates = forward[m][:5]
-        back, moe_part = backs[m]
-        back = jnp.sum(swap(back, GROUP).astype(F32), axis=0)
-        moe = lax.psum_scatter(moe_part, FSDP, scatter_dimension=0, tiled=True)[0]
-        outs.append((middle + moe.astype(F32)).astype(BF))
         grad_top = cot[m * tok : (m + 1) * tok].astype(F32)
         tail = back[:, width:]
         d_gates = tail[:, :experts] + tail[:, 64 : 64 + experts]
@@ -695,44 +736,84 @@
         d_branch = d_middle.astype(BF)
         grad_out = t_mm(mixed, d_branch)
         d_mixed = mm_t(d_branch, out_full).astype(BF)
-        d_mixed = swap(d_mixed.reshape(tok, n_ctx, heads).transpose(1, 0, 2), CTX)
+        d_mixed = d_mixed.reshape(tok, n_ctx, heads).transpose(1, 0, 2)
+        return d_middle, d_mixed, (grad_out, grad_router, grad_mlp)
+
+    def attention_back(m, d_mixed):
         d_hidden, grad_heads, grad_attn, grad_qk = attend_backward(
             *saved[m], d_mixed.reshape(length, heads), *attention_args(m)
         )
-        d_hidden = jnp.sum(to_owner(d_hidden).astype(F32), axis=0)
+        grad_qk = jnp.concatenate(
+            [grad_qk[0, :DH] + grad_qk[0, DH : 2 * DH], grad_qk[0, 2 * DH : 3 * DH]]
+        )
+        return d_hidden, (grad_heads, grad_attn[0], grad_qk)
+
+    def input_grad(m, d_hidden, d_middle):
         start = tokens[m, 0].astype(F32)
         inverse = lax.rsqrt(jnp.mean(start * start, axis=-1, keepdims=True) + EPS)
         u = d_hidden * gain_attn
-        d_inputs.append(
+        return (
             d_middle
             + inverse * u
             - start * (inverse**3 * jnp.mean(u * start, axis=-1, keepdims=True))
         )
-        grad_qk = jnp.concatenate(
-            [grad_qk[0, :DH] + grad_qk[0, DH : 2 * DH], grad_qk[0, 2 * DH : 3 * DH]]
-        )
-        grads.append((grad_out, grad_heads, grad_router, grad_attn[0], grad_mlp, grad_qk))
-    grad_out, grad_heads, grad_router, grad_attn, grad_mlp, grad_qk = jax.tree.map(
-        jnp.add, grads[0], grads[1]
-    )
-
-    grad_out = swap(grad_out.astype(BF).reshape(n_all, rows, width), ALL)
-    own_out = jnp.sum(grad_out.astype(F32), axis=0)
+
+    moe_0, back_own, back_other, *kept_0 = experts_of(0, forward[0][5])
+    x_1, back_own, back_other, moe_0 = lax.optimization_barrier(
+        (forward[1][5], back_own, back_other, moe_0)
+    )
+    back_0 = back_sum(back_own, back_other)
+    moe_0 = lax.psum_scatter(moe_0, FSDP, scatter_dimension=0, tiled=True)[0]
+    x_1 = after_all(x_1, back_0)
+    back_0 = exchange(back_0, GROUP)
+    moe_own, moe_other, back_own, back_other, *kept_1 = experts_of(1, x_1)
+    back_0, back_own, back_other, moe_own, moe_other = lax.optimization_barrier(
+        (back_0, back_own, back_other, moe_own, moe_other)
+    )
+    back_1 = back_sum(back_own, back_other)
+    d_middle_0, d_mixed_0, grads_0 = middle_back(0, sum_parts(back_0))
+    d_mixed_0 = exchange(d_mixed_0, CTX)
+    expert_sums = expert_grads((kept_0, kept_1), n_ctx)
+    back_1 = exchange(back_1, GROUP)
+    d_hidden_0, head_grads_0 = attention_back(0, d_mixed_0)
+    back_1, d_hidden_0, expert_sums, moe_0 = lax.optimization_barrier(
+        (back_1, d_hidden_0, expert_sums, moe_0)
+    )
+    expert_own = lax.psum_scatter(expert_sums, CTX, scatter_dimension=0, tiled=True)[0]
+    d_middle_1, d_mixed_1, grads_1 = middle_back(1, sum_parts(back_1))
+    d_mixed_1 = exchange(d_mixed_1, CTX)
+    moe_1 = back_sum(moe_own, moe_other)
+    d_hidden_0 = to_owner(d_hidden_0)
+    d_hidden_1, head_grads_1 = attention_back(1, d_mixed_1)
+    d_hidden_0, d_hidden_1 = lax.optimization_barrier((d_hidden_0, d_hidden_1))
+    d_hidden_1 = to_owner(d_hidden_1)
+    grad_out, grad_router, grad_mlp = jax.tree.map(jnp.add, grads_0, grads_1)
+    grad_heads, grad_attn, grad_qk = jax.tree.map(jnp.add, head_grads_0, head_grads_1)
+
     grad_qk = jnp.pad(grad_qk[:, None], ((0, 0), (0, rows - 1))).reshape(-1)
     grad_small = jnp.concatenate(
         [grad_router, grad_attn[:, None], grad_mlp[:, None], grad_qk[:, None]], axis=1
     )
     grad_small = jnp.pad(grad_small, ((0, 0), (0, 128 - grad_small.shape[1])))
     grad_pack = jnp.concatenate([grad_heads, grad_small], axis=1).astype(BF)
-    grad_pack = swap(grad_pack.reshape(n_all, rows, -1), ALL).astype(F32)
+    grad_pack = exchange(grad_pack.reshape(n_all, rows, -1), ALL).astype(F32)
     own_heads = jnp.sum(grad_pack[:, :, :span].reshape(n_ctx, n_fsdp, rows, -1), axis=1)
     own_heads = own_heads.transpose(1, 0, 2)
     own_small = jnp.sum(grad_pack[:, :, span:], axis=0)
-    kept[1][0] = after_all(kept[1][0], backs[1][0])
-    expert_own = lax.psum_scatter(
-        expert_grads(kept, n_ctx), CTX, scatter_dimension=0, tiled=True
-    )[0].astype(F32)
-    expert_own = expert_own.reshape((local, 3) + expert_own.shape[1:])
+    grad_out = grad_out.astype(BF).reshape(n_all // 2, 2, rows, width)
+    grad_own = lax.dynamic_index_in_dim(grad_out, core, axis=1, keepdims=False)
+    grad_other = lax.dynamic_index_in_dim(grad_out, 1 - core, axis=1, keepdims=False)
+    own_out = sum_parts(exchange(back_sum(grad_own, grad_other), CTX + GROUP))
+    moe_1 = sum_parts(exchange(moe_1, GROUP))
+    expert_own = expert_own.astype(F32).reshape((local, 3) + expert_own.shape[1:])
+    outs = [
+        (forward[0][1] + moe_0.astype(F32)).astype(BF),
+        (forward[1][1] + moe_1).astype(BF),
+    ]
+    d_inputs = [
+        input_grad(0, sum_parts(d_hidden_0), d_middle_0),
+        input_grad(1, sum_parts(d_hidden_1), d_middle_1),
+    ]
 
     return (
         jnp.stack(outs)[:, None],

time: 698 us -> 634 us (0.908)
  blocking collectives: 112 us -> 0 us
  starting transfers between devices: 86.5 us -> 123 us
  waiting for transfers between devices: 196 us -> 211 us
  local copies, waits for them, and re-layouts: 76.6 us -> 62.4 us
  other arithmetic: 41.8 us -> 55.9 us
    all_to_all x3 -> x0, blocking collectives: 112 us -> none  [swap(): return lax.all_to_all(parts, axis, split_axis=0, concat_axis=0, tiled=True)]
    all_to_all x11 -> x15, waiting for transfers between devices: 120 us -> 170 us  [swap(): return lax.all_to_all(parts, axis, split_axis=0, concat_axis=0, tiled=True)]
    reduce_scatter x3 -> x2, waiting for transfers between devices: 42.5 us -> 0.01 us  [the longest x1 0.01 us: body(): moe_0 = lax.psum_scatter(moe_0, FSDP, scatter_dimension=0, tiled=True)[0]]
    all_to_all x11 -> x15, starting transfers between devices: 62.8 us -> 93.9 us  [swap(): return lax.all_to_all(parts, axis, split_axis=0, concat_axis=0, tiled=True)]
    unnamed x208 -> x165, local copies, waits for them, and re-layouts: 42.6 us -> 30.3 us
    ppermute x12 -> x16, waiting for transfers between devices: 17.7 us -> 27 us  [the longest x3 18.6 us: ring_of(): before = lax.ppermute(both, 'z', UP)]
    convert_element_type x5 -> x8, other arithmetic: 9.98 us -> 18.3 us  [the longest x4 15.4 us: back_sum(): return (own.astype(F32) + flip(other, 'core').astype(F32)).astype(BF)]
    ppermute x12 -> x16, starting transfers between devices: 16.6 us -> 23.7 us  [the longest x3 7.64 us: ring_of(): after = lax.ppermute(both, 'z', DOWN)]
  transfers between devices with their start and end apart: 35 -> 45, of which waited for: 14 -> 15; matrix products, arithmetic and copies ran while one was open for 15% -> 15% of each run, Pallas kernels for 20% -> 23%
where the time goes in v4:
time: 634 us; the launch traced here: 625 us
  waiting for transfers between devices  211 us (33%)
  Pallas kernels  141 us (22%)
  starting transfers between devices  123 us (19%)
  local copies, waits for them, and re-layouts  62.4 us (10%)
  other arithmetic  55.9 us (9%)
  between operations  15.9 us (3%)
  matrix products  15.5 us (2%)
    all_to_all x15, waiting for transfers between devices, swap(): return lax.all_to_all(parts, axis, split_axis=0, concat_axis=0, tiled=True)  170 us
    all_to_all x15, starting transfers between devices, swap(): return lax.all_to_all(parts, axis, split_axis=0, concat_axis=0, tiled=True)  93.9 us
    pallas_call x2, Pallas kernels, run_experts(): pl.pallas_call(functools.partial(expert_kernel, joined=joined), out_shape...  80.7 us
    unnamed x165, local copies, waits for them, and re-layouts  30.3 us
    pallas_call x2, Pallas kernels, attend_backward(): pl.pallas_call(attend_back_kernel, out_shape=outs, grid=(1,), in_specs=[w...  24.5 us
    ppermute x3, waiting for transfers between devices, ring_of(): before = lax.ppermute(both, 'z', UP)  18.6 us
    pallas_call x1, Pallas kernels, expert_grads(): pl.pallas_call(expert_grad_kernel, out_shape=jax.ShapeDtypeStruct((pieces...  18.1 us
    pallas_call x2, Pallas kernels, attend_forward(): pl.pallas_call(attend_kernel, out_shape=outs, grid=(1,), in_specs=[pl.Blo...  17.5 us
  transfers between devices with their start and end apart: 45, of which 15 were waited for; matrix products, arithmetic and copies ran while one was open for 15% of the time, Pallas kernels for 23%

profile of v4, /device:TPU:0, one launch (start us, length us, event | category | flops | bytes accessed | tf_op | source)
XLA Modules:
  0.0 624.8 jit_solution(7826246975686728695)
XLA Ops:
  15.9 11.1 %all-to-all-start = ((bf16[128,8,384]{2,1,0:T(8,128)(2,1)}), bf16[128,8,384]{2,1,0:T(8,128)(2,1)S(1)}, u32[]{:S(2)}, u32[]{:S(2)}) async-start(bf16[128,8,384]{2,1,0:T(8,128)(2,1)} %bitcast.7), calls=%async_computation | async-start | bytes 1572864 | tf_op jit(solution)/shard_map/all_to_all | solution.py:523
  30.4 15.7 %all-to-all-done = bf16[128,8,384]{2,1,0:T(8,128)(2,1)S(1)} async-done(((bf16[128,8,384]{2,1,0:T(8,128)(2,1)}), bf16[128,8,384]{2,1,0:T(8,128)(2,1)S(1)}, u32[]{:S(2)}, u32[]{:S(2)}) %all-to-all-start) | async-done | bytes 786464 | tf_op jit(solution)/shard_map/all_to_all | solution.py:523
  47.4 5.5 all-to-all-start.1
  60.2 18.6 %collective-permute-done.2.before_ref = bf16[2,128,1024]{2,1,0:T(8,128)(2,1)S(1)} collective-permute-done((bf16[2,128,1024]{2,1,0:T(8,128)(2,1)S(1)}, bf16[2,128,1024]{2,1,0:T(8,128)(2,1)S(1)}, u32[]{:S(2)}, u32[]{:S(2)}) %collective-permute-start.2) | collective-permute-done | bytes 524320 | tf_op jit(solution)/shard_map/ppermute | solution.py:531
  93.5 8.8 %shard_map.246 = (bf16[1024,128]{1,0:T(8,128)(2,1)S(1)}, bf16[1024,1024]{1,0:T(8,128)(2,1)S(1)}, bf16[1024,128]{1,0:T(8,128)(2,1)S(1)}, bf16[1024,128]{1,0:T(8,128)(2,1)S(1)}) custom-call(s32[8]{0:T(128)S(1)} %fusion.37.order_ref, bf16[2,128,1024]{2,1,0:T(8,128)(2,1)S(1)} %pad_maximum_fusion.4.own_ref, ...), custom_call_target="tpu_custom_call" | custom-call | flops 12000000000 | bytes 8388608 | tf_op jit(solution)/shard_map/pallas_call | solution.py:243
  105.8 5.6 all-to-all-start.2
  124.2 6.3 %all-to-all-start.3 = ((bf16[8,128,1024]{2,1,0:T(8,128)(2,1)}), bf16[8,128,1024]{2,1,0:T(8,128)(2,1)}, u32[]{:S(2)}, u32[]{:S(2)}) async-start(bf16[8,128,1024]{2,1,0:T(8,128)(2,1)} %broadcast_in_dim.47), calls=%async_computation.3 | async-start | bytes 4194304 | tf_op jit(solution)/shard_map/all_to_all | solution.py:523
  134.7 6.7 %collective-permute-done.14 = bf16[1,3,128,512]{3,2,1,0:T(8,128)(2,1)S(1)} collective-permute-done((bf16[1,3,128,512]{3,2,1,0:T(8,128)(2,1)S(1)}, bf16[1,3,128,512]{3,2,1,0:T(8,128)(2,1)S(1)}, u32[]{:S(2)}, u32[]{:S(2)}) %collective-permute-start.14) | collective-permute-done | bytes 393248 | tf_op jit(solution)/shard_map/ppermute | solution.py:653
  150.7 9.2 %collective-permute-done.12 = bf16[1,3,128,512]{3,2,1,0:T(8,128)(2,1)} collective-permute-done((bf16[1,3,128,512]{3,2,1,0:T(8,128)(2,1)}, bf16[1,3,128,512]{3,2,1,0:T(8,128)(2,1)}, u32[]{:S(2)}, u32[]{:S(2)}) %collective-permute-start.12) | collective-permute-done | bytes 393248 | tf_op jit(solution)/shard_map/ppermute | solution.py:527
  170.8 8.7 %shard_map.247 = (bf16[1024,128]{1,0:T(8,128)(2,1)S(1)}, bf16[1024,1024]{1,0:T(8,128)(2,1)S(1)}, bf16[1024,128]{1,0:T(8,128)(2,1)S(1)}, bf16[1024,128]{1,0:T(8,128)(2,1)S(1)}) custom-call(s32[8]{0:T(128)S(1)} %fusion.37.order_ref, bf16[2,128,1024]{2,1,0:T(8,128)(2,1)S(1)} %pad_maximum_fusion.5.own_ref, ...), custom_call_target="tpu_custom_call" | custom-call | flops 12000000000 | bytes 8388608 | tf_op jit(solution)/shard_map/pallas_call | solution.py:243
  195.0 8.9 %all-to-all-done.4 = bf16[8,128,128]{1,2,0:T(8,128)(2,1)S(1)} async-done(((bf16[8,128,128]{1,2,0:T(8,128)(2,1)}), bf16[8,128,128]{1,2,0:T(8,128)(2,1)S(1)}, u32[]{:S(2)}, u32[]{:S(2)}) %all-to-all-start.4) | async-done | bytes 262176 | tf_op jit(solution)/shard_map/all_to_all | solution.py:523
  209.3 8.6 %all-to-all-start.5 = ((bf16[8,128,1024]{2,1,0:T(8,128)(2,1)}), bf16[8,128,1024]{2,1,0:T(8,128)(2,1)}, u32[]{:S(2)}, u32[]{:S(2)}) async-start(bf16[8,128,1024]{2,1,0:T(8,128)(2,1)} %broadcast_in_dim.48), calls=%async_computation.5 | async-start | bytes 4194304 | tf_op jit(solution)/shard_map/all_to_all | solution.py:523
  218.2 40.1 %shard_map.248 = (bf16[16,128,1024]{2,1,0:T(8,128)(2,1)}, bf16[8,128,1152]{2,1,0:T(8,128)(2,1)}, bf16[8,128,1152]{2,1,0:T(8,128)(2,1)}, bf16[2,768,1024]{2,1,0:T...) custom-call(s32[10]{0:T(128)} %pad_add_fusion.scalar_ref, ...), custom_call_target="tpu_custom_call" | custom-call | flops 40000000000 | bytes 41943040 | tf_op jit(solution)/shard_map/pallas_call | solution.py:446
  258.4 4.7 collective-permute-done.22
  267.6 7.3 %all-to-all-start.6 = ((bf16[8,128,1152]{2,1,0:T(8,128)(2,1)}), bf16[8,128,1152]{2,1,0:T(8,128)(2,1)}, u32[]{:S(2)}, u32[]{:S(2)}) async-start(bf16[8,128,1152]{2,1,0:T(8,128)(2,1)} %add_convert_fusion.1), calls=%async_computation.6 | async-start | bytes 4718592 | tf_op jit(solution)/shard_map/all_to_all | solution.py:523
  274.9 40.6 %shard_map.249 = (bf16[8,128,1024]{2,1,0:T(8,128)(2,1)}, bf16[8,128,1024]{2,1,0:T(8,128)(2,1)}, bf16[8,128,1152]{2,1,0:T(8,128)(2,1)}, bf16[8,128,1152]{2,1,0:T(...) custom-call(s32[10]{0:T(128)} %pad_add_fusion.scalar_ref, ...), custom_call_target="tpu_custom_call" | custom-call | flops 40000000000 | bytes 41943040 | tf_op jit(solution)/shard_map/pallas_call | solution.py:446
  329.1 18.1 %shard_map.251 = bf16[8,6,128,512]{3,2,1,0:T(8,128)(2,1)} custom-call(bf16[2,768,1024]{2,1,0:T(8,128)(2,1)} %get-tuple-element.112.xe0, bf16[2,768,1024]{2,1,0:T(8,128)(2,1)} %get-tuple-element.113.xe1, bf16[2,768,1024]{2,1,0:T(8,128)(2,1)} %get-tuple-element.114.de0, bf16[2,768,1024]{2,1,0:T(8,128)(2,1)} %get-tuple-element.115.de1, ...), custom_call_target="tpu_custom_call" | custom-call | flops 14000000000 | bytes 29360128 | tf_op jit(solution)/shard_map/pallas_call | solution.py:486
  351.7 8.2 %all-to-all-start.8 = ((bf16[8,128,1152]{2,1,0:T(8,128)(2,1)}), bf16[8,128,1152]{2,1,0:T(8,128)(2,1)}, u32[]{:S(2)}, u32[]{:S(2)}) async-start(bf16[8,128,1152]{2,1,0:T(8,128)(2,1)} %add_convert_fusion), calls=%async_computation.8 | async-start | bytes 4718592 | tf_op jit(solution)/shard_map/all_to_all | solution.py:523
  363.8 12.2 %shard_map.250 = (bf16[1024,1024]{1,0:T(8,128)(2,1)}, f32[1024,256]{1,0:T(8,128)S(1)}, f32[1,1024]{1,0:T(1,128)S(1)}, f32[1,256]{1,0:T(1,128)S(1)}) custom-call(bf16[1024,1024]{1,0:T(8,128)(2,1)S(1)} %copy-done.14, bf16[1024,128]{1,0:T(8,128)(2,1)S(1)} %copy-done.18, bf16[1024,128]{1,0:T(8,128)(2,1)S(1)} %copy-done.20, bf16[1024,128]{1,0:T(8,128)(2,1)S(1)} %bitcast.173, ...), custom_call_target="tpu_custom_call" | custom-call | flops 24999999488 | bytes 8388608 | tf_op jit(solution)/shard_map/pallas_call | solution.py:267
  376.0 15.4 %all-to-all-done.8 = bf16[8,128,1152]{2,1,0:T(8,128)(2,1)} async-done(((bf16[8,128,1152]{2,1,0:T(8,128)(2,1)}), bf16[8,128,1152]{2,1,0:T(8,128)(2,1)}, u32[]{:S(2)}, u32[]{:S(2)}) %all-to-all-start.8) | async-done | bytes 2359328 | tf_op jit(solution)/shard_map/all_to_all | solution.py:523
  403.4 4.8 all-to-all-start.9
  408.4 11.0 %all-to-all-done.9 = bf16[8,128,128]{2,1,0:T(8,128)(2,1)S(1)} async-done(((bf16[8,128,128]{2,1,0:T(8,128)(2,1)}), bf16[8,128,128]{2,1,0:T(8,128)(2,1)S(1)}, u32[]{:S(2)}, u32[]{:S(2)}) %all-to-all-start.9) | async-done | bytes 262176 | tf_op jit(solution)/shard_map/all_to_all | solution.py:523
  419.4 4.5 all-to-all-start.10
  429.5 12.2 %shard_map.252 = (bf16[1024,1024]{1,0:T(8,128)(2,1)}, f32[1024,256]{1,0:T(8,128)S(1)}, f32[1,1024]{1,0:T(1,128)S(1)}, f32[1,256]{1,0:T(1,128)S(1)}) custom-call(bf16[1024,1024]{1,0:T(8,128)(2,1)S(1)} %copy-done.16, bf16[1024,128]{1,0:T(8,128)(2,1)S(1)} %copy-done.22, bf16[1024,128]{1,0:T(8,128)(2,1)S(1)} %copy-done.24, bf16[1024,128]{1,0:T(8,128)(2,1)S(1)} %bitcast.174, ...), custom_call_target="tpu_custom_call" | custom-call | flops 24999999488 | bytes 8388608 | tf_op jit(solution)/shard_map/pallas_call | solution.py:267
  441.7 32.7 %all-to-all-done.10 = bf16[8,128,1024]{2,1,0:T(8,128)(2,1)} async-done(((bf16[8,128,1024]{2,1,0:T(8,128)(2,1)}), bf16[8,128,1024]{2,1,0:T(8,128)(2,1)}, u32[]{:S(2)}, u32[]{:S(2)}) %all-to-all-start.10) | async-done | bytes 2097184 | tf_op jit(solution)/shard_map/all_to_all | solution.py:523
  485.4 43.8 %all-to-all-done.11 = bf16[8,128,1024]{2,1,0:T(8,128)(2,1)} async-done(((bf16[8,128,1024]{2,1,0:T(8,128)(2,1)}), bf16[8,128,1024]{2,1,0:T(8,128)(2,1)}, u32[]{:S(2)}, u32[]{:S(2)}) %all-to-all-start.11) | async-done | bytes 2097184 | tf_op jit(solution)/shard_map/all_to_all | solution.py:523
  529.1 9.7 %all-to-all-start.12 = ((bf16[128,8,384]{2,1,0:T(8,128)(2,1)}), bf16[128,8,384]{2,1,0:T(8,128)(2,1)}, u32[]{:S(2)}, u32[]{:S(2)}) async-start(bf16[128,8,384]{2,1,0:T(8,128)(2,1)} %pad_maximum_fusion.3), calls=%async_computation.13 | async-start | bytes 1572864 | tf_op jit(solution)/shard_map/all_to_all | solution.py:523
  541.5 13.3 %all-to-all-done.12 = bf16[128,8,384]{2,1,0:T(8,128)(2,1)} async-done(((bf16[128,8,384]{2,1,0:T(8,128)(2,1)}), bf16[128,8,384]{2,1,0:T(8,128)(2,1)}, u32[]{:S(2)}, u32[]{:S(2)}) %all-to-all-start.12) | async-done | bytes 786464 | tf_op jit(solution)/shard_map/all_to_all | solution.py:523
  554.8 7.0 %all-to-all-start.13 = ((bf16[64,8,1024]{2,1,0:T(8,128)(2,1)}), bf16[64,8,1024]{2,1,0:T(8,128)(2,1)S(1)}, u32[]{:S(2)}, u32[]{:S(2)}) async-start(bf16[64,8,1024]{2,1,0:T(8,128)(2,1)} %fusion), calls=%async_computation.14 | async-start | bytes 2097152 | tf_op jit(solution)/shard_map/all_to_all | solution.py:523
  561.8 4.7 add_convert_fusion.3
  572.2 9.5 %all-to-all-done.13 = bf16[64,8,1024]{2,1,0:T(8,128)(2,1)S(1)} async-done(((bf16[64,8,1024]{2,1,0:T(8,128)(2,1)}), bf16[64,8,1024]{2,1,0:T(8,128)(2,1)S(1)}, u32[]{:S(2)}, u32[]{:S(2)}) %all-to-all-start.13) | async-done | bytes 1048608 | tf_op jit(solution)/shard_map/all_to_all | solution.py:523
  597.6 16.6 %all-to-all-done.14 = bf16[8,128,1024]{2,1,0:T(8,128)(2,1)S(1)} async-done(((bf16[8,128,1024]{2,1,0:T(8,128)(2,1)}), bf16[8,128,1024]{2,1,0:T(8,128)(2,1)S(1)}, u32[]{:S(2)}, u32[]{:S(2)}) %all-to-all-start.14) | async-done | bytes 2097184 | tf_op jit(solution)/shard_map/all_to_all | solution.py:523
  (362 shorter events, 178.7 us)
Async XLA Ops:
  7.2 211.0 %all-gather.3.cloned.1.call-start = ((), (), s32[]{:S(2)}) async-start(), calls=%async_computation.19 | async-start | bytes 10027008 | tf_op jit(solution)/shard_map/all_gather | solution.py:675
  15.9 30.3 %all-to-all-start = ((bf16[128,8,384]{2,1,0:T(8,128)(2,1)}), bf16[128,8,384]{2,1,0:T(8,128)(2,1)S(1)}, u32[]{:S(2)}, u32[]{:S(2)}) async-start(bf16[128,8,384]{2,1,0:T(8,128)(2,1)} %bitcast.7), calls=%async_computation | async-start | bytes 1572864 | tf_op jit(solution)/shard_map/all_to_all | solution.py:523
  27.1 25.8 %collective-permute-start = (bf16[1,128,1024]{2,1,0:T(8,128)(2,1)S(1)}, bf16[1,128,1024]{2,1,0:T(8,128)(2,1)S(1)}, u32[]{:S(2)}, u32[]{:S(2)}) collective-permute-start(bf16[1,128,1024]{2,1,0:T(8,128)(2,1)S(1)} %get-tuple-element.260), channel_id=1, source_target_pairs={{0,16},{16,0},{1,17},{17,1},{2,18},{18,2},{3,19},{19,3},{4,20},{20... | collective-permute-start | bytes 786440 | tf_op jit(solution)/shard_map/ppermute | solution.py:527
  28.1 30.0 %collective-permute-start.5 = (bf16[1,128,1024]{2,1,0:T(8,128)(2,1)S(1)}, bf16[1,128,1024]{2,1,0:T(8,128)(2,1)}, u32[]{:S(2)}, u32[]{:S(2)}) collective-permute-start(bf16[1,128,1024]{2,1,0:T(8,128)(2,1)S(1)} %get-tuple-element.261), channel_id=1, source_target_pairs={{0,16},{16,0},{1,17},{17,1},{2,18},{18,2},{3,19},{19,3},{4,20},{20... | collective-permute-start | bytes 786440 | tf_op jit(solution)/shard_map/ppermute | solution.py:527
  47.4 41.5 %all-to-all-start.1 = ((bf16[64,8,1024]{2,1,0:T(8,128)(2,1)}), bf16[64,8,1024]{2,1,0:T(8,128)(2,1)}, u32[]{:S(2)}, u32[]{:S(2)}) async-start(bf16[64,8,1024]{2,1,0:T(8,128)(2,1)} %broadcast_in_dim.46), calls=%async_computation.1 | async-start | bytes 2097152 | tf_op jit(solution)/shard_map/all_to_all | solution.py:523
  53.0 25.7 %collective-permute-start.2 = (bf16[2,128,1024]{2,1,0:T(8,128)(2,1)S(1)}, bf16[2,128,1024]{2,1,0:T(8,128)(2,1)S(1)}, u32[]{:S(2)}, u32[]{:S(2)}) collective-permute-start(bf16[2,128,1024]{2,1,0:T(8,128)(2,1)S(1)} %pad_maximum_fusion.4.own_ref), channel_id=1, source_target_pairs={{0,32},{32,64},{64,96},{96,0},{1,33},{33,65},{65,97},{97,1},{2,34}... | collective-permute-start | bytes 1572872 | tf_op jit(solution)/shard_map/ppermute | solution.py:531
  54.6 24.9 %collective-permute-start.1 = (bf16[2,128,1024]{2,1,0:T(8,128)(2,1)S(1)}, bf16[2,128,1024]{2,1,0:T(8,128)(2,1)}, u32[]{:S(2)}, u32[]{:S(2)}) collective-permute-start(bf16[2,128,1024]{2,1,0:T(8,128)(2,1)S(1)} %pad_maximum_fusion.4.own_ref), channel_id=1, source_target_pairs={{0,96},{32,0},{64,32},{96,64},{1,97},{33,1},{65,33},{97,65},{2,98}... | collective-permute-start | bytes 1572872 | tf_op jit(solution)/shard_map/ppermute | solution.py:532
  88.9 22.5 %collective-permute-start.8 = (bf16[64,8,1024]{2,1,0:T(8,128)(2,1)}, bf16[64,8,1024]{2,1,0:T(8,128)(2,1)}, u32[]{:S(2)}, u32[]{:S(2)}) collective-permute-start(bf16[64,8,1024]{2,1,0:T(8,128)(2,1)} %all-to-all-done.1), channel_id=1, source_target_pairs={{0,1},{1,0},{2,3},{3,2},{4,5},{5,4},{6,7},{7,6},{8,9},{9,8},{10,11... | collective-permute-start | bytes 3145736 | tf_op jit(solution)/shard_map/ppermute | solution.py:527
  124.2 45.6 %all-to-all-start.3 = ((bf16[8,128,1024]{2,1,0:T(8,128)(2,1)}), bf16[8,128,1024]{2,1,0:T(8,128)(2,1)}, u32[]{:S(2)}, u32[]{:S(2)}) async-start(bf16[8,128,1024]{2,1,0:T(8,128)(2,1)} %broadcast_in_dim.47), calls=%async_computation.3 | async-start | bytes 4194304 | tf_op jit(solution)/shard_map/all_to_all | solution.py:523
  134.4 25.5 %collective-permute-start.12 = (bf16[1,3,128,512]{3,2,1,0:T(8,128)(2,1)}, bf16[1,3,128,512]{3,2,1,0:T(8,128)(2,1)}, u32[]{:S(2)}, u32[]{:S(2)}) collective-permute-start(bf16[1,3,128,512]{3,2,1,0:T(8,128)(2,1)} %get-tuple-element.257), channel_id=1, source_target_pairs={{0,16},{16,0},{1,17},{17,1},{2,18},{18,2},{3,19},{19,3},{4,20},{20... | collective-permute-start | bytes 1179656 | tf_op jit(solution)/shard_map/ppermute | solution.py:527
  146.4 22.7 %collective-permute-start.9 = (bf16[1,128,1024]{2,1,0:T(8,128)(2,1)S(1)}, bf16[1,128,1024]{2,1,0:T(8,128)(2,1)S(1)}, u32[]{:S(2)}, u32[]{:S(2)}) collective-permute-start(bf16[1,128,1024]{2,1,0:T(8,128)(2,1)S(1)} %slice.237), channel_id=1, source_target_pairs={{0,32},{32,64},{64,96},{96,0},{1,33},{33,65},{65,97},{97,1},{2,34}... | collective-permute-start | bytes 786440 | tf_op jit(solution)/shard_map/ppermute | solution.py:533
  147.6 22.2 %collective-permute-start.10 = (bf16[1,128,1024]{2,1,0:T(8,128)(2,1)S(1)}, bf16[1,128,1024]{2,1,0:T(8,128)(2,1)}, u32[]{:S(2)}, u32[]{:S(2)}) collective-permute-start(bf16[1,128,1024]{2,1,0:T(8,128)(2,1)S(1)} %slice.238), channel_id=1, source_target_pairs={{0,96},{32,0},{64,32},{96,64},{1,97},{33,1},{65,33},{97,65},{2,98}... | collective-permute-start | bytes 786440 | tf_op jit(solution)/shard_map/ppermute | solution.py:534
  162.0 26.9 %collective-permute-start.16 = (bf16[2,3,128,512]{3,2,1,0:T(8,128)(2,1)}, bf16[2,3,128,512]{3,2,1,0:T(8,128)(2,1)}, u32[]{:S(2)}, u32[]{:S(2)}) collective-permute-start(bf16[2,3,128,512]{3,2,1,0:T(8,128)(2,1)} %pad_maximum_fusion.2.refs_4_), channel_id=1, source_target_pairs={{0,32},{32,64},{64,96},{96,0},{1,33},{33,65},{65,97},{97,1},{2,34}... | collective-permute-start | bytes 2359304 | tf_op jit(solution)/shard_map/ppermute | solution.py:531
  162.5 29.3 %collective-permute-start.15 = (bf16[2,3,128,512]{3,2,1,0:T(8,128)(2,1)}, bf16[2,3,128,512]{3,2,1,0:T(8,128)(2,1)}, u32[]{:S(2)}, u32[]{:S(2)}) collective-permute-start(bf16[2,3,128,512]{3,2,1,0:T(8,128)(2,1)} %pad_maximum_fusion.2.refs_4_), channel_id=1, source_target_pairs={{0,96},{32,0},{64,32},{96,64},{1,97},{33,1},{65,33},{97,65},{2,98}... | collective-permute-start | bytes 2359304 | tf_op jit(solution)/shard_map/ppermute | solution.py:532
  167.5 50.6 %collective-permute-start.21 = (bf16[4,3,128,512]{3,2,1,0:T(8,128)(2,1)}, bf16[4,3,128,512]{3,2,1,0:T(8,128)(2,1)}, u32[]{:S(2)}, u32[]{:S(2)}) collective-permute-start(bf16[4,3,128,512]{3,2,1,0:T(8,128)(2,1)} %pad_maximum_fusion.refs_9_), channel_id=1, source_target_pairs={{0,16},{16,0},{1,17},{17,1},{2,18},{18,2},{3,19},{19,3},{4,20},{20... | collective-permute-start | bytes 4718600 | tf_op jit(solution)/shard_map/ppermute | solution.py:527
  169.8 48.4 %collective-permute-start.11 = (bf16[8,128,1024]{2,1,0:T(8,128)(2,1)}, bf16[8,128,1024]{2,1,0:T(8,128)(2,1)}, u32[]{:S(2)}, u32[]{:S(2)}) collective-permute-start(bf16[8,128,1024]{2,1,0:T(8,128)(2,1)} %all-to-all-done.3.refs_0_), channel_id=1, source_target_pairs={{0,1},{1,0},{2,3},{3,2},{4,5},{5,4},{6,7},{7,6},{8,9},{9,8},{10,11... | collective-permute-start | bytes 6291464 | tf_op jit(solution)/shard_map/ppermute | solution.py:527
  189.9 28.3 %collective-permute-start.17 = (bf16[1,3,128,512]{3,2,1,0:T(8,128)(2,1)S(1)}, bf16[1,3,128,512]{3,2,1,0:T(8,128)(2,1)}, u32[]{:S(2)}, u32[]{:S(2)}) collective-permute-start(bf16[1,3,128,512]{3,2,1,0:T(8,128)(2,1)S(1)} %slice.243), channel_id=1, source_target_pairs={{0,32},{32,64},{64,96},{96,0},{1,33},{33,65},{65,97},{97,1},{2,34}... | collective-permute-start | bytes 1179656 | tf_op jit(solution)/shard_map/ppermute | solution.py:533
  193.6 24.5 %collective-permute-start.18 = (bf16[1,3,128,512]{3,2,1,0:T(8,128)(2,1)}, bf16[1,3,128,512]{3,2,1,0:T(8,128)(2,1)}, u32[]{:S(2)}, u32[]{:S(2)}) collective-permute-start(bf16[1,3,128,512]{3,2,1,0:T(8,128)(2,1)} %slice.244), channel_id=1, source_target_pairs={{0,96},{32,0},{64,32},{96,64},{1,97},{33,1},{65,33},{97,65},{2,98}... | collective-permute-start | bytes 1179656 | tf_op jit(solution)/shard_map/ppermute | solution.py:534
  209.3 49.0 %all-to-all-start.5 = ((bf16[8,128,1024]{2,1,0:T(8,128)(2,1)}), bf16[8,128,1024]{2,1,0:T(8,128)(2,1)}, u32[]{:S(2)}, u32[]{:S(2)}) async-start(bf16[8,128,1024]{2,1,0:T(8,128)(2,1)} %broadcast_in_dim.48), calls=%async_computation.5 | async-start | bytes 4194304 | tf_op jit(solution)/shard_map/all_to_all | solution.py:523
  217.9 158.1 %reduce-scatter.3.cloned.1.call-start = ((), (), s32[]{:S(2)}) async-start(), calls=%async_computation.17 | async-start | bytes 4456448 | tf_op jit(solution)/shard_map/reduce_scatter | solution.py:766
  267.6 47.9 %all-to-all-start.6 = ((bf16[8,128,1152]{2,1,0:T(8,128)(2,1)}), bf16[8,128,1152]{2,1,0:T(8,128)(2,1)}, u32[]{:S(2)}, u32[]{:S(2)}) async-start(bf16[8,128,1152]{2,1,0:T(8,128)(2,1)} %add_convert_fusion.1), calls=%async_computation.6 | async-start | bytes 4718592 | tf_op jit(solution)/shard_map/all_to_all | solution.py:523
  315.6 31.7 %collective-permute-start.24 = (bf16[8,128,1152]{2,1,0:T(8,128)(2,1)}, bf16[8,128,1152]{2,1,0:T(8,128)(2,1)}, u32[]{:S(2)}, u32[]{:S(2)}) collective-permute-start(bf16[8,128,1152]{2,1,0:T(8,128)(2,1)} %get-tuple-element.104), channel_id=1, source_target_pairs={{0,1},{1,0},{2,3},{3,2},{4,5},{5,4},{6,7},{7,6},{8,9},{9,8},{10,11... | collective-permute-start | bytes 7077896 | tf_op jit(solution)/shard_map/ppermute | solution.py:527
  321.1 30.6 %all-to-all-start.7 = ((bf16[8,128,128]{2,1,0:T(8,128)(2,1)}), bf16[8,128,128]{2,1,0:T(8,128)(2,1)S(1)}, u32[]{:S(2)}, u32[]{:S(2)}) async-start(bf16[8,128,128]{2,1,0:T(8,128)(2,1)} %bitcast.170), calls=%async_computation.7 | async-start | bytes 524288 | tf_op jit(solution)/shard_map/all_to_all | solution.py:523
  351.7 39.8 %all-to-all-start.8 = ((bf16[8,128,1152]{2,1,0:T(8,128)(2,1)}), bf16[8,128,1152]{2,1,0:T(8,128)(2,1)}, u32[]{:S(2)}, u32[]{:S(2)}) async-start(bf16[8,128,1152]{2,1,0:T(8,128)(2,1)} %add_convert_fusion), calls=%async_computation.8 | async-start | bytes 4718592 | tf_op jit(solution)/shard_map/all_to_all | solution.py:523
  359.8 255.7 %reduce-scatter.5.cloned.1.call-start = ((), (), s32[]{:S(2)}) async-start(), calls=%async_computation.18 | async-start | bytes 7077888 | tf_op jit(solution)/shard_map/reduce_scatter | solution.py:782
  393.1 168.7 %collective-permute-start.25 = (bf16[8,128,1024]{2,1,0:T(8,128)(2,1)}, bf16[8,128,1024]{2,1,0:T(8,128)(2,1)}, u32[]{:S(2)}, u32[]{:S(2)}) collective-permute-start(bf16[8,128,1024]{2,1,0:T(8,128)(2,1)} %get-tuple-element.125), channel_id=1, source_target_pairs={{0,1},{1,0},{2,3},{3,2},{4,5},{5,4},{6,7},{7,6},{8,9},{9,8},{10,11... | collective-permute-start | bytes 6291464 | tf_op jit(solution)/shard_map/ppermute | solution.py:527
  419.4 55.0 %all-to-all-start.10 = ((bf16[8,128,1024]{2,1,0:T(8,128)(2,1)}), bf16[8,128,1024]{2,1,0:T(8,128)(2,1)}, u32[]{:S(2)}, u32[]{:S(2)}) async-start(bf16[8,128,1024]{2,1,0:T(8,128)(2,1)} %bitcast.57), calls=%async_computation.11 | async-start | bytes 4194304 | tf_op jit(solution)/shard_map/all_to_all | solution.py:523
  474.4 54.7 %all-to-all-start.11 = ((bf16[8,128,1024]{2,1,0:T(8,128)(2,1)}), bf16[8,128,1024]{2,1,0:T(8,128)(2,1)}, u32[]{:S(2)}, u32[]{:S(2)}) async-start(bf16[8,128,1024]{2,1,0:T(8,128)(2,1)} %bitcast.58), calls=%async_computation.12 | async-start | bytes 4194304 | tf_op jit(solution)/shard_map/all_to_all | solution.py:523
  483.0 55.8 %collective-permute-start.26 = (bf16[64,8,1024]{2,1,0:T(8,128)(2,1)}, bf16[64,8,1024]{2,1,0:T(8,128)(2,1)}, u32[]{:S(2)}, u32[]{:S(2)}) collective-permute-start(bf16[64,8,1024]{2,1,0:T(8,128)(2,1)} %dynamic-slice_bitcast_fusion), channel_id=1, source_target_pairs={{0,1},{1,0},{2,3},{3,2},{4,5},{5,4},{6,7},{7,6},{8,9},{9,8},{10,11... | collective-permute-start | bytes 3145736 | tf_op jit(solution)/shard_map/ppermute | solution.py:527
  529.1 25.7 %all-to-all-start.12 = ((bf16[128,8,384]{2,1,0:T(8,128)(2,1)}), bf16[128,8,384]{2,1,0:T(8,128)(2,1)}, u32[]{:S(2)}, u32[]{:S(2)}) async-start(bf16[128,8,384]{2,1,0:T(8,128)(2,1)} %pad_maximum_fusion.3), calls=%async_computation.13 | async-start | bytes 1572864 | tf_op jit(solution)/shard_map/all_to_all | solution.py:523
  554.8 26.9 %all-to-all-start.13 = ((bf16[64,8,1024]{2,1,0:T(8,128)(2,1)}), bf16[64,8,1024]{2,1,0:T(8,128)(2,1)S(1)}, u32[]{:S(2)}, u32[]{:S(2)}) async-start(bf16[64,8,1024]{2,1,0:T(8,128)(2,1)} %fusion), calls=%async_computation.14 | async-start | bytes 2097152 | tf_op jit(solution)/shard_map/all_to_all | solution.py:523
  582.7 31.5 %all-to-all-start.14 = ((bf16[8,128,1024]{2,1,0:T(8,128)(2,1)}), bf16[8,128,1024]{2,1,0:T(8,128)(2,1)S(1)}, u32[]{:S(2)}, u32[]{:S(2)}) async-start(bf16[8,128,1024]{2,1,0:T(8,128)(2,1)} %add_convert_fusion.3), calls=%async_computation.15 | async-start | bytes 4194304 | tf_op jit(solution)/shard_map/all_to_all | solution.py:523
  (93 other events, 996.4 us)
Sparse Core Ops, SparseCore 0:
  10.4 95.6 all-gather.2
  267.7 81.6 reduce-scatter.2
  391.6 201.2 reduce-scatter.4

commit v5 on v4

--- a/solution.py
+++ b/solution.py
@@ -283,41 +283,19 @@
     return high, (v - high.astype(F32)).astype(BF)
 
 
-def expert_kernel(scalar_ref, *refs, joined):
+def expert_kernel(scalar_ref, *refs):
     x_own_ref, x_other_ref, g_ref, router_ref = refs[:4]
-    first_pieces, second_pieces = refs[4:9], refs[9:11]
-    refs = refs[11:]
-    if joined:
-        out_ref, refs = refs[0], refs[1:]
-    else:
-        (out_own_ref, out_other_ref), refs = refs[:2], refs[2:]
-    back_own_ref, back_other_ref, xe_ref, de_ref, act_ref, da_ref, db_ref = refs[:7]
-    pick_ref, weight_ref, dgate_ref, eo_ref, dr_ref, w_ref = refs[7:]
+    pieces, refs = refs[4:12], refs[12:]
+    out_ref, back_own_ref, back_other_ref, xe_ref, de_ref, act_ref, da_ref, db_ref = refs[:8]
+    pick_ref, weight_ref, dgate_ref, eo_ref, dr_ref, w_ref = refs[8:]
     half, tok, width = x_own_ref.shape
     sources = 2 * half
     core = scalar_ref[1]
     depth = w_ref.shape[2] // 8
 
-    def place(expert, r, ref, i):
+    for r, ref in enumerate(pieces):
         rows = pl.ds(pl.multiple_of(scalar_ref[2 + r] * depth, depth), depth)
-        w_ref[expert, :, rows] = ref[i]
-
-    both_ref, after_ref, far_low_ref, far_high_ref, before_ref = first_pieces
-    for r, (ref, i) in enumerate(
-        [
-            (both_ref, 0),
-            (both_ref, 1),
-            (after_ref, 0),
-            (after_ref, 1),
-            (far_low_ref, 0),
-            (far_high_ref, 0),
-            (before_ref, 0),
-            (before_ref, 1),
-        ]
-    ):
-        place(0, r, ref, i)
-    for r in range(8):
-        place(1, r, second_pieces[r % 2], r // 2)
+        w_ref[:, :, rows] = ref[...]
     local, slots, hidden = act_ref.shape
     cap = slots // sources
     first = scalar_ref[0]
@@ -394,7 +372,7 @@
 
     lax.fori_loop(0, local * (slots // chunk), work, 0)
 
-    def give(i, carry, back_ref, part_ref, offset, column):
+    def give(i, carry, back_ref, offset, column):
         s = i + offset
         rows = pl.ds(pl.multiple_of(s * cap, 16), cap)
         pick = pick_ref[s]
@@ -405,32 +383,26 @@
         spread = jnp.where(own_lane, high.astype(F32), 0.0) + jnp.where(
             slot_lane == first + row_expert + 64, low.astype(F32), 0.0
         )
-        part_ref[2 * i + column if joined else i] = dot(pick, eo, 1, 0).astype(BF)
+        out_ref[2 * i + column] = dot(pick, eo, 1, 0).astype(BF)
         back_ref[i, :, :width] = dot(pick, dr, 1, 0).astype(BF)
         back_ref[i, :, width:] = dot(pick, spread.astype(BF), 1, 0).astype(BF)
         return carry
 
-    parts = (out_ref, out_ref) if joined else (out_own_ref, out_other_ref)
-    for back_ref, part_ref, offset, column in (
-        (back_own_ref, parts[0], 0, core),
-        (back_other_ref, parts[1], half, 1 - core),
-    ):
-        step = functools.partial(
-            give, back_ref=back_ref, part_ref=part_ref, offset=offset, column=column
-        )
-        lax.fori_loop(0, half, step, 0)
-
-
-def run_experts(scalars, x_own, x_other, g_all, micro, router, first, second, cap, joined):
+    for back_ref, offset, column in ((back_own_ref, 0, core), (back_other_ref, half, 1 - core)):
+        lax.fori_loop(
+            0, half, functools.partial(give, back_ref=back_ref, offset=offset, column=column), 0
+        )
+
+
+def run_experts(scalars, x_own, x_other, g_all, micro, router, pieces, cap):
     half, tok, width = x_own.shape
     sources = 2 * half
-    local = 2
-    hidden = second[0].shape[3]
+    local, _, _, hidden = pieces[0].shape
     slots = sources * cap
     wide = g_all.shape[2]
     shape = jax.ShapeDtypeStruct
-    outs = [shape((sources, tok, width), BF)] if joined else [shape((half, tok, width), BF)] * 2
-    outs = outs + [
+    outs = [
+        shape((sources, tok, width), BF),
         shape((half, tok, wide), BF),
         shape((half, tok, wide), BF),
         shape((local, slots, width), BF),
@@ -442,9 +414,9 @@
     g_spec = pl.BlockSpec(
         (sources, tok, wide), lambda i: (0, micro, 0), pipeline_mode=pl.Buffered(1)
     )
-    args = [router, *first, *second]
+    args = [router, *pieces]
     return pl.pallas_call(
-        functools.partial(expert_kernel, joined=joined),
+        expert_kernel,
         out_shape=outs,
         grid=(1,),
         in_specs=[pl.BlockSpec(memory_space=pltpu.SMEM), whole(x_own), whole(x_other), g_spec]
@@ -463,35 +435,53 @@
     )(scalars, x_own, x_other, g_all, *args)
 
 
-def expert_grad_kernel(xe0, xe1, de0, de1, act0, act1, da0, da1, db0, db1, out_ref):
-    left = {0: (xe0, xe1), 1: (xe0, xe1), 2: (de0, de1)}
-    right = {0: (da0, da1), 1: (db0, db1), 2: (act0, act1)}
+def expert_grad_kernel(order_ref, *refs):
+    kept, outs, total_ref = refs[:10], refs[10:16], refs[16]
+    left = (kept[0:2], kept[0:2], kept[2:4])
+    right = (kept[6:8], kept[8:10], kept[4:6])
+    own_ref, other_ref = outs[:2]
     step = pl.program_id(0)
-    pieces, depth = out_ref.shape[0], out_ref.shape[2]
+    depth = own_ref.shape[2]
     for kind in range(3):
 
         @pl.when(step % 3 == kind)
         def _(kind=kind):
             total = dot(left[kind][0][0], right[kind][0][0], 0, 0)
-            total = total + dot(left[kind][1][0], right[kind][1][0], 0, 0)
-            out_ref[:, 0] = total.reshape(pieces, depth, -1).astype(BF)
-
-
-def expert_grads(kept, pieces):
+            total_ref[...] = total + dot(left[kind][1][0], right[kind][1][0], 0, 0)
+
+    def part(r):
+        rows = pl.ds(pl.multiple_of(order_ref[r] * depth, depth), depth)
+        return total_ref[rows].astype(BF)
+
+    @pl.when(step < 3)
+    def _():
+        for r in range(8):
+            (own_ref, other_ref)[r % 2][r // 2, 0] = part(r)
+
+    @pl.when(step >= 3)
+    def _():
+        for r in range(8):
+            outs[2 + r // 2][r % 2, 0] = part(r)
+
+
+def expert_grads(order, kept):
     local, slots, width = kept[0][0].shape
     hidden = kept[0][2].shape[2]
     args = [kept[m][i] for i in range(5) for m in range(2)]
-    spec = lambda a: pl.BlockSpec((1,) + a.shape[1:], lambda i: (i // 3, 0, 0))
-    depth = width // pieces
+    depth = width // 8
+    shape = jax.ShapeDtypeStruct
     return pl.pallas_call(
         expert_grad_kernel,
-        out_shape=jax.ShapeDtypeStruct((pieces, 3 * local, depth, hidden), BF),
-        grid=(3 * local,),
-        in_specs=[spec(a) for a in args],
-        out_specs=pl.BlockSpec((pieces, 1, depth, hidden), lambda i: (0, i, 0, 0)),
+        out_shape=[shape((4, 3, depth, hidden), BF)] * 2 + [shape((2, 3, depth, hidden), BF)] * 4,
+        grid=(6,),
+        in_specs=[pl.BlockSpec(memory_space=pltpu.SMEM)]
+        + [pl.BlockSpec((1,) + a.shape[1:], lambda i: (i // 3, 0, 0)) for a in args],
+        out_specs=[pl.BlockSpec((4, 1, depth, hidden), lambda i: (0, jnp.minimum(i, 2), 0, 0))] * 2
+        + [pl.BlockSpec((2, 1, depth, hidden), lambda i: (0, jnp.maximum(i - 3, 0), 0, 0))] * 4,
+        scratch_shapes=[pltpu.VMEM((width, hidden), F32)],
         compiler_params=pltpu.CompilerParams(vmem_limit_bytes=48 * 1024 * 1024),
         cost_estimate=pl.CostEstimate(flops=14 * 10**9, bytes_accessed=28 << 20, transcendentals=0),
-    )(*args)
+    )(order, *args)
 
 
 CTX = ("z", "yl")
@@ -500,6 +490,7 @@
 ALL = CTX + FSDP
 UP = [(i, (i + 1) % 4) for i in range(4)]
 DOWN = [(i, (i - 1) % 4) for i in range(4)]
+TWO = [(i, (i + 2) % 4) for i in range(4)]
 FLIP = [(0, 1), (1, 0)]
 
 
@@ -547,6 +538,10 @@
 
     def copies(self, block, axis, count):
         return self(jnp.broadcast_to(block[None], (count,) + block.shape), axis)
+
+
+def add(a, b):
+    return (a.astype(F32) + b.astype(F32)).astype(BF)
 
 
 def sum_parts(parts):
@@ -623,7 +618,11 @@
         axis=2,
     ).transpose(1, 0, 2)
     pieces = jnp.broadcast_to(pieces[:, None], (n_ctx, n_fsdp) + pieces.shape[1:])
+    both_0 = jnp.concatenate([tokens[0], flip(tokens[0], "yl")], axis=0)
+    pieces = after_all(pieces, both_0)
     head_all = exchange(pieces.reshape((n_all,) + pieces.shape[2:]), ALL).reshape(width, -1)
+    seq_rows = [ring_of(both_0)]
+    head_all = after_all(head_all, seq_rows[0][1], seq_rows[0][4])
     w_heads = head_all[:, :span]
     small_all = head_all[:, span:]
     router = small_all[:, :experts]
@@ -643,26 +642,18 @@
         core == 0, jnp.stack([own, other], axis=1), jnp.stack([other, own], axis=1)
     ).reshape(width, width)
 
-    both = [jnp.concatenate([tokens[m], flip(tokens[m], "yl")], axis=0) for m in range(micro)]
-    seq_rows = [ring_of(both[0])]
-    seq_rows.append(ring_of(after_all(both[1], seq_rows[0][1], seq_rows[0][4])))
-
     stack = jnp.stack([w_gate, w_up, w_down], axis=1)
-    second_own = after_all(stack[1:], seq_rows[1][1], seq_rows[1][4])
-    second_before = lax.ppermute(second_own, "z", UP)
-    second_after = lax.ppermute(second_own, "z", DOWN)
-    half = stack.shape[2] // 2
-    second_far = jnp.concatenate(
-        [
-            lax.ppermute(second_before[:, :, :half], "z", UP),
-            lax.ppermute(second_after[:, :, half:], "z", DOWN),
-        ],
-        axis=2,
-    )
-    second_near = jnp.concatenate([second_own, second_after, second_far, second_before], axis=0)
-    second = [second_near, flip(second_near, "yl")]
-    first_own = jnp.concatenate([stack[:1], flip(stack[:1], "yl")], axis=0)
-    first = ring_of(after_all(first_own, second_before, second_after))
+    by_yl = flip(stack, "yl")
+    stack_z = after_all(stack, *seq_rows[0][1:])
+    by_up = lax.ppermute(stack_z, "z", UP)
+    by_down = lax.ppermute(stack_z, "z", DOWN)
+    both_1 = jnp.concatenate([tokens[1], flip(tokens[1], "yl")], axis=0)
+    seq_rows.append(ring_of(after_all(both_1, by_up, by_down)))
+    by_two = lax.ppermute(after_all(stack, seq_rows[1][1], seq_rows[1][4]), "z", TWO)
+    by_up_yl = flip(by_up, "yl")
+    by_down_yl = flip(by_down, "yl")
+    by_two_yl = flip(by_two, "yl")
+    pieces = [stack, by_yl, by_down, by_down_yl, by_two, by_two_yl, by_up, by_up_yl]
 
     expert_ids = jnp.arange(experts, dtype=jnp.int32)
     cot = cotangent.reshape(all_tok, width)
@@ -693,7 +684,9 @@
         mixed_h, *keep = attend_forward(order, seq_rows[m], *attention_args(m))
         saved.append(keep)
         if m == 0:
-            mixed_h = after_all(mixed_h, seq_rows[1][1], seq_rows[1][4])
+            mixed_h = after_all(mixed_h, by_up, by_down)
+        else:
+            mixed_h = after_all(mixed_h, by_two, by_down_yl)
         mixed = to_owner(mixed_h).transpose(1, 0, 2).reshape(tok, width)
         start = tokens[m, 0].astype(F32)
         middle = start + mm(mixed, out_full)
@@ -702,7 +695,11 @@
         chosen_m = chosen[m * tok : (m + 1) * tok]
         logits = jnp.where(chosen_m, mm(hidden_two, router), -1e30)
         gates = jnp.where(chosen_m, jax.nn.softmax(logits, axis=-1), 0.0)
-        x_own = exchange.copies(hidden_two, GROUP, n_ctx)
+        if m == 0:
+            hidden_two_x = after_all(hidden_two, seq_rows[1][1], seq_rows[1][4], by_up_yl)
+        else:
+            hidden_two_x = hidden_two
+        x_own = exchange.copies(hidden_two_x, GROUP, n_ctx)
         forward.append((mixed, middle, norm_back, hidden_two, gates, x_own))
 
     def experts_of(m, x_own):
@@ -713,14 +710,12 @@
             g_all,
             m,
             router_pad,
-            first,
-            second,
+            pieces,
             cap,
-            m == 0,
         )
 
     def back_sum(own, other):
-        return (own.astype(F32) + flip(other, "core").astype(F32)).astype(BF)
+        return add(own, flip(other, "core"))
 
     def middle_back(m, back):
         mixed, middle, norm_back, hidden_two, gates = forward[m][:5]
@@ -766,30 +761,55 @@
     moe_0 = lax.psum_scatter(moe_0, FSDP, scatter_dimension=0, tiled=True)[0]
     x_1 = after_all(x_1, back_0)
     back_0 = exchange(back_0, GROUP)
-    moe_own, moe_other, back_own, back_other, *kept_1 = experts_of(1, x_1)
-    back_0, back_own, back_other, moe_own, moe_other = lax.optimization_barrier(
-        (back_0, back_own, back_other, moe_own, moe_other)
+    moe_1, back_own, back_other, *kept_1 = experts_of(1, x_1)
+    back_0, back_own, back_other, moe_1 = lax.optimization_barrier(
+        (back_0, back_own, back_other, moe_1)
     )
     back_1 = back_sum(back_own, back_other)
     d_middle_0, d_mixed_0, grads_0 = middle_back(0, sum_parts(back_0))
     d_mixed_0 = exchange(d_mixed_0, CTX)
-    expert_sums = expert_grads((kept_0, kept_1), n_ctx)
+    kept_1[0], back_1 = lax.optimization_barrier((kept_1[0], back_1))
+    kept_1[0] = after_all(kept_1[0], d_mixed_0)
     back_1 = exchange(back_1, GROUP)
+    own_0, other_0, *parts_1 = expert_grads(order, (kept_0, kept_1))
     d_hidden_0, head_grads_0 = attention_back(0, d_mixed_0)
-    back_1, d_hidden_0, expert_sums, moe_0 = lax.optimization_barrier(
-        (back_1, d_hidden_0, expert_sums, moe_0)
-    )
-    expert_own = lax.psum_scatter(expert_sums, CTX, scatter_dimension=0, tiled=True)[0]
+    back_1, d_hidden_0, own_0, other_0, parts_1 = lax.optimization_barrier(
+        (back_1, d_hidden_0, own_0, other_0, parts_1)
+    )
+    other_0 = flip(other_0, "yl")
+    from_up = lax.ppermute(parts_1[1], "z", UP)
+    from_down = lax.ppermute(parts_1[3], "z", DOWN)
+    from_two = lax.ppermute(parts_1[2], "z", TWO)
     d_middle_1, d_mixed_1, grads_1 = middle_back(1, sum_parts(back_1))
+    d_mixed_1, moe_0 = lax.optimization_barrier((d_mixed_1, moe_0))
+    moe_1 = after_all(moe_1, moe_0)
+    moe_1 = lax.psum_scatter(moe_1, FSDP, scatter_dimension=0, tiled=True)[0]
     d_mixed_1 = exchange(d_mixed_1, CTX)
-    moe_1 = back_sum(moe_own, moe_other)
     d_hidden_0 = to_owner(d_hidden_0)
     d_hidden_1, head_grads_1 = attention_back(1, d_mixed_1)
-    d_hidden_0, d_hidden_1 = lax.optimization_barrier((d_hidden_0, d_hidden_1))
+    d_hidden_0, d_hidden_1, other_0, from_up, from_down = lax.optimization_barrier(
+        (d_hidden_0, d_hidden_1, other_0, from_up, from_down)
+    )
+    own_0 = [add(own_0[k], other_0[k]) for k in range(4)]
+    from_up_0 = lax.ppermute(own_0[1], "z", UP)
+    from_down_0 = lax.ppermute(own_0[3], "z", DOWN)
     d_hidden_1 = to_owner(d_hidden_1)
     grad_out, grad_router, grad_mlp = jax.tree.map(jnp.add, grads_0, grads_1)
     grad_heads, grad_attn, grad_qk = jax.tree.map(jnp.add, head_grads_0, head_grads_1)
-
+    d_hidden_1, from_two, from_up_0, from_down_0 = lax.optimization_barrier(
+        (d_hidden_1, from_two, from_up_0, from_down_0)
+    )
+    from_two_0 = lax.ppermute(own_0[2], "z", TWO)
+    second = [
+        sum(part[i].astype(F32) for part in (parts_1[0], from_up, from_down, from_two))
+        for i in range(2)
+    ]
+    from_yl = flip(second[1].astype(BF), "yl")
+
+    grad_out = grad_out.astype(BF).reshape(n_all // 2, 2, rows, width)
+    grad_own = lax.dynamic_index_in_dim(grad_out, core, axis=1, keepdims=False)
+    grad_other = lax.dynamic_index_in_dim(grad_out, 1 - core, axis=1, keepdims=False)
+    own_out = sum_parts(exchange(back_sum(grad_own, grad_other), CTX + GROUP))
     grad_qk = jnp.pad(grad_qk[:, None], ((0, 0), (0, rows - 1))).reshape(-1)
     grad_small = jnp.concatenate(
         [grad_router, grad_attn[:, None], grad_mlp[:, None], grad_qk[:, None]], axis=1
@@ -800,15 +820,13 @@
     own_heads = jnp.sum(grad_pack[:, :, :span].reshape(n_ctx, n_fsdp, rows, -1), axis=1)
     own_heads = own_heads.transpose(1, 0, 2)
     own_small = jnp.sum(grad_pack[:, :, span:], axis=0)
-    grad_out = grad_out.astype(BF).reshape(n_all // 2, 2, rows, width)
-    grad_own = lax.dynamic_index_in_dim(grad_out, core, axis=1, keepdims=False)
-    grad_other = lax.dynamic_index_in_dim(grad_out, 1 - core, axis=1, keepdims=False)
-    own_out = sum_parts(exchange(back_sum(grad_own, grad_other), CTX + GROUP))
-    moe_1 = sum_parts(exchange(moe_1, GROUP))
-    expert_own = expert_own.astype(F32).reshape((local, 3) + expert_own.shape[1:])
+    expert_own = [
+        sum(part.astype(F32) for part in (own_0[0], from_up_0, from_down_0, from_two_0)),
+        second[0] + from_yl.astype(F32),
+    ]
     outs = [
         (forward[0][1] + moe_0.astype(F32)).astype(BF),
-        (forward[1][1] + moe_1).astype(BF),
+        (forward[1][1] + moe_1.astype(F32)).astype(BF),
     ]
     d_inputs = [
         input_grad(0, sum_parts(d_hidden_0), d_middle_0),
@@ -826,9 +844,9 @@
         own_small[:, experts],
         own_small[:, experts + 1],
         own_small[:1, experts + 2],
-        expert_own[:, 0],
-        expert_own[:, 1],
-        expert_own[:, 2],
+        jnp.stack([part[0] for part in expert_own]),
+        jnp.stack([part[1] for part in expert_own]),
+        jnp.stack([part[2] for part in expert_own]),
     )
 
 

time: 634 us -> 630 us (level)
  local copies, waits for them, and re-layouts: 62.4 us -> 55.9 us
    all_to_all x15 -> x14, waiting for transfers between devices: 170 us -> 81.7 us  [swap(): return lax.all_to_all(parts, axis, split_axis=0, concat_axis=0, tiled=True)]
    ppermute x11 -> x14, waiting for transfers between devices: 13.9 us -> 66.3 us  [flip(): return lax.ppermute(block, axis, FLIP)]
    reduce_scatter x1, waiting for transfers between devices: 0.01 us -> 24.6 us  [body(): moe_0 = lax.psum_scatter(moe_0, FSDP, scatter_dimension=0, tiled=True)[0]]
    ppermute x4 -> x9, waiting for transfers between devices: 6.75 us -> 22.5 us  [the longest x1 15.5 us: body(): from_down_0 = lax.ppermute(own_0[3], 'z', DOWN)]
    ppermute x3 -> x2, waiting for transfers between devices: 18.6 us -> 4.14 us  [ring_of(): before = lax.ppermute(both, 'z', UP)]
    ppermute x3 -> x2, waiting for transfers between devices: 0.01 us -> 12.3 us  [ring_of(): far_low = lax.ppermute(before[:1], 'z', UP)]
    all_to_all x15 -> x14, starting transfers between devices: 93.9 us -> 81.8 us  [swap(): return lax.all_to_all(parts, axis, split_axis=0, concat_axis=0, tiled=True)]
    ppermute x4 -> x9, starting transfers between devices: 4.05 us -> 13.8 us  [the longest x1 3.37 us: body(): from_down_0 = lax.ppermute(own_0[3], 'z', DOWN)]
  transfers between devices with their start and end apart: 45 -> 48, of which waited for: 15 -> 20; matrix products, arithmetic and copies ran while one was open for 15% -> 15% of each run, Pallas kernels for 23% -> 23%
where the time goes in v5:
time: 630 us; the launch traced here: 621 us
  waiting for transfers between devices  212 us (34%)
  Pallas kernels  142 us (23%)
  starting transfers between devices  121 us (19%)
  other arithmetic  56.4 us (9%)
  local copies, waits for them, and re-layouts  55.9 us (9%)
  matrix products  18.2 us (3%)
  between operations  16 us (3%)
    all_to_all x14, starting transfers between devices, swap(): return lax.all_to_all(parts, axis, split_axis=0, concat_axis=0, tiled=True)  81.8 us
    all_to_all x14, waiting for transfers between devices, swap(): return lax.all_to_all(parts, axis, split_axis=0, concat_axis=0, tiled=True)  81.7 us
    pallas_call x2, Pallas kernels, run_experts(): pl.pallas_call(expert_kernel, out_shape=outs, grid=(1,), in_specs=[pl.Blo...  80.1 us
    ppermute x14, waiting for transfers between devices, flip(): return lax.ppermute(block, axis, FLIP)  66.3 us
    unnamed x193, local copies, waits for them, and re-layouts  30.4 us
    pallas_call x2, Pallas kernels, attend_backward(): pl.pallas_call(attend_back_kernel, out_shape=outs, grid=(1,), in_specs=[w...  25.2 us
    reduce_scatter x1, waiting for transfers between devices, body(): moe_0 = lax.psum_scatter(moe_0, FSDP, scatter_dimension=0, tiled=True)[0]  24.6 us
    pallas_call x1, Pallas kernels, expert_grads(): pl.pallas_call(expert_grad_kernel, out_shape=[shape((4, 3, depth, hidden)...  19.8 us
  transfers between devices with their start and end apart: 48, of which 20 were waited for; matrix products, arithmetic and copies ran while one was open for 15% of the time, Pallas kernels for 23%

profile of v5, /device:TPU:0, one launch (start us, length us, event | category | flops | bytes accessed | tf_op | source)
XLA Modules:
  0.0 620.7 jit_solution(12412948492950432685)
XLA Ops:
  14.5 5.0 collective-permute-done
  20.6 11.2 %all-to-all-start = ((bf16[128,8,384]{2,1,0:T(8,128)(2,1)}), bf16[128,8,384]{2,1,0:T(8,128)(2,1)S(1)}, u32[]{:S(2)}, u32[]{:S(2)}) async-start(bf16[128,8,384]{2,1,0:T(8,128)(2,1)} %bitcast.7), calls=%async_computation | async-start | bytes 1572864 | tf_op jit(solution)/shard_map/all_to_all | solution.py:514
  37.3 14.8 %all-to-all-done = bf16[128,8,384]{2,1,0:T(8,128)(2,1)S(1)} async-done(((bf16[128,8,384]{2,1,0:T(8,128)(2,1)}), bf16[128,8,384]{2,1,0:T(8,128)(2,1)S(1)}, u32[]{:S(2)}, u32[]{:S(2)}) %all-to-all-start) | async-done | bytes 786464 | tf_op jit(solution)/shard_map/all_to_all | solution.py:514
  53.3 5.5 all-to-all-start.1
  70.2 12.3 %collective-permute-done.3.far_low_ref = bf16[1,128,1024]{2,1,0:T(8,128)(2,1)S(1)} collective-permute-done((bf16[1,128,1024]{2,1,0:T(8,128)(2,1)}, bf16[1,128,1024]{2,1,0:T(8,128)(2,1)S(1)}, u32[]{:S(2)}, u32[]{:S(2)}) %collective-permute-start.3) | collective-permute-done | bytes 262176 | tf_op jit(solution)/shard_map/ppermute | solution.py:524
  87.0 8.3 %shard_map.246 = (bf16[1024,128]{1,0:T(8,128)(2,1)S(1)}, bf16[1024,1024]{1,0:T(8,128)(2,1)S(1)}, bf16[1024,128]{1,0:T(8,128)(2,1)S(1)}, bf16[1024,128]{1,0:T(8,128)(2,1)S(1)}) custom-call(s32[8]{0:T(128)S(1)} %fusion.45.order_ref, bf16[2,128,1024]{2,1,0:T(8,128)(2,1)S(1)} %pad_maximum_fusion.2.own_ref, bf16[2,128,1024]{2,1,0:T(8,128)(2,1)S(1)} %copy-done.12, ...), custom_call_target="tpu_custom_call" | custom-call | flops 12000000000 | bytes 8388608 | tf_op jit(solution)/shard_map/pallas_call | solution.py:243
  125.0 5.8 collective-permute-done.15.refs_11_
  132.4 5.4 all-to-all-start.3
  145.4 19.9 %all-to-all-done.3.refs_0_ = bf16[8,128,1024]{2,1,0:T(8,128)(2,1)} async-done(((bf16[8,128,1024]{2,1,0:T(8,128)(2,1)}), bf16[8,128,1024]{2,1,0:T(8,128)(2,1)}, u32[]{:S(2)}, u32[]{:S(2)}) %all-to-all-start.3) | async-done | bytes 2097184 | tf_op jit(solution)/shard_map/all_to_all | solution.py:514
  168.2 8.5 %shard_map.247 = (bf16[1024,128]{1,0:T(8,128)(2,1)S(1)}, bf16[1024,1024]{1,0:T(8,128)(2,1)S(1)}, bf16[1024,128]{1,0:T(8,128)(2,1)S(1)}, bf16[1024,128]{1,0:T(8,128)(2,1)S(1)}) custom-call(s32[8]{0:T(128)S(1)} %fusion.45.order_ref, bf16[2,128,1024]{2,1,0:T(8,128)(2,1)S(1)} %pad_maximum_fusion.3.own_ref, ...), custom_call_target="tpu_custom_call" | custom-call | flops 12000000000 | bytes 8388608 | tf_op jit(solution)/shard_map/pallas_call | solution.py:243
  196.8 6.2 all-to-all-start.5
  203.0 15.9 %collective-permute-done.17.refs_5_ = bf16[2,3,128,512]{3,2,1,0:T(8,128)(2,1)} collective-permute-done((bf16[2,3,128,512]{3,2,1,0:T(8,128)(2,1)}, bf16[2,3,128,512]{3,2,1,0:T(8,128)(2,1)}, u32[]{:S(2)}, u32[]{:S(2)}) %collective-permute-start.17) | collective-permute-done | bytes 786464 | tf_op jit(solution)/shard_map/ppermute | solution.py:518
  218.9 22.5 %collective-permute-done.18.refs_9_ = bf16[2,3,128,512]{3,2,1,0:T(8,128)(2,1)} collective-permute-done((bf16[2,3,128,512]{3,2,1,0:T(8,128)(2,1)}, bf16[2,3,128,512]{3,2,1,0:T(8,128)(2,1)}, u32[]{:S(2)}, u32[]{:S(2)}) %collective-permute-start.18) | collective-permute-done | bytes 786464 | tf_op jit(solution)/shard_map/ppermute | solution.py:518
  241.4 40.0 %shard_map.248 = (bf16[16,128,1024]{2,1,0:T(8,128)(2,1)}, bf16[8,128,1152]{2,1,0:T(8,128)(2,1)}, bf16[8,128,1152]{2,1,0:T(8,128)(2,1)}, bf16[2,768,1024]{2,1,0:T...) custom-call(s32[10]{0:T(128)} %pad_add_fusion.scalar_ref, ...), custom_call_target="tpu_custom_call" | custom-call | flops 40000000000 | bytes 41943040 | tf_op jit(solution)/shard_map/pallas_call | solution.py:418
  281.7 4.7 collective-permute-done.19
  291.6 5.7 all-to-all-start.6
  297.4 40.1 %shard_map.249 = (bf16[16,128,1024]{2,1,0:T(8,128)(2,1)}, bf16[8,128,1152]{2,1,0:T(8,128)(2,1)}, bf16[8,128,1152]{2,1,0:T(8,128)(2,1)}, bf16[2,768,1024]{2,1,0:T...) custom-call(s32[10]{0:T(128)} %pad_add_fusion.scalar_ref, ...), custom_call_target="tpu_custom_call" | custom-call | flops 40000000000 | bytes 41943040 | tf_op jit(solution)/shard_map/pallas_call | solution.py:418
  353.7 4.6 add_convert_fusion
  360.7 7.3 %all-to-all-start.8 = ((bf16[8,128,1152]{2,1,0:T(8,128)(2,1)}), bf16[8,128,1152]{2,1,0:T(8,128)(2,1)}, u32[]{:S(2)}, u32[]{:S(2)}) async-start(bf16[8,128,1152]{2,1,0:T(8,128)(2,1)} %add_convert_fusion), calls=%async_computation.8 | async-start | bytes 4718592 | tf_op jit(solution)/shard_map/all_to_all | solution.py:514
  371.9 12.1 %shard_map.250 = (bf16[1024,1024]{1,0:T(8,128)(2,1)}, f32[1024,256]{1,0:T(8,128)S(1)}, f32[1,1024]{1,0:T(1,128)S(1)}, f32[1,256]{1,0:T(1,128)S(1)}) custom-call(bf16[1024,1024]{1,0:T(8,128)(2,1)S(1)} %copy-done.23, bf16[1024,128]{1,0:T(8,128)(2,1)S(1)} %copy-done.29, bf16[1024,128]{1,0:T(8,128)(2,1)S(1)} %copy-done.31, bf16[1024,128]{1,0:T(8,128)(2,1)S(1)} %bitcast.177, ...), custom_call_target="tpu_custom_call" | custom-call | flops 24999999488 | bytes 8388608 | tf_op jit(solution)/shard_map/pallas_call | solution.py:267
  384.0 19.8 %shard_map.251 = (bf16[4,3,128,512]{3,2,1,0:T(8,128)(2,1)S(1)}, bf16[4,3,128,512]{3,2,1,0:T(8,128)(2,1)}, bf16[2,3,128,512]{3,2,1,0:T(8,128)(2,1)S(1)}, bf16[2,3...) custom-call(s32[8]{0:T(128)S(1)} %fusion.45.order_ref, ...), custom_call_target="tpu_custom_call" | custom-call | flops 14000000000 | bytes 29360128 | tf_op jit(solution)/shard_map/pallas_call | solution.py:473
  412.6 24.6 %reduce-scatter.3.cloned.1.call-done = bf16[1,128,1024]{2,1,0:T(8,128)(2,1)} async-done(((bf16[16,128,1024]{2,1,0:T(8,128)(2,1)}), bf16[1,128,1024]{2,1,0:T(8,128)(2,1)}) %reduce-scatter.3.cloned.1.call-update) | async-done | bytes 262160 | tf_op jit(solution)/shard_map/reduce_scatter | solution.py:761
  439.8 4.5 all-to-all-start.9
  457.8 4.6 all-to-all-start.10
  470.2 13.1 %shard_map.252 = (bf16[1024,1024]{1,0:T(8,128)(2,1)}, f32[1024,256]{1,0:T(8,128)S(1)}, f32[1,1024]{1,0:T(1,128)S(1)}, f32[1,256]{1,0:T(1,128)S(1)}) custom-call(bf16[1024,1024]{1,0:T(8,128)(2,1)S(1)} %copy-done.21, bf16[1024,128]{1,0:T(8,128)(2,1)S(1)} %copy-done.25, bf16[1024,128]{1,0:T(8,128)(2,1)S(1)} %copy-done.27, ...), custom_call_target="tpu_custom_call" | custom-call | flops 24999999488 | bytes 8388608 | tf_op jit(solution)/shard_map/pallas_call | solution.py:267
  484.2 12.3 %collective-permute-done.22 = bf16[4,3,128,512]{3,2,1,0:T(8,128)(2,1)} collective-permute-done((bf16[4,3,128,512]{3,2,1,0:T(8,128)(2,1)}, bf16[4,3,128,512]{3,2,1,0:T(8,128)(2,1)}, u32[]{:S(2)}, u32[]{:S(2)}) %collective-permute-start.22) | collective-permute-done | bytes 1572896 | tf_op jit(solution)/shard_map/ppermute | solution.py:518
  496.5 22.5 %all-to-all-done.10 = bf16[8,128,1024]{2,1,0:T(8,128)(2,1)} async-done(((bf16[8,128,1024]{2,1,0:T(8,128)(2,1)}), bf16[8,128,1024]{2,1,0:T(8,128)(2,1)}, u32[]{:S(2)}, u32[]{:S(2)}) %all-to-all-start.10) | async-done | bytes 2097184 | tf_op jit(solution)/shard_map/all_to_all | solution.py:514
  542.5 15.5 %collective-permute-done.27 = bf16[3,128,512]{2,1,0:T(8,128)(2,1)S(1)} collective-permute-done((bf16[3,128,512]{2,1,0:T(8,128)(2,1)S(1)}, bf16[3,128,512]{2,1,0:T(8,128)(2,1)S(1)}, u32[]{:S(2)}, u32[]{:S(2)}) %collective-permute-start.27) | collective-permute-done | bytes 393248 | tf_op jit(solution)/shard_map/ppermute | solution.py:795
  562.2 10.8 %all-to-all-start.12 = ((bf16[64,8,1024]{2,1,0:T(8,128)(2,1)}), bf16[64,8,1024]{2,1,0:T(8,128)(2,1)}, u32[]{:S(2)}, u32[]{:S(2)}) async-start(bf16[64,8,1024]{2,1,0:T(8,128)(2,1)} %fusion), calls=%async_computation.14 | async-start | bytes 2097152 | tf_op jit(solution)/shard_map/all_to_all | solution.py:514
  580.3 7.0 %all-to-all-done.12 = bf16[64,8,1024]{2,1,0:T(8,128)(2,1)} async-done(((bf16[64,8,1024]{2,1,0:T(8,128)(2,1)}), bf16[64,8,1024]{2,1,0:T(8,128)(2,1)}, u32[]{:S(2)}, u32[]{:S(2)}) %all-to-all-start.12) | async-done | bytes 1048608 | tf_op jit(solution)/shard_map/all_to_all | solution.py:514
  587.3 4.6 all-to-all-start.13
  597.5 10.8 %all-to-all-done.13 = bf16[128,8,384]{2,1,0:T(8,128)(2,1)S(1)} async-done(((bf16[128,8,384]{2,1,0:T(8,128)(2,1)}), bf16[128,8,384]{2,1,0:T(8,128)(2,1)S(1)}, u32[]{:S(2)}, u32[]{:S(2)}) %all-to-all-start.13) | async-done | bytes 786464 | tf_op jit(solution)/shard_map/all_to_all | solution.py:514
  (393 shorter events, 198.4 us)
Async XLA Ops:
  7.3 234.1 %all-gather.3.cloned.1.call-start = ((), (), s32[]{:S(2)}) async-start(), calls=%async_computation.18 | async-start | bytes 10027008 | tf_op jit(solution)/shard_map/all_gather | solution.py:666
  20.6 31.5 %all-to-all-start = ((bf16[128,8,384]{2,1,0:T(8,128)(2,1)}), bf16[128,8,384]{2,1,0:T(8,128)(2,1)S(1)}, u32[]{:S(2)}, u32[]{:S(2)}) async-start(bf16[128,8,384]{2,1,0:T(8,128)(2,1)} %bitcast.7), calls=%async_computation | async-start | bytes 1572864 | tf_op jit(solution)/shard_map/all_to_all | solution.py:514
  31.8 76.2 %collective-permute-start.8 = (bf16[1,128,1024]{2,1,0:T(8,128)(2,1)}, bf16[1,128,1024]{2,1,0:T(8,128)(2,1)}, u32[]{:S(2)}, u32[]{:S(2)}) collective-permute-start(bf16[1,128,1024]{2,1,0:T(8,128)(2,1)} %get-tuple-element.313), channel_id=1, source_target_pairs={{0,16},{16,0},{1,17},{17,1},{2,18},{18,2},{3,19},{19,3},{4,20},{20... | collective-permute-start | bytes 786440 | tf_op jit(solution)/shard_map/ppermute | solution.py:518
  33.4 30.7 %collective-permute-start.2 = (bf16[2,128,1024]{2,1,0:T(8,128)(2,1)S(1)}, bf16[2,128,1024]{2,1,0:T(8,128)(2,1)S(1)}, u32[]{:S(2)}, u32[]{:S(2)}) collective-permute-start(bf16[2,128,1024]{2,1,0:T(8,128)(2,1)S(1)} %pad_maximum_fusion.2.own_ref), channel_id=1, source_target_pairs={{0,32},{32,64},{64,96},{96,0},{1,33},{33,65},{65,97},{97,1},{2,34}... | collective-permute-start | bytes 1572872 | tf_op jit(solution)/shard_map/ppermute | solution.py:522
  35.1 31.2 %collective-permute-start.1 = (bf16[2,128,1024]{2,1,0:T(8,128)(2,1)S(1)}, bf16[2,128,1024]{2,1,0:T(8,128)(2,1)S(1)}, u32[]{:S(2)}, u32[]{:S(2)}) collective-permute-start(bf16[2,128,1024]{2,1,0:T(8,128)(2,1)S(1)} %pad_maximum_fusion.2.own_ref), channel_id=1, source_target_pairs={{0,96},{32,0},{64,32},{96,64},{1,97},{33,1},{65,33},{97,65},{2,98}... | collective-permute-start | bytes 1572872 | tf_op jit(solution)/shard_map/ppermute | solution.py:523
  53.3 31.1 %all-to-all-start.1 = ((bf16[64,8,1024]{2,1,0:T(8,128)(2,1)}), bf16[64,8,1024]{2,1,0:T(8,128)(2,1)}, u32[]{:S(2)}, u32[]{:S(2)}) async-start(bf16[64,8,1024]{2,1,0:T(8,128)(2,1)} %broadcast_in_dim.46), calls=%async_computation.1 | async-start | bytes 2097152 | tf_op jit(solution)/shard_map/all_to_all | solution.py:514
  84.4 30.1 %collective-permute-start.7 = (bf16[64,8,1024]{2,1,0:T(8,128)(2,1)}, bf16[64,8,1024]{2,1,0:T(8,128)(2,1)}, u32[]{:S(2)}, u32[]{:S(2)}) collective-permute-start(bf16[64,8,1024]{2,1,0:T(8,128)(2,1)} %all-to-all-done.1), channel_id=1, source_target_pairs={{0,1},{1,0},{2,3},{3,2},{4,5},{5,4},{6,7},{7,6},{8,9},{9,8},{10,11... | collective-permute-start | bytes 3145736 | tf_op jit(solution)/shard_map/ppermute | solution.py:518
  132.4 32.9 %all-to-all-start.3 = ((bf16[8,128,1024]{2,1,0:T(8,128)(2,1)}), bf16[8,128,1024]{2,1,0:T(8,128)(2,1)}, u32[]{:S(2)}, u32[]{:S(2)}) async-start(bf16[8,128,1024]{2,1,0:T(8,128)(2,1)} %broadcast_in_dim.47), calls=%async_computation.3 | async-start | bytes 4194304 | tf_op jit(solution)/shard_map/all_to_all | solution.py:514
  138.6 26.9 %collective-permute-start.11 = (bf16[1,128,1024]{2,1,0:T(8,128)(2,1)}, bf16[1,128,1024]{2,1,0:T(8,128)(2,1)S(1)}, u32[]{:S(2)}, u32[]{:S(2)}) collective-permute-start(bf16[1,128,1024]{2,1,0:T(8,128)(2,1)} %slice.286), channel_id=1, source_target_pairs={{0,32},{32,64},{64,96},{96,0},{1,33},{33,65},{65,97},{97,1},{2,34}... | collective-permute-start | bytes 786440 | tf_op jit(solution)/shard_map/ppermute | solution.py:524
  141.2 25.0 %collective-permute-start.12 = (bf16[1,128,1024]{2,1,0:T(8,128)(2,1)}, bf16[1,128,1024]{2,1,0:T(8,128)(2,1)}, u32[]{:S(2)}, u32[]{:S(2)}) collective-permute-start(bf16[1,128,1024]{2,1,0:T(8,128)(2,1)} %slice.287), channel_id=1, source_target_pairs={{0,96},{32,0},{64,32},{96,64},{1,97},{33,1},{65,33},{97,65},{2,98}... | collective-permute-start | bytes 786440 | tf_op jit(solution)/shard_map/ppermute | solution.py:525
  143.7 35.8 %collective-permute-start.14 = (bf16[2,3,128,512]{3,2,1,0:T(8,128)(2,1)}, bf16[2,3,128,512]{3,2,1,0:T(8,128)(2,1)}, u32[]{:S(2)}, u32[]{:S(2)}) collective-permute-start(bf16[2,3,128,512]{3,2,1,0:T(8,128)(2,1)} %collective-permute-done.6.refs_6_), channel_id=1, source_target_pairs={{0,16},{16,0},{1,17},{17,1},{2,18},{18,2},{3,19},{19,3},{4,20},{20... | collective-permute-start | bytes 2359304 | tf_op jit(solution)/shard_map/ppermute | solution.py:518
  144.8 34.7 %collective-permute-start.13 = (bf16[2,3,128,512]{3,2,1,0:T(8,128)(2,1)}, bf16[2,3,128,512]{3,2,1,0:T(8,128)(2,1)}, u32[]{:S(2)}, u32[]{:S(2)}) collective-permute-start(bf16[2,3,128,512]{3,2,1,0:T(8,128)(2,1)} %pad_maximum_fusion.refs_4_), channel_id=1, source_target_pairs={{0,64},{32,96},{64,0},{96,32},{1,65},{33,97},{65,1},{97,33},{2,66}... | collective-permute-start | bytes 2359304 | tf_op jit(solution)/shard_map/ppermute | solution.py:652
  165.3 76.0 %collective-permute-start.16 = (bf16[8,128,1024]{2,1,0:T(8,128)(2,1)}, bf16[8,128,1024]{2,1,0:T(8,128)(2,1)}, u32[]{:S(2)}, u32[]{:S(2)}) collective-permute-start(bf16[8,128,1024]{2,1,0:T(8,128)(2,1)} %all-to-all-done.3.refs_0_), channel_id=1, source_target_pairs={{0,1},{1,0},{2,3},{3,2},{4,5},{5,4},{6,7},{7,6},{8,9},{9,8},{10,11... | collective-permute-start | bytes 6291464 | tf_op jit(solution)/shard_map/ppermute | solution.py:518
  184.1 34.7 %collective-permute-start.17 = (bf16[2,3,128,512]{3,2,1,0:T(8,128)(2,1)}, bf16[2,3,128,512]{3,2,1,0:T(8,128)(2,1)}, u32[]{:S(2)}, u32[]{:S(2)}) collective-permute-start(bf16[2,3,128,512]{3,2,1,0:T(8,128)(2,1)} %pad_maximum_fusion.refs_4_), channel_id=1, source_target_pairs={{0,16},{16,0},{1,17},{17,1},{2,18},{18,2},{3,19},{19,3},{4,20},{20... | collective-permute-start | bytes 2359304 | tf_op jit(solution)/shard_map/ppermute | solution.py:518
  186.2 55.2 %collective-permute-start.18 = (bf16[2,3,128,512]{3,2,1,0:T(8,128)(2,1)}, bf16[2,3,128,512]{3,2,1,0:T(8,128)(2,1)}, u32[]{:S(2)}, u32[]{:S(2)}) collective-permute-start(bf16[2,3,128,512]{3,2,1,0:T(8,128)(2,1)} %collective-permute-done.13.refs_8_), channel_id=1, source_target_pairs={{0,16},{16,0},{1,17},{17,1},{2,18},{18,2},{3,19},{19,3},{4,20},{20... | collective-permute-start | bytes 2359304 | tf_op jit(solution)/shard_map/ppermute | solution.py:518
  196.8 84.5 %all-to-all-start.5 = ((bf16[8,128,1024]{2,1,0:T(8,128)(2,1)}), bf16[8,128,1024]{2,1,0:T(8,128)(2,1)}, u32[]{:S(2)}, u32[]{:S(2)}) async-start(bf16[8,128,1024]{2,1,0:T(8,128)(2,1)} %broadcast_in_dim.48), calls=%async_computation.5 | async-start | bytes 4194304 | tf_op jit(solution)/shard_map/all_to_all | solution.py:514
  291.6 45.9 %all-to-all-start.6 = ((bf16[8,128,1152]{2,1,0:T(8,128)(2,1)}), bf16[8,128,1152]{2,1,0:T(8,128)(2,1)}, u32[]{:S(2)}, u32[]{:S(2)}) async-start(bf16[8,128,1152]{2,1,0:T(8,128)(2,1)} %add_convert_fusion.1), calls=%async_computation.6 | async-start | bytes 4718592 | tf_op jit(solution)/shard_map/all_to_all | solution.py:514
  297.3 139.9 %reduce-scatter.3.cloned.1.call-start = ((), (), s32[]{:S(2)}) async-start(), calls=%async_computation.16 | async-start | bytes 4456448 | tf_op jit(solution)/shard_map/reduce_scatter | solution.py:761
  360.7 45.8 %all-to-all-start.8 = ((bf16[8,128,1152]{2,1,0:T(8,128)(2,1)}), bf16[8,128,1152]{2,1,0:T(8,128)(2,1)}, u32[]{:S(2)}, u32[]{:S(2)}) async-start(bf16[8,128,1152]{2,1,0:T(8,128)(2,1)} %add_convert_fusion), calls=%async_computation.8 | async-start | bytes 4718592 | tf_op jit(solution)/shard_map/all_to_all | solution.py:514
  367.9 244.1 %reduce-scatter.5.cloned.1.call-start = ((), (), s32[]{:S(2)}) async-start(), calls=%async_computation.17 | async-start | bytes 4456448 | tf_op jit(solution)/shard_map/reduce_scatter | solution.py:786
  444.2 40.0 %collective-permute-start.23 = (bf16[2,3,128,512]{3,2,1,0:T(8,128)(2,1)}, bf16[2,3,128,512]{3,2,1,0:T(8,128)(2,1)}, u32[]{:S(2)}, u32[]{:S(2)}) collective-permute-start(bf16[2,3,128,512]{3,2,1,0:T(8,128)(2,1)} %copy-done.17), channel_id=1, source_target_pairs={{0,32},{32,64},{64,96},{96,0},{1,33},{33,65},{65,97},{97,1},{2,34}... | collective-permute-start | bytes 2359304 | tf_op jit(solution)/shard_map/ppermute | solution.py:780
  446.2 38.0 %collective-permute-start.24 = (bf16[2,3,128,512]{3,2,1,0:T(8,128)(2,1)}, bf16[2,3,128,512]{3,2,1,0:T(8,128)(2,1)}, u32[]{:S(2)}, u32[]{:S(2)}) collective-permute-start(bf16[2,3,128,512]{3,2,1,0:T(8,128)(2,1)} %copy-done.16), channel_id=1, source_target_pairs={{0,96},{32,0},{64,32},{96,64},{1,97},{33,1},{65,33},{97,65},{2,98}... | collective-permute-start | bytes 2359304 | tf_op jit(solution)/shard_map/ppermute | solution.py:781
  447.5 95.0 %collective-permute-start.25 = (bf16[2,3,128,512]{3,2,1,0:T(8,128)(2,1)}, bf16[2,3,128,512]{3,2,1,0:T(8,128)(2,1)}, u32[]{:S(2)}, u32[]{:S(2)}) collective-permute-start(bf16[2,3,128,512]{3,2,1,0:T(8,128)(2,1)} %copy-done.15), channel_id=1, source_target_pairs={{0,64},{32,96},{64,0},{96,32},{1,65},{33,97},{65,1},{97,33},{2,66}... | collective-permute-start | bytes 2359304 | tf_op jit(solution)/shard_map/ppermute | solution.py:782
  449.8 46.8 %collective-permute-start.22 = (bf16[4,3,128,512]{3,2,1,0:T(8,128)(2,1)}, bf16[4,3,128,512]{3,2,1,0:T(8,128)(2,1)}, u32[]{:S(2)}, u32[]{:S(2)}) collective-permute-start(bf16[4,3,128,512]{3,2,1,0:T(8,128)(2,1)} %get-tuple-element.171), channel_id=1, source_target_pairs={{0,16},{16,0},{1,17},{17,1},{2,18},{18,2},{3,19},{19,3},{4,20},{20... | collective-permute-start | bytes 4718600 | tf_op jit(solution)/shard_map/ppermute | solution.py:518
  457.0 77.7 %collective-permute-start.28 = (bf16[64,8,1024]{2,1,0:T(8,128)(2,1)}, bf16[64,8,1024]{2,1,0:T(8,128)(2,1)}, u32[]{:S(2)}, u32[]{:S(2)}) collective-permute-start(bf16[64,8,1024]{2,1,0:T(8,128)(2,1)} %dynamic-slice_bitcast_fusion), channel_id=1, source_target_pairs={{0,1},{1,0},{2,3},{3,2},{4,5},{5,4},{6,7},{7,6},{8,9},{9,8},{10,11... | collective-permute-start | bytes 3145736 | tf_op jit(solution)/shard_map/ppermute | solution.py:518
  457.8 61.2 %all-to-all-start.10 = ((bf16[8,128,1024]{2,1,0:T(8,128)(2,1)}), bf16[8,128,1024]{2,1,0:T(8,128)(2,1)}, u32[]{:S(2)}, u32[]{:S(2)}) async-start(bf16[8,128,1024]{2,1,0:T(8,128)(2,1)} %bitcast.49), calls=%async_computation.12 | async-start | bytes 4194304 | tf_op jit(solution)/shard_map/all_to_all | solution.py:514
  519.0 40.6 %all-to-all-start.11 = ((bf16[8,128,1024]{2,1,0:T(8,128)(2,1)}), bf16[8,128,1024]{2,1,0:T(8,128)(2,1)}, u32[]{:S(2)}, u32[]{:S(2)}) async-start(bf16[8,128,1024]{2,1,0:T(8,128)(2,1)} %bitcast.53), calls=%async_computation.13 | async-start | bytes 4194304 | tf_op jit(solution)/shard_map/all_to_all | solution.py:514
  531.3 26.7 %collective-permute-start.27 = (bf16[3,128,512]{2,1,0:T(8,128)(2,1)S(1)}, bf16[3,128,512]{2,1,0:T(8,128)(2,1)S(1)}, u32[]{:S(2)}, u32[]{:S(2)}) collective-permute-start(bf16[3,128,512]{2,1,0:T(8,128)(2,1)S(1)} %get-tuple-element.302), channel_id=1, source_target_pairs={{0,96},{32,0},{64,32},{96,64},{1,97},{33,1},{65,33},{97,65},{2,98}... | collective-permute-start | bytes 1179656 | tf_op jit(solution)/shard_map/ppermute | solution.py:795
  534.7 24.9 %collective-permute-start.26 = (bf16[3,128,512]{2,1,0:T(8,128)(2,1)S(1)}, bf16[3,128,512]{2,1,0:T(8,128)(2,1)}, u32[]{:S(2)}, u32[]{:S(2)}) collective-permute-start(bf16[3,128,512]{2,1,0:T(8,128)(2,1)S(1)} %get-tuple-element.303), channel_id=1, source_target_pairs={{0,32},{32,64},{64,96},{96,0},{1,33},{33,65},{65,97},{97,1},{2,34}... | collective-permute-start | bytes 1179656 | tf_op jit(solution)/shard_map/ppermute | solution.py:794
  537.4 39.7 %collective-permute-start.29 = (bf16[3,128,512]{2,1,0:T(8,128)(2,1)}, bf16[3,128,512]{2,1,0:T(8,128)(2,1)}, u32[]{:S(2)}, u32[]{:S(2)}) collective-permute-start(bf16[3,128,512]{2,1,0:T(8,128)(2,1)} %get-tuple-element.301), channel_id=1, source_target_pairs={{0,64},{32,96},{64,0},{96,32},{1,65},{33,97},{65,1},{97,33},{2,66}... | collective-permute-start | bytes 1179656 | tf_op jit(solution)/shard_map/ppermute | solution.py:802
  561.8 30.2 %collective-permute-start.30 = (bf16[3,128,512]{2,1,0:T(8,128)(2,1)}, bf16[3,128,512]{2,1,0:T(8,128)(2,1)}, u32[]{:S(2)}, u32[]{:S(2)}) collective-permute-start(bf16[3,128,512]{2,1,0:T(8,128)(2,1)} %fusion.25), channel_id=1, source_target_pairs={{0,16},{16,0},{1,17},{17,1},{2,18},{18,2},{3,19},{19,3},{4,20},{20... | collective-permute-start | bytes 1179656 | tf_op jit(solution)/shard_map/ppermute | solution.py:518
  562.2 25.1 %all-to-all-start.12 = ((bf16[64,8,1024]{2,1,0:T(8,128)(2,1)}), bf16[64,8,1024]{2,1,0:T(8,128)(2,1)}, u32[]{:S(2)}, u32[]{:S(2)}) async-start(bf16[64,8,1024]{2,1,0:T(8,128)(2,1)} %fusion), calls=%async_computation.14 | async-start | bytes 2097152 | tf_op jit(solution)/shard_map/all_to_all | solution.py:514
  (110 other events, 1841.4 us)
Sparse Core Ops, SparseCore 0:
  11.0 96.6 all-gather.2
  338.8 98.3 reduce-scatter.2
  441.8 93.0 reduce-scatter.4

commit v6 on v5

--- a/solution.py
+++ b/solution.py
@@ -79,8 +79,7 @@
     order_ref,
     own_ref,
     after_ref,
-    far_low_ref,
-    far_high_ref,
+    far_ref,
     before_ref,
     gain_ref,
     w_ref,
@@ -103,8 +102,8 @@
         (own_ref, 1),
         (after_ref, 0),
         (after_ref, 1),
-        (far_low_ref, 0),
-        (far_high_ref, 0),
+        (far_ref, 0),
+        (far_ref, 1),
         (before_ref, 0),
         (before_ref, 1),
     ]
@@ -283,19 +282,20 @@
     return high, (v - high.astype(F32)).astype(BF)
 
 
-def expert_kernel(scalar_ref, *refs):
+def expert_kernel(scalar_ref, *refs, joined):
     x_own_ref, x_other_ref, g_ref, router_ref = refs[:4]
-    pieces, refs = refs[4:12], refs[12:]
-    out_ref, back_own_ref, back_other_ref, xe_ref, de_ref, act_ref, da_ref, db_ref = refs[:8]
-    pick_ref, weight_ref, dgate_ref, eo_ref, dr_ref, w_ref = refs[8:]
+    pieces, refs = refs[4:8], refs[8:]
+    outs, refs = (refs[:1], refs[1:]) if joined else (refs[:2], refs[2:])
+    back_own_ref, back_other_ref, xe_ref, de_ref, act_ref, da_ref, db_ref = refs[:7]
+    pick_ref, weight_ref, dgate_ref, eo_ref, dr_ref, w_ref = refs[7:]
     half, tok, width = x_own_ref.shape
     sources = 2 * half
     core = scalar_ref[1]
     depth = w_ref.shape[2] // 8
 
-    for r, ref in enumerate(pieces):
+    for r in range(8):
         rows = pl.ds(pl.multiple_of(scalar_ref[2 + r] * depth, depth), depth)
-        w_ref[:, :, rows] = ref[...]
+        w_ref[:, :, rows] = pieces[r // 2][r % 2]
     local, slots, hidden = act_ref.shape
     cap = slots // sources
     first = scalar_ref[0]
@@ -383,7 +383,10 @@
         spread = jnp.where(own_lane, high.astype(F32), 0.0) + jnp.where(
             slot_lane == first + row_expert + 64, low.astype(F32), 0.0
         )
-        out_ref[2 * i + column] = dot(pick, eo, 1, 0).astype(BF)
+        if joined:
+            outs[0][2 * i + column] = dot(pick, eo, 1, 0).astype(BF)
+        else:
+            outs[offset // half][scalar_ref[10 + i]] = dot(pick, eo, 1, 0).astype(BF)
         back_ref[i, :, :width] = dot(pick, dr, 1, 0).astype(BF)
         back_ref[i, :, width:] = dot(pick, spread.astype(BF), 1, 0).astype(BF)
         return carry
@@ -394,15 +397,15 @@
         )
 
 
-def run_experts(scalars, x_own, x_other, g_all, micro, router, pieces, cap):
+def run_experts(scalars, x_own, x_other, g_all, micro, router, pieces, cap, joined):
     half, tok, width = x_own.shape
     sources = 2 * half
-    local, _, _, hidden = pieces[0].shape
+    _, local, _, _, hidden = pieces[0].shape
     slots = sources * cap
     wide = g_all.shape[2]
     shape = jax.ShapeDtypeStruct
-    outs = [
-        shape((sources, tok, width), BF),
+    outs = [shape((sources, tok, width), BF)] if joined else [shape((half, tok, width), BF)] * 2
+    outs += [
         shape((half, tok, wide), BF),
         shape((half, tok, wide), BF),
         shape((local, slots, width), BF),
@@ -416,7 +419,7 @@
     )
     args = [router, *pieces]
     return pl.pallas_call(
-        expert_kernel,
+        functools.partial(expert_kernel, joined=joined),
         out_shape=outs,
         grid=(1,),
         in_specs=[pl.BlockSpec(memory_space=pltpu.SMEM), whole(x_own), whole(x_other), g_spec]
@@ -436,12 +439,11 @@
 
 
 def expert_grad_kernel(order_ref, *refs):
-    kept, outs, total_ref = refs[:10], refs[10:16], refs[16]
+    kept, outs, total_ref = refs[:10], refs[10:14], refs[14]
     left = (kept[0:2], kept[0:2], kept[2:4])
     right = (kept[6:8], kept[8:10], kept[4:6])
-    own_ref, other_ref = outs[:2]
     step = pl.program_id(0)
-    depth = own_ref.shape[2]
+    depth = outs[0].shape[3]
     for kind in range(3):
 
         @pl.when(step % 3 == kind)
@@ -449,19 +451,9 @@
             total = dot(left[kind][0][0], right[kind][0][0], 0, 0)
             total_ref[...] = total + dot(left[kind][1][0], right[kind][1][0], 0, 0)
 
-    def part(r):
+    for r in range(8):
         rows = pl.ds(pl.multiple_of(order_ref[r] * depth, depth), depth)
-        return total_ref[rows].astype(BF)
-
-    @pl.when(step < 3)
-    def _():
-        for r in range(8):
-            (own_ref, other_ref)[r % 2][r // 2, 0] = part(r)
-
-    @pl.when(step >= 3)
-    def _():
-        for r in range(8):
-            outs[2 + r // 2][r % 2, 0] = part(r)
+        outs[r // 2][r % 2, 0, 0] = total_ref[rows].astype(BF)
 
 
 def expert_grads(order, kept):
@@ -472,12 +464,14 @@
     shape = jax.ShapeDtypeStruct
     return pl.pallas_call(
         expert_grad_kernel,
-        out_shape=[shape((4, 3, depth, hidden), BF)] * 2 + [shape((2, 3, depth, hidden), BF)] * 4,
-        grid=(6,),
+        out_shape=[shape((2, local, 3, depth, hidden), BF)] * 4,
+        grid=(3 * local,),
         in_specs=[pl.BlockSpec(memory_space=pltpu.SMEM)]
         + [pl.BlockSpec((1,) + a.shape[1:], lambda i: (i // 3, 0, 0)) for a in args],
-        out_specs=[pl.BlockSpec((4, 1, depth, hidden), lambda i: (0, jnp.minimum(i, 2), 0, 0))] * 2
-        + [pl.BlockSpec((2, 1, depth, hidden), lambda i: (0, jnp.maximum(i - 3, 0), 0, 0))] * 4,
+        out_specs=[
+            pl.BlockSpec((2, 1, 1, depth, hidden), lambda i: (0, i // 3, i % 3, 0, 0))
+        ]
+        * 4,
         scratch_shapes=[pltpu.VMEM((width, hidden), F32)],
         compiler_params=pltpu.CompilerParams(vmem_limit_bytes=48 * 1024 * 1024),
         cost_estimate=pl.CostEstimate(flops=14 * 10**9, bytes_accessed=28 << 20, transcendentals=0),
@@ -518,12 +512,13 @@
     return lax.ppermute(block, axis, FLIP)
 
 
-def ring_of(both):
-    before = lax.ppermute(both, "z", UP)
-    after = lax.ppermute(both, "z", DOWN)
-    far_low = lax.ppermute(before[:1], "z", UP)
-    far_high = lax.ppermute(after[1:], "z", DOWN)
-    return [both, after, far_low, far_high, before]
+def by_z(parts):
+    return [lax.ppermute(parts[k], "z", perm) for k, perm in ((1, UP), (2, TWO), (3, DOWN))]
+
+
+def along_z(both):
+    before, far, after = by_z([both] * 4)
+    return [both, after, far, before]
 
 
 class Exchange:
@@ -542,6 +537,16 @@
 
 def add(a, b):
     return (a.astype(F32) + b.astype(F32)).astype(BF)
+
+
+def by_x(parts):
+    return [lax.ppermute(parts[k], "x", perm) for k, perm in ((1, UP), (2, TWO), (3, DOWN))]
+
+
+def pair_sum(parts, place, axis):
+    own = lax.dynamic_index_in_dim(parts, place, 0, keepdims=False)
+    other = lax.dynamic_index_in_dim(parts, 1 - place, 0, keepdims=False)
+    return own + flip(other.astype(BF), axis).astype(F32)
 
 
 def sum_parts(parts):
@@ -619,10 +624,12 @@
     ).transpose(1, 0, 2)
     pieces = jnp.broadcast_to(pieces[:, None], (n_ctx, n_fsdp) + pieces.shape[1:])
     both_0 = jnp.concatenate([tokens[0], flip(tokens[0], "yl")], axis=0)
+    both_w = jnp.stack([w_gate, w_up, w_down], axis=1)[None]
     pieces = after_all(pieces, both_0)
     head_all = exchange(pieces.reshape((n_all,) + pieces.shape[2:]), ALL).reshape(width, -1)
-    seq_rows = [ring_of(both_0)]
-    head_all = after_all(head_all, seq_rows[0][1], seq_rows[0][4])
+    both_w = jnp.concatenate([both_w, flip(both_w, "yl")], axis=0)
+    seq_rows = [along_z(both_0)]
+    head_all = after_all(head_all, *seq_rows[0][1:], both_w)
     w_heads = head_all[:, :span]
     small_all = head_all[:, span:]
     router = small_all[:, :experts]
@@ -642,18 +649,9 @@
         core == 0, jnp.stack([own, other], axis=1), jnp.stack([other, own], axis=1)
     ).reshape(width, width)
 
-    stack = jnp.stack([w_gate, w_up, w_down], axis=1)
-    by_yl = flip(stack, "yl")
-    stack_z = after_all(stack, *seq_rows[0][1:])
-    by_up = lax.ppermute(stack_z, "z", UP)
-    by_down = lax.ppermute(stack_z, "z", DOWN)
+    weights = along_z(both_w)
     both_1 = jnp.concatenate([tokens[1], flip(tokens[1], "yl")], axis=0)
-    seq_rows.append(ring_of(after_all(both_1, by_up, by_down)))
-    by_two = lax.ppermute(after_all(stack, seq_rows[1][1], seq_rows[1][4]), "z", TWO)
-    by_up_yl = flip(by_up, "yl")
-    by_down_yl = flip(by_down, "yl")
-    by_two_yl = flip(by_two, "yl")
-    pieces = [stack, by_yl, by_down, by_down_yl, by_two, by_two_yl, by_up, by_up_yl]
+    seq_rows.append(along_z(after_all(both_1, *seq_rows[0][1:])))
 
     expert_ids = jnp.arange(experts, dtype=jnp.int32)
     cot = cotangent.reshape(all_tok, width)
@@ -670,10 +668,14 @@
     sine = jnp.tile(jnp.concatenate([-sine, sine], axis=1), (1, 2))
     rel = jnp.arange(n_ctx, dtype=jnp.int32)
     order = ((z + rel // 2) % 4) * 2 + (yl + rel % 2) % 2
-    scalars = jnp.concatenate([jnp.stack([shard * local, core]), order]).astype(jnp.int32)
+    g_rel = ((rel % 4 - x) % 4) * 2 + (rel // 4 - yh) % 2
+    scalars = jnp.concatenate([jnp.stack([shard * local, core]), order, g_rel]).astype(jnp.int32)
 
     def to_owner(v):
         return exchange(v.reshape(n_ctx, tok, -1), CTX)
+
+    def z_swap(v):
+        return exchange(v.reshape(4, 2, tok, width), "z")
 
     def attention_args(m):
         seg = segments[m, 0]
@@ -684,9 +686,9 @@
         mixed_h, *keep = attend_forward(order, seq_rows[m], *attention_args(m))
         saved.append(keep)
         if m == 0:
-            mixed_h = after_all(mixed_h, by_up, by_down)
+            mixed_h = after_all(mixed_h, *seq_rows[1][1:])
         else:
-            mixed_h = after_all(mixed_h, by_two, by_down_yl)
+            mixed_h = after_all(mixed_h, weights[2])
         mixed = to_owner(mixed_h).transpose(1, 0, 2).reshape(tok, width)
         start = tokens[m, 0].astype(F32)
         middle = start + mm(mixed, out_full)
@@ -696,7 +698,7 @@
         logits = jnp.where(chosen_m, mm(hidden_two, router), -1e30)
         gates = jnp.where(chosen_m, jax.nn.softmax(logits, axis=-1), 0.0)
         if m == 0:
-            hidden_two_x = after_all(hidden_two, seq_rows[1][1], seq_rows[1][4], by_up_yl)
+            hidden_two_x = after_all(hidden_two, weights[1], weights[3])
         else:
             hidden_two_x = hidden_two
         x_own = exchange.copies(hidden_two_x, GROUP, n_ctx)
@@ -710,8 +712,9 @@
             g_all,
             m,
             router_pad,
-            pieces,
+            weights,
             cap,
+            m == 0,
         )
 
     def back_sum(own, other):
@@ -761,50 +764,48 @@
     moe_0 = lax.psum_scatter(moe_0, FSDP, scatter_dimension=0, tiled=True)[0]
     x_1 = after_all(x_1, back_0)
     back_0 = exchange(back_0, GROUP)
-    moe_1, back_own, back_other, *kept_1 = experts_of(1, x_1)
-    back_0, back_own, back_other, moe_1 = lax.optimization_barrier(
-        (back_0, back_own, back_other, moe_1)
+    moe_own, moe_other, back_own, back_other, *kept_1 = experts_of(1, x_1)
+    back_0, back_own, back_other, moe_own, moe_other = lax.optimization_barrier(
+        (back_0, back_own, back_other, moe_own, moe_other)
     )
     back_1 = back_sum(back_own, back_other)
     d_middle_0, d_mixed_0, grads_0 = middle_back(0, sum_parts(back_0))
     d_mixed_0 = exchange(d_mixed_0, CTX)
-    kept_1[0], back_1 = lax.optimization_barrier((kept_1[0], back_1))
+    d_mixed_0, back_1 = lax.optimization_barrier((d_mixed_0, back_1))
     kept_1[0] = after_all(kept_1[0], d_mixed_0)
     back_1 = exchange(back_1, GROUP)
-    own_0, other_0, *parts_1 = expert_grads(order, (kept_0, kept_1))
+    weight_parts = expert_grads(order, (kept_0, kept_1))
     d_hidden_0, head_grads_0 = attention_back(0, d_mixed_0)
-    back_1, d_hidden_0, own_0, other_0, parts_1 = lax.optimization_barrier(
-        (back_1, d_hidden_0, own_0, other_0, parts_1)
-    )
-    other_0 = flip(other_0, "yl")
-    from_up = lax.ppermute(parts_1[1], "z", UP)
-    from_down = lax.ppermute(parts_1[3], "z", DOWN)
-    from_two = lax.ppermute(parts_1[2], "z", TWO)
+    moe_other = flip(moe_other, "core")
+    back_1, d_hidden_0, weight_parts, moe_other = lax.optimization_barrier(
+        (back_1, d_hidden_0, weight_parts, moe_other)
+    )
+    moe_1 = [add(moe_own[2 * k : 2 * k + 2], moe_other[2 * k : 2 * k + 2]) for k in range(4)]
+    weight_moved = by_z(weight_parts)
     d_middle_1, d_mixed_1, grads_1 = middle_back(1, sum_parts(back_1))
-    d_mixed_1, moe_0 = lax.optimization_barrier((d_mixed_1, moe_0))
-    moe_1 = after_all(moe_1, moe_0)
-    moe_1 = lax.psum_scatter(moe_1, FSDP, scatter_dimension=0, tiled=True)[0]
     d_mixed_1 = exchange(d_mixed_1, CTX)
-    d_hidden_0 = to_owner(d_hidden_0)
+    d_hidden_0 = z_swap(d_hidden_0)
     d_hidden_1, head_grads_1 = attention_back(1, d_mixed_1)
-    d_hidden_0, d_hidden_1, other_0, from_up, from_down = lax.optimization_barrier(
-        (d_hidden_0, d_hidden_1, other_0, from_up, from_down)
-    )
-    own_0 = [add(own_0[k], other_0[k]) for k in range(4)]
-    from_up_0 = lax.ppermute(own_0[1], "z", UP)
-    from_down_0 = lax.ppermute(own_0[3], "z", DOWN)
-    d_hidden_1 = to_owner(d_hidden_1)
+    moe_moved = by_x(moe_1)
+    d_hidden_0, d_hidden_1, weight_moved[0], weight_moved[2], moe_moved = (
+        lax.optimization_barrier(
+            (d_hidden_0, d_hidden_1, weight_moved[0], weight_moved[2], moe_moved)
+        )
+    )
+    d_hidden_1 = z_swap(d_hidden_1)
+    d_hidden_0 = pair_sum(sum_parts(d_hidden_0), yl, "yl")
+    moe_1 = sum(part.astype(F32) for part in [moe_1[0]] + moe_moved)
+    moe_1 = moe_1[0] + flip(moe_1[1].astype(BF), "yh").astype(F32)
     grad_out, grad_router, grad_mlp = jax.tree.map(jnp.add, grads_0, grads_1)
     grad_heads, grad_attn, grad_qk = jax.tree.map(jnp.add, head_grads_0, head_grads_1)
-    d_hidden_1, from_two, from_up_0, from_down_0 = lax.optimization_barrier(
-        (d_hidden_1, from_two, from_up_0, from_down_0)
-    )
-    from_two_0 = lax.ppermute(own_0[2], "z", TWO)
+    d_hidden_1, weight_moved[1], moe_1 = lax.optimization_barrier(
+        (d_hidden_1, weight_moved[1], moe_1)
+    )
     second = [
-        sum(part[i].astype(F32) for part in (parts_1[0], from_up, from_down, from_two))
-        for i in range(2)
+        sum(part[i].astype(F32) for part in [weight_parts[0]] + weight_moved) for i in range(2)
     ]
     from_yl = flip(second[1].astype(BF), "yl")
+    d_hidden_1 = pair_sum(sum_parts(d_hidden_1), yl, "yl")
 
     grad_out = grad_out.astype(BF).reshape(n_all // 2, 2, rows, width)
     grad_own = lax.dynamic_index_in_dim(grad_out, core, axis=1, keepdims=False)
@@ -820,17 +821,14 @@
     own_heads = jnp.sum(grad_pack[:, :, :span].reshape(n_ctx, n_fsdp, rows, -1), axis=1)
     own_heads = own_heads.transpose(1, 0, 2)
     own_small = jnp.sum(grad_pack[:, :, span:], axis=0)
-    expert_own = [
-        sum(part.astype(F32) for part in (own_0[0], from_up_0, from_down_0, from_two_0)),
-        second[0] + from_yl.astype(F32),
-    ]
+    expert_own = second[0] + from_yl.astype(F32)
     outs = [
         (forward[0][1] + moe_0.astype(F32)).astype(BF),
-        (forward[1][1] + moe_1.astype(F32)).astype(BF),
+        (forward[1][1] + moe_1).astype(BF),
     ]
     d_inputs = [
-        input_grad(0, sum_parts(d_hidden_0), d_middle_0),
-        input_grad(1, sum_parts(d_hidden_1), d_middle_1),
+        input_grad(0, d_hidden_0, d_middle_0),
+        input_grad(1, d_hidden_1, d_middle_1),
     ]
 
     return (
@@ -844,9 +842,9 @@
         own_small[:, experts],
         own_small[:, experts + 1],
         own_small[:1, experts + 2],
-        jnp.stack([part[0] for part in expert_own]),
-        jnp.stack([part[1] for part in expert_own]),
-        jnp.stack([part[2] for part in expert_own]),
+        expert_own[:, 0],
+        expert_own[:, 1],
+        expert_own[:, 2],
     )
 
 

time: 630 us -> 601 us (0.954)
  waiting for transfers between devices: 212 us -> 174 us
  starting transfers between devices: 121 us -> 144 us
  local copies, waits for them, and re-layouts: 55.9 us -> 40.2 us
    ppermute x14, waiting for transfers between devices: 66.3 us -> 25 us  [flip(): return lax.ppermute(block, axis, FLIP)]
    ppermute x14, starting transfers between devices: 10.9 us -> 38.5 us  [flip(): return lax.ppermute(block, axis, FLIP)]
    unnamed x193 -> x167, local copies, waits for them, and re-layouts: 30.4 us -> 19.4 us
    ppermute x17 -> x15, starting transfers between devices: 27.2 us -> 23.8 us  [the longest x12 17.5 us: by_z(): lax.ppermute(parts[k], 'z', perm)]
    ppermute x17 -> x15, waiting for transfers between devices: 38.9 us -> 40.9 us  [the longest x12 33.5 us: by_z(): lax.ppermute(parts[k], 'z', perm)]
  transfers between devices with their start and end apart: 48 -> 45, of which waited for: 20 -> 15; matrix products, arithmetic and copies ran while one was open for 15% -> 13% of each run, Pallas kernels for 23% -> 24%
where the time goes in v6:
time: 601 us; the launch traced here: 592 us
  waiting for transfers between devices  174 us (29%)
  starting transfers between devices  144 us (24%)
  Pallas kernels  143 us (24%)
  other arithmetic  57.8 us (10%)
  local copies, waits for them, and re-layouts  40.2 us (7%)
  matrix products  16.4 us (3%)
  between operations  16.3 us (3%)
    all_to_all x14, waiting for transfers between devices, swap(): return lax.all_to_all(parts, axis, split_axis=0, concat_axis=0, tiled=True)  84.5 us
    all_to_all x14, starting transfers between devices, swap(): return lax.all_to_all(parts, axis, split_axis=0, concat_axis=0, tiled=True)  81.8 us
    pallas_call x2, Pallas kernels, run_experts(): pl.pallas_call(functools.partial(expert_kernel, joined=joined), out_shape...  80.9 us
    ppermute x14, starting transfers between devices, flip(): return lax.ppermute(block, axis, FLIP)  38.5 us
    ppermute x12, waiting for transfers between devices, by_z(): lax.ppermute(parts[k], 'z', perm)  33.5 us
    ppermute x14, waiting for transfers between devices, flip(): return lax.ppermute(block, axis, FLIP)  25 us
    pallas_call x2, Pallas kernels, attend_backward(): pl.pallas_call(attend_back_kernel, out_shape=outs, grid=(1,), in_specs=[w...  24.6 us
    reduce_scatter x1, waiting for transfers between devices, body(): moe_0 = lax.psum_scatter(moe_0, FSDP, scatter_dimension=0, tiled=True)[0]  23.4 us
  transfers between devices with their start and end apart: 45, of which 15 were waited for; matrix products, arithmetic and copies ran while one was open for 13% of the time, Pallas kernels for 24%

profile of v6, /device:TPU:0, one launch (start us, length us, event | category | flops | bytes accessed | tf_op | source)
XLA Modules:
  0.0 592.1 jit_solution(9262680569948953077)
XLA Ops:
  14.5 5.9 collective-permute-done
  21.4 11.1 %all-to-all-start = ((bf16[128,8,384]{2,1,0:T(8,128)(2,1)}), bf16[128,8,384]{2,1,0:T(8,128)(2,1)S(1)}, u32[]{:S(2)}, u32[]{:S(2)}) async-start(bf16[128,8,384]{2,1,0:T(8,128)(2,1)} %bitcast.7), calls=%async_computation | async-start | bytes 1572864 | tf_op jit(solution)/shard_map/all_to_all | solution.py:508
  40.0 12.6 %all-to-all-done = bf16[128,8,384]{2,1,0:T(8,128)(2,1)S(1)} async-done(((bf16[128,8,384]{2,1,0:T(8,128)(2,1)}), bf16[128,8,384]{2,1,0:T(8,128)(2,1)S(1)}, u32[]{:S(2)}, u32[]{:S(2)}) %all-to-all-start) | async-done | bytes 786464 | tf_op jit(solution)/shard_map/all_to_all | solution.py:508
  53.9 5.5 all-to-all-start.1
  61.5 10.9 %collective-permute-done.1.after_ref = bf16[2,128,1024]{2,1,0:T(8,128)(2,1)S(1)} collective-permute-done((bf16[2,128,1024]{2,1,0:T(8,128)(2,1)S(1)}, bf16[2,128,1024]{2,1,0:T(8,128)(2,1)S(1)}, u32[]{:S(2)}, u32[]{:S(2)}) %collective-permute-start.1) | collective-permute-done | bytes 524320 | tf_op jit(solution)/shard_map/ppermute | solution.py:516
  72.4 8.1 %collective-permute-done.3.before_ref = bf16[2,128,1024]{2,1,0:T(8,128)(2,1)} collective-permute-done((bf16[2,128,1024]{2,1,0:T(8,128)(2,1)S(1)}, bf16[2,128,1024]{2,1,0:T(8,128)(2,1)}, u32[]{:S(2)}, u32[]{:S(2)}) %collective-permute-start.3) | collective-permute-done | bytes 524320 | tf_op jit(solution)/shard_map/ppermute | solution.py:516
  89.2 14.5 %collective-permute-done.6.after_ref = bf16[2,128,1024]{2,1,0:T(8,128)(2,1)} collective-permute-done((bf16[2,128,1024]{2,1,0:T(8,128)(2,1)S(1)}, bf16[2,128,1024]{2,1,0:T(8,128)(2,1)}, u32[]{:S(2)}, u32[]{:S(2)}) %collective-permute-start.6) | collective-permute-done | bytes 524320 | tf_op jit(solution)/shard_map/ppermute | solution.py:516
  105.0 8.8 %shard_map.246 = (bf16[1024,128]{1,0:T(8,128)(2,1)S(1)}, bf16[1024,1024]{1,0:T(8,128)(2,1)S(1)}, bf16[1024,128]{1,0:T(8,128)(2,1)S(1)}, bf16[1024,128]{1,0:T(8,128)(2,1)S(1)}) custom-call(s32[8]{0:T(128)S(1)} %fusion.45.order_ref, bf16[2,128,1024]{2,1,0:T(8,128)(2,1)S(1)} %pad_maximum_fusion.2.own_ref, bf16[2,128,1024]{2,1,0:T(8,128)(2,1)S(1)} %copy-done.13, ...), custom_call_target="tpu_custom_call" | custom-call | flops 12000000000 | bytes 8388608 | tf_op jit(solution)/shard_map/pallas_call | solution.py:242
  117.4 5.4 all-to-all-start.2
  126.9 15.9 %all-to-all-done.2 = bf16[8,128,128]{1,2,0:T(8,128)(2,1)S(1)} async-done(((bf16[8,128,128]{1,2,0:T(8,128)(2,1)}), bf16[8,128,128]{1,2,0:T(8,128)(2,1)S(1)}, u32[]{:S(2)}, u32[]{:S(2)}) %all-to-all-start.2) | async-done | bytes 262176 | tf_op jit(solution)/shard_map/all_to_all | solution.py:508
  146.8 5.7 all-to-all-start.3
  153.7 27.0 %all-to-all-done.3.refs_0_ = bf16[8,128,1024]{2,1,0:T(8,128)(2,1)} async-done(((bf16[8,128,1024]{2,1,0:T(8,128)(2,1)}), bf16[8,128,1024]{2,1,0:T(8,128)(2,1)}, u32[]{:S(2)}, u32[]{:S(2)}) %all-to-all-start.3) | async-done | bytes 2097184 | tf_op jit(solution)/shard_map/all_to_all | solution.py:508
  181.2 8.8 %shard_map.247 = (bf16[1024,128]{1,0:T(8,128)(2,1)S(1)}, bf16[1024,1024]{1,0:T(8,128)(2,1)S(1)}, bf16[1024,128]{1,0:T(8,128)(2,1)S(1)}, bf16[1024,128]{1,0:T(8,128)(2,1)S(1)}) custom-call(s32[8]{0:T(128)S(1)} %fusion.45.order_ref, bf16[2,128,1024]{2,1,0:T(8,128)(2,1)S(1)} %pad_maximum_fusion.3.own_ref, ...), custom_call_target="tpu_custom_call" | custom-call | flops 12000000000 | bytes 8388608 | tf_op jit(solution)/shard_map/pallas_call | solution.py:242
  199.4 5.8 all-to-all-done.4
  209.0 4.9 all-to-all-start.5
  214.0 40.1 %shard_map.248 = (bf16[16,128,1024]{2,1,0:T(8,128)(2,1)}, bf16[8,128,1152]{2,1,0:T(8,128)(2,1)}, bf16[8,128,1152]{2,1,0:T(8,128)(2,1)}, bf16[2,768,1024]{2,1,0:T...) custom-call(s32[18]{0:T(128)} %pad_add_fusion.scalar_ref, ...), custom_call_target="tpu_custom_call" | custom-call | flops 40000000000 | bytes 41943040 | tf_op jit(solution)/shard_map/pallas_call | solution.py:421
  266.1 7.2 %all-to-all-start.6 = ((bf16[8,128,1152]{2,1,0:T(8,128)(2,1)}), bf16[8,128,1152]{2,1,0:T(8,128)(2,1)}, u32[]{:S(2)}, u32[]{:S(2)}) async-start(bf16[8,128,1152]{2,1,0:T(8,128)(2,1)} %add_convert_fusion.1), calls=%async_computation.7 | async-start | bytes 4718592 | tf_op jit(solution)/shard_map/all_to_all | solution.py:508
  273.3 40.8 %shard_map.249 = (bf16[8,128,1024]{2,1,0:T(8,128)(2,1)}, bf16[8,128,1024]{2,1,0:T(8,128)(2,1)}, bf16[8,128,1152]{2,1,0:T(8,128)(2,1)}, bf16[8,128,1152]{2,1,0:T(...) custom-call(s32[18]{0:T(128)} %pad_add_fusion.scalar_ref, ...), custom_call_target="tpu_custom_call" | custom-call | flops 40000000000 | bytes 41943040 | tf_op jit(solution)/shard_map/pallas_call | solution.py:421
  320.7 23.4 %reduce-scatter.2.cloned.1.call-done = bf16[1,128,1024]{2,1,0:T(8,128)(2,1)} async-done(((bf16[16,128,1024]{2,1,0:T(8,128)(2,1)}), bf16[1,128,1024]{2,1,0:T(8,128)(2,1)}) %reduce-scatter.2.cloned.1.call-update) | async-done | bytes 262160 | tf_op jit(solution)/shard_map/reduce_scatter | solution.py:764
  359.9 5.1 all-to-all-start.8
  365.0 20.3 %shard_map.251 = (bf16[2,2,3,128,512]{4,3,2,1,0:T(8,128)(2,1)S(1)}, bf16[2,2,3,128,512]{4,3,2,1,0:T(8,128)(2,1)S(1)}, bf16[2,2,3,128,512]{4,3,2,1,0:T(8,128)(2,1)}, bf16[2,2,3,128,512]{4,3,2,1,0:T(8,128)(2,1)}) custom-call(s32[8]{0:T(128)S(1)} %fusion.45.order_ref, bf16[2,768,1024]{2,1,0:T(8,128)(2,1)} %get-tuple-element.136.refs_0_, ...), custom_call_target="tpu_custom_call" | custom-call | flops 14000000000 | bytes 29360128 | tf_op jit(solution)/shard_map/pallas_call | solution.py:465
  385.4 12.2 %shard_map.250 = (bf16[1024,1024]{1,0:T(8,128)(2,1)}, f32[1024,256]{1,0:T(8,128)S(1)}, f32[1,1024]{1,0:T(1,128)S(1)}, f32[1,256]{1,0:T(1,128)S(1)}) custom-call(bf16[1024,1024]{1,0:T(8,128)(2,1)S(1)} %copy-done.17, bf16[1024,128]{1,0:T(8,128)(2,1)S(1)} %copy-done.23, bf16[1024,128]{1,0:T(8,128)(2,1)S(1)} %copy-done.25, bf16[1024,128]{1,0:T(8,128)(2,1)S(1)} %bitcast.200, ...), custom_call_target="tpu_custom_call" | custom-call | flops 24999999488 | bytes 8388608 | tf_op jit(solution)/shard_map/pallas_call | solution.py:266
  404.4 5.1 all-to-all-start.9
  435.6 12.4 %shard_map.252 = (bf16[1024,1024]{1,0:T(8,128)(2,1)}, f32[1024,256]{1,0:T(8,128)S(1)}, f32[1,1024]{1,0:T(1,128)S(1)}, f32[1,256]{1,0:T(1,128)S(1)}) custom-call(bf16[1024,1024]{1,0:T(8,128)(2,1)S(1)} %copy-done.15, bf16[1024,128]{1,0:T(8,128)(2,1)S(1)} %copy-done.19, bf16[1024,128]{1,0:T(8,128)(2,1)S(1)} %copy-done.21, bf16[1024,128]{1,0:T(8,128)(2,1)S(1)} %bitcast.199, ...), custom_call_target="tpu_custom_call" | custom-call | flops 24999999488 | bytes 8388608 | tf_op jit(solution)/shard_map/pallas_call | solution.py:266
  456.0 7.5 %collective-permute-done.22 = bf16[2,128,1024]{2,1,0:T(8,128)(2,1)} collective-permute-done((bf16[2,128,1024]{2,1,0:T(8,128)(2,1)}, bf16[2,128,1024]{2,1,0:T(8,128)(2,1)}, u32[]{:S(2)}, u32[]{:S(2)}) %collective-permute-start.22) | collective-permute-done | bytes 524320 | tf_op jit(solution)/shard_map/ppermute | solution.py:543
  463.5 9.7 %all-to-all-done.10 = bf16[4,2,128,1024]{3,2,1,0:T(8,128)(2,1)} async-done(((bf16[4,2,128,1024]{3,2,1,0:T(8,128)(2,1)}), bf16[4,2,128,1024]{3,2,1,0:T(8,128)(2,1)}, u32[]{:S(2)}, u32[]{:S(2)}) %all-to-all-start.10) | async-done | bytes 2097184 | tf_op jit(solution)/shard_map/all_to_all | solution.py:508
  491.1 26.8 %collective-permute-start.25 = (bf16[128,1024]{1,0:T(8,128)(2,1)}, bf16[128,1024]{1,0:T(8,128)(2,1)S(1)}, u32[]{:S(2)}, u32[]{:S(2)}) collective-permute-start(bf16[128,1024]{1,0:T(8,128)(2,1)} %fusion.24), channel_id=1, source_target_pairs={{0,16},{16,0},{1,17},{17,1},{2,18},{18,2},{3,19},{19,3},{4,20},{20... | collective-permute-start | bytes 786440 | tf_op jit(solution)/shard_map/ppermute | solution.py:512
  518.8 7.8 %all-to-all-done.11 = bf16[4,2,128,1024]{3,2,1,0:T(8,128)(2,1)} async-done(((bf16[4,2,128,1024]{3,2,1,0:T(8,128)(2,1)}), bf16[4,2,128,1024]{3,2,1,0:T(8,128)(2,1)}, u32[]{:S(2)}, u32[]{:S(2)}) %all-to-all-start.11) | async-done | bytes 2097184 | tf_op jit(solution)/shard_map/all_to_all | solution.py:508
  531.7 9.6 %all-to-all-start.12 = ((bf16[64,8,1024]{2,1,0:T(8,128)(2,1)}), bf16[64,8,1024]{2,1,0:T(8,128)(2,1)}, u32[]{:S(2)}, u32[]{:S(2)}) async-start(bf16[64,8,1024]{2,1,0:T(8,128)(2,1)} %fusion), calls=%async_computation.13 | async-start | bytes 2097152 | tf_op jit(solution)/shard_map/all_to_all | solution.py:508
  550.8 5.7 all-to-all-done.12
  556.5 5.1 all-to-all-start.13
  561.5 14.3 %collective-permute-done.28 = bf16[2,3,128,512]{3,2,1,0:T(8,128)(2,1)} collective-permute-done((bf16[2,3,128,512]{3,2,1,0:T(8,128)(2,1)}, bf16[2,3,128,512]{3,2,1,0:T(8,128)(2,1)}, u32[]{:S(2)}, u32[]{:S(2)}) %collective-permute-start.28) | collective-permute-done | bytes 786464 | tf_op jit(solution)/shard_map/ppermute | solution.py:512
  (358 shorter events, 171.8 us)
Async XLA Ops:
  7.3 206.8 %all-gather.3.cloned.1.call-start = ((), (), s32[]{:S(2)}) async-start(), calls=%async_computation.16 | async-start | bytes 10027008 | tf_op jit(solution)/shard_map/all_gather | solution.py:664
  12.8 47.4 %collective-permute-start.5 = (bf16[1,128,1024]{2,1,0:T(8,128)(2,1)}, bf16[1,128,1024]{2,1,0:T(8,128)(2,1)}, u32[]{:S(2)}, u32[]{:S(2)}) collective-permute-start(bf16[1,128,1024]{2,1,0:T(8,128)(2,1)} %get-tuple-element.302), channel_id=1, source_target_pairs={{0,16},{16,0},{1,17},{17,1},{2,18},{18,2},{3,19},{19,3},{4,20},{20... | collective-permute-start | bytes 786440 | tf_op jit(solution)/shard_map/ppermute | solution.py:512
  21.4 31.2 %all-to-all-start = ((bf16[128,8,384]{2,1,0:T(8,128)(2,1)}), bf16[128,8,384]{2,1,0:T(8,128)(2,1)S(1)}, u32[]{:S(2)}, u32[]{:S(2)}) async-start(bf16[128,8,384]{2,1,0:T(8,128)(2,1)} %bitcast.7), calls=%async_computation | async-start | bytes 1572864 | tf_op jit(solution)/shard_map/all_to_all | solution.py:508
  33.5 49.0 %collective-permute-start.4 = (bf16[1,2,3,128,512]{4,3,2,1,0:T(8,128)(2,1)}, bf16[1,2,3,128,512]{4,3,2,1,0:T(8,128)(2,1)}, u32[]{:S(2)}, u32[]{:S(2)}) collective-permute-start(bf16[1,2,3,128,512]{4,3,2,1,0:T(8,128)(2,1)} %maximum_bitcast_fusion.1), channel_id=1, source_target_pairs={{0,16},{16,0},{1,17},{17,1},{2,18},{18,2},{3,19},{19,3},{4,20},{20... | collective-permute-start | bytes 2359304 | tf_op jit(solution)/shard_map/ppermute | solution.py:512
  35.1 37.3 %collective-permute-start.1 = (bf16[2,128,1024]{2,1,0:T(8,128)(2,1)S(1)}, bf16[2,128,1024]{2,1,0:T(8,128)(2,1)S(1)}, u32[]{:S(2)}, u32[]{:S(2)}) collective-permute-start(bf16[2,128,1024]{2,1,0:T(8,128)(2,1)S(1)} %pad_maximum_fusion.2.own_ref), channel_id=1, source_target_pairs={{0,96},{32,0},{64,32},{96,64},{1,97},{33,1},{65,33},{97,65},{2,98}... | collective-permute-start | bytes 1572872 | tf_op jit(solution)/shard_map/ppermute | solution.py:516
  38.5 33.9 %collective-permute-start.2 = (bf16[2,128,1024]{2,1,0:T(8,128)(2,1)S(1)}, bf16[2,128,1024]{2,1,0:T(8,128)(2,1)}, u32[]{:S(2)}, u32[]{:S(2)}) collective-permute-start(bf16[2,128,1024]{2,1,0:T(8,128)(2,1)S(1)} %pad_maximum_fusion.2.own_ref), channel_id=1, source_target_pairs={{0,64},{32,96},{64,0},{96,32},{1,65},{33,97},{65,1},{97,33},{2,66}... | collective-permute-start | bytes 1572872 | tf_op jit(solution)/shard_map/ppermute | solution.py:516
  38.9 41.6 %collective-permute-start.3 = (bf16[2,128,1024]{2,1,0:T(8,128)(2,1)S(1)}, bf16[2,128,1024]{2,1,0:T(8,128)(2,1)}, u32[]{:S(2)}, u32[]{:S(2)}) collective-permute-start(bf16[2,128,1024]{2,1,0:T(8,128)(2,1)S(1)} %pad_maximum_fusion.2.own_ref), channel_id=1, source_target_pairs={{0,32},{32,64},{64,96},{96,0},{1,33},{33,65},{65,97},{97,1},{2,34}... | collective-permute-start | bytes 1572872 | tf_op jit(solution)/shard_map/ppermute | solution.py:516
  53.9 49.8 %all-to-all-start.1 = ((bf16[64,8,1024]{2,1,0:T(8,128)(2,1)}), bf16[64,8,1024]{2,1,0:T(8,128)(2,1)}, u32[]{:S(2)}, u32[]{:S(2)}) async-start(bf16[64,8,1024]{2,1,0:T(8,128)(2,1)} %broadcast_in_dim.49), calls=%async_computation.1 | async-start | bytes 2097152 | tf_op jit(solution)/shard_map/all_to_all | solution.py:508
  81.3 35.2 %collective-permute-start.7 = (bf16[2,128,1024]{2,1,0:T(8,128)(2,1)S(1)}, bf16[2,128,1024]{2,1,0:T(8,128)(2,1)}, u32[]{:S(2)}, u32[]{:S(2)}) collective-permute-start(bf16[2,128,1024]{2,1,0:T(8,128)(2,1)S(1)} %pad_maximum_fusion.3.own_ref), channel_id=1, source_target_pairs={{0,64},{32,96},{64,0},{96,32},{1,65},{33,97},{65,1},{97,33},{2,66}... | collective-permute-start | bytes 1572872 | tf_op jit(solution)/shard_map/ppermute | solution.py:516
  81.5 35.0 %collective-permute-start.8 = (bf16[2,128,1024]{2,1,0:T(8,128)(2,1)S(1)}, bf16[2,128,1024]{2,1,0:T(8,128)(2,1)}, u32[]{:S(2)}, u32[]{:S(2)}) collective-permute-start(bf16[2,128,1024]{2,1,0:T(8,128)(2,1)S(1)} %pad_maximum_fusion.3.own_ref), channel_id=1, source_target_pairs={{0,32},{32,64},{64,96},{96,0},{1,33},{33,65},{65,97},{97,1},{2,34}... | collective-permute-start | bytes 1572872 | tf_op jit(solution)/shard_map/ppermute | solution.py:516
  85.2 60.0 %collective-permute-start.11 = (bf16[2,2,3,128,512]{4,3,2,1,0:T(8,128)(2,1)}, bf16[2,2,3,128,512]{4,3,2,1,0:T(8,128)(2,1)}, u32[]{:S(2)}, u32[]{:S(2)}) collective-permute-start(bf16[2,2,3,128,512]{4,3,2,1,0:T(8,128)(2,1)} %pad_maximum_fusion.refs_4_), channel_id=1, source_target_pairs={{0,96},{32,0},{64,32},{96,64},{1,97},{33,1},{65,33},{97,65},{2,98}... | collective-permute-start | bytes 4718600 | tf_op jit(solution)/shard_map/ppermute | solution.py:516
  87.9 57.3 %collective-permute-start.12 = (bf16[2,2,3,128,512]{4,3,2,1,0:T(8,128)(2,1)}, bf16[2,2,3,128,512]{4,3,2,1,0:T(8,128)(2,1)}, u32[]{:S(2)}, u32[]{:S(2)}) collective-permute-start(bf16[2,2,3,128,512]{4,3,2,1,0:T(8,128)(2,1)} %pad_maximum_fusion.refs_4_), channel_id=1, source_target_pairs={{0,32},{32,64},{64,96},{96,0},{1,33},{33,65},{65,97},{97,1},{2,34}... | collective-permute-start | bytes 4718600 | tf_op jit(solution)/shard_map/ppermute | solution.py:516
  146.8 34.0 %all-to-all-start.3 = ((bf16[8,128,1024]{2,1,0:T(8,128)(2,1)}), bf16[8,128,1024]{2,1,0:T(8,128)(2,1)}, u32[]{:S(2)}, u32[]{:S(2)}) async-start(bf16[8,128,1024]{2,1,0:T(8,128)(2,1)} %broadcast_in_dim.50), calls=%async_computation.3 | async-start | bytes 4194304 | tf_op jit(solution)/shard_map/all_to_all | solution.py:508
  152.5 40.3 %collective-permute-start.10 = (bf16[2,2,3,128,512]{4,3,2,1,0:T(8,128)(2,1)}, bf16[2,2,3,128,512]{4,3,2,1,0:T(8,128)(2,1)}, u32[]{:S(2)}, u32[]{:S(2)}) collective-permute-start(bf16[2,2,3,128,512]{4,3,2,1,0:T(8,128)(2,1)} %pad_maximum_fusion.refs_4_), channel_id=1, source_target_pairs={{0,64},{32,96},{64,0},{96,32},{1,65},{33,97},{65,1},{97,33},{2,66}... | collective-permute-start | bytes 4718600 | tf_op jit(solution)/shard_map/ppermute | solution.py:516
  180.8 33.2 %collective-permute-start.13 = (bf16[8,128,1024]{2,1,0:T(8,128)(2,1)}, bf16[8,128,1024]{2,1,0:T(8,128)(2,1)}, u32[]{:S(2)}, u32[]{:S(2)}) collective-permute-start(bf16[8,128,1024]{2,1,0:T(8,128)(2,1)} %all-to-all-done.3.refs_0_), channel_id=1, source_target_pairs={{0,1},{1,0},{2,3},{3,2},{4,5},{5,4},{6,7},{7,6},{8,9},{9,8},{10,11... | collective-permute-start | bytes 6291464 | tf_op jit(solution)/shard_map/ppermute | solution.py:512
  209.0 45.1 %all-to-all-start.5 = ((bf16[8,128,1024]{2,1,0:T(8,128)(2,1)}), bf16[8,128,1024]{2,1,0:T(8,128)(2,1)}, u32[]{:S(2)}, u32[]{:S(2)}) async-start(bf16[8,128,1024]{2,1,0:T(8,128)(2,1)} %broadcast_in_dim.51), calls=%async_computation.5 | async-start | bytes 4194304 | tf_op jit(solution)/shard_map/all_to_all | solution.py:508
  214.0 130.1 %reduce-scatter.2.cloned.1.call-start = ((), (), s32[]{:S(2)}) async-start(), calls=%async_computation.15 | async-start | bytes 4456448 | tf_op jit(solution)/shard_map/reduce_scatter | solution.py:764
  266.1 48.0 %all-to-all-start.6 = ((bf16[8,128,1152]{2,1,0:T(8,128)(2,1)}), bf16[8,128,1152]{2,1,0:T(8,128)(2,1)}, u32[]{:S(2)}, u32[]{:S(2)}) async-start(bf16[8,128,1152]{2,1,0:T(8,128)(2,1)} %add_convert_fusion.1), calls=%async_computation.7 | async-start | bytes 4718592 | tf_op jit(solution)/shard_map/all_to_all | solution.py:508
  314.1 42.1 %collective-permute-start.16 = (bf16[8,128,1152]{2,1,0:T(8,128)(2,1)}, bf16[8,128,1152]{2,1,0:T(8,128)(2,1)}, u32[]{:S(2)}, u32[]{:S(2)}) collective-permute-start(bf16[8,128,1152]{2,1,0:T(8,128)(2,1)} %get-tuple-element.128), channel_id=1, source_target_pairs={{0,1},{1,0},{2,3},{3,2},{4,5},{5,4},{6,7},{7,6},{8,9},{9,8},{10,11... | collective-permute-start | bytes 7077896 | tf_op jit(solution)/shard_map/ppermute | solution.py:512
  315.7 81.9 %collective-permute-start.17 = (bf16[8,128,1024]{2,1,0:T(8,128)(2,1)}, bf16[8,128,1024]{2,1,0:T(8,128)(2,1)}, u32[]{:S(2)}, u32[]{:S(2)}) collective-permute-start(bf16[8,128,1024]{2,1,0:T(8,128)(2,1)} %get-tuple-element.151), channel_id=1, source_target_pairs={{0,1},{1,0},{2,3},{3,2},{4,5},{5,4},{6,7},{7,6},{8,9},{9,8},{10,11... | collective-permute-start | bytes 6291464 | tf_op jit(solution)/shard_map/ppermute | solution.py:512
  359.9 37.8 %all-to-all-start.8 = ((bf16[8,128,1152]{2,1,0:T(8,128)(2,1)}), bf16[8,128,1152]{2,1,0:T(8,128)(2,1)}, u32[]{:S(2)}, u32[]{:S(2)}) async-start(bf16[8,128,1152]{2,1,0:T(8,128)(2,1)} %add_convert_fusion), calls=%async_computation.9 | async-start | bytes 4718592 | tf_op jit(solution)/shard_map/all_to_all | solution.py:508
  409.5 54.0 %collective-permute-start.18 = (bf16[2,2,3,128,512]{4,3,2,1,0:T(8,128)(2,1)}, bf16[2,2,3,128,512]{4,3,2,1,0:T(8,128)(2,1)}, u32[]{:S(2)}, u32[]{:S(2)}) collective-permute-start(bf16[2,2,3,128,512]{4,3,2,1,0:T(8,128)(2,1)} %copy-done.11), channel_id=1, source_target_pairs={{0,32},{32,64},{64,96},{96,0},{1,33},{33,65},{65,97},{97,1},{2,34}... | collective-permute-start | bytes 4718600 | tf_op jit(solution)/shard_map/ppermute | solution.py:516
  411.5 52.0 %collective-permute-start.19 = (bf16[2,2,3,128,512]{4,3,2,1,0:T(8,128)(2,1)}, bf16[2,2,3,128,512]{4,3,2,1,0:T(8,128)(2,1)}, u32[]{:S(2)}, u32[]{:S(2)}) collective-permute-start(bf16[2,2,3,128,512]{4,3,2,1,0:T(8,128)(2,1)} %get-tuple-element.161), channel_id=1, source_target_pairs={{0,96},{32,0},{64,32},{96,64},{1,97},{33,1},{65,33},{97,65},{2,98}... | collective-permute-start | bytes 4718600 | tf_op jit(solution)/shard_map/ppermute | solution.py:516
  416.2 33.1 %collective-permute-start.20 = (bf16[2,128,1024]{2,1,0:T(8,128)(2,1)}, bf16[2,128,1024]{2,1,0:T(8,128)(2,1)}, u32[]{:S(2)}, u32[]{:S(2)}) collective-permute-start(bf16[2,128,1024]{2,1,0:T(8,128)(2,1)} %get-tuple-element.293), channel_id=1, source_target_pairs={{0,2},{2,4},{4,6},{6,0},{1,3},{3,5},{5,7},{7,1},{8,10},{10,12},{12... | collective-permute-start | bytes 1572872 | tf_op jit(solution)/shard_map/ppermute | solution.py:543
  418.2 34.2 %collective-permute-start.21 = (bf16[2,128,1024]{2,1,0:T(8,128)(2,1)}, bf16[2,128,1024]{2,1,0:T(8,128)(2,1)}, u32[]{:S(2)}, u32[]{:S(2)}) collective-permute-start(bf16[2,128,1024]{2,1,0:T(8,128)(2,1)} %get-tuple-element.292), channel_id=1, source_target_pairs={{0,4},{2,6},{4,0},{6,2},{1,5},{3,7},{5,1},{7,3},{8,12},{10,14},{12... | collective-permute-start | bytes 1572872 | tf_op jit(solution)/shard_map/ppermute | solution.py:543
  423.7 55.3 %collective-permute-start.27 = (bf16[64,8,1024]{2,1,0:T(8,128)(2,1)}, bf16[64,8,1024]{2,1,0:T(8,128)(2,1)}, u32[]{:S(2)}, u32[]{:S(2)}) collective-permute-start(bf16[64,8,1024]{2,1,0:T(8,128)(2,1)} %dynamic-slice_bitcast_fusion), channel_id=1, source_target_pairs={{0,1},{1,0},{2,3},{3,2},{4,5},{5,4},{6,7},{7,6},{8,9},{9,8},{10,11... | collective-permute-start | bytes 3145736 | tf_op jit(solution)/shard_map/ppermute | solution.py:512
  424.5 48.7 %all-to-all-start.10 = ((bf16[4,2,128,1024]{3,2,1,0:T(8,128)(2,1)}), bf16[4,2,128,1024]{3,2,1,0:T(8,128)(2,1)}, u32[]{:S(2)}, u32[]{:S(2)}) async-start(bf16[4,2,128,1024]{3,2,1,0:T(8,128)(2,1)} %bitcast.43), calls=%async_computation.11 | async-start | bytes 4194304 | tf_op jit(solution)/shard_map/all_to_all | solution.py:508
  452.5 66.4 %collective-permute-start.23 = (bf16[2,2,3,128,512]{4,3,2,1,0:T(8,128)(2,1)}, bf16[2,2,3,128,512]{4,3,2,1,0:T(8,128)(2,1)}, u32[]{:S(2)}, u32[]{:S(2)}) collective-permute-start(bf16[2,2,3,128,512]{4,3,2,1,0:T(8,128)(2,1)} %get-tuple-element.166), channel_id=1, source_target_pairs={{0,64},{32,96},{64,0},{96,32},{1,65},{33,97},{65,1},{97,33},{2,66}... | collective-permute-start | bytes 4718600 | tf_op jit(solution)/shard_map/ppermute | solution.py:516
  473.2 53.5 %all-to-all-start.11 = ((bf16[4,2,128,1024]{3,2,1,0:T(8,128)(2,1)}), bf16[4,2,128,1024]{3,2,1,0:T(8,128)(2,1)}, u32[]{:S(2)}, u32[]{:S(2)}) async-start(bf16[4,2,128,1024]{3,2,1,0:T(8,128)(2,1)} %bitcast.47), calls=%async_computation.12 | async-start | bytes 4194304 | tf_op jit(solution)/shard_map/all_to_all | solution.py:508
  484.0 33.9 %collective-permute-start.24 = (bf16[128,1024]{1,0:T(8,128)(2,1)S(1)}, bf16[128,1024]{1,0:T(8,128)(2,1)S(1)}, u32[]{:S(2)}, u32[]{:S(2)}) collective-permute-start(bf16[128,1024]{1,0:T(8,128)(2,1)S(1)} %fusion.27), channel_id=1, source_target_pairs={{0,8},{8,0},{1,9},{9,1},{2,10},{10,2},{3,11},{11,3},{4,12},{12,4},... | collective-permute-start | bytes 786440 | tf_op jit(solution)/shard_map/ppermute | solution.py:512
  491.1 55.9 %collective-permute-start.25 = (bf16[128,1024]{1,0:T(8,128)(2,1)}, bf16[128,1024]{1,0:T(8,128)(2,1)S(1)}, u32[]{:S(2)}, u32[]{:S(2)}) collective-permute-start(bf16[128,1024]{1,0:T(8,128)(2,1)} %fusion.24), channel_id=1, source_target_pairs={{0,16},{16,0},{1,17},{17,1},{2,18},{18,2},{3,19},{19,3},{4,20},{20... | collective-permute-start | bytes 786440 | tf_op jit(solution)/shard_map/ppermute | solution.py:512
  544.6 31.2 %collective-permute-start.28 = (bf16[2,3,128,512]{3,2,1,0:T(8,128)(2,1)}, bf16[2,3,128,512]{3,2,1,0:T(8,128)(2,1)}, u32[]{:S(2)}, u32[]{:S(2)}) collective-permute-start(bf16[2,3,128,512]{3,2,1,0:T(8,128)(2,1)} %fusion.6), channel_id=1, source_target_pairs={{0,16},{16,0},{1,17},{17,1},{2,18},{18,2},{3,19},{19,3},{4,20},{20... | collective-permute-start | bytes 2359304 | tf_op jit(solution)/shard_map/ppermute | solution.py:512
  (94 other events, 1199.7 us)
Sparse Core Ops, SparseCore 0:
  10.5 100.1 all-gather.2
  263.1 80.8 reduce-scatter.1

commit v7 on v6

--- a/solution.py
+++ b/solution.py
@@ -77,36 +77,14 @@
 
 def attend_kernel(
     order_ref,
-    own_ref,
-    after_ref,
-    far_ref,
-    before_ref,
-    gain_ref,
-    w_ref,
-    head_gain_ref,
-    cos_ref,
-    sin_ref,
-    seg_col_ref,
-    seg_row_ref,
-    mixed_ref,
-    hidden_ref,
-    q_ref,
-    kv_ref,
-    keys_ref,
-    values_ref,
+    *refs,
 ):
-    tok, width = own_ref.shape[1:]
+    pieces, refs = refs[:-13], refs[-13:]
+    gain_ref, w_ref, head_gain_ref, cos_ref, sin_ref, seg_col_ref, seg_row_ref = refs[:7]
+    mixed_ref, hidden_ref, q_ref, kv_ref, keys_ref, values_ref = refs[7:]
+    tok, width = pieces[0].shape[1:]
     length = hidden_ref.shape[0]
-    pieces = [
-        (own_ref, 0),
-        (own_ref, 1),
-        (after_ref, 0),
-        (after_ref, 1),
-        (far_ref, 0),
-        (far_ref, 1),
-        (before_ref, 0),
-        (before_ref, 1),
-    ]
+    pieces = [(ref, i) for ref in pieces for i in range(ref.shape[0])]
     for r, (ref, i) in enumerate(pieces):
         x = ref[i].astype(F32)
         x = x * lax.rsqrt(jnp.mean(x * x, axis=1, keepdims=True) + EPS) * gain_ref[...]
@@ -284,7 +262,7 @@
 
 def expert_kernel(scalar_ref, *refs, joined):
     x_own_ref, x_other_ref, g_ref, router_ref = refs[:4]
-    pieces, refs = refs[4:8], refs[8:]
+    first_refs, near_refs, far_refs, refs = refs[4:8], refs[8:12], refs[12:16], refs[16:]
     outs, refs = (refs[:1], refs[1:]) if joined else (refs[:2], refs[2:])
     back_own_ref, back_other_ref, xe_ref, de_ref, act_ref, da_ref, db_ref = refs[:7]
     pick_ref, weight_ref, dgate_ref, eo_ref, dr_ref, w_ref = refs[7:]
@@ -295,7 +273,8 @@
 
     for r in range(8):
         rows = pl.ds(pl.multiple_of(scalar_ref[2 + r] * depth, depth), depth)
-        w_ref[:, :, rows] = pieces[r // 2][r % 2]
+        w_ref[0, :, rows] = first_refs[r // 2][r % 2]
+        w_ref[1, :, rows] = (near_refs, far_refs)[r % 2][r // 2][...]
     local, slots, hidden = act_ref.shape
     cap = slots // sources
     first = scalar_ref[0]
@@ -400,7 +379,7 @@
 def run_experts(scalars, x_own, x_other, g_all, micro, router, pieces, cap, joined):
     half, tok, width = x_own.shape
     sources = 2 * half
-    _, local, _, _, hidden = pieces[0].shape
+    local, hidden = 2, pieces[0].shape[3]
     slots = sources * cap
     wide = g_all.shape[2]
     shape = jax.ShapeDtypeStruct
@@ -439,11 +418,11 @@
 
 
 def expert_grad_kernel(order_ref, *refs):
-    kept, outs, total_ref = refs[:10], refs[10:14], refs[14]
+    kept, outs, total_ref = refs[:10], refs[10:16], refs[16]
     left = (kept[0:2], kept[0:2], kept[2:4])
     right = (kept[6:8], kept[8:10], kept[4:6])
     step = pl.program_id(0)
-    depth = outs[0].shape[3]
+    depth = outs[0].shape[2]
     for kind in range(3):
 
         @pl.when(step % 3 == kind)
@@ -451,9 +430,19 @@
             total = dot(left[kind][0][0], right[kind][0][0], 0, 0)
             total_ref[...] = total + dot(left[kind][1][0], right[kind][1][0], 0, 0)
 
-    for r in range(8):
+    def part(r):
         rows = pl.ds(pl.multiple_of(order_ref[r] * depth, depth), depth)
-        outs[r // 2][r % 2, 0, 0] = total_ref[rows].astype(BF)
+        return total_ref[rows].astype(BF)
+
+    @pl.when(step < 3)
+    def _():
+        for r in range(8):
+            outs[r // 2][r % 2, 0] = part(r)
+
+    @pl.when(step >= 3)
+    def _():
+        for r in range(8):
+            outs[4 + r % 2][r // 2, 0] = part(r)
 
 
 def expert_grads(order, kept):
@@ -464,14 +453,12 @@
     shape = jax.ShapeDtypeStruct
     return pl.pallas_call(
         expert_grad_kernel,
-        out_shape=[shape((2, local, 3, depth, hidden), BF)] * 4,
-        grid=(3 * local,),
+        out_shape=[shape((2, 3, depth, hidden), BF)] * 4 + [shape((4, 3, depth, hidden), BF)] * 2,
+        grid=(6,),
         in_specs=[pl.BlockSpec(memory_space=pltpu.SMEM)]
         + [pl.BlockSpec((1,) + a.shape[1:], lambda i: (i // 3, 0, 0)) for a in args],
-        out_specs=[
-            pl.BlockSpec((2, 1, 1, depth, hidden), lambda i: (0, i // 3, i % 3, 0, 0))
-        ]
-        * 4,
+        out_specs=[pl.BlockSpec((2, 1, depth, hidden), lambda i: (0, jnp.minimum(i, 2), 0, 0))] * 4
+        + [pl.BlockSpec((4, 1, depth, hidden), lambda i: (0, jnp.maximum(i - 3, 0), 0, 0))] * 2,
         scratch_shapes=[pltpu.VMEM((width, hidden), F32)],
         compiler_params=pltpu.CompilerParams(vmem_limit_bytes=48 * 1024 * 1024),
         cost_estimate=pl.CostEstimate(flops=14 * 10**9, bytes_accessed=28 << 20, transcendentals=0),
@@ -516,6 +503,20 @@
     return [lax.ppermute(parts[k], "z", perm) for k, perm in ((1, UP), (2, TWO), (3, DOWN))]
 
 
+def across(block):
+    near = [(1, DOWN), (2, TWO), (3, UP)]
+    return [
+        lax.ppermute(
+            block, CTX, [(2 * a + y, 2 * b + 1 - y) for a, b in perm for y in range(2)]
+        )
+        for _, perm in near
+    ]
+
+
+def interleave(first, second):
+    return [block for pair in zip(first, second) for block in pair]
+
+
 def along_z(both):
     before, far, after = by_z([both] * 4)
     return [both, after, far, before]
@@ -547,6 +548,10 @@
     own = lax.dynamic_index_in_dim(parts, place, 0, keepdims=False)
     other = lax.dynamic_index_in_dim(parts, 1 - place, 0, keepdims=False)
     return own + flip(other.astype(BF), axis).astype(F32)
+
+
+def split_parts(parts):
+    return list(parts[:4]), parts[4], parts[5]
 
 
 def sum_parts(parts):
@@ -623,13 +628,10 @@
         axis=2,
     ).transpose(1, 0, 2)
     pieces = jnp.broadcast_to(pieces[:, None], (n_ctx, n_fsdp) + pieces.shape[1:])
-    both_0 = jnp.concatenate([tokens[0], flip(tokens[0], "yl")], axis=0)
-    both_w = jnp.stack([w_gate, w_up, w_down], axis=1)[None]
-    pieces = after_all(pieces, both_0)
+    rows_yl = flip(tokens[0], "yl")
+    seq_rows = [interleave(along_z(tokens[0]), [rows_yl] + across(tokens[0]))]
     head_all = exchange(pieces.reshape((n_all,) + pieces.shape[2:]), ALL).reshape(width, -1)
-    both_w = jnp.concatenate([both_w, flip(both_w, "yl")], axis=0)
-    seq_rows = [along_z(both_0)]
-    head_all = after_all(head_all, *seq_rows[0][1:], both_w)
+    head_all = after_all(head_all, *seq_rows[0][1:])
     w_heads = head_all[:, :span]
     small_all = head_all[:, span:]
     router = small_all[:, :experts]
@@ -649,9 +651,14 @@
         core == 0, jnp.stack([own, other], axis=1), jnp.stack([other, own], axis=1)
     ).reshape(width, width)
 
-    weights = along_z(both_w)
+    stack = jnp.stack([w_gate, w_up, w_down], axis=1)
+    stack = after_all(stack, *seq_rows[0][1:])
+    near = along_z(stack[1])
+    first = along_z(jnp.concatenate([stack[:1], flip(stack[:1], "yl")], axis=0))
     both_1 = jnp.concatenate([tokens[1], flip(tokens[1], "yl")], axis=0)
-    seq_rows.append(along_z(after_all(both_1, *seq_rows[0][1:])))
+    seq_rows.append(along_z(after_all(both_1, near[1], near[3])))
+    far = [flip(block, "yl") for block in near]
+    weights = first + near + far
 
     expert_ids = jnp.arange(experts, dtype=jnp.int32)
     cot = cotangent.reshape(all_tok, width)
@@ -681,14 +688,7 @@
         seg = segments[m, 0]
         return gain_row, w_heads, head_row, cosine, sine, seg[:, None], seg[None, :]
 
-    forward, saved = [], []
-    for m in range(micro):
-        mixed_h, *keep = attend_forward(order, seq_rows[m], *attention_args(m))
-        saved.append(keep)
-        if m == 0:
-            mixed_h = after_all(mixed_h, *seq_rows[1][1:])
-        else:
-            mixed_h = after_all(mixed_h, weights[2])
+    def to_experts(m, mixed_h):
         mixed = to_owner(mixed_h).transpose(1, 0, 2).reshape(tok, width)
         start = tokens[m, 0].astype(F32)
         middle = start + mm(mixed, out_full)
@@ -697,12 +697,20 @@
         chosen_m = chosen[m * tok : (m + 1) * tok]
         logits = jnp.where(chosen_m, mm(hidden_two, router), -1e30)
         gates = jnp.where(chosen_m, jax.nn.softmax(logits, axis=-1), 0.0)
+        hidden_x = hidden_two
         if m == 0:
-            hidden_two_x = after_all(hidden_two, weights[1], weights[3])
-        else:
-            hidden_two_x = hidden_two
-        x_own = exchange.copies(hidden_two_x, GROUP, n_ctx)
-        forward.append((mixed, middle, norm_back, hidden_two, gates, x_own))
+            hidden_x = after_all(hidden_x, *seq_rows[1][1:], near[2])
+        x_own = exchange.copies(hidden_x, GROUP, n_ctx)
+        return [mixed, middle, norm_back, hidden_two, gates, x_own]
+
+    mixed_0, *saved_0 = attend_forward(order, seq_rows[0], *attention_args(0))
+    forward_0 = to_experts(0, after_all(mixed_0, near[1], near[3]))
+    mixed_1, *saved_1 = attend_forward(order, seq_rows[1], *attention_args(1))
+    saved = [saved_0, saved_1]
+    forward_0[5], mixed_1, first[1], first[3] = lax.optimization_barrier(
+        (forward_0[5], mixed_1, first[1], first[3])
+    )
+    forward = [forward_0, to_experts(1, mixed_1)]
 
     def experts_of(m, x_own):
         return run_experts(
@@ -768,43 +776,39 @@
     back_0, back_own, back_other, moe_own, moe_other = lax.optimization_barrier(
         (back_0, back_own, back_other, moe_own, moe_other)
     )
-    back_1 = back_sum(back_own, back_other)
+    back_1 = exchange(back_sum(back_own, back_other), GROUP)
     d_middle_0, d_mixed_0, grads_0 = middle_back(0, sum_parts(back_0))
+    first_parts, own_1, other_1 = split_parts(expert_grads(order, (kept_0, kept_1)))
+    moe_other = flip(moe_other, "core")
+    back_1, d_mixed_0, first_parts, other_1, moe_other = lax.optimization_barrier(
+        (back_1, d_mixed_0, first_parts, other_1, moe_other)
+    )
     d_mixed_0 = exchange(d_mixed_0, CTX)
-    d_mixed_0, back_1 = lax.optimization_barrier((d_mixed_0, back_1))
-    kept_1[0] = after_all(kept_1[0], d_mixed_0)
-    back_1 = exchange(back_1, GROUP)
-    weight_parts = expert_grads(order, (kept_0, kept_1))
-    d_hidden_0, head_grads_0 = attention_back(0, d_mixed_0)
-    moe_other = flip(moe_other, "core")
-    back_1, d_hidden_0, weight_parts, moe_other = lax.optimization_barrier(
-        (back_1, d_hidden_0, weight_parts, moe_other)
-    )
+    first_moved = by_z(first_parts)
+    other_1 = flip(other_1, "yl")
     moe_1 = [add(moe_own[2 * k : 2 * k + 2], moe_other[2 * k : 2 * k + 2]) for k in range(4)]
-    weight_moved = by_z(weight_parts)
+    moe_moved = by_x(moe_1)
     d_middle_1, d_mixed_1, grads_1 = middle_back(1, sum_parts(back_1))
     d_mixed_1 = exchange(d_mixed_1, CTX)
+    d_hidden_0, head_grads_0 = attention_back(0, d_mixed_0)
     d_hidden_0 = z_swap(d_hidden_0)
     d_hidden_1, head_grads_1 = attention_back(1, d_mixed_1)
-    moe_moved = by_x(moe_1)
-    d_hidden_0, d_hidden_1, weight_moved[0], weight_moved[2], moe_moved = (
-        lax.optimization_barrier(
-            (d_hidden_0, d_hidden_1, weight_moved[0], weight_moved[2], moe_moved)
-        )
-    )
+    d_hidden_0, d_hidden_1, other_1, moe_moved = lax.optimization_barrier(
+        (d_hidden_0, d_hidden_1, other_1, moe_moved)
+    )
+    own_1 = [add(own_1[k], other_1[k]) for k in range(4)]
+    second_moved = by_z(own_1)
     d_hidden_1 = z_swap(d_hidden_1)
     d_hidden_0 = pair_sum(sum_parts(d_hidden_0), yl, "yl")
     moe_1 = sum(part.astype(F32) for part in [moe_1[0]] + moe_moved)
     moe_1 = moe_1[0] + flip(moe_1[1].astype(BF), "yh").astype(F32)
     grad_out, grad_router, grad_mlp = jax.tree.map(jnp.add, grads_0, grads_1)
     grad_heads, grad_attn, grad_qk = jax.tree.map(jnp.add, head_grads_0, head_grads_1)
-    d_hidden_1, weight_moved[1], moe_1 = lax.optimization_barrier(
-        (d_hidden_1, weight_moved[1], moe_1)
-    )
-    second = [
-        sum(part[i].astype(F32) for part in [weight_parts[0]] + weight_moved) for i in range(2)
+    d_hidden_1, first_moved, moe_0 = lax.optimization_barrier((d_hidden_1, first_moved, moe_0))
+    first_sums = [
+        sum(part[i].astype(F32) for part in [first_parts[0]] + first_moved) for i in range(2)
     ]
-    from_yl = flip(second[1].astype(BF), "yl")
+    from_yl = flip(first_sums[1].astype(BF), "yl")
     d_hidden_1 = pair_sum(sum_parts(d_hidden_1), yl, "yl")
 
     grad_out = grad_out.astype(BF).reshape(n_all // 2, 2, rows, width)
@@ -821,7 +825,10 @@
     own_heads = jnp.sum(grad_pack[:, :, :span].reshape(n_ctx, n_fsdp, rows, -1), axis=1)
     own_heads = own_heads.transpose(1, 0, 2)
     own_small = jnp.sum(grad_pack[:, :, span:], axis=0)
-    expert_own = second[0] + from_yl.astype(F32)
+    expert_own = [
+        first_sums[0] + from_yl.astype(F32),
+        sum(part.astype(F32) for part in [own_1[0]] + second_moved),
+    ]
     outs = [
         (forward[0][1] + moe_0.astype(F32)).astype(BF),
         (forward[1][1] + moe_1).astype(BF),
@@ -842,9 +849,9 @@
         own_small[:, experts],
         own_small[:, experts + 1],
         own_small[:1, experts + 2],
-        expert_own[:, 0],
-        expert_own[:, 1],
-        expert_own[:, 2],
+        jnp.stack([part[0] for part in expert_own]),
+        jnp.stack([part[1] for part in expert_own]),
+        jnp.stack([part[2] for part in expert_own]),
     )
 
 

time: 601 us -> 655 us (1.090)
  waiting for transfers between devices: 174 us -> 204 us
  local copies, waits for them, and re-layouts: 40.2 us -> 55.5 us
  starting transfers between devices: 144 us -> 152 us
    ppermute x14 -> x19, waiting for transfers between devices: 25 us -> 72.2 us  [flip(): return lax.ppermute(block, axis, FLIP)]
    ppermute x12 -> x18, waiting for transfers between devices: 33.5 us -> 69.3 us  [by_z(): lax.ppermute(parts[k], 'z', perm)]
    reduce_scatter x1, waiting for transfers between devices: 23.4 us -> 0.01 us  [body(): moe_0 = lax.psum_scatter(moe_0, FSDP, scatter_dimension=0, tiled=True)[0]]
    all_to_all x14, waiting for transfers between devices: 84.5 us -> 62.7 us  [swap(): return lax.all_to_all(parts, axis, split_axis=0, concat_axis=0, tiled=True)]
    ppermute x12 -> x18, starting transfers between devices: 17.5 us -> 38.1 us  [by_z(): lax.ppermute(parts[k], 'z', perm)]
    ppermute x14 -> x19, starting transfers between devices: 38.5 us -> 18.2 us  [flip(): return lax.ppermute(block, axis, FLIP)]
    unnamed x167 -> x197, local copies, waits for them, and re-layouts: 19.4 us -> 30.7 us
    ppermute x3, waiting for transfers between devices: 7.46 us -> 0.01 us  [by_x(): lax.ppermute(parts[k], 'x', perm)]
  transfers between devices with their start and end apart: 45 -> 59, of which waited for: 15 -> 18; matrix products, arithmetic and copies ran while one was open for 13% -> 14% of each run, Pallas kernels for 24% -> 22%
where the time goes in v7:
time: 655 us; the launch traced here: 646 us
  waiting for transfers between devices  204 us (31%)
  starting transfers between devices  152 us (23%)
  Pallas kernels  142 us (22%)
  other arithmetic  58.6 us (9%)
  local copies, waits for them, and re-layouts  55.5 us (8%)
  between operations  16.6 us (3%)
  matrix products  16.4 us (3%)
    all_to_all x14, starting transfers between devices, swap(): return lax.all_to_all(parts, axis, split_axis=0, concat_axis=0, tiled=True)  83.4 us
    pallas_call x2, Pallas kernels, run_experts(): pl.pallas_call(functools.partial(expert_kernel, joined=joined), out_shape...  79.9 us
    ppermute x19, waiting for transfers between devices, flip(): return lax.ppermute(block, axis, FLIP)  72.2 us
    ppermute x18, waiting for transfers between devices, by_z(): lax.ppermute(parts[k], 'z', perm)  69.3 us
    all_to_all x14, waiting for transfers between devices, swap(): return lax.all_to_all(parts, axis, split_axis=0, concat_axis=0, tiled=True)  62.7 us
    ppermute x18, starting transfers between devices, by_z(): lax.ppermute(parts[k], 'z', perm)  38.1 us
    unnamed x197, local copies, waits for them, and re-layouts  30.7 us
    pallas_call x2, Pallas kernels, attend_backward(): pl.pallas_call(attend_back_kernel, out_shape=outs, grid=(1,), in_specs=[w...  25.4 us
  transfers between devices with their start and end apart: 59, of which 18 were waited for; matrix products, arithmetic and copies ran while one was open for 14% of the time, Pallas kernels for 22%

profile of v7, /device:TPU:0, one launch (start us, length us, event | category | flops | bytes accessed | tf_op | source)
XLA Modules:
  0.0 645.6 jit_solution(10241397146524281161)
XLA Ops:
  24.1 9.1 %all-to-all-start = ((bf16[128,8,384]{2,1,0:T(8,128)(2,1)}), bf16[128,8,384]{2,1,0:T(8,128)(2,1)S(1)}, u32[]{:S(2)}, u32[]{:S(2)}) async-start(bf16[128,8,384]{2,1,0:T(8,128)(2,1)} %bitcast.7), calls=%async_computation | async-start | bytes 1572864 | tf_op jit(solution)/shard_map/all_to_all | solution.py:495
  38.8 12.5 %all-to-all-done = bf16[128,8,384]{2,1,0:T(8,128)(2,1)S(1)} async-done(((bf16[128,8,384]{2,1,0:T(8,128)(2,1)}), bf16[128,8,384]{2,1,0:T(8,128)(2,1)S(1)}, u32[]{:S(2)}, u32[]{:S(2)}) %all-to-all-start) | async-done | bytes 786464 | tf_op jit(solution)/shard_map/all_to_all | solution.py:495
  52.5 8.1 %all-to-all-start.1 = ((bf16[64,8,1024]{2,1,0:T(8,128)(2,1)}), bf16[64,8,1024]{2,1,0:T(8,128)(2,1)}, u32[]{:S(2)}, u32[]{:S(2)}) async-start(bf16[64,8,1024]{2,1,0:T(8,128)(2,1)} %broadcast_in_dim.46), calls=%async_computation.1 | async-start | bytes 2097152 | tf_op jit(solution)/shard_map/all_to_all | solution.py:495
  76.1 8.7 %all-to-all-done.1 = bf16[64,8,1024]{2,1,0:T(8,128)(2,1)} async-done(((bf16[64,8,1024]{2,1,0:T(8,128)(2,1)}), bf16[64,8,1024]{2,1,0:T(8,128)(2,1)}, u32[]{:S(2)}, u32[]{:S(2)}) %all-to-all-start.1) | async-done | bytes 1048608 | tf_op jit(solution)/shard_map/all_to_all | solution.py:495
  88.2 8.4 %shard_map.246 = (bf16[1024,128]{1,0:T(8,128)(2,1)S(1)}, bf16[1024,1024]{1,0:T(8,128)(2,1)S(1)}, bf16[1024,128]{1,0:T(8,128)(2,1)S(1)}, bf16[1024,128]{1,0:T(8,128)(2,1)S(1)}) custom-call(s32[8]{0:T(128)S(1)} %fusion.52.order_ref, bf16[1,128,1024]{2,1,0:T(8,128)(2,1)S(1)} %get-tuple-element.312.refs_0_, bf16[1,128,1024]{2,1,0:T(8,128)(2,1)} %collective-permute-done.refs_1_, ...), custom_call_target="tpu_custom_call" | custom-call | flops 12000000000 | bytes 8388608 | tf_op jit(solution)/shard_map/pallas_call | solution.py:220
  117.4 4.9 collective-permute-done.13.refs_3_
  122.3 11.4 %collective-permute-done.12.refs_2_ = bf16[2,128,1024]{2,1,0:T(8,128)(2,1)S(1)} collective-permute-done((bf16[2,128,1024]{2,1,0:T(8,128)(2,1)S(1)}, bf16[2,128,1024]{2,1,0:T(8,128)(2,1)S(1)}, u32[]{:S(2)}, u32[]{:S(2)}) %collective-permute-start.12) | collective-permute-done | bytes 524320 | tf_op jit(solution)/shard_map/ppermute | solution.py:503
  141.4 31.5 %collective-permute-done.15 = bf16[1,3,128,512]{3,2,1,0:T(8,128)(2,1)} collective-permute-done((bf16[1,3,128,512]{3,2,1,0:T(8,128)(2,1)}, bf16[1,3,128,512]{3,2,1,0:T(8,128)(2,1)}, u32[]{:S(2)}, u32[]{:S(2)}) %collective-permute-start.15) | collective-permute-done | bytes 393248 | tf_op jit(solution)/shard_map/ppermute | solution.py:499
  178.6 8.5 %shard_map.247 = (bf16[1024,128]{1,0:T(8,128)(2,1)S(1)}, bf16[1024,1024]{1,0:T(8,128)(2,1)S(1)}, bf16[1024,128]{1,0:T(8,128)(2,1)S(1)}, bf16[1024,128]{1,0:T(8,128)(2,1)S(1)}) custom-call(s32[8]{0:T(128)S(1)} %fusion.52.order_ref, bf16[2,128,1024]{2,1,0:T(8,128)(2,1)S(1)} %pad_maximum_fusion.3.refs_0_, ...), custom_call_target="tpu_custom_call" | custom-call | flops 12000000000 | bytes 8388608 | tf_op jit(solution)/shard_map/pallas_call | solution.py:220
  216.2 8.5 %all-to-all-start.5 = ((bf16[8,128,1024]{2,1,0:T(8,128)(2,1)}), bf16[8,128,1024]{2,1,0:T(8,128)(2,1)}, u32[]{:S(2)}, u32[]{:S(2)}) async-start(bf16[8,128,1024]{2,1,0:T(8,128)(2,1)} %broadcast_in_dim.48), calls=%async_computation.5 | async-start | bytes 4194304 | tf_op jit(solution)/shard_map/all_to_all | solution.py:495
  224.7 17.8 %collective-permute-done.23.refs_15_ = bf16[3,128,512]{2,1,0:T(8,128)(2,1)} collective-permute-done((bf16[3,128,512]{2,1,0:T(8,128)(2,1)}, bf16[3,128,512]{2,1,0:T(8,128)(2,1)}, u32[]{:S(2)}, u32[]{:S(2)}) %collective-permute-start.23) | collective-permute-done | bytes 393248 | tf_op jit(solution)/shard_map/ppermute | solution.py:499
  242.5 14.0 %collective-permute-done.21.refs_13_ = bf16[3,128,512]{2,1,0:T(8,128)(2,1)} collective-permute-done((bf16[3,128,512]{2,1,0:T(8,128)(2,1)}, bf16[3,128,512]{2,1,0:T(8,128)(2,1)}, u32[]{:S(2)}, u32[]{:S(2)}) %collective-permute-start.21) | collective-permute-done | bytes 393248 | tf_op jit(solution)/shard_map/ppermute | solution.py:499
  256.6 40.0 %shard_map.248 = (bf16[16,128,1024]{2,1,0:T(8,128)(2,1)}, bf16[8,128,1152]{2,1,0:T(8,128)(2,1)}, bf16[8,128,1152]{2,1,0:T(8,128)(2,1)}, bf16[2,768,1024]{2,1,0:T...) custom-call(s32[18]{0:T(128)} %pad_add_fusion.scalar_ref, ...), custom_call_target="tpu_custom_call" | custom-call | flops 40000000000 | bytes 41943040 | tf_op jit(solution)/shard_map/pallas_call | solution.py:400
  296.7 4.7 collective-permute-done.24
  305.3 8.2 %all-to-all-start.6 = ((bf16[8,128,1152]{2,1,0:T(8,128)(2,1)}), bf16[8,128,1152]{2,1,0:T(8,128)(2,1)}, u32[]{:S(2)}, u32[]{:S(2)}) async-start(bf16[8,128,1152]{2,1,0:T(8,128)(2,1)} %add_convert_fusion.1), calls=%async_computation.6 | async-start | bytes 4718592 | tf_op jit(solution)/shard_map/all_to_all | solution.py:495
  313.6 39.9 %shard_map.249 = (bf16[8,128,1024]{2,1,0:T(8,128)(2,1)}, bf16[8,128,1024]{2,1,0:T(8,128)(2,1)}, bf16[8,128,1152]{2,1,0:T(8,128)(2,1)}, bf16[8,128,1152]{2,1,0:T(...) custom-call(s32[18]{0:T(128)} %pad_add_fusion.scalar_ref, ...), custom_call_target="tpu_custom_call" | custom-call | flops 40000000000 | bytes 41943040 | tf_op jit(solution)/shard_map/pallas_call | solution.py:400
  366.0 7.6 %all-to-all-start.7 = ((bf16[8,128,1152]{2,1,0:T(8,128)(2,1)}), bf16[8,128,1152]{2,1,0:T(8,128)(2,1)}, u32[]{:S(2)}, u32[]{:S(2)}) async-start(bf16[8,128,1152]{2,1,0:T(8,128)(2,1)} %add_convert_fusion), calls=%async_computation.7 | async-start | bytes 4718592 | tf_op jit(solution)/shard_map/all_to_all | solution.py:495
  378.8 20.2 %shard_map.250 = (bf16[2,3,128,512]{3,2,1,0:T(8,128)(2,1)S(1)}, bf16[2,3,128,512]{3,2,1,0:T(8,128)(2,1)}, bf16[2,3,128,512]{3,2,1,0:T(8,128)(2,1)}, bf16[2,3,128...) custom-call(s32[8]{0:T(128)S(1)} %fusion.52.order_ref, ...), custom_call_target="tpu_custom_call" | custom-call | flops 14000000000 | bytes 29360128 | tf_op jit(solution)/shard_map/pallas_call | solution.py:454
  399.9 8.2 %all-to-all-done.7 = bf16[8,128,1152]{2,1,0:T(8,128)(2,1)} async-done(((bf16[8,128,1152]{2,1,0:T(8,128)(2,1)}), bf16[8,128,1152]{2,1,0:T(8,128)(2,1)}, u32[]{:S(2)}, u32[]{:S(2)}) %all-to-all-start.7) | async-done | bytes 2359328 | tf_op jit(solution)/shard_map/all_to_all | solution.py:495
  445.3 12.1 %shard_map.251 = (bf16[1024,1024]{1,0:T(8,128)(2,1)}, f32[1024,256]{1,0:T(8,128)S(1)}, f32[1,1024]{1,0:T(1,128)S(1)}, f32[1,256]{1,0:T(1,128)S(1)}) custom-call(bf16[1024,1024]{1,0:T(8,128)(2,1)S(1)} %copy-done.27, bf16[1024,128]{1,0:T(8,128)(2,1)S(1)} %copy-done.31, bf16[1024,128]{1,0:T(8,128)(2,1)S(1)} %copy-done.33, bf16[1024,128]{1,0:T(8,128)(2,1)S(1)} %bitcast.208, ...), custom_call_target="tpu_custom_call" | custom-call | flops 24999999488 | bytes 8388608 | tf_op jit(solution)/shard_map/pallas_call | solution.py:244
  457.4 12.7 %all-to-all-done.9 = bf16[8,128,128]{2,1,0:T(8,128)(2,1)} async-done(((bf16[8,128,128]{2,1,0:T(8,128)(2,1)}), bf16[8,128,128]{2,1,0:T(8,128)(2,1)}, u32[]{:S(2)}, u32[]{:S(2)}) %all-to-all-start.9) | async-done | bytes 262176 | tf_op jit(solution)/shard_map/all_to_all | solution.py:495
  470.1 4.7 all-to-all-start.10
  482.5 13.3 %shard_map.252 = (bf16[1024,1024]{1,0:T(8,128)(2,1)}, f32[1024,256]{1,0:T(8,128)S(1)}, f32[1,1024]{1,0:T(1,128)S(1)}, f32[1,256]{1,0:T(1,128)S(1)}) custom-call(bf16[1024,1024]{1,0:T(8,128)(2,1)S(1)} %copy-done.29, bf16[1024,128]{1,0:T(8,128)(2,1)S(1)} %copy-done.35, bf16[1024,128]{1,0:T(8,128)(2,1)S(1)} %copy-done.37, ...), custom_call_target="tpu_custom_call" | custom-call | flops 24999999488 | bytes 8388608 | tf_op jit(solution)/shard_map/pallas_call | solution.py:244
  506.2 4.7 all-to-all-start.11
  527.3 26.0 %collective-permute-done.40 = bf16[3,128,512]{2,1,0:T(8,128)(2,1)S(1)} collective-permute-done((bf16[3,128,512]{2,1,0:T(8,128)(2,1)S(1)}, bf16[3,128,512]{2,1,0:T(8,128)(2,1)S(1)}, u32[]{:S(2)}, u32[]{:S(2)}) %collective-permute-start.40) | collective-permute-done | bytes 393248 | tf_op jit(solution)/shard_map/ppermute | solution.py:503
  558.5 5.6 collective-permute-done.41
  566.3 10.7 %collective-permute-done.33 = bf16[2,3,128,512]{3,2,1,0:T(8,128)(2,1)} collective-permute-done((bf16[2,3,128,512]{3,2,1,0:T(8,128)(2,1)}, bf16[2,3,128,512]{3,2,1,0:T(8,128)(2,1)}, u32[]{:S(2)}, u32[]{:S(2)}) %collective-permute-start.33) | collective-permute-done | bytes 786464 | tf_op jit(solution)/shard_map/ppermute | solution.py:503
  577.0 6.5 collective-permute-done.34
  587.3 7.7 %all-to-all-start.12 = ((bf16[64,8,1024]{2,1,0:T(8,128)(2,1)}), bf16[64,8,1024]{2,1,0:T(8,128)(2,1)S(1)}, u32[]{:S(2)}, u32[]{:S(2)}) async-start(bf16[64,8,1024]{2,1,0:T(8,128)(2,1)} %fusion), calls=%async_computation.13 | async-start | bytes 2097152 | tf_op jit(solution)/shard_map/all_to_all | solution.py:495
  604.9 8.8 %all-to-all-done.12 = bf16[64,8,1024]{2,1,0:T(8,128)(2,1)S(1)} async-done(((bf16[64,8,1024]{2,1,0:T(8,128)(2,1)}), bf16[64,8,1024]{2,1,0:T(8,128)(2,1)S(1)}, u32[]{:S(2)}, u32[]{:S(2)}) %all-to-all-start.12) | async-done | bytes 1048608 | tf_op jit(solution)/shard_map/all_to_all | solution.py:495
  613.7 4.6 all-to-all-start.13
  622.8 11.9 %all-to-all-done.13 = bf16[128,8,384]{2,1,0:T(8,128)(2,1)S(1)} async-done(((bf16[128,8,384]{2,1,0:T(8,128)(2,1)}), bf16[128,8,384]{2,1,0:T(8,128)(2,1)S(1)}, u32[]{:S(2)}, u32[]{:S(2)}) %all-to-all-start.13) | async-done | bytes 786464 | tf_op jit(solution)/shard_map/all_to_all | solution.py:495
  (421 shorter events, 227.7 us)
Async XLA Ops:
  7.3 249.3 %all-gather.3.cloned.1.call-start = ((), (), s32[]{:S(2)}) async-start(), calls=%async_computation.16 | async-start | bytes 10027008 | tf_op jit(solution)/shard_map/all_gather | solution.py:671
  16.1 49.6 %collective-permute-start.4 = (bf16[1,128,1024]{2,1,0:T(8,128)(2,1)S(1)}, bf16[1,128,1024]{2,1,0:T(8,128)(2,1)S(1)}, u32[]{:S(2)}, u32[]{:S(2)}) collective-permute-start(bf16[1,128,1024]{2,1,0:T(8,128)(2,1)S(1)} %get-tuple-element.312.refs_0_), channel_id=1, source_target_pairs={{0,80},{16,64},{32,112},{48,96},{64,16},{80,0},{96,48},{112,32},{1... | collective-permute-start | bytes 786440 | tf_op jit(solution)/shard_map/ppermute | solution.py:509
  17.8 49.5 %collective-permute-start.3 = (bf16[1,128,1024]{2,1,0:T(8,128)(2,1)S(1)}, bf16[1,128,1024]{2,1,0:T(8,128)(2,1)S(1)}, u32[]{:S(2)}, u32[]{:S(2)}) collective-permute-start(bf16[1,128,1024]{2,1,0:T(8,128)(2,1)S(1)} %get-tuple-element.312.refs_0_), channel_id=1, source_target_pairs={{0,64},{32,96},{64,0},{96,32},{1,65},{33,97},{65,1},{97,33},{2,66}... | collective-permute-start | bytes 786440 | tf_op jit(solution)/shard_map/ppermute | solution.py:503
  19.5 47.8 %collective-permute-start.2 = (bf16[1,128,1024]{2,1,0:T(8,128)(2,1)S(1)}, bf16[1,128,1024]{2,1,0:T(8,128)(2,1)S(1)}, u32[]{:S(2)}, u32[]{:S(2)}) collective-permute-start(bf16[1,128,1024]{2,1,0:T(8,128)(2,1)S(1)} %get-tuple-element.312.refs_0_), channel_id=1, source_target_pairs={{0,112},{16,96},{32,16},{48,0},{64,48},{80,32},{96,80},{112,64},{1... | collective-permute-start | bytes 786440 | tf_op jit(solution)/shard_map/ppermute | solution.py:509
  34.4 32.9 %collective-permute-start.1 = (bf16[1,128,1024]{2,1,0:T(8,128)(2,1)S(1)}, bf16[1,128,1024]{2,1,0:T(8,128)(2,1)S(1)}, u32[]{:S(2)}, u32[]{:S(2)}) collective-permute-start(bf16[1,128,1024]{2,1,0:T(8,128)(2,1)S(1)} %get-tuple-element.312.refs_0_), channel_id=1, source_target_pairs={{0,96},{32,0},{64,32},{96,64},{1,97},{33,1},{65,33},{97,65},{2,98}... | collective-permute-start | bytes 786440 | tf_op jit(solution)/shard_map/ppermute | solution.py:503
  65.7 37.9 %collective-permute-start.10 = (bf16[1,128,1024]{2,1,0:T(8,128)(2,1)}, bf16[1,128,1024]{2,1,0:T(8,128)(2,1)}, u32[]{:S(2)}, u32[]{:S(2)}) collective-permute-start(bf16[1,128,1024]{2,1,0:T(8,128)(2,1)} %get-tuple-element.311), channel_id=1, source_target_pairs={{0,16},{16,0},{1,17},{17,1},{2,18},{18,2},{3,19},{19,3},{4,20},{20... | collective-permute-start | bytes 786440 | tf_op jit(solution)/shard_map/ppermute | solution.py:499
  68.5 48.9 %collective-permute-start.14 = (bf16[3,128,512]{2,1,0:T(8,128)(2,1)}, bf16[3,128,512]{2,1,0:T(8,128)(2,1)}, u32[]{:S(2)}, u32[]{:S(2)}) collective-permute-start(bf16[3,128,512]{2,1,0:T(8,128)(2,1)} %get-tuple-element.308.refs_8_), channel_id=1, source_target_pairs={{0,64},{32,96},{64,0},{96,32},{1,65},{33,97},{65,1},{97,33},{2,66}... | collective-permute-start | bytes 1179656 | tf_op jit(solution)/shard_map/ppermute | solution.py:503
  135.4 59.5 %all-to-all-start.3 = ((bf16[8,128,1024]{2,1,0:T(8,128)(2,1)}), bf16[8,128,1024]{2,1,0:T(8,128)(2,1)}, u32[]{:S(2)}, u32[]{:S(2)}) async-start(bf16[8,128,1024]{2,1,0:T(8,128)(2,1)} %broadcast_in_dim.47), calls=%async_computation.3 | async-start | bytes 4194304 | tf_op jit(solution)/shard_map/all_to_all | solution.py:495
  139.7 33.1 %collective-permute-start.15 = (bf16[1,3,128,512]{3,2,1,0:T(8,128)(2,1)}, bf16[1,3,128,512]{3,2,1,0:T(8,128)(2,1)}, u32[]{:S(2)}, u32[]{:S(2)}) collective-permute-start(bf16[1,3,128,512]{3,2,1,0:T(8,128)(2,1)} %get-tuple-element.307), channel_id=1, source_target_pairs={{0,16},{16,0},{1,17},{17,1},{2,18},{18,2},{3,19},{19,3},{4,20},{20... | collective-permute-start | bytes 1179656 | tf_op jit(solution)/shard_map/ppermute | solution.py:499
  194.9 61.7 %collective-permute-start.18 = (bf16[8,128,1024]{2,1,0:T(8,128)(2,1)}, bf16[8,128,1024]{2,1,0:T(8,128)(2,1)}, u32[]{:S(2)}, u32[]{:S(2)}) collective-permute-start(bf16[8,128,1024]{2,1,0:T(8,128)(2,1)} %all-to-all-done.3.refs_0_), channel_id=1, source_target_pairs={{0,1},{1,0},{2,3},{3,2},{4,5},{5,4},{6,7},{7,6},{8,9},{9,8},{10,11... | collective-permute-start | bytes 6291464 | tf_op jit(solution)/shard_map/ppermute | solution.py:499
  201.5 55.1 %collective-permute-start.19 = (bf16[2,3,128,512]{3,2,1,0:T(8,128)(2,1)}, bf16[2,3,128,512]{3,2,1,0:T(8,128)(2,1)}, u32[]{:S(2)}, u32[]{:S(2)}) collective-permute-start(bf16[2,3,128,512]{3,2,1,0:T(8,128)(2,1)} %copy-done.75), channel_id=1, source_target_pairs={{0,64},{32,96},{64,0},{96,32},{1,65},{33,97},{65,1},{97,33},{2,66}... | collective-permute-start | bytes 2359304 | tf_op jit(solution)/shard_map/ppermute | solution.py:503
  205.6 36.9 %collective-permute-start.23 = (bf16[3,128,512]{2,1,0:T(8,128)(2,1)}, bf16[3,128,512]{2,1,0:T(8,128)(2,1)}, u32[]{:S(2)}, u32[]{:S(2)}) collective-permute-start(bf16[3,128,512]{2,1,0:T(8,128)(2,1)} %collective-permute-done.8.refs_11_), channel_id=1, source_target_pairs={{0,16},{16,0},{1,17},{17,1},{2,18},{18,2},{3,19},{19,3},{4,20},{20... | collective-permute-start | bytes 1179656 | tf_op jit(solution)/shard_map/ppermute | solution.py:499
  214.4 42.1 %collective-permute-start.21 = (bf16[3,128,512]{2,1,0:T(8,128)(2,1)}, bf16[3,128,512]{2,1,0:T(8,128)(2,1)}, u32[]{:S(2)}, u32[]{:S(2)}) collective-permute-start(bf16[3,128,512]{2,1,0:T(8,128)(2,1)} %collective-permute-done.7.refs_9_), channel_id=1, source_target_pairs={{0,16},{16,0},{1,17},{17,1},{2,18},{18,2},{3,19},{19,3},{4,20},{20... | collective-permute-start | bytes 1179656 | tf_op jit(solution)/shard_map/ppermute | solution.py:499
  216.2 80.4 %all-to-all-start.5 = ((bf16[8,128,1024]{2,1,0:T(8,128)(2,1)}), bf16[8,128,1024]{2,1,0:T(8,128)(2,1)}, u32[]{:S(2)}, u32[]{:S(2)}) async-start(bf16[8,128,1024]{2,1,0:T(8,128)(2,1)} %broadcast_in_dim.48), calls=%async_computation.5 | async-start | bytes 4194304 | tf_op jit(solution)/shard_map/all_to_all | solution.py:495
  305.3 48.2 %all-to-all-start.6 = ((bf16[8,128,1152]{2,1,0:T(8,128)(2,1)}), bf16[8,128,1152]{2,1,0:T(8,128)(2,1)}, u32[]{:S(2)}, u32[]{:S(2)}) async-start(bf16[8,128,1152]{2,1,0:T(8,128)(2,1)} %add_convert_fusion.1), calls=%async_computation.6 | async-start | bytes 4718592 | tf_op jit(solution)/shard_map/all_to_all | solution.py:495
  313.5 252.8 %reduce-scatter.2.cloned.1.call-start = ((), (), s32[]{:S(2)}) async-start(), calls=%async_computation.15 | async-start | bytes 4456448 | tf_op jit(solution)/shard_map/reduce_scatter | solution.py:772
  357.3 42.5 %collective-permute-start.27 = (bf16[8,128,1024]{2,1,0:T(8,128)(2,1)}, bf16[8,128,1024]{2,1,0:T(8,128)(2,1)}, u32[]{:S(2)}, u32[]{:S(2)}) collective-permute-start(bf16[8,128,1024]{2,1,0:T(8,128)(2,1)} %get-tuple-element.149), channel_id=1, source_target_pairs={{0,1},{1,0},{2,3},{3,2},{4,5},{5,4},{6,7},{7,6},{8,9},{9,8},{10,11... | collective-permute-start | bytes 6291464 | tf_op jit(solution)/shard_map/ppermute | solution.py:499
  366.0 42.1 %all-to-all-start.7 = ((bf16[8,128,1152]{2,1,0:T(8,128)(2,1)}), bf16[8,128,1152]{2,1,0:T(8,128)(2,1)}, u32[]{:S(2)}, u32[]{:S(2)}) async-start(bf16[8,128,1152]{2,1,0:T(8,128)(2,1)} %add_convert_fusion), calls=%async_computation.7 | async-start | bytes 4718592 | tf_op jit(solution)/shard_map/all_to_all | solution.py:495
  421.6 84.6 %collective-permute-start.31 = (bf16[2,128,1024]{2,1,0:T(8,128)(2,1)}, bf16[2,128,1024]{2,1,0:T(8,128)(2,1)}, u32[]{:S(2)}, u32[]{:S(2)}) collective-permute-start(bf16[2,128,1024]{2,1,0:T(8,128)(2,1)} %get-tuple-element.295), channel_id=1, source_target_pairs={{0,6},{2,0},{4,2},{6,4},{1,7},{3,1},{5,3},{7,5},{8,14},{10,8},{12,... | collective-permute-start | bytes 1572872 | tf_op jit(solution)/shard_map/ppermute | solution.py:544
  425.5 80.7 %collective-permute-start.30 = (bf16[2,128,1024]{2,1,0:T(8,128)(2,1)}, bf16[2,128,1024]{2,1,0:T(8,128)(2,1)}, u32[]{:S(2)}, u32[]{:S(2)}) collective-permute-start(bf16[2,128,1024]{2,1,0:T(8,128)(2,1)} %get-tuple-element.296), channel_id=1, source_target_pairs={{0,4},{2,6},{4,0},{6,2},{1,5},{3,7},{5,1},{7,3},{8,12},{10,14},{12... | collective-permute-start | bytes 1572872 | tf_op jit(solution)/shard_map/ppermute | solution.py:544
  425.5 80.7 %collective-permute-start.29 = (bf16[2,128,1024]{2,1,0:T(8,128)(2,1)}, bf16[2,128,1024]{2,1,0:T(8,128)(2,1)}, u32[]{:S(2)}, u32[]{:S(2)}) collective-permute-start(bf16[2,128,1024]{2,1,0:T(8,128)(2,1)} %get-tuple-element.297), channel_id=1, source_target_pairs={{0,2},{2,4},{4,6},{6,0},{1,3},{3,5},{5,7},{7,1},{8,10},{10,12},{12... | collective-permute-start | bytes 1572872 | tf_op jit(solution)/shard_map/ppermute | solution.py:544
  426.8 79.3 %collective-permute-start.28 = (bf16[4,3,128,512]{3,2,1,0:T(8,128)(2,1)}, bf16[4,3,128,512]{3,2,1,0:T(8,128)(2,1)}, u32[]{:S(2)}, u32[]{:S(2)}) collective-permute-start(bf16[4,3,128,512]{3,2,1,0:T(8,128)(2,1)} %get-tuple-element.160), channel_id=1, source_target_pairs={{0,16},{16,0},{1,17},{17,1},{2,18},{18,2},{3,19},{19,3},{4,20},{20... | collective-permute-start | bytes 4718600 | tf_op jit(solution)/shard_map/ppermute | solution.py:499
  430.8 70.7 %collective-permute-start.38 = (bf16[64,8,1024]{2,1,0:T(8,128)(2,1)}, bf16[64,8,1024]{2,1,0:T(8,128)(2,1)}, u32[]{:S(2)}, u32[]{:S(2)}) collective-permute-start(bf16[64,8,1024]{2,1,0:T(8,128)(2,1)} %dynamic-slice_bitcast_fusion), channel_id=1, source_target_pairs={{0,1},{1,0},{2,3},{3,2},{4,5},{5,4},{6,7},{7,6},{8,9},{9,8},{10,11... | collective-permute-start | bytes 3145736 | tf_op jit(solution)/shard_map/ppermute | solution.py:499
  432.1 38.0 %all-to-all-start.9 = ((bf16[8,128,128]{2,1,0:T(8,128)(2,1)}), bf16[8,128,128]{2,1,0:T(8,128)(2,1)}, u32[]{:S(2)}, u32[]{:S(2)}) async-start(bf16[8,128,128]{2,1,0:T(8,128)(2,1)} %bitcast.203), calls=%async_computation.9 | async-start | bytes 524288 | tf_op jit(solution)/shard_map/all_to_all | solution.py:495
  470.1 36.0 %all-to-all-start.10 = ((bf16[4,2,128,1024]{3,2,1,0:T(8,128)(2,1)}), bf16[4,2,128,1024]{3,2,1,0:T(8,128)(2,1)}, u32[]{:S(2)}, u32[]{:S(2)}) async-start(bf16[4,2,128,1024]{3,2,1,0:T(8,128)(2,1)} %bitcast.41), calls=%async_computation.10 | async-start | bytes 4194304 | tf_op jit(solution)/shard_map/all_to_all | solution.py:495
  501.4 64.9 %collective-permute-start.32 = (bf16[2,3,128,512]{3,2,1,0:T(8,128)(2,1)}, bf16[2,3,128,512]{3,2,1,0:T(8,128)(2,1)}, u32[]{:S(2)}, u32[]{:S(2)}) collective-permute-start(bf16[2,3,128,512]{3,2,1,0:T(8,128)(2,1)} %get-tuple-element.165), channel_id=1, source_target_pairs={{0,32},{32,64},{64,96},{96,0},{1,33},{33,65},{65,97},{97,1},{2,34}... | collective-permute-start | bytes 2359304 | tf_op jit(solution)/shard_map/ppermute | solution.py:503
  506.2 77.3 %all-to-all-start.11 = ((bf16[4,2,128,1024]{3,2,1,0:T(8,128)(2,1)}), bf16[4,2,128,1024]{3,2,1,0:T(8,128)(2,1)}, u32[]{:S(2)}, u32[]{:S(2)}) async-start(bf16[4,2,128,1024]{3,2,1,0:T(8,128)(2,1)} %bitcast.45), calls=%async_computation.11 | async-start | bytes 4194304 | tf_op jit(solution)/shard_map/all_to_all | solution.py:495
  512.5 40.9 %collective-permute-start.40 = (bf16[3,128,512]{2,1,0:T(8,128)(2,1)S(1)}, bf16[3,128,512]{2,1,0:T(8,128)(2,1)S(1)}, u32[]{:S(2)}, u32[]{:S(2)}) collective-permute-start(bf16[3,128,512]{2,1,0:T(8,128)(2,1)S(1)} %get-tuple-element.298), channel_id=1, source_target_pairs={{0,32},{32,64},{64,96},{96,0},{1,33},{33,65},{65,97},{97,1},{2,34}... | collective-permute-start | bytes 1179656 | tf_op jit(solution)/shard_map/ppermute | solution.py:503
  518.7 38.4 %collective-permute-start.42 = (bf16[3,128,512]{2,1,0:T(8,128)(2,1)S(1)}, bf16[3,128,512]{2,1,0:T(8,128)(2,1)S(1)}, u32[]{:S(2)}, u32[]{:S(2)}) collective-permute-start(bf16[3,128,512]{2,1,0:T(8,128)(2,1)S(1)} %get-tuple-element.299), channel_id=1, source_target_pairs={{0,96},{32,0},{64,32},{96,64},{1,97},{33,1},{65,33},{97,65},{2,98}... | collective-permute-start | bytes 1179656 | tf_op jit(solution)/shard_map/ppermute | solution.py:503
  519.9 44.2 %collective-permute-start.41 = (bf16[3,128,512]{2,1,0:T(8,128)(2,1)S(1)}, bf16[3,128,512]{2,1,0:T(8,128)(2,1)S(1)}, u32[]{:S(2)}, u32[]{:S(2)}) collective-permute-start(bf16[3,128,512]{2,1,0:T(8,128)(2,1)S(1)} %get-tuple-element.300), channel_id=1, source_target_pairs={{0,64},{32,96},{64,0},{96,32},{1,65},{33,97},{65,1},{97,33},{2,66}... | collective-permute-start | bytes 1179656 | tf_op jit(solution)/shard_map/ppermute | solution.py:503
  525.1 51.9 %collective-permute-start.33 = (bf16[2,3,128,512]{3,2,1,0:T(8,128)(2,1)}, bf16[2,3,128,512]{3,2,1,0:T(8,128)(2,1)}, u32[]{:S(2)}, u32[]{:S(2)}) collective-permute-start(bf16[2,3,128,512]{3,2,1,0:T(8,128)(2,1)} %get-tuple-element.166), channel_id=1, source_target_pairs={{0,64},{32,96},{64,0},{96,32},{1,65},{33,97},{65,1},{97,33},{2,66}... | collective-permute-start | bytes 2359304 | tf_op jit(solution)/shard_map/ppermute | solution.py:503
  557.1 43.9 %collective-permute-start.36 = (bf16[128,1024]{1,0:T(8,128)(2,1)}, bf16[128,1024]{1,0:T(8,128)(2,1)}, u32[]{:S(2)}, u32[]{:S(2)}) collective-permute-start(bf16[128,1024]{1,0:T(8,128)(2,1)} %fusion.31), channel_id=1, source_target_pairs={{0,16},{16,0},{1,17},{17,1},{2,18},{18,2},{3,19},{19,3},{4,20},{20... | collective-permute-start | bytes 786440 | tf_op jit(solution)/shard_map/ppermute | solution.py:499
  (123 other events, 2002.5 us)
Sparse Core Ops, SparseCore 0:
  10.5 108.3 all-gather.2
  357.4 94.6 reduce-scatter.1

commit v8 on v6

--- a/solution.py
+++ b/solution.py
@@ -77,36 +77,14 @@
 
 def attend_kernel(
     order_ref,
-    own_ref,
-    after_ref,
-    far_ref,
-    before_ref,
-    gain_ref,
-    w_ref,
-    head_gain_ref,
-    cos_ref,
-    sin_ref,
-    seg_col_ref,
-    seg_row_ref,
-    mixed_ref,
-    hidden_ref,
-    q_ref,
-    kv_ref,
-    keys_ref,
-    values_ref,
+    *refs,
 ):
-    tok, width = own_ref.shape[1:]
+    pieces, refs = refs[:-13], refs[-13:]
+    gain_ref, w_ref, head_gain_ref, cos_ref, sin_ref, seg_col_ref, seg_row_ref = refs[:7]
+    mixed_ref, hidden_ref, q_ref, kv_ref, keys_ref, values_ref = refs[7:]
+    tok, width = pieces[0].shape[1:]
     length = hidden_ref.shape[0]
-    pieces = [
-        (own_ref, 0),
-        (own_ref, 1),
-        (after_ref, 0),
-        (after_ref, 1),
-        (far_ref, 0),
-        (far_ref, 1),
-        (before_ref, 0),
-        (before_ref, 1),
-    ]
+    pieces = [(ref, i) for ref in pieces for i in range(ref.shape[0])]
     for r, (ref, i) in enumerate(pieces):
         x = ref[i].astype(F32)
         x = x * lax.rsqrt(jnp.mean(x * x, axis=1, keepdims=True) + EPS) * gain_ref[...]
@@ -145,6 +123,7 @@
 
 
 def attend_back_kernel(
+    order_ref,
     hidden_ref,
     q_ref,
     kv_ref,
@@ -156,7 +135,10 @@
     sin_ref,
     seg_col_ref,
     seg_row_ref,
-    d_hidden_ref,
+    d_hidden_0_ref,
+    d_hidden_1_ref,
+    d_hidden_2_ref,
+    d_hidden_3_ref,
     grad_w_ref,
     grad_gain_ref,
     grad_heads_ref,
@@ -216,10 +198,12 @@
         d_raw_ref[:, lanes] = d.astype(BF)
     grad_w_ref[...] = dot(hidden_ref[...], d_raw_ref[...], 0, 0)
     total = jnp.zeros(grad_gain_ref.shape, F32)
-    for start in range(0, length, block):
-        rows = slice(start, start + block)
+    outs = (d_hidden_0_ref, d_hidden_1_ref, d_hidden_2_ref, d_hidden_3_ref)
+    tok = length // 8
+    for r in range(8):
+        rows = pl.ds(pl.multiple_of(order_ref[r] * tok, tok), tok)
         d_hidden = dot(d_raw_ref[rows], w_ref[...], 1, 1)
-        d_hidden_ref[rows] = d_hidden.astype(BF)
+        outs[r // 2][r % 2] = d_hidden.astype(BF)
         total = total + jnp.sum(d_hidden * hidden_ref[rows].astype(F32), axis=0, keepdims=True)
     grad_gain_ref[...] = total / gain_ref[...]
 
@@ -252,12 +236,11 @@
 
 
 def attend_backward(
-    hidden, q, kv, d_mixed, gain, w_heads, head_gain, cosine, sine, seg_col, seg_row
+    order, hidden, q, kv, d_mixed, gain, w_heads, head_gain, cosine, sine, seg_col, seg_row
 ):
     length, width = hidden.shape
     shape = jax.ShapeDtypeStruct
-    outs = [
-        shape((length, width), BF),
+    outs = [shape((2, length // 8, width), BF)] * 4 + [
         shape((width, 256), F32),
         shape((1, width), F32),
         shape((1, 256), F32),
@@ -267,14 +250,14 @@
         attend_back_kernel,
         out_shape=outs,
         grid=(1,),
-        in_specs=[whole(a) for a in args],
+        in_specs=[pl.BlockSpec(memory_space=pltpu.SMEM)] + [whole(a) for a in args],
         out_specs=[whole(o) for o in outs],
         scratch_shapes=[pltpu.VMEM((length, 128), BF)] * 2
         + [pltpu.VMEM((length, 128), F32)] * 3
         + [pltpu.VMEM((length, 256), BF)],
         compiler_params=pltpu.CompilerParams(vmem_limit_bytes=40 * 1024 * 1024),
         cost_estimate=pl.CostEstimate(flops=25 * 10**9, bytes_accessed=8 << 20, transcendentals=0),
-    )(*args)
+    )(order, *args)
 
 
 def halves(v):
@@ -516,6 +499,19 @@
     return [lax.ppermute(parts[k], "z", perm) for k, perm in ((1, UP), (2, TWO), (3, DOWN))]
 
 
+def across(block):
+    return [
+        lax.ppermute(
+            block, CTX, [(2 * a + y, 2 * b + 1 - y) for a, b in perm for y in range(2)]
+        )
+        for perm in (DOWN, TWO, UP)
+    ]
+
+
+def interleave(first, second):
+    return [block for pair in zip(first, second) for block in pair]
+
+
 def along_z(both):
     before, far, after = by_z([both] * 4)
     return [both, after, far, before]
@@ -543,10 +539,8 @@
     return [lax.ppermute(parts[k], "x", perm) for k, perm in ((1, UP), (2, TWO), (3, DOWN))]
 
 
-def pair_sum(parts, place, axis):
-    own = lax.dynamic_index_in_dim(parts, place, 0, keepdims=False)
-    other = lax.dynamic_index_in_dim(parts, 1 - place, 0, keepdims=False)
-    return own + flip(other.astype(BF), axis).astype(F32)
+def pair_sums(parts, moved):
+    return [sum(part[i].astype(F32) for part in [parts[0]] + moved) for i in range(2)]
 
 
 def sum_parts(parts):
@@ -623,12 +617,10 @@
         axis=2,
     ).transpose(1, 0, 2)
     pieces = jnp.broadcast_to(pieces[:, None], (n_ctx, n_fsdp) + pieces.shape[1:])
-    both_0 = jnp.concatenate([tokens[0], flip(tokens[0], "yl")], axis=0)
+    seq_rows = [interleave(along_z(tokens[0]), [flip(tokens[0], "yl")] + across(tokens[0]))]
     both_w = jnp.stack([w_gate, w_up, w_down], axis=1)[None]
-    pieces = after_all(pieces, both_0)
     head_all = exchange(pieces.reshape((n_all,) + pieces.shape[2:]), ALL).reshape(width, -1)
     both_w = jnp.concatenate([both_w, flip(both_w, "yl")], axis=0)
-    seq_rows = [along_z(both_0)]
     head_all = after_all(head_all, *seq_rows[0][1:], both_w)
     w_heads = head_all[:, :span]
     small_all = head_all[:, span:]
@@ -643,11 +635,7 @@
     )[None]
     router_pad = jnp.pad(router, ((0, 0), (0, 128 - experts)))
 
-    own = exchange.copies(w_out, CTX + GROUP, n_all // 2)
-    other = flip(own, "core")
-    out_full = jnp.where(
-        core == 0, jnp.stack([own, other], axis=1), jnp.stack([other, own], axis=1)
-    ).reshape(width, width)
+    out_own = exchange.copies(w_out, CTX + GROUP, n_all // 2)
 
     weights = along_z(both_w)
     both_1 = jnp.concatenate([tokens[1], flip(tokens[1], "yl")], axis=0)
@@ -674,22 +662,11 @@
     def to_owner(v):
         return exchange(v.reshape(n_ctx, tok, -1), CTX)
 
-    def z_swap(v):
-        return exchange(v.reshape(4, 2, tok, width), "z")
-
     def attention_args(m):
         seg = segments[m, 0]
         return gain_row, w_heads, head_row, cosine, sine, seg[:, None], seg[None, :]
 
-    forward, saved = [], []
-    for m in range(micro):
-        mixed_h, *keep = attend_forward(order, seq_rows[m], *attention_args(m))
-        saved.append(keep)
-        if m == 0:
-            mixed_h = after_all(mixed_h, *seq_rows[1][1:])
-        else:
-            mixed_h = after_all(mixed_h, weights[2])
-        mixed = to_owner(mixed_h).transpose(1, 0, 2).reshape(tok, width)
+    def to_experts(m, mixed, out_full, *before):
         start = tokens[m, 0].astype(F32)
         middle = start + mm(mixed, out_full)
         normed, norm_back = jax.vjp(rms_scale, middle, gain_mlp)
@@ -697,12 +674,27 @@
         chosen_m = chosen[m * tok : (m + 1) * tok]
         logits = jnp.where(chosen_m, mm(hidden_two, router), -1e30)
         gates = jnp.where(chosen_m, jax.nn.softmax(logits, axis=-1), 0.0)
-        if m == 0:
-            hidden_two_x = after_all(hidden_two, weights[1], weights[3])
-        else:
-            hidden_two_x = hidden_two
-        x_own = exchange.copies(hidden_two_x, GROUP, n_ctx)
-        forward.append((mixed, middle, norm_back, hidden_two, gates, x_own))
+        x_own = exchange.copies(after_all(hidden_two, *before), GROUP, n_ctx)
+        return [mixed, middle, norm_back, hidden_two, gates, x_own]
+
+    def from_heads(mixed_h):
+        return to_owner(mixed_h).transpose(1, 0, 2).reshape(tok, width)
+
+    mixed_0, *saved_0 = attend_forward(order, seq_rows[0], *attention_args(0))
+    out_own, mixed_0 = lax.optimization_barrier((out_own, mixed_0))
+    out_other = flip(out_own, "core")
+    mixed_0 = from_heads(mixed_0)
+    out_full = jnp.where(
+        core == 0,
+        jnp.stack([out_own, out_other], axis=1),
+        jnp.stack([out_other, out_own], axis=1),
+    ).reshape(width, width)
+    forward_0 = to_experts(0, mixed_0, out_full, weights[1], weights[3], *seq_rows[1][1:])
+    mixed_1, *saved_1 = attend_forward(order, seq_rows[1], *attention_args(1))
+    saved = [saved_0, saved_1]
+    forward_0[5], mixed_1 = lax.optimization_barrier((forward_0[5], mixed_1))
+    mixed_1 = from_heads(after_all(mixed_1, weights[2]))
+    forward = [forward_0, to_experts(1, mixed_1, out_full)]
 
     def experts_of(m, x_own):
         return run_experts(
@@ -738,8 +730,8 @@
         return d_middle, d_mixed, (grad_out, grad_router, grad_mlp)
 
     def attention_back(m, d_mixed):
-        d_hidden, grad_heads, grad_attn, grad_qk = attend_backward(
-            *saved[m], d_mixed.reshape(length, heads), *attention_args(m)
+        *d_hidden, grad_heads, grad_attn, grad_qk = attend_backward(
+            order, *saved[m], d_mixed.reshape(length, heads), *attention_args(m)
         )
         grad_qk = jnp.concatenate(
             [grad_qk[0, :DH] + grad_qk[0, DH : 2 * DH], grad_qk[0, 2 * DH : 3 * DH]]
@@ -772,45 +764,35 @@
     d_middle_0, d_mixed_0, grads_0 = middle_back(0, sum_parts(back_0))
     d_mixed_0 = exchange(d_mixed_0, CTX)
     d_mixed_0, back_1 = lax.optimization_barrier((d_mixed_0, back_1))
-    kept_1[0] = after_all(kept_1[0], d_mixed_0)
     back_1 = exchange(back_1, GROUP)
+    d_hidden_0, head_grads_0 = attention_back(0, d_mixed_0)
+    kept_1[0] = after_all(kept_1[0], head_grads_0[0])
     weight_parts = expert_grads(order, (kept_0, kept_1))
-    d_hidden_0, head_grads_0 = attention_back(0, d_mixed_0)
+    hidden_moved_0 = by_z(d_hidden_0)
     moe_other = flip(moe_other, "core")
-    back_1, d_hidden_0, weight_parts, moe_other = lax.optimization_barrier(
-        (back_1, d_hidden_0, weight_parts, moe_other)
-    )
+    back_1, weight_parts, moe_other = lax.optimization_barrier((back_1, weight_parts, moe_other))
+    weight_moved = by_z(weight_parts)
     moe_1 = [add(moe_own[2 * k : 2 * k + 2], moe_other[2 * k : 2 * k + 2]) for k in range(4)]
-    weight_moved = by_z(weight_parts)
+    moe_moved = by_x(moe_1)
     d_middle_1, d_mixed_1, grads_1 = middle_back(1, sum_parts(back_1))
+    d_mixed_1, hidden_moved_0 = lax.optimization_barrier((d_mixed_1, hidden_moved_0))
     d_mixed_1 = exchange(d_mixed_1, CTX)
-    d_hidden_0 = z_swap(d_hidden_0)
-    d_hidden_1, head_grads_1 = attention_back(1, d_mixed_1)
-    moe_moved = by_x(moe_1)
-    d_hidden_0, d_hidden_1, weight_moved[0], weight_moved[2], moe_moved = (
-        lax.optimization_barrier(
-            (d_hidden_0, d_hidden_1, weight_moved[0], weight_moved[2], moe_moved)
-        )
-    )
-    d_hidden_1 = z_swap(d_hidden_1)
-    d_hidden_0 = pair_sum(sum_parts(d_hidden_0), yl, "yl")
-    moe_1 = sum(part.astype(F32) for part in [moe_1[0]] + moe_moved)
-    moe_1 = moe_1[0] + flip(moe_1[1].astype(BF), "yh").astype(F32)
     grad_out, grad_router, grad_mlp = jax.tree.map(jnp.add, grads_0, grads_1)
-    grad_heads, grad_attn, grad_qk = jax.tree.map(jnp.add, head_grads_0, head_grads_1)
-    d_hidden_1, weight_moved[1], moe_1 = lax.optimization_barrier(
-        (d_hidden_1, weight_moved[1], moe_1)
-    )
-    second = [
-        sum(part[i].astype(F32) for part in [weight_parts[0]] + weight_moved) for i in range(2)
-    ]
-    from_yl = flip(second[1].astype(BF), "yl")
-    d_hidden_1 = pair_sum(sum_parts(d_hidden_1), yl, "yl")
-
     grad_out = grad_out.astype(BF).reshape(n_all // 2, 2, rows, width)
     grad_own = lax.dynamic_index_in_dim(grad_out, core, axis=1, keepdims=False)
     grad_other = lax.dynamic_index_in_dim(grad_out, 1 - core, axis=1, keepdims=False)
-    own_out = sum_parts(exchange(back_sum(grad_own, grad_other), CTX + GROUP))
+    grad_out = exchange(back_sum(grad_own, grad_other), CTX + GROUP)
+    d_hidden_1, head_grads_1 = attention_back(1, d_mixed_1)
+    d_hidden_1, weight_moved[0], weight_moved[2], moe_moved = lax.optimization_barrier(
+        (d_hidden_1, weight_moved[0], weight_moved[2], moe_moved)
+    )
+    hidden_moved_1 = by_z(d_hidden_1)
+    hidden_sums = pair_sums(d_hidden_0, hidden_moved_0)
+    d_hidden_0 = hidden_sums[0] + flip(hidden_sums[1].astype(BF), "yl").astype(F32)
+    moe_sums = pair_sums(moe_1, moe_moved)
+    moe_1 = moe_sums[0] + flip(moe_sums[1].astype(BF), "yh").astype(F32)
+    grad_heads, grad_attn, grad_qk = jax.tree.map(jnp.add, head_grads_0, head_grads_1)
+
     grad_qk = jnp.pad(grad_qk[:, None], ((0, 0), (0, rows - 1))).reshape(-1)
     grad_small = jnp.concatenate(
         [grad_router, grad_attn[:, None], grad_mlp[:, None], grad_qk[:, None]], axis=1
@@ -821,7 +803,14 @@
     own_heads = jnp.sum(grad_pack[:, :, :span].reshape(n_ctx, n_fsdp, rows, -1), axis=1)
     own_heads = own_heads.transpose(1, 0, 2)
     own_small = jnp.sum(grad_pack[:, :, span:], axis=0)
-    expert_own = second[0] + from_yl.astype(F32)
+    own_out = sum_parts(grad_out)
+    weight_moved[1], hidden_moved_1, moe_0 = lax.optimization_barrier(
+        (weight_moved[1], hidden_moved_1, after_all(moe_0, grad_pack))
+    )
+    weight_sums = pair_sums(weight_parts, weight_moved)
+    hidden_sums = pair_sums(d_hidden_1, hidden_moved_1)
+    d_hidden_1 = hidden_sums[0] + flip(hidden_sums[1].astype(BF), "yl").astype(F32)
+    expert_own = weight_sums[0] + flip(weight_sums[1].astype(BF), "yl").astype(F32)
     outs = [
         (forward[0][1] + moe_0.astype(F32)).astype(BF),
         (forward[1][1] + moe_1).astype(BF),

time: 601 us -> 616 us (1.025)
  waiting for transfers between devices: 174 us -> 146 us
  starting transfers between devices: 144 us -> 169 us
  local copies, waits for them, and re-layouts: 40.2 us -> 47.5 us
  other arithmetic: 57.8 us -> 64.8 us
    ppermute x14, waiting for transfers between devices: 25 us -> 58.8 us  [flip(): return lax.ppermute(block, axis, FLIP)]
    all_to_all x14 -> x12, starting transfers between devices: 81.8 us -> 109 us  [swap(): return lax.all_to_all(parts, axis, split_axis=0, concat_axis=0, tiled=True)]
    ppermute x14, starting transfers between devices: 38.5 us -> 12.4 us  [flip(): return lax.ppermute(block, axis, FLIP)]
    reduce_scatter x1, waiting for transfers between devices: 23.4 us -> 0.01 us  [body(): moe_0 = lax.psum_scatter(moe_0, FSDP, scatter_dimension=0, tiled=True)[0]]
    all_to_all x14 -> x12, waiting for transfers between devices: 84.5 us -> 61.8 us  [swap(): return lax.all_to_all(parts, axis, split_axis=0, concat_axis=0, tiled=True)]
    ppermute x12 -> x18, starting transfers between devices: 17.5 us -> 33.9 us  [by_z(): lax.ppermute(parts[k], 'z', perm)]
    ppermute x0 -> x3, starting transfers between devices: none -> 8.08 us  [across(): lax.ppermute(block, CTX, [(2 * a + y, 2 * b + 1 - y) for a, b in perm for...]
    ppermute x12 -> x18, waiting for transfers between devices: 33.5 us -> 25.6 us  [by_z(): lax.ppermute(parts[k], 'z', perm)]
  transfers between devices with their start and end apart: 45 -> 52, of which waited for: 15 -> 14; matrix products, arithmetic and copies ran while one was open for 13% -> 16% of each run, Pallas kernels for 24% -> 24%
where the time goes in v8:
time: 616 us; the launch traced here: 608 us
  starting transfers between devices  169 us (27%)
  waiting for transfers between devices  146 us (24%)
  Pallas kernels  146 us (24%)
  other arithmetic  64.8 us (11%)
  local copies, waits for them, and re-layouts  47.5 us (8%)
  matrix products  19.3 us (3%)
  between operations  16.4 us (3%)
    all_to_all x12, starting transfers between devices, swap(): return lax.all_to_all(parts, axis, split_axis=0, concat_axis=0, tiled=True)  109 us
    pallas_call x2, Pallas kernels, run_experts(): pl.pallas_call(functools.partial(expert_kernel, joined=joined), out_shape...  80.1 us
    all_to_all x12, waiting for transfers between devices, swap(): return lax.all_to_all(parts, axis, split_axis=0, concat_axis=0, tiled=True)  61.8 us
    ppermute x14, waiting for transfers between devices, flip(): return lax.ppermute(block, axis, FLIP)  58.8 us
    ppermute x18, starting transfers between devices, by_z(): lax.ppermute(parts[k], 'z', perm)  33.9 us
    pallas_call x2, Pallas kernels, attend_backward(): pl.pallas_call(attend_back_kernel, out_shape=outs, grid=(1,), in_specs=[p...  28.6 us
    unnamed x175, local copies, waits for them, and re-layouts  26 us
    ppermute x18, waiting for transfers between devices, by_z(): lax.ppermute(parts[k], 'z', perm)  25.6 us
  transfers between devices with their start and end apart: 52, of which 14 were waited for; matrix products, arithmetic and copies ran while one was open for 16% of the time, Pallas kernels for 24%

profile of v8, /device:TPU:0, one launch (start us, length us, event | category | flops | bytes accessed | tf_op | source)
XLA Modules:
  0.0 608.4 jit_solution(12090549339611512491)
XLA Ops:
  21.7 9.2 %all-to-all-start = ((bf16[128,8,384]{2,1,0:T(8,128)(2,1)}), bf16[128,8,384]{2,1,0:T(8,128)(2,1)}, u32[]{:S(2)}, u32[]{:S(2)}) async-start(bf16[128,8,384]{2,1,0:T(8,128)(2,1)} %bitcast.6), calls=%async_computation | async-start | bytes 1572864 | tf_op jit(solution)/shard_map/all_to_all | solution.py:491
  38.2 21.0 %collective-permute-done.7 = bf16[1,2,3,128,512]{4,3,2,1,0:T(8,128)(2,1)} collective-permute-done((bf16[1,2,3,128,512]{4,3,2,1,0:T(8,128)(2,1)}, bf16[1,2,3,128,512]{4,3,2,1,0:T(8,128)(2,1)}, u32[]{:S(2)}, u32[]{:S(2)}) %collective-permute-start.7) | collective-permute-done | bytes 786464 | tf_op jit(solution)/shard_map/ppermute | solution.py:495
  62.9 10.2 %all-to-all-start.1 = ((bf16[64,8,1024]{2,1,0:T(8,128)(2,1)}), bf16[64,8,1024]{2,1,0:T(8,128)(2,1)}, u32[]{:S(2)}, u32[]{:S(2)}) async-start(bf16[64,8,1024]{2,1,0:T(8,128)(2,1)} %broadcast_in_dim.41), calls=%async_computation.1 | async-start | bytes 2097152 | tf_op jit(solution)/shard_map/all_to_all | solution.py:491
  77.3 12.8 %collective-permute-done.refs_1_ = bf16[1,128,1024]{2,1,0:T(8,128)(2,1)} collective-permute-done((bf16[1,128,1024]{2,1,0:T(8,128)(2,1)S(1)}, bf16[1,128,1024]{2,1,0:T(8,128)(2,1)}, u32[]{:S(2)}, u32[]{:S(2)}) %collective-permute-start) | collective-permute-done | bytes 262176 | tf_op jit(solution)/shard_map/ppermute | solution.py:495
  96.4 8.4 %shard_map.246 = (bf16[1024,128]{1,0:T(8,128)(2,1)S(1)}, bf16[1024,1024]{1,0:T(8,128)(2,1)S(1)}, bf16[1024,128]{1,0:T(8,128)(2,1)S(1)}, bf16[1024,128]{1,0:T(8,128)(2,1)S(1)}) custom-call(s32[8]{0:T(128)S(1)} %fusion.45.order_ref, bf16[1,128,1024]{2,1,0:T(8,128)(2,1)S(1)} %get-tuple-element.329.refs_0_, bf16[1,128,1024]{2,1,0:T(8,128)(2,1)} %collective-permute-done.refs_1_, ...), custom_call_target="tpu_custom_call" | custom-call | flops 12000000000 | bytes 8388608 | tf_op jit(solution)/shard_map/pallas_call | solution.py:226
  125.1 4.0 maximum_select_fusion
  129.1 30.6 %all-to-all-done.2 = bf16[8,128,128]{1,2,0:T(8,128)(2,1)S(1)} async-done(((bf16[8,128,128]{1,2,0:T(8,128)(2,1)}), bf16[8,128,128]{1,2,0:T(8,128)(2,1)S(1)}, u32[]{:S(2)}, u32[]{:S(2)}) %all-to-all-start.2) | async-done | bytes 262176 | tf_op jit(solution)/shard_map/all_to_all | solution.py:491
  162.1 8.9 %collective-permute-done.14.refs_3_ = bf16[2,128,1024]{2,1,0:T(8,128)(2,1)S(1)} collective-permute-done((bf16[2,128,1024]{2,1,0:T(8,128)(2,1)S(1)}, bf16[2,128,1024]{2,1,0:T(8,128)(2,1)S(1)}, u32[]{:S(2)}, u32[]{:S(2)}) %collective-permute-start.14) | collective-permute-done | bytes 524320 | tf_op jit(solution)/shard_map/ppermute | solution.py:499
  172.7 7.1 %all-to-all-start.3 = ((bf16[8,128,1024]{2,1,0:T(8,128)(2,1)}), bf16[8,128,1024]{2,1,0:T(8,128)(2,1)}, u32[]{:S(2)}, u32[]{:S(2)}) async-start(bf16[8,128,1024]{2,1,0:T(8,128)(2,1)} %broadcast_in_dim.50), calls=%async_computation.3 | async-start | bytes 4194304 | tf_op jit(solution)/shard_map/all_to_all | solution.py:491
  183.2 8.7 %shard_map.247 = (bf16[1024,128]{1,0:T(8,128)(2,1)S(1)}, bf16[1024,1024]{1,0:T(8,128)(2,1)S(1)}, bf16[1024,128]{1,0:T(8,128)(2,1)S(1)}, bf16[1024,128]{1,0:T(8,128)(2,1)S(1)}) custom-call(s32[8]{0:T(128)S(1)} %fusion.45.order_ref, bf16[2,128,1024]{2,1,0:T(8,128)(2,1)S(1)} %pad_maximum_fusion.2.refs_0_, ...), custom_call_target="tpu_custom_call" | custom-call | flops 12000000000 | bytes 8388608 | tf_op jit(solution)/shard_map/pallas_call | solution.py:226
  194.5 13.9 %all-to-all-done.3.refs_0_ = bf16[8,128,1024]{2,1,0:T(8,128)(2,1)} async-done(((bf16[8,128,1024]{2,1,0:T(8,128)(2,1)}), bf16[8,128,1024]{2,1,0:T(8,128)(2,1)}, u32[]{:S(2)}, u32[]{:S(2)}) %all-to-all-start.3) | async-done | bytes 2097184 | tf_op jit(solution)/shard_map/all_to_all | solution.py:491
  208.5 9.6 %collective-permute-done.15.refs_6_ = bf16[2,2,3,128,512]{4,3,2,1,0:T(8,128)(2,1)} collective-permute-done((bf16[2,2,3,128,512]{4,3,2,1,0:T(8,128)(2,1)}, bf16[2,2,3,128,512]{4,3,2,1,0:T(8,128)(2,1)}, u32[]{:S(2)}, u32[]{:S(2)}) %collective-permute-start.15) | collective-permute-done | bytes 1572896 | tf_op jit(solution)/shard_map/ppermute | solution.py:499
  218.9 3.9 all-to-all-start.4
  225.1 4.9 all-to-all-done.4
  234.9 7.5 %all-to-all-start.5 = ((bf16[8,128,1024]{2,1,0:T(8,128)(2,1)}), bf16[8,128,1024]{2,1,0:T(8,128)(2,1)}, u32[]{:S(2)}, u32[]{:S(2)}) async-start(bf16[8,128,1024]{2,1,0:T(8,128)(2,1)} %broadcast_in_dim.51), calls=%async_computation.5 | async-start | bytes 4194304 | tf_op jit(solution)/shard_map/all_to_all | solution.py:491
  242.4 40.0 %shard_map.248 = (bf16[16,128,1024]{2,1,0:T(8,128)(2,1)}, bf16[8,128,1152]{2,1,0:T(8,128)(2,1)}, bf16[8,128,1152]{2,1,0:T(8,128)(2,1)}, bf16[2,768,1024]{2,1,0:T...) custom-call(s32[18]{0:T(128)} %pad_add_fusion.scalar_ref, ...), custom_call_target="tpu_custom_call" | custom-call | flops 40000000000 | bytes 41943040 | tf_op jit(solution)/shard_map/pallas_call | solution.py:404
  282.7 4.7 collective-permute-done.17
  287.4 3.7 add_convert_fusion.1
  292.9 7.2 %all-to-all-start.6 = ((bf16[8,128,1152]{2,1,0:T(8,128)(2,1)}), bf16[8,128,1152]{2,1,0:T(8,128)(2,1)}, u32[]{:S(2)}, u32[]{:S(2)}) async-start(bf16[8,128,1152]{2,1,0:T(8,128)(2,1)} %add_convert_fusion.1), calls=%async_computation.6 | async-start | bytes 4718592 | tf_op jit(solution)/shard_map/all_to_all | solution.py:491
  300.2 40.1 %shard_map.249 = (bf16[8,128,1024]{2,1,0:T(8,128)(2,1)}, bf16[8,128,1024]{2,1,0:T(8,128)(2,1)}, bf16[8,128,1152]{2,1,0:T(8,128)(2,1)}, bf16[8,128,1152]{2,1,0:T(...) custom-call(s32[18]{0:T(128)} %pad_add_fusion.scalar_ref, ...), custom_call_target="tpu_custom_call" | custom-call | flops 40000000000 | bytes 41943040 | tf_op jit(solution)/shard_map/pallas_call | solution.py:404
  355.9 3.7 add_convert_fusion
  359.9 7.6 %all-to-all-start.8 = ((bf16[8,128,1152]{2,1,0:T(8,128)(2,1)}), bf16[8,128,1152]{2,1,0:T(8,128)(2,1)}, u32[]{:S(2)}, u32[]{:S(2)}) async-start(bf16[8,128,1152]{2,1,0:T(8,128)(2,1)} %add_convert_fusion), calls=%async_computation.8 | async-start | bytes 4718592 | tf_op jit(solution)/shard_map/all_to_all | solution.py:491
  370.1 14.3 %shard_map.250 = (bf16[2,128,1024]{2,1,0:T(8,128)(2,1)S(1)}, bf16[2,128,1024]{2,1,0:T(8,128)(2,1)}, bf16[2,128,1024]{2,1,0:T(8,128)(2,1)}, bf16[2,128,1024]{2,1,...) custom-call(s32[8]{0:T(128)S(1)} %fusion.45.order_ref, ...), custom_call_target="tpu_custom_call" | custom-call | flops 24999999488 | bytes 8388608 | tf_op jit(solution)/shard_map/pallas_call | solution.py:249
  391.8 19.9 %shard_map.251 = (bf16[2,2,3,128,512]{4,3,2,1,0:T(8,128)(2,1)S(1)}, bf16[2,2,3,128,512]{4,3,2,1,0:T(8,128)(2,1)S(1)}, bf16[2,2,3,128,512]{4,3,2,1,0:T(8,128)(2,1)}, bf16[2,2,3,128,512]{4,3,2,1,0:T(8,128)(2,1)}) custom-call(s32[8]{0:T(128)S(1)} %fusion.45.order_ref, bf16[2,768,1024]{2,1,0:T(8,128)(2,1)} %get-tuple-element.146.refs_0_, ...), custom_call_target="tpu_custom_call" | custom-call | flops 14000000000 | bytes 29360128 | tf_op jit(solution)/shard_map/pallas_call | solution.py:448
  412.9 4.3 add_convert_fusion.6
  446.2 14.3 %shard_map.252 = (bf16[2,128,1024]{2,1,0:T(8,128)(2,1)S(1)}, bf16[2,128,1024]{2,1,0:T(8,128)(2,1)}, bf16[2,128,1024]{2,1,0:T(8,128)(2,1)}, bf16[2,128,1024]{2,1,...) custom-call(s32[8]{0:T(128)S(1)} %fusion.45.order_ref, ...), custom_call_target="tpu_custom_call" | custom-call | flops 24999999488 | bytes 8388608 | tf_op jit(solution)/shard_map/pallas_call | solution.py:249
  465.8 9.0 %all-to-all-start.10 = ((bf16[64,8,1024]{2,1,0:T(8,128)(2,1)}), bf16[64,8,1024]{2,1,0:T(8,128)(2,1)}, u32[]{:S(2)}, u32[]{:S(2)}) async-start(bf16[64,8,1024]{2,1,0:T(8,128)(2,1)} %fusion), calls=%async_computation.11 | async-start | bytes 2097152 | tf_op jit(solution)/shard_map/all_to_all | solution.py:491
  481.4 12.0 %all-to-all-done.10 = bf16[64,8,1024]{2,1,0:T(8,128)(2,1)} async-done(((bf16[64,8,1024]{2,1,0:T(8,128)(2,1)}), bf16[64,8,1024]{2,1,0:T(8,128)(2,1)}, u32[]{:S(2)}, u32[]{:S(2)}) %all-to-all-start.10) | async-done | bytes 1048608 | tf_op jit(solution)/shard_map/all_to_all | solution.py:491
  493.4 37.1 %all-to-all-start.11 = ((bf16[128,8,384]{2,1,0:T(8,128)(2,1)}), bf16[128,8,384]{2,1,0:T(8,128)(2,1)}, u32[]{:S(2)}, u32[]{:S(2)}) async-start(bf16[128,8,384]{2,1,0:T(8,128)(2,1)} %pad_maximum_fusion.1), calls=%async_computation.12 | async-start | bytes 1572864 | tf_op jit(solution)/shard_map/all_to_all | solution.py:491
  542.0 5.4 collective-permute-done.34
  559.8 7.0 %collective-permute-done.31 = bf16[2,128,1024]{2,1,0:T(8,128)(2,1)} collective-permute-done((bf16[2,128,1024]{2,1,0:T(8,128)(2,1)}, bf16[2,128,1024]{2,1,0:T(8,128)(2,1)}, u32[]{:S(2)}, u32[]{:S(2)}) %collective-permute-start.31) | collective-permute-done | bytes 524320 | tf_op jit(solution)/shard_map/ppermute | solution.py:499
  585.8 12.0 %collective-permute-done.37 = bf16[2,3,128,512]{3,2,1,0:T(8,128)(2,1)S(1)} collective-permute-done((bf16[2,3,128,512]{3,2,1,0:T(8,128)(2,1)}, bf16[2,3,128,512]{3,2,1,0:T(8,128)(2,1)S(1)}, u32[]{:S(2)}, u32[]{:S(2)}) %collective-permute-start.37) | collective-permute-done | bytes 786464 | tf_op jit(solution)/shard_map/ppermute | solution.py:495
  (377 shorter events, 188.8 us)
Async XLA Ops:
  7.3 235.2 %all-gather.3.cloned.1.call-start = ((), (), s32[]{:S(2)}) async-start(), calls=%async_computation.14 | async-start | bytes 10027008 | tf_op jit(solution)/shard_map/all_gather | solution.py:652
  16.1 59.7 %collective-permute-start.4 = (bf16[1,128,1024]{2,1,0:T(8,128)(2,1)S(1)}, bf16[1,128,1024]{2,1,0:T(8,128)(2,1)S(1)}, u32[]{:S(2)}, u32[]{:S(2)}) collective-permute-start(bf16[1,128,1024]{2,1,0:T(8,128)(2,1)S(1)} %get-tuple-element.329.refs_0_), channel_id=1, source_target_pairs={{0,80},{16,64},{32,112},{48,96},{64,16},{80,0},{96,48},{112,32},{1... | collective-permute-start | bytes 786440 | tf_op jit(solution)/shard_map/ppermute | solution.py:504
  17.8 58.0 %collective-permute-start.3 = (bf16[1,128,1024]{2,1,0:T(8,128)(2,1)S(1)}, bf16[1,128,1024]{2,1,0:T(8,128)(2,1)S(1)}, u32[]{:S(2)}, u32[]{:S(2)}) collective-permute-start(bf16[1,128,1024]{2,1,0:T(8,128)(2,1)S(1)} %get-tuple-element.329.refs_0_), channel_id=1, source_target_pairs={{0,64},{32,96},{64,0},{96,32},{1,65},{33,97},{65,1},{97,33},{2,66}... | collective-permute-start | bytes 786440 | tf_op jit(solution)/shard_map/ppermute | solution.py:499
  21.7 40.0 %all-to-all-start = ((bf16[128,8,384]{2,1,0:T(8,128)(2,1)}), bf16[128,8,384]{2,1,0:T(8,128)(2,1)}, u32[]{:S(2)}, u32[]{:S(2)}) async-start(bf16[128,8,384]{2,1,0:T(8,128)(2,1)} %bitcast.6), calls=%async_computation | async-start | bytes 1572864 | tf_op jit(solution)/shard_map/all_to_all | solution.py:491
  34.2 41.6 %collective-permute-start.2 = (bf16[1,128,1024]{2,1,0:T(8,128)(2,1)S(1)}, bf16[1,128,1024]{2,1,0:T(8,128)(2,1)S(1)}, u32[]{:S(2)}, u32[]{:S(2)}) collective-permute-start(bf16[1,128,1024]{2,1,0:T(8,128)(2,1)S(1)} %get-tuple-element.329.refs_0_), channel_id=1, source_target_pairs={{0,112},{16,96},{32,16},{48,0},{64,48},{80,32},{96,80},{112,64},{1... | collective-permute-start | bytes 786440 | tf_op jit(solution)/shard_map/ppermute | solution.py:504
  37.6 39.0 %collective-permute-start.1 = (bf16[1,128,1024]{2,1,0:T(8,128)(2,1)S(1)}, bf16[1,128,1024]{2,1,0:T(8,128)(2,1)S(1)}, u32[]{:S(2)}, u32[]{:S(2)}) collective-permute-start(bf16[1,128,1024]{2,1,0:T(8,128)(2,1)S(1)} %get-tuple-element.329.refs_0_), channel_id=1, source_target_pairs={{0,96},{32,0},{64,32},{96,64},{1,97},{33,1},{65,33},{97,65},{2,98}... | collective-permute-start | bytes 786440 | tf_op jit(solution)/shard_map/ppermute | solution.py:499
  59.2 30.8 %collective-permute-start = (bf16[1,128,1024]{2,1,0:T(8,128)(2,1)S(1)}, bf16[1,128,1024]{2,1,0:T(8,128)(2,1)}, u32[]{:S(2)}, u32[]{:S(2)}) collective-permute-start(bf16[1,128,1024]{2,1,0:T(8,128)(2,1)S(1)} %get-tuple-element.329.refs_0_), channel_id=1, source_target_pairs={{0,16},{16,0},{1,17},{17,1},{2,18},{18,2},{3,19},{19,3},{4,20},{20... | collective-permute-start | bytes 786440 | tf_op jit(solution)/shard_map/ppermute | solution.py:495
  62.9 44.7 %all-to-all-start.1 = ((bf16[64,8,1024]{2,1,0:T(8,128)(2,1)}), bf16[64,8,1024]{2,1,0:T(8,128)(2,1)}, u32[]{:S(2)}, u32[]{:S(2)}) async-start(bf16[64,8,1024]{2,1,0:T(8,128)(2,1)} %broadcast_in_dim.41), calls=%async_computation.1 | async-start | bytes 2097152 | tf_op jit(solution)/shard_map/all_to_all | solution.py:491
  107.5 63.5 %collective-permute-start.10 = (bf16[2,2,3,128,512]{4,3,2,1,0:T(8,128)(2,1)}, bf16[2,2,3,128,512]{4,3,2,1,0:T(8,128)(2,1)}, u32[]{:S(2)}, u32[]{:S(2)}) collective-permute-start(bf16[2,2,3,128,512]{4,3,2,1,0:T(8,128)(2,1)} %pad_maximum_fusion.refs_4_), channel_id=1, source_target_pairs={{0,32},{32,64},{64,96},{96,0},{1,33},{33,65},{65,97},{97,1},{2,34}... | collective-permute-start | bytes 4718600 | tf_op jit(solution)/shard_map/ppermute | solution.py:499
  108.5 62.6 %collective-permute-start.9 = (bf16[2,2,3,128,512]{4,3,2,1,0:T(8,128)(2,1)}, bf16[2,2,3,128,512]{4,3,2,1,0:T(8,128)(2,1)}, u32[]{:S(2)}, u32[]{:S(2)}) collective-permute-start(bf16[2,2,3,128,512]{4,3,2,1,0:T(8,128)(2,1)} %pad_maximum_fusion.refs_4_), channel_id=1, source_target_pairs={{0,96},{32,0},{64,32},{96,64},{1,97},{33,1},{65,33},{97,65},{2,98}... | collective-permute-start | bytes 4718600 | tf_op jit(solution)/shard_map/ppermute | solution.py:499
  114.2 45.5 %all-to-all-start.2 = ((bf16[8,128,128]{1,2,0:T(8,128)(2,1)}), bf16[8,128,128]{1,2,0:T(8,128)(2,1)S(1)}, u32[]{:S(2)}, u32[]{:S(2)}) async-start(bf16[8,128,128]{1,2,0:T(8,128)(2,1)} %copy.201), calls=%async_computation.2 | async-start | bytes 524288 | tf_op jit(solution)/shard_map/all_to_all | solution.py:491
  121.4 49.7 %collective-permute-start.14 = (bf16[2,128,1024]{2,1,0:T(8,128)(2,1)S(1)}, bf16[2,128,1024]{2,1,0:T(8,128)(2,1)S(1)}, u32[]{:S(2)}, u32[]{:S(2)}) collective-permute-start(bf16[2,128,1024]{2,1,0:T(8,128)(2,1)S(1)} %pad_maximum_fusion.2.refs_0_), channel_id=1, source_target_pairs={{0,32},{32,64},{64,96},{96,0},{1,33},{33,65},{65,97},{97,1},{2,34}... | collective-permute-start | bytes 1572872 | tf_op jit(solution)/shard_map/ppermute | solution.py:499
  121.5 49.6 %collective-permute-start.13 = (bf16[2,128,1024]{2,1,0:T(8,128)(2,1)S(1)}, bf16[2,128,1024]{2,1,0:T(8,128)(2,1)}, u32[]{:S(2)}, u32[]{:S(2)}) collective-permute-start(bf16[2,128,1024]{2,1,0:T(8,128)(2,1)S(1)} %pad_maximum_fusion.2.refs_0_), channel_id=1, source_target_pairs={{0,64},{32,96},{64,0},{96,32},{1,65},{33,97},{65,1},{97,33},{2,66}... | collective-permute-start | bytes 1572872 | tf_op jit(solution)/shard_map/ppermute | solution.py:499
  123.3 47.7 %collective-permute-start.12 = (bf16[2,128,1024]{2,1,0:T(8,128)(2,1)S(1)}, bf16[2,128,1024]{2,1,0:T(8,128)(2,1)}, u32[]{:S(2)}, u32[]{:S(2)}) collective-permute-start(bf16[2,128,1024]{2,1,0:T(8,128)(2,1)S(1)} %pad_maximum_fusion.2.refs_0_), channel_id=1, source_target_pairs={{0,96},{32,0},{64,32},{96,64},{1,97},{33,1},{65,33},{97,65},{2,98}... | collective-permute-start | bytes 1572872 | tf_op jit(solution)/shard_map/ppermute | solution.py:499
  172.7 35.8 %all-to-all-start.3 = ((bf16[8,128,1024]{2,1,0:T(8,128)(2,1)}), bf16[8,128,1024]{2,1,0:T(8,128)(2,1)}, u32[]{:S(2)}, u32[]{:S(2)}) async-start(bf16[8,128,1024]{2,1,0:T(8,128)(2,1)} %broadcast_in_dim.50), calls=%async_computation.3 | async-start | bytes 4194304 | tf_op jit(solution)/shard_map/all_to_all | solution.py:491
  180.1 38.0 %collective-permute-start.15 = (bf16[2,2,3,128,512]{4,3,2,1,0:T(8,128)(2,1)}, bf16[2,2,3,128,512]{4,3,2,1,0:T(8,128)(2,1)}, u32[]{:S(2)}, u32[]{:S(2)}) collective-permute-start(bf16[2,2,3,128,512]{4,3,2,1,0:T(8,128)(2,1)} %pad_maximum_fusion.refs_4_), channel_id=1, source_target_pairs={{0,64},{32,96},{64,0},{96,32},{1,65},{33,97},{65,1},{97,33},{2,66}... | collective-permute-start | bytes 4718600 | tf_op jit(solution)/shard_map/ppermute | solution.py:499
  208.5 33.9 %collective-permute-start.16 = (bf16[8,128,1024]{2,1,0:T(8,128)(2,1)}, bf16[8,128,1024]{2,1,0:T(8,128)(2,1)}, u32[]{:S(2)}, u32[]{:S(2)}) collective-permute-start(bf16[8,128,1024]{2,1,0:T(8,128)(2,1)} %all-to-all-done.3.refs_0_), channel_id=1, source_target_pairs={{0,1},{1,0},{2,3},{3,2},{4,5},{5,4},{6,7},{7,6},{8,9},{9,8},{10,11... | collective-permute-start | bytes 6291464 | tf_op jit(solution)/shard_map/ppermute | solution.py:495
  234.9 47.5 %all-to-all-start.5 = ((bf16[8,128,1024]{2,1,0:T(8,128)(2,1)}), bf16[8,128,1024]{2,1,0:T(8,128)(2,1)}, u32[]{:S(2)}, u32[]{:S(2)}) async-start(bf16[8,128,1024]{2,1,0:T(8,128)(2,1)} %broadcast_in_dim.51), calls=%async_computation.5 | async-start | bytes 4194304 | tf_op jit(solution)/shard_map/all_to_all | solution.py:491
  292.9 47.4 %all-to-all-start.6 = ((bf16[8,128,1152]{2,1,0:T(8,128)(2,1)}), bf16[8,128,1152]{2,1,0:T(8,128)(2,1)}, u32[]{:S(2)}, u32[]{:S(2)}) async-start(bf16[8,128,1152]{2,1,0:T(8,128)(2,1)} %add_convert_fusion.1), calls=%async_computation.6 | async-start | bytes 4718592 | tf_op jit(solution)/shard_map/all_to_all | solution.py:491
  300.1 257.2 %reduce-scatter.2.cloned.1.call-start = ((), (), s32[]{:S(2)}) async-start(), calls=%async_computation.13 | async-start | bytes 4456448 | tf_op jit(solution)/shard_map/reduce_scatter | solution.py:756
  351.9 61.0 %collective-permute-start.20 = (bf16[8,128,1024]{2,1,0:T(8,128)(2,1)}, bf16[8,128,1024]{2,1,0:T(8,128)(2,1)}, u32[]{:S(2)}, u32[]{:S(2)}) collective-permute-start(bf16[8,128,1024]{2,1,0:T(8,128)(2,1)} %get-tuple-element.166), channel_id=1, source_target_pairs={{0,1},{1,0},{2,3},{3,2},{4,5},{5,4},{6,7},{7,6},{8,9},{9,8},{10,11... | collective-permute-start | bytes 6291464 | tf_op jit(solution)/shard_map/ppermute | solution.py:495
  359.9 53.0 %all-to-all-start.8 = ((bf16[8,128,1152]{2,1,0:T(8,128)(2,1)}), bf16[8,128,1152]{2,1,0:T(8,128)(2,1)}, u32[]{:S(2)}, u32[]{:S(2)}) async-start(bf16[8,128,1152]{2,1,0:T(8,128)(2,1)} %add_convert_fusion), calls=%async_computation.8 | async-start | bytes 4718592 | tf_op jit(solution)/shard_map/all_to_all | solution.py:491
  385.4 41.8 %collective-permute-start.22 = (bf16[2,128,1024]{2,1,0:T(8,128)(2,1)}, bf16[2,128,1024]{2,1,0:T(8,128)(2,1)}, u32[]{:S(2)}, u32[]{:S(2)}) collective-permute-start(bf16[2,128,1024]{2,1,0:T(8,128)(2,1)} %get-tuple-element.172), channel_id=1, source_target_pairs={{0,32},{32,64},{64,96},{96,0},{1,33},{33,65},{65,97},{97,1},{2,34}... | collective-permute-start | bytes 1572872 | tf_op jit(solution)/shard_map/ppermute | solution.py:499
  387.0 40.2 %collective-permute-start.23 = (bf16[2,128,1024]{2,1,0:T(8,128)(2,1)}, bf16[2,128,1024]{2,1,0:T(8,128)(2,1)}, u32[]{:S(2)}, u32[]{:S(2)}) collective-permute-start(bf16[2,128,1024]{2,1,0:T(8,128)(2,1)} %get-tuple-element.173), channel_id=1, source_target_pairs={{0,64},{32,96},{64,0},{96,32},{1,65},{33,97},{65,1},{97,33},{2,66}... | collective-permute-start | bytes 1572872 | tf_op jit(solution)/shard_map/ppermute | solution.py:499
  389.8 37.4 %collective-permute-start.24 = (bf16[2,128,1024]{2,1,0:T(8,128)(2,1)}, bf16[2,128,1024]{2,1,0:T(8,128)(2,1)}, u32[]{:S(2)}, u32[]{:S(2)}) collective-permute-start(bf16[2,128,1024]{2,1,0:T(8,128)(2,1)} %get-tuple-element.174), channel_id=1, source_target_pairs={{0,96},{32,0},{64,32},{96,64},{1,97},{33,1},{65,33},{97,65},{2,98}... | collective-permute-start | bytes 1572872 | tf_op jit(solution)/shard_map/ppermute | solution.py:499
  417.2 59.7 %collective-permute-start.29 = (bf16[2,128,1024]{2,1,0:T(8,128)(2,1)}, bf16[2,128,1024]{2,1,0:T(8,128)(2,1)}, u32[]{:S(2)}, u32[]{:S(2)}) collective-permute-start(bf16[2,128,1024]{2,1,0:T(8,128)(2,1)} %get-tuple-element.319), channel_id=1, source_target_pairs={{0,6},{2,0},{4,2},{6,4},{1,7},{3,1},{5,3},{7,5},{8,14},{10,8},{12,... | collective-permute-start | bytes 1572872 | tf_op jit(solution)/shard_map/ppermute | solution.py:539
  420.5 60.9 %collective-permute-start.28 = (bf16[2,128,1024]{2,1,0:T(8,128)(2,1)}, bf16[2,128,1024]{2,1,0:T(8,128)(2,1)}, u32[]{:S(2)}, u32[]{:S(2)}) collective-permute-start(bf16[2,128,1024]{2,1,0:T(8,128)(2,1)} %get-tuple-element.321), channel_id=1, source_target_pairs={{0,4},{2,6},{4,0},{6,2},{1,5},{3,7},{5,1},{7,3},{8,12},{10,14},{12... | collective-permute-start | bytes 1572872 | tf_op jit(solution)/shard_map/ppermute | solution.py:539
  430.7 50.7 %collective-permute-start.25 = (bf16[2,2,3,128,512]{4,3,2,1,0:T(8,128)(2,1)}, bf16[2,2,3,128,512]{4,3,2,1,0:T(8,128)(2,1)}, u32[]{:S(2)}, u32[]{:S(2)}) collective-permute-start(bf16[2,2,3,128,512]{4,3,2,1,0:T(8,128)(2,1)} %copy-done.8), channel_id=1, source_target_pairs={{0,32},{32,64},{64,96},{96,0},{1,33},{33,65},{65,97},{97,1},{2,34}... | collective-permute-start | bytes 4718600 | tf_op jit(solution)/shard_map/ppermute | solution.py:499
  432.6 48.8 %collective-permute-start.26 = (bf16[2,2,3,128,512]{4,3,2,1,0:T(8,128)(2,1)}, bf16[2,2,3,128,512]{4,3,2,1,0:T(8,128)(2,1)}, u32[]{:S(2)}, u32[]{:S(2)}) collective-permute-start(bf16[2,2,3,128,512]{4,3,2,1,0:T(8,128)(2,1)} %get-tuple-element.182), channel_id=1, source_target_pairs={{0,96},{32,0},{64,32},{96,64},{1,97},{33,1},{65,33},{97,65},{2,98}... | collective-permute-start | bytes 4718600 | tf_op jit(solution)/shard_map/ppermute | solution.py:499
  476.9 82.9 %collective-permute-start.21 = (bf16[2,2,3,128,512]{4,3,2,1,0:T(8,128)(2,1)}, bf16[2,2,3,128,512]{4,3,2,1,0:T(8,128)(2,1)}, u32[]{:S(2)}, u32[]{:S(2)}) collective-permute-start(bf16[2,2,3,128,512]{4,3,2,1,0:T(8,128)(2,1)} %get-tuple-element.167), channel_id=1, source_target_pairs={{0,64},{32,96},{64,0},{96,32},{1,65},{33,97},{65,1},{97,33},{2,66}... | collective-permute-start | bytes 4718600 | tf_op jit(solution)/shard_map/ppermute | solution.py:499
  493.4 61.5 %all-to-all-start.11 = ((bf16[128,8,384]{2,1,0:T(8,128)(2,1)}), bf16[128,8,384]{2,1,0:T(8,128)(2,1)}, u32[]{:S(2)}, u32[]{:S(2)}) async-start(bf16[128,8,384]{2,1,0:T(8,128)(2,1)} %pad_maximum_fusion.1), calls=%async_computation.12 | async-start | bytes 1572864 | tf_op jit(solution)/shard_map/all_to_all | solution.py:491
  536.4 44.1 %collective-permute-start.35 = (bf16[128,1024]{1,0:T(8,128)(2,1)}, bf16[128,1024]{1,0:T(8,128)(2,1)S(1)}, u32[]{:S(2)}, u32[]{:S(2)}) collective-permute-start(bf16[128,1024]{1,0:T(8,128)(2,1)} %fusion.25), channel_id=1, source_target_pairs={{0,16},{16,0},{1,17},{17,1},{2,18},{18,2},{3,19},{19,3},{4,20},{20... | collective-permute-start | bytes 786440 | tf_op jit(solution)/shard_map/ppermute | solution.py:495
  (105 other events, 1692.2 us)
Sparse Core Ops, SparseCore 0:
  10.5 111.6 all-gather.2
  342.6 104.3 reduce-scatter.1

commit v9 on v8

--- a/solution.py
+++ b/solution.py
@@ -267,7 +267,7 @@
 
 def expert_kernel(scalar_ref, *refs, joined):
     x_own_ref, x_other_ref, g_ref, router_ref = refs[:4]
-    pieces, refs = refs[4:8], refs[8:]
+    pieces, refs = refs[4:9], refs[9:]
     outs, refs = (refs[:1], refs[1:]) if joined else (refs[:2], refs[2:])
     back_own_ref, back_other_ref, xe_ref, de_ref, act_ref, da_ref, db_ref = refs[:7]
     pick_ref, weight_ref, dgate_ref, eo_ref, dr_ref, w_ref = refs[7:]
@@ -276,9 +276,10 @@
     core = scalar_ref[1]
     depth = w_ref.shape[2] // 8
 
-    for r in range(8):
+    pieces = [(ref, i) for ref in pieces for i in range(ref.shape[0])]
+    for r, (ref, i) in enumerate(pieces):
         rows = pl.ds(pl.multiple_of(scalar_ref[2 + r] * depth, depth), depth)
-        w_ref[:, :, rows] = pieces[r // 2][r % 2]
+        w_ref[:, :, rows] = ref[i]
     local, slots, hidden = act_ref.shape
     cap = slots // sources
     first = scalar_ref[0]
@@ -499,19 +500,6 @@
     return [lax.ppermute(parts[k], "z", perm) for k, perm in ((1, UP), (2, TWO), (3, DOWN))]
 
 
-def across(block):
-    return [
-        lax.ppermute(
-            block, CTX, [(2 * a + y, 2 * b + 1 - y) for a, b in perm for y in range(2)]
-        )
-        for perm in (DOWN, TWO, UP)
-    ]
-
-
-def interleave(first, second):
-    return [block for pair in zip(first, second) for block in pair]
-
-
 def along_z(both):
     before, far, after = by_z([both] * 4)
     return [both, after, far, before]
@@ -537,6 +525,12 @@
 
 def by_x(parts):
     return [lax.ppermute(parts[k], "x", perm) for k, perm in ((1, UP), (2, TWO), (3, DOWN))]
+
+
+def add_part(parts, i, more):
+    pieces = [parts[:1], parts[1:]]
+    pieces[i] = add(pieces[i], more)
+    return jnp.concatenate(pieces, axis=0)
 
 
 def pair_sums(parts, moved):
@@ -617,10 +611,14 @@
         axis=2,
     ).transpose(1, 0, 2)
     pieces = jnp.broadcast_to(pieces[:, None], (n_ctx, n_fsdp) + pieces.shape[1:])
-    seq_rows = [interleave(along_z(tokens[0]), [flip(tokens[0], "yl")] + across(tokens[0]))]
+    both_0, both_1 = (
+        jnp.concatenate([tokens[m], flip(tokens[m], "yl")], axis=0) for m in range(micro)
+    )
     both_w = jnp.stack([w_gate, w_up, w_down], axis=1)[None]
     head_all = exchange(pieces.reshape((n_all,) + pieces.shape[2:]), ALL).reshape(width, -1)
     both_w = jnp.concatenate([both_w, flip(both_w, "yl")], axis=0)
+    seq_rows = [along_z(both_0)]
+    seq_rows.append(along_z(after_all(both_1, *seq_rows[0][1:])))
     head_all = after_all(head_all, *seq_rows[0][1:], both_w)
     w_heads = head_all[:, :span]
     small_all = head_all[:, span:]
@@ -637,9 +635,10 @@
 
     out_own = exchange.copies(w_out, CTX + GROUP, n_all // 2)
 
-    weights = along_z(both_w)
-    both_1 = jnp.concatenate([tokens[1], flip(tokens[1], "yl")], axis=0)
-    seq_rows.append(along_z(after_all(both_1, *seq_rows[0][1:])))
+    both_w = after_all(both_w, *seq_rows[1][1:])
+    w_before = lax.ppermute(both_w, "z", UP)
+    w_after = lax.ppermute(both_w, "z", DOWN)
+    w_far = [lax.ppermute(w_before[:1], "z", UP), lax.ppermute(w_after[1:], "z", DOWN)]
 
     expert_ids = jnp.arange(experts, dtype=jnp.int32)
     cot = cotangent.reshape(all_tok, width)
@@ -666,35 +665,32 @@
         seg = segments[m, 0]
         return gain_row, w_heads, head_row, cosine, sine, seg[:, None], seg[None, :]
 
-    def to_experts(m, mixed, out_full, *before):
-        start = tokens[m, 0].astype(F32)
-        middle = start + mm(mixed, out_full)
-        normed, norm_back = jax.vjp(rms_scale, middle, gain_mlp)
-        hidden_two = normed.astype(BF)
-        chosen_m = chosen[m * tok : (m + 1) * tok]
-        logits = jnp.where(chosen_m, mm(hidden_two, router), -1e30)
-        gates = jnp.where(chosen_m, jax.nn.softmax(logits, axis=-1), 0.0)
-        x_own = exchange.copies(after_all(hidden_two, *before), GROUP, n_ctx)
-        return [mixed, middle, norm_back, hidden_two, gates, x_own]
-
-    def from_heads(mixed_h):
-        return to_owner(mixed_h).transpose(1, 0, 2).reshape(tok, width)
-
     mixed_0, *saved_0 = attend_forward(order, seq_rows[0], *attention_args(0))
-    out_own, mixed_0 = lax.optimization_barrier((out_own, mixed_0))
+    mixed_1, *saved_1 = attend_forward(order, seq_rows[1], *attention_args(1))
+    saved = [saved_0, saved_1]
+    out_own, mixed_0, mixed_1 = lax.optimization_barrier((out_own, mixed_0, mixed_1))
     out_other = flip(out_own, "core")
-    mixed_0 = from_heads(mixed_0)
+    mixed = jnp.stack([mixed_0, mixed_1]).reshape(micro, n_ctx, tok, heads).transpose(1, 0, 2, 3)
+    mixed = exchange(mixed.reshape(n_ctx, all_tok, heads), CTX)
+    mixed = mixed.transpose(1, 0, 2).reshape(all_tok, width)
     out_full = jnp.where(
         core == 0,
         jnp.stack([out_own, out_other], axis=1),
         jnp.stack([out_other, out_own], axis=1),
     ).reshape(width, width)
-    forward_0 = to_experts(0, mixed_0, out_full, weights[1], weights[3], *seq_rows[1][1:])
-    mixed_1, *saved_1 = attend_forward(order, seq_rows[1], *attention_args(1))
-    saved = [saved_0, saved_1]
-    forward_0[5], mixed_1 = lax.optimization_barrier((forward_0[5], mixed_1))
-    mixed_1 = from_heads(after_all(mixed_1, weights[2]))
-    forward = [forward_0, to_experts(1, mixed_1, out_full)]
+    middle = tokens.reshape(all_tok, width).astype(F32) + mm(mixed, out_full)
+    inv_two = lax.rsqrt(jnp.mean(middle * middle, axis=-1, keepdims=True) + EPS)
+    hidden_two = (middle * inv_two * gain_mlp).astype(BF)
+    x_0 = after_all(hidden_two[:tok], w_before, w_after)
+    x_0 = exchange.copies(x_0, GROUP, n_ctx)
+    x_0, *w_far = lax.optimization_barrier((x_0, *w_far))
+    x_1 = exchange.copies(hidden_two[tok:], GROUP, n_ctx)
+    weights = [both_w, w_after, *w_far, w_before]
+    logits = jnp.where(chosen, mm(hidden_two, router), -1e30)
+    gates_all = jnp.where(chosen, jax.nn.softmax(logits, axis=-1), 0.0)
+
+    def own_rows(v, m):
+        return v[m * tok : (m + 1) * tok]
 
     def experts_of(m, x_own):
         return run_experts(
@@ -713,18 +709,25 @@
         return add(own, flip(other, "core"))
 
     def middle_back(m, back):
-        mixed, middle, norm_back, hidden_two, gates = forward[m][:5]
-        grad_top = cot[m * tok : (m + 1) * tok].astype(F32)
+        rows_mixed, rows_middle, inv, hidden, gates = (
+            own_rows(v, m) for v in (mixed, middle, inv_two, hidden_two, gates_all)
+        )
+        grad_top = own_rows(cot, m).astype(F32)
         tail = back[:, width:]
         d_gates = tail[:, :experts] + tail[:, 64 : 64 + experts]
         d_select = gates * (d_gates - jnp.sum(gates * d_gates, axis=-1, keepdims=True))
         d_logits = d_select.astype(BF)
-        grad_router = t_mm(hidden_two, d_logits)
+        grad_router = t_mm(hidden, d_logits)
         d_two = back[:, :width] + mm_t(d_logits, router)
-        d_middle, grad_mlp = norm_back(d_two)
-        d_middle = d_middle + grad_top
+        grad_mlp = jnp.sum(d_two * rows_middle * inv, axis=0)
+        u = d_two * gain_mlp
+        d_middle = (
+            grad_top
+            + inv * u
+            - rows_middle * (inv**3 * jnp.mean(u * rows_middle, axis=-1, keepdims=True))
+        )
         d_branch = d_middle.astype(BF)
-        grad_out = t_mm(mixed, d_branch)
+        grad_out = t_mm(rows_mixed, d_branch)
         d_mixed = mm_t(d_branch, out_full).astype(BF)
         d_mixed = d_mixed.reshape(tok, n_ctx, heads).transpose(1, 0, 2)
         return d_middle, d_mixed, (grad_out, grad_router, grad_mlp)
@@ -748,9 +751,9 @@
             - start * (inverse**3 * jnp.mean(u * start, axis=-1, keepdims=True))
         )
 
-    moe_0, back_own, back_other, *kept_0 = experts_of(0, forward[0][5])
+    moe_0, back_own, back_other, *kept_0 = experts_of(0, x_0)
     x_1, back_own, back_other, moe_0 = lax.optimization_barrier(
-        (forward[1][5], back_own, back_other, moe_0)
+        (x_1, back_own, back_other, moe_0)
     )
     back_0 = back_sum(back_own, back_other)
     moe_0 = lax.psum_scatter(moe_0, FSDP, scatter_dimension=0, tiled=True)[0]
@@ -765,32 +768,49 @@
     d_mixed_0 = exchange(d_mixed_0, CTX)
     d_mixed_0, back_1 = lax.optimization_barrier((d_mixed_0, back_1))
     back_1 = exchange(back_1, GROUP)
-    d_hidden_0, head_grads_0 = attention_back(0, d_mixed_0)
-    kept_1[0] = after_all(kept_1[0], head_grads_0[0])
+    kept_1[0] = after_all(kept_1[0], d_mixed_0)
     weight_parts = expert_grads(order, (kept_0, kept_1))
+    weight_far = [
+        lax.ppermute(weight_parts[2][:1], "z", UP),
+        lax.ppermute(weight_parts[2][1:], "z", DOWN),
+    ]
+    d_hidden_0, head_grads_0 = attention_back(0, after_all(d_mixed_0, weight_parts[0]))
     hidden_moved_0 = by_z(d_hidden_0)
     moe_other = flip(moe_other, "core")
-    back_1, weight_parts, moe_other = lax.optimization_barrier((back_1, weight_parts, moe_other))
-    weight_moved = by_z(weight_parts)
+    back_1, d_hidden_0[0], moe_other, *weight_far = lax.optimization_barrier(
+        (back_1, d_hidden_0[0], moe_other, *weight_far)
+    )
+    d_middle_1, d_mixed_1, grads_1 = middle_back(1, sum_parts(back_1))
+    weight_after = add_part(weight_parts[1], 0, weight_far[0])
+    weight_before = add_part(weight_parts[3], 1, weight_far[1])
     moe_1 = [add(moe_own[2 * k : 2 * k + 2], moe_other[2 * k : 2 * k + 2]) for k in range(4)]
+    d_mixed_1, hidden_moved_0 = lax.optimization_barrier((d_mixed_1, hidden_moved_0))
+    weight_moved = [
+        lax.ppermute(weight_after, "z", UP),
+        lax.ppermute(weight_before, "z", DOWN),
+    ]
+    d_mixed_1 = exchange(d_mixed_1, CTX)
     moe_moved = by_x(moe_1)
-    d_middle_1, d_mixed_1, grads_1 = middle_back(1, sum_parts(back_1))
-    d_mixed_1, hidden_moved_0 = lax.optimization_barrier((d_mixed_1, hidden_moved_0))
-    d_mixed_1 = exchange(d_mixed_1, CTX)
     grad_out, grad_router, grad_mlp = jax.tree.map(jnp.add, grads_0, grads_1)
     grad_out = grad_out.astype(BF).reshape(n_all // 2, 2, rows, width)
     grad_own = lax.dynamic_index_in_dim(grad_out, core, axis=1, keepdims=False)
     grad_other = lax.dynamic_index_in_dim(grad_out, 1 - core, axis=1, keepdims=False)
-    grad_out = exchange(back_sum(grad_own, grad_other), CTX + GROUP)
+    grad_out = back_sum(grad_own, grad_other)
     d_hidden_1, head_grads_1 = attention_back(1, d_mixed_1)
-    d_hidden_1, weight_moved[0], weight_moved[2], moe_moved = lax.optimization_barrier(
-        (d_hidden_1, weight_moved[0], weight_moved[2], moe_moved)
-    )
+    grad_out = exchange(grad_out, CTX + GROUP)
     hidden_moved_1 = by_z(d_hidden_1)
     hidden_sums = pair_sums(d_hidden_0, hidden_moved_0)
     d_hidden_0 = hidden_sums[0] + flip(hidden_sums[1].astype(BF), "yl").astype(F32)
+    grad_out, hidden_moved_1, weight_moved, moe_moved = lax.optimization_barrier(
+        (grad_out, hidden_moved_1, weight_moved, moe_moved)
+    )
+    exchange.last = grad_out
+    weight_sums = pair_sums(weight_parts, weight_moved)
+    weight_yl = flip(weight_sums[1].astype(BF), "yl")
+    hidden_sums = pair_sums(d_hidden_1, hidden_moved_1)
+    hidden_yl = flip(hidden_sums[1].astype(BF), "yl")
     moe_sums = pair_sums(moe_1, moe_moved)
-    moe_1 = moe_sums[0] + flip(moe_sums[1].astype(BF), "yh").astype(F32)
+    moe_yh = flip(moe_sums[1].astype(BF), "yh")
     grad_heads, grad_attn, grad_qk = jax.tree.map(jnp.add, head_grads_0, head_grads_1)
 
     grad_qk = jnp.pad(grad_qk[:, None], ((0, 0), (0, rows - 1))).reshape(-1)
@@ -804,16 +824,13 @@
     own_heads = own_heads.transpose(1, 0, 2)
     own_small = jnp.sum(grad_pack[:, :, span:], axis=0)
     own_out = sum_parts(grad_out)
-    weight_moved[1], hidden_moved_1, moe_0 = lax.optimization_barrier(
-        (weight_moved[1], hidden_moved_1, after_all(moe_0, grad_pack))
-    )
-    weight_sums = pair_sums(weight_parts, weight_moved)
-    hidden_sums = pair_sums(d_hidden_1, hidden_moved_1)
-    d_hidden_1 = hidden_sums[0] + flip(hidden_sums[1].astype(BF), "yl").astype(F32)
-    expert_own = weight_sums[0] + flip(weight_sums[1].astype(BF), "yl").astype(F32)
+    moe_0 = after_all(moe_0, grad_pack)
+    d_hidden_1 = hidden_sums[0] + hidden_yl.astype(F32)
+    expert_own = weight_sums[0] + weight_yl.astype(F32)
+    moe_1 = moe_sums[0] + moe_yh.astype(F32)
     outs = [
-        (forward[0][1] + moe_0.astype(F32)).astype(BF),
-        (forward[1][1] + moe_1).astype(BF),
+        (own_rows(middle, 0) + moe_0.astype(F32)).astype(BF),
+        (own_rows(middle, 1) + moe_1).astype(BF),
     ]
     d_inputs = [
         input_grad(0, d_hidden_0, d_middle_0),

time: 616 us -> 600 us (0.974)
  starting transfers between devices: 169 us -> 125 us
  waiting for transfers between devices: 146 us -> 176 us
    ppermute x3 -> x8, waiting for transfers between devices: 0.01 us -> 45.2 us  [the longest x1 29.2 us: body(): w_before = lax.ppermute(both_w, 'z', UP)]
    all_to_all x12 -> x11, waiting for transfers between devices: 61.8 us -> 21.6 us  [swap(): return lax.all_to_all(parts, axis, split_axis=0, concat_axis=0, tiled=True)]
    all_to_all x12 -> x11, starting transfers between devices: 109 us -> 75.3 us  [swap(): return lax.all_to_all(parts, axis, split_axis=0, concat_axis=0, tiled=True)]
    ppermute x18 -> x12, waiting for transfers between devices: 25.6 us -> 49.2 us  [by_z(): lax.ppermute(parts[k], 'z', perm)]
    ppermute x18 -> x12, starting transfers between devices: 33.9 us -> 20.1 us  [by_z(): lax.ppermute(parts[k], 'z', perm)]
    ppermute x3 -> x8, starting transfers between devices: 8.08 us -> 14.1 us  [the longest x1 3.01 us: body(): lax.ppermute(w_after[1:], 'z', DOWN)]
    convert_element_type x4 -> x6, other arithmetic: 14.3 us -> 16.7 us  [add(): return (a.astype(F32) + b.astype(F32)).astype(BF)]
    unnamed x175 -> x173, local copies, waits for them, and re-layouts: 26 us -> 24.8 us
  transfers between devices with their start and end apart: 52 -> 50, of which waited for: 14 -> 18; matrix products, arithmetic and copies ran while one was open for 16% -> 16% of each run, Pallas kernels for 24% -> 25%
where the time goes in v9:
time: 600 us; the launch traced here: 592 us
  waiting for transfers between devices  176 us (29%)
  Pallas kernels  146 us (24%)
  starting transfers between devices  125 us (21%)
  other arithmetic  62.7 us (10%)
  local copies, waits for them, and re-layouts  51.2 us (9%)
  between operations  16.2 us (3%)
  matrix products  14.5 us (2%)
    pallas_call x2, Pallas kernels, run_experts(): pl.pallas_call(functools.partial(expert_kernel, joined=joined), out_shape...  80.2 us
    all_to_all x11, starting transfers between devices, swap(): return lax.all_to_all(parts, axis, split_axis=0, concat_axis=0, tiled=True)  75.3 us
    ppermute x14, waiting for transfers between devices, flip(): return lax.ppermute(block, axis, FLIP)  60.4 us
    ppermute x12, waiting for transfers between devices, by_z(): lax.ppermute(parts[k], 'z', perm)  49.2 us
    ppermute x1, waiting for transfers between devices, body(): w_before = lax.ppermute(both_w, 'z', UP)  29.2 us
    pallas_call x2, Pallas kernels, attend_backward(): pl.pallas_call(attend_back_kernel, out_shape=outs, grid=(1,), in_specs=[p...  27.9 us
    unnamed x173, local copies, waits for them, and re-layouts  24.8 us
    all_to_all x11, waiting for transfers between devices, swap(): return lax.all_to_all(parts, axis, split_axis=0, concat_axis=0, tiled=True)  21.6 us
  transfers between devices with their start and end apart: 50, of which 18 were waited for; matrix products, arithmetic and copies ran while one was open for 16% of the time, Pallas kernels for 25%

profile of v9, /device:TPU:0, one launch (start us, length us, event | category | flops | bytes accessed | tf_op | source)
XLA Modules:
  0.0 592.2 jit_solution(4686362428889024825)
XLA Ops:
  15.9 11.6 %all-to-all-start = ((bf16[128,8,384]{2,1,0:T(8,128)(2,1)}), bf16[128,8,384]{2,1,0:T(8,128)(2,1)}, u32[]{:S(2)}, u32[]{:S(2)}) async-start(bf16[128,8,384]{2,1,0:T(8,128)(2,1)} %bitcast.6), calls=%async_computation | async-start | bytes 1572864 | tf_op jit(solution)/shard_map/all_to_all | solution.py:492
  32.4 14.2 %collective-permute-done = bf16[1,128,1024]{2,1,0:T(8,128)(2,1)S(1)} collective-permute-done((bf16[1,128,1024]{2,1,0:T(8,128)(2,1)S(1)}, bf16[1,128,1024]{2,1,0:T(8,128)(2,1)S(1)}, u32[]{:S(2)}, u32[]{:S(2)}) %collective-permute-start) | collective-permute-done | bytes 262176 | tf_op jit(solution)/shard_map/ppermute | solution.py:496
  52.0 26.9 %collective-permute-done.5 = bf16[1,128,1024]{2,1,0:T(8,128)(2,1)} collective-permute-done((bf16[1,128,1024]{2,1,0:T(8,128)(2,1)S(1)}, bf16[1,128,1024]{2,1,0:T(8,128)(2,1)}, u32[]{:S(2)}, u32[]{:S(2)}) %collective-permute-start.5) | collective-permute-done | bytes 262176 | tf_op jit(solution)/shard_map/ppermute | solution.py:496
  81.9 10.3 %all-to-all-start.1 = ((bf16[64,8,1024]{2,1,0:T(8,128)(2,1)}), bf16[64,8,1024]{2,1,0:T(8,128)(2,1)}, u32[]{:S(2)}, u32[]{:S(2)}) async-start(bf16[64,8,1024]{2,1,0:T(8,128)(2,1)} %broadcast_in_dim.34), calls=%async_computation.1 | async-start | bytes 2097152 | tf_op jit(solution)/shard_map/all_to_all | solution.py:492
  104.5 8.6 %shard_map.246 = (bf16[1024,128]{1,0:T(8,128)(2,1)S(1)}, bf16[1024,1024]{1,0:T(8,128)(2,1)S(1)}, bf16[1024,128]{1,0:T(8,128)(2,1)S(1)}, bf16[1024,128]{1,0:T(8,128)(2,1)S(1)}) custom-call(s32[8]{0:T(128)S(1)} %fusion.44.order_ref, bf16[2,128,1024]{2,1,0:T(8,128)(2,1)S(1)} %pad_maximum_fusion.4.refs_0_, bf16[2,128,1024]{2,1,0:T(8,128)(2,1)S(1)} %copy-done.27, ...), custom_call_target="tpu_custom_call" | custom-call | flops 12000000000 | bytes 8388608 | tf_op jit(solution)/shard_map/pallas_call | solution.py:226
  115.8 11.7 %collective-permute-done.6.refs_1_ = bf16[2,128,1024]{2,1,0:T(8,128)(2,1)} collective-permute-done((bf16[2,128,1024]{2,1,0:T(8,128)(2,1)}, bf16[2,128,1024]{2,1,0:T(8,128)(2,1)}, u32[]{:S(2)}, u32[]{:S(2)}) %collective-permute-start.6) | collective-permute-done | bytes 524320 | tf_op jit(solution)/shard_map/ppermute | solution.py:500
  131.7 9.3 %shard_map.247 = (bf16[1024,128]{1,0:T(8,128)(2,1)S(1)}, bf16[1024,1024]{1,0:T(8,128)(2,1)S(1)}, bf16[1024,128]{1,0:T(8,128)(2,1)S(1)}, bf16[1024,128]{1,0:T(8,128)(2,1)S(1)}) custom-call(s32[8]{0:T(128)S(1)} %fusion.44.order_ref, bf16[2,128,1024]{2,1,0:T(8,128)(2,1)} %pad_maximum_fusion.5.refs_0_, bf16[2,128,1024]{2,1,0:T(8,128)(2,1)} %collective-permute-done.6.refs_1_, ...), custom_call_target="tpu_custom_call" | custom-call | flops 12000000000 | bytes 8388608 | tf_op jit(solution)/shard_map/pallas_call | solution.py:226
  153.1 7.7 %all-to-all-done.2 = bf16[8,256,128]{2,1,0:T(8,128)(2,1)S(1)} async-done(((bf16[8,256,128]{2,1,0:T(8,128)(2,1)}), bf16[8,256,128]{2,1,0:T(8,128)(2,1)S(1)}, u32[]{:S(2)}, u32[]{:S(2)}) %all-to-all-start.2) | async-done | bytes 524320 | tf_op jit(solution)/shard_map/all_to_all | solution.py:492
  164.5 29.2 %collective-permute-done.10.refs_8_ = bf16[2,2,3,128,512]{4,3,2,1,0:T(8,128)(2,1)} collective-permute-done((bf16[2,2,3,128,512]{4,3,2,1,0:T(8,128)(2,1)}, bf16[2,2,3,128,512]{4,3,2,1,0:T(8,128)(2,1)}, u32[]{:S(2)}, u32[]{:S(2)}) %collective-permute-start.10) | collective-permute-done | bytes 1572896 | tf_op jit(solution)/shard_map/ppermute | solution.py:639
  195.3 4.9 all-to-all-start.3
  206.0 15.5 %collective-permute-done.12.refs_6_ = bf16[1,2,3,128,512]{4,3,2,1,0:T(8,128)(2,1)S(1)} collective-permute-done((bf16[1,2,3,128,512]{4,3,2,1,0:T(8,128)(2,1)S(1)}, bf16[1,2,3,128,512]{4,3,2,1,0:T(8,128)(2,1)S(1)}, u32[]{:S(2)}, u32[]{:S(2)}) %collective-permute-start.12) | collective-permute-done | bytes 786464 | tf_op jit(solution)/shard_map/ppermute | solution.py:641
  222.1 6.5 %all-to-all-done.3.refs_0_ = bf16[8,128,1024]{2,1,0:T(8,128)(2,1)} async-done(((bf16[8,128,1024]{2,1,0:T(8,128)(2,1)}), bf16[8,128,1024]{2,1,0:T(8,128)(2,1)}, u32[]{:S(2)}, u32[]{:S(2)}) %all-to-all-start.3) | async-done | bytes 2097184 | tf_op jit(solution)/shard_map/all_to_all | solution.py:492
  232.5 5.0 all-to-all-start.4
  237.5 39.9 %shard_map.248 = (bf16[16,128,1024]{2,1,0:T(8,128)(2,1)}, bf16[8,128,1152]{2,1,0:T(8,128)(2,1)}, bf16[8,128,1152]{2,1,0:T(8,128)(2,1)}, bf16[2,768,1024]{2,1,0:T...) custom-call(s32[18]{0:T(128)} %pad_add_fusion.scalar_ref, ...), custom_call_target="tpu_custom_call" | custom-call | flops 40000000000 | bytes 41943040 | tf_op jit(solution)/shard_map/pallas_call | solution.py:405
  277.8 4.5 collective-permute-done.15
  289.1 7.1 %all-to-all-start.5 = ((bf16[8,128,1152]{2,1,0:T(8,128)(2,1)}), bf16[8,128,1152]{2,1,0:T(8,128)(2,1)}, u32[]{:S(2)}, u32[]{:S(2)}) async-start(bf16[8,128,1152]{2,1,0:T(8,128)(2,1)} %add_convert_fusion.1), calls=%async_computation.6 | async-start | bytes 4718592 | tf_op jit(solution)/shard_map/all_to_all | solution.py:492
  296.4 40.3 %shard_map.249 = (bf16[8,128,1024]{2,1,0:T(8,128)(2,1)}, bf16[8,128,1024]{2,1,0:T(8,128)(2,1)}, bf16[8,128,1152]{2,1,0:T(8,128)(2,1)}, bf16[8,128,1152]{2,1,0:T(...) custom-call(s32[18]{0:T(128)} %pad_add_fusion.scalar_ref, ...), custom_call_target="tpu_custom_call" | custom-call | flops 40000000000 | bytes 41943040 | tf_op jit(solution)/shard_map/pallas_call | solution.py:405
  342.6 6.5 %all-to-all-start.6 = ((bf16[8,128,128]{2,1,0:T(8,128)(2,1)}), bf16[8,128,128]{2,1,0:T(8,128)(2,1)S(1)}, u32[]{:S(2)}, u32[]{:S(2)}) async-start(bf16[8,128,128]{2,1,0:T(8,128)(2,1)} %bitcast.216), calls=%async_computation.7 | async-start | bytes 524288 | tf_op jit(solution)/shard_map/all_to_all | solution.py:492
  352.8 3.8 add_convert_fusion
  357.0 20.1 %shard_map.250 = (bf16[2,2,3,128,512]{4,3,2,1,0:T(8,128)(2,1)S(1)}, bf16[2,2,3,128,512]{4,3,2,1,0:T(8,128)(2,1)S(1)}, bf16[2,2,3,128,512]{4,3,2,1,0:T(8,128)(2,1)S(1)}, bf16[2,2,3,128,512]{4,3,2,1,0:T(8,128)(2,1)}) custom-call(s32[8]{0:T(128)S(1)} %fusion.44.order_ref, bf16[2,768,1024]{2,1,0:T(8,128)(2,1)} %get-tuple-element.146.refs_0_, ...), custom_call_target="tpu_custom_call" | custom-call | flops 14000000000 | bytes 29360128 | tf_op jit(solution)/shard_map/pallas_call | solution.py:449
  378.2 7.8 %all-to-all-start.7 = ((bf16[8,128,1152]{2,1,0:T(8,128)(2,1)}), bf16[8,128,1152]{2,1,0:T(8,128)(2,1)}, u32[]{:S(2)}, u32[]{:S(2)}) async-start(bf16[8,128,1152]{2,1,0:T(8,128)(2,1)} %add_convert_fusion), calls=%async_computation.8 | async-start | bytes 4718592 | tf_op jit(solution)/shard_map/all_to_all | solution.py:492
  391.3 14.3 %shard_map.251 = (bf16[2,128,1024]{2,1,0:T(8,128)(2,1)S(1)}, bf16[2,128,1024]{2,1,0:T(8,128)(2,1)}, bf16[2,128,1024]{2,1,0:T(8,128)(2,1)}, bf16[2,128,1024]{2,1,...) custom-call(s32[8]{0:T(128)S(1)} %fusion.44.order_ref, ...), custom_call_target="tpu_custom_call" | custom-call | flops 24999999488 | bytes 8388608 | tf_op jit(solution)/shard_map/pallas_call | solution.py:249
  414.3 7.1 %all-to-all-done.7 = bf16[8,128,1152]{2,1,0:T(8,128)(2,1)} async-done(((bf16[8,128,1152]{2,1,0:T(8,128)(2,1)}), bf16[8,128,1152]{2,1,0:T(8,128)(2,1)}, u32[]{:S(2)}, u32[]{:S(2)}) %all-to-all-start.7) | async-done | bytes 2359328 | tf_op jit(solution)/shard_map/all_to_all | solution.py:492
  427.2 6.5 %collective-permute-done.22 = bf16[2,128,1024]{2,1,0:T(8,128)(2,1)} collective-permute-done((bf16[2,128,1024]{2,1,0:T(8,128)(2,1)}, bf16[2,128,1024]{2,1,0:T(8,128)(2,1)}, u32[]{:S(2)}, u32[]{:S(2)}) %collective-permute-start.22) | collective-permute-done | bytes 524320 | tf_op jit(solution)/shard_map/ppermute | solution.py:500
  434.3 4.4 all-to-all-start.8
  470.2 13.7 %shard_map.252 = (bf16[2,128,1024]{2,1,0:T(8,128)(2,1)S(1)}, bf16[2,128,1024]{2,1,0:T(8,128)(2,1)S(1)}, bf16[2,128,1024]{2,1,0:T(8,128)(2,1)S(1)}, bf16[2,128,10...) custom-call(s32[8]{0:T(128)S(1)} %fusion.44.order_ref, ...), custom_call_target="tpu_custom_call" | custom-call | flops 24999999488 | bytes 8388608 | tf_op jit(solution)/shard_map/pallas_call | solution.py:249
  491.4 7.4 %all-to-all-start.9 = ((bf16[64,8,1024]{2,1,0:T(8,128)(2,1)}), bf16[64,8,1024]{2,1,0:T(8,128)(2,1)}, u32[]{:S(2)}, u32[]{:S(2)}) async-start(bf16[64,8,1024]{2,1,0:T(8,128)(2,1)} %fusion), calls=%async_computation.10 | async-start | bytes 2097152 | tf_op jit(solution)/shard_map/all_to_all | solution.py:492
  507.9 16.6 %collective-permute-done.25 = bf16[2,128,1024]{2,1,0:T(8,128)(2,1)S(1)} collective-permute-done((bf16[2,128,1024]{2,1,0:T(8,128)(2,1)}, bf16[2,128,1024]{2,1,0:T(8,128)(2,1)S(1)}, u32[]{:S(2)}, u32[]{:S(2)}) %collective-permute-start.25) | collective-permute-done | bytes 524320 | tf_op jit(solution)/shard_map/ppermute | solution.py:500
  525.2 10.7 %collective-permute-done.26 = bf16[2,128,1024]{2,1,0:T(8,128)(2,1)S(1)} collective-permute-done((bf16[2,128,1024]{2,1,0:T(8,128)(2,1)}, bf16[2,128,1024]{2,1,0:T(8,128)(2,1)S(1)}, u32[]{:S(2)}, u32[]{:S(2)}) %collective-permute-start.26) | collective-permute-done | bytes 524320 | tf_op jit(solution)/shard_map/ppermute | solution.py:500
  536.8 6.9 %all-to-all-start.10 = ((bf16[128,8,384]{2,1,0:T(8,128)(2,1)}), bf16[128,8,384]{2,1,0:T(8,128)(2,1)S(1)}, u32[]{:S(2)}, u32[]{:S(2)}) async-start(bf16[128,8,384]{2,1,0:T(8,128)(2,1)} %pad_maximum_fusion.3), calls=%async_computation.11 | async-start | bytes 1572864 | tf_op jit(solution)/shard_map/all_to_all | solution.py:492
  556.3 9.0 %collective-permute-done.35 = bf16[128,1024]{1,0:T(8,128)(2,1)S(1)} collective-permute-done((bf16[128,1024]{1,0:T(8,128)(2,1)S(1)}, bf16[128,1024]{1,0:T(8,128)(2,1)S(1)}, u32[]{:S(2)}, u32[]{:S(2)}) %collective-permute-start.35) | collective-permute-done | bytes 262176 | tf_op jit(solution)/shard_map/ppermute | solution.py:496
  576.1 5.8 collective-permute-done.36
  (381 shorter events, 182.5 us)
Async XLA Ops:
  7.2 230.3 %all-gather.3.cloned.1.call-start = ((), (), s32[]{:S(2)}) async-start(), calls=%async_computation.13 | async-start | bytes 10027008 | tf_op jit(solution)/shard_map/all_gather | solution.py:651
  15.9 64.9 %all-to-all-start = ((bf16[128,8,384]{2,1,0:T(8,128)(2,1)}), bf16[128,8,384]{2,1,0:T(8,128)(2,1)}, u32[]{:S(2)}, u32[]{:S(2)}) async-start(bf16[128,8,384]{2,1,0:T(8,128)(2,1)} %bitcast.6), calls=%async_computation | async-start | bytes 1572864 | tf_op jit(solution)/shard_map/all_to_all | solution.py:492
  29.5 67.5 %collective-permute-start.4 = (bf16[1,2,3,128,512]{4,3,2,1,0:T(8,128)(2,1)}, bf16[1,2,3,128,512]{4,3,2,1,0:T(8,128)(2,1)}, u32[]{:S(2)}, u32[]{:S(2)}) collective-permute-start(bf16[1,2,3,128,512]{4,3,2,1,0:T(8,128)(2,1)} %maximum_bitcast_fusion.1), channel_id=1, source_target_pairs={{0,16},{16,0},{1,17},{17,1},{2,18},{18,2},{3,19},{19,3},{4,20},{20... | collective-permute-start | bytes 2359304 | tf_op jit(solution)/shard_map/ppermute | solution.py:496
  30.6 48.4 %collective-permute-start.5 = (bf16[1,128,1024]{2,1,0:T(8,128)(2,1)S(1)}, bf16[1,128,1024]{2,1,0:T(8,128)(2,1)}, u32[]{:S(2)}, u32[]{:S(2)}) collective-permute-start(bf16[1,128,1024]{2,1,0:T(8,128)(2,1)S(1)} %get-tuple-element.328), channel_id=1, source_target_pairs={{0,16},{16,0},{1,17},{17,1},{2,18},{18,2},{3,19},{19,3},{4,20},{20... | collective-permute-start | bytes 786440 | tf_op jit(solution)/shard_map/ppermute | solution.py:496
  46.6 45.6 %collective-permute-start.1 = (bf16[2,128,1024]{2,1,0:T(8,128)(2,1)S(1)}, bf16[2,128,1024]{2,1,0:T(8,128)(2,1)S(1)}, u32[]{:S(2)}, u32[]{:S(2)}) collective-permute-start(bf16[2,128,1024]{2,1,0:T(8,128)(2,1)S(1)} %pad_maximum_fusion.4.refs_0_), channel_id=1, source_target_pairs={{0,96},{32,0},{64,32},{96,64},{1,97},{33,1},{65,33},{97,65},{2,98}... | collective-permute-start | bytes 1572872 | tf_op jit(solution)/shard_map/ppermute | solution.py:500
  49.6 42.6 %collective-permute-start.2 = (bf16[2,128,1024]{2,1,0:T(8,128)(2,1)S(1)}, bf16[2,128,1024]{2,1,0:T(8,128)(2,1)}, u32[]{:S(2)}, u32[]{:S(2)}) collective-permute-start(bf16[2,128,1024]{2,1,0:T(8,128)(2,1)S(1)} %pad_maximum_fusion.4.refs_0_), channel_id=1, source_target_pairs={{0,64},{32,96},{64,0},{96,32},{1,65},{33,97},{65,1},{97,33},{2,66}... | collective-permute-start | bytes 1572872 | tf_op jit(solution)/shard_map/ppermute | solution.py:500
  50.3 41.9 %collective-permute-start.3 = (bf16[2,128,1024]{2,1,0:T(8,128)(2,1)S(1)}, bf16[2,128,1024]{2,1,0:T(8,128)(2,1)}, u32[]{:S(2)}, u32[]{:S(2)}) collective-permute-start(bf16[2,128,1024]{2,1,0:T(8,128)(2,1)S(1)} %pad_maximum_fusion.4.refs_0_), channel_id=1, source_target_pairs={{0,32},{32,64},{64,96},{96,0},{1,33},{33,65},{65,97},{97,1},{2,34}... | collective-permute-start | bytes 1572872 | tf_op jit(solution)/shard_map/ppermute | solution.py:500
  81.9 62.5 %all-to-all-start.1 = ((bf16[64,8,1024]{2,1,0:T(8,128)(2,1)}), bf16[64,8,1024]{2,1,0:T(8,128)(2,1)}, u32[]{:S(2)}, u32[]{:S(2)}) async-start(bf16[64,8,1024]{2,1,0:T(8,128)(2,1)} %broadcast_in_dim.34), calls=%async_computation.1 | async-start | bytes 2097152 | tf_op jit(solution)/shard_map/all_to_all | solution.py:492
  92.2 35.3 %collective-permute-start.6 = (bf16[2,128,1024]{2,1,0:T(8,128)(2,1)}, bf16[2,128,1024]{2,1,0:T(8,128)(2,1)}, u32[]{:S(2)}, u32[]{:S(2)}) collective-permute-start(bf16[2,128,1024]{2,1,0:T(8,128)(2,1)} %pad_maximum_fusion.5.refs_0_), channel_id=1, source_target_pairs={{0,96},{32,0},{64,32},{96,64},{1,97},{33,1},{65,33},{97,65},{2,98}... | collective-permute-start | bytes 1572872 | tf_op jit(solution)/shard_map/ppermute | solution.py:500
  95.2 32.3 %collective-permute-start.7 = (bf16[2,128,1024]{2,1,0:T(8,128)(2,1)}, bf16[2,128,1024]{2,1,0:T(8,128)(2,1)}, u32[]{:S(2)}, u32[]{:S(2)}) collective-permute-start(bf16[2,128,1024]{2,1,0:T(8,128)(2,1)} %pad_maximum_fusion.5.refs_0_), channel_id=1, source_target_pairs={{0,64},{32,96},{64,0},{96,32},{1,65},{33,97},{65,1},{97,33},{2,66}... | collective-permute-start | bytes 1572872 | tf_op jit(solution)/shard_map/ppermute | solution.py:500
  95.9 34.8 %collective-permute-start.8 = (bf16[2,128,1024]{2,1,0:T(8,128)(2,1)}, bf16[2,128,1024]{2,1,0:T(8,128)(2,1)}, u32[]{:S(2)}, u32[]{:S(2)}) collective-permute-start(bf16[2,128,1024]{2,1,0:T(8,128)(2,1)} %pad_maximum_fusion.5.refs_0_), channel_id=1, source_target_pairs={{0,32},{32,64},{64,96},{96,0},{1,33},{33,65},{65,97},{97,1},{2,34}... | collective-permute-start | bytes 1572872 | tf_op jit(solution)/shard_map/ppermute | solution.py:500
  149.8 43.8 %collective-permute-start.10 = (bf16[2,2,3,128,512]{4,3,2,1,0:T(8,128)(2,1)}, bf16[2,2,3,128,512]{4,3,2,1,0:T(8,128)(2,1)}, u32[]{:S(2)}, u32[]{:S(2)}) collective-permute-start(bf16[2,2,3,128,512]{4,3,2,1,0:T(8,128)(2,1)} %pad_maximum_fusion.refs_4_), channel_id=1, source_target_pairs={{0,32},{32,64},{64,96},{96,0},{1,33},{33,65},{65,97},{97,1},{2,34}... | collective-permute-start | bytes 4718600 | tf_op jit(solution)/shard_map/ppermute | solution.py:639
  151.8 41.9 %collective-permute-start.11 = (bf16[2,2,3,128,512]{4,3,2,1,0:T(8,128)(2,1)}, bf16[2,2,3,128,512]{4,3,2,1,0:T(8,128)(2,1)}, u32[]{:S(2)}, u32[]{:S(2)}) collective-permute-start(bf16[2,2,3,128,512]{4,3,2,1,0:T(8,128)(2,1)} %pad_maximum_fusion.refs_4_), channel_id=1, source_target_pairs={{0,96},{32,0},{64,32},{96,64},{1,97},{33,1},{65,33},{97,65},{2,98}... | collective-permute-start | bytes 4718600 | tf_op jit(solution)/shard_map/ppermute | solution.py:640
  195.3 33.3 %all-to-all-start.3 = ((bf16[8,128,1024]{2,1,0:T(8,128)(2,1)}), bf16[8,128,1024]{2,1,0:T(8,128)(2,1)}, u32[]{:S(2)}, u32[]{:S(2)}) async-start(bf16[8,128,1024]{2,1,0:T(8,128)(2,1)} %broadcast_in_dim.44), calls=%async_computation.3 | async-start | bytes 4194304 | tf_op jit(solution)/shard_map/all_to_all | solution.py:492
  232.5 45.0 %all-to-all-start.4 = ((bf16[8,128,1024]{2,1,0:T(8,128)(2,1)}), bf16[8,128,1024]{2,1,0:T(8,128)(2,1)}, u32[]{:S(2)}, u32[]{:S(2)}) async-start(bf16[8,128,1024]{2,1,0:T(8,128)(2,1)} %broadcast_in_dim.43), calls=%async_computation.4 | async-start | bytes 4194304 | tf_op jit(solution)/shard_map/all_to_all | solution.py:492
  289.1 47.6 %all-to-all-start.5 = ((bf16[8,128,1152]{2,1,0:T(8,128)(2,1)}), bf16[8,128,1152]{2,1,0:T(8,128)(2,1)}, u32[]{:S(2)}, u32[]{:S(2)}) async-start(bf16[8,128,1152]{2,1,0:T(8,128)(2,1)} %add_convert_fusion.1), calls=%async_computation.6 | async-start | bytes 4718592 | tf_op jit(solution)/shard_map/all_to_all | solution.py:492
  296.1 274.2 %reduce-scatter.2.cloned.1.call-start = ((), (), s32[]{:S(2)}) async-start(), calls=%async_computation.12 | async-start | bytes 4456448 | tf_op jit(solution)/shard_map/reduce_scatter | solution.py:759
  349.2 63.5 %collective-permute-start.18 = (bf16[8,128,1024]{2,1,0:T(8,128)(2,1)}, bf16[8,128,1024]{2,1,0:T(8,128)(2,1)}, u32[]{:S(2)}, u32[]{:S(2)}) collective-permute-start(bf16[8,128,1024]{2,1,0:T(8,128)(2,1)} %get-tuple-element.166), channel_id=1, source_target_pairs={{0,1},{1,0},{2,3},{3,2},{4,5},{5,4},{6,7},{7,6},{8,9},{9,8},{10,11... | collective-permute-start | bytes 6291464 | tf_op jit(solution)/shard_map/ppermute | solution.py:496
  378.2 43.1 %all-to-all-start.7 = ((bf16[8,128,1152]{2,1,0:T(8,128)(2,1)}), bf16[8,128,1152]{2,1,0:T(8,128)(2,1)}, u32[]{:S(2)}, u32[]{:S(2)}) async-start(bf16[8,128,1152]{2,1,0:T(8,128)(2,1)} %add_convert_fusion), calls=%async_computation.8 | async-start | bytes 4718592 | tf_op jit(solution)/shard_map/all_to_all | solution.py:492
  386.2 28.1 %collective-permute-start.19 = (bf16[1,2,3,128,512]{4,3,2,1,0:T(8,128)(2,1)S(1)}, bf16[1,2,3,128,512]{4,3,2,1,0:T(8,128)(2,1)}, u32[]{:S(2)}, u32[]{:S(2)}) collective-permute-start(bf16[1,2,3,128,512]{4,3,2,1,0:T(8,128)(2,1)S(1)} %get-tuple-element.319), channel_id=1, source_target_pairs={{0,32},{32,64},{64,96},{96,0},{1,33},{33,65},{65,97},{97,1},{2,34}... | collective-permute-start | bytes 2359304 | tf_op jit(solution)/shard_map/ppermute | solution.py:774
  434.3 29.3 %all-to-all-start.8 = ((bf16[8,128,128]{2,1,0:T(8,128)(2,1)}), bf16[8,128,128]{2,1,0:T(8,128)(2,1)S(1)}, u32[]{:S(2)}, u32[]{:S(2)}) async-start(bf16[8,128,128]{2,1,0:T(8,128)(2,1)} %bitcast.246), calls=%async_computation.9 | async-start | bytes 524288 | tf_op jit(solution)/shard_map/all_to_all | solution.py:492
  443.0 44.3 %collective-permute-start.24 = (bf16[64,8,1024]{2,1,0:T(8,128)(2,1)}, bf16[64,8,1024]{2,1,0:T(8,128)(2,1)}, u32[]{:S(2)}, u32[]{:S(2)}) collective-permute-start(bf16[64,8,1024]{2,1,0:T(8,128)(2,1)} %dynamic-slice_bitcast_fusion), channel_id=1, source_target_pairs={{0,1},{1,0},{2,3},{3,2},{4,5},{5,4},{6,7},{7,6},{8,9},{9,8},{10,11... | collective-permute-start | bytes 3145736 | tf_op jit(solution)/shard_map/ppermute | solution.py:496
  446.0 89.9 %collective-permute-start.28 = (bf16[2,2,3,128,512]{4,3,2,1,0:T(8,128)(2,1)}, bf16[2,2,3,128,512]{4,3,2,1,0:T(8,128)(2,1)}, u32[]{:S(2)}, u32[]{:S(2)}) collective-permute-start(bf16[2,2,3,128,512]{4,3,2,1,0:T(8,128)(2,1)} %pad_maximum_fusion.1), channel_id=1, source_target_pairs={{0,32},{32,64},{64,96},{96,0},{1,33},{33,65},{65,97},{97,1},{2,34}... | collective-permute-start | bytes 4718600 | tf_op jit(solution)/shard_map/ppermute | solution.py:789
  450.7 86.1 %collective-permute-start.29 = (bf16[2,2,3,128,512]{4,3,2,1,0:T(8,128)(2,1)}, bf16[2,2,3,128,512]{4,3,2,1,0:T(8,128)(2,1)}, u32[]{:S(2)}, u32[]{:S(2)}) collective-permute-start(bf16[2,2,3,128,512]{4,3,2,1,0:T(8,128)(2,1)} %pad_maximum_fusion.2), channel_id=1, source_target_pairs={{0,96},{32,0},{64,32},{96,64},{1,97},{33,1},{65,33},{97,65},{2,98}... | collective-permute-start | bytes 4718600 | tf_op jit(solution)/shard_map/ppermute | solution.py:790
  456.2 43.2 %collective-permute-start.30 = (bf16[2,128,1024]{2,1,0:T(8,128)(2,1)}, bf16[2,128,1024]{2,1,0:T(8,128)(2,1)}, u32[]{:S(2)}, u32[]{:S(2)}) collective-permute-start(bf16[2,128,1024]{2,1,0:T(8,128)(2,1)} %get-tuple-element.314), channel_id=1, source_target_pairs={{0,2},{2,4},{4,6},{6,0},{1,3},{3,5},{5,7},{7,1},{8,10},{10,12},{12... | collective-permute-start | bytes 1572872 | tf_op jit(solution)/shard_map/ppermute | solution.py:527
  458.0 43.1 %collective-permute-start.31 = (bf16[2,128,1024]{2,1,0:T(8,128)(2,1)}, bf16[2,128,1024]{2,1,0:T(8,128)(2,1)}, u32[]{:S(2)}, u32[]{:S(2)}) collective-permute-start(bf16[2,128,1024]{2,1,0:T(8,128)(2,1)} %get-tuple-element.313), channel_id=1, source_target_pairs={{0,4},{2,6},{4,0},{6,2},{1,5},{3,7},{5,1},{7,3},{8,12},{10,14},{12... | collective-permute-start | bytes 1572872 | tf_op jit(solution)/shard_map/ppermute | solution.py:527
  491.4 45.4 %all-to-all-start.9 = ((bf16[64,8,1024]{2,1,0:T(8,128)(2,1)}), bf16[64,8,1024]{2,1,0:T(8,128)(2,1)}, u32[]{:S(2)}, u32[]{:S(2)}) async-start(bf16[64,8,1024]{2,1,0:T(8,128)(2,1)} %fusion), calls=%async_computation.10 | async-start | bytes 2097152 | tf_op jit(solution)/shard_map/all_to_all | solution.py:492
  501.0 34.8 %collective-permute-start.26 = (bf16[2,128,1024]{2,1,0:T(8,128)(2,1)}, bf16[2,128,1024]{2,1,0:T(8,128)(2,1)S(1)}, u32[]{:S(2)}, u32[]{:S(2)}) collective-permute-start(bf16[2,128,1024]{2,1,0:T(8,128)(2,1)} %copy-done.25), channel_id=1, source_target_pairs={{0,64},{32,96},{64,0},{96,32},{1,65},{33,97},{65,1},{97,33},{2,66}... | collective-permute-start | bytes 1572872 | tf_op jit(solution)/shard_map/ppermute | solution.py:500
  503.9 31.9 %collective-permute-start.27 = (bf16[2,128,1024]{2,1,0:T(8,128)(2,1)S(1)}, bf16[2,128,1024]{2,1,0:T(8,128)(2,1)S(1)}, u32[]{:S(2)}, u32[]{:S(2)}) collective-permute-start(bf16[2,128,1024]{2,1,0:T(8,128)(2,1)S(1)} %copy-done.24), channel_id=1, source_target_pairs={{0,96},{32,0},{64,32},{96,64},{1,97},{33,1},{65,33},{97,65},{2,98}... | collective-permute-start | bytes 1572872 | tf_op jit(solution)/shard_map/ppermute | solution.py:500
  524.5 31.7 %collective-permute-start.34 = (bf16[128,1024]{1,0:T(8,128)(2,1)}, bf16[128,1024]{1,0:T(8,128)(2,1)}, u32[]{:S(2)}, u32[]{:S(2)}) collective-permute-start(bf16[128,1024]{1,0:T(8,128)(2,1)} %fusion.25), channel_id=1, source_target_pairs={{0,16},{16,0},{1,17},{17,1},{2,18},{18,2},{3,19},{19,3},{4,20},{20... | collective-permute-start | bytes 786440 | tf_op jit(solution)/shard_map/ppermute | solution.py:496
  536.8 33.1 %all-to-all-start.10 = ((bf16[128,8,384]{2,1,0:T(8,128)(2,1)}), bf16[128,8,384]{2,1,0:T(8,128)(2,1)S(1)}, u32[]{:S(2)}, u32[]{:S(2)}) async-start(bf16[128,8,384]{2,1,0:T(8,128)(2,1)} %pad_maximum_fusion.3), calls=%async_computation.11 | async-start | bytes 1572864 | tf_op jit(solution)/shard_map/all_to_all | solution.py:492
  552.8 29.0 %collective-permute-start.36 = (bf16[2,3,128,512]{3,2,1,0:T(8,128)(2,1)}, bf16[2,3,128,512]{3,2,1,0:T(8,128)(2,1)}, u32[]{:S(2)}, u32[]{:S(2)}) collective-permute-start(bf16[2,3,128,512]{3,2,1,0:T(8,128)(2,1)} %fusion.6), channel_id=1, source_target_pairs={{0,16},{16,0},{1,17},{17,1},{2,18},{18,2},{3,19},{19,3},{4,20},{20... | collective-permute-start | bytes 2359304 | tf_op jit(solution)/shard_map/ppermute | solution.py:496
  (103 other events, 1628.9 us)
Sparse Core Ops, SparseCore 0:
  10.4 105.2 all-gather.2
  337.0 110.7 reduce-scatter.1

commit v10 on v9

--- a/solution.py
+++ b/solution.py
@@ -17,6 +17,7 @@
 WINDOW = 1024
 EPS = 1e-06
 THETA = 10000.0
+COST = pl.CostEstimate(flops=10**7, bytes_accessed=10**5, transcendentals=0)
 
 
 def dot(a, b, ca, cb):
@@ -200,10 +201,12 @@
     total = jnp.zeros(grad_gain_ref.shape, F32)
     outs = (d_hidden_0_ref, d_hidden_1_ref, d_hidden_2_ref, d_hidden_3_ref)
     tok = length // 8
-    for r in range(8):
-        rows = pl.ds(pl.multiple_of(order_ref[r] * tok, tok), tok)
+    for step in range(4):
+        rows = pl.ds(pl.multiple_of(order_ref[2 * step] // 2 * (2 * tok), 2 * tok), 2 * tok)
         d_hidden = dot(d_raw_ref[rows], w_ref[...], 1, 1)
-        outs[r // 2][r % 2] = d_hidden.astype(BF)
+        own = order_ref[0] % 2
+        outs[step][own] = d_hidden[:tok].astype(BF)
+        outs[step][1 - own] = d_hidden[tok:].astype(BF)
         total = total + jnp.sum(d_hidden * hidden_ref[rows].astype(F32), axis=0, keepdims=True)
     grad_gain_ref[...] = total / gain_ref[...]
 
@@ -231,7 +234,7 @@
         out_specs=[whole(o) for o in outs],
         scratch_shapes=[pltpu.VMEM((length, 128), BF), pltpu.VMEM((length, 128), BF)],
         compiler_params=pltpu.CompilerParams(vmem_limit_bytes=40 * 1024 * 1024),
-        cost_estimate=pl.CostEstimate(flops=12 * 10**9, bytes_accessed=8 << 20, transcendentals=0),
+        cost_estimate=COST,
     )(order, *args)
 
 
@@ -256,7 +259,7 @@
         + [pltpu.VMEM((length, 128), F32)] * 3
         + [pltpu.VMEM((length, 256), BF)],
         compiler_params=pltpu.CompilerParams(vmem_limit_bytes=40 * 1024 * 1024),
-        cost_estimate=pl.CostEstimate(flops=25 * 10**9, bytes_accessed=8 << 20, transcendentals=0),
+        cost_estimate=COST,
     )(order, *args)
 
 
@@ -265,10 +268,12 @@
     return high, (v - high.astype(F32)).astype(BF)
 
 
-def expert_kernel(scalar_ref, *refs, joined):
+def expert_kernel(scalar_ref, *refs, again):
     x_own_ref, x_other_ref, g_ref, router_ref = refs[:4]
-    pieces, refs = refs[4:9], refs[9:]
-    outs, refs = (refs[:1], refs[1:]) if joined else (refs[:2], refs[2:])
+    pieces, refs = (refs[4:9], refs[9:14]), refs[14:]
+    if again:
+        refs = refs[1:]
+    out_ref, refs = refs[0], refs[1:]
     back_own_ref, back_other_ref, xe_ref, de_ref, act_ref, da_ref, db_ref = refs[:7]
     pick_ref, weight_ref, dgate_ref, eo_ref, dr_ref, w_ref = refs[7:]
     half, tok, width = x_own_ref.shape
@@ -276,10 +281,11 @@
     core = scalar_ref[1]
     depth = w_ref.shape[2] // 8
 
-    pieces = [(ref, i) for ref in pieces for i in range(ref.shape[0])]
-    for r, (ref, i) in enumerate(pieces):
-        rows = pl.ds(pl.multiple_of(scalar_ref[2 + r] * depth, depth), depth)
-        w_ref[:, :, rows] = ref[i]
+    for e in range(2):
+        blocks = [(ref, i) for ref in pieces[e] for i in range(ref.shape[0])]
+        for r, (ref, i) in enumerate(blocks):
+            rows = pl.ds(pl.multiple_of(scalar_ref[2 + r] * depth, depth), depth)
+            w_ref[e, :, rows] = ref[i]
     local, slots, hidden = act_ref.shape
     cap = slots // sources
     first = scalar_ref[0]
@@ -367,10 +373,7 @@
         spread = jnp.where(own_lane, high.astype(F32), 0.0) + jnp.where(
             slot_lane == first + row_expert + 64, low.astype(F32), 0.0
         )
-        if joined:
-            outs[0][2 * i + column] = dot(pick, eo, 1, 0).astype(BF)
-        else:
-            outs[offset // half][scalar_ref[10 + i]] = dot(pick, eo, 1, 0).astype(BF)
+        out_ref[2 * i + column, 0] = dot(pick, eo, 1, 0).astype(BF)
         back_ref[i, :, :width] = dot(pick, dr, 1, 0).astype(BF)
         back_ref[i, :, width:] = dot(pick, spread.astype(BF), 1, 0).astype(BF)
         return carry
@@ -381,15 +384,15 @@
         )
 
 
-def run_experts(scalars, x_own, x_other, g_all, micro, router, pieces, cap, joined):
+def run_experts(scalars, x_own, x_other, g_all, micro, router, pieces, cap, moe=None):
     half, tok, width = x_own.shape
     sources = 2 * half
-    _, local, _, _, hidden = pieces[0].shape
+    local, hidden = len(pieces), pieces[0][0].shape[3]
     slots = sources * cap
     wide = g_all.shape[2]
     shape = jax.ShapeDtypeStruct
-    outs = [shape((sources, tok, width), BF)] if joined else [shape((half, tok, width), BF)] * 2
-    outs += [
+    outs = [
+        shape((sources, 2, tok, width), BF),
         shape((half, tok, wide), BF),
         shape((half, tok, wide), BF),
         shape((local, slots, width), BF),
@@ -401,14 +404,20 @@
     g_spec = pl.BlockSpec(
         (sources, tok, wide), lambda i: (0, micro, 0), pipeline_mode=pl.Buffered(1)
     )
-    args = [router, *pieces]
+    args = [router, *pieces[0], *pieces[1]]
+    held = [] if moe is None else [moe]
+    moe_spec = pl.BlockSpec(
+        (sources, 1, tok, width), lambda i: (0, micro, 0, 0), pipeline_mode=pl.Buffered(1)
+    )
     return pl.pallas_call(
-        functools.partial(expert_kernel, joined=joined),
+        functools.partial(expert_kernel, again=moe is not None),
         out_shape=outs,
         grid=(1,),
         in_specs=[pl.BlockSpec(memory_space=pltpu.SMEM), whole(x_own), whole(x_other), g_spec]
-        + [whole(a) for a in args],
-        out_specs=[whole(o) for o in outs],
+        + [whole(a) for a in args]
+        + [pl.BlockSpec(memory_space=pl.ANY)] * len(held),
+        out_specs=[moe_spec] + [whole(o) for o in outs[1:]],
+        input_output_aliases={4 + len(args): 0} if held else {},
         scratch_shapes=[
             pltpu.VMEM((sources, tok, local * cap), BF),
             pltpu.VMEM((local, slots, 1), F32),
@@ -418,8 +427,8 @@
             pltpu.VMEM((local, 3, width, hidden), BF),
         ],
         compiler_params=pltpu.CompilerParams(vmem_limit_bytes=60 * 1024 * 1024),
-        cost_estimate=pl.CostEstimate(flops=40 * 10**9, bytes_accessed=40 << 20, transcendentals=0),
-    )(scalars, x_own, x_other, g_all, *args)
+        cost_estimate=COST,
+    )(scalars, x_own, x_other, g_all, *args, *held)
 
 
 def expert_grad_kernel(order_ref, *refs):
@@ -427,38 +436,35 @@
     left = (kept[0:2], kept[0:2], kept[2:4])
     right = (kept[6:8], kept[8:10], kept[4:6])
     step = pl.program_id(0)
-    depth = outs[0].shape[3]
+    depth = outs[0].shape[2]
     for kind in range(3):
 
-        @pl.when(step % 3 == kind)
+        @pl.when(step == kind)
         def _(kind=kind):
             total = dot(left[kind][0][0], right[kind][0][0], 0, 0)
             total_ref[...] = total + dot(left[kind][1][0], right[kind][1][0], 0, 0)
 
     for r in range(8):
         rows = pl.ds(pl.multiple_of(order_ref[r] * depth, depth), depth)
-        outs[r // 2][r % 2, 0, 0] = total_ref[rows].astype(BF)
-
-
-def expert_grads(order, kept):
-    local, slots, width = kept[0][0].shape
+        outs[r // 2][r % 2, 0] = total_ref[rows].astype(BF)
+
+
+def expert_grads(order, kept, expert):
+    _, slots, width = kept[0][0].shape
     hidden = kept[0][2].shape[2]
     args = [kept[m][i] for i in range(5) for m in range(2)]
     depth = width // 8
     shape = jax.ShapeDtypeStruct
     return pl.pallas_call(
         expert_grad_kernel,
-        out_shape=[shape((2, local, 3, depth, hidden), BF)] * 4,
-        grid=(3 * local,),
+        out_shape=[shape((2, 3, depth, hidden), BF)] * 4,
+        grid=(3,),
         in_specs=[pl.BlockSpec(memory_space=pltpu.SMEM)]
-        + [pl.BlockSpec((1,) + a.shape[1:], lambda i: (i // 3, 0, 0)) for a in args],
-        out_specs=[
-            pl.BlockSpec((2, 1, 1, depth, hidden), lambda i: (0, i // 3, i % 3, 0, 0))
-        ]
-        * 4,
+        + [pl.BlockSpec((1,) + a.shape[1:], lambda i: (expert, 0, 0)) for a in args],
+        out_specs=[pl.BlockSpec((2, 1, depth, hidden), lambda i: (0, i, 0, 0))] * 4,
         scratch_shapes=[pltpu.VMEM((width, hidden), F32)],
         compiler_params=pltpu.CompilerParams(vmem_limit_bytes=48 * 1024 * 1024),
-        cost_estimate=pl.CostEstimate(flops=14 * 10**9, bytes_accessed=28 << 20, transcendentals=0),
+        cost_estimate=COST,
     )(order, *args)
 
 
@@ -523,14 +529,21 @@
     return (a.astype(F32) + b.astype(F32)).astype(BF)
 
 
-def by_x(parts):
-    return [lax.ppermute(parts[k], "x", perm) for k, perm in ((1, UP), (2, TWO), (3, DOWN))]
-
-
 def add_part(parts, i, more):
     pieces = [parts[:1], parts[1:]]
     pieces[i] = add(pieces[i], more)
     return jnp.concatenate(pieces, axis=0)
+
+
+def relay(far):
+    return [lax.ppermute(far[:1], "z", UP), lax.ppermute(far[1:], "z", DOWN)]
+
+
+def ring_sums(parts, far):
+    return [
+        lax.ppermute(add_part(parts[1], 0, far[0]), "z", UP),
+        lax.ppermute(add_part(parts[3], 1, far[1]), "z", DOWN),
+    ]
 
 
 def pair_sums(parts, moved):
@@ -614,12 +627,13 @@
     both_0, both_1 = (
         jnp.concatenate([tokens[m], flip(tokens[m], "yl")], axis=0) for m in range(micro)
     )
-    both_w = jnp.stack([w_gate, w_up, w_down], axis=1)[None]
+    both_w = jnp.stack([w_gate, w_up, w_down], axis=1)
     head_all = exchange(pieces.reshape((n_all,) + pieces.shape[2:]), ALL).reshape(width, -1)
-    both_w = jnp.concatenate([both_w, flip(both_w, "yl")], axis=0)
+    other_w = flip(both_w, "yl")
+    both_w = [jnp.stack([both_w[e], other_w[e]]) for e in range(local)]
     seq_rows = [along_z(both_0)]
     seq_rows.append(along_z(after_all(both_1, *seq_rows[0][1:])))
-    head_all = after_all(head_all, *seq_rows[0][1:], both_w)
+    head_all = after_all(head_all, *seq_rows[1][1:], *both_w)
     w_heads = head_all[:, :span]
     small_all = head_all[:, span:]
     router = small_all[:, :experts]
@@ -635,10 +649,12 @@
 
     out_own = exchange.copies(w_out, CTX + GROUP, n_all // 2)
 
-    both_w = after_all(both_w, *seq_rows[1][1:])
-    w_before = lax.ppermute(both_w, "z", UP)
-    w_after = lax.ppermute(both_w, "z", DOWN)
-    w_far = [lax.ppermute(w_before[:1], "z", UP), lax.ppermute(w_after[1:], "z", DOWN)]
+    moved_w = []
+    last = seq_rows[1][1:]
+    for e in range(local):
+        block = after_all(both_w[e], *last)
+        last = [lax.ppermute(block, "z", UP), lax.ppermute(block, "z", DOWN)]
+        moved_w.append(last)
 
     expert_ids = jnp.arange(experts, dtype=jnp.int32)
     cot = cotangent.reshape(all_tok, width)
@@ -648,15 +664,15 @@
     counts = ein("ut,mte->mue", lower, chosen.reshape(micro, tok, experts).astype(BF))
     held = jnp.where(chosen, counts.reshape(all_tok, experts) - 1.0, -1.0)
     held = jnp.pad(held, ((0, 0), (0, 128 - experts)), constant_values=-1.0).astype(BF)
-    g_all = lax.all_gather(jnp.concatenate([cot, held], axis=1), FSDP, axis=0)
+    pack = after_all(jnp.concatenate([cot, held], axis=1), both_0, both_1)
+    g_all = lax.all_gather(pack, FSDP, axis=0)
 
     cosine, sine = rope_tables(jnp.arange(length, dtype=jnp.int32))
     cosine = jnp.tile(cosine, (1, 4))
     sine = jnp.tile(jnp.concatenate([-sine, sine], axis=1), (1, 2))
     rel = jnp.arange(n_ctx, dtype=jnp.int32)
     order = ((z + rel // 2) % 4) * 2 + (yl + rel % 2) % 2
-    g_rel = ((rel % 4 - x) % 4) * 2 + (rel // 4 - yh) % 2
-    scalars = jnp.concatenate([jnp.stack([shard * local, core]), order, g_rel]).astype(jnp.int32)
+    scalars = jnp.concatenate([jnp.stack([shard * local, core]), order]).astype(jnp.int32)
 
     def to_owner(v):
         return exchange(v.reshape(n_ctx, tok, -1), CTX)
@@ -669,6 +685,7 @@
     mixed_1, *saved_1 = attend_forward(order, seq_rows[1], *attention_args(1))
     saved = [saved_0, saved_1]
     out_own, mixed_0, mixed_1 = lax.optimization_barrier((out_own, mixed_0, mixed_1))
+    mixed_1 = after_all(mixed_1, *moved_w[0], *moved_w[1])
     out_other = flip(out_own, "core")
     mixed = jnp.stack([mixed_0, mixed_1]).reshape(micro, n_ctx, tok, heads).transpose(1, 0, 2, 3)
     mixed = exchange(mixed.reshape(n_ctx, all_tok, heads), CTX)
@@ -681,18 +698,21 @@
     middle = tokens.reshape(all_tok, width).astype(F32) + mm(mixed, out_full)
     inv_two = lax.rsqrt(jnp.mean(middle * middle, axis=-1, keepdims=True) + EPS)
     hidden_two = (middle * inv_two * gain_mlp).astype(BF)
-    x_0 = after_all(hidden_two[:tok], w_before, w_after)
+    x_0 = hidden_two[:tok]
+    weights = []
+    for e, (w_before, w_after) in enumerate(moved_w):
+        w_far = [lax.ppermute(w_before[:1], "z", UP), lax.ppermute(w_after[1:], "z", DOWN)]
+        weights.append([both_w[e], w_after, *w_far, w_before])
     x_0 = exchange.copies(x_0, GROUP, n_ctx)
-    x_0, *w_far = lax.optimization_barrier((x_0, *w_far))
+    x_0, weights = lax.optimization_barrier((x_0, weights))
     x_1 = exchange.copies(hidden_two[tok:], GROUP, n_ctx)
-    weights = [both_w, w_after, *w_far, w_before]
     logits = jnp.where(chosen, mm(hidden_two, router), -1e30)
     gates_all = jnp.where(chosen, jax.nn.softmax(logits, axis=-1), 0.0)
 
     def own_rows(v, m):
         return v[m * tok : (m + 1) * tok]
 
-    def experts_of(m, x_own):
+    def experts_of(m, x_own, *moe):
         return run_experts(
             scalars,
             x_own,
@@ -702,7 +722,7 @@
             router_pad,
             weights,
             cap,
-            m == 0,
+            *moe,
         )
 
     def back_sum(own, other):
@@ -751,66 +771,55 @@
             - start * (inverse**3 * jnp.mean(u * start, axis=-1, keepdims=True))
         )
 
-    moe_0, back_own, back_other, *kept_0 = experts_of(0, x_0)
-    x_1, back_own, back_other, moe_0 = lax.optimization_barrier(
-        (x_1, back_own, back_other, moe_0)
-    )
+    moe, back_own, back_other, *kept_0 = experts_of(0, x_0)
+    x_1, back_own, back_other = lax.optimization_barrier((x_1, back_own, back_other))
     back_0 = back_sum(back_own, back_other)
-    moe_0 = lax.psum_scatter(moe_0, FSDP, scatter_dimension=0, tiled=True)[0]
     x_1 = after_all(x_1, back_0)
     back_0 = exchange(back_0, GROUP)
-    moe_own, moe_other, back_own, back_other, *kept_1 = experts_of(1, x_1)
-    back_0, back_own, back_other, moe_own, moe_other = lax.optimization_barrier(
-        (back_0, back_own, back_other, moe_own, moe_other)
-    )
+    moe, back_own, back_other, *kept_1 = experts_of(1, x_1, moe)
+    back_0, back_own, back_other, moe = lax.optimization_barrier(
+        (back_0, back_own, back_other, moe)
+    )
+    moe = lax.psum_scatter(moe, FSDP, scatter_dimension=0, tiled=True)[0]
     back_1 = back_sum(back_own, back_other)
     d_middle_0, d_mixed_0, grads_0 = middle_back(0, sum_parts(back_0))
     d_mixed_0 = exchange(d_mixed_0, CTX)
     d_mixed_0, back_1 = lax.optimization_barrier((d_mixed_0, back_1))
     back_1 = exchange(back_1, GROUP)
     kept_1[0] = after_all(kept_1[0], d_mixed_0)
-    weight_parts = expert_grads(order, (kept_0, kept_1))
-    weight_far = [
-        lax.ppermute(weight_parts[2][:1], "z", UP),
-        lax.ppermute(weight_parts[2][1:], "z", DOWN),
-    ]
-    d_hidden_0, head_grads_0 = attention_back(0, after_all(d_mixed_0, weight_parts[0]))
+    parts = [expert_grads(order, (kept_0, kept_1), 0)]
+    far = [relay(parts[0][2])]
+    d_hidden_0, head_grads_0 = attention_back(0, after_all(d_mixed_0, parts[0][0]))
     hidden_moved_0 = by_z(d_hidden_0)
-    moe_other = flip(moe_other, "core")
-    back_1, d_hidden_0[0], moe_other, *weight_far = lax.optimization_barrier(
-        (back_1, d_hidden_0[0], moe_other, *weight_far)
-    )
+    back_1, d_hidden_0[0], far[0] = lax.optimization_barrier((back_1, d_hidden_0[0], far[0]))
     d_middle_1, d_mixed_1, grads_1 = middle_back(1, sum_parts(back_1))
-    weight_after = add_part(weight_parts[1], 0, weight_far[0])
-    weight_before = add_part(weight_parts[3], 1, weight_far[1])
-    moe_1 = [add(moe_own[2 * k : 2 * k + 2], moe_other[2 * k : 2 * k + 2]) for k in range(4)]
-    d_mixed_1, hidden_moved_0 = lax.optimization_barrier((d_mixed_1, hidden_moved_0))
-    weight_moved = [
-        lax.ppermute(weight_after, "z", UP),
-        lax.ppermute(weight_before, "z", DOWN),
-    ]
     d_mixed_1 = exchange(d_mixed_1, CTX)
-    moe_moved = by_x(moe_1)
+    kept_1[0] = after_all(kept_1[0], back_1)
+    parts.append(expert_grads(order, (kept_0, kept_1), 1))
+    moved = [ring_sums(parts[0], far[0])]
     grad_out, grad_router, grad_mlp = jax.tree.map(jnp.add, grads_0, grads_1)
     grad_out = grad_out.astype(BF).reshape(n_all // 2, 2, rows, width)
     grad_own = lax.dynamic_index_in_dim(grad_out, core, axis=1, keepdims=False)
     grad_other = lax.dynamic_index_in_dim(grad_out, 1 - core, axis=1, keepdims=False)
     grad_out = back_sum(grad_own, grad_other)
+    d_mixed_1, parts[1], hidden_moved_0, grad_out = lax.optimization_barrier(
+        (d_mixed_1, parts[1], hidden_moved_0, grad_out)
+    )
+    far.append(relay(parts[1][2]))
+    grad_out = exchange(grad_out, CTX + GROUP)
     d_hidden_1, head_grads_1 = attention_back(1, d_mixed_1)
-    grad_out = exchange(grad_out, CTX + GROUP)
+    d_hidden_1, grad_out, far[1], moved[0] = lax.optimization_barrier(
+        (d_hidden_1, grad_out, far[1], moved[0])
+    )
     hidden_moved_1 = by_z(d_hidden_1)
+    moved.append(ring_sums(parts[1], after_all(far[1], hidden_moved_1[0])))
     hidden_sums = pair_sums(d_hidden_0, hidden_moved_0)
     d_hidden_0 = hidden_sums[0] + flip(hidden_sums[1].astype(BF), "yl").astype(F32)
-    grad_out, hidden_moved_1, weight_moved, moe_moved = lax.optimization_barrier(
-        (grad_out, hidden_moved_1, weight_moved, moe_moved)
-    )
     exchange.last = grad_out
-    weight_sums = pair_sums(weight_parts, weight_moved)
-    weight_yl = flip(weight_sums[1].astype(BF), "yl")
+    weight_sums = [pair_sums(p, q) for p, q in zip(parts, moved)]
+    weight_yl = [flip(sums[1].astype(BF), "yl") for sums in weight_sums]
     hidden_sums = pair_sums(d_hidden_1, hidden_moved_1)
     hidden_yl = flip(hidden_sums[1].astype(BF), "yl")
-    moe_sums = pair_sums(moe_1, moe_moved)
-    moe_yh = flip(moe_sums[1].astype(BF), "yh")
     grad_heads, grad_attn, grad_qk = jax.tree.map(jnp.add, head_grads_0, head_grads_1)
 
     grad_qk = jnp.pad(grad_qk[:, None], ((0, 0), (0, rows - 1))).reshape(-1)
@@ -824,21 +833,17 @@
     own_heads = own_heads.transpose(1, 0, 2)
     own_small = jnp.sum(grad_pack[:, :, span:], axis=0)
     own_out = sum_parts(grad_out)
-    moe_0 = after_all(moe_0, grad_pack)
+    moe = after_all(moe, grad_pack)
     d_hidden_1 = hidden_sums[0] + hidden_yl.astype(F32)
-    expert_own = weight_sums[0] + weight_yl.astype(F32)
-    moe_1 = moe_sums[0] + moe_yh.astype(F32)
-    outs = [
-        (own_rows(middle, 0) + moe_0.astype(F32)).astype(BF),
-        (own_rows(middle, 1) + moe_1).astype(BF),
-    ]
+    expert_own = [sums[0] + other.astype(F32) for sums, other in zip(weight_sums, weight_yl)]
+    out = (middle.reshape(moe.shape) + moe.astype(F32)).astype(BF)
     d_inputs = [
         input_grad(0, d_hidden_0, d_middle_0),
         input_grad(1, d_hidden_1, d_middle_1),
     ]
 
     return (
-        jnp.stack(outs)[:, None],
+        out[:, None],
         jnp.stack(d_inputs)[:, None],
         own_heads[:, :, :heads].reshape(rows, -1),
         own_heads[:, :, heads : heads + DH].reshape(rows, -1),
@@ -848,9 +853,9 @@
         own_small[:, experts],
         own_small[:, experts + 1],
         own_small[:1, experts + 2],
-        expert_own[:, 0],
-        expert_own[:, 1],
-        expert_own[:, 2],
+        jnp.stack([part[0] for part in expert_own]),
+        jnp.stack([part[1] for part in expert_own]),
+        jnp.stack([part[2] for part in expert_own]),
     )
 
 

time: 600 us -> 559 us (0.932)
  waiting for transfers between devices: 176 us -> 129 us
  other arithmetic: 62.7 us -> 68.8 us
    ppermute x14 -> x13, waiting for transfers between devices: 60.4 us -> 19.3 us  [flip(): return lax.ppermute(block, axis, FLIP)]
    ppermute x9 -> x12, waiting for transfers between devices: 29.2 us -> 14.8 us  [the longest x4 12.4 us: body(): last = [lax.ppermute(block, 'z', UP), lax.ppermute(block, 'z', DOWN)]]
    ppermute x12, waiting for transfers between devices: 49.2 us -> 61.2 us  [by_z(): lax.ppermute(parts[k], 'z', perm)]
    unnamed x173 -> x187, local copies, waits for them, and re-layouts: 24.8 us -> 15.9 us
    slice x2 -> x7, local copies, waits for them, and re-layouts: 0.14 us -> 7.38 us  [the longest x2 4.1 us: body(): both_w = [jnp.stack([both_w[e], other_w[e]]) for e in range(local)]]
    ppermute x1 -> x2, waiting for transfers between devices: 15.5 us -> 9.91 us  [body(): lax.ppermute(w_before[:1], 'z', UP)]
    ppermute x9 -> x12, starting transfers between devices: 16.8 us -> 18.8 us  [the longest x4 6.95 us: relay(): return [lax.ppermute(far[:1], 'z', UP), lax.ppermute(far[1:], 'z', DOWN)]]
    pallas_call x3 -> x4, Pallas kernels: 100 us -> 102 us  [the longest x2 80.4 us: run_experts(): pl.pallas_call(functools.partial(expert_kernel, again=moe is not None), o...]
  transfers between devices with their start and end apart: 50 -> 54, of which waited for: 18 -> 21; matrix products, arithmetic and copies ran while one was open for 16% -> 21% of each run, Pallas kernels for 25% -> 26%
where the time goes in v10:
time: 559 us; the launch traced here: 550 us
  Pallas kernels  143 us (26%)
  waiting for transfers between devices  129 us (23%)
  starting transfers between devices  127 us (23%)
  other arithmetic  68.8 us (12%)
  local copies, waits for them, and re-layouts  52 us (9%)
  between operations  16.5 us (3%)
  matrix products  14.3 us (3%)
    pallas_call x2, Pallas kernels, run_experts(): pl.pallas_call(functools.partial(expert_kernel, again=moe is not None), o...  80.4 us
    all_to_all x11, starting transfers between devices, swap(): return lax.all_to_all(parts, axis, split_axis=0, concat_axis=0, tiled=True)  77.9 us
    ppermute x12, waiting for transfers between devices, by_z(): lax.ppermute(parts[k], 'z', perm)  61.2 us
    pallas_call x2, Pallas kernels, attend_backward(): pl.pallas_call(attend_back_kernel, out_shape=outs, grid=(1,), in_specs=[p...  24.2 us
    all_to_all x11, waiting for transfers between devices, swap(): return lax.all_to_all(parts, axis, split_axis=0, concat_axis=0, tiled=True)  21.9 us
    pallas_call x2, Pallas kernels, expert_grads(): pl.pallas_call(expert_grad_kernel, out_shape=[shape((2, 3, depth, hidden)...  21.4 us
    ppermute x13, waiting for transfers between devices, flip(): return lax.ppermute(block, axis, FLIP)  19.3 us
    pallas_call x2, Pallas kernels, attend_forward(): pl.pallas_call(attend_kernel, out_shape=outs, grid=(1,), in_specs=[pl.Blo...  16.7 us
  transfers between devices with their start and end apart: 54, of which 21 were waited for; matrix products, arithmetic and copies ran while one was open for 21% of the time, Pallas kernels for 26%

profile of v10, /device:TPU:0, one launch (start us, length us, event | category | flops | bytes accessed | tf_op | source)
XLA Modules:
  0.0 549.8 jit_solution(16712274708600424038)
XLA Ops:
  17.7 4.3 collective-permute-done.4
  27.1 11.2 %all-to-all-start = ((bf16[128,8,384]{2,1,0:T(8,128)(2,1)}), bf16[128,8,384]{2,1,0:T(8,128)(2,1)}, u32[]{:S(2)}, u32[]{:S(2)}) async-start(bf16[128,8,384]{2,1,0:T(8,128)(2,1)} %bitcast.6), calls=%async_computation | async-start | bytes 1572864 | tf_op jit(solution)/shard_map/all_to_all | solution.py:498
  46.0 25.3 %collective-permute-done.1.refs_1_ = bf16[2,128,1024]{2,1,0:T(8,128)(2,1)S(1)} collective-permute-done((bf16[2,128,1024]{2,1,0:T(8,128)(2,1)S(1)}, bf16[2,128,1024]{2,1,0:T(8,128)(2,1)S(1)}, u32[]{:S(2)}, u32[]{:S(2)}) %collective-permute-start.1) | collective-permute-done | bytes 524320 | tf_op jit(solution)/shard_map/ppermute | solution.py:506
  78.7 10.1 %all-to-all-start.1 = ((bf16[64,8,1024]{2,1,0:T(8,128)(2,1)}), bf16[64,8,1024]{2,1,0:T(8,128)(2,1)}, u32[]{:S(2)}, u32[]{:S(2)}) async-start(bf16[64,8,1024]{2,1,0:T(8,128)(2,1)} %broadcast_in_dim.32), calls=%async_computation.1 | async-start | bytes 2097152 | tf_op jit(solution)/shard_map/all_to_all | solution.py:498
  92.9 20.2 %collective-permute-done.7.refs_3_ = bf16[2,128,1024]{2,1,0:T(8,128)(2,1)} collective-permute-done((bf16[2,128,1024]{2,1,0:T(8,128)(2,1)S(1)}, bf16[2,128,1024]{2,1,0:T(8,128)(2,1)}, u32[]{:S(2)}, u32[]{:S(2)}) %collective-permute-start.7) | collective-permute-done | bytes 524320 | tf_op jit(solution)/shard_map/ppermute | solution.py:506
  121.6 11.2 %collective-permute-done.10.refs_5_ = bf16[2,3,128,512]{3,2,1,0:T(8,128)(2,1)} collective-permute-done((bf16[2,3,128,512]{3,2,1,0:T(8,128)(2,1)}, bf16[2,3,128,512]{3,2,1,0:T(8,128)(2,1)}, u32[]{:S(2)}, u32[]{:S(2)}) %collective-permute-start.10) | collective-permute-done | bytes 786464 | tf_op jit(solution)/shard_map/ppermute | solution.py:656
  140.9 8.6 %shard_map.247 = (bf16[1024,128]{1,0:T(8,128)(2,1)S(1)}, bf16[1024,1024]{1,0:T(8,128)(2,1)S(1)}, bf16[1024,128]{1,0:T(8,128)(2,1)S(1)}, bf16[1024,128]{1,0:T(8,128)(2,1)S(1)}) custom-call(s32[8]{0:T(128)S(1)} %fusion.41.order_ref, bf16[2,128,1024]{2,1,0:T(8,128)(2,1)S(1)} %copy-done.6, bf16[2,128,1024]{2,1,0:T(8,128)(2,1)S(1)} %copy-done.34, ...), custom_call_target="tpu_custom_call" | custom-call | flops 10000000 | bytes 100000 | tf_op jit(solution)/shard_map/pallas_call | solution.py:229
  152.3 8.1 %shard_map.246 = (bf16[1024,128]{1,0:T(8,128)(2,1)S(1)}, bf16[1024,1024]{1,0:T(8,128)(2,1)S(1)}, bf16[1024,128]{1,0:T(8,128)(2,1)S(1)}, bf16[1024,128]{1,0:T(8,128)(2,1)S(1)}) custom-call(s32[8]{0:T(128)S(1)} %fusion.41.order_ref, bf16[2,128,1024]{2,1,0:T(8,128)(2,1)S(1)} %pad_maximum_fusion.8.refs_0_, bf16[2,128,1024]{2,1,0:T(8,128)(2,1)S(1)} %copy-done.28, ...), custom_call_target="tpu_custom_call" | custom-call | flops 10000000 | bytes 100000 | tf_op jit(solution)/shard_map/pallas_call | solution.py:229
  167.5 4.1 maximum_select_fusion
  171.6 6.9 %all-to-all-done.2 = bf16[8,256,128]{2,1,0:T(8,128)(2,1)S(1)} async-done(((bf16[8,256,128]{2,1,0:T(8,128)(2,1)}), bf16[8,256,128]{2,1,0:T(8,128)(2,1)S(1)}, u32[]{:S(2)}, u32[]{:S(2)}) %all-to-all-start.2) | async-done | bytes 524320 | tf_op jit(solution)/shard_map/all_to_all | solution.py:498
  184.0 5.3 all-to-all-start.3
  204.2 6.3 %collective-permute-done.16.refs_11_ = bf16[1,3,128,512]{3,2,1,0:T(8,128)(2,1)} collective-permute-done((bf16[1,3,128,512]{3,2,1,0:T(8,128)(2,1)S(1)}, bf16[1,3,128,512]{3,2,1,0:T(8,128)(2,1)}, u32[]{:S(2)}, u32[]{:S(2)}) %collective-permute-start.16) | collective-permute-done | bytes 393248 | tf_op jit(solution)/shard_map/ppermute | solution.py:704
  210.8 6.9 %all-to-all-done.3.refs_0_ = bf16[8,128,1024]{2,1,0:T(8,128)(2,1)} async-done(((bf16[8,128,1024]{2,1,0:T(8,128)(2,1)}), bf16[8,128,1024]{2,1,0:T(8,128)(2,1)}, u32[]{:S(2)}, u32[]{:S(2)}) %all-to-all-start.3) | async-done | bytes 2097184 | tf_op jit(solution)/shard_map/all_to_all | solution.py:498
  219.2 5.3 all-to-all-start.4
  226.9 40.3 %shard_map.248 = (bf16[16,2,128,1024]{3,2,1,0:T(8,128)(2,1)}, bf16[8,128,1152]{2,1,0:T(8,128)(2,1)}, bf16[8,128,1152]{2,1,0:T(8,128)(2,1)}, bf16[2,768,1024]{2,1...) custom-call(s32[10]{0:T(128)} %pad_add_fusion.scalar_ref, ...), custom_call_target="tpu_custom_call" | custom-call | flops 10000000 | bytes 100000 | tf_op jit(solution)/shard_map/pallas_call | solution.py:412
  267.5 4.5 collective-permute-done.19
  275.9 7.4 %all-to-all-start.5 = ((bf16[8,128,1152]{2,1,0:T(8,128)(2,1)}), bf16[8,128,1152]{2,1,0:T(8,128)(2,1)}, u32[]{:S(2)}, u32[]{:S(2)}) async-start(bf16[8,128,1152]{2,1,0:T(8,128)(2,1)} %add_convert_fusion.1), calls=%async_computation.5 | async-start | bytes 4718592 | tf_op jit(solution)/shard_map/all_to_all | solution.py:498
  283.4 40.2 %shard_map.249 = (bf16[16,2,128,1024]{3,2,1,0:T(8,128)(2,1)}, bf16[8,128,1152]{2,1,0:T(8,128)(2,1)}, bf16[8,128,1152]{2,1,0:T(8,128)(2,1)}, bf16[2,768,1024]{2,1...) custom-call(s32[10]{0:T(128)} %pad_add_fusion.scalar_ref, ...), custom_call_target="tpu_custom_call", output_to_operand_aliasing={{0}: (15, {})} | custom-call | flops 10000000 | bytes 100000 | tf_op jit(solution)/shard_map/pallas_call | solution.py:412
  331.3 3.9 all-to-all-start.6
  336.0 4.5 add_convert_fusion
  343.1 7.8 %all-to-all-start.7 = ((bf16[8,128,1152]{2,1,0:T(8,128)(2,1)}), bf16[8,128,1152]{2,1,0:T(8,128)(2,1)}, u32[]{:S(2)}, u32[]{:S(2)}) async-start(bf16[8,128,1152]{2,1,0:T(8,128)(2,1)} %add_convert_fusion), calls=%async_computation.8 | async-start | bytes 4718592 | tf_op jit(solution)/shard_map/all_to_all | solution.py:498
  352.7 4.0 fusion.28
  356.8 11.1 %shard_map.250 = (bf16[2,3,128,512]{3,2,1,0:T(8,128)(2,1)S(1)}, bf16[2,3,128,512]{3,2,1,0:T(8,128)(2,1)S(1)}, bf16[2,3,128,512]{3,2,1,0:T(8,128)(2,1)S(1)}, bf16[2,3,128,512]{3,2,1,0:T(8,128)(2,1)S(1)}) custom-call(s32[8]{0:T(128)S(1)} %fusion.41.order_ref, bf16[2,768,1024]{2,1,0:T(8,128)(2,1)} %get-tuple-element.173.refs_0_, ...), custom_call_target="tpu_custom_call" | custom-call | flops 10000000 | bytes 100000 | tf_op jit(solution)/shard_map/pallas_call | solution.py:458
  374.2 12.2 %shard_map.251 = (bf16[2,128,1024]{2,1,0:T(8,128)(2,1)S(1)}, bf16[2,128,1024]{2,1,0:T(8,128)(2,1)}, bf16[2,128,1024]{2,1,0:T(8,128)(2,1)}, bf16[2,128,1024]{2,1,...) custom-call(s32[8]{0:T(128)S(1)} %fusion.41.order_ref, ...), custom_call_target="tpu_custom_call" | custom-call | flops 10000000 | bytes 100000 | tf_op jit(solution)/shard_map/pallas_call | solution.py:252
  405.3 3.8 all-to-all-start.8
  412.4 10.3 %shard_map.252 = (bf16[2,3,128,512]{3,2,1,0:T(8,128)(2,1)S(1)}, bf16[2,3,128,512]{3,2,1,0:T(8,128)(2,1)S(1)}, bf16[2,3,128,512]{3,2,1,0:T(8,128)(2,1)S(1)}, bf16[2,3,128,512]{3,2,1,0:T(8,128)(2,1)S(1)}) custom-call(s32[8]{0:T(128)S(1)} %fusion.41.order_ref, bf16[2,768,1024]{2,1,0:T(8,128)(2,1)} %get-tuple-element.173.refs_0_, ...), custom_call_target="tpu_custom_call" | custom-call | flops 10000000 | bytes 100000 | tf_op jit(solution)/shard_map/pallas_call | solution.py:458
  427.7 5.5 all-to-all-done.8
  433.1 10.7 %all-to-all-start.9 = ((bf16[64,8,1024]{2,1,0:T(8,128)(2,1)}), bf16[64,8,1024]{2,1,0:T(8,128)(2,1)}, u32[]{:S(2)}, u32[]{:S(2)}) async-start(bf16[64,8,1024]{2,1,0:T(8,128)(2,1)} %fusion), calls=%async_computation.10 | async-start | bytes 2097152 | tf_op jit(solution)/shard_map/all_to_all | solution.py:498
  455.6 12.0 %shard_map.253 = (bf16[2,128,1024]{2,1,0:T(8,128)(2,1)S(1)}, bf16[2,128,1024]{2,1,0:T(8,128)(2,1)}, bf16[2,128,1024]{2,1,0:T(8,128)(2,1)}, bf16[2,128,1024]{2,1,...) custom-call(s32[8]{0:T(128)S(1)} %fusion.41.order_ref, ...), custom_call_target="tpu_custom_call" | custom-call | flops 10000000 | bytes 100000 | tf_op jit(solution)/shard_map/pallas_call | solution.py:252
  480.1 8.9 %all-to-all-start.10 = ((bf16[128,8,384]{2,1,0:T(8,128)(2,1)}), bf16[128,8,384]{2,1,0:T(8,128)(2,1)}, u32[]{:S(2)}, u32[]{:S(2)}) async-start(bf16[128,8,384]{2,1,0:T(8,128)(2,1)} %pad_maximum_fusion.3), calls=%async_computation.11 | async-start | bytes 1572864 | tf_op jit(solution)/shard_map/all_to_all | solution.py:498
  493.5 12.2 %collective-permute-done.33 = bf16[2,128,1024]{2,1,0:T(8,128)(2,1)} collective-permute-done((bf16[2,128,1024]{2,1,0:T(8,128)(2,1)}, bf16[2,128,1024]{2,1,0:T(8,128)(2,1)}, u32[]{:S(2)}, u32[]{:S(2)}) %collective-permute-start.33) | collective-permute-done | bytes 524320 | tf_op jit(solution)/shard_map/ppermute | solution.py:506
  531.8 5.5 collective-permute-done.40
  (417 shorter events, 194.8 us)
Async XLA Ops:
  7.2 219.7 %all-gather.3.cloned.1.call-start = ((), (), s32[]{:S(2)}) async-start(), calls=%async_computation.13 | async-start | bytes 10027008 | tf_op jit(solution)/shard_map/all_gather | solution.py:668
  23.1 65.7 %collective-permute-start.8 = (bf16[2,3,128,512]{3,2,1,0:T(8,128)(2,1)}, bf16[2,3,128,512]{3,2,1,0:T(8,128)(2,1)}, u32[]{:S(2)}, u32[]{:S(2)}) collective-permute-start(bf16[2,3,128,512]{3,2,1,0:T(8,128)(2,1)} %pad_maximum_fusion), channel_id=1, source_target_pairs={{0,16},{16,0},{1,17},{17,1},{2,18},{18,2},{3,19},{19,3},{4,20},{20... | collective-permute-start | bytes 2359304 | tf_op jit(solution)/shard_map/ppermute | solution.py:502
  27.1 50.5 %all-to-all-start = ((bf16[128,8,384]{2,1,0:T(8,128)(2,1)}), bf16[128,8,384]{2,1,0:T(8,128)(2,1)}, u32[]{:S(2)}, u32[]{:S(2)}) async-start(bf16[128,8,384]{2,1,0:T(8,128)(2,1)} %bitcast.6), calls=%async_computation | async-start | bytes 1572864 | tf_op jit(solution)/shard_map/all_to_all | solution.py:498
  38.4 32.9 %collective-permute-start.1 = (bf16[2,128,1024]{2,1,0:T(8,128)(2,1)S(1)}, bf16[2,128,1024]{2,1,0:T(8,128)(2,1)S(1)}, u32[]{:S(2)}, u32[]{:S(2)}) collective-permute-start(bf16[2,128,1024]{2,1,0:T(8,128)(2,1)S(1)} %pad_maximum_fusion.8.refs_0_), channel_id=1, source_target_pairs={{0,96},{32,0},{64,32},{96,64},{1,97},{33,1},{65,33},{97,65},{2,98}... | collective-permute-start | bytes 1572872 | tf_op jit(solution)/shard_map/ppermute | solution.py:506
  41.2 30.1 %collective-permute-start.2 = (bf16[2,128,1024]{2,1,0:T(8,128)(2,1)S(1)}, bf16[2,128,1024]{2,1,0:T(8,128)(2,1)S(1)}, u32[]{:S(2)}, u32[]{:S(2)}) collective-permute-start(bf16[2,128,1024]{2,1,0:T(8,128)(2,1)S(1)} %pad_maximum_fusion.8.refs_0_), channel_id=1, source_target_pairs={{0,64},{32,96},{64,0},{96,32},{1,65},{33,97},{65,1},{97,33},{2,66}... | collective-permute-start | bytes 1572872 | tf_op jit(solution)/shard_map/ppermute | solution.py:506
  41.5 33.2 %collective-permute-start.3 = (bf16[2,128,1024]{2,1,0:T(8,128)(2,1)S(1)}, bf16[2,128,1024]{2,1,0:T(8,128)(2,1)S(1)}, u32[]{:S(2)}, u32[]{:S(2)}) collective-permute-start(bf16[2,128,1024]{2,1,0:T(8,128)(2,1)S(1)} %pad_maximum_fusion.8.refs_0_), channel_id=1, source_target_pairs={{0,32},{32,64},{64,96},{96,0},{1,33},{33,65},{65,97},{97,1},{2,34}... | collective-permute-start | bytes 1572872 | tf_op jit(solution)/shard_map/ppermute | solution.py:506
  76.7 36.4 %collective-permute-start.7 = (bf16[2,128,1024]{2,1,0:T(8,128)(2,1)S(1)}, bf16[2,128,1024]{2,1,0:T(8,128)(2,1)}, u32[]{:S(2)}, u32[]{:S(2)}) collective-permute-start(bf16[2,128,1024]{2,1,0:T(8,128)(2,1)S(1)} %pad_maximum_fusion.9.refs_0_), channel_id=1, source_target_pairs={{0,32},{32,64},{64,96},{96,0},{1,33},{33,65},{65,97},{97,1},{2,34}... | collective-permute-start | bytes 1572872 | tf_op jit(solution)/shard_map/ppermute | solution.py:506
  78.7 84.4 %all-to-all-start.1 = ((bf16[64,8,1024]{2,1,0:T(8,128)(2,1)}), bf16[64,8,1024]{2,1,0:T(8,128)(2,1)}, u32[]{:S(2)}, u32[]{:S(2)}) async-start(bf16[64,8,1024]{2,1,0:T(8,128)(2,1)} %broadcast_in_dim.32), calls=%async_computation.1 | async-start | bytes 2097152 | tf_op jit(solution)/shard_map/all_to_all | solution.py:498
  134.0 29.1 %collective-permute-start.11 = (bf16[2,3,128,512]{3,2,1,0:T(8,128)(2,1)}, bf16[2,3,128,512]{3,2,1,0:T(8,128)(2,1)}, u32[]{:S(2)}, u32[]{:S(2)}) collective-permute-start(bf16[2,3,128,512]{3,2,1,0:T(8,128)(2,1)} %pad_maximum_fusion.2.refs_9_), channel_id=1, source_target_pairs={{0,32},{32,64},{64,96},{96,0},{1,33},{33,65},{65,97},{97,1},{2,34}... | collective-permute-start | bytes 2359304 | tf_op jit(solution)/shard_map/ppermute | solution.py:656
  134.6 28.6 %collective-permute-start.12 = (bf16[2,3,128,512]{3,2,1,0:T(8,128)(2,1)}, bf16[2,3,128,512]{3,2,1,0:T(8,128)(2,1)}, u32[]{:S(2)}, u32[]{:S(2)}) collective-permute-start(bf16[2,3,128,512]{3,2,1,0:T(8,128)(2,1)} %pad_maximum_fusion.2.refs_9_), channel_id=1, source_target_pairs={{0,96},{32,0},{64,32},{96,64},{1,97},{33,1},{65,33},{97,65},{2,98}... | collective-permute-start | bytes 2359304 | tf_op jit(solution)/shard_map/ppermute | solution.py:656
  184.0 33.7 %all-to-all-start.3 = ((bf16[8,128,1024]{2,1,0:T(8,128)(2,1)}), bf16[8,128,1024]{2,1,0:T(8,128)(2,1)}, u32[]{:S(2)}, u32[]{:S(2)}) async-start(bf16[8,128,1024]{2,1,0:T(8,128)(2,1)} %broadcast_in_dim.41), calls=%async_computation.3 | async-start | bytes 4194304 | tf_op jit(solution)/shard_map/all_to_all | solution.py:498
  219.2 47.9 %all-to-all-start.4 = ((bf16[8,128,1024]{2,1,0:T(8,128)(2,1)}), bf16[8,128,1024]{2,1,0:T(8,128)(2,1)}, u32[]{:S(2)}, u32[]{:S(2)}) async-start(bf16[8,128,1024]{2,1,0:T(8,128)(2,1)} %broadcast_in_dim.40), calls=%async_computation.4 | async-start | bytes 4194304 | tf_op jit(solution)/shard_map/all_to_all | solution.py:498
  275.9 47.7 %all-to-all-start.5 = ((bf16[8,128,1152]{2,1,0:T(8,128)(2,1)}), bf16[8,128,1152]{2,1,0:T(8,128)(2,1)}, u32[]{:S(2)}, u32[]{:S(2)}) async-start(bf16[8,128,1152]{2,1,0:T(8,128)(2,1)} %add_convert_fusion.1), calls=%async_computation.5 | async-start | bytes 4718592 | tf_op jit(solution)/shard_map/all_to_all | solution.py:498
  335.2 205.3 %reduce-scatter.2.cloned.1.call-start = ((), (), s32[]{:S(2)}) async-start(), calls=%async_computation.12 | async-start | bytes 8912896 | tf_op jit(solution)/shard_map/reduce_scatter | solution.py:783
  343.1 48.6 %all-to-all-start.7 = ((bf16[8,128,1152]{2,1,0:T(8,128)(2,1)}), bf16[8,128,1152]{2,1,0:T(8,128)(2,1)}, u32[]{:S(2)}, u32[]{:S(2)}) async-start(bf16[8,128,1152]{2,1,0:T(8,128)(2,1)} %add_convert_fusion), calls=%async_computation.8 | async-start | bytes 4718592 | tf_op jit(solution)/shard_map/all_to_all | solution.py:498
  368.1 23.7 %collective-permute-start.22 = (bf16[1,3,128,512]{3,2,1,0:T(8,128)(2,1)S(1)}, bf16[1,3,128,512]{3,2,1,0:T(8,128)(2,1)}, u32[]{:S(2)}, u32[]{:S(2)}) collective-permute-start(bf16[1,3,128,512]{3,2,1,0:T(8,128)(2,1)S(1)} %get-tuple-element.356), channel_id=1, source_target_pairs={{0,32},{32,64},{64,96},{96,0},{1,33},{33,65},{65,97},{97,1},{2,34}... | collective-permute-start | bytes 1179656 | tf_op jit(solution)/shard_map/ppermute | solution.py:539
  368.7 23.1 %collective-permute-start.23 = (bf16[1,3,128,512]{3,2,1,0:T(8,128)(2,1)S(1)}, bf16[1,3,128,512]{3,2,1,0:T(8,128)(2,1)}, u32[]{:S(2)}, u32[]{:S(2)}) collective-permute-start(bf16[1,3,128,512]{3,2,1,0:T(8,128)(2,1)S(1)} %get-tuple-element.355), channel_id=1, source_target_pairs={{0,96},{32,0},{64,32},{96,64},{1,97},{33,1},{65,33},{97,65},{2,98}... | collective-permute-start | bytes 1179656 | tf_op jit(solution)/shard_map/ppermute | solution.py:539
  388.2 39.4 %collective-permute-start.24 = (bf16[2,128,1024]{2,1,0:T(8,128)(2,1)}, bf16[2,128,1024]{2,1,0:T(8,128)(2,1)}, u32[]{:S(2)}, u32[]{:S(2)}) collective-permute-start(bf16[2,128,1024]{2,1,0:T(8,128)(2,1)} %get-tuple-element.201), channel_id=1, source_target_pairs={{0,32},{32,64},{64,96},{96,0},{1,33},{33,65},{65,97},{97,1},{2,34}... | collective-permute-start | bytes 1572872 | tf_op jit(solution)/shard_map/ppermute | solution.py:506
  388.2 39.4 %collective-permute-start.25 = (bf16[2,128,1024]{2,1,0:T(8,128)(2,1)}, bf16[2,128,1024]{2,1,0:T(8,128)(2,1)}, u32[]{:S(2)}, u32[]{:S(2)}) collective-permute-start(bf16[2,128,1024]{2,1,0:T(8,128)(2,1)} %get-tuple-element.202), channel_id=1, source_target_pairs={{0,64},{32,96},{64,0},{96,32},{1,65},{33,97},{65,1},{97,33},{2,66}... | collective-permute-start | bytes 1572872 | tf_op jit(solution)/shard_map/ppermute | solution.py:506
  389.7 38.0 %collective-permute-start.26 = (bf16[2,128,1024]{2,1,0:T(8,128)(2,1)}, bf16[2,128,1024]{2,1,0:T(8,128)(2,1)}, u32[]{:S(2)}, u32[]{:S(2)}) collective-permute-start(bf16[2,128,1024]{2,1,0:T(8,128)(2,1)} %get-tuple-element.203), channel_id=1, source_target_pairs={{0,96},{32,0},{64,32},{96,64},{1,97},{33,1},{65,33},{97,65},{2,98}... | collective-permute-start | bytes 1572872 | tf_op jit(solution)/shard_map/ppermute | solution.py:506
  395.1 76.6 %collective-permute-start.31 = (bf16[2,3,128,512]{3,2,1,0:T(8,128)(2,1)}, bf16[2,3,128,512]{3,2,1,0:T(8,128)(2,1)}, u32[]{:S(2)}, u32[]{:S(2)}) collective-permute-start(bf16[2,3,128,512]{3,2,1,0:T(8,128)(2,1)} %pad_maximum_fusion.5), channel_id=1, source_target_pairs={{0,96},{32,0},{64,32},{96,64},{1,97},{33,1},{65,33},{97,65},{2,98}... | collective-permute-start | bytes 2359304 | tf_op jit(solution)/shard_map/ppermute | solution.py:545
  402.0 20.9 %collective-permute-start.27 = (bf16[64,8,1024]{2,1,0:T(8,128)(2,1)}, bf16[64,8,1024]{2,1,0:T(8,128)(2,1)}, u32[]{:S(2)}, u32[]{:S(2)}) collective-permute-start(bf16[64,8,1024]{2,1,0:T(8,128)(2,1)} %dynamic-slice_bitcast_fusion), channel_id=1, source_target_pairs={{0,1},{1,0},{2,3},{3,2},{4,5},{5,4},{6,7},{7,6},{8,9},{9,8},{10,11... | collective-permute-start | bytes 3145736 | tf_op jit(solution)/shard_map/ppermute | solution.py:502
  405.3 27.8 %all-to-all-start.8 = ((bf16[8,128,128]{2,1,0:T(8,128)(2,1)}), bf16[8,128,128]{2,1,0:T(8,128)(2,1)S(1)}, u32[]{:S(2)}, u32[]{:S(2)}) async-start(bf16[8,128,128]{2,1,0:T(8,128)(2,1)} %bitcast.231), calls=%async_computation.9 | async-start | bytes 524288 | tf_op jit(solution)/shard_map/all_to_all | solution.py:498
  422.9 48.8 %collective-permute-start.30 = (bf16[2,3,128,512]{3,2,1,0:T(8,128)(2,1)}, bf16[2,3,128,512]{3,2,1,0:T(8,128)(2,1)}, u32[]{:S(2)}, u32[]{:S(2)}) collective-permute-start(bf16[2,3,128,512]{3,2,1,0:T(8,128)(2,1)} %pad_maximum_fusion.4), channel_id=1, source_target_pairs={{0,32},{32,64},{64,96},{96,0},{1,33},{33,65},{65,97},{97,1},{2,34}... | collective-permute-start | bytes 2359304 | tf_op jit(solution)/shard_map/ppermute | solution.py:544
  433.1 38.7 %all-to-all-start.9 = ((bf16[64,8,1024]{2,1,0:T(8,128)(2,1)}), bf16[64,8,1024]{2,1,0:T(8,128)(2,1)}, u32[]{:S(2)}, u32[]{:S(2)}) async-start(bf16[64,8,1024]{2,1,0:T(8,128)(2,1)} %fusion), calls=%async_computation.10 | async-start | bytes 2097152 | tf_op jit(solution)/shard_map/all_to_all | solution.py:498
  446.1 25.7 %collective-permute-start.28 = (bf16[1,3,128,512]{3,2,1,0:T(8,128)(2,1)}, bf16[1,3,128,512]{3,2,1,0:T(8,128)(2,1)}, u32[]{:S(2)}, u32[]{:S(2)}) collective-permute-start(bf16[1,3,128,512]{3,2,1,0:T(8,128)(2,1)} %get-tuple-element.354), channel_id=1, source_target_pairs={{0,32},{32,64},{64,96},{96,0},{1,33},{33,65},{65,97},{97,1},{2,34}... | collective-permute-start | bytes 1179656 | tf_op jit(solution)/shard_map/ppermute | solution.py:539
  447.6 24.2 %collective-permute-start.29 = (bf16[1,3,128,512]{3,2,1,0:T(8,128)(2,1)}, bf16[1,3,128,512]{3,2,1,0:T(8,128)(2,1)}, u32[]{:S(2)}, u32[]{:S(2)}) collective-permute-start(bf16[1,3,128,512]{3,2,1,0:T(8,128)(2,1)} %get-tuple-element.353), channel_id=1, source_target_pairs={{0,96},{32,0},{64,32},{96,64},{1,97},{33,1},{65,33},{97,65},{2,98}... | collective-permute-start | bytes 1179656 | tf_op jit(solution)/shard_map/ppermute | solution.py:539
  453.9 66.4 %collective-permute-start.32 = (bf16[128,1024]{1,0:T(8,128)(2,1)}, bf16[128,1024]{1,0:T(8,128)(2,1)}, u32[]{:S(2)}, u32[]{:S(2)}) collective-permute-start(bf16[128,1024]{1,0:T(8,128)(2,1)} %fusion.23), channel_id=1, source_target_pairs={{0,16},{16,0},{1,17},{17,1},{2,18},{18,2},{3,19},{19,3},{4,20},{20... | collective-permute-start | bytes 786440 | tf_op jit(solution)/shard_map/ppermute | solution.py:502
  475.4 30.3 %collective-permute-start.33 = (bf16[2,128,1024]{2,1,0:T(8,128)(2,1)}, bf16[2,128,1024]{2,1,0:T(8,128)(2,1)}, u32[]{:S(2)}, u32[]{:S(2)}) collective-permute-start(bf16[2,128,1024]{2,1,0:T(8,128)(2,1)} %get-tuple-element.229), channel_id=1, source_target_pairs={{0,32},{32,64},{64,96},{96,0},{1,33},{33,65},{65,97},{97,1},{2,34}... | collective-permute-start | bytes 1572872 | tf_op jit(solution)/shard_map/ppermute | solution.py:506
  475.7 37.3 %collective-permute-start.34 = (bf16[2,128,1024]{2,1,0:T(8,128)(2,1)}, bf16[2,128,1024]{2,1,0:T(8,128)(2,1)}, u32[]{:S(2)}, u32[]{:S(2)}) collective-permute-start(bf16[2,128,1024]{2,1,0:T(8,128)(2,1)} %get-tuple-element.230), channel_id=1, source_target_pairs={{0,64},{32,96},{64,0},{96,32},{1,65},{33,97},{65,1},{97,33},{2,66}... | collective-permute-start | bytes 1572872 | tf_op jit(solution)/shard_map/ppermute | solution.py:506
  478.8 34.2 %collective-permute-start.35 = (bf16[2,128,1024]{2,1,0:T(8,128)(2,1)S(1)}, bf16[2,128,1024]{2,1,0:T(8,128)(2,1)}, u32[]{:S(2)}, u32[]{:S(2)}) collective-permute-start(bf16[2,128,1024]{2,1,0:T(8,128)(2,1)S(1)} %copy-done.46), channel_id=1, source_target_pairs={{0,96},{32,0},{64,32},{96,64},{1,97},{33,1},{65,33},{97,65},{2,98}... | collective-permute-start | bytes 1572872 | tf_op jit(solution)/shard_map/ppermute | solution.py:506
  480.1 35.3 %all-to-all-start.10 = ((bf16[128,8,384]{2,1,0:T(8,128)(2,1)}), bf16[128,8,384]{2,1,0:T(8,128)(2,1)}, u32[]{:S(2)}, u32[]{:S(2)}) async-start(bf16[128,8,384]{2,1,0:T(8,128)(2,1)} %pad_maximum_fusion.3), calls=%async_computation.11 | async-start | bytes 1572864 | tf_op jit(solution)/shard_map/all_to_all | solution.py:498
  (114 other events, 1520.1 us)
Sparse Core Ops, SparseCore 0:
  22.2 102.3 all-gather.2
  340.4 108.6 reduce-scatter.1

commit v11 on v10

--- a/solution.py
+++ b/solution.py
@@ -633,7 +633,7 @@
     both_w = [jnp.stack([both_w[e], other_w[e]]) for e in range(local)]
     seq_rows = [along_z(both_0)]
     seq_rows.append(along_z(after_all(both_1, *seq_rows[0][1:])))
-    head_all = after_all(head_all, *seq_rows[1][1:], *both_w)
+    head_all = after_all(head_all, *seq_rows[0][1:], other_w)
     w_heads = head_all[:, :span]
     small_all = head_all[:, span:]
     router = small_all[:, :experts]
@@ -682,13 +682,14 @@
         return gain_row, w_heads, head_row, cosine, sine, seg[:, None], seg[None, :]
 
     mixed_0, *saved_0 = attend_forward(order, seq_rows[0], *attention_args(0))
+    seq_rows[1], mixed_0 = lax.optimization_barrier((seq_rows[1], mixed_0))
     mixed_1, *saved_1 = attend_forward(order, seq_rows[1], *attention_args(1))
     saved = [saved_0, saved_1]
     out_own, mixed_0, mixed_1 = lax.optimization_barrier((out_own, mixed_0, mixed_1))
-    mixed_1 = after_all(mixed_1, *moved_w[0], *moved_w[1])
     out_other = flip(out_own, "core")
     mixed = jnp.stack([mixed_0, mixed_1]).reshape(micro, n_ctx, tok, heads).transpose(1, 0, 2, 3)
     mixed = exchange(mixed.reshape(n_ctx, all_tok, heads), CTX)
+    mixed, moved_w[0] = lax.optimization_barrier((mixed, moved_w[0]))
     mixed = mixed.transpose(1, 0, 2).reshape(all_tok, width)
     out_full = jnp.where(
         core == 0,
@@ -698,12 +699,11 @@
     middle = tokens.reshape(all_tok, width).astype(F32) + mm(mixed, out_full)
     inv_two = lax.rsqrt(jnp.mean(middle * middle, axis=-1, keepdims=True) + EPS)
     hidden_two = (middle * inv_two * gain_mlp).astype(BF)
-    x_0 = hidden_two[:tok]
+    x_0 = exchange.copies(hidden_two[:tok], GROUP, n_ctx)
     weights = []
     for e, (w_before, w_after) in enumerate(moved_w):
         w_far = [lax.ppermute(w_before[:1], "z", UP), lax.ppermute(w_after[1:], "z", DOWN)]
         weights.append([both_w[e], w_after, *w_far, w_before])
-    x_0 = exchange.copies(x_0, GROUP, n_ctx)
     x_0, weights = lax.optimization_barrier((x_0, weights))
     x_1 = exchange.copies(hidden_two[tok:], GROUP, n_ctx)
     logits = jnp.where(chosen, mm(hidden_two, router), -1e30)
@@ -728,18 +728,14 @@
     def back_sum(own, other):
         return add(own, flip(other, "core"))
 
-    def middle_back(m, back):
-        rows_mixed, rows_middle, inv, hidden, gates = (
-            own_rows(v, m) for v in (mixed, middle, inv_two, hidden_two, gates_all)
-        )
+    def middle_back(m, back, before):
+        rows_middle, inv, gates = (own_rows(v, m) for v in (middle, inv_two, gates_all))
         grad_top = own_rows(cot, m).astype(F32)
         tail = back[:, width:]
         d_gates = tail[:, :experts] + tail[:, 64 : 64 + experts]
         d_select = gates * (d_gates - jnp.sum(gates * d_gates, axis=-1, keepdims=True))
         d_logits = d_select.astype(BF)
-        grad_router = t_mm(hidden, d_logits)
         d_two = back[:, :width] + mm_t(d_logits, router)
-        grad_mlp = jnp.sum(d_two * rows_middle * inv, axis=0)
         u = d_two * gain_mlp
         d_middle = (
             grad_top
@@ -747,10 +743,29 @@
             - rows_middle * (inv**3 * jnp.mean(u * rows_middle, axis=-1, keepdims=True))
         )
         d_branch = d_middle.astype(BF)
-        grad_out = t_mm(rows_mixed, d_branch)
         d_mixed = mm_t(d_branch, out_full).astype(BF)
         d_mixed = d_mixed.reshape(tok, n_ctx, heads).transpose(1, 0, 2)
-        return d_middle, d_mixed, (grad_out, grad_router, grad_mlp)
+        return d_middle, d_mixed, before + [(d_branch, d_logits, d_two)]
+
+    def weight_grads(saved_rows):
+        grad_out = grad_router = grad_mlp = 0.0
+        for m, (d_branch, d_logits, d_two) in enumerate(saved_rows):
+            rows_mixed, rows_middle, inv, hidden = (
+                own_rows(v, m) for v in (mixed, middle, inv_two, hidden_two)
+            )
+            grad_out = grad_out + t_mm(rows_mixed, d_branch)
+            grad_router = grad_router + t_mm(hidden, d_logits)
+            grad_mlp = grad_mlp + jnp.sum(d_two * rows_middle * inv, axis=0)
+        return grad_out, grad_router, grad_mlp
+
+    def pack_grads(grad_heads, grad_router, grad_attn, grad_mlp, grad_qk):
+        grad_qk = jnp.pad(grad_qk[:, None], ((0, 0), (0, rows - 1))).reshape(-1)
+        grad_small = jnp.concatenate(
+            [grad_router, grad_attn[:, None], grad_mlp[:, None], grad_qk[:, None]], axis=1
+        )
+        grad_small = jnp.pad(grad_small, ((0, 0), (0, 128 - grad_small.shape[1])))
+        grad_pack = jnp.concatenate([grad_heads, grad_small], axis=1).astype(BF)
+        return grad_pack.reshape(n_all, rows, -1)
 
     def attention_back(m, d_mixed):
         *d_hidden, grad_heads, grad_attn, grad_qk = attend_backward(
@@ -782,7 +797,7 @@
     )
     moe = lax.psum_scatter(moe, FSDP, scatter_dimension=0, tiled=True)[0]
     back_1 = back_sum(back_own, back_other)
-    d_middle_0, d_mixed_0, grads_0 = middle_back(0, sum_parts(back_0))
+    d_middle_0, d_mixed_0, d_branches = middle_back(0, sum_parts(back_0), [])
     d_mixed_0 = exchange(d_mixed_0, CTX)
     d_mixed_0, back_1 = lax.optimization_barrier((d_mixed_0, back_1))
     back_1 = exchange(back_1, GROUP)
@@ -792,43 +807,41 @@
     d_hidden_0, head_grads_0 = attention_back(0, after_all(d_mixed_0, parts[0][0]))
     hidden_moved_0 = by_z(d_hidden_0)
     back_1, d_hidden_0[0], far[0] = lax.optimization_barrier((back_1, d_hidden_0[0], far[0]))
-    d_middle_1, d_mixed_1, grads_1 = middle_back(1, sum_parts(back_1))
+    d_middle_1, d_mixed_1, d_branches = middle_back(1, sum_parts(back_1), d_branches)
+    far[0], d_mixed_1 = lax.optimization_barrier((far[0], d_mixed_1))
     d_mixed_1 = exchange(d_mixed_1, CTX)
-    kept_1[0] = after_all(kept_1[0], back_1)
+    moved = [ring_sums(parts[0], far[0])]
+    d_mixed_1, hidden_moved_0 = lax.optimization_barrier((d_mixed_1, hidden_moved_0))
+    d_hidden_1, head_grads_1 = attention_back(1, d_mixed_1)
+    d_hidden_1, d_branches, hidden_moved_0, moved[0], kept_1 = lax.optimization_barrier(
+        (d_hidden_1, d_branches, hidden_moved_0, moved[0], kept_1)
+    )
+    hidden_moved_1 = by_z(d_hidden_1)
+    grad_heads, grad_attn, grad_qk = jax.tree.map(jnp.add, head_grads_0, head_grads_1)
+    grad_out, grad_router, grad_mlp = weight_grads(d_branches)
+    grad_pack = pack_grads(grad_heads, grad_router, grad_attn, grad_mlp, grad_qk)
+    grad_pack = exchange(grad_pack, ALL)
     parts.append(expert_grads(order, (kept_0, kept_1), 1))
-    moved = [ring_sums(parts[0], far[0])]
-    grad_out, grad_router, grad_mlp = jax.tree.map(jnp.add, grads_0, grads_1)
+    far.append(relay(parts[1][2]))
     grad_out = grad_out.astype(BF).reshape(n_all // 2, 2, rows, width)
     grad_own = lax.dynamic_index_in_dim(grad_out, core, axis=1, keepdims=False)
     grad_other = lax.dynamic_index_in_dim(grad_out, 1 - core, axis=1, keepdims=False)
     grad_out = back_sum(grad_own, grad_other)
-    d_mixed_1, parts[1], hidden_moved_0, grad_out = lax.optimization_barrier(
-        (d_mixed_1, parts[1], hidden_moved_0, grad_out)
-    )
-    far.append(relay(parts[1][2]))
+    grad_pack, grad_out, hidden_moved_1, far[1] = lax.optimization_barrier(
+        (grad_pack, grad_out, hidden_moved_1, far[1])
+    )
+    exchange.last = grad_pack
     grad_out = exchange(grad_out, CTX + GROUP)
-    d_hidden_1, head_grads_1 = attention_back(1, d_mixed_1)
-    d_hidden_1, grad_out, far[1], moved[0] = lax.optimization_barrier(
-        (d_hidden_1, grad_out, far[1], moved[0])
-    )
-    hidden_moved_1 = by_z(d_hidden_1)
-    moved.append(ring_sums(parts[1], after_all(far[1], hidden_moved_1[0])))
+    moved.append(ring_sums(parts[1], far[1]))
     hidden_sums = pair_sums(d_hidden_0, hidden_moved_0)
     d_hidden_0 = hidden_sums[0] + flip(hidden_sums[1].astype(BF), "yl").astype(F32)
-    exchange.last = grad_out
+    grad_out, moved[1] = lax.optimization_barrier((grad_out, moved[1]))
     weight_sums = [pair_sums(p, q) for p, q in zip(parts, moved)]
     weight_yl = [flip(sums[1].astype(BF), "yl") for sums in weight_sums]
     hidden_sums = pair_sums(d_hidden_1, hidden_moved_1)
     hidden_yl = flip(hidden_sums[1].astype(BF), "yl")
-    grad_heads, grad_attn, grad_qk = jax.tree.map(jnp.add, head_grads_0, head_grads_1)
-
-    grad_qk = jnp.pad(grad_qk[:, None], ((0, 0), (0, rows - 1))).reshape(-1)
-    grad_small = jnp.concatenate(
-        [grad_router, grad_attn[:, None], grad_mlp[:, None], grad_qk[:, None]], axis=1
-    )
-    grad_small = jnp.pad(grad_small, ((0, 0), (0, 128 - grad_small.shape[1])))
-    grad_pack = jnp.concatenate([grad_heads, grad_small], axis=1).astype(BF)
-    grad_pack = exchange(grad_pack.reshape(n_all, rows, -1), ALL).astype(F32)
+
+    grad_pack = grad_pack.astype(F32)
     own_heads = jnp.sum(grad_pack[:, :, :span].reshape(n_ctx, n_fsdp, rows, -1), axis=1)
     own_heads = own_heads.transpose(1, 0, 2)
     own_small = jnp.sum(grad_pack[:, :, span:], axis=0)

time: 559 us -> 589 us (1.054)
  waiting for transfers between devices: 129 us -> 156 us
  local copies, waits for them, and re-layouts: 52 us -> 69 us
  matrix products: 14.3 us -> 7.6 us
  starting transfers between devices: 127 us -> 121 us
    ppermute x4, waiting for transfers between devices: 12.4 us -> 33.4 us  [body(): last = [lax.ppermute(block, 'z', UP), lax.ppermute(block, 'z', DOWN)]]
    unnamed x187 -> x223, local copies, waits for them, and re-layouts: 15.9 us -> 32.6 us
    all_to_all x11, waiting for transfers between devices: 21.9 us -> 32.8 us  [swap(): return lax.all_to_all(parts, axis, split_axis=0, concat_axis=0, tiled=True)]
    ppermute x12, waiting for transfers between devices: 61.2 us -> 50.7 us  [by_z(): lax.ppermute(parts[k], 'z', perm)]
    ppermute x13, waiting for transfers between devices: 19.3 us -> 27.5 us  [flip(): return lax.ppermute(block, axis, FLIP)]
  transfers between devices with their start and end apart: 54 -> 54, of which waited for: 21 -> 21; matrix products, arithmetic and copies ran while one was open for 21% -> 18% of each run, Pallas kernels for 26% -> 25%
where the time goes in v11:
time: 589 us; the launch traced here: 582 us
  waiting for transfers between devices  156 us (26%)
  Pallas kernels  144 us (24%)
  starting transfers between devices  121 us (21%)
  local copies, waits for them, and re-layouts  69 us (12%)
  other arithmetic  67.6 us (11%)
  between operations  16.6 us (3%)
  matrix products  7.6 us (1%)
    pallas_call x2, Pallas kernels, run_experts(): pl.pallas_call(functools.partial(expert_kernel, again=moe is not None), o...  81.9 us
    all_to_all x11, starting transfers between devices, swap(): return lax.all_to_all(parts, axis, split_axis=0, concat_axis=0, tiled=True)  74.3 us
    ppermute x12, waiting for transfers between devices, by_z(): lax.ppermute(parts[k], 'z', perm)  50.7 us
    ppermute x4, waiting for transfers between devices, body(): last = [lax.ppermute(block, 'z', UP), lax.ppermute(block, 'z', DOWN)]  33.4 us
    all_to_all x11, waiting for transfers between devices, swap(): return lax.all_to_all(parts, axis, split_axis=0, concat_axis=0, tiled=True)  32.8 us
    unnamed x223, local copies, waits for them, and re-layouts  32.6 us
    ppermute x13, waiting for transfers between devices, flip(): return lax.ppermute(block, axis, FLIP)  27.5 us
    pallas_call x2, Pallas kernels, attend_backward(): pl.pallas_call(attend_back_kernel, out_shape=outs, grid=(1,), in_specs=[p...  23.7 us
  transfers between devices with their start and end apart: 54, of which 21 were waited for; matrix products, arithmetic and copies ran while one was open for 18% of the time, Pallas kernels for 25%

profile of v11, /device:TPU:0, one launch (start us, length us, event | category | flops | bytes accessed | tf_op | source)
XLA Modules:
  0.0 581.6 jit_solution(5001107621253756019)
XLA Ops:
  24.3 11.2 %all-to-all-start = ((bf16[128,8,384]{2,1,0:T(8,128)(2,1)}), bf16[128,8,384]{2,1,0:T(8,128)(2,1)S(1)}, u32[]{:S(2)}, u32[]{:S(2)}) async-start(bf16[128,8,384]{2,1,0:T(8,128)(2,1)} %bitcast.6), calls=%async_computation | async-start | bytes 1572864 | tf_op jit(solution)/shard_map/all_to_all | solution.py:498
  43.1 13.7 %all-to-all-done = bf16[128,8,384]{2,1,0:T(8,128)(2,1)S(1)} async-done(((bf16[128,8,384]{2,1,0:T(8,128)(2,1)}), bf16[128,8,384]{2,1,0:T(8,128)(2,1)S(1)}, u32[]{:S(2)}, u32[]{:S(2)}) %all-to-all-start) | async-done | bytes 786464 | tf_op jit(solution)/shard_map/all_to_all | solution.py:498
  58.0 5.5 all-to-all-start.1
  66.9 10.0 %collective-permute-done.2.refs_1_ = bf16[2,128,1024]{2,1,0:T(8,128)(2,1)} collective-permute-done((bf16[2,128,1024]{2,1,0:T(8,128)(2,1)S(1)}, bf16[2,128,1024]{2,1,0:T(8,128)(2,1)}, u32[]{:S(2)}, u32[]{:S(2)}) %collective-permute-start.2) | collective-permute-done | bytes 524320 | tf_op jit(solution)/shard_map/ppermute | solution.py:506
  76.9 5.3 collective-permute-done.4.refs_3_
  88.8 8.8 %shard_map.246 = (bf16[1024,128]{1,0:T(8,128)(2,1)S(1)}, bf16[1024,1024]{1,0:T(8,128)(2,1)S(1)}, bf16[1024,128]{1,0:T(8,128)(2,1)S(1)}, bf16[1024,128]{1,0:T(8,128)(2,1)S(1)}) custom-call(s32[8]{0:T(128)S(1)} %fusion.36.order_ref, bf16[2,128,1024]{2,1,0:T(8,128)(2,1)S(1)} %copy-done.6, bf16[2,128,1024]{2,1,0:T(8,128)(2,1)} %collective-permute-done.2.refs_1_, ...), custom_call_target="tpu_custom_call" | custom-call | flops 10000000 | bytes 100000 | tf_op jit(solution)/shard_map/pallas_call | solution.py:229
  100.3 7.6 %collective-permute-done.7.refs_3_ = bf16[2,128,1024]{2,1,0:T(8,128)(2,1)} collective-permute-done((bf16[2,128,1024]{2,1,0:T(8,128)(2,1)S(1)}, bf16[2,128,1024]{2,1,0:T(8,128)(2,1)}, u32[]{:S(2)}, u32[]{:S(2)}) %collective-permute-start.7) | collective-permute-done | bytes 524320 | tf_op jit(solution)/shard_map/ppermute | solution.py:506
  107.9 9.3 %shard_map.247 = (bf16[1024,128]{1,0:T(8,128)(2,1)S(1)}, bf16[1024,1024]{1,0:T(8,128)(2,1)S(1)}, bf16[1024,128]{1,0:T(8,128)(2,1)S(1)}, bf16[1024,128]{1,0:T(8,128)(2,1)S(1)}) custom-call(s32[8]{0:T(128)S(1)} %fusion.36.order_ref, bf16[2,128,1024]{2,1,0:T(8,128)(2,1)S(1)} %pad_maximum_fusion.8.refs_0_, bf16[2,128,1024]{2,1,0:T(8,128)(2,1)} %collective-permute-done.5.refs_1_, ...), custom_call_target="tpu_custom_call" | custom-call | flops 10000000 | bytes 100000 | tf_op jit(solution)/shard_map/pallas_call | solution.py:229
  130.0 16.4 %collective-permute-done.10.refs_5_ = bf16[2,3,128,512]{3,2,1,0:T(8,128)(2,1)} collective-permute-done((bf16[2,3,128,512]{3,2,1,0:T(8,128)(2,1)S(1)}, bf16[2,3,128,512]{3,2,1,0:T(8,128)(2,1)}, u32[]{:S(2)}, u32[]{:S(2)}) %collective-permute-start.10) | collective-permute-done | bytes 786464 | tf_op jit(solution)/shard_map/ppermute | solution.py:656
  158.9 6.2 %all-to-all-start.3 = ((bf16[8,128,1024]{2,1,0:T(8,128)(2,1)}), bf16[8,128,1024]{2,1,0:T(8,128)(2,1)}, u32[]{:S(2)}, u32[]{:S(2)}) async-start(bf16[8,128,1024]{2,1,0:T(8,128)(2,1)} %broadcast_in_dim.41), calls=%async_computation.3 | async-start | bytes 4194304 | tf_op jit(solution)/shard_map/all_to_all | solution.py:498
  173.9 13.0 %collective-permute-done.15.refs_13_ = bf16[2,3,128,512]{3,2,1,0:T(8,128)(2,1)S(1)} collective-permute-done((bf16[2,3,128,512]{3,2,1,0:T(8,128)(2,1)S(1)}, bf16[2,3,128,512]{3,2,1,0:T(8,128)(2,1)S(1)}, u32[]{:S(2)}, u32[]{:S(2)}) %collective-permute-start.15) | collective-permute-done | bytes 786464 | tf_op jit(solution)/shard_map/ppermute | solution.py:656
  191.1 4.3 collective-permute-done.12.refs_6_
  195.4 6.6 %collective-permute-done.16.refs_11_ = bf16[1,3,128,512]{3,2,1,0:T(8,128)(2,1)} collective-permute-done((bf16[1,3,128,512]{3,2,1,0:T(8,128)(2,1)S(1)}, bf16[1,3,128,512]{3,2,1,0:T(8,128)(2,1)}, u32[]{:S(2)}, u32[]{:S(2)}) %collective-permute-start.16) | collective-permute-done | bytes 393248 | tf_op jit(solution)/shard_map/ppermute | solution.py:705
  203.6 7.1 %all-to-all-start.4 = ((bf16[8,128,1024]{2,1,0:T(8,128)(2,1)}), bf16[8,128,1024]{2,1,0:T(8,128)(2,1)}, u32[]{:S(2)}, u32[]{:S(2)}) async-start(bf16[8,128,1024]{2,1,0:T(8,128)(2,1)} %broadcast_in_dim.40), calls=%async_computation.4 | async-start | bytes 4194304 | tf_op jit(solution)/shard_map/all_to_all | solution.py:498
  212.1 41.0 %shard_map.248 = (bf16[16,2,128,1024]{3,2,1,0:T(8,128)(2,1)}, bf16[8,128,1152]{2,1,0:T(8,128)(2,1)}, bf16[8,128,1152]{2,1,0:T(8,128)(2,1)}, bf16[2,768,1024]{2,1...) custom-call(s32[10]{0:T(128)} %pad_add_fusion.scalar_ref, ...), custom_call_target="tpu_custom_call" | custom-call | flops 10000000 | bytes 100000 | tf_op jit(solution)/shard_map/pallas_call | solution.py:412
  253.6 4.5 collective-permute-done.19
  262.2 7.1 %all-to-all-start.5 = ((bf16[8,128,1152]{2,1,0:T(8,128)(2,1)}), bf16[8,128,1152]{2,1,0:T(8,128)(2,1)}, u32[]{:S(2)}, u32[]{:S(2)}) async-start(bf16[8,128,1152]{2,1,0:T(8,128)(2,1)} %add_convert_fusion.1), calls=%async_computation.5 | async-start | bytes 4718592 | tf_op jit(solution)/shard_map/all_to_all | solution.py:498
  269.4 40.9 %shard_map.249 = (bf16[16,2,128,1024]{3,2,1,0:T(8,128)(2,1)}, bf16[8,128,1152]{2,1,0:T(8,128)(2,1)}, bf16[8,128,1152]{2,1,0:T(8,128)(2,1)}, bf16[2,768,1024]{2,1...) custom-call(s32[10]{0:T(128)} %pad_add_fusion.scalar_ref, ...), custom_call_target="tpu_custom_call", output_to_operand_aliasing={{0}: (15, {})} | custom-call | flops 10000000 | bytes 100000 | tf_op jit(solution)/shard_map/pallas_call | solution.py:412
  322.0 4.4 add_convert_fusion
  329.9 7.7 %all-to-all-start.7 = ((bf16[8,128,1152]{2,1,0:T(8,128)(2,1)}), bf16[8,128,1152]{2,1,0:T(8,128)(2,1)}, u32[]{:S(2)}, u32[]{:S(2)}) async-start(bf16[8,128,1152]{2,1,0:T(8,128)(2,1)} %add_convert_fusion), calls=%async_computation.8 | async-start | bytes 4718592 | tf_op jit(solution)/shard_map/all_to_all | solution.py:498
  339.0 10.1 %shard_map.250 = (bf16[2,3,128,512]{3,2,1,0:T(8,128)(2,1)S(1)}, bf16[2,3,128,512]{3,2,1,0:T(8,128)(2,1)S(1)}, bf16[2,3,128,512]{3,2,1,0:T(8,128)(2,1)S(1)}, bf16[2,3,128,512]{3,2,1,0:T(8,128)(2,1)S(1)}) custom-call(s32[8]{0:T(128)S(1)} %fusion.36.order_ref, bf16[2,768,1024]{2,1,0:T(8,128)(2,1)} %get-tuple-element.203.refs_0_, ...), custom_call_target="tpu_custom_call" | custom-call | flops 10000000 | bytes 100000 | tf_op jit(solution)/shard_map/pallas_call | solution.py:458
  368.1 12.3 %shard_map.251 = (bf16[2,128,1024]{2,1,0:T(8,128)(2,1)S(1)}, bf16[2,128,1024]{2,1,0:T(8,128)(2,1)}, bf16[2,128,1024]{2,1,0:T(8,128)(2,1)}, bf16[2,128,1024]{2,1,...) custom-call(s32[8]{0:T(128)S(1)} %fusion.36.order_ref, ...), custom_call_target="tpu_custom_call" | custom-call | flops 10000000 | bytes 100000 | tf_op jit(solution)/shard_map/pallas_call | solution.py:252
  404.4 6.2 %collective-permute-done.24 = bf16[2,128,1024]{2,1,0:T(8,128)(2,1)} collective-permute-done((bf16[2,128,1024]{2,1,0:T(8,128)(2,1)}, bf16[2,128,1024]{2,1,0:T(8,128)(2,1)}, u32[]{:S(2)}, u32[]{:S(2)}) %collective-permute-start.24) | collective-permute-done | bytes 524320 | tf_op jit(solution)/shard_map/ppermute | solution.py:506
  412.1 15.0 %all-to-all-done.8 = bf16[8,128,128]{2,1,0:T(8,128)(2,1)S(1)} async-done(((bf16[8,128,128]{2,1,0:T(8,128)(2,1)}), bf16[8,128,128]{2,1,0:T(8,128)(2,1)S(1)}, u32[]{:S(2)}, u32[]{:S(2)}) %all-to-all-start.8) | async-done | bytes 262176 | tf_op jit(solution)/shard_map/all_to_all | solution.py:498
  431.8 11.4 %shard_map.252 = (bf16[2,128,1024]{2,1,0:T(8,128)(2,1)S(1)}, bf16[2,128,1024]{2,1,0:T(8,128)(2,1)S(1)}, bf16[2,128,1024]{2,1,0:T(8,128)(2,1)S(1)}, bf16[2,128,10...) custom-call(s32[8]{0:T(128)S(1)} %fusion.36.order_ref, ...), custom_call_target="tpu_custom_call" | custom-call | flops 10000000 | bytes 100000 | tf_op jit(solution)/shard_map/pallas_call | solution.py:252
  452.5 10.1 %shard_map.253 = (bf16[2,3,128,512]{3,2,1,0:T(8,128)(2,1)S(1)}, bf16[2,3,128,512]{3,2,1,0:T(8,128)(2,1)S(1)}, bf16[2,3,128,512]{3,2,1,0:T(8,128)(2,1)S(1)}, bf16[2,3,128,512]{3,2,1,0:T(8,128)(2,1)S(1)}) custom-call(s32[8]{0:T(128)S(1)} %fusion.36.order_ref, bf16[2,768,1024]{2,1,0:T(8,128)(2,1)} %get-tuple-element.203.refs_0_, ...), custom_call_target="tpu_custom_call" | custom-call | flops 10000000 | bytes 100000 | tf_op jit(solution)/shard_map/pallas_call | solution.py:458
  473.4 9.9 %all-to-all-start.9 = ((bf16[128,8,384]{2,1,0:T(8,128)(2,1)}), bf16[128,8,384]{2,1,0:T(8,128)(2,1)}, u32[]{:S(2)}, u32[]{:S(2)}) async-start(bf16[128,8,384]{2,1,0:T(8,128)(2,1)} %pad_maximum_fusion.5), calls=%async_computation.10 | async-start | bytes 1572864 | tf_op jit(solution)/shard_map/all_to_all | solution.py:498
  498.4 8.2 %collective-permute-done.30 = bf16[2,128,1024]{2,1,0:T(8,128)(2,1)S(1)} collective-permute-done((bf16[2,128,1024]{2,1,0:T(8,128)(2,1)}, bf16[2,128,1024]{2,1,0:T(8,128)(2,1)S(1)}, u32[]{:S(2)}, u32[]{:S(2)}) %collective-permute-start.30) | collective-permute-done | bytes 524320 | tf_op jit(solution)/shard_map/ppermute | solution.py:506
  506.6 11.9 %collective-permute-done.31 = bf16[2,128,1024]{2,1,0:T(8,128)(2,1)S(1)} collective-permute-done((bf16[2,128,1024]{2,1,0:T(8,128)(2,1)S(1)}, bf16[2,128,1024]{2,1,0:T(8,128)(2,1)S(1)}, u32[]{:S(2)}, u32[]{:S(2)}) %collective-permute-start.31) | collective-permute-done | bytes 524320 | tf_op jit(solution)/shard_map/ppermute | solution.py:506
  526.8 7.5 %all-to-all-start.10 = ((bf16[64,8,1024]{2,1,0:T(8,128)(2,1)}), bf16[64,8,1024]{2,1,0:T(8,128)(2,1)}, u32[]{:S(2)}, u32[]{:S(2)}) async-start(bf16[64,8,1024]{2,1,0:T(8,128)(2,1)} %fusion), calls=%async_computation.11 | async-start | bytes 2097152 | tf_op jit(solution)/shard_map/all_to_all | solution.py:498
  542.7 9.6 %collective-permute-done.36 = bf16[128,1024]{1,0:T(8,128)(2,1)} collective-permute-done((bf16[128,1024]{1,0:T(8,128)(2,1)}, bf16[128,1024]{1,0:T(8,128)(2,1)}, u32[]{:S(2)}, u32[]{:S(2)}) %collective-permute-start.36) | collective-permute-done | bytes 262176 | tf_op jit(solution)/shard_map/ppermute | solution.py:502
  564.1 4.9 collective-permute-done.40
  (455 shorter events, 217.3 us)
Async XLA Ops:
  7.2 204.9 %all-gather.3.cloned.1.call-start = ((), (), s32[]{:S(2)}) async-start(), calls=%async_computation.13 | async-start | bytes 10027008 | tf_op jit(solution)/shard_map/all_gather | solution.py:668
  24.3 32.4 %all-to-all-start = ((bf16[128,8,384]{2,1,0:T(8,128)(2,1)}), bf16[128,8,384]{2,1,0:T(8,128)(2,1)S(1)}, u32[]{:S(2)}, u32[]{:S(2)}) async-start(bf16[128,8,384]{2,1,0:T(8,128)(2,1)} %bitcast.6), calls=%async_computation | async-start | bytes 1572864 | tf_op jit(solution)/shard_map/all_to_all | solution.py:498
  36.6 47.8 %collective-permute-start.8 = (bf16[2,3,128,512]{3,2,1,0:T(8,128)(2,1)}, bf16[2,3,128,512]{3,2,1,0:T(8,128)(2,1)}, u32[]{:S(2)}, u32[]{:S(2)}) collective-permute-start(bf16[2,3,128,512]{3,2,1,0:T(8,128)(2,1)} %pad_maximum_fusion), channel_id=1, source_target_pairs={{0,16},{16,0},{1,17},{17,1},{2,18},{18,2},{3,19},{19,3},{4,20},{20... | collective-permute-start | bytes 2359304 | tf_op jit(solution)/shard_map/ppermute | solution.py:502
  38.2 38.7 %collective-permute-start.2 = (bf16[2,128,1024]{2,1,0:T(8,128)(2,1)S(1)}, bf16[2,128,1024]{2,1,0:T(8,128)(2,1)}, u32[]{:S(2)}, u32[]{:S(2)}) collective-permute-start(bf16[2,128,1024]{2,1,0:T(8,128)(2,1)S(1)} %pad_maximum_fusion.9.refs_0_), channel_id=1, source_target_pairs={{0,96},{32,0},{64,32},{96,64},{1,97},{33,1},{65,33},{97,65},{2,98}... | collective-permute-start | bytes 1572872 | tf_op jit(solution)/shard_map/ppermute | solution.py:506
  41.6 35.2 %collective-permute-start.3 = (bf16[2,128,1024]{2,1,0:T(8,128)(2,1)S(1)}, bf16[2,128,1024]{2,1,0:T(8,128)(2,1)}, u32[]{:S(2)}, u32[]{:S(2)}) collective-permute-start(bf16[2,128,1024]{2,1,0:T(8,128)(2,1)S(1)} %pad_maximum_fusion.9.refs_0_), channel_id=1, source_target_pairs={{0,64},{32,96},{64,0},{96,32},{1,65},{33,97},{65,1},{97,33},{2,66}... | collective-permute-start | bytes 1572872 | tf_op jit(solution)/shard_map/ppermute | solution.py:506
  42.0 40.2 %collective-permute-start.4 = (bf16[2,128,1024]{2,1,0:T(8,128)(2,1)S(1)}, bf16[2,128,1024]{2,1,0:T(8,128)(2,1)}, u32[]{:S(2)}, u32[]{:S(2)}) collective-permute-start(bf16[2,128,1024]{2,1,0:T(8,128)(2,1)S(1)} %pad_maximum_fusion.9.refs_0_), channel_id=1, source_target_pairs={{0,32},{32,64},{64,96},{96,0},{1,33},{33,65},{65,97},{97,1},{2,34}... | collective-permute-start | bytes 1572872 | tf_op jit(solution)/shard_map/ppermute | solution.py:506
  58.0 61.9 %all-to-all-start.1 = ((bf16[64,8,1024]{2,1,0:T(8,128)(2,1)}), bf16[64,8,1024]{2,1,0:T(8,128)(2,1)}, u32[]{:S(2)}, u32[]{:S(2)}) async-start(bf16[64,8,1024]{2,1,0:T(8,128)(2,1)} %broadcast_in_dim.32), calls=%async_computation.1 | async-start | bytes 2097152 | tf_op jit(solution)/shard_map/all_to_all | solution.py:498
  119.9 31.2 %collective-permute-start.11 = (bf16[64,8,1024]{2,1,0:T(8,128)(2,1)}, bf16[64,8,1024]{2,1,0:T(8,128)(2,1)}, u32[]{:S(2)}, u32[]{:S(2)}) collective-permute-start(bf16[64,8,1024]{2,1,0:T(8,128)(2,1)} %all-to-all-done.1), channel_id=1, source_target_pairs={{0,1},{1,0},{2,3},{3,2},{4,5},{5,4},{6,7},{7,6},{8,9},{9,8},{10,11... | collective-permute-start | bytes 3145736 | tf_op jit(solution)/shard_map/ppermute | solution.py:502
  158.9 43.2 %all-to-all-start.3 = ((bf16[8,128,1024]{2,1,0:T(8,128)(2,1)}), bf16[8,128,1024]{2,1,0:T(8,128)(2,1)}, u32[]{:S(2)}, u32[]{:S(2)}) async-start(bf16[8,128,1024]{2,1,0:T(8,128)(2,1)} %broadcast_in_dim.41), calls=%async_computation.3 | async-start | bytes 4194304 | tf_op jit(solution)/shard_map/all_to_all | solution.py:498
  169.5 26.0 %collective-permute-start.12 = (bf16[1,3,128,512]{3,2,1,0:T(8,128)(2,1)S(1)}, bf16[1,3,128,512]{3,2,1,0:T(8,128)(2,1)}, u32[]{:S(2)}, u32[]{:S(2)}) collective-permute-start(bf16[1,3,128,512]{3,2,1,0:T(8,128)(2,1)S(1)} %slice.356), channel_id=1, source_target_pairs={{0,32},{32,64},{64,96},{96,0},{1,33},{33,65},{65,97},{97,1},{2,34}... | collective-permute-start | bytes 1179656 | tf_op jit(solution)/shard_map/ppermute | solution.py:705
  203.6 49.5 %all-to-all-start.4 = ((bf16[8,128,1024]{2,1,0:T(8,128)(2,1)}), bf16[8,128,1024]{2,1,0:T(8,128)(2,1)}, u32[]{:S(2)}, u32[]{:S(2)}) async-start(bf16[8,128,1024]{2,1,0:T(8,128)(2,1)} %broadcast_in_dim.40), calls=%async_computation.4 | async-start | bytes 4194304 | tf_op jit(solution)/shard_map/all_to_all | solution.py:498
  262.2 48.1 %all-to-all-start.5 = ((bf16[8,128,1152]{2,1,0:T(8,128)(2,1)}), bf16[8,128,1152]{2,1,0:T(8,128)(2,1)}, u32[]{:S(2)}, u32[]{:S(2)}) async-start(bf16[8,128,1152]{2,1,0:T(8,128)(2,1)} %add_convert_fusion.1), calls=%async_computation.5 | async-start | bytes 4718592 | tf_op jit(solution)/shard_map/all_to_all | solution.py:498
  329.9 55.9 %all-to-all-start.7 = ((bf16[8,128,1152]{2,1,0:T(8,128)(2,1)}), bf16[8,128,1152]{2,1,0:T(8,128)(2,1)}, u32[]{:S(2)}, u32[]{:S(2)}) async-start(bf16[8,128,1152]{2,1,0:T(8,128)(2,1)} %add_convert_fusion), calls=%async_computation.8 | async-start | bytes 4718592 | tf_op jit(solution)/shard_map/all_to_all | solution.py:498
  337.6 234.7 %reduce-scatter.2.cloned.1.call-start = ((), (), s32[]{:S(2)}) async-start(), calls=%async_computation.12 | async-start | bytes 8912896 | tf_op jit(solution)/shard_map/reduce_scatter | solution.py:798
  351.4 34.3 %collective-permute-start.22 = (bf16[1,3,128,512]{3,2,1,0:T(8,128)(2,1)}, bf16[1,3,128,512]{3,2,1,0:T(8,128)(2,1)}, u32[]{:S(2)}, u32[]{:S(2)}) collective-permute-start(bf16[1,3,128,512]{3,2,1,0:T(8,128)(2,1)} %get-tuple-element.402), channel_id=1, source_target_pairs={{0,32},{32,64},{64,96},{96,0},{1,33},{33,65},{65,97},{97,1},{2,34}... | collective-permute-start | bytes 1179656 | tf_op jit(solution)/shard_map/ppermute | solution.py:539
  351.6 34.1 %collective-permute-start.23 = (bf16[1,3,128,512]{3,2,1,0:T(8,128)(2,1)}, bf16[1,3,128,512]{3,2,1,0:T(8,128)(2,1)}, u32[]{:S(2)}, u32[]{:S(2)}) collective-permute-start(bf16[1,3,128,512]{3,2,1,0:T(8,128)(2,1)} %get-tuple-element.401), channel_id=1, source_target_pairs={{0,96},{32,0},{64,32},{96,64},{1,97},{33,1},{65,33},{97,65},{2,98}... | collective-permute-start | bytes 1179656 | tf_op jit(solution)/shard_map/ppermute | solution.py:539
  382.2 28.3 %collective-permute-start.24 = (bf16[2,128,1024]{2,1,0:T(8,128)(2,1)}, bf16[2,128,1024]{2,1,0:T(8,128)(2,1)}, u32[]{:S(2)}, u32[]{:S(2)}) collective-permute-start(bf16[2,128,1024]{2,1,0:T(8,128)(2,1)} %get-tuple-element.229), channel_id=1, source_target_pairs={{0,32},{32,64},{64,96},{96,0},{1,33},{33,65},{65,97},{97,1},{2,34}... | collective-permute-start | bytes 1572872 | tf_op jit(solution)/shard_map/ppermute | solution.py:506
  382.2 28.3 %collective-permute-start.25 = (bf16[2,128,1024]{2,1,0:T(8,128)(2,1)}, bf16[2,128,1024]{2,1,0:T(8,128)(2,1)}, u32[]{:S(2)}, u32[]{:S(2)}) collective-permute-start(bf16[2,128,1024]{2,1,0:T(8,128)(2,1)} %get-tuple-element.230), channel_id=1, source_target_pairs={{0,64},{32,96},{64,0},{96,32},{1,65},{33,97},{65,1},{97,33},{2,66}... | collective-permute-start | bytes 1572872 | tf_op jit(solution)/shard_map/ppermute | solution.py:506
  383.7 28.4 %collective-permute-start.26 = (bf16[2,128,1024]{2,1,0:T(8,128)(2,1)}, bf16[2,128,1024]{2,1,0:T(8,128)(2,1)}, u32[]{:S(2)}, u32[]{:S(2)}) collective-permute-start(bf16[2,128,1024]{2,1,0:T(8,128)(2,1)} %get-tuple-element.231), channel_id=1, source_target_pairs={{0,96},{32,0},{64,32},{96,64},{1,97},{33,1},{65,33},{97,65},{2,98}... | collective-permute-start | bytes 1572872 | tf_op jit(solution)/shard_map/ppermute | solution.py:506
  394.4 55.8 %collective-permute-start.28 = (bf16[2,3,128,512]{3,2,1,0:T(8,128)(2,1)}, bf16[2,3,128,512]{3,2,1,0:T(8,128)(2,1)}, u32[]{:S(2)}, u32[]{:S(2)}) collective-permute-start(bf16[2,3,128,512]{3,2,1,0:T(8,128)(2,1)} %pad_maximum_fusion.4), channel_id=1, source_target_pairs={{0,96},{32,0},{64,32},{96,64},{1,97},{33,1},{65,33},{97,65},{2,98}... | collective-permute-start | bytes 2359304 | tf_op jit(solution)/shard_map/ppermute | solution.py:545
  395.3 31.9 %all-to-all-start.8 = ((bf16[8,128,128]{2,1,0:T(8,128)(2,1)}), bf16[8,128,128]{2,1,0:T(8,128)(2,1)S(1)}, u32[]{:S(2)}, u32[]{:S(2)}) async-start(bf16[8,128,128]{2,1,0:T(8,128)(2,1)} %bitcast.249), calls=%async_computation.9 | async-start | bytes 524288 | tf_op jit(solution)/shard_map/all_to_all | solution.py:498
  402.4 47.8 %collective-permute-start.27 = (bf16[2,3,128,512]{3,2,1,0:T(8,128)(2,1)}, bf16[2,3,128,512]{3,2,1,0:T(8,128)(2,1)}, u32[]{:S(2)}, u32[]{:S(2)}) collective-permute-start(bf16[2,3,128,512]{3,2,1,0:T(8,128)(2,1)} %pad_maximum_fusion.3), channel_id=1, source_target_pairs={{0,32},{32,64},{64,96},{96,0},{1,33},{33,65},{65,97},{97,1},{2,34}... | collective-permute-start | bytes 2359304 | tf_op jit(solution)/shard_map/ppermute | solution.py:544
  452.3 35.0 %collective-permute-start.39 = (bf16[3,128,512]{2,1,0:T(8,128)(2,1)}, bf16[3,128,512]{2,1,0:T(8,128)(2,1)}, u32[]{:S(2)}, u32[]{:S(2)}) collective-permute-start(bf16[3,128,512]{2,1,0:T(8,128)(2,1)} %fusion.21), channel_id=1, source_target_pairs={{0,16},{16,0},{1,17},{17,1},{2,18},{18,2},{3,19},{19,3},{4,20},{20... | collective-permute-start | bytes 1179656 | tf_op jit(solution)/shard_map/ppermute | solution.py:502
  463.7 33.1 %collective-permute-start.33 = (bf16[1,3,128,512]{3,2,1,0:T(8,128)(2,1)}, bf16[1,3,128,512]{3,2,1,0:T(8,128)(2,1)}, u32[]{:S(2)}, u32[]{:S(2)}) collective-permute-start(bf16[1,3,128,512]{3,2,1,0:T(8,128)(2,1)} %get-tuple-element.400), channel_id=1, source_target_pairs={{0,32},{32,64},{64,96},{96,0},{1,33},{33,65},{65,97},{97,1},{2,34}... | collective-permute-start | bytes 1179656 | tf_op jit(solution)/shard_map/ppermute | solution.py:539
  464.6 33.8 %collective-permute-start.34 = (bf16[1,3,128,512]{3,2,1,0:T(8,128)(2,1)}, bf16[1,3,128,512]{3,2,1,0:T(8,128)(2,1)}, u32[]{:S(2)}, u32[]{:S(2)}) collective-permute-start(bf16[1,3,128,512]{3,2,1,0:T(8,128)(2,1)} %get-tuple-element.399), channel_id=1, source_target_pairs={{0,96},{32,0},{64,32},{96,64},{1,97},{33,1},{65,33},{97,65},{2,98}... | collective-permute-start | bytes 1179656 | tf_op jit(solution)/shard_map/ppermute | solution.py:539
  473.4 45.9 %all-to-all-start.9 = ((bf16[128,8,384]{2,1,0:T(8,128)(2,1)}), bf16[128,8,384]{2,1,0:T(8,128)(2,1)}, u32[]{:S(2)}, u32[]{:S(2)}) async-start(bf16[128,8,384]{2,1,0:T(8,128)(2,1)} %pad_maximum_fusion.5), calls=%async_computation.10 | async-start | bytes 1572864 | tf_op jit(solution)/shard_map/all_to_all | solution.py:498
  487.3 31.2 %collective-permute-start.31 = (bf16[2,128,1024]{2,1,0:T(8,128)(2,1)S(1)}, bf16[2,128,1024]{2,1,0:T(8,128)(2,1)S(1)}, u32[]{:S(2)}, u32[]{:S(2)}) collective-permute-start(bf16[2,128,1024]{2,1,0:T(8,128)(2,1)S(1)} %copy-done.40), channel_id=1, source_target_pairs={{0,64},{32,96},{64,0},{96,32},{1,65},{33,97},{65,1},{97,33},{2,66}... | collective-permute-start | bytes 1572872 | tf_op jit(solution)/shard_map/ppermute | solution.py:506
  492.0 27.2 %collective-permute-start.32 = (bf16[2,128,1024]{2,1,0:T(8,128)(2,1)S(1)}, bf16[2,128,1024]{2,1,0:T(8,128)(2,1)}, u32[]{:S(2)}, u32[]{:S(2)}) collective-permute-start(bf16[2,128,1024]{2,1,0:T(8,128)(2,1)S(1)} %copy-done.38), channel_id=1, source_target_pairs={{0,96},{32,0},{64,32},{96,64},{1,97},{33,1},{65,33},{97,65},{2,98}... | collective-permute-start | bytes 1572872 | tf_op jit(solution)/shard_map/ppermute | solution.py:506
  496.8 45.9 %collective-permute-start.35 = (bf16[128,1024]{1,0:T(8,128)(2,1)}, bf16[128,1024]{1,0:T(8,128)(2,1)}, u32[]{:S(2)}, u32[]{:S(2)}) collective-permute-start(bf16[128,1024]{1,0:T(8,128)(2,1)} %fusion.23), channel_id=1, source_target_pairs={{0,16},{16,0},{1,17},{17,1},{2,18},{18,2},{3,19},{19,3},{4,20},{20... | collective-permute-start | bytes 786440 | tf_op jit(solution)/shard_map/ppermute | solution.py:502
  521.4 35.8 %collective-permute-start.38 = (bf16[2,3,128,512]{3,2,1,0:T(8,128)(2,1)}, bf16[2,3,128,512]{3,2,1,0:T(8,128)(2,1)}, u32[]{:S(2)}, u32[]{:S(2)}) collective-permute-start(bf16[2,3,128,512]{3,2,1,0:T(8,128)(2,1)} %pad_maximum_fusion.7), channel_id=1, source_target_pairs={{0,96},{32,0},{64,32},{96,64},{1,97},{33,1},{65,33},{97,65},{2,98}... | collective-permute-start | bytes 2359304 | tf_op jit(solution)/shard_map/ppermute | solution.py:545
  523.6 33.5 %collective-permute-start.37 = (bf16[2,3,128,512]{3,2,1,0:T(8,128)(2,1)}, bf16[2,3,128,512]{3,2,1,0:T(8,128)(2,1)}, u32[]{:S(2)}, u32[]{:S(2)}) collective-permute-start(bf16[2,3,128,512]{3,2,1,0:T(8,128)(2,1)} %pad_maximum_fusion.6), channel_id=1, source_target_pairs={{0,32},{32,64},{64,96},{96,0},{1,33},{33,65},{65,97},{97,1},{2,34}... | collective-permute-start | bytes 2359304 | tf_op jit(solution)/shard_map/ppermute | solution.py:544
  526.8 30.4 %all-to-all-start.10 = ((bf16[64,8,1024]{2,1,0:T(8,128)(2,1)}), bf16[64,8,1024]{2,1,0:T(8,128)(2,1)}, u32[]{:S(2)}, u32[]{:S(2)}) async-start(bf16[64,8,1024]{2,1,0:T(8,128)(2,1)} %fusion), calls=%async_computation.11 | async-start | bytes 2097152 | tf_op jit(solution)/shard_map/all_to_all | solution.py:498
  (132 other events, 1625.7 us)
Sparse Core Ops, SparseCore 0:
  22.2 97.8 all-gather.2
  342.7 103.6 reduce-scatter.1

commit v12 on v11

--- a/solution.py
+++ b/solution.py
@@ -709,9 +709,6 @@
     logits = jnp.where(chosen, mm(hidden_two, router), -1e30)
     gates_all = jnp.where(chosen, jax.nn.softmax(logits, axis=-1), 0.0)
 
-    def own_rows(v, m):
-        return v[m * tok : (m + 1) * tok]
-
     def experts_of(m, x_own, *moe):
         return run_experts(
             scalars,
@@ -728,35 +725,26 @@
     def back_sum(own, other):
         return add(own, flip(other, "core"))
 
-    def middle_back(m, back, before):
-        rows_middle, inv, gates = (own_rows(v, m) for v in (middle, inv_two, gates_all))
-        grad_top = own_rows(cot, m).astype(F32)
+    def middle_back(back):
         tail = back[:, width:]
         d_gates = tail[:, :experts] + tail[:, 64 : 64 + experts]
-        d_select = gates * (d_gates - jnp.sum(gates * d_gates, axis=-1, keepdims=True))
+        d_select = gates_all * (d_gates - jnp.sum(gates_all * d_gates, axis=-1, keepdims=True))
         d_logits = d_select.astype(BF)
         d_two = back[:, :width] + mm_t(d_logits, router)
         u = d_two * gain_mlp
         d_middle = (
-            grad_top
-            + inv * u
-            - rows_middle * (inv**3 * jnp.mean(u * rows_middle, axis=-1, keepdims=True))
+            cot.astype(F32)
+            + inv_two * u
+            - middle * (inv_two**3 * jnp.mean(u * middle, axis=-1, keepdims=True))
         )
         d_branch = d_middle.astype(BF)
         d_mixed = mm_t(d_branch, out_full).astype(BF)
-        d_mixed = d_mixed.reshape(tok, n_ctx, heads).transpose(1, 0, 2)
-        return d_middle, d_mixed, before + [(d_branch, d_logits, d_two)]
-
-    def weight_grads(saved_rows):
-        grad_out = grad_router = grad_mlp = 0.0
-        for m, (d_branch, d_logits, d_two) in enumerate(saved_rows):
-            rows_mixed, rows_middle, inv, hidden = (
-                own_rows(v, m) for v in (mixed, middle, inv_two, hidden_two)
-            )
-            grad_out = grad_out + t_mm(rows_mixed, d_branch)
-            grad_router = grad_router + t_mm(hidden, d_logits)
-            grad_mlp = grad_mlp + jnp.sum(d_two * rows_middle * inv, axis=0)
-        return grad_out, grad_router, grad_mlp
+        d_mixed = d_mixed.reshape(all_tok, n_ctx, heads).transpose(1, 0, 2)
+        return d_middle, d_mixed, (d_branch, d_logits, d_two)
+
+    def weight_grads(d_branch, d_logits, d_two):
+        grad_mlp = jnp.sum(d_two * middle * inv_two, axis=0)
+        return t_mm(mixed, d_branch), t_mm(hidden_two, d_logits), grad_mlp
 
     def pack_grads(grad_heads, grad_router, grad_attn, grad_mlp, grad_qk):
         grad_qk = jnp.pad(grad_qk[:, None], ((0, 0), (0, rows - 1))).reshape(-1)
@@ -775,16 +763,6 @@
             [grad_qk[0, :DH] + grad_qk[0, DH : 2 * DH], grad_qk[0, 2 * DH : 3 * DH]]
         )
         return d_hidden, (grad_heads, grad_attn[0], grad_qk)
-
-    def input_grad(m, d_hidden, d_middle):
-        start = tokens[m, 0].astype(F32)
-        inverse = lax.rsqrt(jnp.mean(start * start, axis=-1, keepdims=True) + EPS)
-        u = d_hidden * gain_attn
-        return (
-            d_middle
-            + inverse * u
-            - start * (inverse**3 * jnp.mean(u * start, axis=-1, keepdims=True))
-        )
 
     moe, back_own, back_other, *kept_0 = experts_of(0, x_0)
     x_1, back_own, back_other = lax.optimization_barrier((x_1, back_own, back_other))
@@ -797,48 +775,49 @@
     )
     moe = lax.psum_scatter(moe, FSDP, scatter_dimension=0, tiled=True)[0]
     back_1 = back_sum(back_own, back_other)
-    d_middle_0, d_mixed_0, d_branches = middle_back(0, sum_parts(back_0), [])
-    d_mixed_0 = exchange(d_mixed_0, CTX)
-    d_mixed_0, back_1 = lax.optimization_barrier((d_mixed_0, back_1))
+    kept_1[0], back_1 = lax.optimization_barrier((kept_1[0], back_1))
     back_1 = exchange(back_1, GROUP)
-    kept_1[0] = after_all(kept_1[0], d_mixed_0)
-    parts = [expert_grads(order, (kept_0, kept_1), 0)]
-    far = [relay(parts[0][2])]
-    d_hidden_0, head_grads_0 = attention_back(0, after_all(d_mixed_0, parts[0][0]))
+    parts = [expert_grads(order, (kept_0, kept_1), e) for e in range(local)]
+    far = [relay(part[2]) for part in parts]
+    back_1, parts, far[0] = lax.optimization_barrier((back_1, parts, far[0]))
+    d_middle, d_mixed, d_rows = middle_back(
+        jnp.concatenate([sum_parts(back_0), sum_parts(back_1)], axis=0)
+    )
+    d_mixed, far[0] = lax.optimization_barrier((d_mixed, far[0]))
+    d_mixed = exchange(d_mixed, CTX)
+    moved = [ring_sums(parts[0], far[0])]
+    d_mixed, far[1], moved[0] = lax.optimization_barrier((d_mixed, far[1], moved[0]))
+    moved.append(ring_sums(parts[1], far[1]))
+    d_mixed = d_mixed.reshape(n_ctx, micro, tok, heads)
+    d_hidden_0, head_grads_0 = attention_back(0, d_mixed[:, 0])
+    d_hidden_0, d_mixed, moved[1] = lax.optimization_barrier((d_hidden_0, d_mixed, moved[1]))
     hidden_moved_0 = by_z(d_hidden_0)
-    back_1, d_hidden_0[0], far[0] = lax.optimization_barrier((back_1, d_hidden_0[0], far[0]))
-    d_middle_1, d_mixed_1, d_branches = middle_back(1, sum_parts(back_1), d_branches)
-    far[0], d_mixed_1 = lax.optimization_barrier((far[0], d_mixed_1))
-    d_mixed_1 = exchange(d_mixed_1, CTX)
-    moved = [ring_sums(parts[0], far[0])]
-    d_mixed_1, hidden_moved_0 = lax.optimization_barrier((d_mixed_1, hidden_moved_0))
-    d_hidden_1, head_grads_1 = attention_back(1, d_mixed_1)
-    d_hidden_1, d_branches, hidden_moved_0, moved[0], kept_1 = lax.optimization_barrier(
-        (d_hidden_1, d_branches, hidden_moved_0, moved[0], kept_1)
+    d_hidden_1, head_grads_1 = attention_back(1, d_mixed[:, 1])
+    d_hidden_1, d_rows, parts, moved = lax.optimization_barrier(
+        (d_hidden_1, d_rows, parts, moved)
     )
     hidden_moved_1 = by_z(d_hidden_1)
     grad_heads, grad_attn, grad_qk = jax.tree.map(jnp.add, head_grads_0, head_grads_1)
-    grad_out, grad_router, grad_mlp = weight_grads(d_branches)
+    grad_out, grad_router, grad_mlp = weight_grads(*d_rows)
     grad_pack = pack_grads(grad_heads, grad_router, grad_attn, grad_mlp, grad_qk)
     grad_pack = exchange(grad_pack, ALL)
-    parts.append(expert_grads(order, (kept_0, kept_1), 1))
-    far.append(relay(parts[1][2]))
     grad_out = grad_out.astype(BF).reshape(n_all // 2, 2, rows, width)
     grad_own = lax.dynamic_index_in_dim(grad_out, core, axis=1, keepdims=False)
     grad_other = lax.dynamic_index_in_dim(grad_out, 1 - core, axis=1, keepdims=False)
     grad_out = back_sum(grad_own, grad_other)
-    grad_pack, grad_out, hidden_moved_1, far[1] = lax.optimization_barrier(
-        (grad_pack, grad_out, hidden_moved_1, far[1])
+    weight_sums = [pair_sums(p, q) for p, q in zip(parts, moved)]
+    weight_yl = [flip(sums[1].astype(BF), "yl") for sums in weight_sums]
+    grad_pack, grad_out, hidden_moved_0, hidden_moved_1, weight_yl = lax.optimization_barrier(
+        (grad_pack, grad_out, hidden_moved_0, hidden_moved_1, weight_yl)
     )
     exchange.last = grad_pack
     grad_out = exchange(grad_out, CTX + GROUP)
-    moved.append(ring_sums(parts[1], far[1]))
-    hidden_sums = pair_sums(d_hidden_0, hidden_moved_0)
-    d_hidden_0 = hidden_sums[0] + flip(hidden_sums[1].astype(BF), "yl").astype(F32)
-    grad_out, moved[1] = lax.optimization_barrier((grad_out, moved[1]))
-    weight_sums = [pair_sums(p, q) for p, q in zip(parts, moved)]
-    weight_yl = [flip(sums[1].astype(BF), "yl") for sums in weight_sums]
-    hidden_sums = pair_sums(d_hidden_1, hidden_moved_1)
+    hidden_sums = [
+        jnp.stack(sums)
+        for sums in zip(
+            pair_sums(d_hidden_0, hidden_moved_0), pair_sums(d_hidden_1, hidden_moved_1)
+        )
+    ]
     hidden_yl = flip(hidden_sums[1].astype(BF), "yl")
 
     grad_pack = grad_pack.astype(F32)
@@ -847,17 +826,21 @@
     own_small = jnp.sum(grad_pack[:, :, span:], axis=0)
     own_out = sum_parts(grad_out)
     moe = after_all(moe, grad_pack)
-    d_hidden_1 = hidden_sums[0] + hidden_yl.astype(F32)
+    d_hidden = (hidden_sums[0] + hidden_yl.astype(F32)).reshape(all_tok, width)
     expert_own = [sums[0] + other.astype(F32) for sums, other in zip(weight_sums, weight_yl)]
     out = (middle.reshape(moe.shape) + moe.astype(F32)).astype(BF)
-    d_inputs = [
-        input_grad(0, d_hidden_0, d_middle_0),
-        input_grad(1, d_hidden_1, d_middle_1),
-    ]
+    start = tokens.reshape(all_tok, width).astype(F32)
+    inv_one = lax.rsqrt(jnp.mean(start * start, axis=-1, keepdims=True) + EPS)
+    u = d_hidden * gain_attn
+    d_input = (
+        d_middle
+        + inv_one * u
+        - start * (inv_one**3 * jnp.mean(u * start, axis=-1, keepdims=True))
+    )
 
     return (
         out[:, None],
-        jnp.stack(d_inputs)[:, None],
+        d_input.reshape(tokens.shape),
         own_heads[:, :, :heads].reshape(rows, -1),
         own_heads[:, :, heads : heads + DH].reshape(rows, -1),
         own_heads[:, :, heads + DH :].reshape(rows, -1),

time: 589 us -> 588 us (level)
  waiting for transfers between devices: 156 us -> 175 us
  local copies, waits for them, and re-layouts: 69 us -> 53.3 us
    ppermute x4, waiting for transfers between devices: 0.01 us -> 23.4 us  [relay(): return [lax.ppermute(far[:1], 'z', UP), lax.ppermute(far[1:], 'z', DOWN)]]
    all_to_all x11 -> x10, waiting for transfers between devices: 32.8 us -> 14.5 us  [swap(): return lax.all_to_all(parts, axis, split_axis=0, concat_axis=0, tiled=True)]
    ppermute x12, waiting for transfers between devices: 50.7 us -> 66.3 us  [by_z(): lax.ppermute(parts[k], 'z', perm)]
    unnamed x223 -> x176, local copies, waits for them, and re-layouts: 32.6 us -> 20.8 us
    all_to_all x11 -> x10, starting transfers between devices: 74.3 us -> 71.3 us  [swap(): return lax.all_to_all(parts, axis, split_axis=0, concat_axis=0, tiled=True)]
    ppermute x13 -> x12, waiting for transfers between devices: 27.5 us -> 25.5 us  [flip(): return lax.ppermute(block, axis, FLIP)]
  transfers between devices with their start and end apart: 54 -> 52, of which waited for: 21 -> 22; matrix products, arithmetic and copies ran while one was open for 18% -> 17% of each run, Pallas kernels for 25% -> 25%
where the time goes in v12:
time: 588 us; the launch traced here: 580 us
  waiting for transfers between devices  175 us (30%)
  Pallas kernels  143 us (24%)
  starting transfers between devices  119 us (20%)
  other arithmetic  67.4 us (11%)
  local copies, waits for them, and re-layouts  53.3 us (9%)
  between operations  16.4 us (3%)
  matrix products  6 us (1%)
    pallas_call x2, Pallas kernels, run_experts(): pl.pallas_call(functools.partial(expert_kernel, again=moe is not None), o...  80.7 us
    all_to_all x10, starting transfers between devices, swap(): return lax.all_to_all(parts, axis, split_axis=0, concat_axis=0, tiled=True)  71.3 us
    ppermute x12, waiting for transfers between devices, by_z(): lax.ppermute(parts[k], 'z', perm)  66.3 us
    ppermute x4, waiting for transfers between devices, body(): last = [lax.ppermute(block, 'z', UP), lax.ppermute(block, 'z', DOWN)]  33.2 us
    ppermute x12, waiting for transfers between devices, flip(): return lax.ppermute(block, axis, FLIP)  25.5 us
    pallas_call x2, Pallas kernels, attend_backward(): pl.pallas_call(attend_back_kernel, out_shape=outs, grid=(1,), in_specs=[p...  24.6 us
    ppermute x4, waiting for transfers between devices, relay(): return [lax.ppermute(far[:1], 'z', UP), lax.ppermute(far[1:], 'z', DOWN)]  23.4 us
    unnamed x176, local copies, waits for them, and re-layouts  20.8 us
  transfers between devices with their start and end apart: 52, of which 22 were waited for; matrix products, arithmetic and copies ran while one was open for 17% of the time, Pallas kernels for 25%

profile of v12, /device:TPU:0, one launch (start us, length us, event | category | flops | bytes accessed | tf_op | source)
XLA Modules:
  0.0 580.3 jit_solution(7158385640595033591)
XLA Ops:
  24.3 11.2 %all-to-all-start = ((bf16[128,8,384]{2,1,0:T(8,128)(2,1)}), bf16[128,8,384]{2,1,0:T(8,128)(2,1)S(1)}, u32[]{:S(2)}, u32[]{:S(2)}) async-start(bf16[128,8,384]{2,1,0:T(8,128)(2,1)} %bitcast.7), calls=%async_computation | async-start | bytes 1572864 | tf_op jit(solution)/shard_map/all_to_all | solution.py:498
  43.0 13.7 %all-to-all-done = bf16[128,8,384]{2,1,0:T(8,128)(2,1)S(1)} async-done(((bf16[128,8,384]{2,1,0:T(8,128)(2,1)}), bf16[128,8,384]{2,1,0:T(8,128)(2,1)S(1)}, u32[]{:S(2)}, u32[]{:S(2)}) %all-to-all-start) | async-done | bytes 786464 | tf_op jit(solution)/shard_map/all_to_all | solution.py:498
  58.0 5.5 all-to-all-start.1
  66.8 9.9 %collective-permute-done.2.refs_1_ = bf16[2,128,1024]{2,1,0:T(8,128)(2,1)} collective-permute-done((bf16[2,128,1024]{2,1,0:T(8,128)(2,1)S(1)}, bf16[2,128,1024]{2,1,0:T(8,128)(2,1)}, u32[]{:S(2)}, u32[]{:S(2)}) %collective-permute-start.2) | collective-permute-done | bytes 524320 | tf_op jit(solution)/shard_map/ppermute | solution.py:506
  76.7 5.4 collective-permute-done.4.refs_3_
  89.0 8.8 %shard_map.246 = (bf16[1024,128]{1,0:T(8,128)(2,1)S(1)}, bf16[1024,1024]{1,0:T(8,128)(2,1)S(1)}, bf16[1024,128]{1,0:T(8,128)(2,1)S(1)}, bf16[1024,128]{1,0:T(8,128)(2,1)S(1)}) custom-call(s32[8]{0:T(128)S(1)} %fusion.29.order_ref, bf16[2,128,1024]{2,1,0:T(8,128)(2,1)S(1)} %copy-done.6, bf16[2,128,1024]{2,1,0:T(8,128)(2,1)} %collective-permute-done.2.refs_1_, ...), custom_call_target="tpu_custom_call" | custom-call | flops 10000000 | bytes 100000 | tf_op jit(solution)/shard_map/pallas_call | solution.py:229
  101.3 6.5 %collective-permute-done.7.refs_3_ = bf16[2,128,1024]{2,1,0:T(8,128)(2,1)} collective-permute-done((bf16[2,128,1024]{2,1,0:T(8,128)(2,1)S(1)}, bf16[2,128,1024]{2,1,0:T(8,128)(2,1)}, u32[]{:S(2)}, u32[]{:S(2)}) %collective-permute-start.7) | collective-permute-done | bytes 524320 | tf_op jit(solution)/shard_map/ppermute | solution.py:506
  107.8 9.0 %shard_map.247 = (bf16[1024,128]{1,0:T(8,128)(2,1)S(1)}, bf16[1024,1024]{1,0:T(8,128)(2,1)S(1)}, bf16[1024,128]{1,0:T(8,128)(2,1)S(1)}, bf16[1024,128]{1,0:T(8,128)(2,1)S(1)}) custom-call(s32[8]{0:T(128)S(1)} %fusion.29.order_ref, bf16[2,128,1024]{2,1,0:T(8,128)(2,1)S(1)} %pad_maximum_fusion.8.refs_0_, bf16[2,128,1024]{2,1,0:T(8,128)(2,1)} %collective-permute-done.5.refs_1_, ...), custom_call_target="tpu_custom_call" | custom-call | flops 10000000 | bytes 100000 | tf_op jit(solution)/shard_map/pallas_call | solution.py:229
  130.0 16.3 %collective-permute-done.10.refs_5_ = bf16[2,3,128,512]{3,2,1,0:T(8,128)(2,1)} collective-permute-done((bf16[2,3,128,512]{3,2,1,0:T(8,128)(2,1)}, bf16[2,3,128,512]{3,2,1,0:T(8,128)(2,1)}, u32[]{:S(2)}, u32[]{:S(2)}) %collective-permute-start.10) | collective-permute-done | bytes 786464 | tf_op jit(solution)/shard_map/ppermute | solution.py:656
  160.7 6.2 %all-to-all-start.3 = ((bf16[8,128,1024]{2,1,0:T(8,128)(2,1)}), bf16[8,128,1024]{2,1,0:T(8,128)(2,1)}, u32[]{:S(2)}, u32[]{:S(2)}) async-start(bf16[8,128,1024]{2,1,0:T(8,128)(2,1)} %broadcast_in_dim.42), calls=%async_computation.3 | async-start | bytes 4194304 | tf_op jit(solution)/shard_map/all_to_all | solution.py:498
  175.7 13.0 %collective-permute-done.15.refs_13_ = bf16[2,3,128,512]{3,2,1,0:T(8,128)(2,1)S(1)} collective-permute-done((bf16[2,3,128,512]{3,2,1,0:T(8,128)(2,1)S(1)}, bf16[2,3,128,512]{3,2,1,0:T(8,128)(2,1)S(1)}, u32[]{:S(2)}, u32[]{:S(2)}) %collective-permute-start.15) | collective-permute-done | bytes 786464 | tf_op jit(solution)/shard_map/ppermute | solution.py:656
  197.3 6.5 %collective-permute-done.16.refs_11_ = bf16[1,3,128,512]{3,2,1,0:T(8,128)(2,1)} collective-permute-done((bf16[1,3,128,512]{3,2,1,0:T(8,128)(2,1)S(1)}, bf16[1,3,128,512]{3,2,1,0:T(8,128)(2,1)}, u32[]{:S(2)}, u32[]{:S(2)}) %collective-permute-start.16) | collective-permute-done | bytes 393248 | tf_op jit(solution)/shard_map/ppermute | solution.py:705
  206.3 6.9 %all-to-all-start.4 = ((bf16[8,128,1024]{2,1,0:T(8,128)(2,1)}), bf16[8,128,1024]{2,1,0:T(8,128)(2,1)}, u32[]{:S(2)}, u32[]{:S(2)}) async-start(bf16[8,128,1024]{2,1,0:T(8,128)(2,1)} %broadcast_in_dim.41), calls=%async_computation.4 | async-start | bytes 4194304 | tf_op jit(solution)/shard_map/all_to_all | solution.py:498
  215.6 40.4 %shard_map.248 = (bf16[16,2,128,1024]{3,2,1,0:T(8,128)(2,1)}, bf16[8,128,1152]{2,1,0:T(8,128)(2,1)}, bf16[8,128,1152]{2,1,0:T(8,128)(2,1)}, bf16[2,768,1024]{2,1...) custom-call(s32[10]{0:T(128)} %pad_add_fusion.scalar_ref, ...), custom_call_target="tpu_custom_call" | custom-call | flops 10000000 | bytes 100000 | tf_op jit(solution)/shard_map/pallas_call | solution.py:412
  256.4 4.5 collective-permute-done.19
  264.8 7.1 %all-to-all-start.5 = ((bf16[8,128,1152]{2,1,0:T(8,128)(2,1)}), bf16[8,128,1152]{2,1,0:T(8,128)(2,1)}, u32[]{:S(2)}, u32[]{:S(2)}) async-start(bf16[8,128,1152]{2,1,0:T(8,128)(2,1)} %add_convert_fusion.1), calls=%async_computation.5 | async-start | bytes 4718592 | tf_op jit(solution)/shard_map/all_to_all | solution.py:498
  271.9 40.3 %shard_map.249 = (bf16[16,2,128,1024]{3,2,1,0:T(8,128)(2,1)}, bf16[8,128,1152]{2,1,0:T(8,128)(2,1)}, bf16[8,128,1152]{2,1,0:T(8,128)(2,1)}, bf16[2,768,1024]{2,1...) custom-call(s32[10]{0:T(128)} %pad_add_fusion.scalar_ref, ...), custom_call_target="tpu_custom_call", output_to_operand_aliasing={{0}: (15, {})} | custom-call | flops 10000000 | bytes 100000 | tf_op jit(solution)/shard_map/pallas_call | solution.py:412
  312.4 4.7 collective-permute-done.21
  320.8 7.4 %all-to-all-start.6 = ((bf16[8,128,1152]{2,1,0:T(8,128)(2,1)}), bf16[8,128,1152]{2,1,0:T(8,128)(2,1)}, u32[]{:S(2)}, u32[]{:S(2)}) async-start(bf16[8,128,1152]{2,1,0:T(8,128)(2,1)} %add_convert_fusion), calls=%async_computation.7 | async-start | bytes 4718592 | tf_op jit(solution)/shard_map/all_to_all | solution.py:498
  328.2 10.2 %shard_map.250 = (bf16[2,3,128,512]{3,2,1,0:T(8,128)(2,1)S(1)}, bf16[2,3,128,512]{3,2,1,0:T(8,128)(2,1)S(1)}, bf16[2,3,128,512]{3,2,1,0:T(8,128)(2,1)S(1)}, bf16[2,3,128,512]{3,2,1,0:T(8,128)(2,1)S(1)}) custom-call(s32[8]{0:T(128)S(1)} %fusion.29.order_ref, bf16[2,768,1024]{2,1,0:T(8,128)(2,1)} %get-tuple-element.207.refs_0_, ...), custom_call_target="tpu_custom_call" | custom-call | flops 10000000 | bytes 100000 | tf_op jit(solution)/shard_map/pallas_call | solution.py:458
  350.2 10.1 %shard_map.251 = (bf16[2,3,128,512]{3,2,1,0:T(8,128)(2,1)S(1)}, bf16[2,3,128,512]{3,2,1,0:T(8,128)(2,1)S(1)}, bf16[2,3,128,512]{3,2,1,0:T(8,128)(2,1)S(1)}, bf16[2,3,128,512]{3,2,1,0:T(8,128)(2,1)S(1)}) custom-call(s32[8]{0:T(128)S(1)} %fusion.29.order_ref, bf16[2,768,1024]{2,1,0:T(8,128)(2,1)} %get-tuple-element.207.refs_0_, ...), custom_call_target="tpu_custom_call" | custom-call | flops 10000000 | bytes 100000 | tf_op jit(solution)/shard_map/pallas_call | solution.py:458
  378.3 4.3 all-to-all-start.7
  388.7 23.4 %collective-permute-done.24 = bf16[1,3,128,512]{3,2,1,0:T(8,128)(2,1)S(1)} collective-permute-done((bf16[1,3,128,512]{3,2,1,0:T(8,128)(2,1)S(1)}, bf16[1,3,128,512]{3,2,1,0:T(8,128)(2,1)S(1)}, u32[]{:S(2)}, u32[]{:S(2)}) %collective-permute-start.24) | collective-permute-done | bytes 393248 | tf_op jit(solution)/shard_map/ppermute | solution.py:539
  423.8 12.0 %shard_map.252 = (bf16[2,128,1024]{2,1,0:T(8,128)(2,1)S(1)}, bf16[2,128,1024]{2,1,0:T(8,128)(2,1)}, bf16[2,128,1024]{2,1,0:T(8,128)(2,1)S(1)}, bf16[2,128,1024]{...) custom-call(s32[8]{0:T(128)S(1)} %fusion.29.order_ref, ...), custom_call_target="tpu_custom_call" | custom-call | flops 10000000 | bytes 100000 | tf_op jit(solution)/shard_map/pallas_call | solution.py:252
  438.4 12.6 %shard_map.253 = (bf16[2,128,1024]{2,1,0:T(8,128)(2,1)S(1)}, bf16[2,128,1024]{2,1,0:T(8,128)(2,1)}, bf16[2,128,1024]{2,1,0:T(8,128)(2,1)}, bf16[2,128,1024]{2,1,...) custom-call(s32[8]{0:T(128)S(1)} %fusion.29.order_ref, ...), custom_call_target="tpu_custom_call" | custom-call | flops 10000000 | bytes 100000 | tf_op jit(solution)/shard_map/pallas_call | solution.py:252
  464.6 9.3 %all-to-all-start.8 = ((bf16[128,8,384]{2,1,0:T(8,128)(2,1)}), bf16[128,8,384]{2,1,0:T(8,128)(2,1)}, u32[]{:S(2)}, u32[]{:S(2)}) async-start(bf16[128,8,384]{2,1,0:T(8,128)(2,1)} %pad_maximum_fusion.7), calls=%async_computation.9 | async-start | bytes 1572864 | tf_op jit(solution)/shard_map/all_to_all | solution.py:498
  485.5 12.5 %collective-permute-done.35 = bf16[2,128,1024]{2,1,0:T(8,128)(2,1)} collective-permute-done((bf16[2,128,1024]{2,1,0:T(8,128)(2,1)}, bf16[2,128,1024]{2,1,0:T(8,128)(2,1)}, u32[]{:S(2)}, u32[]{:S(2)}) %collective-permute-start.35) | collective-permute-done | bytes 524320 | tf_op jit(solution)/shard_map/ppermute | solution.py:506
  498.0 9.7 %collective-permute-done.36 = bf16[2,128,1024]{2,1,0:T(8,128)(2,1)} collective-permute-done((bf16[2,128,1024]{2,1,0:T(8,128)(2,1)}, bf16[2,128,1024]{2,1,0:T(8,128)(2,1)}, u32[]{:S(2)}, u32[]{:S(2)}) %collective-permute-start.36) | collective-permute-done | bytes 524320 | tf_op jit(solution)/shard_map/ppermute | solution.py:506
  509.2 10.6 %collective-permute-done.32 = bf16[2,128,1024]{2,1,0:T(8,128)(2,1)} collective-permute-done((bf16[2,128,1024]{2,1,0:T(8,128)(2,1)S(1)}, bf16[2,128,1024]{2,1,0:T(8,128)(2,1)}, u32[]{:S(2)}, u32[]{:S(2)}) %collective-permute-start.32) | collective-permute-done | bytes 524320 | tf_op jit(solution)/shard_map/ppermute | solution.py:506
  519.8 10.3 %collective-permute-done.33 = bf16[2,128,1024]{2,1,0:T(8,128)(2,1)} collective-permute-done((bf16[2,128,1024]{2,1,0:T(8,128)(2,1)S(1)}, bf16[2,128,1024]{2,1,0:T(8,128)(2,1)}, u32[]{:S(2)}, u32[]{:S(2)}) %collective-permute-start.33) | collective-permute-done | bytes 524320 | tf_op jit(solution)/shard_map/ppermute | solution.py:506
  532.4 9.2 %all-to-all-start.9 = ((bf16[64,8,1024]{2,1,0:T(8,128)(2,1)}), bf16[64,8,1024]{2,1,0:T(8,128)(2,1)}, u32[]{:S(2)}, u32[]{:S(2)}) async-start(bf16[64,8,1024]{2,1,0:T(8,128)(2,1)} %fusion), calls=%async_computation.10 | async-start | bytes 2097152 | tf_op jit(solution)/shard_map/all_to_all | solution.py:498
  558.1 8.0 %collective-permute-done.39 = bf16[2,128,1024]{2,1,0:T(8,128)(2,1)} collective-permute-done((bf16[2,128,1024]{2,1,0:T(8,128)(2,1)}, bf16[2,128,1024]{2,1,0:T(8,128)(2,1)}, u32[]{:S(2)}, u32[]{:S(2)}) %collective-permute-start.39) | collective-permute-done | bytes 524320 | tf_op jit(solution)/shard_map/ppermute | solution.py:502
  (394 shorter events, 198.6 us)
Async XLA Ops:
  7.2 208.4 %all-gather.3.cloned.1.call-start = ((), (), s32[]{:S(2)}) async-start(), calls=%async_computation.12 | async-start | bytes 10027008 | tf_op jit(solution)/shard_map/all_gather | solution.py:668
  24.3 32.4 %all-to-all-start = ((bf16[128,8,384]{2,1,0:T(8,128)(2,1)}), bf16[128,8,384]{2,1,0:T(8,128)(2,1)S(1)}, u32[]{:S(2)}, u32[]{:S(2)}) async-start(bf16[128,8,384]{2,1,0:T(8,128)(2,1)} %bitcast.7), calls=%async_computation | async-start | bytes 1572864 | tf_op jit(solution)/shard_map/all_to_all | solution.py:498
  36.5 48.1 %collective-permute-start.8 = (bf16[2,3,128,512]{3,2,1,0:T(8,128)(2,1)}, bf16[2,3,128,512]{3,2,1,0:T(8,128)(2,1)}, u32[]{:S(2)}, u32[]{:S(2)}) collective-permute-start(bf16[2,3,128,512]{3,2,1,0:T(8,128)(2,1)} %pad_maximum_fusion), channel_id=1, source_target_pairs={{0,16},{16,0},{1,17},{17,1},{2,18},{18,2},{3,19},{19,3},{4,20},{20... | collective-permute-start | bytes 2359304 | tf_op jit(solution)/shard_map/ppermute | solution.py:502
  38.1 38.7 %collective-permute-start.2 = (bf16[2,128,1024]{2,1,0:T(8,128)(2,1)S(1)}, bf16[2,128,1024]{2,1,0:T(8,128)(2,1)}, u32[]{:S(2)}, u32[]{:S(2)}) collective-permute-start(bf16[2,128,1024]{2,1,0:T(8,128)(2,1)S(1)} %pad_maximum_fusion.9.refs_0_), channel_id=1, source_target_pairs={{0,96},{32,0},{64,32},{96,64},{1,97},{33,1},{65,33},{97,65},{2,98}... | collective-permute-start | bytes 1572872 | tf_op jit(solution)/shard_map/ppermute | solution.py:506
  41.5 35.2 %collective-permute-start.3 = (bf16[2,128,1024]{2,1,0:T(8,128)(2,1)S(1)}, bf16[2,128,1024]{2,1,0:T(8,128)(2,1)}, u32[]{:S(2)}, u32[]{:S(2)}) collective-permute-start(bf16[2,128,1024]{2,1,0:T(8,128)(2,1)S(1)} %pad_maximum_fusion.9.refs_0_), channel_id=1, source_target_pairs={{0,64},{32,96},{64,0},{96,32},{1,65},{33,97},{65,1},{97,33},{2,66}... | collective-permute-start | bytes 1572872 | tf_op jit(solution)/shard_map/ppermute | solution.py:506
  41.8 40.3 %collective-permute-start.4 = (bf16[2,128,1024]{2,1,0:T(8,128)(2,1)S(1)}, bf16[2,128,1024]{2,1,0:T(8,128)(2,1)}, u32[]{:S(2)}, u32[]{:S(2)}) collective-permute-start(bf16[2,128,1024]{2,1,0:T(8,128)(2,1)S(1)} %pad_maximum_fusion.9.refs_0_), channel_id=1, source_target_pairs={{0,32},{32,64},{64,96},{96,0},{1,33},{33,65},{65,97},{97,1},{2,34}... | collective-permute-start | bytes 1572872 | tf_op jit(solution)/shard_map/ppermute | solution.py:506
  58.0 60.8 %all-to-all-start.1 = ((bf16[64,8,1024]{2,1,0:T(8,128)(2,1)}), bf16[64,8,1024]{2,1,0:T(8,128)(2,1)}, u32[]{:S(2)}, u32[]{:S(2)}) async-start(bf16[64,8,1024]{2,1,0:T(8,128)(2,1)} %broadcast_in_dim.33), calls=%async_computation.1 | async-start | bytes 2097152 | tf_op jit(solution)/shard_map/all_to_all | solution.py:498
  83.5 24.2 %collective-permute-start.7 = (bf16[2,128,1024]{2,1,0:T(8,128)(2,1)S(1)}, bf16[2,128,1024]{2,1,0:T(8,128)(2,1)}, u32[]{:S(2)}, u32[]{:S(2)}) collective-permute-start(bf16[2,128,1024]{2,1,0:T(8,128)(2,1)S(1)} %pad_maximum_fusion.8.refs_0_), channel_id=1, source_target_pairs={{0,32},{32,64},{64,96},{96,0},{1,33},{33,65},{65,97},{97,1},{2,34}... | collective-permute-start | bytes 1572872 | tf_op jit(solution)/shard_map/ppermute | solution.py:506
  118.8 33.4 %collective-permute-start.11 = (bf16[64,8,1024]{2,1,0:T(8,128)(2,1)}, bf16[64,8,1024]{2,1,0:T(8,128)(2,1)}, u32[]{:S(2)}, u32[]{:S(2)}) collective-permute-start(bf16[64,8,1024]{2,1,0:T(8,128)(2,1)} %all-to-all-done.1), channel_id=1, source_target_pairs={{0,1},{1,0},{2,3},{3,2},{4,5},{5,4},{6,7},{7,6},{8,9},{9,8},{10,11... | collective-permute-start | bytes 3145736 | tf_op jit(solution)/shard_map/ppermute | solution.py:502
  122.9 23.5 %collective-permute-start.10 = (bf16[2,3,128,512]{3,2,1,0:T(8,128)(2,1)}, bf16[2,3,128,512]{3,2,1,0:T(8,128)(2,1)}, u32[]{:S(2)}, u32[]{:S(2)}) collective-permute-start(bf16[2,3,128,512]{3,2,1,0:T(8,128)(2,1)} %pad_maximum_fusion.1.refs_4_), channel_id=1, source_target_pairs={{0,96},{32,0},{64,32},{96,64},{1,97},{33,1},{65,33},{97,65},{2,98}... | collective-permute-start | bytes 2359304 | tf_op jit(solution)/shard_map/ppermute | solution.py:656
  124.2 26.0 %collective-permute-start.9 = (bf16[2,3,128,512]{3,2,1,0:T(8,128)(2,1)}, bf16[2,3,128,512]{3,2,1,0:T(8,128)(2,1)}, u32[]{:S(2)}, u32[]{:S(2)}) collective-permute-start(bf16[2,3,128,512]{3,2,1,0:T(8,128)(2,1)} %pad_maximum_fusion.1.refs_4_), channel_id=1, source_target_pairs={{0,32},{32,64},{64,96},{96,0},{1,33},{33,65},{65,97},{97,1},{2,34}... | collective-permute-start | bytes 2359304 | tf_op jit(solution)/shard_map/ppermute | solution.py:656
  125.8 25.2 %all-to-all-start.2 = ((bf16[8,256,128]{2,1,0:T(8,128)(2,1)}), bf16[8,256,128]{2,1,0:T(8,128)(2,1)}, u32[]{:S(2)}, u32[]{:S(2)}) async-start(bf16[8,256,128]{2,1,0:T(8,128)(2,1)} %bitcast.190), calls=%async_computation.2 | async-start | bytes 1048576 | tf_op jit(solution)/shard_map/all_to_all | solution.py:498
  160.7 43.1 %all-to-all-start.3 = ((bf16[8,128,1024]{2,1,0:T(8,128)(2,1)}), bf16[8,128,1024]{2,1,0:T(8,128)(2,1)}, u32[]{:S(2)}, u32[]{:S(2)}) async-start(bf16[8,128,1024]{2,1,0:T(8,128)(2,1)} %broadcast_in_dim.42), calls=%async_computation.3 | async-start | bytes 4194304 | tf_op jit(solution)/shard_map/all_to_all | solution.py:498
  171.3 26.0 %collective-permute-start.12 = (bf16[1,3,128,512]{3,2,1,0:T(8,128)(2,1)S(1)}, bf16[1,3,128,512]{3,2,1,0:T(8,128)(2,1)}, u32[]{:S(2)}, u32[]{:S(2)}) collective-permute-start(bf16[1,3,128,512]{3,2,1,0:T(8,128)(2,1)S(1)} %slice.298), channel_id=1, source_target_pairs={{0,32},{32,64},{64,96},{96,0},{1,33},{33,65},{65,97},{97,1},{2,34}... | collective-permute-start | bytes 1179656 | tf_op jit(solution)/shard_map/ppermute | solution.py:705
  172.4 24.9 %collective-permute-start.13 = (bf16[1,3,128,512]{3,2,1,0:T(8,128)(2,1)S(1)}, bf16[1,3,128,512]{3,2,1,0:T(8,128)(2,1)}, u32[]{:S(2)}, u32[]{:S(2)}) collective-permute-start(bf16[1,3,128,512]{3,2,1,0:T(8,128)(2,1)S(1)} %slice.299), channel_id=1, source_target_pairs={{0,96},{32,0},{64,32},{96,64},{1,97},{33,1},{65,33},{97,65},{2,98}... | collective-permute-start | bytes 1179656 | tf_op jit(solution)/shard_map/ppermute | solution.py:705
  206.3 49.6 %all-to-all-start.4 = ((bf16[8,128,1024]{2,1,0:T(8,128)(2,1)}), bf16[8,128,1024]{2,1,0:T(8,128)(2,1)}, u32[]{:S(2)}, u32[]{:S(2)}) async-start(bf16[8,128,1024]{2,1,0:T(8,128)(2,1)} %broadcast_in_dim.41), calls=%async_computation.4 | async-start | bytes 4194304 | tf_op jit(solution)/shard_map/all_to_all | solution.py:498
  264.8 47.4 %all-to-all-start.5 = ((bf16[8,128,1152]{2,1,0:T(8,128)(2,1)}), bf16[8,128,1152]{2,1,0:T(8,128)(2,1)}, u32[]{:S(2)}, u32[]{:S(2)}) async-start(bf16[8,128,1152]{2,1,0:T(8,128)(2,1)} %add_convert_fusion.1), calls=%async_computation.5 | async-start | bytes 4718592 | tf_op jit(solution)/shard_map/all_to_all | solution.py:498
  320.8 43.2 %all-to-all-start.6 = ((bf16[8,128,1152]{2,1,0:T(8,128)(2,1)}), bf16[8,128,1152]{2,1,0:T(8,128)(2,1)}, u32[]{:S(2)}, u32[]{:S(2)}) async-start(bf16[8,128,1152]{2,1,0:T(8,128)(2,1)} %add_convert_fusion), calls=%async_computation.7 | async-start | bytes 4718592 | tf_op jit(solution)/shard_map/all_to_all | solution.py:498
  328.1 242.9 %reduce-scatter.2.cloned.1.call-start = ((), (), s32[]{:S(2)}) async-start(), calls=%async_computation.11 | async-start | bytes 8912896 | tf_op jit(solution)/shard_map/reduce_scatter | solution.py:776
  374.2 37.9 %collective-permute-start.27 = (bf16[2,3,128,512]{3,2,1,0:T(8,128)(2,1)}, bf16[2,3,128,512]{3,2,1,0:T(8,128)(2,1)}, u32[]{:S(2)}, u32[]{:S(2)}) collective-permute-start(bf16[2,3,128,512]{3,2,1,0:T(8,128)(2,1)} %pad_maximum_fusion.4), channel_id=1, source_target_pairs={{0,96},{32,0},{64,32},{96,64},{1,97},{33,1},{65,33},{97,65},{2,98}... | collective-permute-start | bytes 2359304 | tf_op jit(solution)/shard_map/ppermute | solution.py:545
  378.1 34.0 %collective-permute-start.26 = (bf16[2,3,128,512]{3,2,1,0:T(8,128)(2,1)}, bf16[2,3,128,512]{3,2,1,0:T(8,128)(2,1)}, u32[]{:S(2)}, u32[]{:S(2)}) collective-permute-start(bf16[2,3,128,512]{3,2,1,0:T(8,128)(2,1)} %pad_maximum_fusion.3), channel_id=1, source_target_pairs={{0,32},{32,64},{64,96},{96,0},{1,33},{33,65},{65,97},{97,1},{2,34}... | collective-permute-start | bytes 2359304 | tf_op jit(solution)/shard_map/ppermute | solution.py:544
  378.3 33.7 %all-to-all-start.7 = ((bf16[8,256,128]{2,1,0:T(8,128)(2,1)}), bf16[8,256,128]{2,1,0:T(8,128)(2,1)}, u32[]{:S(2)}, u32[]{:S(2)}) async-start(bf16[8,256,128]{2,1,0:T(8,128)(2,1)} %bitcast.189), calls=%async_computation.8 | async-start | bytes 1048576 | tf_op jit(solution)/shard_map/all_to_all | solution.py:498
  382.7 29.4 %collective-permute-start.24 = (bf16[1,3,128,512]{3,2,1,0:T(8,128)(2,1)S(1)}, bf16[1,3,128,512]{3,2,1,0:T(8,128)(2,1)S(1)}, u32[]{:S(2)}, u32[]{:S(2)}) collective-permute-start(bf16[1,3,128,512]{3,2,1,0:T(8,128)(2,1)S(1)} %get-tuple-element.406), channel_id=1, source_target_pairs={{0,32},{32,64},{64,96},{96,0},{1,33},{33,65},{65,97},{97,1},{2,34}... | collective-permute-start | bytes 1179656 | tf_op jit(solution)/shard_map/ppermute | solution.py:539
  384.8 27.3 %collective-permute-start.25 = (bf16[1,3,128,512]{3,2,1,0:T(8,128)(2,1)S(1)}, bf16[1,3,128,512]{3,2,1,0:T(8,128)(2,1)S(1)}, u32[]{:S(2)}, u32[]{:S(2)}) collective-permute-start(bf16[1,3,128,512]{3,2,1,0:T(8,128)(2,1)S(1)} %get-tuple-element.405), channel_id=1, source_target_pairs={{0,96},{32,0},{64,32},{96,64},{1,97},{33,1},{65,33},{97,65},{2,98}... | collective-permute-start | bytes 1179656 | tf_op jit(solution)/shard_map/ppermute | solution.py:539
  453.3 23.5 %collective-permute-start.38 = (bf16[3,128,512]{2,1,0:T(8,128)(2,1)}, bf16[3,128,512]{2,1,0:T(8,128)(2,1)}, u32[]{:S(2)}, u32[]{:S(2)}) collective-permute-start(bf16[3,128,512]{2,1,0:T(8,128)(2,1)} %fusion.13), channel_id=1, source_target_pairs={{0,16},{16,0},{1,17},{17,1},{2,18},{18,2},{3,19},{19,3},{4,20},{20... | collective-permute-start | bytes 1179656 | tf_op jit(solution)/shard_map/ppermute | solution.py:502
  464.6 65.4 %all-to-all-start.8 = ((bf16[128,8,384]{2,1,0:T(8,128)(2,1)}), bf16[128,8,384]{2,1,0:T(8,128)(2,1)}, u32[]{:S(2)}, u32[]{:S(2)}) async-start(bf16[128,8,384]{2,1,0:T(8,128)(2,1)} %pad_maximum_fusion.7), calls=%async_computation.9 | async-start | bytes 1572864 | tf_op jit(solution)/shard_map/all_to_all | solution.py:498
  473.9 24.0 %collective-permute-start.35 = (bf16[2,128,1024]{2,1,0:T(8,128)(2,1)}, bf16[2,128,1024]{2,1,0:T(8,128)(2,1)}, u32[]{:S(2)}, u32[]{:S(2)}) collective-permute-start(bf16[2,128,1024]{2,1,0:T(8,128)(2,1)} %get-tuple-element.271), channel_id=1, source_target_pairs={{0,64},{32,96},{64,0},{96,32},{1,65},{33,97},{65,1},{97,33},{2,66}... | collective-permute-start | bytes 1572872 | tf_op jit(solution)/shard_map/ppermute | solution.py:506
  476.8 30.8 %collective-permute-start.36 = (bf16[2,128,1024]{2,1,0:T(8,128)(2,1)}, bf16[2,128,1024]{2,1,0:T(8,128)(2,1)}, u32[]{:S(2)}, u32[]{:S(2)}) collective-permute-start(bf16[2,128,1024]{2,1,0:T(8,128)(2,1)} %get-tuple-element.272), channel_id=1, source_target_pairs={{0,96},{32,0},{64,32},{96,64},{1,97},{33,1},{65,33},{97,65},{2,98}... | collective-permute-start | bytes 1572872 | tf_op jit(solution)/shard_map/ppermute | solution.py:506
  477.7 31.5 %collective-permute-start.31 = (bf16[2,128,1024]{2,1,0:T(8,128)(2,1)}, bf16[2,128,1024]{2,1,0:T(8,128)(2,1)}, u32[]{:S(2)}, u32[]{:S(2)}) collective-permute-start(bf16[2,128,1024]{2,1,0:T(8,128)(2,1)} %get-tuple-element.267), channel_id=1, source_target_pairs={{0,32},{32,64},{64,96},{96,0},{1,33},{33,65},{65,97},{97,1},{2,34}... | collective-permute-start | bytes 1572872 | tf_op jit(solution)/shard_map/ppermute | solution.py:506
  478.8 41.0 %collective-permute-start.32 = (bf16[2,128,1024]{2,1,0:T(8,128)(2,1)S(1)}, bf16[2,128,1024]{2,1,0:T(8,128)(2,1)}, u32[]{:S(2)}, u32[]{:S(2)}) collective-permute-start(bf16[2,128,1024]{2,1,0:T(8,128)(2,1)S(1)} %copy-done.39), channel_id=1, source_target_pairs={{0,64},{32,96},{64,0},{96,32},{1,65},{33,97},{65,1},{97,33},{2,66}... | collective-permute-start | bytes 1572872 | tf_op jit(solution)/shard_map/ppermute | solution.py:506
  479.8 50.2 %collective-permute-start.33 = (bf16[2,128,1024]{2,1,0:T(8,128)(2,1)S(1)}, bf16[2,128,1024]{2,1,0:T(8,128)(2,1)}, u32[]{:S(2)}, u32[]{:S(2)}) collective-permute-start(bf16[2,128,1024]{2,1,0:T(8,128)(2,1)S(1)} %copy-done.37), channel_id=1, source_target_pairs={{0,96},{32,0},{64,32},{96,64},{1,97},{33,1},{65,33},{97,65},{2,98}... | collective-permute-start | bytes 1572872 | tf_op jit(solution)/shard_map/ppermute | solution.py:506
  532.4 36.6 %all-to-all-start.9 = ((bf16[64,8,1024]{2,1,0:T(8,128)(2,1)}), bf16[64,8,1024]{2,1,0:T(8,128)(2,1)}, u32[]{:S(2)}, u32[]{:S(2)}) async-start(bf16[64,8,1024]{2,1,0:T(8,128)(2,1)} %fusion), calls=%async_computation.10 | async-start | bytes 2097152 | tf_op jit(solution)/shard_map/all_to_all | solution.py:498
  (107 other events, 1135.2 us)
Sparse Core Ops, SparseCore 0:
  22.2 97.9 all-gather.2
  346.4 108.2 reduce-scatter.1

commit v13 on v12

--- a/solution.py
+++ b/solution.py
@@ -684,12 +684,13 @@
     mixed_0, *saved_0 = attend_forward(order, seq_rows[0], *attention_args(0))
     seq_rows[1], mixed_0 = lax.optimization_barrier((seq_rows[1], mixed_0))
     mixed_1, *saved_1 = attend_forward(order, seq_rows[1], *attention_args(1))
+    mixed_1, moved_w[0] = lax.optimization_barrier((mixed_1, moved_w[0]))
     saved = [saved_0, saved_1]
     out_own, mixed_0, mixed_1 = lax.optimization_barrier((out_own, mixed_0, mixed_1))
     out_other = flip(out_own, "core")
     mixed = jnp.stack([mixed_0, mixed_1]).reshape(micro, n_ctx, tok, heads).transpose(1, 0, 2, 3)
     mixed = exchange(mixed.reshape(n_ctx, all_tok, heads), CTX)
-    mixed, moved_w[0] = lax.optimization_barrier((mixed, moved_w[0]))
+    mixed, moved_w[1] = lax.optimization_barrier((mixed, moved_w[1]))
     mixed = mixed.transpose(1, 0, 2).reshape(all_tok, width)
     out_full = jnp.where(
         core == 0,
@@ -779,39 +780,38 @@
     back_1 = exchange(back_1, GROUP)
     parts = [expert_grads(order, (kept_0, kept_1), e) for e in range(local)]
     far = [relay(part[2]) for part in parts]
-    back_1, parts, far[0] = lax.optimization_barrier((back_1, parts, far[0]))
+    back_1, parts = lax.optimization_barrier((back_1, parts))
     d_middle, d_mixed, d_rows = middle_back(
         jnp.concatenate([sum_parts(back_0), sum_parts(back_1)], axis=0)
     )
-    d_mixed, far[0] = lax.optimization_barrier((d_mixed, far[0]))
+    d_mixed, far = lax.optimization_barrier((d_mixed, far))
     d_mixed = exchange(d_mixed, CTX)
     moved = [ring_sums(parts[0], far[0])]
-    d_mixed, far[1], moved[0] = lax.optimization_barrier((d_mixed, far[1], moved[0]))
+    grad_out, grad_router, grad_mlp = weight_grads(*d_rows)
+    grad_out = grad_out.astype(BF).reshape(n_all // 2, 2, rows, width)
+    grad_own = lax.dynamic_index_in_dim(grad_out, core, axis=1, keepdims=False)
+    grad_other = lax.dynamic_index_in_dim(grad_out, 1 - core, axis=1, keepdims=False)
+    grad_out = back_sum(grad_own, grad_other)
+    d_mixed, moved[0], grad_out, grad_router, grad_mlp = lax.optimization_barrier(
+        (d_mixed, moved[0], grad_out, grad_router, grad_mlp)
+    )
+    grad_out = exchange(grad_out, CTX + GROUP)
     moved.append(ring_sums(parts[1], far[1]))
     d_mixed = d_mixed.reshape(n_ctx, micro, tok, heads)
     d_hidden_0, head_grads_0 = attention_back(0, d_mixed[:, 0])
     d_hidden_0, d_mixed, moved[1] = lax.optimization_barrier((d_hidden_0, d_mixed, moved[1]))
     hidden_moved_0 = by_z(d_hidden_0)
     d_hidden_1, head_grads_1 = attention_back(1, d_mixed[:, 1])
-    d_hidden_1, d_rows, parts, moved = lax.optimization_barrier(
-        (d_hidden_1, d_rows, parts, moved)
+    d_hidden_1, hidden_moved_0, grad_out = lax.optimization_barrier(
+        (d_hidden_1, hidden_moved_0, grad_out)
     )
     hidden_moved_1 = by_z(d_hidden_1)
     grad_heads, grad_attn, grad_qk = jax.tree.map(jnp.add, head_grads_0, head_grads_1)
-    grad_out, grad_router, grad_mlp = weight_grads(*d_rows)
     grad_pack = pack_grads(grad_heads, grad_router, grad_attn, grad_mlp, grad_qk)
     grad_pack = exchange(grad_pack, ALL)
-    grad_out = grad_out.astype(BF).reshape(n_all // 2, 2, rows, width)
-    grad_own = lax.dynamic_index_in_dim(grad_out, core, axis=1, keepdims=False)
-    grad_other = lax.dynamic_index_in_dim(grad_out, 1 - core, axis=1, keepdims=False)
-    grad_out = back_sum(grad_own, grad_other)
+    hidden_moved_1, parts, moved = lax.optimization_barrier((hidden_moved_1, parts, moved))
     weight_sums = [pair_sums(p, q) for p, q in zip(parts, moved)]
     weight_yl = [flip(sums[1].astype(BF), "yl") for sums in weight_sums]
-    grad_pack, grad_out, hidden_moved_0, hidden_moved_1, weight_yl = lax.optimization_barrier(
-        (grad_pack, grad_out, hidden_moved_0, hidden_moved_1, weight_yl)
-    )
-    exchange.last = grad_pack
-    grad_out = exchange(grad_out, CTX + GROUP)
     hidden_sums = [
         jnp.stack(sums)
         for sums in zip(

time: 588 us -> 578 us (0.983)
  waiting for transfers between devices: 175 us -> 158 us
  starting transfers between devices: 119 us -> 126 us
    all_to_all x10, waiting for transfers between devices: 14.5 us -> 49.8 us  [swap(): return lax.all_to_all(parts, axis, split_axis=0, concat_axis=0, tiled=True)]
    ppermute x4, waiting for transfers between devices: 33.2 us -> 0.01 us  [body(): last = [lax.ppermute(block, 'z', UP), lax.ppermute(block, 'z', DOWN)]]
    ppermute x4, waiting for transfers between devices: 23.4 us -> 0.01 us  [relay(): return [lax.ppermute(far[:1], 'z', UP), lax.ppermute(far[1:], 'z', DOWN)]]
    unnamed x176 -> x190, local copies, waits for them, and re-layouts: 20.8 us -> 20.8 us
  transfers between devices with their start and end apart: 52 -> 52, of which waited for: 22 -> 18; matrix products, arithmetic and copies ran while one was open for 17% -> 17% of each run, Pallas kernels for 25% -> 25%
where the time goes in v13:
time: 578 us; the launch traced here: 570 us
  waiting for transfers between devices  158 us (27%)
  Pallas kernels  143 us (25%)
  starting transfers between devices  126 us (22%)
  other arithmetic  68.5 us (12%)
  local copies, waits for them, and re-layouts  51.7 us (9%)
  between operations  16.2 us (3%)
  matrix products  6.44 us (1%)
    pallas_call x2, Pallas kernels, run_experts(): pl.pallas_call(functools.partial(expert_kernel, again=moe is not None), o...  80.7 us
    all_to_all x10, starting transfers between devices, swap(): return lax.all_to_all(parts, axis, split_axis=0, concat_axis=0, tiled=True)  76.9 us
    ppermute x12, waiting for transfers between devices, by_z(): lax.ppermute(parts[k], 'z', perm)  68.5 us
    all_to_all x10, waiting for transfers between devices, swap(): return lax.all_to_all(parts, axis, split_axis=0, concat_axis=0, tiled=True)  49.8 us
    ppermute x12, waiting for transfers between devices, flip(): return lax.ppermute(block, axis, FLIP)  29.3 us
    pallas_call x2, Pallas kernels, attend_backward(): pl.pallas_call(attend_back_kernel, out_shape=outs, grid=(1,), in_specs=[p...  24.5 us
    pallas_call x2, Pallas kernels, expert_grads(): pl.pallas_call(expert_grad_kernel, out_shape=[shape((2, 3, depth, hidden)...  20.9 us
    unnamed x190, local copies, waits for them, and re-layouts  20.8 us
  transfers between devices with their start and end apart: 52, of which 18 were waited for; matrix products, arithmetic and copies ran while one was open for 17% of the time, Pallas kernels for 25%

profile of v13, /device:TPU:0, one launch (start us, length us, event | category | flops | bytes accessed | tf_op | source)
XLA Modules:
  0.0 569.8 jit_solution(2472093608305039436)
XLA Ops:
  13.6 4.0 collective-permute-done.1
  17.6 4.3 collective-permute-done
  27.0 11.2 %all-to-all-start = ((bf16[128,8,384]{2,1,0:T(8,128)(2,1)}), bf16[128,8,384]{2,1,0:T(8,128)(2,1)}, u32[]{:S(2)}, u32[]{:S(2)}) async-start(bf16[128,8,384]{2,1,0:T(8,128)(2,1)} %bitcast.7), calls=%async_computation | async-start | bytes 1572864 | tf_op jit(solution)/shard_map/all_to_all | solution.py:498
  45.9 25.3 %collective-permute-done.2.refs_1_ = bf16[2,128,1024]{2,1,0:T(8,128)(2,1)S(1)} collective-permute-done((bf16[2,128,1024]{2,1,0:T(8,128)(2,1)S(1)}, bf16[2,128,1024]{2,1,0:T(8,128)(2,1)S(1)}, u32[]{:S(2)}, u32[]{:S(2)}) %collective-permute-start.2) | collective-permute-done | bytes 524320 | tf_op jit(solution)/shard_map/ppermute | solution.py:506
  77.8 10.1 %all-to-all-start.1 = ((bf16[64,8,1024]{2,1,0:T(8,128)(2,1)}), bf16[64,8,1024]{2,1,0:T(8,128)(2,1)}, u32[]{:S(2)}, u32[]{:S(2)}) async-start(bf16[64,8,1024]{2,1,0:T(8,128)(2,1)} %broadcast_in_dim.33), calls=%async_computation.1 | async-start | bytes 2097152 | tf_op jit(solution)/shard_map/all_to_all | solution.py:498
  92.1 20.0 %collective-permute-done.7.refs_3_ = bf16[2,128,1024]{2,1,0:T(8,128)(2,1)} collective-permute-done((bf16[2,128,1024]{2,1,0:T(8,128)(2,1)S(1)}, bf16[2,128,1024]{2,1,0:T(8,128)(2,1)}, u32[]{:S(2)}, u32[]{:S(2)}) %collective-permute-start.7) | collective-permute-done | bytes 524320 | tf_op jit(solution)/shard_map/ppermute | solution.py:506
  123.1 7.9 %shard_map.246 = (bf16[1024,128]{1,0:T(8,128)(2,1)S(1)}, bf16[1024,1024]{1,0:T(8,128)(2,1)S(1)}, bf16[1024,128]{1,0:T(8,128)(2,1)S(1)}, bf16[1024,128]{1,0:T(8,128)(2,1)S(1)}) custom-call(s32[8]{0:T(128)S(1)} %fusion.31.order_ref, bf16[2,128,1024]{2,1,0:T(8,128)(2,1)S(1)} %copy-done.6, bf16[2,128,1024]{2,1,0:T(8,128)(2,1)S(1)} %copy-done.25, ...), custom_call_target="tpu_custom_call" | custom-call | flops 10000000 | bytes 100000 | tf_op jit(solution)/shard_map/pallas_call | solution.py:229
  133.7 8.8 %shard_map.247 = (bf16[1024,128]{1,0:T(8,128)(2,1)S(1)}, bf16[1024,1024]{1,0:T(8,128)(2,1)S(1)}, bf16[1024,128]{1,0:T(8,128)(2,1)S(1)}, bf16[1024,128]{1,0:T(8,128)(2,1)S(1)}) custom-call(s32[8]{0:T(128)S(1)} %fusion.31.order_ref, bf16[2,128,1024]{2,1,0:T(8,128)(2,1)S(1)} %pad_maximum_fusion.8.refs_0_, bf16[2,128,1024]{2,1,0:T(8,128)(2,1)S(1)} %copy-done.31, ...), custom_call_target="tpu_custom_call" | custom-call | flops 10000000 | bytes 100000 | tf_op jit(solution)/shard_map/pallas_call | solution.py:229
  156.6 17.8 %all-to-all-done.2 = bf16[8,256,128]{2,1,0:T(8,128)(2,1)S(1)} async-done(((bf16[8,256,128]{2,1,0:T(8,128)(2,1)}), bf16[8,256,128]{2,1,0:T(8,128)(2,1)S(1)}, u32[]{:S(2)}, u32[]{:S(2)}) %all-to-all-start.2) | async-done | bytes 524320 | tf_op jit(solution)/shard_map/all_to_all | solution.py:498
  183.4 5.3 all-to-all-start.3
  204.0 5.6 collective-permute-done.16.refs_11_
  210.0 6.9 %all-to-all-done.3.refs_0_ = bf16[8,128,1024]{2,1,0:T(8,128)(2,1)} async-done(((bf16[8,128,1024]{2,1,0:T(8,128)(2,1)}), bf16[8,128,1024]{2,1,0:T(8,128)(2,1)}, u32[]{:S(2)}, u32[]{:S(2)}) %all-to-all-start.3) | async-done | bytes 2097184 | tf_op jit(solution)/shard_map/all_to_all | solution.py:498
  219.4 4.7 all-to-all-start.4
  226.4 40.4 %shard_map.248 = (bf16[16,2,128,1024]{3,2,1,0:T(8,128)(2,1)}, bf16[8,128,1152]{2,1,0:T(8,128)(2,1)}, bf16[8,128,1152]{2,1,0:T(8,128)(2,1)}, bf16[2,768,1024]{2,1...) custom-call(s32[10]{0:T(128)} %pad_add_fusion.scalar_ref, ...), custom_call_target="tpu_custom_call" | custom-call | flops 10000000 | bytes 100000 | tf_op jit(solution)/shard_map/pallas_call | solution.py:412
  267.4 4.6 collective-permute-done.19
  272.0 3.7 add_convert_fusion.1
  275.8 7.2 %all-to-all-start.5 = ((bf16[8,128,1152]{2,1,0:T(8,128)(2,1)}), bf16[8,128,1152]{2,1,0:T(8,128)(2,1)}, u32[]{:S(2)}, u32[]{:S(2)}) async-start(bf16[8,128,1152]{2,1,0:T(8,128)(2,1)} %add_convert_fusion.1), calls=%async_computation.5 | async-start | bytes 4718592 | tf_op jit(solution)/shard_map/all_to_all | solution.py:498
  283.1 40.3 %shard_map.249 = (bf16[16,2,128,1024]{3,2,1,0:T(8,128)(2,1)}, bf16[8,128,1152]{2,1,0:T(8,128)(2,1)}, bf16[8,128,1152]{2,1,0:T(8,128)(2,1)}, bf16[2,768,1024]{2,1...) custom-call(s32[10]{0:T(128)} %pad_add_fusion.scalar_ref, ...), custom_call_target="tpu_custom_call", output_to_operand_aliasing={{0}: (15, {})} | custom-call | flops 10000000 | bytes 100000 | tf_op jit(solution)/shard_map/pallas_call | solution.py:412
  323.6 4.8 collective-permute-done.21
  328.4 4.4 add_convert_fusion
  332.7 7.2 %all-to-all-start.6 = ((bf16[8,128,1152]{2,1,0:T(8,128)(2,1)}), bf16[8,128,1152]{2,1,0:T(8,128)(2,1)}, u32[]{:S(2)}, u32[]{:S(2)}) async-start(bf16[8,128,1152]{2,1,0:T(8,128)(2,1)} %add_convert_fusion), calls=%async_computation.7 | async-start | bytes 4718592 | tf_op jit(solution)/shard_map/all_to_all | solution.py:498
  345.5 10.9 %shard_map.251 = (bf16[2,3,128,512]{3,2,1,0:T(8,128)(2,1)S(1)}, bf16[2,3,128,512]{3,2,1,0:T(8,128)(2,1)S(1)}, bf16[2,3,128,512]{3,2,1,0:T(8,128)(2,1)S(1)}, bf16[2,3,128,512]{3,2,1,0:T(8,128)(2,1)S(1)}) custom-call(s32[8]{0:T(128)S(1)} %fusion.31.order_ref, bf16[2,768,1024]{2,1,0:T(8,128)(2,1)} %get-tuple-element.208.refs_0_, ...), custom_call_target="tpu_custom_call" | custom-call | flops 10000000 | bytes 100000 | tf_op jit(solution)/shard_map/pallas_call | solution.py:458
  361.7 10.1 %shard_map.250 = (bf16[2,3,128,512]{3,2,1,0:T(8,128)(2,1)S(1)}, bf16[2,3,128,512]{3,2,1,0:T(8,128)(2,1)S(1)}, bf16[2,3,128,512]{3,2,1,0:T(8,128)(2,1)S(1)}, bf16[2,3,128,512]{3,2,1,0:T(8,128)(2,1)S(1)}) custom-call(s32[8]{0:T(128)S(1)} %fusion.31.order_ref, bf16[2,768,1024]{2,1,0:T(8,128)(2,1)} %get-tuple-element.208.refs_0_, ...), custom_call_target="tpu_custom_call" | custom-call | flops 10000000 | bytes 100000 | tf_op jit(solution)/shard_map/pallas_call | solution.py:458
  400.9 5.4 all-to-all-start.7
  410.1 25.1 %all-to-all-done.7 = bf16[8,256,128]{2,1,0:T(8,128)(2,1)S(1)} async-done(((bf16[8,256,128]{2,1,0:T(8,128)(2,1)}), bf16[8,256,128]{2,1,0:T(8,128)(2,1)S(1)}, u32[]{:S(2)}, u32[]{:S(2)}) %all-to-all-start.7) | async-done | bytes 524320 | tf_op jit(solution)/shard_map/all_to_all | solution.py:498
  435.3 14.1 %all-to-all-start.8 = ((bf16[64,8,1024]{2,1,0:T(8,128)(2,1)}), bf16[64,8,1024]{2,1,0:T(8,128)(2,1)}, u32[]{:S(2)}, u32[]{:S(2)}) async-start(bf16[64,8,1024]{2,1,0:T(8,128)(2,1)} %fusion), calls=%async_computation.9 | async-start | bytes 2097152 | tf_op jit(solution)/shard_map/all_to_all | solution.py:498
  452.9 12.2 %shard_map.252 = (bf16[2,128,1024]{2,1,0:T(8,128)(2,1)S(1)}, bf16[2,128,1024]{2,1,0:T(8,128)(2,1)}, bf16[2,128,1024]{2,1,0:T(8,128)(2,1)}, bf16[2,128,1024]{2,1,...) custom-call(s32[8]{0:T(128)S(1)} %fusion.31.order_ref, ...), custom_call_target="tpu_custom_call" | custom-call | flops 10000000 | bytes 100000 | tf_op jit(solution)/shard_map/pallas_call | solution.py:252
  471.2 12.3 %shard_map.253 = (bf16[2,128,1024]{2,1,0:T(8,128)(2,1)S(1)}, bf16[2,128,1024]{2,1,0:T(8,128)(2,1)}, bf16[2,128,1024]{2,1,0:T(8,128)(2,1)}, bf16[2,128,1024]{2,1,...) custom-call(s32[8]{0:T(128)S(1)} %fusion.31.order_ref, ...), custom_call_target="tpu_custom_call" | custom-call | flops 10000000 | bytes 100000 | tf_op jit(solution)/shard_map/pallas_call | solution.py:252
  497.2 8.2 %all-to-all-start.9 = ((bf16[128,8,384]{2,1,0:T(8,128)(2,1)}), bf16[128,8,384]{2,1,0:T(8,128)(2,1)}, u32[]{:S(2)}, u32[]{:S(2)}) async-start(bf16[128,8,384]{2,1,0:T(8,128)(2,1)} %pad_maximum_fusion.7), calls=%async_computation.10 | async-start | bytes 1572864 | tf_op jit(solution)/shard_map/all_to_all | solution.py:498
  509.9 16.4 %collective-permute-done.35 = bf16[2,128,1024]{2,1,0:T(8,128)(2,1)} collective-permute-done((bf16[2,128,1024]{2,1,0:T(8,128)(2,1)}, bf16[2,128,1024]{2,1,0:T(8,128)(2,1)}, u32[]{:S(2)}, u32[]{:S(2)}) %collective-permute-start.35) | collective-permute-done | bytes 524320 | tf_op jit(solution)/shard_map/ppermute | solution.py:506
  543.0 6.0 %collective-permute-done.39 = bf16[3,128,512]{2,1,0:T(8,128)(2,1)} collective-permute-done((bf16[3,128,512]{2,1,0:T(8,128)(2,1)}, bf16[3,128,512]{2,1,0:T(8,128)(2,1)}, u32[]{:S(2)}, u32[]{:S(2)}) %collective-permute-start.39) | collective-permute-done | bytes 393248 | tf_op jit(solution)/shard_map/ppermute | solution.py:502
  552.5 5.6 collective-permute-done.37
  (406 shorter events, 183.0 us)
Async XLA Ops:
  7.2 219.2 %all-gather.3.cloned.1.call-start = ((), (), s32[]{:S(2)}) async-start(), calls=%async_computation.12 | async-start | bytes 10027008 | tf_op jit(solution)/shard_map/all_gather | solution.py:668
  23.0 64.9 %collective-permute-start.8 = (bf16[2,3,128,512]{3,2,1,0:T(8,128)(2,1)}, bf16[2,3,128,512]{3,2,1,0:T(8,128)(2,1)}, u32[]{:S(2)}, u32[]{:S(2)}) collective-permute-start(bf16[2,3,128,512]{3,2,1,0:T(8,128)(2,1)} %pad_maximum_fusion), channel_id=1, source_target_pairs={{0,16},{16,0},{1,17},{17,1},{2,18},{18,2},{3,19},{19,3},{4,20},{20... | collective-permute-start | bytes 2359304 | tf_op jit(solution)/shard_map/ppermute | solution.py:502
  27.0 49.7 %all-to-all-start = ((bf16[128,8,384]{2,1,0:T(8,128)(2,1)}), bf16[128,8,384]{2,1,0:T(8,128)(2,1)}, u32[]{:S(2)}, u32[]{:S(2)}) async-start(bf16[128,8,384]{2,1,0:T(8,128)(2,1)} %bitcast.7), calls=%async_computation | async-start | bytes 1572864 | tf_op jit(solution)/shard_map/all_to_all | solution.py:498
  38.3 32.9 %collective-permute-start.2 = (bf16[2,128,1024]{2,1,0:T(8,128)(2,1)S(1)}, bf16[2,128,1024]{2,1,0:T(8,128)(2,1)S(1)}, u32[]{:S(2)}, u32[]{:S(2)}) collective-permute-start(bf16[2,128,1024]{2,1,0:T(8,128)(2,1)S(1)} %pad_maximum_fusion.9.refs_0_), channel_id=1, source_target_pairs={{0,96},{32,0},{64,32},{96,64},{1,97},{33,1},{65,33},{97,65},{2,98}... | collective-permute-start | bytes 1572872 | tf_op jit(solution)/shard_map/ppermute | solution.py:506
  41.1 30.1 %collective-permute-start.3 = (bf16[2,128,1024]{2,1,0:T(8,128)(2,1)S(1)}, bf16[2,128,1024]{2,1,0:T(8,128)(2,1)S(1)}, u32[]{:S(2)}, u32[]{:S(2)}) collective-permute-start(bf16[2,128,1024]{2,1,0:T(8,128)(2,1)S(1)} %pad_maximum_fusion.9.refs_0_), channel_id=1, source_target_pairs={{0,64},{32,96},{64,0},{96,32},{1,65},{33,97},{65,1},{97,33},{2,66}... | collective-permute-start | bytes 1572872 | tf_op jit(solution)/shard_map/ppermute | solution.py:506
  41.4 33.2 %collective-permute-start.4 = (bf16[2,128,1024]{2,1,0:T(8,128)(2,1)S(1)}, bf16[2,128,1024]{2,1,0:T(8,128)(2,1)S(1)}, u32[]{:S(2)}, u32[]{:S(2)}) collective-permute-start(bf16[2,128,1024]{2,1,0:T(8,128)(2,1)S(1)} %pad_maximum_fusion.9.refs_0_), channel_id=1, source_target_pairs={{0,32},{32,64},{64,96},{96,0},{1,33},{33,65},{65,97},{97,1},{2,34}... | collective-permute-start | bytes 1572872 | tf_op jit(solution)/shard_map/ppermute | solution.py:506
  75.8 36.3 %collective-permute-start.7 = (bf16[2,128,1024]{2,1,0:T(8,128)(2,1)S(1)}, bf16[2,128,1024]{2,1,0:T(8,128)(2,1)}, u32[]{:S(2)}, u32[]{:S(2)}) collective-permute-start(bf16[2,128,1024]{2,1,0:T(8,128)(2,1)S(1)} %pad_maximum_fusion.8.refs_0_), channel_id=1, source_target_pairs={{0,32},{32,64},{64,96},{96,0},{1,33},{33,65},{65,97},{97,1},{2,34}... | collective-permute-start | bytes 1572872 | tf_op jit(solution)/shard_map/ppermute | solution.py:506
  77.8 66.8 %all-to-all-start.1 = ((bf16[64,8,1024]{2,1,0:T(8,128)(2,1)}), bf16[64,8,1024]{2,1,0:T(8,128)(2,1)}, u32[]{:S(2)}, u32[]{:S(2)}) async-start(bf16[64,8,1024]{2,1,0:T(8,128)(2,1)} %broadcast_in_dim.33), calls=%async_computation.1 | async-start | bytes 2097152 | tf_op jit(solution)/shard_map/all_to_all | solution.py:498
  112.1 32.5 %collective-permute-start.10 = (bf16[2,3,128,512]{3,2,1,0:T(8,128)(2,1)}, bf16[2,3,128,512]{3,2,1,0:T(8,128)(2,1)}, u32[]{:S(2)}, u32[]{:S(2)}) collective-permute-start(bf16[2,3,128,512]{3,2,1,0:T(8,128)(2,1)} %pad_maximum_fusion.1.refs_4_), channel_id=1, source_target_pairs={{0,96},{32,0},{64,32},{96,64},{1,97},{33,1},{65,33},{97,65},{2,98}... | collective-permute-start | bytes 2359304 | tf_op jit(solution)/shard_map/ppermute | solution.py:656
  113.3 31.3 %collective-permute-start.9 = (bf16[2,3,128,512]{3,2,1,0:T(8,128)(2,1)}, bf16[2,3,128,512]{3,2,1,0:T(8,128)(2,1)}, u32[]{:S(2)}, u32[]{:S(2)}) collective-permute-start(bf16[2,3,128,512]{3,2,1,0:T(8,128)(2,1)} %pad_maximum_fusion.1.refs_4_), channel_id=1, source_target_pairs={{0,32},{32,64},{64,96},{96,0},{1,33},{33,65},{65,97},{97,1},{2,34}... | collective-permute-start | bytes 2359304 | tf_op jit(solution)/shard_map/ppermute | solution.py:656
  144.6 31.9 %collective-permute-start.13 = (bf16[64,8,1024]{2,1,0:T(8,128)(2,1)}, bf16[64,8,1024]{2,1,0:T(8,128)(2,1)}, u32[]{:S(2)}, u32[]{:S(2)}) collective-permute-start(bf16[64,8,1024]{2,1,0:T(8,128)(2,1)} %all-to-all-done.1), channel_id=1, source_target_pairs={{0,1},{1,0},{2,3},{3,2},{4,5},{5,4},{6,7},{7,6},{8,9},{9,8},{10,11... | collective-permute-start | bytes 3145736 | tf_op jit(solution)/shard_map/ppermute | solution.py:502
  146.9 27.5 %collective-permute-start.11 = (bf16[2,3,128,512]{3,2,1,0:T(8,128)(2,1)}, bf16[2,3,128,512]{3,2,1,0:T(8,128)(2,1)}, u32[]{:S(2)}, u32[]{:S(2)}) collective-permute-start(bf16[2,3,128,512]{3,2,1,0:T(8,128)(2,1)} %pad_maximum_fusion.2.refs_9_), channel_id=1, source_target_pairs={{0,32},{32,64},{64,96},{96,0},{1,33},{33,65},{65,97},{97,1},{2,34}... | collective-permute-start | bytes 2359304 | tf_op jit(solution)/shard_map/ppermute | solution.py:656
  146.9 27.5 %collective-permute-start.12 = (bf16[2,3,128,512]{3,2,1,0:T(8,128)(2,1)}, bf16[2,3,128,512]{3,2,1,0:T(8,128)(2,1)}, u32[]{:S(2)}, u32[]{:S(2)}) collective-permute-start(bf16[2,3,128,512]{3,2,1,0:T(8,128)(2,1)} %pad_maximum_fusion.2.refs_9_), channel_id=1, source_target_pairs={{0,96},{32,0},{64,32},{96,64},{1,97},{33,1},{65,33},{97,65},{2,98}... | collective-permute-start | bytes 2359304 | tf_op jit(solution)/shard_map/ppermute | solution.py:656
  152.0 22.4 %all-to-all-start.2 = ((bf16[8,256,128]{2,1,0:T(8,128)(2,1)}), bf16[8,256,128]{2,1,0:T(8,128)(2,1)S(1)}, u32[]{:S(2)}, u32[]{:S(2)}) async-start(bf16[8,256,128]{2,1,0:T(8,128)(2,1)} %bitcast.180), calls=%async_computation.2 | async-start | bytes 1048576 | tf_op jit(solution)/shard_map/all_to_all | solution.py:498
  183.4 33.5 %all-to-all-start.3 = ((bf16[8,128,1024]{2,1,0:T(8,128)(2,1)}), bf16[8,128,1024]{2,1,0:T(8,128)(2,1)}, u32[]{:S(2)}, u32[]{:S(2)}) async-start(bf16[8,128,1024]{2,1,0:T(8,128)(2,1)} %broadcast_in_dim.42), calls=%async_computation.3 | async-start | bytes 4194304 | tf_op jit(solution)/shard_map/all_to_all | solution.py:498
  219.4 47.3 %all-to-all-start.4 = ((bf16[8,128,1024]{2,1,0:T(8,128)(2,1)}), bf16[8,128,1024]{2,1,0:T(8,128)(2,1)}, u32[]{:S(2)}, u32[]{:S(2)}) async-start(bf16[8,128,1024]{2,1,0:T(8,128)(2,1)} %broadcast_in_dim.41), calls=%async_computation.4 | async-start | bytes 4194304 | tf_op jit(solution)/shard_map/all_to_all | solution.py:498
  275.8 47.6 %all-to-all-start.5 = ((bf16[8,128,1152]{2,1,0:T(8,128)(2,1)}), bf16[8,128,1152]{2,1,0:T(8,128)(2,1)}, u32[]{:S(2)}, u32[]{:S(2)}) async-start(bf16[8,128,1152]{2,1,0:T(8,128)(2,1)} %add_convert_fusion.1), calls=%async_computation.5 | async-start | bytes 4718592 | tf_op jit(solution)/shard_map/all_to_all | solution.py:498
  283.0 277.8 %reduce-scatter.2.cloned.1.call-start = ((), (), s32[]{:S(2)}) async-start(), calls=%async_computation.11 | async-start | bytes 8912896 | tf_op jit(solution)/shard_map/reduce_scatter | solution.py:777
  332.7 44.6 %all-to-all-start.6 = ((bf16[8,128,1152]{2,1,0:T(8,128)(2,1)}), bf16[8,128,1152]{2,1,0:T(8,128)(2,1)}, u32[]{:S(2)}, u32[]{:S(2)}) async-start(bf16[8,128,1152]{2,1,0:T(8,128)(2,1)} %add_convert_fusion), calls=%async_computation.7 | async-start | bytes 4718592 | tf_op jit(solution)/shard_map/all_to_all | solution.py:498
  358.3 29.7 %collective-permute-start.24 = (bf16[1,3,128,512]{3,2,1,0:T(8,128)(2,1)}, bf16[1,3,128,512]{3,2,1,0:T(8,128)(2,1)}, u32[]{:S(2)}, u32[]{:S(2)}) collective-permute-start(bf16[1,3,128,512]{3,2,1,0:T(8,128)(2,1)} %get-tuple-element.404), channel_id=1, source_target_pairs={{0,32},{32,64},{64,96},{96,0},{1,33},{33,65},{65,97},{97,1},{2,34}... | collective-permute-start | bytes 1179656 | tf_op jit(solution)/shard_map/ppermute | solution.py:539
  358.7 29.2 %collective-permute-start.25 = (bf16[1,3,128,512]{3,2,1,0:T(8,128)(2,1)}, bf16[1,3,128,512]{3,2,1,0:T(8,128)(2,1)}, u32[]{:S(2)}, u32[]{:S(2)}) collective-permute-start(bf16[1,3,128,512]{3,2,1,0:T(8,128)(2,1)} %get-tuple-element.403), channel_id=1, source_target_pairs={{0,96},{32,0},{64,32},{96,64},{1,97},{33,1},{65,33},{97,65},{2,98}... | collective-permute-start | bytes 1179656 | tf_op jit(solution)/shard_map/ppermute | solution.py:539
  390.1 45.2 %collective-permute-start.27 = (bf16[2,3,128,512]{3,2,1,0:T(8,128)(2,1)}, bf16[2,3,128,512]{3,2,1,0:T(8,128)(2,1)}, u32[]{:S(2)}, u32[]{:S(2)}) collective-permute-start(bf16[2,3,128,512]{3,2,1,0:T(8,128)(2,1)} %pad_maximum_fusion.4), channel_id=1, source_target_pairs={{0,96},{32,0},{64,32},{96,64},{1,97},{33,1},{65,33},{97,65},{2,98}... | collective-permute-start | bytes 2359304 | tf_op jit(solution)/shard_map/ppermute | solution.py:545
  393.2 42.0 %collective-permute-start.26 = (bf16[2,3,128,512]{3,2,1,0:T(8,128)(2,1)}, bf16[2,3,128,512]{3,2,1,0:T(8,128)(2,1)}, u32[]{:S(2)}, u32[]{:S(2)}) collective-permute-start(bf16[2,3,128,512]{3,2,1,0:T(8,128)(2,1)} %pad_maximum_fusion.3), channel_id=1, source_target_pairs={{0,32},{32,64},{64,96},{96,0},{1,33},{33,65},{65,97},{97,1},{2,34}... | collective-permute-start | bytes 2359304 | tf_op jit(solution)/shard_map/ppermute | solution.py:544
  396.4 68.8 %collective-permute-start.30 = (bf16[2,3,128,512]{3,2,1,0:T(8,128)(2,1)}, bf16[2,3,128,512]{3,2,1,0:T(8,128)(2,1)}, u32[]{:S(2)}, u32[]{:S(2)}) collective-permute-start(bf16[2,3,128,512]{3,2,1,0:T(8,128)(2,1)} %pad_maximum_fusion.6), channel_id=1, source_target_pairs={{0,96},{32,0},{64,32},{96,64},{1,97},{33,1},{65,33},{97,65},{2,98}... | collective-permute-start | bytes 2359304 | tf_op jit(solution)/shard_map/ppermute | solution.py:545
  400.7 64.4 %collective-permute-start.29 = (bf16[2,3,128,512]{3,2,1,0:T(8,128)(2,1)}, bf16[2,3,128,512]{3,2,1,0:T(8,128)(2,1)}, u32[]{:S(2)}, u32[]{:S(2)}) collective-permute-start(bf16[2,3,128,512]{3,2,1,0:T(8,128)(2,1)} %pad_maximum_fusion.5), channel_id=1, source_target_pairs={{0,32},{32,64},{64,96},{96,0},{1,33},{33,65},{65,97},{97,1},{2,34}... | collective-permute-start | bytes 2359304 | tf_op jit(solution)/shard_map/ppermute | solution.py:544
  400.9 34.3 %all-to-all-start.7 = ((bf16[8,256,128]{2,1,0:T(8,128)(2,1)}), bf16[8,256,128]{2,1,0:T(8,128)(2,1)S(1)}, u32[]{:S(2)}, u32[]{:S(2)}) async-start(bf16[8,256,128]{2,1,0:T(8,128)(2,1)} %bitcast.151), calls=%async_computation.8 | async-start | bytes 1048576 | tf_op jit(solution)/shard_map/all_to_all | solution.py:498
  435.3 55.4 %all-to-all-start.8 = ((bf16[64,8,1024]{2,1,0:T(8,128)(2,1)}), bf16[64,8,1024]{2,1,0:T(8,128)(2,1)}, u32[]{:S(2)}, u32[]{:S(2)}) async-start(bf16[64,8,1024]{2,1,0:T(8,128)(2,1)} %fusion), calls=%async_computation.9 | async-start | bytes 2097152 | tf_op jit(solution)/shard_map/all_to_all | solution.py:498
  466.8 23.9 %collective-permute-start.32 = (bf16[2,128,1024]{2,1,0:T(8,128)(2,1)}, bf16[2,128,1024]{2,1,0:T(8,128)(2,1)}, u32[]{:S(2)}, u32[]{:S(2)}) collective-permute-start(bf16[2,128,1024]{2,1,0:T(8,128)(2,1)} %get-tuple-element.264), channel_id=1, source_target_pairs={{0,64},{32,96},{64,0},{96,32},{1,65},{33,97},{65,1},{97,33},{2,66}... | collective-permute-start | bytes 1572872 | tf_op jit(solution)/shard_map/ppermute | solution.py:506
  492.4 33.9 %collective-permute-start.35 = (bf16[2,128,1024]{2,1,0:T(8,128)(2,1)}, bf16[2,128,1024]{2,1,0:T(8,128)(2,1)}, u32[]{:S(2)}, u32[]{:S(2)}) collective-permute-start(bf16[2,128,1024]{2,1,0:T(8,128)(2,1)} %get-tuple-element.271), channel_id=1, source_target_pairs={{0,64},{32,96},{64,0},{96,32},{1,65},{33,97},{65,1},{97,33},{2,66}... | collective-permute-start | bytes 1572872 | tf_op jit(solution)/shard_map/ppermute | solution.py:506
  494.6 31.6 %collective-permute-start.36 = (bf16[2,128,1024]{2,1,0:T(8,128)(2,1)}, bf16[2,128,1024]{2,1,0:T(8,128)(2,1)}, u32[]{:S(2)}, u32[]{:S(2)}) collective-permute-start(bf16[2,128,1024]{2,1,0:T(8,128)(2,1)} %get-tuple-element.272), channel_id=1, source_target_pairs={{0,96},{32,0},{64,32},{96,64},{1,97},{33,1},{65,33},{97,65},{2,98}... | collective-permute-start | bytes 1572872 | tf_op jit(solution)/shard_map/ppermute | solution.py:506
  497.2 39.6 %all-to-all-start.9 = ((bf16[128,8,384]{2,1,0:T(8,128)(2,1)}), bf16[128,8,384]{2,1,0:T(8,128)(2,1)}, u32[]{:S(2)}, u32[]{:S(2)}) async-start(bf16[128,8,384]{2,1,0:T(8,128)(2,1)} %pad_maximum_fusion.7), calls=%async_computation.10 | async-start | bytes 1572864 | tf_op jit(solution)/shard_map/all_to_all | solution.py:498
  535.5 22.6 %collective-permute-start.37 = (bf16[2,128,1024]{2,1,0:T(8,128)(2,1)}, bf16[2,128,1024]{2,1,0:T(8,128)(2,1)}, u32[]{:S(2)}, u32[]{:S(2)}) collective-permute-start(bf16[2,128,1024]{2,1,0:T(8,128)(2,1)} %pad_maximum_fusion.11), channel_id=1, source_target_pairs={{0,16},{16,0},{1,17},{17,1},{2,18},{18,2},{3,19},{19,3},{4,20},{20... | collective-permute-start | bytes 1572872 | tf_op jit(solution)/shard_map/ppermute | solution.py:502
  (114 other events, 1236.4 us)
Sparse Core Ops, SparseCore 0:
  22.2 102.3 all-gather.2
  323.7 110.6 reduce-scatter.1

commit v14 on v12

--- a/solution.py
+++ b/solution.py
@@ -273,19 +273,24 @@
     pieces, refs = (refs[4:9], refs[9:14]), refs[14:]
     if again:
         refs = refs[1:]
-    out_ref, refs = refs[0], refs[1:]
-    back_own_ref, back_other_ref, xe_ref, de_ref, act_ref, da_ref, db_ref = refs[:7]
-    pick_ref, weight_ref, dgate_ref, eo_ref, dr_ref, w_ref = refs[7:]
+    out_ref, back_own_ref, back_other_ref = refs[:3]
+    kept_refs, refs = refs[3:8], refs[8:]
+    xe_ref, de_ref, act_ref, da_ref, db_ref, *refs = refs
+    pick_ref, weight_ref, dgate_ref, eo_ref, dr_ref, w_ref, in_sem, out_sem = refs
     half, tok, width = x_own_ref.shape
     sources = 2 * half
     core = scalar_ref[1]
     depth = w_ref.shape[2] // 8
 
+    loads = []
     for e in range(2):
         blocks = [(ref, i) for ref in pieces[e] for i in range(ref.shape[0])]
         for r, (ref, i) in enumerate(blocks):
             rows = pl.ds(pl.multiple_of(scalar_ref[2 + r] * depth, depth), depth)
-            w_ref[e, :, rows] = ref[i]
+            loads.append(
+                pltpu.make_async_copy(ref.at[i], w_ref.at[e, :, rows], in_sem.at[8 * e + r])
+            )
+            loads[-1].start()
     local, slots, hidden = act_ref.shape
     cap = slots // sources
     first = scalar_ref[0]
@@ -326,10 +331,11 @@
         return carry
 
     for x_ref, offset, column in ((x_own_ref, 0, core), (x_other_ref, half, 1 - core)):
-        lax.fori_loop(
-            0, half, functools.partial(fetch, x_ref=x_ref, offset=offset, column=column), 0
-        )
-    chunk = 256
+        step = functools.partial(fetch, x_ref=x_ref, offset=offset, column=column)
+        lax.fori_loop(0, half, step, 0, unroll=4)
+    for load in loads:
+        load.wait()
+    chunk = 384
 
     def work(i, carry):
         e = i // (slots // chunk)
@@ -361,6 +367,14 @@
         return carry
 
     lax.fori_loop(0, local * (slots // chunk), work, 0)
+    stores = [
+        pltpu.make_async_copy(ref, kept, out_sem.at[n])
+        for n, (ref, kept) in enumerate(
+            zip((xe_ref, de_ref, act_ref, da_ref, db_ref), kept_refs)
+        )
+    ]
+    for store in stores:
+        store.start()
 
     def give(i, carry, back_ref, offset, column):
         s = i + offset
@@ -379,9 +393,10 @@
         return carry
 
     for back_ref, offset, column in ((back_own_ref, 0, core), (back_other_ref, half, 1 - core)):
-        lax.fori_loop(
-            0, half, functools.partial(give, back_ref=back_ref, offset=offset, column=column), 0
-        )
+        step = functools.partial(give, back_ref=back_ref, offset=offset, column=column)
+        lax.fori_loop(0, half, step, 0, unroll=4)
+    for store in stores:
+        store.wait()
 
 
 def run_experts(scalars, x_own, x_other, g_all, micro, router, pieces, cap, moe=None):
@@ -404,7 +419,8 @@
     g_spec = pl.BlockSpec(
         (sources, tok, wide), lambda i: (0, micro, 0), pipeline_mode=pl.Buffered(1)
     )
-    args = [router, *pieces[0], *pieces[1]]
+    args = [*pieces[0], *pieces[1]]
+    any_place = pl.BlockSpec(memory_space=pl.ANY)
     held = [] if moe is None else [moe]
     moe_spec = pl.BlockSpec(
         (sources, 1, tok, width), lambda i: (0, micro, 0, 0), pipeline_mode=pl.Buffered(1)
@@ -414,21 +430,24 @@
         out_shape=outs,
         grid=(1,),
         in_specs=[pl.BlockSpec(memory_space=pltpu.SMEM), whole(x_own), whole(x_other), g_spec]
-        + [whole(a) for a in args]
-        + [pl.BlockSpec(memory_space=pl.ANY)] * len(held),
-        out_specs=[moe_spec] + [whole(o) for o in outs[1:]],
-        input_output_aliases={4 + len(args): 0} if held else {},
-        scratch_shapes=[
+        + [whole(router)]
+        + [any_place] * (len(args) + len(held)),
+        out_specs=[moe_spec] + [whole(o) for o in outs[1:3]] + [any_place] * 5,
+        input_output_aliases={5 + len(args): 0} if held else {},
+        scratch_shapes=[pltpu.VMEM(o.shape, o.dtype) for o in outs[3:]]
+        + [
             pltpu.VMEM((sources, tok, local * cap), BF),
             pltpu.VMEM((local, slots, 1), F32),
             pltpu.VMEM((local, slots, 1), F32),
             pltpu.VMEM((local, slots, width), BF),
             pltpu.VMEM((local, slots, width), BF),
             pltpu.VMEM((local, 3, width, hidden), BF),
+            pltpu.SemaphoreType.DMA((16,)),
+            pltpu.SemaphoreType.DMA((5,)),
         ],
         compiler_params=pltpu.CompilerParams(vmem_limit_bytes=60 * 1024 * 1024),
         cost_estimate=COST,
-    )(scalars, x_own, x_other, g_all, *args, *held)
+    )(scalars, x_own, x_other, g_all, router, *args, *held)
 
 
 def expert_grad_kernel(order_ref, *refs):
@@ -779,26 +798,25 @@
     back_1 = exchange(back_1, GROUP)
     parts = [expert_grads(order, (kept_0, kept_1), e) for e in range(local)]
     far = [relay(part[2]) for part in parts]
-    back_1, parts, far[0] = lax.optimization_barrier((back_1, parts, far[0]))
+    back_1, parts = lax.optimization_barrier((back_1, parts))
     d_middle, d_mixed, d_rows = middle_back(
         jnp.concatenate([sum_parts(back_0), sum_parts(back_1)], axis=0)
     )
-    d_mixed, far[0] = lax.optimization_barrier((d_mixed, far[0]))
+    d_mixed, far = lax.optimization_barrier((d_mixed, far))
     d_mixed = exchange(d_mixed, CTX)
-    moved = [ring_sums(parts[0], far[0])]
-    d_mixed, far[1], moved[0] = lax.optimization_barrier((d_mixed, far[1], moved[0]))
-    moved.append(ring_sums(parts[1], far[1]))
+    d_mixed, far = lax.optimization_barrier((d_mixed, far))
+    moved = [ring_sums(part, f) for part, f in zip(parts, far)]
     d_mixed = d_mixed.reshape(n_ctx, micro, tok, heads)
     d_hidden_0, head_grads_0 = attention_back(0, d_mixed[:, 0])
-    d_hidden_0, d_mixed, moved[1] = lax.optimization_barrier((d_hidden_0, d_mixed, moved[1]))
+    d_hidden_0, d_mixed, moved[0] = lax.optimization_barrier((d_hidden_0, d_mixed, moved[0]))
+    d_hidden_1, head_grads_1 = attention_back(1, d_mixed[:, 1])
+    d_hidden_1, d_hidden_0, moved[1], d_rows = lax.optimization_barrier(
+        (d_hidden_1, d_hidden_0, moved[1], d_rows)
+    )
     hidden_moved_0 = by_z(d_hidden_0)
-    d_hidden_1, head_grads_1 = attention_back(1, d_mixed[:, 1])
-    d_hidden_1, d_rows, parts, moved = lax.optimization_barrier(
-        (d_hidden_1, d_rows, parts, moved)
-    )
     hidden_moved_1 = by_z(d_hidden_1)
+    grad_out, grad_router, grad_mlp = weight_grads(*d_rows)
     grad_heads, grad_attn, grad_qk = jax.tree.map(jnp.add, head_grads_0, head_grads_1)
-    grad_out, grad_router, grad_mlp = weight_grads(*d_rows)
     grad_pack = pack_grads(grad_heads, grad_router, grad_attn, grad_mlp, grad_qk)
     grad_pack = exchange(grad_pack, ALL)
     grad_out = grad_out.astype(BF).reshape(n_all // 2, 2, rows, width)
@@ -807,18 +825,16 @@
     grad_out = back_sum(grad_own, grad_other)
     weight_sums = [pair_sums(p, q) for p, q in zip(parts, moved)]
     weight_yl = [flip(sums[1].astype(BF), "yl") for sums in weight_sums]
-    grad_pack, grad_out, hidden_moved_0, hidden_moved_1, weight_yl = lax.optimization_barrier(
-        (grad_pack, grad_out, hidden_moved_0, hidden_moved_1, weight_yl)
+    grad_pack, grad_out, hidden_moved_0, weight_yl = lax.optimization_barrier(
+        (grad_pack, grad_out, hidden_moved_0, weight_yl)
     )
     exchange.last = grad_pack
     grad_out = exchange(grad_out, CTX + GROUP)
-    hidden_sums = [
-        jnp.stack(sums)
-        for sums in zip(
-            pair_sums(d_hidden_0, hidden_moved_0), pair_sums(d_hidden_1, hidden_moved_1)
-        )
-    ]
+    hidden_sums_0 = pair_sums(d_hidden_0, hidden_moved_0)
+    hidden_sums_1 = pair_sums(d_hidden_1, hidden_moved_1)
+    hidden_sums = [jnp.stack(sums) for sums in zip(hidden_sums_0, hidden_sums_1)]
     hidden_yl = flip(hidden_sums[1].astype(BF), "yl")
+    grad_out, hidden_yl = lax.optimization_barrier((grad_out, hidden_yl))
 
     grad_pack = grad_pack.astype(F32)
     own_heads = jnp.sum(grad_pack[:, :, :span].reshape(n_ctx, n_fsdp, rows, -1), axis=1)

time: 588 us -> 553 us (0.940)
  Pallas kernels: 143 us -> 121 us
  waiting for transfers between devices: 175 us -> 156 us
    ppermute x4, waiting for transfers between devices: 23.4 us -> 0.06 us  [relay(): return [lax.ppermute(far[:1], 'z', UP), lax.ppermute(far[1:], 'z', DOWN)]]
    pallas_call x2, Pallas kernels: 80.7 us -> 59.6 us  [run_experts(): pl.pallas_call(functools.partial(expert_kernel, again=moe is not None), o...]
    all_to_all x10, waiting for transfers between devices: 14.5 us -> 35.5 us  [swap(): return lax.all_to_all(parts, axis, split_axis=0, concat_axis=0, tiled=True)]
    ppermute x12, waiting for transfers between devices: 66.3 us -> 54.6 us  [by_z(): lax.ppermute(parts[k], 'z', perm)]
    ppermute x12, waiting for transfers between devices: 25.5 us -> 17.6 us  [flip(): return lax.ppermute(block, axis, FLIP)]
    unnamed x176 -> x184, local copies, waits for them, and re-layouts: 20.8 us -> 23.4 us
  transfers between devices with their start and end apart: 52 -> 52, of which waited for: 22 -> 21; matrix products, arithmetic and copies ran while one was open for 17% -> 19% of each run, Pallas kernels for 25% -> 22%
where the time goes in v14:
time: 553 us; the launch traced here: 545 us
  waiting for transfers between devices  156 us (28%)
  Pallas kernels  121 us (22%)
  starting transfers between devices  118 us (21%)
  other arithmetic  70.5 us (13%)
  local copies, waits for them, and re-layouts  57.5 us (10%)
  between operations  16.3 us (3%)
  matrix products  6.52 us (1%)
    all_to_all x10, starting transfers between devices, swap(): return lax.all_to_all(parts, axis, split_axis=0, concat_axis=0, tiled=True)  74.7 us
    pallas_call x2, Pallas kernels, run_experts(): pl.pallas_call(functools.partial(expert_kernel, again=moe is not None), o...  59.6 us
    ppermute x12, waiting for transfers between devices, by_z(): lax.ppermute(parts[k], 'z', perm)  54.6 us
    all_to_all x10, waiting for transfers between devices, swap(): return lax.all_to_all(parts, axis, split_axis=0, concat_axis=0, tiled=True)  35.5 us
    ppermute x4, waiting for transfers between devices, body(): last = [lax.ppermute(block, 'z', UP), lax.ppermute(block, 'z', DOWN)]  31.4 us
    unnamed x184, local copies, waits for them, and re-layouts  23.4 us
    pallas_call x2, Pallas kernels, attend_backward(): pl.pallas_call(attend_back_kernel, out_shape=outs, grid=(1,), in_specs=[p...  22.8 us
    pallas_call x2, Pallas kernels, expert_grads(): pl.pallas_call(expert_grad_kernel, out_shape=[shape((2, 3, depth, hidden)...  21.2 us
  transfers between devices with their start and end apart: 52, of which 21 were waited for; matrix products, arithmetic and copies ran while one was open for 19% of the time, Pallas kernels for 22%

profile of v14, /device:TPU:0, one launch (start us, length us, event | category | flops | bytes accessed | tf_op | source)
XLA Modules:
  0.0 545.2 jit_solution(16709338255215249709)
XLA Ops:
  17.7 4.3 collective-permute-done
  24.3 11.2 %all-to-all-start = ((bf16[128,8,384]{2,1,0:T(8,128)(2,1)}), bf16[128,8,384]{2,1,0:T(8,128)(2,1)S(1)}, u32[]{:S(2)}, u32[]{:S(2)}) async-start(bf16[128,8,384]{2,1,0:T(8,128)(2,1)} %bitcast.7), calls=%async_computation | async-start | bytes 1572864 | tf_op jit(solution)/shard_map/all_to_all | solution.py:517
  43.0 13.7 %all-to-all-done = bf16[128,8,384]{2,1,0:T(8,128)(2,1)S(1)} async-done(((bf16[128,8,384]{2,1,0:T(8,128)(2,1)}), bf16[128,8,384]{2,1,0:T(8,128)(2,1)S(1)}, u32[]{:S(2)}, u32[]{:S(2)}) %all-to-all-start) | async-done | bytes 786464 | tf_op jit(solution)/shard_map/all_to_all | solution.py:517
  58.0 5.5 %all-to-all-start.1 = ((bf16[64,8,1024]{2,1,0:T(8,128)(2,1)}), bf16[64,8,1024]{2,1,0:T(8,128)(2,1)}, u32[]{:S(2)}, u32[]{:S(2)}) async-start(bf16[64,8,1024]{2,1,0:T(8,128)(2,1)} %broadcast_in_dim.33), calls=%async_computation.1 | async-start | bytes 2097152 | tf_op jit(solution)/shard_map/all_to_all | solution.py:517
  66.6 10.1 %collective-permute-done.2.refs_1_ = bf16[2,128,1024]{2,1,0:T(8,128)(2,1)} collective-permute-done((bf16[2,128,1024]{2,1,0:T(8,128)(2,1)S(1)}, bf16[2,128,1024]{2,1,0:T(8,128)(2,1)}, u32[]{:S(2)}, u32[]{:S(2)}) %collective-permute-start.2) | collective-permute-done | bytes 524320 | tf_op jit(solution)/shard_map/ppermute | solution.py:525
  76.7 5.4 collective-permute-done.4.refs_3_
  88.7 8.8 %shard_map.246 = (bf16[1024,128]{1,0:T(8,128)(2,1)S(1)}, bf16[1024,1024]{1,0:T(8,128)(2,1)S(1)}, bf16[1024,128]{1,0:T(8,128)(2,1)S(1)}, bf16[1024,128]{1,0:T(8,128)(2,1)S(1)}) custom-call(s32[8]{0:T(128)S(1)} %fusion.29.order_ref, bf16[2,128,1024]{2,1,0:T(8,128)(2,1)S(1)} %copy-done.2, bf16[2,128,1024]{2,1,0:T(8,128)(2,1)} %collective-permute-done.2.refs_1_, ...), custom_call_target="tpu_custom_call" | custom-call | flops 10000000 | bytes 100000 | tf_op jit(solution)/shard_map/pallas_call | solution.py:229
  100.1 7.7 %collective-permute-done.7.refs_3_ = bf16[2,128,1024]{2,1,0:T(8,128)(2,1)} collective-permute-done((bf16[2,128,1024]{2,1,0:T(8,128)(2,1)S(1)}, bf16[2,128,1024]{2,1,0:T(8,128)(2,1)}, u32[]{:S(2)}, u32[]{:S(2)}) %collective-permute-start.7) | collective-permute-done | bytes 524320 | tf_op jit(solution)/shard_map/ppermute | solution.py:525
  107.8 9.0 %shard_map.247 = (bf16[1024,128]{1,0:T(8,128)(2,1)S(1)}, bf16[1024,1024]{1,0:T(8,128)(2,1)S(1)}, bf16[1024,128]{1,0:T(8,128)(2,1)S(1)}, bf16[1024,128]{1,0:T(8,128)(2,1)S(1)}) custom-call(s32[8]{0:T(128)S(1)} %fusion.29.order_ref, bf16[2,128,1024]{2,1,0:T(8,128)(2,1)S(1)} %pad_maximum_fusion.8.refs_0_, bf16[2,128,1024]{2,1,0:T(8,128)(2,1)} %collective-permute-done.5.refs_1_, ...), custom_call_target="tpu_custom_call" | custom-call | flops 10000000 | bytes 100000 | tf_op jit(solution)/shard_map/pallas_call | solution.py:229
  133.3 14.4 %collective-permute-done.10.refs_5_ = bf16[2,3,128,512]{3,2,1,0:T(8,128)(2,1)} collective-permute-done((bf16[2,3,128,512]{3,2,1,0:T(8,128)(2,1)}, bf16[2,3,128,512]{3,2,1,0:T(8,128)(2,1)}, u32[]{:S(2)}, u32[]{:S(2)}) %collective-permute-start.10) | collective-permute-done | bytes 786464 | tf_op jit(solution)/shard_map/ppermute | solution.py:675
  161.2 6.1 %all-to-all-start.3 = ((bf16[8,128,1024]{2,1,0:T(8,128)(2,1)}), bf16[8,128,1024]{2,1,0:T(8,128)(2,1)}, u32[]{:S(2)}, u32[]{:S(2)}) async-start(bf16[8,128,1024]{2,1,0:T(8,128)(2,1)} %broadcast_in_dim.42), calls=%async_computation.3 | async-start | bytes 4194304 | tf_op jit(solution)/shard_map/all_to_all | solution.py:517
  177.3 13.0 %collective-permute-done.15.refs_13_ = bf16[2,3,128,512]{3,2,1,0:T(8,128)(2,1)S(1)} collective-permute-done((bf16[2,3,128,512]{3,2,1,0:T(8,128)(2,1)S(1)}, bf16[2,3,128,512]{3,2,1,0:T(8,128)(2,1)S(1)}, u32[]{:S(2)}, u32[]{:S(2)}) %collective-permute-start.15) | collective-permute-done | bytes 786464 | tf_op jit(solution)/shard_map/ppermute | solution.py:675
  194.5 4.3 collective-permute-done.12.refs_6_
  198.8 6.6 %collective-permute-done.16.refs_11_ = bf16[1,3,128,512]{3,2,1,0:T(8,128)(2,1)} collective-permute-done((bf16[1,3,128,512]{3,2,1,0:T(8,128)(2,1)S(1)}, bf16[1,3,128,512]{3,2,1,0:T(8,128)(2,1)}, u32[]{:S(2)}, u32[]{:S(2)}) %collective-permute-start.16) | collective-permute-done | bytes 393248 | tf_op jit(solution)/shard_map/ppermute | solution.py:724
  207.0 7.2 %all-to-all-start.4 = ((bf16[8,128,1024]{2,1,0:T(8,128)(2,1)}), bf16[8,128,1024]{2,1,0:T(8,128)(2,1)}, u32[]{:S(2)}, u32[]{:S(2)}) async-start(bf16[8,128,1024]{2,1,0:T(8,128)(2,1)} %broadcast_in_dim.41), calls=%async_computation.4 | async-start | bytes 4194304 | tf_op jit(solution)/shard_map/all_to_all | solution.py:517
  216.6 29.8 %shard_map.248 = (bf16[16,2,128,1024]{3,2,1,0:T(8,128)(2,1)}, bf16[8,128,1152]{2,1,0:T(8,128)(2,1)}, bf16[8,128,1152]{2,1,0:T(8,128)(2,1)}, bf16[2,768,1024]{2,1...) custom-call(s32[10]{0:T(128)} %pad_add_fusion.scalar_ref, ...), custom_call_target="tpu_custom_call" | custom-call | flops 10000000 | bytes 100000 | tf_op jit(solution)/shard_map/pallas_call | solution.py:428
  246.8 4.5 collective-permute-done.19
  255.2 7.6 %all-to-all-start.5 = ((bf16[8,128,1152]{2,1,0:T(8,128)(2,1)}), bf16[8,128,1152]{2,1,0:T(8,128)(2,1)}, u32[]{:S(2)}, u32[]{:S(2)}) async-start(bf16[8,128,1152]{2,1,0:T(8,128)(2,1)} %add_convert_fusion.1), calls=%async_computation.5 | async-start | bytes 4718592 | tf_op jit(solution)/shard_map/all_to_all | solution.py:517
  262.8 29.7 %shard_map.249 = (bf16[16,2,128,1024]{3,2,1,0:T(8,128)(2,1)}, bf16[8,128,1152]{2,1,0:T(8,128)(2,1)}, bf16[8,128,1152]{2,1,0:T(8,128)(2,1)}, bf16[2,768,1024]{2,1...) custom-call(s32[10]{0:T(128)} %pad_add_fusion.scalar_ref, ...), custom_call_target="tpu_custom_call", output_to_operand_aliasing={{0}: (15, {})} | custom-call | flops 10000000 | bytes 100000 | tf_op jit(solution)/shard_map/pallas_call | solution.py:428
  294.7 4.7 collective-permute-done.21
  303.1 9.6 %all-to-all-start.6 = ((bf16[8,128,1152]{2,1,0:T(8,128)(2,1)}), bf16[8,128,1152]{2,1,0:T(8,128)(2,1)}, u32[]{:S(2)}, u32[]{:S(2)}) async-start(bf16[8,128,1152]{2,1,0:T(8,128)(2,1)} %add_convert_fusion), calls=%async_computation.7 | async-start | bytes 4718592 | tf_op jit(solution)/shard_map/all_to_all | solution.py:517
  318.0 10.1 %shard_map.251 = (bf16[2,3,128,512]{3,2,1,0:T(8,128)(2,1)S(1)}, bf16[2,3,128,512]{3,2,1,0:T(8,128)(2,1)S(1)}, bf16[2,3,128,512]{3,2,1,0:T(8,128)(2,1)S(1)}, bf16[2,3,128,512]{3,2,1,0:T(8,128)(2,1)S(1)}) custom-call(s32[8]{0:T(128)S(1)} %fusion.29.order_ref, bf16[2,768,1024]{2,1,0:T(8,128)(2,1)} %get-tuple-element.206.refs_0_, ...), custom_call_target="tpu_custom_call" | custom-call | flops 10000000 | bytes 100000 | tf_op jit(solution)/shard_map/pallas_call | solution.py:477
  332.4 11.1 %shard_map.250 = (bf16[2,3,128,512]{3,2,1,0:T(8,128)(2,1)S(1)}, bf16[2,3,128,512]{3,2,1,0:T(8,128)(2,1)S(1)}, bf16[2,3,128,512]{3,2,1,0:T(8,128)(2,1)S(1)}, bf16[2,3,128,512]{3,2,1,0:T(8,128)(2,1)S(1)}) custom-call(s32[8]{0:T(128)S(1)} %fusion.29.order_ref, bf16[2,768,1024]{2,1,0:T(8,128)(2,1)} %get-tuple-element.206.refs_0_, ...), custom_call_target="tpu_custom_call" | custom-call | flops 10000000 | bytes 100000 | tf_op jit(solution)/shard_map/pallas_call | solution.py:477
  367.2 10.1 %all-to-all-done.7 = bf16[8,256,128]{2,1,0:T(8,128)(2,1)} async-done(((bf16[8,256,128]{2,1,0:T(8,128)(2,1)}), bf16[8,256,128]{2,1,0:T(8,128)(2,1)}, u32[]{:S(2)}, u32[]{:S(2)}) %all-to-all-start.7) | async-done | bytes 524320 | tf_op jit(solution)/shard_map/all_to_all | solution.py:517
  397.0 11.2 %shard_map.252 = (bf16[2,128,1024]{2,1,0:T(8,128)(2,1)S(1)}, bf16[2,128,1024]{2,1,0:T(8,128)(2,1)S(1)}, bf16[2,128,1024]{2,1,0:T(8,128)(2,1)S(1)}, bf16[2,128,10...) custom-call(s32[8]{0:T(128)S(1)} %fusion.29.order_ref, ...), custom_call_target="tpu_custom_call" | custom-call | flops 10000000 | bytes 100000 | tf_op jit(solution)/shard_map/pallas_call | solution.py:252
  410.9 5.1 collective-permute-done.27
  417.0 11.6 %shard_map.253 = (bf16[2,128,1024]{2,1,0:T(8,128)(2,1)S(1)}, bf16[2,128,1024]{2,1,0:T(8,128)(2,1)S(1)}, bf16[2,128,1024]{2,1,0:T(8,128)(2,1)S(1)}, bf16[2,128,10...) custom-call(s32[8]{0:T(128)S(1)} %fusion.29.order_ref, ...), custom_call_target="tpu_custom_call" | custom-call | flops 10000000 | bytes 100000 | tf_op jit(solution)/shard_map/pallas_call | solution.py:252
  443.2 9.6 %all-to-all-start.8 = ((bf16[128,8,384]{2,1,0:T(8,128)(2,1)}), bf16[128,8,384]{2,1,0:T(8,128)(2,1)}, u32[]{:S(2)}, u32[]{:S(2)}) async-start(bf16[128,8,384]{2,1,0:T(8,128)(2,1)} %pad_maximum_fusion.7), calls=%async_computation.9 | async-start | bytes 1572864 | tf_op jit(solution)/shard_map/all_to_all | solution.py:517
  455.2 14.6 %collective-permute-done.37 = bf16[2,128,1024]{2,1,0:T(8,128)(2,1)} collective-permute-done((bf16[2,128,1024]{2,1,0:T(8,128)(2,1)}, bf16[2,128,1024]{2,1,0:T(8,128)(2,1)}, u32[]{:S(2)}, u32[]{:S(2)}) %collective-permute-start.37) | collective-permute-done | bytes 524320 | tf_op jit(solution)/shard_map/ppermute | solution.py:525
  478.4 16.8 %collective-permute-done.31 = bf16[2,128,1024]{2,1,0:T(8,128)(2,1)S(1)} collective-permute-done((bf16[2,128,1024]{2,1,0:T(8,128)(2,1)S(1)}, bf16[2,128,1024]{2,1,0:T(8,128)(2,1)S(1)}, u32[]{:S(2)}, u32[]{:S(2)}) %collective-permute-start.31) | collective-permute-done | bytes 524320 | tf_op jit(solution)/shard_map/ppermute | solution.py:525
  503.2 9.5 %all-to-all-start.9 = ((bf16[64,8,1024]{2,1,0:T(8,128)(2,1)}), bf16[64,8,1024]{2,1,0:T(8,128)(2,1)}, u32[]{:S(2)}, u32[]{:S(2)}) async-start(bf16[64,8,1024]{2,1,0:T(8,128)(2,1)} %fusion), calls=%async_computation.10 | async-start | bytes 2097152 | tf_op jit(solution)/shard_map/all_to_all | solution.py:517
  521.9 9.0 %all-to-all-done.9 = bf16[64,8,1024]{2,1,0:T(8,128)(2,1)} async-done(((bf16[64,8,1024]{2,1,0:T(8,128)(2,1)}), bf16[64,8,1024]{2,1,0:T(8,128)(2,1)}, u32[]{:S(2)}, u32[]{:S(2)}) %all-to-all-start.9) | async-done | bytes 1048608 | tf_op jit(solution)/shard_map/all_to_all | solution.py:517
  (402 shorter events, 196.9 us)
Async XLA Ops:
  7.2 209.4 %all-gather.3.cloned.1.call-start = ((), (), s32[]{:S(2)}) async-start(), calls=%async_computation.12 | async-start | bytes 10027008 | tf_op jit(solution)/shard_map/all_gather | solution.py:687
  24.3 32.4 %all-to-all-start = ((bf16[128,8,384]{2,1,0:T(8,128)(2,1)}), bf16[128,8,384]{2,1,0:T(8,128)(2,1)S(1)}, u32[]{:S(2)}, u32[]{:S(2)}) async-start(bf16[128,8,384]{2,1,0:T(8,128)(2,1)} %bitcast.7), calls=%async_computation | async-start | bytes 1572864 | tf_op jit(solution)/shard_map/all_to_all | solution.py:517
  36.5 47.8 %collective-permute-start.8 = (bf16[2,3,128,512]{3,2,1,0:T(8,128)(2,1)}, bf16[2,3,128,512]{3,2,1,0:T(8,128)(2,1)}, u32[]{:S(2)}, u32[]{:S(2)}) collective-permute-start(bf16[2,3,128,512]{3,2,1,0:T(8,128)(2,1)} %pad_maximum_fusion), channel_id=1, source_target_pairs={{0,16},{16,0},{1,17},{17,1},{2,18},{18,2},{3,19},{19,3},{4,20},{20... | collective-permute-start | bytes 2359304 | tf_op jit(solution)/shard_map/ppermute | solution.py:521
  38.1 38.7 %collective-permute-start.2 = (bf16[2,128,1024]{2,1,0:T(8,128)(2,1)S(1)}, bf16[2,128,1024]{2,1,0:T(8,128)(2,1)}, u32[]{:S(2)}, u32[]{:S(2)}) collective-permute-start(bf16[2,128,1024]{2,1,0:T(8,128)(2,1)S(1)} %pad_maximum_fusion.9.refs_0_), channel_id=1, source_target_pairs={{0,96},{32,0},{64,32},{96,64},{1,97},{33,1},{65,33},{97,65},{2,98}... | collective-permute-start | bytes 1572872 | tf_op jit(solution)/shard_map/ppermute | solution.py:525
  41.5 35.2 %collective-permute-start.3 = (bf16[2,128,1024]{2,1,0:T(8,128)(2,1)S(1)}, bf16[2,128,1024]{2,1,0:T(8,128)(2,1)}, u32[]{:S(2)}, u32[]{:S(2)}) collective-permute-start(bf16[2,128,1024]{2,1,0:T(8,128)(2,1)S(1)} %pad_maximum_fusion.9.refs_0_), channel_id=1, source_target_pairs={{0,64},{32,96},{64,0},{96,32},{1,65},{33,97},{65,1},{97,33},{2,66}... | collective-permute-start | bytes 1572872 | tf_op jit(solution)/shard_map/ppermute | solution.py:525
  41.9 40.3 %collective-permute-start.4 = (bf16[2,128,1024]{2,1,0:T(8,128)(2,1)S(1)}, bf16[2,128,1024]{2,1,0:T(8,128)(2,1)}, u32[]{:S(2)}, u32[]{:S(2)}) collective-permute-start(bf16[2,128,1024]{2,1,0:T(8,128)(2,1)S(1)} %pad_maximum_fusion.9.refs_0_), channel_id=1, source_target_pairs={{0,32},{32,64},{64,96},{96,0},{1,33},{33,65},{65,97},{97,1},{2,34}... | collective-permute-start | bytes 1572872 | tf_op jit(solution)/shard_map/ppermute | solution.py:525
  58.0 62.3 %all-to-all-start.1 = ((bf16[64,8,1024]{2,1,0:T(8,128)(2,1)}), bf16[64,8,1024]{2,1,0:T(8,128)(2,1)}, u32[]{:S(2)}, u32[]{:S(2)}) async-start(bf16[64,8,1024]{2,1,0:T(8,128)(2,1)} %broadcast_in_dim.33), calls=%async_computation.1 | async-start | bytes 2097152 | tf_op jit(solution)/shard_map/all_to_all | solution.py:517
  120.3 34.0 %collective-permute-start.11 = (bf16[64,8,1024]{2,1,0:T(8,128)(2,1)}, bf16[64,8,1024]{2,1,0:T(8,128)(2,1)}, u32[]{:S(2)}, u32[]{:S(2)}) collective-permute-start(bf16[64,8,1024]{2,1,0:T(8,128)(2,1)} %all-to-all-done.1), channel_id=1, source_target_pairs={{0,1},{1,0},{2,3},{3,2},{4,5},{5,4},{6,7},{7,6},{8,9},{9,8},{10,11... | collective-permute-start | bytes 3145736 | tf_op jit(solution)/shard_map/ppermute | solution.py:521
  125.6 26.1 %collective-permute-start.9 = (bf16[2,3,128,512]{3,2,1,0:T(8,128)(2,1)}, bf16[2,3,128,512]{3,2,1,0:T(8,128)(2,1)}, u32[]{:S(2)}, u32[]{:S(2)}) collective-permute-start(bf16[2,3,128,512]{3,2,1,0:T(8,128)(2,1)} %pad_maximum_fusion.1.refs_4_), channel_id=1, source_target_pairs={{0,32},{32,64},{64,96},{96,0},{1,33},{33,65},{65,97},{97,1},{2,34}... | collective-permute-start | bytes 2359304 | tf_op jit(solution)/shard_map/ppermute | solution.py:675
  127.1 25.1 %all-to-all-start.2 = ((bf16[8,256,128]{2,1,0:T(8,128)(2,1)}), bf16[8,256,128]{2,1,0:T(8,128)(2,1)S(1)}, u32[]{:S(2)}, u32[]{:S(2)}) async-start(bf16[8,256,128]{2,1,0:T(8,128)(2,1)} %bitcast.191), calls=%async_computation.2 | async-start | bytes 1048576 | tf_op jit(solution)/shard_map/all_to_all | solution.py:517
  161.2 44.2 %all-to-all-start.3 = ((bf16[8,128,1024]{2,1,0:T(8,128)(2,1)}), bf16[8,128,1024]{2,1,0:T(8,128)(2,1)}, u32[]{:S(2)}, u32[]{:S(2)}) async-start(bf16[8,128,1024]{2,1,0:T(8,128)(2,1)} %broadcast_in_dim.42), calls=%async_computation.3 | async-start | bytes 4194304 | tf_op jit(solution)/shard_map/all_to_all | solution.py:517
  172.9 26.0 %collective-permute-start.12 = (bf16[1,3,128,512]{3,2,1,0:T(8,128)(2,1)S(1)}, bf16[1,3,128,512]{3,2,1,0:T(8,128)(2,1)}, u32[]{:S(2)}, u32[]{:S(2)}) collective-permute-start(bf16[1,3,128,512]{3,2,1,0:T(8,128)(2,1)S(1)} %slice.298), channel_id=1, source_target_pairs={{0,32},{32,64},{64,96},{96,0},{1,33},{33,65},{65,97},{97,1},{2,34}... | collective-permute-start | bytes 1179656 | tf_op jit(solution)/shard_map/ppermute | solution.py:724
  174.0 24.8 %collective-permute-start.13 = (bf16[1,3,128,512]{3,2,1,0:T(8,128)(2,1)S(1)}, bf16[1,3,128,512]{3,2,1,0:T(8,128)(2,1)}, u32[]{:S(2)}, u32[]{:S(2)}) collective-permute-start(bf16[1,3,128,512]{3,2,1,0:T(8,128)(2,1)S(1)} %slice.299), channel_id=1, source_target_pairs={{0,96},{32,0},{64,32},{96,64},{1,97},{33,1},{65,33},{97,65},{2,98}... | collective-permute-start | bytes 1179656 | tf_op jit(solution)/shard_map/ppermute | solution.py:724
  207.0 39.4 %all-to-all-start.4 = ((bf16[8,128,1024]{2,1,0:T(8,128)(2,1)}), bf16[8,128,1024]{2,1,0:T(8,128)(2,1)}, u32[]{:S(2)}, u32[]{:S(2)}) async-start(bf16[8,128,1024]{2,1,0:T(8,128)(2,1)} %broadcast_in_dim.41), calls=%async_computation.4 | async-start | bytes 4194304 | tf_op jit(solution)/shard_map/all_to_all | solution.py:517
  255.2 39.5 %all-to-all-start.5 = ((bf16[8,128,1152]{2,1,0:T(8,128)(2,1)}), bf16[8,128,1152]{2,1,0:T(8,128)(2,1)}, u32[]{:S(2)}, u32[]{:S(2)}) async-start(bf16[8,128,1152]{2,1,0:T(8,128)(2,1)} %add_convert_fusion.1), calls=%async_computation.5 | async-start | bytes 4718592 | tf_op jit(solution)/shard_map/all_to_all | solution.py:517
  303.1 46.0 %all-to-all-start.6 = ((bf16[8,128,1152]{2,1,0:T(8,128)(2,1)}), bf16[8,128,1152]{2,1,0:T(8,128)(2,1)}, u32[]{:S(2)}, u32[]{:S(2)}) async-start(bf16[8,128,1152]{2,1,0:T(8,128)(2,1)} %add_convert_fusion), calls=%async_computation.7 | async-start | bytes 4718592 | tf_op jit(solution)/shard_map/all_to_all | solution.py:517
  312.7 223.4 %reduce-scatter.2.cloned.1.call-start = ((), (), s32[]{:S(2)}) async-start(), calls=%async_computation.11 | async-start | bytes 8912896 | tf_op jit(solution)/shard_map/reduce_scatter | solution.py:795
  329.2 28.5 %collective-permute-start.24 = (bf16[1,3,128,512]{3,2,1,0:T(8,128)(2,1)}, bf16[1,3,128,512]{3,2,1,0:T(8,128)(2,1)}, u32[]{:S(2)}, u32[]{:S(2)}) collective-permute-start(bf16[1,3,128,512]{3,2,1,0:T(8,128)(2,1)} %get-tuple-element.404), channel_id=1, source_target_pairs={{0,32},{32,64},{64,96},{96,0},{1,33},{33,65},{65,97},{97,1},{2,34}... | collective-permute-start | bytes 1179656 | tf_op jit(solution)/shard_map/ppermute | solution.py:558
  329.2 28.4 %collective-permute-start.25 = (bf16[1,3,128,512]{3,2,1,0:T(8,128)(2,1)}, bf16[1,3,128,512]{3,2,1,0:T(8,128)(2,1)}, u32[]{:S(2)}, u32[]{:S(2)}) collective-permute-start(bf16[1,3,128,512]{3,2,1,0:T(8,128)(2,1)} %get-tuple-element.403), channel_id=1, source_target_pairs={{0,96},{32,0},{64,32},{96,64},{1,97},{33,1},{65,33},{97,65},{2,98}... | collective-permute-start | bytes 1179656 | tf_op jit(solution)/shard_map/ppermute | solution.py:558
  380.6 48.0 %collective-permute-start.29 = (bf16[2,3,128,512]{3,2,1,0:T(8,128)(2,1)}, bf16[2,3,128,512]{3,2,1,0:T(8,128)(2,1)}, u32[]{:S(2)}, u32[]{:S(2)}) collective-permute-start(bf16[2,3,128,512]{3,2,1,0:T(8,128)(2,1)} %pad_maximum_fusion.6), channel_id=1, source_target_pairs={{0,96},{32,0},{64,32},{96,64},{1,97},{33,1},{65,33},{97,65},{2,98}... | collective-permute-start | bytes 2359304 | tf_op jit(solution)/shard_map/ppermute | solution.py:564
  383.4 32.5 %collective-permute-start.27 = (bf16[2,3,128,512]{3,2,1,0:T(8,128)(2,1)}, bf16[2,3,128,512]{3,2,1,0:T(8,128)(2,1)}, u32[]{:S(2)}, u32[]{:S(2)}) collective-permute-start(bf16[2,3,128,512]{3,2,1,0:T(8,128)(2,1)} %pad_maximum_fusion.4), channel_id=1, source_target_pairs={{0,96},{32,0},{64,32},{96,64},{1,97},{33,1},{65,33},{97,65},{2,98}... | collective-permute-start | bytes 2359304 | tf_op jit(solution)/shard_map/ppermute | solution.py:564
  386.0 30.0 %collective-permute-start.26 = (bf16[2,3,128,512]{3,2,1,0:T(8,128)(2,1)}, bf16[2,3,128,512]{3,2,1,0:T(8,128)(2,1)}, u32[]{:S(2)}, u32[]{:S(2)}) collective-permute-start(bf16[2,3,128,512]{3,2,1,0:T(8,128)(2,1)} %pad_maximum_fusion.3), channel_id=1, source_target_pairs={{0,32},{32,64},{64,96},{96,0},{1,33},{33,65},{65,97},{97,1},{2,34}... | collective-permute-start | bytes 2359304 | tf_op jit(solution)/shard_map/ppermute | solution.py:563
  389.6 39.0 %collective-permute-start.28 = (bf16[2,3,128,512]{3,2,1,0:T(8,128)(2,1)}, bf16[2,3,128,512]{3,2,1,0:T(8,128)(2,1)}, u32[]{:S(2)}, u32[]{:S(2)}) collective-permute-start(bf16[2,3,128,512]{3,2,1,0:T(8,128)(2,1)} %pad_maximum_fusion.5), channel_id=1, source_target_pairs={{0,32},{32,64},{64,96},{96,0},{1,33},{33,65},{65,97},{97,1},{2,34}... | collective-permute-start | bytes 2359304 | tf_op jit(solution)/shard_map/ppermute | solution.py:563
  431.2 47.2 %collective-permute-start.35 = (bf16[3,128,512]{2,1,0:T(8,128)(2,1)}, bf16[3,128,512]{2,1,0:T(8,128)(2,1)}, u32[]{:S(2)}, u32[]{:S(2)}) collective-permute-start(bf16[3,128,512]{2,1,0:T(8,128)(2,1)} %fusion.13), channel_id=1, source_target_pairs={{0,16},{16,0},{1,17},{17,1},{2,18},{18,2},{3,19},{19,3},{4,20},{20... | collective-permute-start | bytes 1179656 | tf_op jit(solution)/shard_map/ppermute | solution.py:521
  433.1 38.2 %collective-permute-start.30 = (bf16[64,8,1024]{2,1,0:T(8,128)(2,1)}, bf16[64,8,1024]{2,1,0:T(8,128)(2,1)}, u32[]{:S(2)}, u32[]{:S(2)}) collective-permute-start(bf16[64,8,1024]{2,1,0:T(8,128)(2,1)} %dynamic-slice_bitcast_fusion), channel_id=1, source_target_pairs={{0,1},{1,0},{2,3},{3,2},{4,5},{5,4},{6,7},{7,6},{8,9},{9,8},{10,11... | collective-permute-start | bytes 3145736 | tf_op jit(solution)/shard_map/ppermute | solution.py:521
  434.1 35.7 %collective-permute-start.37 = (bf16[2,128,1024]{2,1,0:T(8,128)(2,1)}, bf16[2,128,1024]{2,1,0:T(8,128)(2,1)}, u32[]{:S(2)}, u32[]{:S(2)}) collective-permute-start(bf16[2,128,1024]{2,1,0:T(8,128)(2,1)} %copy-done.41), channel_id=1, source_target_pairs={{0,64},{32,96},{64,0},{96,32},{1,65},{33,97},{65,1},{97,33},{2,66}... | collective-permute-start | bytes 1572872 | tf_op jit(solution)/shard_map/ppermute | solution.py:525
  438.0 31.8 %collective-permute-start.38 = (bf16[2,128,1024]{2,1,0:T(8,128)(2,1)}, bf16[2,128,1024]{2,1,0:T(8,128)(2,1)}, u32[]{:S(2)}, u32[]{:S(2)}) collective-permute-start(bf16[2,128,1024]{2,1,0:T(8,128)(2,1)} %copy-done.40), channel_id=1, source_target_pairs={{0,96},{32,0},{64,32},{96,64},{1,97},{33,1},{65,33},{97,65},{2,98}... | collective-permute-start | bytes 1572872 | tf_op jit(solution)/shard_map/ppermute | solution.py:525
  443.2 53.7 %all-to-all-start.8 = ((bf16[128,8,384]{2,1,0:T(8,128)(2,1)}), bf16[128,8,384]{2,1,0:T(8,128)(2,1)}, u32[]{:S(2)}, u32[]{:S(2)}) async-start(bf16[128,8,384]{2,1,0:T(8,128)(2,1)} %pad_maximum_fusion.7), calls=%async_computation.9 | async-start | bytes 1572864 | tf_op jit(solution)/shard_map/all_to_all | solution.py:517
  469.9 25.4 %collective-permute-start.31 = (bf16[2,128,1024]{2,1,0:T(8,128)(2,1)S(1)}, bf16[2,128,1024]{2,1,0:T(8,128)(2,1)S(1)}, u32[]{:S(2)}, u32[]{:S(2)}) collective-permute-start(bf16[2,128,1024]{2,1,0:T(8,128)(2,1)S(1)} %copy-done.39), channel_id=1, source_target_pairs={{0,32},{32,64},{64,96},{96,0},{1,33},{33,65},{65,97},{97,1},{2,34}... | collective-permute-start | bytes 1572872 | tf_op jit(solution)/shard_map/ppermute | solution.py:525
  469.9 25.4 %collective-permute-start.32 = (bf16[2,128,1024]{2,1,0:T(8,128)(2,1)S(1)}, bf16[2,128,1024]{2,1,0:T(8,128)(2,1)S(1)}, u32[]{:S(2)}, u32[]{:S(2)}) collective-permute-start(bf16[2,128,1024]{2,1,0:T(8,128)(2,1)S(1)} %copy-done.37), channel_id=1, source_target_pairs={{0,64},{32,96},{64,0},{96,32},{1,65},{33,97},{65,1},{97,33},{2,66}... | collective-permute-start | bytes 1572872 | tf_op jit(solution)/shard_map/ppermute | solution.py:525
  471.3 25.6 %collective-permute-start.33 = (bf16[2,128,1024]{2,1,0:T(8,128)(2,1)S(1)}, bf16[2,128,1024]{2,1,0:T(8,128)(2,1)}, u32[]{:S(2)}, u32[]{:S(2)}) collective-permute-start(bf16[2,128,1024]{2,1,0:T(8,128)(2,1)S(1)} %copy-done.35), channel_id=1, source_target_pairs={{0,96},{32,0},{64,32},{96,64},{1,97},{33,1},{65,33},{97,65},{2,98}... | collective-permute-start | bytes 1572872 | tf_op jit(solution)/shard_map/ppermute | solution.py:525
  503.2 27.8 %all-to-all-start.9 = ((bf16[64,8,1024]{2,1,0:T(8,128)(2,1)}), bf16[64,8,1024]{2,1,0:T(8,128)(2,1)}, u32[]{:S(2)}, u32[]{:S(2)}) async-start(bf16[64,8,1024]{2,1,0:T(8,128)(2,1)} %fusion), calls=%async_computation.10 | async-start | bytes 2097152 | tf_op jit(solution)/shard_map/all_to_all | solution.py:517
  (111 other events, 1211.2 us)
Sparse Core Ops, SparseCore 0:
  22.2 97.8 all-gather.2
  317.9 108.1 reduce-scatter.1

commit v15 on v14

--- a/solution.py
+++ b/solution.py
@@ -123,33 +123,13 @@
         )
 
 
-def attend_back_kernel(
-    order_ref,
-    hidden_ref,
-    q_ref,
-    kv_ref,
-    d_mixed_ref,
-    gain_ref,
-    w_ref,
-    head_gain_ref,
-    cos_ref,
-    sin_ref,
-    seg_col_ref,
-    seg_row_ref,
-    d_hidden_0_ref,
-    d_hidden_1_ref,
-    d_hidden_2_ref,
-    d_hidden_3_ref,
-    grad_w_ref,
-    grad_gain_ref,
-    grad_heads_ref,
-    keys_ref,
-    values_ref,
-    d_q_ref,
-    d_k_ref,
-    d_v_ref,
-    d_raw_ref,
-):
+def attend_back_kernel(order_ref, *refs, again):
+    hidden_ref, q_ref, kv_ref, d_mixed_ref, gain_ref, w_ref, head_gain_ref = refs[:7]
+    cos_ref, sin_ref, seg_col_ref, seg_row_ref = refs[7:11]
+    refs = refs[15:] if again else refs[11:]
+    outs, refs = refs[:4], refs[4:]
+    grad_w_ref, grad_gain_ref, grad_heads_ref = refs[:3]
+    keys_ref, values_ref, d_q_ref, d_k_ref, d_v_ref, d_raw_ref = refs[3:]
     length = hidden_ref.shape[0]
     kv = kv_ref[...].astype(F32)
     keys_ref[...] = both_halves(kv, False).astype(BF)
@@ -199,14 +179,13 @@
         d_raw_ref[:, lanes] = d.astype(BF)
     grad_w_ref[...] = dot(hidden_ref[...], d_raw_ref[...], 0, 0)
     total = jnp.zeros(grad_gain_ref.shape, F32)
-    outs = (d_hidden_0_ref, d_hidden_1_ref, d_hidden_2_ref, d_hidden_3_ref)
     tok = length // 8
     for step in range(4):
         rows = pl.ds(pl.multiple_of(order_ref[2 * step] // 2 * (2 * tok), 2 * tok), 2 * tok)
         d_hidden = dot(d_raw_ref[rows], w_ref[...], 1, 1)
         own = order_ref[0] % 2
-        outs[step][own] = d_hidden[:tok].astype(BF)
-        outs[step][1 - own] = d_hidden[tok:].astype(BF)
+        outs[step][0, own] = d_hidden[:tok].astype(BF)
+        outs[step][0, 1 - own] = d_hidden[tok:].astype(BF)
         total = total + jnp.sum(d_hidden * hidden_ref[rows].astype(F32), axis=0, keepdims=True)
     grad_gain_ref[...] = total / gain_ref[...]
 
@@ -238,29 +217,32 @@
     )(order, *args)
 
 
-def attend_backward(
-    order, hidden, q, kv, d_mixed, gain, w_heads, head_gain, cosine, sine, seg_col, seg_row
-):
-    length, width = hidden.shape
+def attend_backward(micro, held, order, *args):
+    length, width = args[0].shape
     shape = jax.ShapeDtypeStruct
-    outs = [shape((2, length // 8, width), BF)] * 4 + [
+    outs = [shape((2, 2, length // 8, width), BF)] * 4 + [
         shape((width, 256), F32),
         shape((1, width), F32),
         shape((1, 256), F32),
     ]
-    args = [hidden, q, kv, d_mixed, gain, w_heads, head_gain, cosine, sine, seg_col, seg_row]
+    part = pl.BlockSpec(
+        (1, 2, length // 8, width), lambda i: (micro, 0, 0, 0), pipeline_mode=pl.Buffered(1)
+    )
     return pl.pallas_call(
-        attend_back_kernel,
+        functools.partial(attend_back_kernel, again=len(held) > 0),
         out_shape=outs,
         grid=(1,),
-        in_specs=[pl.BlockSpec(memory_space=pltpu.SMEM)] + [whole(a) for a in args],
-        out_specs=[whole(o) for o in outs],
+        in_specs=[pl.BlockSpec(memory_space=pltpu.SMEM)]
+        + [whole(a) for a in args]
+        + [pl.BlockSpec(memory_space=pl.ANY)] * len(held),
+        out_specs=[part] * 4 + [whole(o) for o in outs[4:]],
+        input_output_aliases={1 + len(args) + n: n for n in range(len(held))},
         scratch_shapes=[pltpu.VMEM((length, 128), BF)] * 2
         + [pltpu.VMEM((length, 128), F32)] * 3
         + [pltpu.VMEM((length, 256), BF)],
         compiler_params=pltpu.CompilerParams(vmem_limit_bytes=40 * 1024 * 1024),
         cost_estimate=COST,
-    )(order, *args)
+    )(order, *args, *held)
 
 
 def halves(v):
@@ -270,7 +252,7 @@
 
 def expert_kernel(scalar_ref, *refs, again):
     x_own_ref, x_other_ref, g_ref, router_ref = refs[:4]
-    pieces, refs = (refs[4:9], refs[9:14]), refs[14:]
+    pieces, refs = refs[4:9], refs[9:]
     if again:
         refs = refs[1:]
     out_ref, back_own_ref, back_other_ref = refs[:3]
@@ -283,14 +265,11 @@
     depth = w_ref.shape[2] // 8
 
     loads = []
-    for e in range(2):
-        blocks = [(ref, i) for ref in pieces[e] for i in range(ref.shape[0])]
-        for r, (ref, i) in enumerate(blocks):
-            rows = pl.ds(pl.multiple_of(scalar_ref[2 + r] * depth, depth), depth)
-            loads.append(
-                pltpu.make_async_copy(ref.at[i], w_ref.at[e, :, rows], in_sem.at[8 * e + r])
-            )
-            loads[-1].start()
+    blocks = [(ref, i) for ref in pieces for i in range(ref.shape[0])]
+    for r, (ref, i) in enumerate(blocks):
+        rows = pl.ds(pl.multiple_of(scalar_ref[2 + r] * depth, depth), depth)
+        loads.append(pltpu.make_async_copy(ref.at[i], w_ref.at[:, :, rows], in_sem.at[r]))
+        loads[-1].start()
     local, slots, hidden = act_ref.shape
     cap = slots // sources
     first = scalar_ref[0]
@@ -402,7 +381,7 @@
 def run_experts(scalars, x_own, x_other, g_all, micro, router, pieces, cap, moe=None):
     half, tok, width = x_own.shape
     sources = 2 * half
-    local, hidden = len(pieces), pieces[0][0].shape[3]
+    _, local, _, _, hidden = pieces[0].shape
     slots = sources * cap
     wide = g_all.shape[2]
     shape = jax.ShapeDtypeStruct
@@ -419,7 +398,7 @@
     g_spec = pl.BlockSpec(
         (sources, tok, wide), lambda i: (0, micro, 0), pipeline_mode=pl.Buffered(1)
     )
-    args = [*pieces[0], *pieces[1]]
+    args = list(pieces)
     any_place = pl.BlockSpec(memory_space=pl.ANY)
     held = [] if moe is None else [moe]
     moe_spec = pl.BlockSpec(
@@ -442,7 +421,7 @@
             pltpu.VMEM((local, slots, width), BF),
             pltpu.VMEM((local, slots, width), BF),
             pltpu.VMEM((local, 3, width, hidden), BF),
-            pltpu.SemaphoreType.DMA((16,)),
+            pltpu.SemaphoreType.DMA((8,)),
             pltpu.SemaphoreType.DMA((5,)),
         ],
         compiler_params=pltpu.CompilerParams(vmem_limit_bytes=60 * 1024 * 1024),
@@ -455,32 +434,35 @@
     left = (kept[0:2], kept[0:2], kept[2:4])
     right = (kept[6:8], kept[8:10], kept[4:6])
     step = pl.program_id(0)
-    depth = outs[0].shape[2]
+    depth = outs[0].shape[3]
     for kind in range(3):
 
-        @pl.when(step == kind)
+        @pl.when(step % 3 == kind)
         def _(kind=kind):
             total = dot(left[kind][0][0], right[kind][0][0], 0, 0)
             total_ref[...] = total + dot(left[kind][1][0], right[kind][1][0], 0, 0)
 
     for r in range(8):
         rows = pl.ds(pl.multiple_of(order_ref[r] * depth, depth), depth)
-        outs[r // 2][r % 2, 0] = total_ref[rows].astype(BF)
-
-
-def expert_grads(order, kept, expert):
-    _, slots, width = kept[0][0].shape
+        outs[r // 2][r % 2, 0, 0] = total_ref[rows].astype(BF)
+
+
+def expert_grads(order, kept):
+    local, slots, width = kept[0][0].shape
     hidden = kept[0][2].shape[2]
     args = [kept[m][i] for i in range(5) for m in range(2)]
     depth = width // 8
     shape = jax.ShapeDtypeStruct
     return pl.pallas_call(
         expert_grad_kernel,
-        out_shape=[shape((2, 3, depth, hidden), BF)] * 4,
-        grid=(3,),
+        out_shape=[shape((2, local, 3, depth, hidden), BF)] * 4,
+        grid=(3 * local,),
         in_specs=[pl.BlockSpec(memory_space=pltpu.SMEM)]
-        + [pl.BlockSpec((1,) + a.shape[1:], lambda i: (expert, 0, 0)) for a in args],
-        out_specs=[pl.BlockSpec((2, 1, depth, hidden), lambda i: (0, i, 0, 0))] * 4,
+        + [pl.BlockSpec((1,) + a.shape[1:], lambda i: (i // 3, 0, 0)) for a in args],
+        out_specs=[
+            pl.BlockSpec((2, 1, 1, depth, hidden), lambda i: (0, i // 3, i % 3, 0, 0))
+        ]
+        * 4,
         scratch_shapes=[pltpu.VMEM((width, hidden), F32)],
         compiler_params=pltpu.CompilerParams(vmem_limit_bytes=48 * 1024 * 1024),
         cost_estimate=COST,
@@ -649,7 +631,7 @@
     both_w = jnp.stack([w_gate, w_up, w_down], axis=1)
     head_all = exchange(pieces.reshape((n_all,) + pieces.shape[2:]), ALL).reshape(width, -1)
     other_w = flip(both_w, "yl")
-    both_w = [jnp.stack([both_w[e], other_w[e]]) for e in range(local)]
+    both_w = jnp.stack([both_w, other_w])
     seq_rows = [along_z(both_0)]
     seq_rows.append(along_z(after_all(both_1, *seq_rows[0][1:])))
     head_all = after_all(head_all, *seq_rows[0][1:], other_w)
@@ -666,14 +648,11 @@
     )[None]
     router_pad = jnp.pad(router, ((0, 0), (0, 128 - experts)))
 
-    out_own = exchange.copies(w_out, CTX + GROUP, n_all // 2)
-
-    moved_w = []
-    last = seq_rows[1][1:]
-    for e in range(local):
-        block = after_all(both_w[e], *last)
-        last = [lax.ppermute(block, "z", UP), lax.ppermute(block, "z", DOWN)]
-        moved_w.append(last)
+    out_own = exchange.copies(after_all(w_out, *seq_rows[0][1:]), CTX + GROUP, n_all // 2)
+
+    both_w = after_all(both_w, *seq_rows[1][1:])
+    w_before = lax.ppermute(both_w, "z", UP)
+    w_after = lax.ppermute(both_w, "z", DOWN)
 
     expert_ids = jnp.arange(experts, dtype=jnp.int32)
     cot = cotangent.reshape(all_tok, width)
@@ -708,7 +687,7 @@
     out_other = flip(out_own, "core")
     mixed = jnp.stack([mixed_0, mixed_1]).reshape(micro, n_ctx, tok, heads).transpose(1, 0, 2, 3)
     mixed = exchange(mixed.reshape(n_ctx, all_tok, heads), CTX)
-    mixed, moved_w[0] = lax.optimization_barrier((mixed, moved_w[0]))
+    mixed, w_before, w_after = lax.optimization_barrier((mixed, w_before, w_after))
     mixed = mixed.transpose(1, 0, 2).reshape(all_tok, width)
     out_full = jnp.where(
         core == 0,
@@ -719,10 +698,8 @@
     inv_two = lax.rsqrt(jnp.mean(middle * middle, axis=-1, keepdims=True) + EPS)
     hidden_two = (middle * inv_two * gain_mlp).astype(BF)
     x_0 = exchange.copies(hidden_two[:tok], GROUP, n_ctx)
-    weights = []
-    for e, (w_before, w_after) in enumerate(moved_w):
-        w_far = [lax.ppermute(w_before[:1], "z", UP), lax.ppermute(w_after[1:], "z", DOWN)]
-        weights.append([both_w[e], w_after, *w_far, w_before])
+    w_far = [lax.ppermute(w_before[:1], "z", UP), lax.ppermute(w_after[1:], "z", DOWN)]
+    weights = [both_w, w_after, *w_far, w_before]
     x_0, weights = lax.optimization_barrier((x_0, weights))
     x_1 = exchange.copies(hidden_two[tok:], GROUP, n_ctx)
     logits = jnp.where(chosen, mm(hidden_two, router), -1e30)
@@ -774,9 +751,9 @@
         grad_pack = jnp.concatenate([grad_heads, grad_small], axis=1).astype(BF)
         return grad_pack.reshape(n_all, rows, -1)
 
-    def attention_back(m, d_mixed):
+    def attention_back(m, d_mixed, held):
         *d_hidden, grad_heads, grad_attn, grad_qk = attend_backward(
-            order, *saved[m], d_mixed.reshape(length, heads), *attention_args(m)
+            m, held, order, *saved[m], d_mixed.reshape(length, heads), *attention_args(m)
         )
         grad_qk = jnp.concatenate(
             [grad_qk[0, :DH] + grad_qk[0, DH : 2 * DH], grad_qk[0, 2 * DH : 3 * DH]]
@@ -796,8 +773,8 @@
     back_1 = back_sum(back_own, back_other)
     kept_1[0], back_1 = lax.optimization_barrier((kept_1[0], back_1))
     back_1 = exchange(back_1, GROUP)
-    parts = [expert_grads(order, (kept_0, kept_1), e) for e in range(local)]
-    far = [relay(part[2]) for part in parts]
+    parts = expert_grads(order, (kept_0, kept_1))
+    far = relay(parts[2])
     back_1, parts = lax.optimization_barrier((back_1, parts))
     d_middle, d_mixed, d_rows = middle_back(
         jnp.concatenate([sum_parts(back_0), sum_parts(back_1)], axis=0)
@@ -805,16 +782,12 @@
     d_mixed, far = lax.optimization_barrier((d_mixed, far))
     d_mixed = exchange(d_mixed, CTX)
     d_mixed, far = lax.optimization_barrier((d_mixed, far))
-    moved = [ring_sums(part, f) for part, f in zip(parts, far)]
+    moved = ring_sums(parts, far)
     d_mixed = d_mixed.reshape(n_ctx, micro, tok, heads)
-    d_hidden_0, head_grads_0 = attention_back(0, d_mixed[:, 0])
-    d_hidden_0, d_mixed, moved[0] = lax.optimization_barrier((d_hidden_0, d_mixed, moved[0]))
-    d_hidden_1, head_grads_1 = attention_back(1, d_mixed[:, 1])
-    d_hidden_1, d_hidden_0, moved[1], d_rows = lax.optimization_barrier(
-        (d_hidden_1, d_hidden_0, moved[1], d_rows)
-    )
-    hidden_moved_0 = by_z(d_hidden_0)
-    hidden_moved_1 = by_z(d_hidden_1)
+    d_hidden, head_grads_0 = attention_back(0, d_mixed[:, 0], [])
+    d_hidden, head_grads_1 = attention_back(1, d_mixed[:, 1], d_hidden)
+    d_hidden, moved, d_rows = lax.optimization_barrier((d_hidden, moved, d_rows))
+    hidden_moved = by_z(d_hidden)
     grad_out, grad_router, grad_mlp = weight_grads(*d_rows)
     grad_heads, grad_attn, grad_qk = jax.tree.map(jnp.add, head_grads_0, head_grads_1)
     grad_pack = pack_grads(grad_heads, grad_router, grad_attn, grad_mlp, grad_qk)
@@ -823,16 +796,14 @@
     grad_own = lax.dynamic_index_in_dim(grad_out, core, axis=1, keepdims=False)
     grad_other = lax.dynamic_index_in_dim(grad_out, 1 - core, axis=1, keepdims=False)
     grad_out = back_sum(grad_own, grad_other)
-    weight_sums = [pair_sums(p, q) for p, q in zip(parts, moved)]
-    weight_yl = [flip(sums[1].astype(BF), "yl") for sums in weight_sums]
-    grad_pack, grad_out, hidden_moved_0, weight_yl = lax.optimization_barrier(
-        (grad_pack, grad_out, hidden_moved_0, weight_yl)
-    )
+    weight_sums = pair_sums(parts, moved)
+    weight_yl = flip(weight_sums[1].astype(BF), "yl")
+    grad_pack, grad_out, weight_yl = lax.optimization_barrier((grad_pack, grad_out, weight_yl))
     exchange.last = grad_pack
     grad_out = exchange(grad_out, CTX + GROUP)
-    hidden_sums_0 = pair_sums(d_hidden_0, hidden_moved_0)
-    hidden_sums_1 = pair_sums(d_hidden_1, hidden_moved_1)
-    hidden_sums = [jnp.stack(sums) for sums in zip(hidden_sums_0, hidden_sums_1)]
+    hidden_sums = [
+        sum(part[:, i].astype(F32) for part in [d_hidden[0]] + hidden_moved) for i in range(2)
+    ]
     hidden_yl = flip(hidden_sums[1].astype(BF), "yl")
     grad_out, hidden_yl = lax.optimization_barrier((grad_out, hidden_yl))
 
@@ -843,7 +814,7 @@
     own_out = sum_parts(grad_out)
     moe = after_all(moe, grad_pack)
     d_hidden = (hidden_sums[0] + hidden_yl.astype(F32)).reshape(all_tok, width)
-    expert_own = [sums[0] + other.astype(F32) for sums, other in zip(weight_sums, weight_yl)]
+    expert_own = weight_sums[0] + weight_yl.astype(F32)
     out = (middle.reshape(moe.shape) + moe.astype(F32)).astype(BF)
     start = tokens.reshape(all_tok, width).astype(F32)
     inv_one = lax.rsqrt(jnp.mean(start * start, axis=-1, keepdims=True) + EPS)
@@ -865,9 +836,9 @@
         own_small[:, experts],
         own_small[:, experts + 1],
         own_small[:1, experts + 2],
-        jnp.stack([part[0] for part in expert_own]),
-        jnp.stack([part[1] for part in expert_own]),
-        jnp.stack([part[2] for part in expert_own]),
+        expert_own[:, 0],
+        expert_own[:, 1],
+        expert_own[:, 2],
     )
 
 

time: 553 us -> 549 us (level)
  waiting for transfers between devices: 156 us -> 174 us
  starting transfers between devices: 118 us -> 103 us
  other arithmetic: 70.5 us -> 63.3 us
    all_to_all x10, waiting for transfers between devices: 35.5 us -> 77.5 us  [swap(): return lax.all_to_all(parts, axis, split_axis=0, concat_axis=0, tiled=True)]
    ppermute x4 -> x2, waiting for transfers between devices: 31.4 us -> 0.01 us  [the longest x1 0.01 us: body(): w_before = lax.ppermute(both_w, 'z', UP)]
    ppermute x2 -> x1, waiting for transfers between devices: 10.9 us -> 15.5 us  [body(): lax.ppermute(w_before[:1], 'z', UP)]
    ppermute x12 -> x9, starting transfers between devices: 14.9 us -> 12.2 us  [by_z(): lax.ppermute(parts[k], 'z', perm)]
    ppermute x12 -> x9, waiting for transfers between devices: 54.6 us -> 56.2 us  [by_z(): lax.ppermute(parts[k], 'z', perm)]
    ppermute x12 -> x11, waiting for transfers between devices: 17.6 us -> 18.6 us  [flip(): return lax.ppermute(block, axis, FLIP)]
    pallas_call x4 -> x3, Pallas kernels: 44 us -> 45 us  [the longest x2 24.4 us: attend_backward(): pl.pallas_call(functools.partial(attend_back_kernel, again=len(held) > 0)...]
    unnamed x184 -> x146, local copies, waits for them, and re-layouts: 23.4 us -> 22.8 us
  transfers between devices with their start and end apart: 52 -> 40, of which waited for: 21 -> 19; matrix products, arithmetic and copies ran while one was open for 19% -> 18% of each run, Pallas kernels for 22% -> 22%
where the time goes in v15:
time: 549 us; the launch traced here: 541 us
  waiting for transfers between devices  174 us (32%)
  Pallas kernels  121 us (22%)
  starting transfers between devices  103 us (19%)
  other arithmetic  63.3 us (12%)
  local copies, waits for them, and re-layouts  55.9 us (10%)
  between operations  16.1 us (3%)
  matrix products  7.45 us (1%)
    all_to_all x10, waiting for transfers between devices, swap(): return lax.all_to_all(parts, axis, split_axis=0, concat_axis=0, tiled=True)  77.5 us
    all_to_all x10, starting transfers between devices, swap(): return lax.all_to_all(parts, axis, split_axis=0, concat_axis=0, tiled=True)  73.4 us
    pallas_call x2, Pallas kernels, run_experts(): pl.pallas_call(functools.partial(expert_kernel, again=moe is not None), o...  59.4 us
    ppermute x9, waiting for transfers between devices, by_z(): lax.ppermute(parts[k], 'z', perm)  56.2 us
    pallas_call x2, Pallas kernels, attend_backward(): pl.pallas_call(functools.partial(attend_back_kernel, again=len(held) > 0)...  24.4 us
    unnamed x146, local copies, waits for them, and re-layouts  22.8 us
    pallas_call x1, Pallas kernels, expert_grads(): pl.pallas_call(expert_grad_kernel, out_shape=[shape((2, local, 3, depth,...  20.6 us
    ppermute x11, waiting for transfers between devices, flip(): return lax.ppermute(block, axis, FLIP)  18.6 us
  transfers between devices with their start and end apart: 40, of which 19 were waited for; matrix products, arithmetic and copies ran while one was open for 18% of the time, Pallas kernels for 22%

profile of v15, /device:TPU:0, one launch (start us, length us, event | category | flops | bytes accessed | tf_op | source)
XLA Modules:
  0.0 540.9 jit_solution(11008368088976597212)
XLA Ops:
  12.6 5.1 collective-permute-done
  17.7 4.3 collective-permute-done.4
  24.4 11.7 %all-to-all-start = ((bf16[128,8,384]{2,1,0:T(8,128)(2,1)}), bf16[128,8,384]{2,1,0:T(8,128)(2,1)}, u32[]{:S(2)}, u32[]{:S(2)}) async-start(bf16[128,8,384]{2,1,0:T(8,128)(2,1)} %bitcast.8), calls=%async_computation | async-start | bytes 1572864 | tf_op jit(solution)/shard_map/all_to_all | solution.py:499
  43.8 24.5 %collective-permute-done.1.refs_1_ = bf16[2,128,1024]{2,1,0:T(8,128)(2,1)S(1)} collective-permute-done((bf16[2,128,1024]{2,1,0:T(8,128)(2,1)S(1)}, bf16[2,128,1024]{2,1,0:T(8,128)(2,1)S(1)}, u32[]{:S(2)}, u32[]{:S(2)}) %collective-permute-start.1) | collective-permute-done | bytes 524320 | tf_op jit(solution)/shard_map/ppermute | solution.py:507
  72.9 6.8 %all-to-all-start.1 = ((bf16[64,8,1024]{2,1,0:T(8,128)(2,1)}), bf16[64,8,1024]{2,1,0:T(8,128)(2,1)}, u32[]{:S(2)}, u32[]{:S(2)}) async-start(bf16[64,8,1024]{2,1,0:T(8,128)(2,1)} %broadcast_in_dim.33), calls=%async_computation.1 | async-start | bytes 2097152 | tf_op jit(solution)/shard_map/all_to_all | solution.py:499
  90.1 24.9 %collective-permute-done.5.refs_1_ = bf16[2,128,1024]{2,1,0:T(8,128)(2,1)} collective-permute-done((bf16[2,128,1024]{2,1,0:T(8,128)(2,1)S(1)}, bf16[2,128,1024]{2,1,0:T(8,128)(2,1)}, u32[]{:S(2)}, u32[]{:S(2)}) %collective-permute-start.5) | collective-permute-done | bytes 524320 | tf_op jit(solution)/shard_map/ppermute | solution.py:507
  126.2 7.9 %shard_map.246 = (bf16[1024,128]{1,0:T(8,128)(2,1)S(1)}, bf16[1024,1024]{1,0:T(8,128)(2,1)S(1)}, bf16[1024,128]{1,0:T(8,128)(2,1)S(1)}, bf16[1024,128]{1,0:T(8,128)(2,1)S(1)}) custom-call(s32[8]{0:T(128)S(1)} %fusion.30.order_ref, bf16[2,128,1024]{2,1,0:T(8,128)(2,1)S(1)} %copy-done.7, bf16[2,128,1024]{2,1,0:T(8,128)(2,1)S(1)} %copy-done.19, ...), custom_call_target="tpu_custom_call" | custom-call | flops 10000000 | bytes 100000 | tf_op jit(solution)/shard_map/pallas_call | solution.py:208
  137.6 8.9 %shard_map.247 = (bf16[1024,128]{1,0:T(8,128)(2,1)S(1)}, bf16[1024,1024]{1,0:T(8,128)(2,1)S(1)}, bf16[1024,128]{1,0:T(8,128)(2,1)S(1)}, bf16[1024,128]{1,0:T(8,128)(2,1)S(1)}) custom-call(s32[8]{0:T(128)S(1)} %fusion.30.order_ref, bf16[2,128,1024]{2,1,0:T(8,128)(2,1)S(1)} %pad_maximum_fusion.6.refs_0_, bf16[2,128,1024]{2,1,0:T(8,128)(2,1)} %collective-permute-done.5.refs_1_, ...), custom_call_target="tpu_custom_call" | custom-call | flops 10000000 | bytes 100000 | tf_op jit(solution)/shard_map/pallas_call | solution.py:208
  151.2 4.1 all-to-all-start.2
  156.4 4.0 maximum_select_fusion
  160.4 5.9 %all-to-all-done.2 = bf16[8,256,128]{2,1,0:T(8,128)(2,1)} async-done(((bf16[8,256,128]{2,1,0:T(8,128)(2,1)}), bf16[8,256,128]{2,1,0:T(8,128)(2,1)}, u32[]{:S(2)}, u32[]{:S(2)}) %all-to-all-start.2) | async-done | bytes 524320 | tf_op jit(solution)/shard_map/all_to_all | solution.py:499
  174.0 5.1 all-to-all-start.3
  184.9 15.5 %collective-permute-done.12.refs_6_ = bf16[1,2,3,128,512]{4,3,2,1,0:T(8,128)(2,1)} collective-permute-done((bf16[1,2,3,128,512]{4,3,2,1,0:T(8,128)(2,1)S(1)}, bf16[1,2,3,128,512]{4,3,2,1,0:T(8,128)(2,1)}, u32[]{:S(2)}, u32[]{:S(2)}) %collective-permute-start.12) | collective-permute-done | bytes 786464 | tf_op jit(solution)/shard_map/ppermute | solution.py:701
  200.8 6.5 %all-to-all-done.3.refs_0_ = bf16[8,128,1024]{2,1,0:T(8,128)(2,1)} async-done(((bf16[8,128,1024]{2,1,0:T(8,128)(2,1)}), bf16[8,128,1024]{2,1,0:T(8,128)(2,1)}, u32[]{:S(2)}, u32[]{:S(2)}) %all-to-all-start.3) | async-done | bytes 2097184 | tf_op jit(solution)/shard_map/all_to_all | solution.py:499
  209.9 4.6 all-to-all-start.4
  216.8 29.7 %shard_map.248 = (bf16[16,2,128,1024]{3,2,1,0:T(8,128)(2,1)}, bf16[8,128,1152]{2,1,0:T(8,128)(2,1)}, bf16[8,128,1152]{2,1,0:T(8,128)(2,1)}, bf16[2,768,1024]{2,1...) custom-call(s32[10]{0:T(128)} %pad_add_fusion.scalar_ref, ...), custom_call_target="tpu_custom_call" | custom-call | flops 10000000 | bytes 100000 | tf_op jit(solution)/shard_map/pallas_call | solution.py:407
  246.9 4.4 collective-permute-done.15
  255.4 7.0 %all-to-all-start.5 = ((bf16[8,128,1152]{2,1,0:T(8,128)(2,1)}), bf16[8,128,1152]{2,1,0:T(8,128)(2,1)}, u32[]{:S(2)}, u32[]{:S(2)}) async-start(bf16[8,128,1152]{2,1,0:T(8,128)(2,1)} %add_convert_fusion.1), calls=%async_computation.5 | async-start | bytes 4718592 | tf_op jit(solution)/shard_map/all_to_all | solution.py:499
  262.6 29.7 %shard_map.249 = (bf16[16,2,128,1024]{3,2,1,0:T(8,128)(2,1)}, bf16[8,128,1152]{2,1,0:T(8,128)(2,1)}, bf16[8,128,1152]{2,1,0:T(8,128)(2,1)}, bf16[2,768,1024]{2,1...) custom-call(s32[10]{0:T(128)} %pad_add_fusion.scalar_ref, ...), custom_call_target="tpu_custom_call", output_to_operand_aliasing={{0}: (10, {})} | custom-call | flops 10000000 | bytes 100000 | tf_op jit(solution)/shard_map/pallas_call | solution.py:407
  294.3 4.8 collective-permute-done.17
  299.1 4.4 add_convert_fusion
  303.5 10.1 %all-to-all-start.6 = ((bf16[8,128,1152]{2,1,0:T(8,128)(2,1)}), bf16[8,128,1152]{2,1,0:T(8,128)(2,1)}, u32[]{:S(2)}, u32[]{:S(2)}) async-start(bf16[8,128,1152]{2,1,0:T(8,128)(2,1)} %add_convert_fusion), calls=%async_computation.7 | async-start | bytes 4718592 | tf_op jit(solution)/shard_map/all_to_all | solution.py:499
  318.9 20.6 %shard_map.250 = (bf16[2,2,3,128,512]{4,3,2,1,0:T(8,128)(2,1)S(1)}, bf16[2,2,3,128,512]{4,3,2,1,0:T(8,128)(2,1)S(1)}, bf16[2,2,3,128,512]{4,3,2,1,0:T(8,128)(2,1)S(1)}, bf16[2,2,3,128,512]{4,3,2,1,0:T(8,128)(2,1)}) custom-call(s32[8]{0:T(128)S(1)} %fusion.30.order_ref, bf16[2,768,1024]{2,1,0:T(8,128)(2,1)} %get-tuple-element.170.refs_0_, ...), custom_call_target="tpu_custom_call" | custom-call | flops 10000000 | bytes 100000 | tf_op jit(solution)/shard_map/pallas_call | solution.py:456
  344.8 4.5 all-to-all-done.6
  362.4 5.2 all-to-all-start.7
  370.9 12.7 %all-to-all-done.7 = bf16[8,256,128]{2,1,0:T(8,128)(2,1)S(1)} async-done(((bf16[8,256,128]{2,1,0:T(8,128)(2,1)}), bf16[8,256,128]{2,1,0:T(8,128)(2,1)S(1)}, u32[]{:S(2)}, u32[]{:S(2)}) %all-to-all-start.7) | async-done | bytes 524320 | tf_op jit(solution)/shard_map/all_to_all | solution.py:499
  394.4 12.1 %shard_map.251 = (bf16[2,2,128,1024]{3,2,1,0:T(8,128)(2,1)S(1)}, bf16[2,2,128,1024]{3,2,1,0:T(8,128)(2,1)S(1)}, bf16[2,2,128,1024]{3,2,1,0:T(8,128)(2,1)S(1)}, b...) custom-call(s32[8]{0:T(128)S(1)} %fusion.30.order_ref, ...), custom_call_target="tpu_custom_call" | custom-call | flops 10000000 | bytes 100000 | tf_op jit(solution)/shard_map/pallas_call | solution.py:231
  406.4 12.3 %shard_map.252 = (bf16[2,2,128,1024]{3,2,1,0:T(8,128)(2,1)S(1)}, bf16[2,2,128,1024]{3,2,1,0:T(8,128)(2,1)S(1)}, bf16[2,2,128,1024]{3,2,1,0:T(8,128)(2,1)S(1)}, b...) custom-call(s32[8]{0:T(128)S(1)} %fusion.30.order_ref, ...), custom_call_target="tpu_custom_call", output_to_operand_aliasing={{0}: (12, {}), {1}: (13, {}), {2}: (14, {}), {3}: (15, {})} | custom-call | flops 10000000 | bytes 100000 | tf_op jit(solution)/shard_map/pallas_call | solution.py:231
  439.7 9.7 %all-to-all-start.8 = ((bf16[128,8,384]{2,1,0:T(8,128)(2,1)}), bf16[128,8,384]{2,1,0:T(8,128)(2,1)}, u32[]{:S(2)}, u32[]{:S(2)}) async-start(bf16[128,8,384]{2,1,0:T(8,128)(2,1)} %pad_maximum_fusion.4), calls=%async_computation.9 | async-start | bytes 1572864 | tf_op jit(solution)/shard_map/all_to_all | solution.py:499
  452.6 38.9 %all-to-all-done.8 = bf16[128,8,384]{2,1,0:T(8,128)(2,1)} async-done(((bf16[128,8,384]{2,1,0:T(8,128)(2,1)}), bf16[128,8,384]{2,1,0:T(8,128)(2,1)}, u32[]{:S(2)}, u32[]{:S(2)}) %all-to-all-start.8) | async-done | bytes 786464 | tf_op jit(solution)/shard_map/all_to_all | solution.py:499
  497.8 9.2 %all-to-all-start.9 = ((bf16[64,8,1024]{2,1,0:T(8,128)(2,1)}), bf16[64,8,1024]{2,1,0:T(8,128)(2,1)}, u32[]{:S(2)}, u32[]{:S(2)}) async-start(bf16[64,8,1024]{2,1,0:T(8,128)(2,1)} %fusion), calls=%async_computation.10 | async-start | bytes 2097152 | tf_op jit(solution)/shard_map/all_to_all | solution.py:499
  518.5 7.0 %all-to-all-done.9 = bf16[64,8,1024]{2,1,0:T(8,128)(2,1)} async-done(((bf16[64,8,1024]{2,1,0:T(8,128)(2,1)}), bf16[64,8,1024]{2,1,0:T(8,128)(2,1)}, u32[]{:S(2)}, u32[]{:S(2)}) %all-to-all-start.9) | async-done | bytes 1048608 | tf_op jit(solution)/shard_map/all_to_all | solution.py:499
  (320 shorter events, 162.6 us)
Async XLA Ops:
  7.2 209.6 %all-gather.3.cloned.1.call-start = ((), (), s32[]{:S(2)}) async-start(), calls=%async_computation.12 | async-start | bytes 10027008 | tf_op jit(solution)/shard_map/all_gather | solution.py:666
  24.4 47.4 %all-to-all-start = ((bf16[128,8,384]{2,1,0:T(8,128)(2,1)}), bf16[128,8,384]{2,1,0:T(8,128)(2,1)}, u32[]{:S(2)}, u32[]{:S(2)}) async-start(bf16[128,8,384]{2,1,0:T(8,128)(2,1)} %bitcast.8), calls=%async_computation | async-start | bytes 1572864 | tf_op jit(solution)/shard_map/all_to_all | solution.py:499
  36.1 32.2 %collective-permute-start.1 = (bf16[2,128,1024]{2,1,0:T(8,128)(2,1)S(1)}, bf16[2,128,1024]{2,1,0:T(8,128)(2,1)S(1)}, u32[]{:S(2)}, u32[]{:S(2)}) collective-permute-start(bf16[2,128,1024]{2,1,0:T(8,128)(2,1)S(1)} %pad_maximum_fusion.5.refs_0_), channel_id=1, source_target_pairs={{0,96},{32,0},{64,32},{96,64},{1,97},{33,1},{65,33},{97,65},{2,98}... | collective-permute-start | bytes 1572872 | tf_op jit(solution)/shard_map/ppermute | solution.py:507
  38.9 29.4 %collective-permute-start.2 = (bf16[2,128,1024]{2,1,0:T(8,128)(2,1)S(1)}, bf16[2,128,1024]{2,1,0:T(8,128)(2,1)S(1)}, u32[]{:S(2)}, u32[]{:S(2)}) collective-permute-start(bf16[2,128,1024]{2,1,0:T(8,128)(2,1)S(1)} %pad_maximum_fusion.5.refs_0_), channel_id=1, source_target_pairs={{0,64},{32,96},{64,0},{96,32},{1,65},{33,97},{65,1},{97,33},{2,66}... | collective-permute-start | bytes 1572872 | tf_op jit(solution)/shard_map/ppermute | solution.py:507
  39.2 32.5 %collective-permute-start.3 = (bf16[2,128,1024]{2,1,0:T(8,128)(2,1)S(1)}, bf16[2,128,1024]{2,1,0:T(8,128)(2,1)S(1)}, u32[]{:S(2)}, u32[]{:S(2)}) collective-permute-start(bf16[2,128,1024]{2,1,0:T(8,128)(2,1)S(1)} %pad_maximum_fusion.5.refs_0_), channel_id=1, source_target_pairs={{0,32},{32,64},{64,96},{96,0},{1,33},{33,65},{65,97},{97,1},{2,34}... | collective-permute-start | bytes 1572872 | tf_op jit(solution)/shard_map/ppermute | solution.py:507
  41.7 43.7 %collective-permute-start.8 = (bf16[2,3,128,512]{3,2,1,0:T(8,128)(2,1)}, bf16[2,3,128,512]{3,2,1,0:T(8,128)(2,1)}, u32[]{:S(2)}, u32[]{:S(2)}) collective-permute-start(bf16[2,3,128,512]{3,2,1,0:T(8,128)(2,1)} %get-tuple-element.337), channel_id=1, source_target_pairs={{0,16},{16,0},{1,17},{17,1},{2,18},{18,2},{3,19},{19,3},{4,20},{20... | collective-permute-start | bytes 2359304 | tf_op jit(solution)/shard_map/ppermute | solution.py:503
  72.9 76.4 %all-to-all-start.1 = ((bf16[64,8,1024]{2,1,0:T(8,128)(2,1)}), bf16[64,8,1024]{2,1,0:T(8,128)(2,1)}, u32[]{:S(2)}, u32[]{:S(2)}) async-start(bf16[64,8,1024]{2,1,0:T(8,128)(2,1)} %broadcast_in_dim.33), calls=%async_computation.1 | async-start | bytes 2097152 | tf_op jit(solution)/shard_map/all_to_all | solution.py:499
  79.7 35.3 %collective-permute-start.5 = (bf16[2,128,1024]{2,1,0:T(8,128)(2,1)S(1)}, bf16[2,128,1024]{2,1,0:T(8,128)(2,1)}, u32[]{:S(2)}, u32[]{:S(2)}) collective-permute-start(bf16[2,128,1024]{2,1,0:T(8,128)(2,1)S(1)} %pad_maximum_fusion.6.refs_0_), channel_id=1, source_target_pairs={{0,96},{32,0},{64,32},{96,64},{1,97},{33,1},{65,33},{97,65},{2,98}... | collective-permute-start | bytes 1572872 | tf_op jit(solution)/shard_map/ppermute | solution.py:507
  82.7 32.3 %collective-permute-start.6 = (bf16[2,128,1024]{2,1,0:T(8,128)(2,1)S(1)}, bf16[2,128,1024]{2,1,0:T(8,128)(2,1)}, u32[]{:S(2)}, u32[]{:S(2)}) collective-permute-start(bf16[2,128,1024]{2,1,0:T(8,128)(2,1)S(1)} %pad_maximum_fusion.6.refs_0_), channel_id=1, source_target_pairs={{0,64},{32,96},{64,0},{96,32},{1,65},{33,97},{65,1},{97,33},{2,66}... | collective-permute-start | bytes 1572872 | tf_op jit(solution)/shard_map/ppermute | solution.py:507
  83.3 35.0 %collective-permute-start.7 = (bf16[2,128,1024]{2,1,0:T(8,128)(2,1)S(1)}, bf16[2,128,1024]{2,1,0:T(8,128)(2,1)}, u32[]{:S(2)}, u32[]{:S(2)}) collective-permute-start(bf16[2,128,1024]{2,1,0:T(8,128)(2,1)S(1)} %pad_maximum_fusion.6.refs_0_), channel_id=1, source_target_pairs={{0,32},{32,64},{64,96},{96,0},{1,33},{33,65},{65,97},{97,1},{2,34}... | collective-permute-start | bytes 1572872 | tf_op jit(solution)/shard_map/ppermute | solution.py:507
  118.3 48.0 %collective-permute-start.10 = (bf16[2,2,3,128,512]{4,3,2,1,0:T(8,128)(2,1)}, bf16[2,2,3,128,512]{4,3,2,1,0:T(8,128)(2,1)}, u32[]{:S(2)}, u32[]{:S(2)}) collective-permute-start(bf16[2,2,3,128,512]{4,3,2,1,0:T(8,128)(2,1)} %pad_maximum_fusion.refs_4_), channel_id=1, source_target_pairs={{0,96},{32,0},{64,32},{96,64},{1,97},{33,1},{65,33},{97,65},{2,98}... | collective-permute-start | bytes 4718600 | tf_op jit(solution)/shard_map/ppermute | solution.py:655
  119.0 47.4 %collective-permute-start.9 = (bf16[2,2,3,128,512]{4,3,2,1,0:T(8,128)(2,1)}, bf16[2,2,3,128,512]{4,3,2,1,0:T(8,128)(2,1)}, u32[]{:S(2)}, u32[]{:S(2)}) collective-permute-start(bf16[2,2,3,128,512]{4,3,2,1,0:T(8,128)(2,1)} %pad_maximum_fusion.refs_4_), channel_id=1, source_target_pairs={{0,32},{32,64},{64,96},{96,0},{1,33},{33,65},{65,97},{97,1},{2,34}... | collective-permute-start | bytes 4718600 | tf_op jit(solution)/shard_map/ppermute | solution.py:654
  174.0 33.3 %all-to-all-start.3 = ((bf16[8,128,1024]{2,1,0:T(8,128)(2,1)}), bf16[8,128,1024]{2,1,0:T(8,128)(2,1)}, u32[]{:S(2)}, u32[]{:S(2)}) async-start(bf16[8,128,1024]{2,1,0:T(8,128)(2,1)} %broadcast_in_dim.42), calls=%async_computation.3 | async-start | bytes 4194304 | tf_op jit(solution)/shard_map/all_to_all | solution.py:499
  180.3 20.1 %collective-permute-start.12 = (bf16[1,2,3,128,512]{4,3,2,1,0:T(8,128)(2,1)S(1)}, bf16[1,2,3,128,512]{4,3,2,1,0:T(8,128)(2,1)}, u32[]{:S(2)}, u32[]{:S(2)}) collective-permute-start(bf16[1,2,3,128,512]{4,3,2,1,0:T(8,128)(2,1)S(1)} %slice.209), channel_id=1, source_target_pairs={{0,32},{32,64},{64,96},{96,0},{1,33},{33,65},{65,97},{97,1},{2,34}... | collective-permute-start | bytes 2359304 | tf_op jit(solution)/shard_map/ppermute | solution.py:701
  181.6 19.2 %collective-permute-start.13 = (bf16[1,2,3,128,512]{4,3,2,1,0:T(8,128)(2,1)S(1)}, bf16[1,2,3,128,512]{4,3,2,1,0:T(8,128)(2,1)}, u32[]{:S(2)}, u32[]{:S(2)}) collective-permute-start(bf16[1,2,3,128,512]{4,3,2,1,0:T(8,128)(2,1)S(1)} %slice.210), channel_id=1, source_target_pairs={{0,96},{32,0},{64,32},{96,64},{1,97},{33,1},{65,33},{97,65},{2,98}... | collective-permute-start | bytes 2359304 | tf_op jit(solution)/shard_map/ppermute | solution.py:701
  209.9 36.6 %all-to-all-start.4 = ((bf16[8,128,1024]{2,1,0:T(8,128)(2,1)}), bf16[8,128,1024]{2,1,0:T(8,128)(2,1)}, u32[]{:S(2)}, u32[]{:S(2)}) async-start(bf16[8,128,1024]{2,1,0:T(8,128)(2,1)} %broadcast_in_dim.41), calls=%async_computation.4 | async-start | bytes 4194304 | tf_op jit(solution)/shard_map/all_to_all | solution.py:499
  255.4 38.9 %all-to-all-start.5 = ((bf16[8,128,1152]{2,1,0:T(8,128)(2,1)}), bf16[8,128,1152]{2,1,0:T(8,128)(2,1)}, u32[]{:S(2)}, u32[]{:S(2)}) async-start(bf16[8,128,1152]{2,1,0:T(8,128)(2,1)} %add_convert_fusion.1), calls=%async_computation.5 | async-start | bytes 4718592 | tf_op jit(solution)/shard_map/all_to_all | solution.py:499
  262.4 269.3 %reduce-scatter.2.cloned.1.call-start = ((), (), s32[]{:S(2)}) async-start(), calls=%async_computation.11 | async-start | bytes 8912896 | tf_op jit(solution)/shard_map/reduce_scatter | solution.py:772
  303.5 45.9 %all-to-all-start.6 = ((bf16[8,128,1152]{2,1,0:T(8,128)(2,1)}), bf16[8,128,1152]{2,1,0:T(8,128)(2,1)}, u32[]{:S(2)}, u32[]{:S(2)}) async-start(bf16[8,128,1152]{2,1,0:T(8,128)(2,1)} %add_convert_fusion), calls=%async_computation.7 | async-start | bytes 4718592 | tf_op jit(solution)/shard_map/all_to_all | solution.py:499
  341.6 20.8 %collective-permute-start.18 = (bf16[1,2,3,128,512]{4,3,2,1,0:T(8,128)(2,1)}, bf16[1,2,3,128,512]{4,3,2,1,0:T(8,128)(2,1)}, u32[]{:S(2)}, u32[]{:S(2)}) collective-permute-start(bf16[1,2,3,128,512]{4,3,2,1,0:T(8,128)(2,1)} %get-tuple-element.335), channel_id=1, source_target_pairs={{0,32},{32,64},{64,96},{96,0},{1,33},{33,65},{65,97},{97,1},{2,34}... | collective-permute-start | bytes 2359304 | tf_op jit(solution)/shard_map/ppermute | solution.py:540
  341.6 20.8 %collective-permute-start.19 = (bf16[1,2,3,128,512]{4,3,2,1,0:T(8,128)(2,1)}, bf16[1,2,3,128,512]{4,3,2,1,0:T(8,128)(2,1)}, u32[]{:S(2)}, u32[]{:S(2)}) collective-permute-start(bf16[1,2,3,128,512]{4,3,2,1,0:T(8,128)(2,1)} %get-tuple-element.334), channel_id=1, source_target_pairs={{0,96},{32,0},{64,32},{96,64},{1,97},{33,1},{65,33},{97,65},{2,98}... | collective-permute-start | bytes 2359304 | tf_op jit(solution)/shard_map/ppermute | solution.py:540
  362.4 21.2 %all-to-all-start.7 = ((bf16[8,256,128]{2,1,0:T(8,128)(2,1)}), bf16[8,256,128]{2,1,0:T(8,128)(2,1)S(1)}, u32[]{:S(2)}, u32[]{:S(2)}) async-start(bf16[8,256,128]{2,1,0:T(8,128)(2,1)} %bitcast.206), calls=%async_computation.8 | async-start | bytes 1048576 | tf_op jit(solution)/shard_map/all_to_all | solution.py:499
  386.7 37.6 %collective-permute-start.21 = (bf16[2,2,3,128,512]{4,3,2,1,0:T(8,128)(2,1)}, bf16[2,2,3,128,512]{4,3,2,1,0:T(8,128)(2,1)}, u32[]{:S(2)}, u32[]{:S(2)}) collective-permute-start(bf16[2,2,3,128,512]{4,3,2,1,0:T(8,128)(2,1)} %pad_maximum_fusion.2), channel_id=1, source_target_pairs={{0,96},{32,0},{64,32},{96,64},{1,97},{33,1},{65,33},{97,65},{2,98}... | collective-permute-start | bytes 4718600 | tf_op jit(solution)/shard_map/ppermute | solution.py:546
  390.2 35.9 %collective-permute-start.20 = (bf16[2,2,3,128,512]{4,3,2,1,0:T(8,128)(2,1)}, bf16[2,2,3,128,512]{4,3,2,1,0:T(8,128)(2,1)}, u32[]{:S(2)}, u32[]{:S(2)}) collective-permute-start(bf16[2,2,3,128,512]{4,3,2,1,0:T(8,128)(2,1)} %pad_maximum_fusion.1), channel_id=1, source_target_pairs={{0,32},{32,64},{64,96},{96,0},{1,33},{33,65},{65,97},{97,1},{2,34}... | collective-permute-start | bytes 4718600 | tf_op jit(solution)/shard_map/ppermute | solution.py:545
  428.7 62.8 %collective-permute-start.23 = (bf16[2,3,128,512]{3,2,1,0:T(8,128)(2,1)}, bf16[2,3,128,512]{3,2,1,0:T(8,128)(2,1)}, u32[]{:S(2)}, u32[]{:S(2)}) collective-permute-start(bf16[2,3,128,512]{3,2,1,0:T(8,128)(2,1)} %fusion.10), channel_id=1, source_target_pairs={{0,16},{16,0},{1,17},{17,1},{2,18},{18,2},{3,19},{19,3},{4,20},{20... | collective-permute-start | bytes 2359304 | tf_op jit(solution)/shard_map/ppermute | solution.py:503
  430.7 18.9 %collective-permute-start.22 = (bf16[64,8,1024]{2,1,0:T(8,128)(2,1)}, bf16[64,8,1024]{2,1,0:T(8,128)(2,1)}, u32[]{:S(2)}, u32[]{:S(2)}) collective-permute-start(bf16[64,8,1024]{2,1,0:T(8,128)(2,1)} %dynamic-slice_bitcast_fusion), channel_id=1, source_target_pairs={{0,1},{1,0},{2,3},{3,2},{4,5},{5,4},{6,7},{7,6},{8,9},{9,8},{10,11... | collective-permute-start | bytes 3145736 | tf_op jit(solution)/shard_map/ppermute | solution.py:503
  433.6 57.9 %collective-permute-start.24 = (bf16[2,2,128,1024]{3,2,0,1:T(8,128)(2,1)}, bf16[2,2,128,1024]{3,2,0,1:T(8,128)(2,1)}, u32[]{:S(2)}, u32[]{:S(2)}) collective-permute-start(bf16[2,2,128,1024]{3,2,0,1:T(8,128)(2,1)} %copy.264), channel_id=1, source_target_pairs={{0,32},{32,64},{64,96},{96,0},{1,33},{33,65},{65,97},{97,1},{2,34}... | collective-permute-start | bytes 3145736 | tf_op jit(solution)/shard_map/ppermute | solution.py:507
  434.8 56.7 %collective-permute-start.25 = (bf16[2,2,128,1024]{3,2,0,1:T(8,128)(2,1)}, bf16[2,2,128,1024]{3,2,0,1:T(8,128)(2,1)}, u32[]{:S(2)}, u32[]{:S(2)}) collective-permute-start(bf16[2,2,128,1024]{3,2,0,1:T(8,128)(2,1)} %copy.265), channel_id=1, source_target_pairs={{0,64},{32,96},{64,0},{96,32},{1,65},{33,97},{65,1},{97,33},{2,66}... | collective-permute-start | bytes 3145736 | tf_op jit(solution)/shard_map/ppermute | solution.py:507
  436.3 55.2 %collective-permute-start.26 = (bf16[2,2,128,1024]{3,2,1,0:T(8,128)(2,1)}, bf16[2,2,128,1024]{3,2,1,0:T(8,128)(2,1)}, u32[]{:S(2)}, u32[]{:S(2)}) collective-permute-start(bf16[2,2,128,1024]{3,2,1,0:T(8,128)(2,1)} %get-tuple-element.223), channel_id=1, source_target_pairs={{0,96},{32,0},{64,32},{96,64},{1,97},{33,1},{65,33},{97,65},{2,98}... | collective-permute-start | bytes 3145736 | tf_op jit(solution)/shard_map/ppermute | solution.py:507
  439.7 51.9 %all-to-all-start.8 = ((bf16[128,8,384]{2,1,0:T(8,128)(2,1)}), bf16[128,8,384]{2,1,0:T(8,128)(2,1)}, u32[]{:S(2)}, u32[]{:S(2)}) async-start(bf16[128,8,384]{2,1,0:T(8,128)(2,1)} %pad_maximum_fusion.4), calls=%async_computation.9 | async-start | bytes 1572864 | tf_op jit(solution)/shard_map/all_to_all | solution.py:499
  493.3 25.2 %collective-permute-start.27 = (bf16[2,128,1024]{2,1,0:T(8,128)(2,1)S(1)}, bf16[2,128,1024]{2,1,0:T(8,128)(2,1)}, u32[]{:S(2)}, u32[]{:S(2)}) collective-permute-start(bf16[2,128,1024]{2,1,0:T(8,128)(2,1)S(1)} %fusion.14), channel_id=1, source_target_pairs={{0,16},{16,0},{1,17},{17,1},{2,18},{18,2},{3,19},{19,3},{4,20},{20... | collective-permute-start | bytes 1572872 | tf_op jit(solution)/shard_map/ppermute | solution.py:503
  497.8 27.7 %all-to-all-start.9 = ((bf16[64,8,1024]{2,1,0:T(8,128)(2,1)}), bf16[64,8,1024]{2,1,0:T(8,128)(2,1)}, u32[]{:S(2)}, u32[]{:S(2)}) async-start(bf16[64,8,1024]{2,1,0:T(8,128)(2,1)} %fusion), calls=%async_computation.10 | async-start | bytes 2097152 | tf_op jit(solution)/shard_map/all_to_all | solution.py:499
  (80 other events, 635.7 us)
Sparse Core Ops, SparseCore 0:
  22.3 102.6 all-gather.2
  294.4 119.1 reduce-scatter.1

commit v16 on v15

--- a/solution.py
+++ b/solution.py
@@ -252,7 +252,7 @@
 
 def expert_kernel(scalar_ref, *refs, again):
     x_own_ref, x_other_ref, g_ref, router_ref = refs[:4]
-    pieces, refs = refs[4:9], refs[9:]
+    pieces, refs = refs[4:12], refs[12:]
     if again:
         refs = refs[1:]
     out_ref, back_own_ref, back_other_ref = refs[:3]
@@ -265,10 +265,9 @@
     depth = w_ref.shape[2] // 8
 
     loads = []
-    blocks = [(ref, i) for ref in pieces for i in range(ref.shape[0])]
-    for r, (ref, i) in enumerate(blocks):
+    for r, ref in enumerate(pieces):
         rows = pl.ds(pl.multiple_of(scalar_ref[2 + r] * depth, depth), depth)
-        loads.append(pltpu.make_async_copy(ref.at[i], w_ref.at[:, :, rows], in_sem.at[r]))
+        loads.append(pltpu.make_async_copy(ref.at[0], w_ref.at[:, :, rows], in_sem.at[r]))
         loads[-1].start()
     local, slots, hidden = act_ref.shape
     cap = slots // sources
@@ -628,10 +627,12 @@
     both_0, both_1 = (
         jnp.concatenate([tokens[m], flip(tokens[m], "yl")], axis=0) for m in range(micro)
     )
-    both_w = jnp.stack([w_gate, w_up, w_down], axis=1)
+    own_w = jnp.stack([w_gate, w_up, w_down], axis=1)[None]
+    own_before = lax.ppermute(own_w, "z", UP)
+    own_after = lax.ppermute(own_w, "z", DOWN)
+    both_0 = after_all(both_0, own_before, own_after)
     head_all = exchange(pieces.reshape((n_all,) + pieces.shape[2:]), ALL).reshape(width, -1)
-    other_w = flip(both_w, "yl")
-    both_w = jnp.stack([both_w, other_w])
+    other_w = flip(own_w, "yl")
     seq_rows = [along_z(both_0)]
     seq_rows.append(along_z(after_all(both_1, *seq_rows[0][1:])))
     head_all = after_all(head_all, *seq_rows[0][1:], other_w)
@@ -650,10 +651,6 @@
 
     out_own = exchange.copies(after_all(w_out, *seq_rows[0][1:]), CTX + GROUP, n_all // 2)
 
-    both_w = after_all(both_w, *seq_rows[1][1:])
-    w_before = lax.ppermute(both_w, "z", UP)
-    w_after = lax.ppermute(both_w, "z", DOWN)
-
     expert_ids = jnp.arange(experts, dtype=jnp.int32)
     cot = cotangent.reshape(all_tok, width)
     chosen = jnp.any(routes.reshape(all_tok, TOPK)[:, :, None] == expert_ids, axis=1)
@@ -681,13 +678,20 @@
 
     mixed_0, *saved_0 = attend_forward(order, seq_rows[0], *attention_args(0))
     seq_rows[1], mixed_0 = lax.optimization_barrier((seq_rows[1], mixed_0))
+    late_w = after_all(other_w, *seq_rows[1][1:])
+    other_before = lax.ppermute(late_w, "z", UP)
+    other_after = lax.ppermute(late_w, "z", DOWN)
+    own_far = lax.ppermute(after_all(own_before, other_before), "z", UP)
+    other_far = lax.ppermute(other_after, "z", DOWN)
     mixed_1, *saved_1 = attend_forward(order, seq_rows[1], *attention_args(1))
     saved = [saved_0, saved_1]
     out_own, mixed_0, mixed_1 = lax.optimization_barrier((out_own, mixed_0, mixed_1))
     out_other = flip(out_own, "core")
     mixed = jnp.stack([mixed_0, mixed_1]).reshape(micro, n_ctx, tok, heads).transpose(1, 0, 2, 3)
     mixed = exchange(mixed.reshape(n_ctx, all_tok, heads), CTX)
-    mixed, w_before, w_after = lax.optimization_barrier((mixed, w_before, w_after))
+    mixed, other_before, other_after = lax.optimization_barrier(
+        (mixed, other_before, other_after)
+    )
     mixed = mixed.transpose(1, 0, 2).reshape(all_tok, width)
     out_full = jnp.where(
         core == 0,
@@ -698,8 +702,7 @@
     inv_two = lax.rsqrt(jnp.mean(middle * middle, axis=-1, keepdims=True) + EPS)
     hidden_two = (middle * inv_two * gain_mlp).astype(BF)
     x_0 = exchange.copies(hidden_two[:tok], GROUP, n_ctx)
-    w_far = [lax.ppermute(w_before[:1], "z", UP), lax.ppermute(w_after[1:], "z", DOWN)]
-    weights = [both_w, w_after, *w_far, w_before]
+    weights = [own_w, other_w, own_after, other_after, own_far, other_far, own_before, other_before]
     x_0, weights = lax.optimization_barrier((x_0, weights))
     x_1 = exchange.copies(hidden_two[tok:], GROUP, n_ctx)
     logits = jnp.where(chosen, mm(hidden_two, router), -1e30)
@@ -785,27 +788,28 @@
     moved = ring_sums(parts, far)
     d_mixed = d_mixed.reshape(n_ctx, micro, tok, heads)
     d_hidden, head_grads_0 = attention_back(0, d_mixed[:, 0], [])
-    d_hidden, head_grads_1 = attention_back(1, d_mixed[:, 1], d_hidden)
-    d_hidden, moved, d_rows = lax.optimization_barrier((d_hidden, moved, d_rows))
-    hidden_moved = by_z(d_hidden)
+    d_hidden, d_mixed, d_rows = lax.optimization_barrier((d_hidden, d_mixed, d_rows))
     grad_out, grad_router, grad_mlp = weight_grads(*d_rows)
-    grad_heads, grad_attn, grad_qk = jax.tree.map(jnp.add, head_grads_0, head_grads_1)
-    grad_pack = pack_grads(grad_heads, grad_router, grad_attn, grad_mlp, grad_qk)
-    grad_pack = exchange(grad_pack, ALL)
     grad_out = grad_out.astype(BF).reshape(n_all // 2, 2, rows, width)
     grad_own = lax.dynamic_index_in_dim(grad_out, core, axis=1, keepdims=False)
     grad_other = lax.dynamic_index_in_dim(grad_out, 1 - core, axis=1, keepdims=False)
     grad_out = back_sum(grad_own, grad_other)
+    d_mixed, grad_out = lax.optimization_barrier((d_mixed, grad_out))
+    grad_out = exchange(grad_out, CTX + GROUP)
+    d_hidden, head_grads_1 = attention_back(1, d_mixed[:, 1], d_hidden)
+    d_hidden, moved = lax.optimization_barrier((d_hidden, moved))
+    hidden_moved = by_z(d_hidden)
+    grad_heads, grad_attn, grad_qk = jax.tree.map(jnp.add, head_grads_0, head_grads_1)
+    grad_pack = pack_grads(grad_heads, grad_router, grad_attn, grad_mlp, grad_qk)
+    grad_pack, grad_out = lax.optimization_barrier((grad_pack, grad_out))
+    grad_pack = exchange(grad_pack, ALL)
     weight_sums = pair_sums(parts, moved)
     weight_yl = flip(weight_sums[1].astype(BF), "yl")
-    grad_pack, grad_out, weight_yl = lax.optimization_barrier((grad_pack, grad_out, weight_yl))
-    exchange.last = grad_pack
-    grad_out = exchange(grad_out, CTX + GROUP)
     hidden_sums = [
         sum(part[:, i].astype(F32) for part in [d_hidden[0]] + hidden_moved) for i in range(2)
     ]
     hidden_yl = flip(hidden_sums[1].astype(BF), "yl")
-    grad_out, hidden_yl = lax.optimization_barrier((grad_out, hidden_yl))
+    grad_pack, hidden_yl, weight_yl = lax.optimization_barrier((grad_pack, hidden_yl, weight_yl))
 
     grad_pack = grad_pack.astype(F32)
     own_heads = jnp.sum(grad_pack[:, :, :span].reshape(n_ctx, n_fsdp, rows, -1), axis=1)

time: 549 us -> 567 us (1.033)
  waiting for transfers between devices: 174 us -> 194 us
  Pallas kernels: 121 us -> 131 us
    all_to_all x10, waiting for transfers between devices: 77.5 us -> 26.9 us  [swap(): return lax.all_to_all(parts, axis, split_axis=0, concat_axis=0, tiled=True)]
    ppermute x9, waiting for transfers between devices: 56.2 us -> 83.6 us  [by_z(): lax.ppermute(parts[k], 'z', perm)]
    ppermute x4 -> x6, waiting for transfers between devices: 15.9 us -> 34.5 us  [the longest x1 17 us: body(): own_far = lax.ppermute(after_all(own_before, other_before), 'z', UP)]
    ppermute x1, waiting for transfers between devices: 1.72 us -> 16.5 us  [ring_sums(): lax.ppermute(add_part(parts[1], 0, far[0]), 'z', UP)]
    pallas_call x2, Pallas kernels: 16.9 us -> 27 us  [attend_forward(): pl.pallas_call(attend_kernel, out_shape=outs, grid=(1,), in_specs=[pl.Blo...]
    ppermute x11, waiting for transfers between devices: 18.6 us -> 28.6 us  [flip(): return lax.ppermute(block, axis, FLIP)]
    all_to_all x10, starting transfers between devices: 73.4 us -> 67.4 us  [swap(): return lax.all_to_all(parts, axis, split_axis=0, concat_axis=0, tiled=True)]
    unnamed x146 -> x156, local copies, waits for them, and re-layouts: 22.8 us -> 24.5 us
  transfers between devices with their start and end apart: 40 -> 42, of which waited for: 19 -> 22; matrix products, arithmetic and copies ran while one was open for 18% -> 16% of each run, Pallas kernels for 22% -> 23%
where the time goes in v16:
time: 567 us; the launch traced here: 564 us
  waiting for transfers between devices  194 us (34%)
  Pallas kernels  131 us (23%)
  starting transfers between devices  102 us (18%)
  other arithmetic  60.5 us (11%)
  local copies, waits for them, and re-layouts  52.6 us (9%)
  between operations  16.2 us (3%)
  matrix products  8.04 us (1%)
    ppermute x9, waiting for transfers between devices, by_z(): lax.ppermute(parts[k], 'z', perm)  83.6 us
    all_to_all x10, starting transfers between devices, swap(): return lax.all_to_all(parts, axis, split_axis=0, concat_axis=0, tiled=True)  67.4 us
    pallas_call x2, Pallas kernels, run_experts(): pl.pallas_call(functools.partial(expert_kernel, again=moe is not None), o...  59.3 us
    ppermute x11, waiting for transfers between devices, flip(): return lax.ppermute(block, axis, FLIP)  28.6 us
    pallas_call x2, Pallas kernels, attend_forward(): pl.pallas_call(attend_kernel, out_shape=outs, grid=(1,), in_specs=[pl.Blo...  27 us
    all_to_all x10, waiting for transfers between devices, swap(): return lax.all_to_all(parts, axis, split_axis=0, concat_axis=0, tiled=True)  26.9 us
    unnamed x156, local copies, waits for them, and re-layouts  24.5 us
    pallas_call x2, Pallas kernels, attend_backward(): pl.pallas_call(functools.partial(attend_back_kernel, again=len(held) > 0)...  24.1 us
  transfers between devices with their start and end apart: 42, of which 22 were waited for; matrix products, arithmetic and copies ran while one was open for 16% of the time, Pallas kernels for 23%

profile of v16, /device:TPU:0, one launch (start us, length us, event | category | flops | bytes accessed | tf_op | source)
XLA Modules:
  0.0 564.3 jit_solution(4632443856732379662)
XLA Ops:
  17.4 5.9 %collective-permute-done = bf16[1,128,1024]{2,1,0:T(8,128)(2,1)} collective-permute-done((bf16[1,128,1024]{2,1,0:T(8,128)(2,1)S(1)}, bf16[1,128,1024]{2,1,0:T(8,128)(2,1)}, u32[]{:S(2)}, u32[]{:S(2)}) %collective-permute-start) | collective-permute-done | bytes 262176 | tf_op jit(solution)/shard_map/ppermute | solution.py:502
  32.5 10.6 %all-to-all-start = ((bf16[128,8,384]{2,1,0:T(8,128)(2,1)}), bf16[128,8,384]{2,1,0:T(8,128)(2,1)}, u32[]{:S(2)}, u32[]{:S(2)}) async-start(bf16[128,8,384]{2,1,0:T(8,128)(2,1)} %bitcast.12), calls=%async_computation | async-start | bytes 1572864 | tf_op jit(solution)/shard_map/all_to_all | solution.py:498
  49.5 25.8 %collective-permute-done.3.refs_1_ = bf16[2,128,1024]{2,1,0:T(8,128)(2,1)S(1)} collective-permute-done((bf16[2,128,1024]{2,1,0:T(8,128)(2,1)S(1)}, bf16[2,128,1024]{2,1,0:T(8,128)(2,1)S(1)}, u32[]{:S(2)}, u32[]{:S(2)}) %collective-permute-start.3) | collective-permute-done | bytes 524320 | tf_op jit(solution)/shard_map/ppermute | solution.py:506
  79.9 6.8 %all-to-all-start.1 = ((bf16[64,8,1024]{2,1,0:T(8,128)(2,1)}), bf16[64,8,1024]{2,1,0:T(8,128)(2,1)}, u32[]{:S(2)}, u32[]{:S(2)}) async-start(bf16[64,8,1024]{2,1,0:T(8,128)(2,1)} %broadcast_in_dim.36), calls=%async_computation.1 | async-start | bytes 2097152 | tf_op jit(solution)/shard_map/all_to_all | solution.py:498
  100.3 7.9 %shard_map.246 = (bf16[1024,128]{1,0:T(8,128)(2,1)S(1)}, bf16[1024,1024]{1,0:T(8,128)(2,1)S(1)}, bf16[1024,128]{1,0:T(8,128)(2,1)S(1)}, bf16[1024,128]{1,0:T(8,128)(2,1)S(1)}) custom-call(s32[8]{0:T(128)S(1)} %fusion.29.order_ref, bf16[2,128,1024]{2,1,0:T(8,128)(2,1)S(1)} %copy-done.9, bf16[2,128,1024]{2,1,0:T(8,128)(2,1)S(1)} %copy-done.23, ...), custom_call_target="tpu_custom_call" | custom-call | flops 10000000 | bytes 100000 | tf_op jit(solution)/shard_map/pallas_call | solution.py:208
  115.8 10.0 %collective-permute-done.9.refs_3_ = bf16[2,128,1024]{2,1,0:T(8,128)(2,1)} collective-permute-done((bf16[2,128,1024]{2,1,0:T(8,128)(2,1)S(1)}, bf16[2,128,1024]{2,1,0:T(8,128)(2,1)}, u32[]{:S(2)}, u32[]{:S(2)}) %collective-permute-start.9) | collective-permute-done | bytes 524320 | tf_op jit(solution)/shard_map/ppermute | solution.py:506
  125.9 19.0 %shard_map.247 = (bf16[1024,128]{1,0:T(8,128)(2,1)S(1)}, bf16[1024,1024]{1,0:T(8,128)(2,1)S(1)}, bf16[1024,128]{1,0:T(8,128)(2,1)S(1)}, bf16[1024,128]{1,0:T(8,128)(2,1)S(1)}) custom-call(s32[8]{0:T(128)S(1)} %fusion.29.order_ref, bf16[2,128,1024]{2,1,0:T(8,128)(2,1)S(1)} %pad_maximum_fusion.4.refs_0_, bf16[2,128,1024]{2,1,0:T(8,128)(2,1)} %collective-permute-done.7.refs_1_, ...), custom_call_target="tpu_custom_call" | custom-call | flops 10000000 | bytes 100000 | tf_op jit(solution)/shard_map/pallas_call | solution.py:208
  153.6 4.1 all-to-all-start.2
  158.8 15.7 %collective-permute-done.11.refs_11_ = bf16[1,2,3,128,512]{4,3,2,1,0:T(8,128)(2,1)} collective-permute-done((bf16[1,2,3,128,512]{4,3,2,1,0:T(8,128)(2,1)}, bf16[1,2,3,128,512]{4,3,2,1,0:T(8,128)(2,1)}, u32[]{:S(2)}, u32[]{:S(2)}) %collective-permute-start.11) | collective-permute-done | bytes 786464 | tf_op jit(solution)/shard_map/ppermute | solution.py:682
  184.4 4.9 all-to-all-start.3
  192.5 17.0 %collective-permute-done.14.refs_8_ = bf16[1,2,3,128,512]{4,3,2,1,0:T(8,128)(2,1)} collective-permute-done((bf16[1,2,3,128,512]{4,3,2,1,0:T(8,128)(2,1)}, bf16[1,2,3,128,512]{4,3,2,1,0:T(8,128)(2,1)}, u32[]{:S(2)}, u32[]{:S(2)}) %collective-permute-start.14) | collective-permute-done | bytes 786464 | tf_op jit(solution)/shard_map/ppermute | solution.py:684
  209.5 8.0 %all-to-all-done.3.refs_0_ = bf16[8,128,1024]{2,1,0:T(8,128)(2,1)} async-done(((bf16[8,128,1024]{2,1,0:T(8,128)(2,1)}), bf16[8,128,1024]{2,1,0:T(8,128)(2,1)}, u32[]{:S(2)}, u32[]{:S(2)}) %all-to-all-start.3) | async-done | bytes 2097184 | tf_op jit(solution)/shard_map/all_to_all | solution.py:498
  220.0 4.4 all-to-all-start.4
  226.7 29.7 %shard_map.248 = (bf16[16,2,128,1024]{3,2,1,0:T(8,128)(2,1)}, bf16[8,128,1152]{2,1,0:T(8,128)(2,1)}, bf16[8,128,1152]{2,1,0:T(8,128)(2,1)}, bf16[2,768,1024]{2,1...) custom-call(s32[10]{0:T(128)} %pad_add_fusion.scalar_ref, ...), custom_call_target="tpu_custom_call" | custom-call | flops 10000000 | bytes 100000 | tf_op jit(solution)/shard_map/pallas_call | solution.py:406
  257.0 4.4 collective-permute-done.17
  265.4 6.8 %all-to-all-start.5 = ((bf16[8,128,1152]{2,1,0:T(8,128)(2,1)}), bf16[8,128,1152]{2,1,0:T(8,128)(2,1)}, u32[]{:S(2)}, u32[]{:S(2)}) async-start(bf16[8,128,1152]{2,1,0:T(8,128)(2,1)} %add_convert_fusion.1), calls=%async_computation.5 | async-start | bytes 4718592 | tf_op jit(solution)/shard_map/all_to_all | solution.py:498
  272.5 29.6 %shard_map.249 = (bf16[16,2,128,1024]{3,2,1,0:T(8,128)(2,1)}, bf16[8,128,1152]{2,1,0:T(8,128)(2,1)}, bf16[8,128,1152]{2,1,0:T(8,128)(2,1)}, bf16[2,768,1024]{2,1...) custom-call(s32[10]{0:T(128)} %pad_add_fusion.scalar_ref, ...), custom_call_target="tpu_custom_call", output_to_operand_aliasing={{0}: (13, {})} | custom-call | flops 10000000 | bytes 100000 | tf_op jit(solution)/shard_map/pallas_call | solution.py:406
  304.2 4.8 collective-permute-done.19
  309.0 4.4 add_convert_fusion
  313.4 10.1 %all-to-all-start.6 = ((bf16[8,128,1152]{2,1,0:T(8,128)(2,1)}), bf16[8,128,1152]{2,1,0:T(8,128)(2,1)}, u32[]{:S(2)}, u32[]{:S(2)}) async-start(bf16[8,128,1152]{2,1,0:T(8,128)(2,1)} %add_convert_fusion), calls=%async_computation.7 | async-start | bytes 4718592 | tf_op jit(solution)/shard_map/all_to_all | solution.py:498
  328.8 20.5 %shard_map.250 = (bf16[2,2,3,128,512]{4,3,2,1,0:T(8,128)(2,1)S(1)}, bf16[2,2,3,128,512]{4,3,2,1,0:T(8,128)(2,1)S(1)}, bf16[2,2,3,128,512]{4,3,2,1,0:T(8,128)(2,1)S(1)}, bf16[2,2,3,128,512]{4,3,2,1,0:T(8,128)(2,1)}) custom-call(s32[8]{0:T(128)S(1)} %fusion.29.order_ref, bf16[2,768,1024]{2,1,0:T(8,128)(2,1)} %get-tuple-element.187.refs_0_, ...), custom_call_target="tpu_custom_call" | custom-call | flops 10000000 | bytes 100000 | tf_op jit(solution)/shard_map/pallas_call | solution.py:455
  355.4 4.2 all-to-all-done.6
  369.1 4.0 collective-permute-done.20
  373.1 5.9 %all-to-all-start.7 = ((bf16[8,256,128]{2,1,0:T(8,128)(2,1)}), bf16[8,256,128]{2,1,0:T(8,128)(2,1)S(1)}, u32[]{:S(2)}, u32[]{:S(2)}) async-start(bf16[8,256,128]{2,1,0:T(8,128)(2,1)} %bitcast.204), calls=%async_computation.8 | async-start | bytes 1048576 | tf_op jit(solution)/shard_map/all_to_all | solution.py:498
  382.2 11.8 %all-to-all-done.7 = bf16[8,256,128]{2,1,0:T(8,128)(2,1)S(1)} async-done(((bf16[8,256,128]{2,1,0:T(8,128)(2,1)}), bf16[8,256,128]{2,1,0:T(8,128)(2,1)S(1)}, u32[]{:S(2)}, u32[]{:S(2)}) %all-to-all-start.7) | async-done | bytes 524320 | tf_op jit(solution)/shard_map/all_to_all | solution.py:498
  398.1 12.0 %shard_map.251 = (bf16[2,2,128,1024]{3,2,1,0:T(8,128)(2,1)S(1)}, bf16[2,2,128,1024]{3,2,1,0:T(8,128)(2,1)S(1)}, bf16[2,2,128,1024]{3,2,1,0:T(8,128)(2,1)S(1)}, b...) custom-call(s32[8]{0:T(128)S(1)} %fusion.29.order_ref, ...), custom_call_target="tpu_custom_call" | custom-call | flops 10000000 | bytes 100000 | tf_op jit(solution)/shard_map/pallas_call | solution.py:231
  424.4 6.6 %all-to-all-start.8 = ((bf16[64,8,1024]{2,1,0:T(8,128)(2,1)}), bf16[64,8,1024]{2,1,0:T(8,128)(2,1)}, u32[]{:S(2)}, u32[]{:S(2)}) async-start(bf16[64,8,1024]{2,1,0:T(8,128)(2,1)} %fusion), calls=%async_computation.9 | async-start | bytes 2097152 | tf_op jit(solution)/shard_map/all_to_all | solution.py:498
  436.9 12.0 %shard_map.252 = (bf16[2,2,128,1024]{3,2,1,0:T(8,128)(2,1)S(1)}, bf16[2,2,128,1024]{3,2,1,0:T(8,128)(2,1)S(1)}, bf16[2,2,128,1024]{3,2,1,0:T(8,128)(2,1)S(1)}, b...) custom-call(s32[8]{0:T(128)S(1)} %fusion.29.order_ref, ...), custom_call_target="tpu_custom_call", output_to_operand_aliasing={{0}: (12, {}), {1}: (13, {}), {2}: (14, {}), {3}: (15, {})} | custom-call | flops 10000000 | bytes 100000 | tf_op jit(solution)/shard_map/pallas_call | solution.py:231
  449.0 16.5 %collective-permute-done.23 = bf16[2,2,3,128,512]{4,3,2,1,0:T(8,128)(2,1)} collective-permute-done((bf16[2,2,3,128,512]{4,3,2,1,0:T(8,128)(2,1)}, bf16[2,2,3,128,512]{4,3,2,1,0:T(8,128)(2,1)}, u32[]{:S(2)}, u32[]{:S(2)}) %collective-permute-start.23) | collective-permute-done | bytes 1572896 | tf_op jit(solution)/shard_map/ppermute | solution.py:544
  477.3 7.3 %all-to-all-start.9 = ((bf16[128,8,384]{2,1,0:T(8,128)(2,1)}), bf16[128,8,384]{2,1,0:T(8,128)(2,1)}, u32[]{:S(2)}, u32[]{:S(2)}) async-start(bf16[128,8,384]{2,1,0:T(8,128)(2,1)} %pad_maximum_fusion.2), calls=%async_computation.10 | async-start | bytes 1572864 | tf_op jit(solution)/shard_map/all_to_all | solution.py:498
  484.6 37.7 %collective-permute-done.25 = bf16[2,2,128,1024]{3,2,0,1:T(8,128)(2,1)} collective-permute-done((bf16[2,2,128,1024]{3,2,0,1:T(8,128)(2,1)}, bf16[2,2,128,1024]{3,2,0,1:T(8,128)(2,1)}, u32[]{:S(2)}, u32[]{:S(2)}) %collective-permute-start.25) | collective-permute-done | bytes 1048608 | tf_op jit(solution)/shard_map/ppermute | solution.py:506
  529.0 10.3 %collective-permute-done.28 = bf16[2,128,1024]{2,1,0:T(8,128)(2,1)} collective-permute-done((bf16[2,128,1024]{2,1,0:T(8,128)(2,1)}, bf16[2,128,1024]{2,1,0:T(8,128)(2,1)}, u32[]{:S(2)}, u32[]{:S(2)}) %collective-permute-start.28) | collective-permute-done | bytes 524320 | tf_op jit(solution)/shard_map/ppermute | solution.py:502
  (332 shorter events, 169.5 us)
Async XLA Ops:
  7.2 219.5 %all-gather.3.cloned.1.call-start = ((), (), s32[]{:S(2)}) async-start(), calls=%async_computation.12 | async-start | bytes 10027008 | tf_op jit(solution)/shard_map/all_gather | solution.py:663
  8.5 21.7 %collective-permute-start.1 = (bf16[1,2,3,128,512]{4,3,2,1,0:T(8,128)(2,1)S(1)}, bf16[1,2,3,128,512]{4,3,2,1,0:T(8,128)(2,1)S(1)}, u32[]{:S(2)}, u32[]{:S(2)}) collective-permute-start(bf16[1,2,3,128,512]{4,3,2,1,0:T(8,128)(2,1)S(1)} %maximum_bitcast_fusion.refs_4_), channel_id=1, source_target_pairs={{0,32},{32,64},{64,96},{96,0},{1,33},{33,65},{65,97},{97,1},{2,34}... | collective-permute-start | bytes 2359304 | tf_op jit(solution)/shard_map/ppermute | solution.py:631
  32.5 46.3 %all-to-all-start = ((bf16[128,8,384]{2,1,0:T(8,128)(2,1)}), bf16[128,8,384]{2,1,0:T(8,128)(2,1)}, u32[]{:S(2)}, u32[]{:S(2)}) async-start(bf16[128,8,384]{2,1,0:T(8,128)(2,1)} %bitcast.12), calls=%async_computation | async-start | bytes 1572864 | tf_op jit(solution)/shard_map/all_to_all | solution.py:498
  43.1 32.2 %collective-permute-start.3 = (bf16[2,128,1024]{2,1,0:T(8,128)(2,1)S(1)}, bf16[2,128,1024]{2,1,0:T(8,128)(2,1)S(1)}, u32[]{:S(2)}, u32[]{:S(2)}) collective-permute-start(bf16[2,128,1024]{2,1,0:T(8,128)(2,1)S(1)} %pad_maximum_fusion.3.refs_0_), channel_id=1, source_target_pairs={{0,96},{32,0},{64,32},{96,64},{1,97},{33,1},{65,33},{97,65},{2,98}... | collective-permute-start | bytes 1572872 | tf_op jit(solution)/shard_map/ppermute | solution.py:506
  46.0 29.4 %collective-permute-start.4 = (bf16[2,128,1024]{2,1,0:T(8,128)(2,1)S(1)}, bf16[2,128,1024]{2,1,0:T(8,128)(2,1)S(1)}, u32[]{:S(2)}, u32[]{:S(2)}) collective-permute-start(bf16[2,128,1024]{2,1,0:T(8,128)(2,1)S(1)} %pad_maximum_fusion.3.refs_0_), channel_id=1, source_target_pairs={{0,64},{32,96},{64,0},{96,32},{1,65},{33,97},{65,1},{97,33},{2,66}... | collective-permute-start | bytes 1572872 | tf_op jit(solution)/shard_map/ppermute | solution.py:506
  46.3 32.5 %collective-permute-start.5 = (bf16[2,128,1024]{2,1,0:T(8,128)(2,1)S(1)}, bf16[2,128,1024]{2,1,0:T(8,128)(2,1)S(1)}, u32[]{:S(2)}, u32[]{:S(2)}) collective-permute-start(bf16[2,128,1024]{2,1,0:T(8,128)(2,1)S(1)} %pad_maximum_fusion.3.refs_0_), channel_id=1, source_target_pairs={{0,32},{32,64},{64,96},{96,0},{1,33},{33,65},{65,97},{97,1},{2,34}... | collective-permute-start | bytes 1572872 | tf_op jit(solution)/shard_map/ppermute | solution.py:506
  47.4 45.5 %collective-permute-start.10 = (bf16[1,2,3,128,512]{4,3,2,1,0:T(8,128)(2,1)}, bf16[1,2,3,128,512]{4,3,2,1,0:T(8,128)(2,1)}, u32[]{:S(2)}, u32[]{:S(2)}) collective-permute-start(bf16[1,2,3,128,512]{4,3,2,1,0:T(8,128)(2,1)} %copy-done.47), channel_id=1, source_target_pairs={{0,16},{16,0},{1,17},{17,1},{2,18},{18,2},{3,19},{19,3},{4,20},{20... | collective-permute-start | bytes 2359304 | tf_op jit(solution)/shard_map/ppermute | solution.py:502
  79.9 68.4 %all-to-all-start.1 = ((bf16[64,8,1024]{2,1,0:T(8,128)(2,1)}), bf16[64,8,1024]{2,1,0:T(8,128)(2,1)}, u32[]{:S(2)}, u32[]{:S(2)}) async-start(bf16[64,8,1024]{2,1,0:T(8,128)(2,1)} %broadcast_in_dim.36), calls=%async_computation.1 | async-start | bytes 2097152 | tf_op jit(solution)/shard_map/all_to_all | solution.py:498
  87.9 24.7 %collective-permute-start.7 = (bf16[2,128,1024]{2,1,0:T(8,128)(2,1)S(1)}, bf16[2,128,1024]{2,1,0:T(8,128)(2,1)}, u32[]{:S(2)}, u32[]{:S(2)}) collective-permute-start(bf16[2,128,1024]{2,1,0:T(8,128)(2,1)S(1)} %pad_maximum_fusion.4.refs_0_), channel_id=1, source_target_pairs={{0,96},{32,0},{64,32},{96,64},{1,97},{33,1},{65,33},{97,65},{2,98}... | collective-permute-start | bytes 1572872 | tf_op jit(solution)/shard_map/ppermute | solution.py:506
  90.9 24.9 %collective-permute-start.8 = (bf16[2,128,1024]{2,1,0:T(8,128)(2,1)S(1)}, bf16[2,128,1024]{2,1,0:T(8,128)(2,1)}, u32[]{:S(2)}, u32[]{:S(2)}) collective-permute-start(bf16[2,128,1024]{2,1,0:T(8,128)(2,1)S(1)} %pad_maximum_fusion.4.refs_0_), channel_id=1, source_target_pairs={{0,64},{32,96},{64,0},{96,32},{1,65},{33,97},{65,1},{97,33},{2,66}... | collective-permute-start | bytes 1572872 | tf_op jit(solution)/shard_map/ppermute | solution.py:506
  91.6 34.3 %collective-permute-start.9 = (bf16[2,128,1024]{2,1,0:T(8,128)(2,1)S(1)}, bf16[2,128,1024]{2,1,0:T(8,128)(2,1)}, u32[]{:S(2)}, u32[]{:S(2)}) collective-permute-start(bf16[2,128,1024]{2,1,0:T(8,128)(2,1)S(1)} %pad_maximum_fusion.4.refs_0_), channel_id=1, source_target_pairs={{0,32},{32,64},{64,96},{96,0},{1,33},{33,65},{65,97},{97,1},{2,34}... | collective-permute-start | bytes 1572872 | tf_op jit(solution)/shard_map/ppermute | solution.py:506
  148.4 28.4 %collective-permute-start.13 = (bf16[64,8,1024]{2,1,0:T(8,128)(2,1)}, bf16[64,8,1024]{2,1,0:T(8,128)(2,1)}, u32[]{:S(2)}, u32[]{:S(2)}) collective-permute-start(bf16[64,8,1024]{2,1,0:T(8,128)(2,1)} %all-to-all-done.1), channel_id=1, source_target_pairs={{0,1},{1,0},{2,3},{3,2},{4,5},{5,4},{6,7},{7,6},{8,9},{9,8},{10,11... | collective-permute-start | bytes 3145736 | tf_op jit(solution)/shard_map/ppermute | solution.py:502
  148.4 26.2 %collective-permute-start.11 = (bf16[1,2,3,128,512]{4,3,2,1,0:T(8,128)(2,1)}, bf16[1,2,3,128,512]{4,3,2,1,0:T(8,128)(2,1)}, u32[]{:S(2)}, u32[]{:S(2)}) collective-permute-start(bf16[1,2,3,128,512]{4,3,2,1,0:T(8,128)(2,1)} %collective-permute-done.10.refs_5_), channel_id=1, source_target_pairs={{0,32},{32,64},{64,96},{96,0},{1,33},{33,65},{65,97},{97,1},{2,34}... | collective-permute-start | bytes 2359304 | tf_op jit(solution)/shard_map/ppermute | solution.py:682
  148.5 26.1 %collective-permute-start.12 = (bf16[1,2,3,128,512]{4,3,2,1,0:T(8,128)(2,1)}, bf16[1,2,3,128,512]{4,3,2,1,0:T(8,128)(2,1)}, u32[]{:S(2)}, u32[]{:S(2)}) collective-permute-start(bf16[1,2,3,128,512]{4,3,2,1,0:T(8,128)(2,1)} %collective-permute-done.10.refs_5_), channel_id=1, source_target_pairs={{0,96},{32,0},{64,32},{96,64},{1,97},{33,1},{65,33},{97,65},{2,98}... | collective-permute-start | bytes 2359304 | tf_op jit(solution)/shard_map/ppermute | solution.py:683
  153.6 21.9 %all-to-all-start.2 = ((bf16[8,256,128]{2,1,0:T(8,128)(2,1)}), bf16[8,256,128]{2,1,0:T(8,128)(2,1)}, u32[]{:S(2)}, u32[]{:S(2)}) async-start(bf16[8,256,128]{2,1,0:T(8,128)(2,1)} %bitcast.205), calls=%async_computation.2 | async-start | bytes 1048576 | tf_op jit(solution)/shard_map/all_to_all | solution.py:498
  184.4 33.0 %all-to-all-start.3 = ((bf16[8,128,1024]{2,1,0:T(8,128)(2,1)}), bf16[8,128,1024]{2,1,0:T(8,128)(2,1)}, u32[]{:S(2)}, u32[]{:S(2)}) async-start(bf16[8,128,1024]{2,1,0:T(8,128)(2,1)} %broadcast_in_dim.87), calls=%async_computation.3 | async-start | bytes 4194304 | tf_op jit(solution)/shard_map/all_to_all | solution.py:498
  189.3 20.2 %collective-permute-start.14 = (bf16[1,2,3,128,512]{4,3,2,1,0:T(8,128)(2,1)}, bf16[1,2,3,128,512]{4,3,2,1,0:T(8,128)(2,1)}, u32[]{:S(2)}, u32[]{:S(2)}) collective-permute-start(bf16[1,2,3,128,512]{4,3,2,1,0:T(8,128)(2,1)} %copy-done.56), channel_id=1, source_target_pairs={{0,32},{32,64},{64,96},{96,0},{1,33},{33,65},{65,97},{97,1},{2,34}... | collective-permute-start | bytes 2359304 | tf_op jit(solution)/shard_map/ppermute | solution.py:684
  220.0 36.4 %all-to-all-start.4 = ((bf16[8,128,1024]{2,1,0:T(8,128)(2,1)}), bf16[8,128,1024]{2,1,0:T(8,128)(2,1)}, u32[]{:S(2)}, u32[]{:S(2)}) async-start(bf16[8,128,1024]{2,1,0:T(8,128)(2,1)} %broadcast_in_dim.86), calls=%async_computation.4 | async-start | bytes 4194304 | tf_op jit(solution)/shard_map/all_to_all | solution.py:498
  265.4 38.7 %all-to-all-start.5 = ((bf16[8,128,1152]{2,1,0:T(8,128)(2,1)}), bf16[8,128,1152]{2,1,0:T(8,128)(2,1)}, u32[]{:S(2)}, u32[]{:S(2)}) async-start(bf16[8,128,1152]{2,1,0:T(8,128)(2,1)} %add_convert_fusion.1), calls=%async_computation.5 | async-start | bytes 4718592 | tf_op jit(solution)/shard_map/all_to_all | solution.py:498
  272.3 282.8 %reduce-scatter.2.cloned.1.call-start = ((), (), s32[]{:S(2)}) async-start(), calls=%async_computation.11 | async-start | bytes 8912896 | tf_op jit(solution)/shard_map/reduce_scatter | solution.py:775
  313.4 46.2 %all-to-all-start.6 = ((bf16[8,128,1152]{2,1,0:T(8,128)(2,1)}), bf16[8,128,1152]{2,1,0:T(8,128)(2,1)}, u32[]{:S(2)}, u32[]{:S(2)}) async-start(bf16[8,128,1152]{2,1,0:T(8,128)(2,1)} %add_convert_fusion), calls=%async_computation.7 | async-start | bytes 4718592 | tf_op jit(solution)/shard_map/all_to_all | solution.py:498
  352.2 20.9 %collective-permute-start.20 = (bf16[1,2,3,128,512]{4,3,2,1,0:T(8,128)(2,1)}, bf16[1,2,3,128,512]{4,3,2,1,0:T(8,128)(2,1)}, u32[]{:S(2)}, u32[]{:S(2)}) collective-permute-start(bf16[1,2,3,128,512]{4,3,2,1,0:T(8,128)(2,1)} %get-tuple-element.359), channel_id=1, source_target_pairs={{0,32},{32,64},{64,96},{96,0},{1,33},{33,65},{65,97},{97,1},{2,34}... | collective-permute-start | bytes 2359304 | tf_op jit(solution)/shard_map/ppermute | solution.py:539
  352.8 20.2 %collective-permute-start.21 = (bf16[1,2,3,128,512]{4,3,2,1,0:T(8,128)(2,1)}, bf16[1,2,3,128,512]{4,3,2,1,0:T(8,128)(2,1)}, u32[]{:S(2)}, u32[]{:S(2)}) collective-permute-start(bf16[1,2,3,128,512]{4,3,2,1,0:T(8,128)(2,1)} %get-tuple-element.358), channel_id=1, source_target_pairs={{0,96},{32,0},{64,32},{96,64},{1,97},{33,1},{65,33},{97,65},{2,98}... | collective-permute-start | bytes 2359304 | tf_op jit(solution)/shard_map/ppermute | solution.py:539
  373.1 20.8 %all-to-all-start.7 = ((bf16[8,256,128]{2,1,0:T(8,128)(2,1)}), bf16[8,256,128]{2,1,0:T(8,128)(2,1)S(1)}, u32[]{:S(2)}, u32[]{:S(2)}) async-start(bf16[8,256,128]{2,1,0:T(8,128)(2,1)} %bitcast.204), calls=%async_computation.8 | async-start | bytes 1048576 | tf_op jit(solution)/shard_map/all_to_all | solution.py:498
  397.1 52.0 %collective-permute-start.24 = (bf16[2,2,3,128,512]{4,3,2,1,0:T(8,128)(2,1)}, bf16[2,2,3,128,512]{4,3,2,1,0:T(8,128)(2,1)}, u32[]{:S(2)}, u32[]{:S(2)}) collective-permute-start(bf16[2,2,3,128,512]{4,3,2,1,0:T(8,128)(2,1)} %pad_maximum_fusion.1), channel_id=1, source_target_pairs={{0,96},{32,0},{64,32},{96,64},{1,97},{33,1},{65,33},{97,65},{2,98}... | collective-permute-start | bytes 4718600 | tf_op jit(solution)/shard_map/ppermute | solution.py:545
  416.8 48.7 %collective-permute-start.23 = (bf16[2,2,3,128,512]{4,3,2,1,0:T(8,128)(2,1)}, bf16[2,2,3,128,512]{4,3,2,1,0:T(8,128)(2,1)}, u32[]{:S(2)}, u32[]{:S(2)}) collective-permute-start(bf16[2,2,3,128,512]{4,3,2,1,0:T(8,128)(2,1)} %pad_maximum_fusion), channel_id=1, source_target_pairs={{0,32},{32,64},{64,96},{96,0},{1,33},{33,65},{65,97},{97,1},{2,34}... | collective-permute-start | bytes 4718600 | tf_op jit(solution)/shard_map/ppermute | solution.py:544
  424.4 52.9 %all-to-all-start.8 = ((bf16[64,8,1024]{2,1,0:T(8,128)(2,1)}), bf16[64,8,1024]{2,1,0:T(8,128)(2,1)}, u32[]{:S(2)}, u32[]{:S(2)}) async-start(bf16[64,8,1024]{2,1,0:T(8,128)(2,1)} %fusion), calls=%async_computation.9 | async-start | bytes 2097152 | tf_op jit(solution)/shard_map/all_to_all | solution.py:498
  466.5 55.8 %collective-permute-start.25 = (bf16[2,2,128,1024]{3,2,0,1:T(8,128)(2,1)}, bf16[2,2,128,1024]{3,2,0,1:T(8,128)(2,1)}, u32[]{:S(2)}, u32[]{:S(2)}) collective-permute-start(bf16[2,2,128,1024]{3,2,0,1:T(8,128)(2,1)} %copy.264), channel_id=1, source_target_pairs={{0,32},{32,64},{64,96},{96,0},{1,33},{33,65},{65,97},{97,1},{2,34}... | collective-permute-start | bytes 3145736 | tf_op jit(solution)/shard_map/ppermute | solution.py:506
  467.6 54.7 %collective-permute-start.26 = (bf16[2,2,128,1024]{3,2,0,1:T(8,128)(2,1)}, bf16[2,2,128,1024]{3,2,0,1:T(8,128)(2,1)}, u32[]{:S(2)}, u32[]{:S(2)}) collective-permute-start(bf16[2,2,128,1024]{3,2,0,1:T(8,128)(2,1)} %copy.265), channel_id=1, source_target_pairs={{0,64},{32,96},{64,0},{96,32},{1,65},{33,97},{65,1},{97,33},{2,66}... | collective-permute-start | bytes 3145736 | tf_op jit(solution)/shard_map/ppermute | solution.py:506
  468.6 55.3 %collective-permute-start.27 = (bf16[2,2,128,1024]{3,2,1,0:T(8,128)(2,1)}, bf16[2,2,128,1024]{3,2,1,0:T(8,128)(2,1)}, u32[]{:S(2)}, u32[]{:S(2)}) collective-permute-start(bf16[2,2,128,1024]{3,2,1,0:T(8,128)(2,1)} %get-tuple-element.244), channel_id=1, source_target_pairs={{0,96},{32,0},{64,32},{96,64},{1,97},{33,1},{65,33},{97,65},{2,98}... | collective-permute-start | bytes 3145736 | tf_op jit(solution)/shard_map/ppermute | solution.py:506
  476.9 52.1 %collective-permute-start.29 = (bf16[2,3,128,512]{3,2,1,0:T(8,128)(2,1)}, bf16[2,3,128,512]{3,2,1,0:T(8,128)(2,1)}, u32[]{:S(2)}, u32[]{:S(2)}) collective-permute-start(bf16[2,3,128,512]{3,2,1,0:T(8,128)(2,1)} %fusion.9), channel_id=1, source_target_pairs={{0,16},{16,0},{1,17},{17,1},{2,18},{18,2},{3,19},{19,3},{4,20},{20... | collective-permute-start | bytes 2359304 | tf_op jit(solution)/shard_map/ppermute | solution.py:502
  477.3 51.7 %all-to-all-start.9 = ((bf16[128,8,384]{2,1,0:T(8,128)(2,1)}), bf16[128,8,384]{2,1,0:T(8,128)(2,1)}, u32[]{:S(2)}, u32[]{:S(2)}) async-start(bf16[128,8,384]{2,1,0:T(8,128)(2,1)} %pad_maximum_fusion.2), calls=%async_computation.10 | async-start | bytes 1572864 | tf_op jit(solution)/shard_map/all_to_all | solution.py:498
  (87 other events, 789.2 us)
Sparse Core Ops, SparseCore 0:
  30.4 101.6 all-gather.2
  304.3 117.9 reduce-scatter.1

commit v17 on v16

--- a/solution.py
+++ b/solution.py
@@ -649,7 +649,7 @@
     )[None]
     router_pad = jnp.pad(router, ((0, 0), (0, 128 - experts)))
 
-    out_own = exchange.copies(after_all(w_out, *seq_rows[0][1:]), CTX + GROUP, n_all // 2)
+    out_own = exchange.copies(w_out, CTX + GROUP, n_all // 2)
 
     expert_ids = jnp.arange(experts, dtype=jnp.int32)
     cot = cotangent.reshape(all_tok, width)
@@ -659,7 +659,7 @@
     counts = ein("ut,mte->mue", lower, chosen.reshape(micro, tok, experts).astype(BF))
     held = jnp.where(chosen, counts.reshape(all_tok, experts) - 1.0, -1.0)
     held = jnp.pad(held, ((0, 0), (0, 128 - experts)), constant_values=-1.0).astype(BF)
-    pack = after_all(jnp.concatenate([cot, held], axis=1), both_0, both_1)
+    pack = after_all(jnp.concatenate([cot, held], axis=1), *seq_rows[0][1:])
     g_all = lax.all_gather(pack, FSDP, axis=0)
 
     cosine, sine = rope_tables(jnp.arange(length, dtype=jnp.int32))
@@ -788,28 +788,27 @@
     moved = ring_sums(parts, far)
     d_mixed = d_mixed.reshape(n_ctx, micro, tok, heads)
     d_hidden, head_grads_0 = attention_back(0, d_mixed[:, 0], [])
-    d_hidden, d_mixed, d_rows = lax.optimization_barrier((d_hidden, d_mixed, d_rows))
+    d_hidden, head_grads_1 = attention_back(1, d_mixed[:, 1], d_hidden)
+    d_hidden, moved, d_rows = lax.optimization_barrier((d_hidden, moved, d_rows))
+    hidden_moved = by_z(d_hidden)
     grad_out, grad_router, grad_mlp = weight_grads(*d_rows)
+    grad_heads, grad_attn, grad_qk = jax.tree.map(jnp.add, head_grads_0, head_grads_1)
+    grad_pack = pack_grads(grad_heads, grad_router, grad_attn, grad_mlp, grad_qk)
+    grad_pack = exchange(grad_pack, ALL)
     grad_out = grad_out.astype(BF).reshape(n_all // 2, 2, rows, width)
     grad_own = lax.dynamic_index_in_dim(grad_out, core, axis=1, keepdims=False)
     grad_other = lax.dynamic_index_in_dim(grad_out, 1 - core, axis=1, keepdims=False)
     grad_out = back_sum(grad_own, grad_other)
-    d_mixed, grad_out = lax.optimization_barrier((d_mixed, grad_out))
-    grad_out = exchange(grad_out, CTX + GROUP)
-    d_hidden, head_grads_1 = attention_back(1, d_mixed[:, 1], d_hidden)
-    d_hidden, moved = lax.optimization_barrier((d_hidden, moved))
-    hidden_moved = by_z(d_hidden)
-    grad_heads, grad_attn, grad_qk = jax.tree.map(jnp.add, head_grads_0, head_grads_1)
-    grad_pack = pack_grads(grad_heads, grad_router, grad_attn, grad_mlp, grad_qk)
-    grad_pack, grad_out = lax.optimization_barrier((grad_pack, grad_out))
-    grad_pack = exchange(grad_pack, ALL)
     weight_sums = pair_sums(parts, moved)
     weight_yl = flip(weight_sums[1].astype(BF), "yl")
+    grad_pack, grad_out, weight_yl = lax.optimization_barrier((grad_pack, grad_out, weight_yl))
+    exchange.last = grad_pack
+    grad_out = exchange(grad_out, CTX + GROUP)
     hidden_sums = [
         sum(part[:, i].astype(F32) for part in [d_hidden[0]] + hidden_moved) for i in range(2)
     ]
     hidden_yl = flip(hidden_sums[1].astype(BF), "yl")
-    grad_pack, hidden_yl, weight_yl = lax.optimization_barrier((grad_pack, hidden_yl, weight_yl))
+    grad_out, hidden_yl = lax.optimization_barrier((grad_out, hidden_yl))
 
     grad_pack = grad_pack.astype(F32)
     own_heads = jnp.sum(grad_pack[:, :, :span].reshape(n_ctx, n_fsdp, rows, -1), axis=1)

time: 567 us -> 584 us (1.030)
  waiting for transfers between devices: 194 us -> 208 us
    all_to_all x10, waiting for transfers between devices: 26.9 us -> 108 us  [swap(): return lax.all_to_all(parts, axis, split_axis=0, concat_axis=0, tiled=True)]
    ppermute x9, waiting for transfers between devices: 83.6 us -> 29.3 us  [by_z(): lax.ppermute(parts[k], 'z', perm)]
    ppermute x1, waiting for transfers between devices: 15.7 us -> 0.01 us  [body(): other_before = lax.ppermute(late_w, 'z', UP)]
    ppermute x1, waiting for transfers between devices: 16.5 us -> 1 us  [ring_sums(): lax.ppermute(add_part(parts[1], 0, far[0]), 'z', UP)]
    ppermute x11, waiting for transfers between devices: 28.6 us -> 40.7 us  [flip(): return lax.ppermute(block, axis, FLIP)]
    ppermute x1, waiting for transfers between devices: 1.8 us -> 8.7 us  [body(): own_before = lax.ppermute(own_w, 'z', UP)]
    unnamed x156 -> x132, local copies, waits for them, and re-layouts: 24.5 us -> 21.7 us
  transfers between devices with their start and end apart: 42 -> 42, of which waited for: 22 -> 20; matrix products, arithmetic and copies ran while one was open for 16% -> 16% of each run, Pallas kernels for 23% -> 23%
where the time goes in v17:
time: 584 us; the launch traced here: 581 us
  waiting for transfers between devices  208 us (36%)
  Pallas kernels  131 us (22%)
  starting transfers between devices  103 us (18%)
  other arithmetic  62.9 us (11%)
  local copies, waits for them, and re-layouts  54 us (9%)
  between operations  16 us (3%)
    all_to_all x10, waiting for transfers between devices, swap(): return lax.all_to_all(parts, axis, split_axis=0, concat_axis=0, tiled=True)  108 us
    all_to_all x10, starting transfers between devices, swap(): return lax.all_to_all(parts, axis, split_axis=0, concat_axis=0, tiled=True)  66.9 us
    pallas_call x2, Pallas kernels, run_experts(): pl.pallas_call(functools.partial(expert_kernel, again=moe is not None), o...  59.3 us
    ppermute x11, waiting for transfers between devices, flip(): return lax.ppermute(block, axis, FLIP)  40.7 us
    ppermute x9, waiting for transfers between devices, by_z(): lax.ppermute(parts[k], 'z', perm)  29.3 us
    pallas_call x2, Pallas kernels, attend_forward(): pl.pallas_call(attend_kernel, out_shape=outs, grid=(1,), in_specs=[pl.Blo...  27.2 us
    pallas_call x2, Pallas kernels, attend_backward(): pl.pallas_call(functools.partial(attend_back_kernel, again=len(held) > 0)...  24.6 us
    unnamed x132, local copies, waits for them, and re-layouts  21.7 us
  transfers between devices with their start and end apart: 42, of which 20 were waited for; matrix products, arithmetic and copies ran while one was open for 16% of the time, Pallas kernels for 23%

profile of v17, /device:TPU:0, one launch (start us, length us, event | category | flops | bytes accessed | tf_op | source)
XLA Modules:
  0.0 581.2 jit_solution(16977145876231127463)
XLA Ops:
  16.5 6.1 %collective-permute-done.1 = bf16[1,128,1024]{2,1,0:T(8,128)(2,1)S(1)} collective-permute-done((bf16[1,128,1024]{2,1,0:T(8,128)(2,1)S(1)}, bf16[1,128,1024]{2,1,0:T(8,128)(2,1)S(1)}, u32[]{:S(2)}, u32[]{:S(2)}) %collective-permute-start.1) | collective-permute-done | bytes 262176 | tf_op jit(solution)/shard_map/ppermute | solution.py:502
  22.7 8.7 %collective-permute-done.2.refs_10_ = bf16[1,2,3,128,512]{4,3,2,1,0:T(8,128)(2,1)S(1)} collective-permute-done((bf16[1,2,3,128,512]{4,3,2,1,0:T(8,128)(2,1)}, bf16[1,2,3,128,512]{4,3,2,1,0:T(8,128)(2,1)S(1)}, u32[]{:S(2)}, u32[]{:S(2)}) %collective-permute-start.2) | collective-permute-done | bytes 786464 | tf_op jit(solution)/shard_map/ppermute | solution.py:631
  37.0 19.0 %collective-permute-done.4.refs_1_ = bf16[2,128,1024]{2,1,0:T(8,128)(2,1)S(1)} collective-permute-done((bf16[2,128,1024]{2,1,0:T(8,128)(2,1)S(1)}, bf16[2,128,1024]{2,1,0:T(8,128)(2,1)S(1)}, u32[]{:S(2)}, u32[]{:S(2)}) %collective-permute-start.4) | collective-permute-done | bytes 524320 | tf_op jit(solution)/shard_map/ppermute | solution.py:506
  61.7 8.3 %all-to-all-start = ((bf16[128,8,384]{2,1,0:T(8,128)(2,1)}), bf16[128,8,384]{2,1,0:T(8,128)(2,1)}, u32[]{:S(2)}, u32[]{:S(2)}) async-start(bf16[128,8,384]{2,1,0:T(8,128)(2,1)} %bitcast.7), calls=%async_computation | async-start | bytes 1572864 | tf_op jit(solution)/shard_map/all_to_all | solution.py:498
  74.8 15.9 %all-to-all-done = bf16[128,8,384]{2,1,0:T(8,128)(2,1)} async-done(((bf16[128,8,384]{2,1,0:T(8,128)(2,1)}), bf16[128,8,384]{2,1,0:T(8,128)(2,1)}, u32[]{:S(2)}, u32[]{:S(2)}) %all-to-all-start) | async-done | bytes 786464 | tf_op jit(solution)/shard_map/all_to_all | solution.py:498
  91.9 5.5 all-to-all-start.1
  97.9 25.2 %collective-permute-done = bf16[1,128,1024]{2,1,0:T(8,128)(2,1)} collective-permute-done((bf16[1,128,1024]{2,1,0:T(8,128)(2,1)S(1)}, bf16[1,128,1024]{2,1,0:T(8,128)(2,1)}, u32[]{:S(2)}, u32[]{:S(2)}) %collective-permute-start) | collective-permute-done | bytes 262176 | tf_op jit(solution)/shard_map/ppermute | solution.py:502
  136.7 8.0 %shard_map.246 = (bf16[1024,128]{1,0:T(8,128)(2,1)S(1)}, bf16[1024,1024]{1,0:T(8,128)(2,1)S(1)}, bf16[1024,128]{1,0:T(8,128)(2,1)S(1)}, bf16[1024,128]{1,0:T(8,128)(2,1)S(1)}) custom-call(s32[8]{0:T(128)S(1)} %fusion.30.order_ref, bf16[2,128,1024]{2,1,0:T(8,128)(2,1)S(1)} %pad_maximum_fusion.4.refs_0_, bf16[2,128,1024]{2,1,0:T(8,128)(2,1)S(1)} %copy-done.18, ...), custom_call_target="tpu_custom_call" | custom-call | flops 10000000 | bytes 100000 | tf_op jit(solution)/shard_map/pallas_call | solution.py:208
  154.3 19.3 %shard_map.247 = (bf16[1024,128]{1,0:T(8,128)(2,1)S(1)}, bf16[1024,1024]{1,0:T(8,128)(2,1)S(1)}, bf16[1024,128]{1,0:T(8,128)(2,1)S(1)}, bf16[1024,128]{1,0:T(8,128)(2,1)S(1)}) custom-call(s32[8]{0:T(128)S(1)} %fusion.30.order_ref, bf16[2,128,1024]{2,1,0:T(8,128)(2,1)} %pad_maximum_fusion.3.refs_0_, bf16[2,128,1024]{2,1,0:T(8,128)(2,1)} %collective-permute-done.7.refs_1_, ...), custom_call_target="tpu_custom_call" | custom-call | flops 10000000 | bytes 100000 | tf_op jit(solution)/shard_map/pallas_call | solution.py:208
  180.7 4.1 all-to-all-start.2
  187.0 15.7 %all-to-all-done.2 = bf16[8,256,128]{2,1,0:T(8,128)(2,1)} async-done(((bf16[8,256,128]{2,1,0:T(8,128)(2,1)}), bf16[8,256,128]{2,1,0:T(8,128)(2,1)}, u32[]{:S(2)}, u32[]{:S(2)}) %all-to-all-start.2) | async-done | bytes 524320 | tf_op jit(solution)/shard_map/all_to_all | solution.py:498
  213.1 7.8 %all-to-all-start.3 = ((bf16[8,128,1024]{2,1,0:T(8,128)(2,1)}), bf16[8,128,1024]{2,1,0:T(8,128)(2,1)}, u32[]{:S(2)}, u32[]{:S(2)}) async-start(bf16[8,128,1024]{2,1,0:T(8,128)(2,1)} %broadcast_in_dim.87), calls=%async_computation.3 | async-start | bytes 4194304 | tf_op jit(solution)/shard_map/all_to_all | solution.py:498
  224.1 17.2 %collective-permute-done.14.refs_8_ = bf16[1,2,3,128,512]{4,3,2,1,0:T(8,128)(2,1)} collective-permute-done((bf16[1,2,3,128,512]{4,3,2,1,0:T(8,128)(2,1)}, bf16[1,2,3,128,512]{4,3,2,1,0:T(8,128)(2,1)}, u32[]{:S(2)}, u32[]{:S(2)}) %collective-permute-start.14) | collective-permute-done | bytes 786464 | tf_op jit(solution)/shard_map/ppermute | solution.py:684
  241.3 8.0 %all-to-all-done.3.refs_0_ = bf16[8,128,1024]{2,1,0:T(8,128)(2,1)} async-done(((bf16[8,128,1024]{2,1,0:T(8,128)(2,1)}), bf16[8,128,1024]{2,1,0:T(8,128)(2,1)}, u32[]{:S(2)}, u32[]{:S(2)}) %all-to-all-start.3) | async-done | bytes 2097184 | tf_op jit(solution)/shard_map/all_to_all | solution.py:498
  251.9 5.3 all-to-all-start.4
  259.5 29.7 %shard_map.248 = (bf16[16,2,128,1024]{3,2,1,0:T(8,128)(2,1)}, bf16[8,128,1152]{2,1,0:T(8,128)(2,1)}, bf16[8,128,1152]{2,1,0:T(8,128)(2,1)}, bf16[2,768,1024]{2,1...) custom-call(s32[10]{0:T(128)} %pad_add_fusion.scalar_ref, ...), custom_call_target="tpu_custom_call" | custom-call | flops 10000000 | bytes 100000 | tf_op jit(solution)/shard_map/pallas_call | solution.py:406
  289.5 4.5 collective-permute-done.17
  298.0 7.1 %all-to-all-start.5 = ((bf16[8,128,1152]{2,1,0:T(8,128)(2,1)}), bf16[8,128,1152]{2,1,0:T(8,128)(2,1)}, u32[]{:S(2)}, u32[]{:S(2)}) async-start(bf16[8,128,1152]{2,1,0:T(8,128)(2,1)} %add_convert_fusion.1), calls=%async_computation.5 | async-start | bytes 4718592 | tf_op jit(solution)/shard_map/all_to_all | solution.py:498
  305.4 29.6 %shard_map.249 = (bf16[16,2,128,1024]{3,2,1,0:T(8,128)(2,1)}, bf16[8,128,1152]{2,1,0:T(8,128)(2,1)}, bf16[8,128,1152]{2,1,0:T(8,128)(2,1)}, bf16[2,768,1024]{2,1...) custom-call(s32[10]{0:T(128)} %pad_add_fusion.scalar_ref, ...), custom_call_target="tpu_custom_call", output_to_operand_aliasing={{0}: (13, {})} | custom-call | flops 10000000 | bytes 100000 | tf_op jit(solution)/shard_map/pallas_call | solution.py:406
  337.0 4.8 collective-permute-done.19
  341.9 4.4 add_convert_fusion
  346.2 10.1 %all-to-all-start.6 = ((bf16[8,128,1152]{2,1,0:T(8,128)(2,1)}), bf16[8,128,1152]{2,1,0:T(8,128)(2,1)}, u32[]{:S(2)}, u32[]{:S(2)}) async-start(bf16[8,128,1152]{2,1,0:T(8,128)(2,1)} %add_convert_fusion), calls=%async_computation.7 | async-start | bytes 4718592 | tf_op jit(solution)/shard_map/all_to_all | solution.py:498
  361.9 20.2 %shard_map.250 = (bf16[2,2,3,128,512]{4,3,2,1,0:T(8,128)(2,1)S(1)}, bf16[2,2,3,128,512]{4,3,2,1,0:T(8,128)(2,1)S(1)}, bf16[2,2,3,128,512]{4,3,2,1,0:T(8,128)(2,1)S(1)}, bf16[2,2,3,128,512]{4,3,2,1,0:T(8,128)(2,1)}) custom-call(s32[8]{0:T(128)S(1)} %fusion.30.order_ref, bf16[2,768,1024]{2,1,0:T(8,128)(2,1)} %get-tuple-element.178.refs_0_, ...), custom_call_target="tpu_custom_call" | custom-call | flops 10000000 | bytes 100000 | tf_op jit(solution)/shard_map/pallas_call | solution.py:455
  388.1 5.5 all-to-all-done.6
  405.8 4.2 all-to-all-start.7
  413.3 11.5 %all-to-all-done.7 = bf16[8,256,128]{2,1,0:T(8,128)(2,1)} async-done(((bf16[8,256,128]{2,1,0:T(8,128)(2,1)}), bf16[8,256,128]{2,1,0:T(8,128)(2,1)}, u32[]{:S(2)}, u32[]{:S(2)}) %all-to-all-start.7) | async-done | bytes 524320 | tf_op jit(solution)/shard_map/all_to_all | solution.py:498
  436.3 12.2 %shard_map.251 = (bf16[2,2,128,1024]{3,2,1,0:T(8,128)(2,1)S(1)}, bf16[2,2,128,1024]{3,2,1,0:T(8,128)(2,1)S(1)}, bf16[2,2,128,1024]{3,2,1,0:T(8,128)(2,1)S(1)}, b...) custom-call(s32[8]{0:T(128)S(1)} %fusion.30.order_ref, ...), custom_call_target="tpu_custom_call" | custom-call | flops 10000000 | bytes 100000 | tf_op jit(solution)/shard_map/pallas_call | solution.py:231
  448.5 12.4 %shard_map.252 = (bf16[2,2,128,1024]{3,2,1,0:T(8,128)(2,1)S(1)}, bf16[2,2,128,1024]{3,2,1,0:T(8,128)(2,1)S(1)}, bf16[2,2,128,1024]{3,2,1,0:T(8,128)(2,1)S(1)}, b...) custom-call(s32[8]{0:T(128)S(1)} %fusion.30.order_ref, ...), custom_call_target="tpu_custom_call", output_to_operand_aliasing={{0}: (12, {}), {1}: (13, {}), {2}: (14, {}), {3}: (15, {})} | custom-call | flops 10000000 | bytes 100000 | tf_op jit(solution)/shard_map/pallas_call | solution.py:231
  481.3 7.2 %all-to-all-start.8 = ((bf16[128,8,384]{2,1,0:T(8,128)(2,1)}), bf16[128,8,384]{2,1,0:T(8,128)(2,1)}, u32[]{:S(2)}, u32[]{:S(2)}) async-start(bf16[128,8,384]{2,1,0:T(8,128)(2,1)} %pad_maximum_fusion.2), calls=%async_computation.9 | async-start | bytes 1572864 | tf_op jit(solution)/shard_map/all_to_all | solution.py:498
  491.8 42.4 %all-to-all-done.8 = bf16[128,8,384]{2,1,0:T(8,128)(2,1)} async-done(((bf16[128,8,384]{2,1,0:T(8,128)(2,1)}), bf16[128,8,384]{2,1,0:T(8,128)(2,1)}, u32[]{:S(2)}, u32[]{:S(2)}) %all-to-all-start.8) | async-done | bytes 786464 | tf_op jit(solution)/shard_map/all_to_all | solution.py:498
  540.3 7.2 %all-to-all-start.9 = ((bf16[64,8,1024]{2,1,0:T(8,128)(2,1)}), bf16[64,8,1024]{2,1,0:T(8,128)(2,1)}, u32[]{:S(2)}, u32[]{:S(2)}) async-start(bf16[64,8,1024]{2,1,0:T(8,128)(2,1)} %fusion), calls=%async_computation.10 | async-start | bytes 2097152 | tf_op jit(solution)/shard_map/all_to_all | solution.py:498
  559.1 7.0 %all-to-all-done.9 = bf16[64,8,1024]{2,1,0:T(8,128)(2,1)} async-done(((bf16[64,8,1024]{2,1,0:T(8,128)(2,1)}), bf16[64,8,1024]{2,1,0:T(8,128)(2,1)}, u32[]{:S(2)}, u32[]{:S(2)}) %all-to-all-start.9) | async-done | bytes 1048608 | tf_op jit(solution)/shard_map/all_to_all | solution.py:498
  (307 shorter events, 171.1 us)
Async XLA Ops:
  7.2 252.3 %all-gather.3.cloned.1.call-start = ((), (), s32[]{:S(2)}) async-start(), calls=%async_computation.12 | async-start | bytes 10027008 | tf_op jit(solution)/shard_map/all_gather | solution.py:663
  9.4 21.9 %collective-permute-start.2 = (bf16[1,2,3,128,512]{4,3,2,1,0:T(8,128)(2,1)}, bf16[1,2,3,128,512]{4,3,2,1,0:T(8,128)(2,1)S(1)}, u32[]{:S(2)}, u32[]{:S(2)}) collective-permute-start(bf16[1,2,3,128,512]{4,3,2,1,0:T(8,128)(2,1)} %maximum_bitcast_fusion.refs_4_), channel_id=1, source_target_pairs={{0,32},{32,64},{64,96},{96,0},{1,33},{33,65},{65,97},{97,1},{2,34}... | collective-permute-start | bytes 2359304 | tf_op jit(solution)/shard_map/ppermute | solution.py:631
  31.4 24.6 %collective-permute-start.4 = (bf16[2,128,1024]{2,1,0:T(8,128)(2,1)S(1)}, bf16[2,128,1024]{2,1,0:T(8,128)(2,1)S(1)}, u32[]{:S(2)}, u32[]{:S(2)}) collective-permute-start(bf16[2,128,1024]{2,1,0:T(8,128)(2,1)S(1)} %pad_maximum_fusion.4.refs_0_), channel_id=1, source_target_pairs={{0,96},{32,0},{64,32},{96,64},{1,97},{33,1},{65,33},{97,65},{2,98}... | collective-permute-start | bytes 1572872 | tf_op jit(solution)/shard_map/ppermute | solution.py:506
  34.4 21.6 %collective-permute-start.5 = (bf16[2,128,1024]{2,1,0:T(8,128)(2,1)S(1)}, bf16[2,128,1024]{2,1,0:T(8,128)(2,1)S(1)}, u32[]{:S(2)}, u32[]{:S(2)}) collective-permute-start(bf16[2,128,1024]{2,1,0:T(8,128)(2,1)S(1)} %pad_maximum_fusion.4.refs_0_), channel_id=1, source_target_pairs={{0,64},{32,96},{64,0},{96,32},{1,65},{33,97},{65,1},{97,33},{2,66}... | collective-permute-start | bytes 1572872 | tf_op jit(solution)/shard_map/ppermute | solution.py:506
  34.7 24.7 %collective-permute-start.6 = (bf16[2,128,1024]{2,1,0:T(8,128)(2,1)S(1)}, bf16[2,128,1024]{2,1,0:T(8,128)(2,1)S(1)}, u32[]{:S(2)}, u32[]{:S(2)}) collective-permute-start(bf16[2,128,1024]{2,1,0:T(8,128)(2,1)S(1)} %pad_maximum_fusion.4.refs_0_), channel_id=1, source_target_pairs={{0,32},{32,64},{64,96},{96,0},{1,33},{33,65},{65,97},{97,1},{2,34}... | collective-permute-start | bytes 1572872 | tf_op jit(solution)/shard_map/ppermute | solution.py:506
  61.7 29.1 %all-to-all-start = ((bf16[128,8,384]{2,1,0:T(8,128)(2,1)}), bf16[128,8,384]{2,1,0:T(8,128)(2,1)}, u32[]{:S(2)}, u32[]{:S(2)}) async-start(bf16[128,8,384]{2,1,0:T(8,128)(2,1)} %bitcast.7), calls=%async_computation | async-start | bytes 1572864 | tf_op jit(solution)/shard_map/all_to_all | solution.py:498
  70.0 60.3 %collective-permute-start.10 = (bf16[1,2,3,128,512]{4,3,2,1,0:T(8,128)(2,1)}, bf16[1,2,3,128,512]{4,3,2,1,0:T(8,128)(2,1)}, u32[]{:S(2)}, u32[]{:S(2)}) collective-permute-start(bf16[1,2,3,128,512]{4,3,2,1,0:T(8,128)(2,1)} %maximum_bitcast_fusion.refs_4_), channel_id=1, source_target_pairs={{0,16},{16,0},{1,17},{17,1},{2,18},{18,2},{3,19},{19,3},{4,20},{20... | collective-permute-start | bytes 2359304 | tf_op jit(solution)/shard_map/ppermute | solution.py:502
  71.0 52.1 %collective-permute-start = (bf16[1,128,1024]{2,1,0:T(8,128)(2,1)S(1)}, bf16[1,128,1024]{2,1,0:T(8,128)(2,1)}, u32[]{:S(2)}, u32[]{:S(2)}) collective-permute-start(bf16[1,128,1024]{2,1,0:T(8,128)(2,1)S(1)} %get-tuple-element.349), channel_id=1, source_target_pairs={{0,16},{16,0},{1,17},{17,1},{2,18},{18,2},{3,19},{19,3},{4,20},{20... | collective-permute-start | bytes 786440 | tf_op jit(solution)/shard_map/ppermute | solution.py:502
  91.9 83.7 %all-to-all-start.1 = ((bf16[64,8,1024]{2,1,0:T(8,128)(2,1)}), bf16[64,8,1024]{2,1,0:T(8,128)(2,1)}, u32[]{:S(2)}, u32[]{:S(2)}) async-start(bf16[64,8,1024]{2,1,0:T(8,128)(2,1)} %broadcast_in_dim.35), calls=%async_computation.1 | async-start | bytes 2097152 | tf_op jit(solution)/shard_map/all_to_all | solution.py:498
  124.9 26.0 %collective-permute-start.7 = (bf16[2,128,1024]{2,1,0:T(8,128)(2,1)}, bf16[2,128,1024]{2,1,0:T(8,128)(2,1)}, u32[]{:S(2)}, u32[]{:S(2)}) collective-permute-start(bf16[2,128,1024]{2,1,0:T(8,128)(2,1)} %pad_maximum_fusion.3.refs_0_), channel_id=1, source_target_pairs={{0,96},{32,0},{64,32},{96,64},{1,97},{33,1},{65,33},{97,65},{2,98}... | collective-permute-start | bytes 1572872 | tf_op jit(solution)/shard_map/ppermute | solution.py:506
  128.7 22.1 %collective-permute-start.8 = (bf16[2,128,1024]{2,1,0:T(8,128)(2,1)}, bf16[2,128,1024]{2,1,0:T(8,128)(2,1)}, u32[]{:S(2)}, u32[]{:S(2)}) collective-permute-start(bf16[2,128,1024]{2,1,0:T(8,128)(2,1)} %pad_maximum_fusion.3.refs_0_), channel_id=1, source_target_pairs={{0,64},{32,96},{64,0},{96,32},{1,65},{33,97},{65,1},{97,33},{2,66}... | collective-permute-start | bytes 1572872 | tf_op jit(solution)/shard_map/ppermute | solution.py:506
  128.7 25.6 %collective-permute-start.9 = (bf16[2,128,1024]{2,1,0:T(8,128)(2,1)}, bf16[2,128,1024]{2,1,0:T(8,128)(2,1)}, u32[]{:S(2)}, u32[]{:S(2)}) collective-permute-start(bf16[2,128,1024]{2,1,0:T(8,128)(2,1)} %pad_maximum_fusion.3.refs_0_), channel_id=1, source_target_pairs={{0,32},{32,64},{64,96},{96,0},{1,33},{33,65},{65,97},{97,1},{2,34}... | collective-permute-start | bytes 1572872 | tf_op jit(solution)/shard_map/ppermute | solution.py:506
  175.6 29.2 %collective-permute-start.13 = (bf16[64,8,1024]{2,1,0:T(8,128)(2,1)}, bf16[64,8,1024]{2,1,0:T(8,128)(2,1)}, u32[]{:S(2)}, u32[]{:S(2)}) collective-permute-start(bf16[64,8,1024]{2,1,0:T(8,128)(2,1)} %all-to-all-done.1), channel_id=1, source_target_pairs={{0,1},{1,0},{2,3},{3,2},{4,5},{5,4},{6,7},{7,6},{8,9},{9,8},{10,11... | collective-permute-start | bytes 3145736 | tf_op jit(solution)/shard_map/ppermute | solution.py:502
  175.6 27.1 %collective-permute-start.11 = (bf16[1,2,3,128,512]{4,3,2,1,0:T(8,128)(2,1)}, bf16[1,2,3,128,512]{4,3,2,1,0:T(8,128)(2,1)}, u32[]{:S(2)}, u32[]{:S(2)}) collective-permute-start(bf16[1,2,3,128,512]{4,3,2,1,0:T(8,128)(2,1)} %collective-permute-done.10.refs_5_), channel_id=1, source_target_pairs={{0,32},{32,64},{64,96},{96,0},{1,33},{33,65},{65,97},{97,1},{2,34}... | collective-permute-start | bytes 2359304 | tf_op jit(solution)/shard_map/ppermute | solution.py:682
  175.6 27.1 %collective-permute-start.12 = (bf16[1,2,3,128,512]{4,3,2,1,0:T(8,128)(2,1)}, bf16[1,2,3,128,512]{4,3,2,1,0:T(8,128)(2,1)}, u32[]{:S(2)}, u32[]{:S(2)}) collective-permute-start(bf16[1,2,3,128,512]{4,3,2,1,0:T(8,128)(2,1)} %collective-permute-done.10.refs_5_), channel_id=1, source_target_pairs={{0,96},{32,0},{64,32},{96,64},{1,97},{33,1},{65,33},{97,65},{2,98}... | collective-permute-start | bytes 2359304 | tf_op jit(solution)/shard_map/ppermute | solution.py:683
  180.7 22.0 %all-to-all-start.2 = ((bf16[8,256,128]{2,1,0:T(8,128)(2,1)}), bf16[8,256,128]{2,1,0:T(8,128)(2,1)}, u32[]{:S(2)}, u32[]{:S(2)}) async-start(bf16[8,256,128]{2,1,0:T(8,128)(2,1)} %bitcast.205), calls=%async_computation.2 | async-start | bytes 1048576 | tf_op jit(solution)/shard_map/all_to_all | solution.py:498
  213.1 36.2 %all-to-all-start.3 = ((bf16[8,128,1024]{2,1,0:T(8,128)(2,1)}), bf16[8,128,1024]{2,1,0:T(8,128)(2,1)}, u32[]{:S(2)}, u32[]{:S(2)}) async-start(bf16[8,128,1024]{2,1,0:T(8,128)(2,1)} %broadcast_in_dim.87), calls=%async_computation.3 | async-start | bytes 4194304 | tf_op jit(solution)/shard_map/all_to_all | solution.py:498
  220.9 20.4 %collective-permute-start.14 = (bf16[1,2,3,128,512]{4,3,2,1,0:T(8,128)(2,1)}, bf16[1,2,3,128,512]{4,3,2,1,0:T(8,128)(2,1)}, u32[]{:S(2)}, u32[]{:S(2)}) collective-permute-start(bf16[1,2,3,128,512]{4,3,2,1,0:T(8,128)(2,1)} %copy-done.47), channel_id=1, source_target_pairs={{0,32},{32,64},{64,96},{96,0},{1,33},{33,65},{65,97},{97,1},{2,34}... | collective-permute-start | bytes 2359304 | tf_op jit(solution)/shard_map/ppermute | solution.py:684
  251.9 37.3 %all-to-all-start.4 = ((bf16[8,128,1024]{2,1,0:T(8,128)(2,1)}), bf16[8,128,1024]{2,1,0:T(8,128)(2,1)}, u32[]{:S(2)}, u32[]{:S(2)}) async-start(bf16[8,128,1024]{2,1,0:T(8,128)(2,1)} %broadcast_in_dim.86), calls=%async_computation.4 | async-start | bytes 4194304 | tf_op jit(solution)/shard_map/all_to_all | solution.py:498
  298.0 39.0 %all-to-all-start.5 = ((bf16[8,128,1152]{2,1,0:T(8,128)(2,1)}), bf16[8,128,1152]{2,1,0:T(8,128)(2,1)}, u32[]{:S(2)}, u32[]{:S(2)}) async-start(bf16[8,128,1152]{2,1,0:T(8,128)(2,1)} %add_convert_fusion.1), calls=%async_computation.5 | async-start | bytes 4718592 | tf_op jit(solution)/shard_map/all_to_all | solution.py:498
  305.1 266.8 %reduce-scatter.2.cloned.1.call-start = ((), (), s32[]{:S(2)}) async-start(), calls=%async_computation.11 | async-start | bytes 8912896 | tf_op jit(solution)/shard_map/reduce_scatter | solution.py:775
  346.2 47.4 %all-to-all-start.6 = ((bf16[8,128,1152]{2,1,0:T(8,128)(2,1)}), bf16[8,128,1152]{2,1,0:T(8,128)(2,1)}, u32[]{:S(2)}, u32[]{:S(2)}) async-start(bf16[8,128,1152]{2,1,0:T(8,128)(2,1)} %add_convert_fusion), calls=%async_computation.7 | async-start | bytes 4718592 | tf_op jit(solution)/shard_map/all_to_all | solution.py:498
  384.9 20.9 %collective-permute-start.20 = (bf16[1,2,3,128,512]{4,3,2,1,0:T(8,128)(2,1)}, bf16[1,2,3,128,512]{4,3,2,1,0:T(8,128)(2,1)}, u32[]{:S(2)}, u32[]{:S(2)}) collective-permute-start(bf16[1,2,3,128,512]{4,3,2,1,0:T(8,128)(2,1)} %get-tuple-element.343), channel_id=1, source_target_pairs={{0,32},{32,64},{64,96},{96,0},{1,33},{33,65},{65,97},{97,1},{2,34}... | collective-permute-start | bytes 2359304 | tf_op jit(solution)/shard_map/ppermute | solution.py:539
  427.7 39.3 %collective-permute-start.23 = (bf16[2,2,3,128,512]{4,3,2,1,0:T(8,128)(2,1)}, bf16[2,2,3,128,512]{4,3,2,1,0:T(8,128)(2,1)}, u32[]{:S(2)}, u32[]{:S(2)}) collective-permute-start(bf16[2,2,3,128,512]{4,3,2,1,0:T(8,128)(2,1)} %pad_maximum_fusion.1), channel_id=1, source_target_pairs={{0,96},{32,0},{64,32},{96,64},{1,97},{33,1},{65,33},{97,65},{2,98}... | collective-permute-start | bytes 4718600 | tf_op jit(solution)/shard_map/ppermute | solution.py:545
  431.3 36.7 %collective-permute-start.22 = (bf16[2,2,3,128,512]{4,3,2,1,0:T(8,128)(2,1)}, bf16[2,2,3,128,512]{4,3,2,1,0:T(8,128)(2,1)}, u32[]{:S(2)}, u32[]{:S(2)}) collective-permute-start(bf16[2,2,3,128,512]{4,3,2,1,0:T(8,128)(2,1)} %pad_maximum_fusion), channel_id=1, source_target_pairs={{0,32},{32,64},{64,96},{96,0},{1,33},{33,65},{65,97},{97,1},{2,34}... | collective-permute-start | bytes 4718600 | tf_op jit(solution)/shard_map/ppermute | solution.py:544
  470.6 63.6 %collective-permute-start.25 = (bf16[2,3,128,512]{3,2,1,0:T(8,128)(2,1)}, bf16[2,3,128,512]{3,2,1,0:T(8,128)(2,1)}, u32[]{:S(2)}, u32[]{:S(2)}) collective-permute-start(bf16[2,3,128,512]{3,2,1,0:T(8,128)(2,1)} %fusion.10), channel_id=1, source_target_pairs={{0,16},{16,0},{1,17},{17,1},{2,18},{18,2},{3,19},{19,3},{4,20},{20... | collective-permute-start | bytes 2359304 | tf_op jit(solution)/shard_map/ppermute | solution.py:502
  475.3 59.0 %collective-permute-start.26 = (bf16[2,2,128,1024]{3,2,0,1:T(8,128)(2,1)}, bf16[2,2,128,1024]{3,2,0,1:T(8,128)(2,1)}, u32[]{:S(2)}, u32[]{:S(2)}) collective-permute-start(bf16[2,2,128,1024]{3,2,0,1:T(8,128)(2,1)} %copy.264), channel_id=1, source_target_pairs={{0,32},{32,64},{64,96},{96,0},{1,33},{33,65},{65,97},{97,1},{2,34}... | collective-permute-start | bytes 3145736 | tf_op jit(solution)/shard_map/ppermute | solution.py:506
  476.3 57.9 %collective-permute-start.27 = (bf16[2,2,128,1024]{3,2,0,1:T(8,128)(2,1)}, bf16[2,2,128,1024]{3,2,0,1:T(8,128)(2,1)}, u32[]{:S(2)}, u32[]{:S(2)}) collective-permute-start(bf16[2,2,128,1024]{3,2,0,1:T(8,128)(2,1)} %copy.265), channel_id=1, source_target_pairs={{0,64},{32,96},{64,0},{96,32},{1,65},{33,97},{65,1},{97,33},{2,66}... | collective-permute-start | bytes 3145736 | tf_op jit(solution)/shard_map/ppermute | solution.py:506
  479.2 55.1 %collective-permute-start.28 = (bf16[2,2,128,1024]{3,2,1,0:T(8,128)(2,1)}, bf16[2,2,128,1024]{3,2,1,0:T(8,128)(2,1)}, u32[]{:S(2)}, u32[]{:S(2)}) collective-permute-start(bf16[2,2,128,1024]{3,2,1,0:T(8,128)(2,1)} %get-tuple-element.231), channel_id=1, source_target_pairs={{0,96},{32,0},{64,32},{96,64},{1,97},{33,1},{65,33},{97,65},{2,98}... | collective-permute-start | bytes 3145736 | tf_op jit(solution)/shard_map/ppermute | solution.py:506
  481.3 52.9 %all-to-all-start.8 = ((bf16[128,8,384]{2,1,0:T(8,128)(2,1)}), bf16[128,8,384]{2,1,0:T(8,128)(2,1)}, u32[]{:S(2)}, u32[]{:S(2)}) async-start(bf16[128,8,384]{2,1,0:T(8,128)(2,1)} %pad_maximum_fusion.2), calls=%async_computation.9 | async-start | bytes 1572864 | tf_op jit(solution)/shard_map/all_to_all | solution.py:498
  536.8 22.3 %collective-permute-start.29 = (bf16[2,128,1024]{2,1,0:T(8,128)(2,1)}, bf16[2,128,1024]{2,1,0:T(8,128)(2,1)}, u32[]{:S(2)}, u32[]{:S(2)}) collective-permute-start(bf16[2,128,1024]{2,1,0:T(8,128)(2,1)} %fusion.14), channel_id=1, source_target_pairs={{0,16},{16,0},{1,17},{17,1},{2,18},{18,2},{3,19},{19,3},{4,20},{20... | collective-permute-start | bytes 1572872 | tf_op jit(solution)/shard_map/ppermute | solution.py:502
  540.3 25.7 %all-to-all-start.9 = ((bf16[64,8,1024]{2,1,0:T(8,128)(2,1)}), bf16[64,8,1024]{2,1,0:T(8,128)(2,1)}, u32[]{:S(2)}, u32[]{:S(2)}) async-start(bf16[64,8,1024]{2,1,0:T(8,128)(2,1)} %fusion), calls=%async_computation.10 | async-start | bytes 2097152 | tf_op jit(solution)/shard_map/all_to_all | solution.py:498
  (75 other events, 736.6 us)
Sparse Core Ops, SparseCore 0:
  59.6 100.0 all-gather.2
  337.1 116.9 reduce-scatter.1
